TPU v7x, 32 devices: a whole 2x2x4 slice. The times are simulated.
32 devices in a mesh: groups: 2 (over x), gx: 16 (over z, y, core).
Axes of the slice: x: 2, y: 2, z: 4, core: 2. Of those that a mesh axis runs over, the one named last changes fastest.
Arguments:
- tokens: bfloat16 [256, 8192], P(('groups', 'gx')), parts along dimension 0, may hold values from -6 to 6
- gate_weight: bfloat16 [8192, 3584], P(None, 'gx'), may hold values from -0.0625 to 0.0625
- up_weight: bfloat16 [8192, 3584], P(None, 'gx'), may hold values from -0.0625 to 0.0625
- down_weight: bfloat16 [3584, 8192], P('gx'), may hold values from -0.09375 to 0.09375
- sign_pattern: int32 [8192], replicated, may hold values from -1 to 1, as said below
Outputs:
- mixed: bfloat16 [256, 8192], P(('groups', 'gx')), parts along dimension 0
There are 2 independent parts, one for each index of `groups`. A program takes and returns all parts, laid end to end along the dimension named above; an argument that names none is the same for every part. Nothing has to cross between parts.
Inputs may be any that keep to these rules, and one draw needn't show every extreme that they name: `sign_pattern`: each entry is -1 or 1.
All inputs are finite; a program needn't handle non-finite values.
Results may differ from a plain program's by a relative error of at most 0.0052.
Values may be sent and summed in bfloat16 or wider, within the bound.
No kernel may reach another device: no remote copies, remote signals or barrier semaphores. Data moves between devices by JAX's collectives and lax.ppermute only.
A program may use at most 128 MiB of HBM per device.

v0:
```python
import jax
import jax.numpy as jnp
from jax import lax
from jax.sharding import PartitionSpec as P


def hadamard_table(order):
    row_index = jnp.arange(order, dtype=jnp.int32)[:, None]
    col_index = jnp.arange(order, dtype=jnp.int32)[None, :]
    common = jnp.bitwise_and(row_index, col_index)
    parity = jnp.zeros((order, order), jnp.int32)
    for shift_bit in range(order.bit_length() - 1):
        parity = parity + jnp.bitwise_and(jnp.right_shift(common, shift_bit), 1)
    values = 1.0 - 2.0 * jnp.remainder(parity, 2).astype(jnp.float32)
    return values / jnp.sqrt(jnp.float32(order))


def rotate_rows(values, sign_blocks, rotation):
    count, features = values.shape
    blocks = values.reshape(count, features // 128, 128) * sign_blocks
    rotated = jnp.einsum("rbk,kl->rbl", blocks, rotation, precision=lax.Precision.HIGHEST)
    return rotated.reshape(count, features)


def on_device(tokens, gate_weight, up_weight, down_weight, sign_pattern):
    rows_dev, features = tokens.shape
    blocks_count = features // 128
    rotation = hadamard_table(128)
    sign_blocks = sign_pattern.astype(jnp.float32).reshape(blocks_count, 128)
    gathered = lax.all_gather(tokens, "gx", axis=0, tiled=True)
    gate = jnp.dot(gathered, gate_weight, preferred_element_type=jnp.float32)
    up = jnp.dot(gathered, up_weight, preferred_element_type=jnp.float32)
    hidden = (jax.nn.silu(gate) * up).astype(jnp.bfloat16)
    partial_value = jnp.dot(hidden, down_weight, preferred_element_type=jnp.float32)
    summed = lax.psum_scatter(partial_value, "gx", scatter_dimension=0, tiled=True)
    summed = rotate_rows(summed, sign_blocks, rotation)
    return summed.astype(jnp.bfloat16)


def solution(mesh):
    placed = (P(("groups", "gx"), None), P(None, "gx"), P(None, "gx"), P("gx", None), P())
    return jax.shard_map(
        on_device, mesh=mesh, in_specs=placed, out_specs=P(("groups", "gx"), None), check_vma=False
    )
```

profile of v0, /device:TPU:0, one launch (start us, length us, event | category | flops | bytes accessed | tf_op | source)
XLA Modules:
  0.0 146.0 jit_solution(1247741972288721903)
XLA Ops:
  6.5 0.0 all-gather.2.cloned.1.call-start
  6.5 0.7 all-gather.2.cloned.1.call-update
  7.3 0.0 reduce-scatter.2.cloned.1.call-start
  7.3 46.3 %all-gather.2.cloned.1.call-done = bf16[128,8192]{1,0:T(8,128)(2,1)} async-done(((bf16[8,8192]{1,0:T(8,128)(2,1)}), bf16[128,8192]{1,0:T(8,128)(2,1)}) %all-gather.2.cloned.1.call-update) | async-done | bytes 2097168 | tf_op jit(solution)/shard_map/all_gather | solution.py:30
  53.7 0.0 copy-start
  53.7 3.9 %fusion.41 = f32[128,224]{0,1:T(8,128)S(1)} fusion(bf16[128,8192]{1,0:T(8,128)(2,1)} %all-gather.2.cloned.1.call-done, bf16[8192,224]{0,1:T(8,128)(2,1)} %param.6), kind=kOutput, calls=%fused_computation.48 | convolution fusion | flops 469762048 | bytes 5881856 | tf_op jit(solution)/shard_map/dot_general | solution.py:31
  57.6 0.0 copy-done
  57.6 8.0 %fusion.2 = f32[128,8192]{1,0:T(8,128)} fusion(bf16[224,8192]{1,0:T(8,128)(2,1)} %param.8, bf16[128,8192]{1,0:T(8,128)(2,1)S(1)} %copy-done, bf16[8192,224]{0,1:T(8,128)(2,1)} %param.7, f32[128,224]{0,1:T(8,128)S(1)} %fusion.41), kind=kOutput, calls=%fused_computation.4 | convolution fusion | flops 939696128 | bytes 13746176 | tf_op jit(solution)/shard_map/dot_general | solution.py:34
  65.6 0.0 copy-start.1
  65.6 0.0 reduce-scatter.2.cloned.1.call-update
  65.6 0.7 copy-done.1
  66.4 70.6 %reduce-scatter.2.cloned.1.call-done = f32[8,8192]{1,0:T(8,128)} async-done(((f32[128,8192]{1,0:T(8,128)}), f32[8,8192]{1,0:T(8,128)}) %reduce-scatter.2.cloned.1.call-update) | async-done | bytes 262160 | tf_op jit(solution)/shard_map/reduce_scatter | solution.py:35
  137.0 1.4 fusion
  138.4 0.7 copy.11
  (1 shorter events, 0.0 us)
Async XLA Ops:
  6.5 47.1 %all-gather.2.cloned.1.call-start = ((), (), s32[]{:S(2)}) async-start(), calls=%async_computation.1 | async-start | bytes 2228224 | tf_op jit(solution)/shard_map/all_gather | solution.py:30
  7.3 129.7 %reduce-scatter.2.cloned.1.call-start = ((), (), s32[]{:S(2)}) async-start(), calls=%async_computation.2 | async-start | bytes 4456448 | tf_op jit(solution)/shard_map/reduce_scatter | solution.py:35
  53.7 3.9 %copy-start = (bf16[128,8192]{1,0:T(8,128)(2,1)S(1)}, bf16[128,8192]{1,0:T(8,128)(2,1)}, u32[]{:S(2)}) copy-start(bf16[128,8192]{1,0:T(8,128)(2,1)} %all-gather.2.cloned.1.call-done) | copy-start | bytes 6291460
  65.6 0.8 copy-start.1
Sparse Core Ops, SparseCore 0:
  9.5 44.0 all-gather.1
  65.7 71.2 reduce-scatter.1
where the time goes:
time: 146 us
  waiting for transfers between devices  118 us (81%)
  between operations  13.4 us (9%)
  matrix products  13.3 us (9%)
  local copies, waits for them, and re-layouts  1.48 us (1%)
    reduce_scatter x1, waiting for transfers between devices, on_device(): lax.psum_scatter(partial_value, 'gx', scatter_dimension=0, tiled=True)  70.6 us
    all_gather x1, waiting for transfers between devices, on_device(): gathered = lax.all_gather(tokens, 'gx', axis=0, tiled=True)  46.3 us
    dot_general x1, matrix products, on_device(): jnp.dot(hidden, down_weight, preferred_element_type=jnp.float32)  7.99 us
    dot_general x1, matrix products, on_device(): gate = jnp.dot(gathered, gate_weight, preferred_element_type=jnp.float32)  3.92 us
  transfers between devices with their start and end apart: 2, of which 2 were waited for; matrix products, arithmetic and copies ran while one was open for 0% of the time, Pallas kernels for 0%

commit v1 on v0

v1 whole, which is shorter than its diff:
```python
import jax
import jax.numpy as jnp
from jax import lax
from jax.sharding import PartitionSpec as P


def hadamard_table(order):
    row_index = jnp.arange(order, dtype=jnp.int32)[:, None]
    col_index = jnp.arange(order, dtype=jnp.int32)[None, :]
    common = jnp.bitwise_and(row_index, col_index)
    parity = jnp.zeros((order, order), jnp.int32)
    for shift_bit in range(order.bit_length() - 1):
        parity = parity + jnp.bitwise_and(jnp.right_shift(common, shift_bit), 1)
    values = 1.0 - 2.0 * jnp.remainder(parity, 2).astype(jnp.float32)
    return values / jnp.sqrt(jnp.float32(order))


def rotate_rows(values, sign_blocks, rotation):
    count, features = values.shape
    blocks = values.reshape(count, features // 128, 128) * sign_blocks
    rotated = jnp.einsum("rbk,kl->rbl", blocks, rotation, precision=lax.Precision.HIGHEST)
    return rotated.reshape(count, features)


def solution(mesh):
    members = mesh.shape["gx"]
    assert members & (members - 1) == 0 and members >= 4

    def swap(value, mask):
        return lax.ppermute(value, "gx", [(i, i ^ mask) for i in range(members)])

    def on_device(tokens, gate_weight, up_weight, down_weight, sign_pattern):
        rows, features = tokens.shape
        rotation = hadamard_table(128)
        sign_blocks = sign_pattern.astype(jnp.float32).reshape(features // 128, 128)
        column = jnp.concatenate([tokens] + [swap(tokens, m) for m in range(4, members, 4)])
        plane = jnp.concatenate([column, swap(column, 2)])
        gathered = jnp.concatenate([plane, swap(plane, 1)])
        gate = jnp.dot(gathered, gate_weight, preferred_element_type=jnp.float32)
        up = jnp.dot(gathered, up_weight, preferred_element_type=jnp.float32)
        hidden = (jax.nn.silu(gate) * up).astype(jnp.bfloat16)
        total = jnp.dot(hidden, down_weight, preferred_element_type=jnp.float32)
        for mask in (1, 2):
            half = total.shape[0] // 2
            total = total[:half] + swap(total[half:].astype(jnp.bfloat16), mask).astype(jnp.float32)
        arrived = [
            swap(total[m // 4 * rows : (m // 4 + 1) * rows].astype(jnp.bfloat16), m)
            for m in range(4, members, 4)
        ]
        summed = total[:rows]
        for block in arrived:
            summed = summed + block.astype(jnp.float32)
        return rotate_rows(summed, sign_blocks, rotation).astype(jnp.bfloat16)

    placed = (P(("groups", "gx"), None), P(None, "gx"), P(None, "gx"), P("gx", None), P())
    return jax.shard_map(
        on_device, mesh=mesh, in_specs=placed, out_specs=P(("groups", "gx"), None), check_vma=False
    )
```

time: 146 us -> 78.1 us (0.53)
  waiting for transfers between devices: 118 us -> 46.5 us
  starting transfers between devices: 0.04 us -> 15.1 us
  between operations: 13.4 us -> 0.13 us
  matrix products: 13.3 us -> 9.56 us
  other arithmetic: 0.01 us -> 2.95 us
  local copies, waits for them, and re-layouts: 1.48 us -> 3.72 us
    reduce_scatter x1 -> x0, waiting for transfers between devices: 70.6 us -> none  [on_device(): lax.psum_scatter(partial_value, 'gx', scatter_dimension=0, tiled=True)]
    ppermute x0 -> x10, waiting for transfers between devices: none -> 46.5 us  [swap(): return lax.ppermute(value, 'gx', [(i, i ^ mask) for i in range(members)])]
    all_gather x1 -> x0, waiting for transfers between devices: 46.3 us -> none  [on_device(): gathered = lax.all_gather(tokens, 'gx', axis=0, tiled=True)]
    ppermute x0 -> x10, starting transfers between devices: none -> 15.1 us  [swap(): return lax.ppermute(value, 'gx', [(i, i ^ mask) for i in range(members)])]
    dot_general x1, matrix products: 3.92 us -> 1.1 us  [on_device(): gate = jnp.dot(gathered, gate_weight, preferred_element_type=jnp.float32)]
    add x0 -> x1, other arithmetic: none -> 1.82 us  [on_device(): total[:half]]
    slice x0 -> x3, local copies, waits for them, and re-layouts: none -> 1.78 us  [the longest x2 1.75 us: on_device(): total[half:].astype(jnp.bfloat16)]
  transfers between devices with their start and end apart: 2 -> 10, of which waited for: 2 -> 8; matrix products, arithmetic and copies ran while one was open for 0% -> 1% of each run, Pallas kernels for 0% -> 0%
where the time goes in v1:
time: 78.1 us; the launch traced here: 77.9 us
  waiting for transfers between devices  46.5 us (60%)
  starting transfers between devices  15.1 us (19%)
  matrix products  9.56 us (12%)
  local copies, waits for them, and re-layouts  3.72 us (5%)
  other arithmetic  2.95 us (4%)
    ppermute x10, waiting for transfers between devices, swap(): return lax.ppermute(value, 'gx', [(i, i ^ mask) for i in range(members)])  46.5 us
    ppermute x10, starting transfers between devices, swap(): return lax.ppermute(value, 'gx', [(i, i ^ mask) for i in range(members)])  15.1 us
    dot_general x1, matrix products, on_device(): total = jnp.dot(hidden, down_weight, preferred_element_type=jnp.float32)  8.02 us
    add x1, other arithmetic, on_device(): total[:half]  1.82 us
    unnamed x9, local copies, waits for them, and re-layouts  1.8 us
    slice x2, local copies, waits for them, and re-layouts, on_device(): total[half:].astype(jnp.bfloat16)  1.75 us
  transfers between devices with their start and end apart: 10, of which 8 were waited for; matrix products, arithmetic and copies ran while one was open for 1% of the time, Pallas kernels for 0%

profile of v1, /device:TPU:0, one launch (start us, length us, event | category | flops | bytes accessed | tf_op | source)
XLA Modules:
  0.0 77.9 jit_solution(10864535432908675194)
XLA Ops:
  0.0 3.0 %collective-permute-start = (bf16[8,8192]{1,0:T(8,128)(2,1)}, bf16[8,8192]{1,0:T(8,128)(2,1)S(1)}, u32[]{:S(2)}, u32[]{:S(2)}) collective-permute-start(bf16[8,8192]{1,0:T(8,128)(2,1)} %param.5), channel_id=1, source_target_pairs={{0,4},{1,5},{2,6},{3,7},{4,0},{5,1},{6,2},{7,3},{8,12},{9,13},{10,... | collective-permute-start | bytes 393224 | tf_op jit(solution)/shard_map/ppermute | solution.py:30
  3.0 2.6 %collective-permute-start.1 = (bf16[8,8192]{1,0:T(8,128)(2,1)}, bf16[8,8192]{1,0:T(8,128)(2,1)S(1)}, u32[]{:S(2)}, u32[]{:S(2)}) collective-permute-start(bf16[8,8192]{1,0:T(8,128)(2,1)} %param.5), channel_id=1, source_target_pairs={{0,8},{1,9},{2,10},{3,11},{4,12},{5,13},{6,14},{7,15},{8,0},{9,1},... | collective-permute-start | bytes 393224 | tf_op jit(solution)/shard_map/ppermute | solution.py:30
  5.6 0.0 collective-permute-start.2
  5.6 1.0 %constant_dynamic-update-slice_fusion.4 = (bf16[64,8192]{1,0:T(8,128)(2,1)S(1)}, bf16[128,8192]{1,0:T(8,128)(2,1)S(1)}) fusion(bf16[8,8192]{1,0:T(8,128)(2,1)} %param.5), kind=kLoop, calls=%fused_computation.44 | loop fusion | bytes 393216
  6.6 1.7 %collective-permute-done = bf16[8,8192]{1,0:T(8,128)(2,1)S(1)} collective-permute-done((bf16[8,8192]{1,0:T(8,128)(2,1)}, bf16[8,8192]{1,0:T(8,128)(2,1)S(1)}, u32[]{:S(2)}, u32[]{:S(2)}) %collective-permute-start) | collective-permute-done | bytes 131104 | tf_op jit(solution)/shard_map/ppermute | solution.py:30
  8.3 7.9 %collective-permute-done.1 = bf16[8,8192]{1,0:T(8,128)(2,1)S(1)} collective-permute-done((bf16[8,8192]{1,0:T(8,128)(2,1)}, bf16[8,8192]{1,0:T(8,128)(2,1)S(1)}, u32[]{:S(2)}, u32[]{:S(2)}) %collective-permute-start.1) | collective-permute-done | bytes 131104 | tf_op jit(solution)/shard_map/ppermute | solution.py:30
  16.2 0.0 collective-permute-done.2
  16.2 0.9 %pad_maximum_fusion = bf16[32,8192]{1,0:T(8,128)(2,1)S(1)} fusion(bf16[8,8192]{1,0:T(8,128)(2,1)S(1)} %collective-permute-done.2, bf16[8,8192]{1,0:T(8,128)(2,1)S(1)} %collective-permute-done.1, bf16[8,8192]{1,0:T(8,128)(2,1)S(1)} %collective-permute-done, bf16[8,8192]{1,0:T(8,128)(2,1)} %param.5), kind=kLoop, calls=%fused_computation.6 | loop fusion | flops 2097152 | bytes 1048576 | tf_op jit(solution)/shard_map/concatenate | solution.py:36
  17.1 1.6 %collective-permute-start.3 = (bf16[32,8192]{1,0:T(8,128)(2,1)S(1)}, bf16[32,8192]{1,0:T(8,128)(2,1)S(1)}, u32[]{:S(2)}, u32[]{:S(2)}) collective-permute-start(bf16[32,8192]{1,0:T(8,128)(2,1)S(1)} %pad_maximum_fusion), channel_id=1, source_target_pairs={{0,2},{1,3},{2,0},{3,1},{4,6},{5,7},{6,4},{7,5},{8,10},{9,11},{10,... | collective-permute-start | bytes 1572872 | tf_op jit(solution)/shard_map/ppermute | solution.py:30
  18.8 0.0 copy-start
  18.8 9.6 %collective-permute-done.3 = bf16[32,8192]{1,0:T(8,128)(2,1)S(1)} collective-permute-done((bf16[32,8192]{1,0:T(8,128)(2,1)S(1)}, bf16[32,8192]{1,0:T(8,128)(2,1)S(1)}, u32[]{:S(2)}, u32[]{:S(2)}) %collective-permute-start.3) | collective-permute-done | bytes 524320 | tf_op jit(solution)/shard_map/ppermute | solution.py:30
  28.4 0.1 constant_dynamic-update-slice_fusion
  28.5 0.1 collective-permute-start.4
  28.5 2.6 %collective-permute-done.4 = bf16[64,8192]{1,0:T(8,128)(2,1)S(1)} collective-permute-done((bf16[64,8192]{1,0:T(8,128)(2,1)S(1)}, bf16[64,8192]{1,0:T(8,128)(2,1)S(1)}, u32[]{:S(2)}, u32[]{:S(2)}) %collective-permute-start.4) | collective-permute-done | bytes 1048608 | tf_op jit(solution)/shard_map/ppermute | solution.py:30
  31.2 0.1 constant_dynamic-update-slice_fusion.5
  31.3 0.0 copy-done
  31.3 1.1 %fusion.42 = f32[128,224]{0,1:T(8,128)S(1)} fusion(bf16[128,8192]{1,0:T(8,128)(2,1)S(1)} %constant_dynamic-update-slice_fusion.5, bf16[8192,224]{0,1:T(8,128)(2,1)S(1)} %copy-done), kind=kOutput, calls=%fused_computation.65 | convolution fusion | flops 469762048 | bytes 5881856 | tf_op jit(solution)/shard_map/dot_general | solution.py:39
  32.4 8.0 %fusion.15 = f32[128,8192]{1,0:T(8,128)} fusion(bf16[224,8192]{1,0:T(8,128)(2,1)} %param.8, f32[128,224]{0,1:T(8,128)S(1)} %fusion.42, bf16[128,8192]{1,0:T(8,128)(2,1)S(1)} %constant_dynamic-update-slice_fusion.5, bf16[8192,224]{0,1:T(8,128)(2,1)} %param.7), kind=kOutput, calls=%fused_computation.27 | convolution fusion | flops 939696128 | bytes 13746176 | tf_op jit(solution)/shard_map/dot_general | solution.py:42
  40.4 1.7 %slice.56 = bf16[64,8192]{1,0:T(8,128)(2,1)S(1)} slice(f32[128,8192]{1,0:T(8,128)} %fusion.15), slice={[64:128], [0:8192]} | slice | bytes 2097152 | tf_op jit(solution)/shard_map/slice | solution.py:45
  42.1 0.2 collective-permute-start.5
  42.3 2.5 %collective-permute-done.5 = bf16[64,8192]{1,0:T(8,128)(2,1)S(1)} collective-permute-done((bf16[64,8192]{1,0:T(8,128)(2,1)S(1)}, bf16[64,8192]{1,0:T(8,128)(2,1)S(1)}, u32[]{:S(2)}, u32[]{:S(2)}) %collective-permute-start.5) | collective-permute-done | bytes 1048608 | tf_op jit(solution)/shard_map/ppermute | solution.py:30
  44.8 1.8 %slice_add_fusion = f32[64,8192]{1,0:T(8,128)S(1)} fusion(f32[128,8192]{1,0:T(8,128)} %fusion.15, bf16[64,8192]{1,0:T(8,128)(2,1)S(1)} %collective-permute-done.5), kind=kLoop, calls=%fused_computation.1 | loop fusion | flops 1048576 | bytes 5242880 | tf_op jit(solution)/shard_map/add | solution.py:45
  46.6 0.1 slice.57
  46.7 0.0 copy-start.1
  46.7 1.6 %collective-permute-start.6 = (bf16[32,8192]{1,0:T(8,128)(2,1)S(1)}, bf16[32,8192]{1,0:T(8,128)(2,1)S(1)}, u32[]{:S(2)}, u32[]{:S(2)}) collective-permute-start(bf16[32,8192]{1,0:T(8,128)(2,1)S(1)} %slice.57), channel_id=1, source_target_pairs={{0,2},{1,3},{2,0},{3,1},{4,6},{5,7},{6,4},{7,5},{8,10},{9,11},{10,... | collective-permute-start | bytes 1572872 | tf_op jit(solution)/shard_map/ppermute | solution.py:30
  48.3 12.4 %collective-permute-done.6 = bf16[32,8192]{1,0:T(8,128)(2,1)S(1)} collective-permute-done((bf16[32,8192]{1,0:T(8,128)(2,1)S(1)}, bf16[32,8192]{1,0:T(8,128)(2,1)S(1)}, u32[]{:S(2)}, u32[]{:S(2)}) %collective-permute-start.6) | collective-permute-done | bytes 524320 | tf_op jit(solution)/shard_map/ppermute | solution.py:30
  60.8 0.1 fusion.38
  60.9 3.1 %collective-permute-start.7 = (bf16[8,8192]{1,0:T(8,128)(2,1)S(1)}, bf16[8,8192]{1,0:T(8,128)(2,1)S(1)}, u32[]{:S(2)}, u32[]{:S(2)}) collective-permute-start(bf16[8,8192]{1,0:T(8,128)(2,1)S(1)} %get-tuple-element.7), channel_id=1, source_target_pairs={{0,4},{1,5},{2,6},{3,7},{4,0},{5,1},{6,2},{7,3},{8,12},{9,13},{10,... | collective-permute-start | bytes 393224 | tf_op jit(solution)/shard_map/ppermute | solution.py:30
  64.0 1.5 %collective-permute-start.8 = (bf16[8,8192]{1,0:T(8,128)(2,1)S(1)}, bf16[8,8192]{1,0:T(8,128)(2,1)S(1)}, u32[]{:S(2)}, u32[]{:S(2)}) collective-permute-start(bf16[8,8192]{1,0:T(8,128)(2,1)S(1)} %get-tuple-element.9), channel_id=1, source_target_pairs={{0,8},{1,9},{2,10},{3,11},{4,12},{5,13},{6,14},{7,15},{8,0},{9,1},... | collective-permute-start | bytes 393224 | tf_op jit(solution)/shard_map/ppermute | solution.py:30
  65.5 1.4 %collective-permute-start.9 = (bf16[8,8192]{1,0:T(8,128)(2,1)S(1)}, bf16[8,8192]{1,0:T(8,128)(2,1)S(1)}, u32[]{:S(2)}, u32[]{:S(2)}) collective-permute-start(bf16[8,8192]{1,0:T(8,128)(2,1)S(1)} %get-tuple-element.8), channel_id=1, source_target_pairs={{0,12},{1,13},{2,14},{3,15},{4,8},{5,9},{6,10},{7,11},{8,4},{9,5},... | collective-permute-start | bytes 393224 | tf_op jit(solution)/shard_map/ppermute | solution.py:30
  66.9 0.0 copy-done.1
  66.9 1.4 %collective-permute-done.7 = bf16[8,8192]{1,0:T(8,128)(2,1)S(1)} collective-permute-done((bf16[8,8192]{1,0:T(8,128)(2,1)S(1)}, bf16[8,8192]{1,0:T(8,128)(2,1)S(1)}, u32[]{:S(2)}, u32[]{:S(2)}) %collective-permute-start.7) | collective-permute-done | bytes 131104 | tf_op jit(solution)/shard_map/ppermute | solution.py:30
  68.4 8.3 %collective-permute-done.8 = bf16[8,8192]{1,0:T(8,128)(2,1)S(1)} collective-permute-done((bf16[8,8192]{1,0:T(8,128)(2,1)S(1)}, bf16[8,8192]{1,0:T(8,128)(2,1)S(1)}, u32[]{:S(2)}, u32[]{:S(2)}) %collective-permute-start.8) | collective-permute-done | bytes 131104 | tf_op jit(solution)/shard_map/ppermute | solution.py:30
  76.6 0.0 collective-permute-done.9
  76.6 0.1 fusion.3
  76.7 0.4 fusion
  77.1 0.7 copy.11
  (5 shorter events, 0.1 us)
Async XLA Ops:
  0.0 8.3 %collective-permute-start = (bf16[8,8192]{1,0:T(8,128)(2,1)}, bf16[8,8192]{1,0:T(8,128)(2,1)S(1)}, u32[]{:S(2)}, u32[]{:S(2)}) collective-permute-start(bf16[8,8192]{1,0:T(8,128)(2,1)} %param.5), channel_id=1, source_target_pairs={{0,4},{1,5},{2,6},{3,7},{4,0},{5,1},{6,2},{7,3},{8,12},{9,13},{10,... | collective-permute-start | bytes 393224 | tf_op jit(solution)/shard_map/ppermute | solution.py:30
  3.0 13.2 %collective-permute-start.1 = (bf16[8,8192]{1,0:T(8,128)(2,1)}, bf16[8,8192]{1,0:T(8,128)(2,1)S(1)}, u32[]{:S(2)}, u32[]{:S(2)}) collective-permute-start(bf16[8,8192]{1,0:T(8,128)(2,1)} %param.5), channel_id=1, source_target_pairs={{0,8},{1,9},{2,10},{3,11},{4,12},{5,13},{6,14},{7,15},{8,0},{9,1},... | collective-permute-start | bytes 393224 | tf_op jit(solution)/shard_map/ppermute | solution.py:30
  5.6 10.6 %collective-permute-start.2 = (bf16[8,8192]{1,0:T(8,128)(2,1)}, bf16[8,8192]{1,0:T(8,128)(2,1)S(1)}, u32[]{:S(2)}, u32[]{:S(2)}) collective-permute-start(bf16[8,8192]{1,0:T(8,128)(2,1)} %param.5), channel_id=1, source_target_pairs={{0,12},{1,13},{2,14},{3,15},{4,8},{5,9},{6,10},{7,11},{8,4},{9,5},... | collective-permute-start | bytes 393224 | tf_op jit(solution)/shard_map/ppermute | solution.py:30
  17.1 11.3 %collective-permute-start.3 = (bf16[32,8192]{1,0:T(8,128)(2,1)S(1)}, bf16[32,8192]{1,0:T(8,128)(2,1)S(1)}, u32[]{:S(2)}, u32[]{:S(2)}) collective-permute-start(bf16[32,8192]{1,0:T(8,128)(2,1)S(1)} %pad_maximum_fusion), channel_id=1, source_target_pairs={{0,2},{1,3},{2,0},{3,1},{4,6},{5,7},{6,4},{7,5},{8,10},{9,11},{10,... | collective-permute-start | bytes 1572872 | tf_op jit(solution)/shard_map/ppermute | solution.py:30
  18.8 12.5 %copy-start = (bf16[8192,224]{0,1:T(8,128)(2,1)S(1)}, bf16[8192,224]{0,1:T(8,128)(2,1)}, u32[]{:S(2)}) copy-start(bf16[8192,224]{0,1:T(8,128)(2,1)} %param.6) | copy-start | bytes 11010052
  28.5 2.7 %collective-permute-start.4 = (bf16[64,8192]{1,0:T(8,128)(2,1)S(1)}, bf16[64,8192]{1,0:T(8,128)(2,1)S(1)}, u32[]{:S(2)}, u32[]{:S(2)}) collective-permute-start(bf16[64,8192]{1,0:T(8,128)(2,1)S(1)} %get-tuple-element.10), channel_id=1, source_target_pairs={{0,1},{1,0},{2,3},{3,2},{4,5},{5,4},{6,7},{7,6},{8,9},{9,8},{10,11... | collective-permute-start | bytes 3145736 | tf_op jit(solution)/shard_map/ppermute | solution.py:30
  42.1 2.7 %collective-permute-start.5 = (bf16[64,8192]{1,0:T(8,128)(2,1)S(1)}, bf16[64,8192]{1,0:T(8,128)(2,1)S(1)}, u32[]{:S(2)}, u32[]{:S(2)}) collective-permute-start(bf16[64,8192]{1,0:T(8,128)(2,1)S(1)} %slice.56), channel_id=1, source_target_pairs={{0,1},{1,0},{2,3},{3,2},{4,5},{5,4},{6,7},{7,6},{8,9},{9,8},{10,11... | collective-permute-start | bytes 3145736 | tf_op jit(solution)/shard_map/ppermute | solution.py:30
  46.7 20.2 %copy-start.1 = (s32[8192]{0:T(1024)S(1)}, s32[8192]{0:T(1024)}, u32[]{:S(2)}) copy-start(s32[8192]{0:T(1024)} %param.9) | copy-start | bytes 98308
  46.7 14.0 %collective-permute-start.6 = (bf16[32,8192]{1,0:T(8,128)(2,1)S(1)}, bf16[32,8192]{1,0:T(8,128)(2,1)S(1)}, u32[]{:S(2)}, u32[]{:S(2)}) collective-permute-start(bf16[32,8192]{1,0:T(8,128)(2,1)S(1)} %slice.57), channel_id=1, source_target_pairs={{0,2},{1,3},{2,0},{3,1},{4,6},{5,7},{6,4},{7,5},{8,10},{9,11},{10,... | collective-permute-start | bytes 1572872 | tf_op jit(solution)/shard_map/ppermute | solution.py:30
  60.9 7.4 %collective-permute-start.7 = (bf16[8,8192]{1,0:T(8,128)(2,1)S(1)}, bf16[8,8192]{1,0:T(8,128)(2,1)S(1)}, u32[]{:S(2)}, u32[]{:S(2)}) collective-permute-start(bf16[8,8192]{1,0:T(8,128)(2,1)S(1)} %get-tuple-element.7), channel_id=1, source_target_pairs={{0,4},{1,5},{2,6},{3,7},{4,0},{5,1},{6,2},{7,3},{8,12},{9,13},{10,... | collective-permute-start | bytes 393224 | tf_op jit(solution)/shard_map/ppermute | solution.py:30
  64.0 12.6 %collective-permute-start.8 = (bf16[8,8192]{1,0:T(8,128)(2,1)S(1)}, bf16[8,8192]{1,0:T(8,128)(2,1)S(1)}, u32[]{:S(2)}, u32[]{:S(2)}) collective-permute-start(bf16[8,8192]{1,0:T(8,128)(2,1)S(1)} %get-tuple-element.9), channel_id=1, source_target_pairs={{0,8},{1,9},{2,10},{3,11},{4,12},{5,13},{6,14},{7,15},{8,0},{9,1},... | collective-permute-start | bytes 393224 | tf_op jit(solution)/shard_map/ppermute | solution.py:30
  65.5 11.1 %collective-permute-start.9 = (bf16[8,8192]{1,0:T(8,128)(2,1)S(1)}, bf16[8,8192]{1,0:T(8,128)(2,1)S(1)}, u32[]{:S(2)}, u32[]{:S(2)}) collective-permute-start(bf16[8,8192]{1,0:T(8,128)(2,1)S(1)} %get-tuple-element.8), channel_id=1, source_target_pairs={{0,12},{1,13},{2,14},{3,15},{4,8},{5,9},{6,10},{7,11},{8,4},{9,5},... | collective-permute-start | bytes 393224 | tf_op jit(solution)/shard_map/ppermute | solution.py:30

commit v2 on v1

--- a/solution.py
+++ b/solution.py
@@ -29,11 +29,17 @@
     def swap(value, mask):
         return lax.ppermute(value, "gx", [(i, i ^ mask) for i in range(members)])
 
+    lines = [list(range(first, members, 4)) for first in range(4)]
+
+    def along_z(value):
+        return lax.all_to_all(value, "gx", 0, 0, axis_index_groups=lines)
+
     def on_device(tokens, gate_weight, up_weight, down_weight, sign_pattern):
         rows, features = tokens.shape
         rotation = hadamard_table(128)
         sign_blocks = sign_pattern.astype(jnp.float32).reshape(features // 128, 128)
-        column = jnp.concatenate([tokens] + [swap(tokens, m) for m in range(4, members, 4)])
+        column = jnp.broadcast_to(tokens[None], (members // 4, rows, features))
+        column = along_z(column).reshape(members // 4 * rows, features)
         plane = jnp.concatenate([column, swap(column, 2)])
         gathered = jnp.concatenate([plane, swap(plane, 1)])
         gate = jnp.dot(gathered, gate_weight, preferred_element_type=jnp.float32)
@@ -43,13 +49,8 @@
         for mask in (1, 2):
             half = total.shape[0] // 2
             total = total[:half] + swap(total[half:].astype(jnp.bfloat16), mask).astype(jnp.float32)
-        arrived = [
-            swap(total[m // 4 * rows : (m // 4 + 1) * rows].astype(jnp.bfloat16), m)
-            for m in range(4, members, 4)
-        ]
-        summed = total[:rows]
-        for block in arrived:
-            summed = summed + block.astype(jnp.float32)
+        arrived = along_z(total.astype(jnp.bfloat16).reshape(members // 4, rows, features))
+        summed = jnp.sum(arrived.astype(jnp.float32), axis=0)
         return rotate_rows(summed, sign_blocks, rotation).astype(jnp.bfloat16)
 
     placed = (P(("groups", "gx"), None), P(None, "gx"), P(None, "gx"), P("gx", None), P())

time: 78.1 us -> 86.8 us (1.11)
  blocking collectives: 0 us -> 20.7 us
  starting transfers between devices: 15.1 us -> 6.84 us
  waiting for transfers between devices: 46.5 us -> 42.8 us
    all_to_all x0 -> x1, blocking collectives: none -> 20.7 us  [along_z(): return lax.all_to_all(value, 'gx', 0, 0, axis_index_groups=lines)]
    ppermute x10 -> x4, waiting for transfers between devices: 46.5 us -> 28.6 us  [swap(): return lax.ppermute(value, 'gx', [(i, i ^ mask) for i in range(members)])]
    all_to_all x0 -> x1, waiting for transfers between devices: none -> 14.2 us  [along_z(): return lax.all_to_all(value, 'gx', 0, 0, axis_index_groups=lines)]
    ppermute x10 -> x4, starting transfers between devices: 15.1 us -> 3.37 us  [swap(): return lax.ppermute(value, 'gx', [(i, i ^ mask) for i in range(members)])]
    all_to_all x0 -> x1, starting transfers between devices: none -> 3.47 us  [along_z(): return lax.all_to_all(value, 'gx', 0, 0, axis_index_groups=lines)]
    broadcast_in_dim x0 -> x1, local copies, waits for them, and re-layouts: none -> 1.09 us  [on_device(): column = jnp.broadcast_to(tokens[None], (members // 4, rows, features))]
    unnamed x9 -> x5, local copies, waits for them, and re-layouts: 1.8 us -> 0.75 us
    concatenate x1, other arithmetic: 0.94 us -> 0.07 us  [on_device(): plane = jnp.concatenate([column, swap(column, 2)])]
  transfers between devices with their start and end apart: 10 -> 5, of which waited for: 8 -> 5; matrix products, arithmetic and copies ran while one was open for 1% -> 0% of each run, Pallas kernels for 0% -> 0%
where the time goes in v2:
time: 86.8 us; the launch traced here: 86.6 us
  waiting for transfers between devices  42.8 us (49%)
  blocking collectives  20.7 us (24%)
  matrix products  9.62 us (11%)
  starting transfers between devices  6.84 us (8%)
  local copies, waits for them, and re-layouts  3.59 us (4%)
  other arithmetic  2.87 us (3%)
    ppermute x4, waiting for transfers between devices, swap(): return lax.ppermute(value, 'gx', [(i, i ^ mask) for i in range(members)])  28.6 us
    all_to_all x1, blocking collectives, along_z(): return lax.all_to_all(value, 'gx', 0, 0, axis_index_groups=lines)  20.7 us
    all_to_all x1, waiting for transfers between devices, along_z(): return lax.all_to_all(value, 'gx', 0, 0, axis_index_groups=lines)  14.2 us
    dot_general x1, matrix products, on_device(): total = jnp.dot(hidden, down_weight, preferred_element_type=jnp.float32)  8.01 us
    all_to_all x1, starting transfers between devices, along_z(): return lax.all_to_all(value, 'gx', 0, 0, axis_index_groups=lines)  3.47 us
    ppermute x4, starting transfers between devices, swap(): return lax.ppermute(value, 'gx', [(i, i ^ mask) for i in range(members)])  3.37 us
    add x1, other arithmetic, on_device(): total[:half]  1.82 us
    slice x2, local copies, waits for them, and re-layouts, on_device(): total[half:].astype(jnp.bfloat16)  1.75 us
  transfers between devices with their start and end apart: 5, of which 5 were waited for; matrix products, arithmetic and copies ran while one was open for 0% of the time, Pallas kernels for 0%

profile of v2, /device:TPU:0, one launch (start us, length us, event | category | flops | bytes accessed | tf_op | source)
XLA Modules:
  0.0 86.6 jit_solution(6769085094580687750)
XLA Ops:
  0.0 0.0 copy-start.1
  0.0 1.1 %broadcast_in_dim.2 = bf16[4,8,8192]{2,1,0:T(8,128)(2,1)S(1)} broadcast(bf16[8,8192]{1,0:T(8,128)(2,1)} %param.5), dimensions={1,2} | broadcast | bytes 655360 | tf_op jit(solution)/shard_map/broadcast_in_dim | solution.py:41
  1.1 20.7 %all_to_all.10 = bf16[4,8,8192]{2,1,0:T(8,128)(2,1)S(1)} all-to-all(bf16[4,8,8192]{2,1,0:T(8,128)(2,1)S(1)} %broadcast_in_dim.2), channel_id=1, replica_groups={{0,4,8,12},{1,5,9,13},{2,6,10,14},{3,7,11,15},{16,20,24,28},{17,21,25,2..., dimensions={0} | all-to-all | bytes 1048576 | tf_op jit(solution)/shard_map/all_to_all | solution.py:35
  21.8 1.5 %collective-permute-start = (bf16[32,8192]{1,0:T(8,128)(2,1)S(1)}, bf16[32,8192]{1,0:T(8,128)(2,1)S(1)}, u32[]{:S(2)}, u32[]{:S(2)}) collective-permute-start(bf16[32,8192]{1,0:T(8,128)(2,1)S(1)} %bitcast.20), channel_id=1, source_target_pairs={{0,2},{1,3},{2,0},{3,1},{4,6},{5,7},{6,4},{7,5},{8,10},{9,11},{10,... | collective-permute-start | bytes 1572872 | tf_op jit(solution)/shard_map/ppermute | solution.py:30
  23.4 11.0 %collective-permute-done = bf16[32,8192]{1,0:T(8,128)(2,1)S(1)} collective-permute-done((bf16[32,8192]{1,0:T(8,128)(2,1)S(1)}, bf16[32,8192]{1,0:T(8,128)(2,1)S(1)}, u32[]{:S(2)}, u32[]{:S(2)}) %collective-permute-start) | collective-permute-done | bytes 524320 | tf_op jit(solution)/shard_map/ppermute | solution.py:30
  34.4 0.1 pad_maximum_fusion.1
  34.4 0.1 collective-permute-start.1
  34.5 2.6 %collective-permute-done.1 = bf16[64,8192]{1,0:T(8,128)(2,1)S(1)} collective-permute-done((bf16[64,8192]{1,0:T(8,128)(2,1)S(1)}, bf16[64,8192]{1,0:T(8,128)(2,1)S(1)}, u32[]{:S(2)}, u32[]{:S(2)}) %collective-permute-start.1) | collective-permute-done | bytes 1048608 | tf_op jit(solution)/shard_map/ppermute | solution.py:30
  37.2 0.0 copy-done.1
  37.2 1.2 %fusion.2 = f32[128,224]{0,1:T(8,128)S(1)} fusion(bf16[8192,224]{0,1:T(8,128)(2,1)S(1)} %copy-done.1, bf16[64,8192]{1,0:T(8,128)(2,1)S(1)} %collective-permute-done.1, bf16[32,8192]{1,0:T(8,128)(2,1)S(1)} %collective-permute-done, bf16[32,8192]{1,0:T(8,128)(2,1)S(1)} %bitcast.22), kind=kOutput, calls=%fused_computation.10 | convolution fusion | flops 476053504 | bytes 5881856 | tf_op jit(solution)/shard_map/dot_general | solution.py:46
  38.3 8.0 %fusion.17 = f32[128,8192]{1,0:T(8,128)} fusion(bf16[224,8192]{1,0:T(8,128)(2,1)} %param.8, f32[128,224]{0,1:T(8,128)S(1)} %fusion.2, bf16[8192,224]{0,1:T(8,128)(2,1)} %param.6, bf16[64,8192]{1,0:T(8,128)(2,1)S(1)} %collective-permute-done.1, bf16[32,8192]{1,0:T(8,128)(2,1)S(1)} %collective-permute-done, bf16[32,8192]{1,0:T(8,128)(2,1)S(1)} %bitcast.23), kind=kOutput, calls=%fused_computation.30 | convolution fusion | flops 945987584 | bytes 13746176 | tf_op jit(solution)/shard_map/dot_general | solution.py:48
  46.4 1.7 %slice.30 = bf16[64,8192]{1,0:T(8,128)(2,1)S(1)} slice(f32[128,8192]{1,0:T(8,128)} %fusion.17), slice={[64:128], [0:8192]} | slice | bytes 2097152 | tf_op jit(solution)/shard_map/slice | solution.py:51
  48.1 0.0 copy-start
  48.1 0.2 collective-permute-start.2
  48.3 2.5 %collective-permute-done.2 = bf16[64,8192]{1,0:T(8,128)(2,1)S(1)} collective-permute-done((bf16[64,8192]{1,0:T(8,128)(2,1)S(1)}, bf16[64,8192]{1,0:T(8,128)(2,1)S(1)}, u32[]{:S(2)}, u32[]{:S(2)}) %collective-permute-start.2) | collective-permute-done | bytes 1048608 | tf_op jit(solution)/shard_map/ppermute | solution.py:30
  50.8 1.8 %slice_add_fusion = f32[64,8192]{1,0:T(8,128)S(1)} fusion(f32[128,8192]{1,0:T(8,128)} %fusion.17, bf16[64,8192]{1,0:T(8,128)(2,1)S(1)} %collective-permute-done.2), kind=kLoop, calls=%fused_computation.1 | loop fusion | flops 1048576 | bytes 5242880 | tf_op jit(solution)/shard_map/add | solution.py:51
  52.6 0.1 slice.31
  52.7 1.6 %collective-permute-start.3 = (bf16[32,8192]{1,0:T(8,128)(2,1)S(1)}, bf16[32,8192]{1,0:T(8,128)(2,1)S(1)}, u32[]{:S(2)}, u32[]{:S(2)}) collective-permute-start(bf16[32,8192]{1,0:T(8,128)(2,1)S(1)} %slice.31), channel_id=1, source_target_pairs={{0,2},{1,3},{2,0},{3,1},{4,6},{5,7},{6,4},{7,5},{8,10},{9,11},{10,... | collective-permute-start | bytes 1572872 | tf_op jit(solution)/shard_map/ppermute | solution.py:30
  54.3 12.4 %collective-permute-done.3 = bf16[32,8192]{1,0:T(8,128)(2,1)S(1)} collective-permute-done((bf16[32,8192]{1,0:T(8,128)(2,1)S(1)}, bf16[32,8192]{1,0:T(8,128)(2,1)S(1)}, u32[]{:S(2)}, u32[]{:S(2)}) %collective-permute-start.3) | collective-permute-done | bytes 524320 | tf_op jit(solution)/shard_map/ppermute | solution.py:30
  66.7 0.9 %fusion.4 = bf16[4,8,8192]{2,1,0:T(8,128)(2,1)} fusion(bf16[32,8192]{1,0:T(8,128)(2,1)S(1)} %collective-permute-done.3, f32[64,8192]{1,0:T(8,128)S(1)} %slice_add_fusion), kind=kLoop, calls=%fused_computation.12 | loop fusion | flops 786432 | bytes 2097152 | tf_op jit(solution)/shard_map/reshape | solution.py:52
  67.6 3.5 %all-to-all-start.1 = ((bf16[4,8,8192]{2,1,0:T(8,128)(2,1)}), bf16[4,8,8192]{2,1,0:T(8,128)(2,1)S(1)}, u32[]{:S(2)}, u32[]{:S(2)}) async-start(bf16[4,8,8192]{2,1,0:T(8,128)(2,1)} %fusion.4), calls=%async_computation.1 | async-start | bytes 1048576 | tf_op jit(solution)/shard_map/all_to_all | solution.py:35
  71.1 0.0 copy-done
  71.1 14.2 %all-to-all-done.1 = bf16[4,8,8192]{2,1,0:T(8,128)(2,1)S(1)} async-done(((bf16[4,8,8192]{2,1,0:T(8,128)(2,1)}), bf16[4,8,8192]{2,1,0:T(8,128)(2,1)S(1)}, u32[]{:S(2)}, u32[]{:S(2)}) %all-to-all-start.1) | async-done | bytes 524320 | tf_op jit(solution)/shard_map/all_to_all | solution.py:35
  85.3 0.1 convert_reduce_fusion
  85.4 0.4 fusion
  85.8 0.7 copy.13
  (1 shorter events, 0.0 us)
Async XLA Ops:
  0.0 37.2 %copy-start.1 = (bf16[8192,224]{0,1:T(8,128)(2,1)S(1)}, bf16[8192,224]{0,1:T(8,128)(2,1)}, u32[]{:S(2)}) copy-start(bf16[8192,224]{0,1:T(8,128)(2,1)} %param.7) | copy-start | bytes 11010052
  21.8 12.5 %collective-permute-start = (bf16[32,8192]{1,0:T(8,128)(2,1)S(1)}, bf16[32,8192]{1,0:T(8,128)(2,1)S(1)}, u32[]{:S(2)}, u32[]{:S(2)}) collective-permute-start(bf16[32,8192]{1,0:T(8,128)(2,1)S(1)} %bitcast.20), channel_id=1, source_target_pairs={{0,2},{1,3},{2,0},{3,1},{4,6},{5,7},{6,4},{7,5},{8,10},{9,11},{10,... | collective-permute-start | bytes 1572872 | tf_op jit(solution)/shard_map/ppermute | solution.py:30
  34.4 2.7 %collective-permute-start.1 = (bf16[64,8192]{1,0:T(8,128)(2,1)S(1)}, bf16[64,8192]{1,0:T(8,128)(2,1)S(1)}, u32[]{:S(2)}, u32[]{:S(2)}) collective-permute-start(bf16[64,8192]{1,0:T(8,128)(2,1)S(1)} %pad_maximum_fusion.1), channel_id=1, source_target_pairs={{0,1},{1,0},{2,3},{3,2},{4,5},{5,4},{6,7},{7,6},{8,9},{9,8},{10,11... | collective-permute-start | bytes 3145736 | tf_op jit(solution)/shard_map/ppermute | solution.py:30
  48.1 23.0 %copy-start = (s32[8192]{0:T(1024)S(1)}, s32[8192]{0:T(1024)}, u32[]{:S(2)}) copy-start(s32[8192]{0:T(1024)} %param.9) | copy-start | bytes 98308
  48.1 2.7 %collective-permute-start.2 = (bf16[64,8192]{1,0:T(8,128)(2,1)S(1)}, bf16[64,8192]{1,0:T(8,128)(2,1)S(1)}, u32[]{:S(2)}, u32[]{:S(2)}) collective-permute-start(bf16[64,8192]{1,0:T(8,128)(2,1)S(1)} %slice.30), channel_id=1, source_target_pairs={{0,1},{1,0},{2,3},{3,2},{4,5},{5,4},{6,7},{7,6},{8,9},{9,8},{10,11... | collective-permute-start | bytes 3145736 | tf_op jit(solution)/shard_map/ppermute | solution.py:30
  52.7 14.0 %collective-permute-start.3 = (bf16[32,8192]{1,0:T(8,128)(2,1)S(1)}, bf16[32,8192]{1,0:T(8,128)(2,1)S(1)}, u32[]{:S(2)}, u32[]{:S(2)}) collective-permute-start(bf16[32,8192]{1,0:T(8,128)(2,1)S(1)} %slice.31), channel_id=1, source_target_pairs={{0,2},{1,3},{2,0},{3,1},{4,6},{5,7},{6,4},{7,5},{8,10},{9,11},{10,... | collective-permute-start | bytes 1572872 | tf_op jit(solution)/shard_map/ppermute | solution.py:30
  67.6 17.7 %all-to-all-start.1 = ((bf16[4,8,8192]{2,1,0:T(8,128)(2,1)}), bf16[4,8,8192]{2,1,0:T(8,128)(2,1)S(1)}, u32[]{:S(2)}, u32[]{:S(2)}) async-start(bf16[4,8,8192]{2,1,0:T(8,128)(2,1)} %fusion.4), calls=%async_computation.1 | async-start | bytes 1048576 | tf_op jit(solution)/shard_map/all_to_all | solution.py:35

commit v3 on v2

v3 whole, which is shorter than its diff:
```python
import jax
import jax.numpy as jnp
from jax import lax
from jax.sharding import PartitionSpec as P


def hadamard_table(order):
    row_index = jnp.arange(order, dtype=jnp.int32)[:, None]
    col_index = jnp.arange(order, dtype=jnp.int32)[None, :]
    common = jnp.bitwise_and(row_index, col_index)
    parity = jnp.zeros((order, order), jnp.int32)
    for shift_bit in range(order.bit_length() - 1):
        parity = parity + jnp.bitwise_and(jnp.right_shift(common, shift_bit), 1)
    values = 1.0 - 2.0 * jnp.remainder(parity, 2).astype(jnp.float32)
    return values / jnp.sqrt(jnp.float32(order))


def rotate_rows(values, sign_blocks, rotation):
    count, features = values.shape
    blocks = values.reshape(count, features // 128, 128) * sign_blocks
    rotated = jnp.einsum("rbk,kl->rbl", blocks, rotation, precision=lax.Precision.HIGHEST)
    return rotated.reshape(count, features)


def solution(mesh):
    members = mesh.shape["gx"]
    assert members & (members - 1) == 0 and members >= 8

    steps = []
    mask = members // 2
    while mask > 4:
        steps.append((mask, mask))
        mask //= 2
    steps += [(4, 2), (2, 4), (1, 1)]

    def swap(value, masks):
        return lax.ppermute(value, "gx", [(i, i ^ masks[i % 2]) for i in range(members)])

    def on_device(tokens, gate_weight, up_weight, down_weight, sign_pattern):
        rows, features = tokens.shape
        rotation = hadamard_table(128)
        sign_blocks = sign_pattern.astype(jnp.float32).reshape(features // 128, 128)
        gathered = tokens
        for masks in steps:
            gathered = jnp.concatenate([gathered, swap(gathered, masks)])
        gate = jnp.dot(gathered, gate_weight, preferred_element_type=jnp.float32)
        up = jnp.dot(gathered, up_weight, preferred_element_type=jnp.float32)
        hidden = (jax.nn.silu(gate) * up).astype(jnp.bfloat16)
        total = jnp.dot(hidden, down_weight, preferred_element_type=jnp.float32)
        for masks in reversed(steps):
            half = total.shape[0] // 2
            total = total[:half] + swap(total[half:].astype(jnp.bfloat16), masks).astype(jnp.float32)
        return rotate_rows(total, sign_blocks, rotation).astype(jnp.bfloat16)

    placed = (P(("groups", "gx"), None), P(None, "gx"), P(None, "gx"), P("gx", None), P())
    return jax.shard_map(
        on_device, mesh=mesh, in_specs=placed, out_specs=P(("groups", "gx"), None), check_vma=False
    )
```

time: 86.8 us -> 71.5 us (0.82)
  blocking collectives: 20.7 us -> 0 us
  starting transfers between devices: 6.84 us -> 11.2 us
  other arithmetic: 2.87 us -> 3.97 us
    all_to_all x1 -> x0, blocking collectives: 20.7 us -> none  [along_z(): return lax.all_to_all(value, 'gx', 0, 0, axis_index_groups=lines)]
    ppermute x4 -> x8, waiting for transfers between devices: 28.6 us -> 42.8 us  [swap(): lax.ppermute(value, 'gx', [(i, i ^ masks[i % 2]) for i in range(members)])]
    all_to_all x1 -> x0, waiting for transfers between devices: 14.2 us -> none  [along_z(): return lax.all_to_all(value, 'gx', 0, 0, axis_index_groups=lines)]
    ppermute x4 -> x8, starting transfers between devices: 3.37 us -> 11.2 us  [swap(): lax.ppermute(value, 'gx', [(i, i ^ masks[i % 2]) for i in range(members)])]
    all_to_all x1 -> x0, starting transfers between devices: 3.47 us -> none  [along_z(): return lax.all_to_all(value, 'gx', 0, 0, axis_index_groups=lines)]
    concatenate x1 -> x3, other arithmetic: 0.07 us -> 1.93 us  [on_device(): gathered = jnp.concatenate([gathered, swap(gathered, masks)])]
    broadcast_in_dim x1 -> x0, local copies, waits for them, and re-layouts: 1.09 us -> none  [on_device(): column = jnp.broadcast_to(tokens[None], (members // 4, rows, features))]
    unnamed x5 -> x11, local copies, waits for them, and re-layouts: 0.75 us -> 1.74 us
  transfers between devices with their start and end apart: 5 -> 8, of which waited for: 5 -> 8; matrix products, arithmetic and copies ran while one was open for 0% -> 1% of each run, Pallas kernels for 0% -> 0%
where the time goes in v3:
time: 71.5 us; the launch traced here: 71.3 us
  waiting for transfers between devices  42.8 us (60%)
  starting transfers between devices  11.2 us (16%)
  matrix products  9.55 us (13%)
  other arithmetic  3.97 us (6%)
  local copies, waits for them, and re-layouts  3.6 us (5%)
    ppermute x8, waiting for transfers between devices, swap(): lax.ppermute(value, 'gx', [(i, i ^ masks[i % 2]) for i in range(members)])  42.8 us
    ppermute x8, starting transfers between devices, swap(): lax.ppermute(value, 'gx', [(i, i ^ masks[i % 2]) for i in range(members)])  11.2 us
    dot_general x1, matrix products, on_device(): total = jnp.dot(hidden, down_weight, preferred_element_type=jnp.float32)  8.01 us
    add x3, other arithmetic, on_device(): total[:half]  2.01 us
    concatenate x3, other arithmetic, on_device(): gathered = jnp.concatenate([gathered, swap(gathered, masks)])  1.93 us
    slice x4, local copies, waits for them, and re-layouts, on_device(): total[half:].astype(jnp.bfloat16)  1.79 us
    unnamed x11, local copies, waits for them, and re-layouts  1.74 us
  transfers between devices with their start and end apart: 8, of which 8 were waited for; matrix products, arithmetic and copies ran while one was open for 1% of the time, Pallas kernels for 0%

profile of v3, /device:TPU:0, one launch (start us, length us, event | category | flops | bytes accessed | tf_op | source)
XLA Modules:
  0.0 71.3 jit_solution(15607656419110384800)
XLA Ops:
  0.0 0.0 copy-start.1
  0.0 4.0 %collective-permute-start = (bf16[8,8192]{1,0:T(8,128)(2,1)}, bf16[8,8192]{1,0:T(8,128)(2,1)S(1)}, u32[]{:S(2)}, u32[]{:S(2)}) collective-permute-start(bf16[8,8192]{1,0:T(8,128)(2,1)} %param.5), channel_id=1, source_target_pairs={{0,8},{1,9},{2,10},{3,11},{4,12},{5,13},{6,14},{7,15},{8,0},{9,1},... | collective-permute-start | bytes 393224 | tf_op jit(solution)/shard_map/ppermute | solution.py:37
  4.0 6.6 %collective-permute-done = bf16[8,8192]{1,0:T(8,128)(2,1)S(1)} collective-permute-done((bf16[8,8192]{1,0:T(8,128)(2,1)}, bf16[8,8192]{1,0:T(8,128)(2,1)S(1)}, u32[]{:S(2)}, u32[]{:S(2)}) %collective-permute-start) | collective-permute-done | bytes 131104 | tf_op jit(solution)/shard_map/ppermute | solution.py:37
  10.6 0.9 %pad_maximum_fusion.2 = bf16[16,8192]{1,0:T(8,128)(2,1)S(1)} fusion(bf16[8,8192]{1,0:T(8,128)(2,1)S(1)} %collective-permute-done, bf16[8,8192]{1,0:T(8,128)(2,1)} %param.5), kind=kLoop, calls=%fused_computation.13 | loop fusion | flops 524288 | bytes 524288 | tf_op jit(solution)/shard_map/concatenate | solution.py:45
  11.5 0.8 %collective-permute-start.1 = (bf16[16,8192]{1,0:T(8,128)(2,1)S(1)}, bf16[16,8192]{1,0:T(8,128)(2,1)S(1)}, u32[]{:S(2)}, u32[]{:S(2)}) collective-permute-start(bf16[16,8192]{1,0:T(8,128)(2,1)S(1)} %pad_maximum_fusion.2), channel_id=1, source_target_pairs={{0,4},{1,3},{2,6},{3,1},{4,0},{5,7},{6,2},{7,5},{8,12},{9,11},{10,... | collective-permute-start | bytes 786440 | tf_op jit(solution)/shard_map/ppermute | solution.py:37
  12.4 0.9 %constant_dynamic-update-slice_fusion.4 = bf16[128,8192]{1,0:T(8,128)(2,1)S(1)} fusion(bf16[8,8192]{1,0:T(8,128)(2,1)} %param.5), kind=kLoop, calls=%fused_computation.47 | loop fusion | bytes 262144
  13.3 4.7 %collective-permute-done.1 = bf16[16,8192]{1,0:T(8,128)(2,1)S(1)} collective-permute-done((bf16[16,8192]{1,0:T(8,128)(2,1)S(1)}, bf16[16,8192]{1,0:T(8,128)(2,1)S(1)}, u32[]{:S(2)}, u32[]{:S(2)}) %collective-permute-start.1) | collective-permute-done | bytes 262176 | tf_op jit(solution)/shard_map/ppermute | solution.py:37
  18.0 0.9 %pad_maximum_fusion.1 = bf16[32,8192]{1,0:T(8,128)(2,1)S(1)} fusion(bf16[16,8192]{1,0:T(8,128)(2,1)S(1)} %collective-permute-done.1, bf16[8,8192]{1,0:T(8,128)(2,1)S(1)} %collective-permute-done, bf16[8,8192]{1,0:T(8,128)(2,1)} %param.5), kind=kLoop, calls=%fused_computation.9 | loop fusion | flops 1572864 | bytes 1048576 | tf_op jit(solution)/shard_map/concatenate | solution.py:45
  18.9 1.6 %collective-permute-start.2 = (bf16[32,8192]{1,0:T(8,128)(2,1)S(1)}, bf16[32,8192]{1,0:T(8,128)(2,1)S(1)}, u32[]{:S(2)}, u32[]{:S(2)}) collective-permute-start(bf16[32,8192]{1,0:T(8,128)(2,1)S(1)} %pad_maximum_fusion.1), channel_id=1, source_target_pairs={{0,2},{1,5},{2,0},{3,7},{4,6},{5,1},{6,4},{7,3},{8,10},{9,13},{10,... | collective-permute-start | bytes 1572872 | tf_op jit(solution)/shard_map/ppermute | solution.py:37
  20.5 7.6 %collective-permute-done.2 = bf16[32,8192]{1,0:T(8,128)(2,1)S(1)} collective-permute-done((bf16[32,8192]{1,0:T(8,128)(2,1)S(1)}, bf16[32,8192]{1,0:T(8,128)(2,1)S(1)}, u32[]{:S(2)}, u32[]{:S(2)}) %collective-permute-start.2) | collective-permute-done | bytes 524320 | tf_op jit(solution)/shard_map/ppermute | solution.py:37
  28.2 0.0 copy-done.1
  28.2 0.0 copy-start
  28.2 0.1 pad_maximum_fusion
  28.3 0.1 collective-permute-start.3
  28.4 2.6 %collective-permute-done.3 = bf16[64,8192]{1,0:T(8,128)(2,1)S(1)} collective-permute-done((bf16[64,8192]{1,0:T(8,128)(2,1)S(1)}, bf16[64,8192]{1,0:T(8,128)(2,1)S(1)}, u32[]{:S(2)}, u32[]{:S(2)}) %collective-permute-start.3) | collective-permute-done | bytes 1048608 | tf_op jit(solution)/shard_map/ppermute | solution.py:37
  31.0 0.1 constant_dynamic-update-slice_fusion
  31.1 0.0 copy-done
  31.1 1.1 %fusion.38 = f32[128,224]{0,1:T(8,128)S(1)} fusion(bf16[128,8192]{1,0:T(8,128)(2,1)S(1)} %constant_dynamic-update-slice_fusion, bf16[8192,224]{0,1:T(8,128)(2,1)S(1)} %copy-done), kind=kOutput, calls=%fused_computation.60 | convolution fusion | flops 469762048 | bytes 5881856 | tf_op jit(solution)/shard_map/dot_general | solution.py:46
  32.2 8.0 %fusion.13 = f32[128,8192]{1,0:T(8,128)} fusion(bf16[224,8192]{1,0:T(8,128)(2,1)} %param.8, f32[128,224]{0,1:T(8,128)S(1)} %fusion.38, bf16[128,8192]{1,0:T(8,128)(2,1)S(1)} %constant_dynamic-update-slice_fusion, bf16[8192,224]{0,1:T(8,128)(2,1)} %param.7), kind=kOutput, calls=%fused_computation.30 | convolution fusion | flops 939696128 | bytes 13746176 | tf_op jit(solution)/shard_map/dot_general | solution.py:49
  40.2 1.7 %slice.54 = bf16[64,8192]{1,0:T(8,128)(2,1)S(1)} slice(f32[128,8192]{1,0:T(8,128)} %fusion.13), slice={[64:128], [0:8192]} | slice | bytes 2097152 | tf_op jit(solution)/shard_map/slice | solution.py:52
  41.9 0.2 collective-permute-start.4
  42.1 2.5 %collective-permute-done.4 = bf16[64,8192]{1,0:T(8,128)(2,1)S(1)} collective-permute-done((bf16[64,8192]{1,0:T(8,128)(2,1)S(1)}, bf16[64,8192]{1,0:T(8,128)(2,1)S(1)}, u32[]{:S(2)}, u32[]{:S(2)}) %collective-permute-start.4) | collective-permute-done | bytes 1048608 | tf_op jit(solution)/shard_map/ppermute | solution.py:37
  44.6 1.8 %slice_add_fusion = f32[64,8192]{1,0:T(8,128)S(1)} fusion(f32[128,8192]{1,0:T(8,128)} %fusion.13, bf16[64,8192]{1,0:T(8,128)(2,1)S(1)} %collective-permute-done.4), kind=kLoop, calls=%fused_computation.1 | loop fusion | flops 1048576 | bytes 5242880 | tf_op jit(solution)/shard_map/add | solution.py:52
  46.4 0.1 slice.55
  46.5 0.0 copy-start.2
  46.5 1.6 %collective-permute-start.5 = (bf16[32,8192]{1,0:T(8,128)(2,1)S(1)}, bf16[32,8192]{1,0:T(8,128)(2,1)S(1)}, u32[]{:S(2)}, u32[]{:S(2)}) collective-permute-start(bf16[32,8192]{1,0:T(8,128)(2,1)S(1)} %slice.55), channel_id=1, source_target_pairs={{0,2},{1,5},{2,0},{3,7},{4,6},{5,1},{6,4},{7,3},{8,10},{9,13},{10,... | collective-permute-start | bytes 1572872 | tf_op jit(solution)/shard_map/ppermute | solution.py:37
  48.1 7.7 %collective-permute-done.5 = bf16[32,8192]{1,0:T(8,128)(2,1)S(1)} collective-permute-done((bf16[32,8192]{1,0:T(8,128)(2,1)S(1)}, bf16[32,8192]{1,0:T(8,128)(2,1)S(1)}, u32[]{:S(2)}, u32[]{:S(2)}) %collective-permute-start.5) | collective-permute-done | bytes 524320 | tf_op jit(solution)/shard_map/ppermute | solution.py:37
  55.8 0.1 slice_add_fusion.1
  55.9 0.8 %collective-permute-start.6 = (bf16[16,8192]{1,0:T(8,128)(2,1)S(1)}, bf16[16,8192]{1,0:T(8,128)(2,1)S(1)}, u32[]{:S(2)}, u32[]{:S(2)}) collective-permute-start(bf16[16,8192]{1,0:T(8,128)(2,1)S(1)} %slice.56), channel_id=1, source_target_pairs={{0,4},{1,3},{2,6},{3,1},{4,0},{5,7},{6,2},{7,5},{8,12},{9,11},{10,... | collective-permute-start | bytes 786440 | tf_op jit(solution)/shard_map/ppermute | solution.py:37
  56.7 5.6 %collective-permute-done.6 = bf16[16,8192]{1,0:T(8,128)(2,1)S(1)} collective-permute-done((bf16[16,8192]{1,0:T(8,128)(2,1)S(1)}, bf16[16,8192]{1,0:T(8,128)(2,1)S(1)}, u32[]{:S(2)}, u32[]{:S(2)}) %collective-permute-start.6) | collective-permute-done | bytes 262176 | tf_op jit(solution)/shard_map/ppermute | solution.py:37
  62.4 0.1 slice_add_fusion.2
  62.4 2.1 %collective-permute-start.7 = (bf16[8,8192]{1,0:T(8,128)(2,1)S(1)}, bf16[8,8192]{1,0:T(8,128)(2,1)S(1)}, u32[]{:S(2)}, u32[]{:S(2)}) collective-permute-start(bf16[8,8192]{1,0:T(8,128)(2,1)S(1)} %slice.57), channel_id=1, source_target_pairs={{0,8},{1,9},{2,10},{3,11},{4,12},{5,13},{6,14},{7,15},{8,0},{9,1},... | collective-permute-start | bytes 393224 | tf_op jit(solution)/shard_map/ppermute | solution.py:37
  64.5 0.0 copy-done.2
  64.5 5.5 %collective-permute-done.7 = bf16[8,8192]{1,0:T(8,128)(2,1)S(1)} collective-permute-done((bf16[8,8192]{1,0:T(8,128)(2,1)S(1)}, bf16[8,8192]{1,0:T(8,128)(2,1)S(1)}, u32[]{:S(2)}, u32[]{:S(2)}) %collective-permute-start.7) | collective-permute-done | bytes 131104 | tf_op jit(solution)/shard_map/ppermute | solution.py:37
  70.1 0.4 fusion
  70.5 0.7 %copy.11 = bf16[1,8,64,128]{3,1,2,0:T(8,128)(2,1)} copy(bf16[1,8,64,128]{3,2,1,0:T(8,128)(2,1)S(1)} %fusion) | data formatting | bytes 262144
  (7 shorter events, 0.1 us)
Async XLA Ops:
  0.0 28.2 %copy-start.1 = (bf16[8,8192]{1,0:T(8,128)(2,1)S(1)}, bf16[8,8192]{1,0:T(8,128)(2,1)}, u32[]{:S(2)}) copy-start(bf16[8,8192]{1,0:T(8,128)(2,1)} %param.5) | copy-start | bytes 393220
  0.0 10.6 %collective-permute-start = (bf16[8,8192]{1,0:T(8,128)(2,1)}, bf16[8,8192]{1,0:T(8,128)(2,1)S(1)}, u32[]{:S(2)}, u32[]{:S(2)}) collective-permute-start(bf16[8,8192]{1,0:T(8,128)(2,1)} %param.5), channel_id=1, source_target_pairs={{0,8},{1,9},{2,10},{3,11},{4,12},{5,13},{6,14},{7,15},{8,0},{9,1},... | collective-permute-start | bytes 393224 | tf_op jit(solution)/shard_map/ppermute | solution.py:37
  11.5 6.4 %collective-permute-start.1 = (bf16[16,8192]{1,0:T(8,128)(2,1)S(1)}, bf16[16,8192]{1,0:T(8,128)(2,1)S(1)}, u32[]{:S(2)}, u32[]{:S(2)}) collective-permute-start(bf16[16,8192]{1,0:T(8,128)(2,1)S(1)} %pad_maximum_fusion.2), channel_id=1, source_target_pairs={{0,4},{1,3},{2,6},{3,1},{4,0},{5,7},{6,2},{7,5},{8,12},{9,11},{10,... | collective-permute-start | bytes 786440 | tf_op jit(solution)/shard_map/ppermute | solution.py:37
  18.9 9.2 %collective-permute-start.2 = (bf16[32,8192]{1,0:T(8,128)(2,1)S(1)}, bf16[32,8192]{1,0:T(8,128)(2,1)S(1)}, u32[]{:S(2)}, u32[]{:S(2)}) collective-permute-start(bf16[32,8192]{1,0:T(8,128)(2,1)S(1)} %pad_maximum_fusion.1), channel_id=1, source_target_pairs={{0,2},{1,5},{2,0},{3,7},{4,6},{5,1},{6,4},{7,3},{8,10},{9,13},{10,... | collective-permute-start | bytes 1572872 | tf_op jit(solution)/shard_map/ppermute | solution.py:37
  28.2 2.9 %copy-start = (bf16[8192,224]{0,1:T(8,128)(2,1)S(1)}, bf16[8192,224]{0,1:T(8,128)(2,1)}, u32[]{:S(2)}) copy-start(bf16[8192,224]{0,1:T(8,128)(2,1)} %param.6) | copy-start | bytes 11010052
  28.3 2.7 %collective-permute-start.3 = (bf16[64,8192]{1,0:T(8,128)(2,1)S(1)}, bf16[64,8192]{1,0:T(8,128)(2,1)S(1)}, u32[]{:S(2)}, u32[]{:S(2)}) collective-permute-start(bf16[64,8192]{1,0:T(8,128)(2,1)S(1)} %pad_maximum_fusion), channel_id=1, source_target_pairs={{0,1},{1,0},{2,3},{3,2},{4,5},{5,4},{6,7},{7,6},{8,9},{9,8},{10,11... | collective-permute-start | bytes 3145736 | tf_op jit(solution)/shard_map/ppermute | solution.py:37
  41.9 2.7 %collective-permute-start.4 = (bf16[64,8192]{1,0:T(8,128)(2,1)S(1)}, bf16[64,8192]{1,0:T(8,128)(2,1)S(1)}, u32[]{:S(2)}, u32[]{:S(2)}) collective-permute-start(bf16[64,8192]{1,0:T(8,128)(2,1)S(1)} %slice.54), channel_id=1, source_target_pairs={{0,1},{1,0},{2,3},{3,2},{4,5},{5,4},{6,7},{7,6},{8,9},{9,8},{10,11... | collective-permute-start | bytes 3145736 | tf_op jit(solution)/shard_map/ppermute | solution.py:37
  46.5 18.0 %copy-start.2 = (s32[8192]{0:T(1024)S(1)}, s32[8192]{0:T(1024)}, u32[]{:S(2)}) copy-start(s32[8192]{0:T(1024)} %param.9) | copy-start | bytes 98308
  46.5 9.2 %collective-permute-start.5 = (bf16[32,8192]{1,0:T(8,128)(2,1)S(1)}, bf16[32,8192]{1,0:T(8,128)(2,1)S(1)}, u32[]{:S(2)}, u32[]{:S(2)}) collective-permute-start(bf16[32,8192]{1,0:T(8,128)(2,1)S(1)} %slice.55), channel_id=1, source_target_pairs={{0,2},{1,5},{2,0},{3,7},{4,6},{5,1},{6,4},{7,3},{8,10},{9,13},{10,... | collective-permute-start | bytes 1572872 | tf_op jit(solution)/shard_map/ppermute | solution.py:37
  55.9 6.4 %collective-permute-start.6 = (bf16[16,8192]{1,0:T(8,128)(2,1)S(1)}, bf16[16,8192]{1,0:T(8,128)(2,1)S(1)}, u32[]{:S(2)}, u32[]{:S(2)}) collective-permute-start(bf16[16,8192]{1,0:T(8,128)(2,1)S(1)} %slice.56), channel_id=1, source_target_pairs={{0,4},{1,3},{2,6},{3,1},{4,0},{5,7},{6,2},{7,5},{8,12},{9,11},{10,... | collective-permute-start | bytes 786440 | tf_op jit(solution)/shard_map/ppermute | solution.py:37
  62.4 7.6 %collective-permute-start.7 = (bf16[8,8192]{1,0:T(8,128)(2,1)S(1)}, bf16[8,8192]{1,0:T(8,128)(2,1)S(1)}, u32[]{:S(2)}, u32[]{:S(2)}) collective-permute-start(bf16[8,8192]{1,0:T(8,128)(2,1)S(1)} %slice.57), channel_id=1, source_target_pairs={{0,8},{1,9},{2,10},{3,11},{4,12},{5,13},{6,14},{7,15},{8,0},{9,1},... | collective-permute-start | bytes 393224 | tf_op jit(solution)/shard_map/ppermute | solution.py:37

commit v4 on v3

v4 whole, which is shorter than its diff:
```python
import functools
import math

import jax
import jax.numpy as jnp
from jax import lax
from jax.experimental import pallas as pl
from jax.experimental.pallas import tpu as pltpu
from jax.sharding import PartitionSpec as P

CHUNKS = 2
BLOCK = 128
NT = (((1,), (1,)), ((), ()))


def vmem():
    return pl.BlockSpec(memory_space=pltpu.VMEM)


def gate_up_kernel(start, width, has_sum, last, *refs):
    gate_w, up_w, *refs = refs
    pieces, refs = refs[:4], refs[4:]
    if has_sum:
        gate_in, up_in, *refs = refs
    if last:
        hidden_ref, gate_sum, up_sum = refs
    else:
        gate_sum, up_sum = refs
    if has_sum:
        gate_sum[...] = gate_in[...]
        up_sum[...] = up_in[...]
    else:
        gate_sum[...] = jnp.zeros_like(gate_sum)
        up_sum[...] = jnp.zeros_like(up_sum)
    tile = math.gcd(width, 1024)

    def step(index, carry):
        here = pl.ds(pl.multiple_of(index * tile, tile), tile)
        there = pl.ds(pl.multiple_of(start + index * tile, tile), tile)
        rows = jnp.concatenate([piece[:, here] for piece in pieces])
        gate_sum[...] += lax.dot_general(gate_w[:, there], rows, NT, preferred_element_type=jnp.float32)
        up_sum[...] += lax.dot_general(up_w[:, there], rows, NT, preferred_element_type=jnp.float32)
        return carry

    lax.fori_loop(0, width // tile, step, 0)
    if last:
        gate = gate_sum[...]
        hidden = gate / (1.0 + jnp.exp(-gate)) * up_sum[...]
        hidden_ref[...] = hidden.T.astype(jnp.bfloat16)


def gate_up(gate_w, up_w, pieces, sums, start, last):
    units, rows, width = gate_w.shape[0], sum(p.shape[0] for p in pieces), pieces[0].shape[1]
    total = jax.ShapeDtypeStruct((units, rows), jnp.float32)
    return pl.pallas_call(
        functools.partial(gate_up_kernel, start, width, bool(sums), last),
        out_shape=jax.ShapeDtypeStruct((rows, units), jnp.bfloat16) if last else (total, total),
        in_specs=[vmem()] * (6 + len(sums)),
        out_specs=vmem() if last else (vmem(), vmem()),
        scratch_shapes=[pltpu.VMEM((units, rows), jnp.float32)] * 2 if last else [],
        cost_estimate=pl.CostEstimate(
            flops=4 * units * rows * width, bytes_accessed=4 * units * width, transcendentals=0
        ),
        compiler_params=pltpu.CompilerParams(vmem_limit_bytes=40 << 20),
    )(gate_w, up_w, *pieces, *sums)


def down_kernel(start, hidden_ref, down_ref, keep_ref, send_ref):
    half, width = keep_ref.shape
    tile = math.gcd(width, 512)

    def step(index, carry):
        here = pl.ds(pl.multiple_of(index * tile, tile), tile)
        there = pl.ds(pl.multiple_of(start + index * tile, tile), tile)
        part = jnp.dot(hidden_ref[...], down_ref[:, there], preferred_element_type=jnp.float32)
        keep_ref[:, here] = part[:half]
        send_ref[:, here] = part[half:].astype(jnp.bfloat16)
        return carry

    lax.fori_loop(0, width // tile, step, 0)


def down(hidden, down_w, start, width):
    rows, units = hidden.shape
    return pl.pallas_call(
        functools.partial(down_kernel, start),
        out_shape=(
            jax.ShapeDtypeStruct((rows // 2, width), jnp.float32),
            jax.ShapeDtypeStruct((rows // 2, width), jnp.bfloat16),
        ),
        in_specs=[vmem()] * 2,
        out_specs=(vmem(), vmem()),
        cost_estimate=pl.CostEstimate(
            flops=2 * units * rows * width, bytes_accessed=2 * units * width, transcendentals=0
        ),
        compiler_params=pltpu.CompilerParams(vmem_limit_bytes=40 << 20),
    )(hidden, down_w)


def rotate_kernel(count, *refs):
    sums, arrived = refs[:count], refs[count : 2 * count]
    sign_ref, out_ref = refs[2 * count :]
    rows, width = sums[0].shape
    common = lax.broadcasted_iota(jnp.int32, (BLOCK, BLOCK), 0) & lax.broadcasted_iota(
        jnp.int32, (BLOCK, BLOCK), 1
    )
    for shift in (4, 2, 1):
        common = common ^ (common >> shift)
    flips = (1 - 2 * (common & 1)).astype(jnp.float32).astype(jnp.bfloat16)
    scale = 1.0 / math.sqrt(BLOCK)
    for c in range(count):
        value = (sums[c][...] + arrived[c][...].astype(jnp.float32)) * sign_ref[
            :, c * width : (c + 1) * width
        ].astype(jnp.float32)
        value = jnp.concatenate([value[:, b : b + BLOCK] for b in range(0, width, BLOCK)])
        high = value.astype(jnp.bfloat16)
        low = (value - high.astype(jnp.float32)).astype(jnp.bfloat16)
        turned = jnp.dot(high, flips, preferred_element_type=jnp.float32)
        turned = (turned + jnp.dot(low, flips, preferred_element_type=jnp.float32)) * scale
        for b in range(width // BLOCK):
            first = c * width + b * BLOCK
            out_ref[:, first : first + BLOCK] = turned[b * rows : (b + 1) * rows].astype(jnp.bfloat16)


def rotate(sums, arrived, signs):
    rows, width = sums[0].shape
    features = signs.shape[0]
    return pl.pallas_call(
        functools.partial(rotate_kernel, len(sums)),
        out_shape=jax.ShapeDtypeStruct((rows, features), jnp.bfloat16),
        in_specs=[vmem()] * (2 * len(sums) + 1),
        out_specs=vmem(),
        compiler_params=pltpu.CompilerParams(vmem_limit_bytes=16 << 20),
    )(*sums, *arrived, signs.reshape(1, features))


def solution(mesh):
    members = mesh.shape["gx"]
    assert members & (members - 1) == 0 and members >= 8

    far = []
    mask = members // 2
    while mask > 4:
        far.append((mask, mask))
        mask //= 2
    near = [(4, 2), (2, 4)]
    core = (1, 1)

    def swap(value, masks):
        return lax.ppermute(value, "gx", [(i, i ^ masks[i % 2]) for i in range(members)])

    def halve(total, arrived):
        total = total + arrived.astype(jnp.float32)
        half = total.shape[0] // 2
        return total[:half], total[half:].astype(jnp.bfloat16)

    def on_device(tokens, gate_weight, up_weight, down_weight, sign_pattern):
        features = tokens.shape[1]
        width = features // CHUNKS
        gate_w, up_w = gate_weight.T, up_weight.T

        wide = tokens
        for masks in far:
            wide = jnp.concatenate([wide, swap(wide, masks)])
        sums = ()
        for c in range(CHUNKS):
            part = wide[:, c * width : (c + 1) * width]
            part = jnp.concatenate([part, swap(part, near[0])])
            there = swap(part, near[1])
            pieces = (part, there, swap(part, core), swap(there, core))
            sums = gate_up(gate_w, up_w, pieces, sums, c * width, c == CHUNKS - 1)
        hidden = sums

        totals, arrived = [], []
        for c in range(CHUNKS):
            total, send = down(hidden, down_weight, c * width, width)
            for masks in [core] + near[::-1] + far[::-1]:
                total, send = halve(total, swap(send, masks)) if masks != far[0] else (total, swap(send, masks))
            totals.append(total)
            arrived.append(send)
        return rotate(totals, arrived, sign_pattern)

    placed = (P(("groups", "gx"), None), P(None, "gx"), P(None, "gx"), P("gx", None), P())
    return jax.shard_map(
        on_device, mesh=mesh, in_specs=placed, out_specs=P(("groups", "gx"), None), check_vma=False
    )
```

time: 71.5 us -> 58.4 us (0.82)
  waiting for transfers between devices: 42.8 us -> 24.6 us
  matrix products: 9.55 us -> 0 us
  starting transfers between devices: 11.2 us -> 20.2 us
  Pallas kernels: 0 us -> 7.3 us
  other arithmetic: 3.97 us -> 0.37 us
  local copies, waits for them, and re-layouts: 3.6 us -> 5.46 us
    ppermute x8 -> x17, waiting for transfers between devices: 42.8 us -> 24.6 us  [swap(): lax.ppermute(value, 'gx', [(i, i ^ masks[i % 2]) for i in range(members)])]
    dot_general x3 -> x0, matrix products: 9.55 us -> none  [the longest x1 8.01 us: on_device(): total = jnp.dot(hidden, down_weight, preferred_element_type=jnp.float32)]
    ppermute x8 -> x17, starting transfers between devices: 11.2 us -> 20.2 us  [swap(): lax.ppermute(value, 'gx', [(i, i ^ masks[i % 2]) for i in range(members)])]
    pallas_call x0 -> x5, Pallas kernels: none -> 7.3 us  [the longest x2 3.38 us: gate_up(): pl.pallas_call(functools.partial(gate_up_kernel, start, width, bool(sums)...]
    unnamed x11 -> x9, local copies, waits for them, and re-layouts: 1.74 us -> 5.3 us
    concatenate x3 -> x2, other arithmetic: 1.93 us -> 0.04 us  [on_device(): part = jnp.concatenate([part, swap(part, near[0])])]
    add x3 -> x6, other arithmetic: 2.01 us -> 0.33 us  [halve(): total = total + arrived.astype(jnp.float32)]
    slice x4 -> x9, local copies, waits for them, and re-layouts: 1.79 us -> 0.15 us  [the longest x8 0.13 us: halve(): return (total[:half], total[half:].astype(jnp.bfloat16))]
  transfers between devices with their start and end apart: 8 -> 17, of which waited for: 8 -> 12; matrix products, arithmetic and copies ran while one was open for 1% -> 2% of each run, Pallas kernels for 0% -> 5%
where the time goes in v4:
time: 58.4 us; the launch traced here: 58.2 us
  waiting for transfers between devices  24.6 us (42%)
  starting transfers between devices  20.2 us (35%)
  Pallas kernels  7.3 us (12%)
  local copies, waits for them, and re-layouts  5.46 us (9%)
    ppermute x17, waiting for transfers between devices, swap(): lax.ppermute(value, 'gx', [(i, i ^ masks[i % 2]) for i in range(members)])  24.6 us
    ppermute x17, starting transfers between devices, swap(): lax.ppermute(value, 'gx', [(i, i ^ masks[i % 2]) for i in range(members)])  20.2 us
    unnamed x9, local copies, waits for them, and re-layouts  5.3 us
    pallas_call x2, Pallas kernels, gate_up(): pl.pallas_call(functools.partial(gate_up_kernel, start, width, bool(sums)...  3.38 us
    pallas_call x2, Pallas kernels, down(): pl.pallas_call(functools.partial(down_kernel, start), out_shape=(jax.Shap...  3.02 us
  transfers between devices with their start and end apart: 17, of which 12 were waited for; matrix products, arithmetic and copies ran while one was open for 2% of the time, Pallas kernels for 5%

profile of v4, /device:TPU:0, one launch (start us, length us, event | category | flops | bytes accessed | tf_op | source)
XLA Modules:
  0.0 58.2 jit_solution(14455348783935029770)
XLA Ops:
  0.0 4.0 %collective-permute-start = (bf16[8,8192]{1,0:T(8,128)(2,1)}, bf16[8,8192]{1,0:T(8,128)(2,1)S(1)}, u32[]{:S(2)}, u32[]{:S(2)}) collective-permute-start(bf16[8,8192]{1,0:T(8,128)(2,1)} %param.5), channel_id=1, source_target_pairs={{0,8},{1,9},{2,10},{3,11},{4,12},{5,13},{6,14},{7,15},{8,0},{9,1},... | collective-permute-start | bytes 393224 | tf_op jit(solution)/shard_map/ppermute | solution.py:150
  4.0 0.9 %constant_dynamic-update-slice_fusion.1 = bf16[16,8192]{1,0:T(8,128)(2,1)S(1)} fusion(bf16[8,8192]{1,0:T(8,128)(2,1)} %param.5), kind=kLoop, calls=%fused_computation.15 | loop fusion | bytes 262144
  5.0 5.6 %collective-permute-done = bf16[8,8192]{1,0:T(8,128)(2,1)S(1)} collective-permute-done((bf16[8,8192]{1,0:T(8,128)(2,1)}, bf16[8,8192]{1,0:T(8,128)(2,1)S(1)}, u32[]{:S(2)}, u32[]{:S(2)}) %collective-permute-start) | collective-permute-done | bytes 131104 | tf_op jit(solution)/shard_map/ppermute | solution.py:150
  10.6 0.9 %collective-permute-start.5 = (bf16[16,4096]{1,0:T(8,128)(2,1)S(1)}, bf16[16,4096]{1,0:T(8,128)(2,1)S(1)}, u32[]{:S(2)}, u32[]{:S(2)}) collective-permute-start(bf16[16,4096]{1,0:T(8,128)(2,1)S(1)} %get-tuple-element.17), channel_id=1, source_target_pairs={{0,4},{1,3},{2,6},{3,1},{4,0},{5,7},{6,2},{7,5},{8,12},{9,11},{10,... | collective-permute-start | bytes 393224 | tf_op jit(solution)/shard_map/ppermute | solution.py:150
  11.5 1.2 %collective-permute-start.1 = (bf16[16,4096]{1,0:T(8,128)(2,1)S(1)}, bf16[16,4096]{1,0:T(8,128)(2,1)S(1)}, u32[]{:S(2)}, u32[]{:S(2)}) collective-permute-start(bf16[16,4096]{1,0:T(8,128)(2,1)S(1)} %get-tuple-element.18), channel_id=1, source_target_pairs={{0,4},{1,3},{2,6},{3,1},{4,0},{5,7},{6,2},{7,5},{8,12},{9,11},{10,... | collective-permute-start | bytes 393224 | tf_op jit(solution)/shard_map/ppermute | solution.py:150
  12.7 2.9 %collective-permute-done.5 = bf16[16,4096]{1,0:T(8,128)(2,1)S(1)} collective-permute-done((bf16[16,4096]{1,0:T(8,128)(2,1)S(1)}, bf16[16,4096]{1,0:T(8,128)(2,1)S(1)}, u32[]{:S(2)}, u32[]{:S(2)}) %collective-permute-start.5) | collective-permute-done | bytes 131104 | tf_op jit(solution)/shard_map/ppermute | solution.py:150
  15.6 1.6 %collective-permute-start.6 = (bf16[32,4096]{1,0:T(8,128)(2,1)S(1)}, bf16[32,4096]{1,0:T(8,128)(2,1)S(1)}, u32[]{:S(2)}, u32[]{:S(2)}) collective-permute-start(bf16[32,4096]{1,0:T(8,128)(2,1)S(1)} %pad_maximum_fusion.1.refs_2_), channel_id=1, source_target_pairs={{0,2},{1,5},{2,0},{3,7},{4,6},{5,1},{6,4},{7,3},{8,10},{9,13},{10,... | collective-permute-start | bytes 786440 | tf_op jit(solution)/shard_map/ppermute | solution.py:150
  17.3 0.1 collective-permute-done.1
  17.5 1.7 %collective-permute-start.2 = (bf16[32,4096]{1,0:T(8,128)(2,1)S(1)}, bf16[32,4096]{1,0:T(8,128)(2,1)S(1)}, u32[]{:S(2)}, u32[]{:S(2)}) collective-permute-start(bf16[32,4096]{1,0:T(8,128)(2,1)S(1)} %pad_maximum_fusion.refs_2_), channel_id=1, source_target_pairs={{0,2},{1,5},{2,0},{3,7},{4,6},{5,1},{6,4},{7,3},{8,10},{9,13},{10,... | collective-permute-start | bytes 786440 | tf_op jit(solution)/shard_map/ppermute | solution.py:150
  19.1 0.0 collective-permute-start.7
  19.1 2.9 %collective-permute-done.6.refs_3_ = bf16[32,4096]{1,0:T(8,128)(2,1)S(1)} collective-permute-done((bf16[32,4096]{1,0:T(8,128)(2,1)S(1)}, bf16[32,4096]{1,0:T(8,128)(2,1)S(1)}, u32[]{:S(2)}, u32[]{:S(2)}) %collective-permute-start.6) | collective-permute-done | bytes 262176 | tf_op jit(solution)/shard_map/ppermute | solution.py:150
  22.1 0.0 collective-permute-start.8
  22.1 0.5 collective-permute-start.3
  22.6 2.3 %collective-permute-done.2.refs_3_ = bf16[32,4096]{1,0:T(8,128)(2,1)S(1)} collective-permute-done((bf16[32,4096]{1,0:T(8,128)(2,1)S(1)}, bf16[32,4096]{1,0:T(8,128)(2,1)S(1)}, u32[]{:S(2)}, u32[]{:S(2)}) %collective-permute-start.2) | collective-permute-done | bytes 262176 | tf_op jit(solution)/shard_map/ppermute | solution.py:150
  24.9 0.0 collective-permute-start.4
  24.9 0.0 collective-permute-done.7.refs_4_
  24.9 0.0 collective-permute-done.8.refs_5_
  24.9 0.0 copy-start.1
  24.9 2.0 %copy-done.1 = bf16[8192,224]{0,1:T(8,128)(2,1)S(1)} copy-done((bf16[8192,224]{0,1:T(8,128)(2,1)S(1)}, bf16[8192,224]{0,1:T(8,128)(2,1)}, u32[]{:S(2)}) %copy-start.1) | copy-done | bytes 3670040
  26.9 0.0 copy-start.2
  26.9 2.0 %copy-done.2 = bf16[8192,224]{0,1:T(8,128)(2,1)S(1)} copy-done((bf16[8192,224]{0,1:T(8,128)(2,1)S(1)}, bf16[8192,224]{0,1:T(8,128)(2,1)}, u32[]{:S(2)}) %copy-start.2) | copy-done | bytes 3670040
  29.0 1.6 %shard_map.55 = (f32[224,128]{1,0:T(8,128)S(1)}, f32[224,128]{1,0:T(8,128)S(1)}) custom-call(bf16[224,8192]{1,0:T(8,128)(2,1)S(1)} %bitcast.3, bf16[224,8192]{1,0:T(8,128)(2,1)S(1)} %bitcast.5, bf16[32,4096]{1,0:T(8,128)(2,1)S(1)} %pad_maximum_fusion.1.refs_2_, bf16[32,4096]{1,0:T(8,128)(2,1)S(1)} %collective-permute-done.6.refs_3_, ...), custom_call_target="tpu_custom_call" | custom-call | flops 469762048 | bytes 3670016 | tf_op jit(solution)/shard_map/pallas_call | solution.py:55
  30.6 0.0 collective-permute-done.3.refs_4_
  30.6 0.0 collective-permute-done.4.refs_5_
  30.6 0.0 copy-start
  30.7 1.8 %shard_map.56.hidden_ref = bf16[128,224]{1,0:T(8,128)(2,1)S(1)} custom-call(bf16[224,8192]{1,0:T(8,128)(2,1)S(1)} %bitcast.4, bf16[224,8192]{1,0:T(8,128)(2,1)S(1)} %bitcast.6, bf16[32,4096]{1,0:T(8,128)(2,1)S(1)} %pad_maximum_fusion.refs_2_, bf16[32,4096]{1,0:T(8,128)(2,1)S(1)} %collective-permute-done.2.refs_3_, ...), custom_call_target="tpu_custom_call" | custom-call | flops 469762048 | bytes 3670016 | tf_op jit(solution)/shard_map/pallas_call | solution.py:55
  32.4 0.3 copy-done
  32.7 1.5 %shard_map.58 = (f32[64,4096]{1,0:T(8,128)S(1)}, bf16[64,4096]{1,0:T(8,128)(2,1)S(1)}) custom-call(bf16[128,224]{1,0:T(8,128)(2,1)S(1)} %shard_map.56.hidden_ref, bf16[224,8192]{1,0:T(8,128)(2,1)S(1)} %copy-done), custom_call_target="tpu_custom_call" | custom-call | flops 234881024 | bytes 1835008 | tf_op jit(solution)/shard_map/pallas_call | solution.py:85
  34.2 0.6 collective-permute-start.12
  34.8 1.5 %shard_map.57 = (f32[64,4096]{1,0:T(8,128)S(1)}, bf16[64,4096]{1,0:T(8,128)(2,1)S(1)}) custom-call(bf16[128,224]{1,0:T(8,128)(2,1)S(1)} %shard_map.56.hidden_ref, bf16[224,8192]{1,0:T(8,128)(2,1)S(1)} %copy-done), custom_call_target="tpu_custom_call" | custom-call | flops 234881024 | bytes 1835008 | tf_op jit(solution)/shard_map/pallas_call | solution.py:85
  36.3 0.1 collective-permute-start.9
  36.4 0.0 collective-permute-done.12
  36.4 0.1 convert_add_fusion
  36.5 1.6 %collective-permute-start.13 = (bf16[32,4096]{1,0:T(8,128)(2,1)S(1)}, bf16[32,4096]{1,0:T(8,128)(2,1)S(1)}, u32[]{:S(2)}, u32[]{:S(2)}) collective-permute-start(bf16[32,4096]{1,0:T(8,128)(2,1)S(1)} %slice.86), channel_id=1, source_target_pairs={{0,2},{1,5},{2,0},{3,7},{4,6},{5,1},{6,4},{7,3},{8,10},{9,13},{10,... | collective-permute-start | bytes 786440 | tf_op jit(solution)/shard_map/ppermute | solution.py:150
  38.1 0.1 collective-permute-done.9
  38.3 0.0 copy-start.3
  38.3 0.1 convert_add_fusion.1
  38.4 1.6 %collective-permute-start.10 = (bf16[32,4096]{1,0:T(8,128)(2,1)S(1)}, bf16[32,4096]{1,0:T(8,128)(2,1)S(1)}, u32[]{:S(2)}, u32[]{:S(2)}) collective-permute-start(bf16[32,4096]{1,0:T(8,128)(2,1)S(1)} %slice.87), channel_id=1, source_target_pairs={{0,2},{1,5},{2,0},{3,7},{4,6},{5,1},{6,4},{7,3},{8,10},{9,13},{10,... | collective-permute-start | bytes 786440 | tf_op jit(solution)/shard_map/ppermute | solution.py:150
  40.0 2.9 %collective-permute-done.13 = bf16[32,4096]{1,0:T(8,128)(2,1)S(1)} collective-permute-done((bf16[32,4096]{1,0:T(8,128)(2,1)S(1)}, bf16[32,4096]{1,0:T(8,128)(2,1)S(1)}, u32[]{:S(2)}, u32[]{:S(2)}) %collective-permute-start.13) | collective-permute-done | bytes 262176 | tf_op jit(solution)/shard_map/ppermute | solution.py:150
  43.0 0.9 %collective-permute-start.14 = (bf16[16,4096]{1,0:T(8,128)(2,1)S(1)}, bf16[16,4096]{1,0:T(8,128)(2,1)S(1)}, u32[]{:S(2)}, u32[]{:S(2)}) collective-permute-start(bf16[16,4096]{1,0:T(8,128)(2,1)S(1)} %slice.88), channel_id=1, source_target_pairs={{0,4},{1,3},{2,6},{3,1},{4,0},{5,7},{6,2},{7,5},{8,12},{9,11},{10,... | collective-permute-start | bytes 393224 | tf_op jit(solution)/shard_map/ppermute | solution.py:150
  43.9 2.2 %collective-permute-done.10 = bf16[32,4096]{1,0:T(8,128)(2,1)S(1)} collective-permute-done((bf16[32,4096]{1,0:T(8,128)(2,1)S(1)}, bf16[32,4096]{1,0:T(8,128)(2,1)S(1)}, u32[]{:S(2)}, u32[]{:S(2)}) %collective-permute-start.10) | collective-permute-done | bytes 262176 | tf_op jit(solution)/shard_map/ppermute | solution.py:150
  46.1 0.1 slice_add_fusion.1
  46.2 0.9 %collective-permute-start.11 = (bf16[16,4096]{1,0:T(8,128)(2,1)S(1)}, bf16[16,4096]{1,0:T(8,128)(2,1)S(1)}, u32[]{:S(2)}, u32[]{:S(2)}) collective-permute-start(bf16[16,4096]{1,0:T(8,128)(2,1)S(1)} %slice.89), channel_id=1, source_target_pairs={{0,4},{1,3},{2,6},{3,1},{4,0},{5,7},{6,2},{7,5},{8,12},{9,11},{10,... | collective-permute-start | bytes 393224 | tf_op jit(solution)/shard_map/ppermute | solution.py:150
  47.1 0.9 %collective-permute-done.14 = bf16[16,4096]{1,0:T(8,128)(2,1)S(1)} collective-permute-done((bf16[16,4096]{1,0:T(8,128)(2,1)S(1)}, bf16[16,4096]{1,0:T(8,128)(2,1)S(1)}, u32[]{:S(2)}, u32[]{:S(2)}) %collective-permute-start.14) | collective-permute-done | bytes 131104 | tf_op jit(solution)/shard_map/ppermute | solution.py:150
  48.1 2.4 %collective-permute-start.16 = (bf16[8,4096]{1,0:T(8,128)(2,1)S(1)}, bf16[8,4096]{1,0:T(8,128)(2,1)S(1)}, u32[]{:S(2)}, u32[]{:S(2)}) collective-permute-start(bf16[8,4096]{1,0:T(8,128)(2,1)S(1)} %slice.90), channel_id=1, source_target_pairs={{0,8},{1,9},{2,10},{3,11},{4,12},{5,13},{6,14},{7,15},{8,0},{9,1},... | collective-permute-start | bytes 196616 | tf_op jit(solution)/shard_map/ppermute | solution.py:150
  50.5 1.5 %collective-permute-done.11 = bf16[16,4096]{1,0:T(8,128)(2,1)S(1)} collective-permute-done((bf16[16,4096]{1,0:T(8,128)(2,1)S(1)}, bf16[16,4096]{1,0:T(8,128)(2,1)S(1)}, u32[]{:S(2)}, u32[]{:S(2)}) %collective-permute-start.11) | collective-permute-done | bytes 131104 | tf_op jit(solution)/shard_map/ppermute | solution.py:150
  52.0 2.1 %collective-permute-start.15 = (bf16[8,4096]{1,0:T(8,128)(2,1)S(1)}, bf16[8,4096]{1,0:T(8,128)(2,1)S(1)}, u32[]{:S(2)}, u32[]{:S(2)}) collective-permute-start(bf16[8,4096]{1,0:T(8,128)(2,1)S(1)} %slice.91), channel_id=1, source_target_pairs={{0,8},{1,9},{2,10},{3,11},{4,12},{5,13},{6,14},{7,15},{8,0},{9,1},... | collective-permute-start | bytes 196616 | tf_op jit(solution)/shard_map/ppermute | solution.py:150
  54.2 1.3 %collective-permute-done.16.refs_3_ = bf16[8,4096]{1,0:T(8,128)(2,1)S(1)} collective-permute-done((bf16[8,4096]{1,0:T(8,128)(2,1)S(1)}, bf16[8,4096]{1,0:T(8,128)(2,1)S(1)}, u32[]{:S(2)}, u32[]{:S(2)}) %collective-permute-start.16) | collective-permute-done | bytes 65568 | tf_op jit(solution)/shard_map/ppermute | solution.py:150
  55.5 1.7 %collective-permute-done.15.refs_2_ = bf16[8,4096]{1,0:T(8,128)(2,1)S(1)} collective-permute-done((bf16[8,4096]{1,0:T(8,128)(2,1)S(1)}, bf16[8,4096]{1,0:T(8,128)(2,1)S(1)}, u32[]{:S(2)}, u32[]{:S(2)}) %collective-permute-start.15) | collective-permute-done | bytes 65568 | tf_op jit(solution)/shard_map/ppermute | solution.py:150
  57.2 0.0 copy-done.3
  57.2 0.9 %shard_map.59 = bf16[8,8192]{1,0:T(8,128)(2,1)} custom-call(f32[8,4096]{1,0:T(8,128)S(1)} %slice.68.refs_0_, f32[8,4096]{1,0:T(8,128)S(1)} %slice.73.refs_1_, bf16[8,4096]{1,0:T(8,128)(2,1)S(1)} %collective-permute-done.15.refs_2_, bf16[8,4096]{1,0:T(8,128)(2,1)S(1)} %collective-permute-done.16.refs_3_, s32[1,8192]{1,0:T(1,128)S(1)} %bitcast.7), custom_call_target="tpu_custom_call" | custom-call | tf_op jit(solution)/shard_map/pallas_call | solution.py:128
  (15 shorter events, 0.3 us)
Async XLA Ops:
  0.0 10.5 %collective-permute-start = (bf16[8,8192]{1,0:T(8,128)(2,1)}, bf16[8,8192]{1,0:T(8,128)(2,1)S(1)}, u32[]{:S(2)}, u32[]{:S(2)}) collective-permute-start(bf16[8,8192]{1,0:T(8,128)(2,1)} %param.5), channel_id=1, source_target_pairs={{0,8},{1,9},{2,10},{3,11},{4,12},{5,13},{6,14},{7,15},{8,0},{9,1},... | collective-permute-start | bytes 393224 | tf_op jit(solution)/shard_map/ppermute | solution.py:150
  10.6 5.0 %collective-permute-start.5 = (bf16[16,4096]{1,0:T(8,128)(2,1)S(1)}, bf16[16,4096]{1,0:T(8,128)(2,1)S(1)}, u32[]{:S(2)}, u32[]{:S(2)}) collective-permute-start(bf16[16,4096]{1,0:T(8,128)(2,1)S(1)} %get-tuple-element.17), channel_id=1, source_target_pairs={{0,4},{1,3},{2,6},{3,1},{4,0},{5,7},{6,2},{7,5},{8,12},{9,11},{10,... | collective-permute-start | bytes 393224 | tf_op jit(solution)/shard_map/ppermute | solution.py:150
  11.5 5.9 %collective-permute-start.1 = (bf16[16,4096]{1,0:T(8,128)(2,1)S(1)}, bf16[16,4096]{1,0:T(8,128)(2,1)S(1)}, u32[]{:S(2)}, u32[]{:S(2)}) collective-permute-start(bf16[16,4096]{1,0:T(8,128)(2,1)S(1)} %get-tuple-element.18), channel_id=1, source_target_pairs={{0,4},{1,3},{2,6},{3,1},{4,0},{5,7},{6,2},{7,5},{8,12},{9,11},{10,... | collective-permute-start | bytes 393224 | tf_op jit(solution)/shard_map/ppermute | solution.py:150
  15.6 6.4 %collective-permute-start.6 = (bf16[32,4096]{1,0:T(8,128)(2,1)S(1)}, bf16[32,4096]{1,0:T(8,128)(2,1)S(1)}, u32[]{:S(2)}, u32[]{:S(2)}) collective-permute-start(bf16[32,4096]{1,0:T(8,128)(2,1)S(1)} %pad_maximum_fusion.1.refs_2_), channel_id=1, source_target_pairs={{0,2},{1,5},{2,0},{3,7},{4,6},{5,1},{6,4},{7,3},{8,10},{9,13},{10,... | collective-permute-start | bytes 786440 | tf_op jit(solution)/shard_map/ppermute | solution.py:150
  17.5 7.4 %collective-permute-start.2 = (bf16[32,4096]{1,0:T(8,128)(2,1)S(1)}, bf16[32,4096]{1,0:T(8,128)(2,1)S(1)}, u32[]{:S(2)}, u32[]{:S(2)}) collective-permute-start(bf16[32,4096]{1,0:T(8,128)(2,1)S(1)} %pad_maximum_fusion.refs_2_), channel_id=1, source_target_pairs={{0,2},{1,5},{2,0},{3,7},{4,6},{5,1},{6,4},{7,3},{8,10},{9,13},{10,... | collective-permute-start | bytes 786440 | tf_op jit(solution)/shard_map/ppermute | solution.py:150
  19.1 5.8 %collective-permute-start.7 = (bf16[32,4096]{1,0:T(8,128)(2,1)S(1)}, bf16[32,4096]{1,0:T(8,128)(2,1)S(1)}, u32[]{:S(2)}, u32[]{:S(2)}) collective-permute-start(bf16[32,4096]{1,0:T(8,128)(2,1)S(1)} %pad_maximum_fusion.1.refs_2_), channel_id=1, source_target_pairs={{0,1},{1,0},{2,3},{3,2},{4,5},{5,4},{6,7},{7,6},{8,9},{9,8},{10,11... | collective-permute-start | bytes 786440 | tf_op jit(solution)/shard_map/ppermute | solution.py:150
  22.1 2.8 %collective-permute-start.8 = (bf16[32,4096]{1,0:T(8,128)(2,1)S(1)}, bf16[32,4096]{1,0:T(8,128)(2,1)S(1)}, u32[]{:S(2)}, u32[]{:S(2)}) collective-permute-start(bf16[32,4096]{1,0:T(8,128)(2,1)S(1)} %collective-permute-done.6.refs_3_), channel_id=1, source_target_pairs={{0,1},{1,0},{2,3},{3,2},{4,5},{5,4},{6,7},{7,6},{8,9},{9,8},{10,11... | collective-permute-start | bytes 786440 | tf_op jit(solution)/shard_map/ppermute | solution.py:150
  22.1 8.5 %collective-permute-start.3 = (bf16[32,4096]{1,0:T(8,128)(2,1)S(1)}, bf16[32,4096]{1,0:T(8,128)(2,1)S(1)}, u32[]{:S(2)}, u32[]{:S(2)}) collective-permute-start(bf16[32,4096]{1,0:T(8,128)(2,1)S(1)} %pad_maximum_fusion.refs_2_), channel_id=1, source_target_pairs={{0,1},{1,0},{2,3},{3,2},{4,5},{5,4},{6,7},{7,6},{8,9},{9,8},{10,11... | collective-permute-start | bytes 786440 | tf_op jit(solution)/shard_map/ppermute | solution.py:150
  24.9 5.7 %collective-permute-start.4 = (bf16[32,4096]{1,0:T(8,128)(2,1)S(1)}, bf16[32,4096]{1,0:T(8,128)(2,1)S(1)}, u32[]{:S(2)}, u32[]{:S(2)}) collective-permute-start(bf16[32,4096]{1,0:T(8,128)(2,1)S(1)} %collective-permute-done.2.refs_3_), channel_id=1, source_target_pairs={{0,1},{1,0},{2,3},{3,2},{4,5},{5,4},{6,7},{7,6},{8,9},{9,8},{10,11... | collective-permute-start | bytes 786440 | tf_op jit(solution)/shard_map/ppermute | solution.py:150
  24.9 2.0 %copy-start.1 = (bf16[8192,224]{0,1:T(8,128)(2,1)S(1)}, bf16[8192,224]{0,1:T(8,128)(2,1)}, u32[]{:S(2)}) copy-start(bf16[8192,224]{0,1:T(8,128)(2,1)} %param.6) | copy-start | bytes 11010052
  26.9 2.0 %copy-start.2 = (bf16[8192,224]{0,1:T(8,128)(2,1)S(1)}, bf16[8192,224]{0,1:T(8,128)(2,1)}, u32[]{:S(2)}) copy-start(bf16[8192,224]{0,1:T(8,128)(2,1)} %param.7) | copy-start | bytes 11010052
  30.6 2.0 %copy-start = (bf16[224,8192]{1,0:T(8,128)(2,1)S(1)}, bf16[224,8192]{1,0:T(8,128)(2,1)}, u32[]{:S(2)}) copy-start(bf16[224,8192]{1,0:T(8,128)(2,1)} %down_ref.3) | copy-start | bytes 11010052
  34.2 2.2 %collective-permute-start.12 = (bf16[64,4096]{1,0:T(8,128)(2,1)S(1)}, bf16[64,4096]{1,0:T(8,128)(2,1)S(1)}, u32[]{:S(2)}, u32[]{:S(2)}) collective-permute-start(bf16[64,4096]{1,0:T(8,128)(2,1)S(1)} %get-tuple-element.16), channel_id=1, source_target_pairs={{0,1},{1,0},{2,3},{3,2},{4,5},{5,4},{6,7},{7,6},{8,9},{9,8},{10,11... | collective-permute-start | bytes 1572872 | tf_op jit(solution)/shard_map/ppermute | solution.py:150
  36.3 2.0 %collective-permute-start.9 = (bf16[64,4096]{1,0:T(8,128)(2,1)S(1)}, bf16[64,4096]{1,0:T(8,128)(2,1)S(1)}, u32[]{:S(2)}, u32[]{:S(2)}) collective-permute-start(bf16[64,4096]{1,0:T(8,128)(2,1)S(1)} %get-tuple-element.14), channel_id=1, source_target_pairs={{0,1},{1,0},{2,3},{3,2},{4,5},{5,4},{6,7},{7,6},{8,9},{9,8},{10,11... | collective-permute-start | bytes 1572872 | tf_op jit(solution)/shard_map/ppermute | solution.py:150
  36.5 6.4 %collective-permute-start.13 = (bf16[32,4096]{1,0:T(8,128)(2,1)S(1)}, bf16[32,4096]{1,0:T(8,128)(2,1)S(1)}, u32[]{:S(2)}, u32[]{:S(2)}) collective-permute-start(bf16[32,4096]{1,0:T(8,128)(2,1)S(1)} %slice.86), channel_id=1, source_target_pairs={{0,2},{1,5},{2,0},{3,7},{4,6},{5,1},{6,4},{7,3},{8,10},{9,13},{10,... | collective-permute-start | bytes 786440 | tf_op jit(solution)/shard_map/ppermute | solution.py:150
  38.3 19.0 %copy-start.3 = (s32[8192]{0:T(1024)S(1)}, s32[8192]{0:T(1024)}, u32[]{:S(2)}) copy-start(s32[8192]{0:T(1024)} %param.9) | copy-start | bytes 98308
  38.4 7.7 %collective-permute-start.10 = (bf16[32,4096]{1,0:T(8,128)(2,1)S(1)}, bf16[32,4096]{1,0:T(8,128)(2,1)S(1)}, u32[]{:S(2)}, u32[]{:S(2)}) collective-permute-start(bf16[32,4096]{1,0:T(8,128)(2,1)S(1)} %slice.87), channel_id=1, source_target_pairs={{0,2},{1,5},{2,0},{3,7},{4,6},{5,1},{6,4},{7,3},{8,10},{9,13},{10,... | collective-permute-start | bytes 786440 | tf_op jit(solution)/shard_map/ppermute | solution.py:150
  43.0 5.0 %collective-permute-start.14 = (bf16[16,4096]{1,0:T(8,128)(2,1)S(1)}, bf16[16,4096]{1,0:T(8,128)(2,1)S(1)}, u32[]{:S(2)}, u32[]{:S(2)}) collective-permute-start(bf16[16,4096]{1,0:T(8,128)(2,1)S(1)} %slice.88), channel_id=1, source_target_pairs={{0,4},{1,3},{2,6},{3,1},{4,0},{5,7},{6,2},{7,5},{8,12},{9,11},{10,... | collective-permute-start | bytes 393224 | tf_op jit(solution)/shard_map/ppermute | solution.py:150
  46.2 5.7 %collective-permute-start.11 = (bf16[16,4096]{1,0:T(8,128)(2,1)S(1)}, bf16[16,4096]{1,0:T(8,128)(2,1)S(1)}, u32[]{:S(2)}, u32[]{:S(2)}) collective-permute-start(bf16[16,4096]{1,0:T(8,128)(2,1)S(1)} %slice.89), channel_id=1, source_target_pairs={{0,4},{1,3},{2,6},{3,1},{4,0},{5,7},{6,2},{7,5},{8,12},{9,11},{10,... | collective-permute-start | bytes 393224 | tf_op jit(solution)/shard_map/ppermute | solution.py:150
  48.1 7.4 %collective-permute-start.16 = (bf16[8,4096]{1,0:T(8,128)(2,1)S(1)}, bf16[8,4096]{1,0:T(8,128)(2,1)S(1)}, u32[]{:S(2)}, u32[]{:S(2)}) collective-permute-start(bf16[8,4096]{1,0:T(8,128)(2,1)S(1)} %slice.90), channel_id=1, source_target_pairs={{0,8},{1,9},{2,10},{3,11},{4,12},{5,13},{6,14},{7,15},{8,0},{9,1},... | collective-permute-start | bytes 196616 | tf_op jit(solution)/shard_map/ppermute | solution.py:150
  52.0 5.2 %collective-permute-start.15 = (bf16[8,4096]{1,0:T(8,128)(2,1)S(1)}, bf16[8,4096]{1,0:T(8,128)(2,1)S(1)}, u32[]{:S(2)}, u32[]{:S(2)}) collective-permute-start(bf16[8,4096]{1,0:T(8,128)(2,1)S(1)} %slice.91), channel_id=1, source_target_pairs={{0,8},{1,9},{2,10},{3,11},{4,12},{5,13},{6,14},{7,15},{8,0},{9,1},... | collective-permute-start | bytes 196616 | tf_op jit(solution)/shard_map/ppermute | solution.py:150

commit v5 on v0

v5 whole, which is shorter than its diff:
```python
import functools
import math

import jax
import jax.numpy as jnp
from jax import lax
from jax.experimental import pallas as pl
from jax.experimental.pallas import tpu as pltpu
from jax.sharding import PartitionSpec as P

BLOCK = 128
NT = (((1,), (1,)), ((), ()))


def vmem():
    return pl.BlockSpec(memory_space=pltpu.VMEM)


def fetch_kernel(gate_hbm, up_hbm, down_hbm, gate_up_ref, down_ref, sems):
    units = gate_hbm.shape[0]
    copies = [
        pltpu.make_async_copy(gate_hbm, gate_up_ref.at[:units], sems.at[0]),
        pltpu.make_async_copy(up_hbm, gate_up_ref.at[units:], sems.at[1]),
        pltpu.make_async_copy(down_hbm, down_ref, sems.at[2]),
    ]
    for copy in copies:
        copy.start()
    for copy in copies:
        copy.wait()


def fetch(gate_w, up_w, down_w):
    units, features = gate_w.shape
    return pl.pallas_call(
        fetch_kernel,
        out_shape=(
            jax.ShapeDtypeStruct((2 * units, features), gate_w.dtype),
            jax.ShapeDtypeStruct(down_w.shape, down_w.dtype),
        ),
        in_specs=[pl.BlockSpec(memory_space=pltpu.HBM)] * 3,
        out_specs=(vmem(), vmem()),
        scratch_shapes=[pltpu.SemaphoreType.DMA((3,))],
        cost_estimate=pl.CostEstimate(flops=0, bytes_accessed=6 * units * features, transcendentals=0),
        compiler_params=pltpu.CompilerParams(vmem_limit_bytes=24 << 20),
    )(*(pltpu.with_memory_space_constraint(w, pltpu.HBM) for w in (gate_w, up_w, down_w)))


def hidden_kernel(weights_ref, rows_ref, hidden_ref, sums):
    units, features = sums.shape[0] // 2, rows_ref.shape[1]
    tile = math.gcd(features, 1024)
    sums[...] = jnp.zeros_like(sums)

    def step(index, carry):
        here = pl.ds(pl.multiple_of(index * tile, tile), tile)
        sums[...] += lax.dot_general(
            weights_ref[:, here], rows_ref[:, here], NT, preferred_element_type=jnp.float32
        )
        return carry

    lax.fori_loop(0, features // tile, step, 0)
    gate = sums[:units]
    hidden = gate / (1.0 + jnp.exp(-gate)) * sums[units:]
    hidden_ref[...] = hidden.T.astype(jnp.bfloat16)


def hidden_units(weights, rows):
    units, count = weights.shape[0] // 2, rows.shape[0]
    return pl.pallas_call(
        hidden_kernel,
        out_shape=jax.ShapeDtypeStruct((count, units), jnp.bfloat16),
        in_specs=[vmem()] * 2,
        out_specs=vmem(),
        scratch_shapes=[pltpu.VMEM((2 * units, count), jnp.float32)],
        cost_estimate=pl.CostEstimate(
            flops=4 * units * rows.size, bytes_accessed=2 * weights.size, transcendentals=0
        ),
        compiler_params=pltpu.CompilerParams(vmem_limit_bytes=24 << 20),
    )(weights, rows)


def down_kernel(own, other, hidden_ref, down_ref, keep_ref, send_ref):
    count, features = keep_ref.shape
    tile = math.gcd(features, 512)
    hidden = jnp.concatenate([hidden_ref[own : own + count], hidden_ref[other : other + count]])

    def step(index, carry):
        here = pl.ds(pl.multiple_of(index * tile, tile), tile)
        part = jnp.dot(hidden, down_ref[:, here], preferred_element_type=jnp.float32)
        keep_ref[:, here] = part[:count]
        send_ref[:, here] = part[count:].astype(jnp.bfloat16)
        return carry

    lax.fori_loop(0, features // tile, step, 0)


def down(hidden, down_w, own, other, count):
    units, features = down_w.shape
    return pl.pallas_call(
        functools.partial(down_kernel, own, other),
        out_shape=(
            jax.ShapeDtypeStruct((count, features), jnp.float32),
            jax.ShapeDtypeStruct((count, features), jnp.bfloat16),
        ),
        in_specs=[vmem()] * 2,
        out_specs=(vmem(), vmem()),
        cost_estimate=pl.CostEstimate(
            flops=4 * count * down_w.size, bytes_accessed=2 * down_w.size, transcendentals=0
        ),
        compiler_params=pltpu.CompilerParams(vmem_limit_bytes=24 << 20),
    )(hidden, down_w)


def rotate_kernel(count, *refs):
    total_ref, *arrived = refs[: count + 1]
    sign_ref, out_ref = refs[count + 1 :]
    rows, features = total_ref.shape
    common = lax.broadcasted_iota(jnp.int32, (BLOCK, BLOCK), 0) & lax.broadcasted_iota(
        jnp.int32, (BLOCK, BLOCK), 1
    )
    for shift in (4, 2, 1):
        common = common ^ (common >> shift)
    flips = (1 - 2 * (common & 1)).astype(jnp.float32).astype(jnp.bfloat16)
    scale = 1.0 / math.sqrt(BLOCK)
    value = total_ref[...]
    for piece in arrived:
        value = value + piece[...].astype(jnp.float32)
    value = value * sign_ref[...].astype(jnp.float32)
    value = jnp.concatenate([value[:, b : b + BLOCK] for b in range(0, features, BLOCK)])
    high = value.astype(jnp.bfloat16)
    low = (value - high.astype(jnp.float32)).astype(jnp.bfloat16)
    turned = jnp.dot(high, flips, preferred_element_type=jnp.float32)
    turned = (turned + jnp.dot(low, flips, preferred_element_type=jnp.float32)) * scale
    for b in range(features // BLOCK):
        out_ref[:, b * BLOCK : (b + 1) * BLOCK] = turned[b * rows : (b + 1) * rows].astype(jnp.bfloat16)


def rotate(total, arrived, signs):
    features = signs.shape[0]
    return pl.pallas_call(
        functools.partial(rotate_kernel, len(arrived)),
        out_shape=jax.ShapeDtypeStruct(total.shape, jnp.bfloat16),
        in_specs=[vmem()] * (len(arrived) + 2),
        out_specs=vmem(),
        compiler_params=pltpu.CompilerParams(vmem_limit_bytes=16 << 20),
    )(total, *arrived, signs.reshape(1, features))


def solution(mesh):
    members = mesh.shape["gx"]
    assert members & (members - 1) == 0 and members >= 16

    square = (4, 2, 6)
    far = []
    mask = members // 2
    while mask > 4:
        far.append(mask)
        mask //= 2
    others = members // 8 - 1

    def swap(value, mask):
        return lax.ppermute(value, "gx", [(i, i ^ mask) for i in range(members)])

    def on_device(tokens, gate_weight, up_weight, down_weight, sign_pattern):
        rows = tokens.shape[0]
        gate_up_w, down_w = fetch(gate_weight.T, up_weight.T, down_weight)

        away = []
        for mask in far:
            away.append(swap(jnp.concatenate([tokens] + away), mask))
        away = jnp.concatenate(away)
        own_there = jnp.concatenate([swap(tokens, m) for m in square])
        away_there = jnp.concatenate([swap(away, m) for m in square])
        pieces = [tokens, own_there, away, away_there]
        gathered = jnp.concatenate(pieces + [swap(piece, 1) for piece in pieces])
        hidden = hidden_units(gate_up_w, gathered)

        near, half = 4 * rows, members // 2 * rows
        away_keep, away_send = down(hidden, down_w, near, half + near, 4 * others * rows)
        own_keep, own_send = down(hidden, down_w, 0, half, near)

        def scatter(keep, send, count):
            total = keep + swap(send, 1).astype(jnp.float32)
            leave = total[count:].astype(jnp.bfloat16)
            arrived = [swap(leave[k * count : (k + 1) * count], m) for k, m in enumerate(square)]
            return total[:count], arrived

        total, arrived = scatter(away_keep, away_send, others * rows)
        for piece in arrived:
            total = total + piece.astype(jnp.float32)
        own, arrived = scatter(own_keep, own_send, rows)
        for mask in reversed(far):
            split = total.shape[0] // 2 // rows * rows
            piece = swap(total[split:].astype(jnp.bfloat16), mask)
            arrived.append(piece[:rows])
            total = total[:split] + piece[rows:].astype(jnp.float32)
        return rotate(own, arrived, sign_pattern)

    placed = (P(("groups", "gx"), None), P(None, "gx"), P(None, "gx"), P("gx", None), P())
    return jax.shard_map(
        on_device, mesh=mesh, in_specs=placed, out_specs=P(("groups", "gx"), None), check_vma=False
    )
```

time: 146 us -> 58 us (0.40)
  waiting for transfers between devices: 118 us -> 22.4 us
  starting transfers between devices: 0.04 us -> 19.8 us
  Pallas kernels: 0 us -> 13.9 us
  matrix products: 13.3 us -> 0 us
  between operations: 13.4 us -> 0.23 us
    reduce_scatter x1 -> x0, waiting for transfers between devices: 70.6 us -> none  [on_device(): lax.psum_scatter(partial_value, 'gx', scatter_dimension=0, tiled=True)]
    all_gather x1 -> x0, waiting for transfers between devices: 46.3 us -> none  [on_device(): gathered = lax.all_gather(tokens, 'gx', axis=0, tiled=True)]
    ppermute x0 -> x20, waiting for transfers between devices: none -> 22.4 us  [swap(): return lax.ppermute(value, 'gx', [(i, i ^ mask) for i in range(members)])]
    ppermute x0 -> x20, starting transfers between devices: none -> 19.8 us  [swap(): return lax.ppermute(value, 'gx', [(i, i ^ mask) for i in range(members)])]
    pallas_call x0 -> x5, Pallas kernels: none -> 13.9 us  [the longest x2 5.36 us: down(): pl.pallas_call(functools.partial(down_kernel, own, other), out_shape=(jax...]
    dot_general x3 -> x0, matrix products: 13.3 us -> none  [the longest x1 7.99 us: on_device(): jnp.dot(hidden, down_weight, preferred_element_type=jnp.float32)]
  transfers between devices with their start and end apart: 2 -> 20, of which waited for: 2 -> 10; matrix products, arithmetic and copies ran while one was open for 0% -> 3% of each run, Pallas kernels for 0% -> 12%
where the time goes in v5:
time: 58 us; the launch traced here: 57.8 us
  waiting for transfers between devices  22.4 us (39%)
  starting transfers between devices  19.8 us (34%)
  Pallas kernels  13.9 us (24%)
  local copies, waits for them, and re-layouts  1.17 us (2%)
    ppermute x20, waiting for transfers between devices, swap(): return lax.ppermute(value, 'gx', [(i, i ^ mask) for i in range(members)])  22.4 us
    ppermute x20, starting transfers between devices, swap(): return lax.ppermute(value, 'gx', [(i, i ^ mask) for i in range(members)])  19.8 us
    pallas_call x2, Pallas kernels, down(): pl.pallas_call(functools.partial(down_kernel, own, other), out_shape=(jax...  5.36 us
    pallas_call x1, Pallas kernels, fetch(): pl.pallas_call(fetch_kernel, out_shape=(jax.ShapeDtypeStruct((2 * units,...  4.23 us
    pallas_call x1, Pallas kernels, hidden_units(): pl.pallas_call(hidden_kernel, out_shape=jax.ShapeDtypeStruct((count, unit...  3.36 us
  transfers between devices with their start and end apart: 20, of which 10 were waited for; matrix products, arithmetic and copies ran while one was open for 3% of the time, Pallas kernels for 12%

profile of v5, /device:TPU:0, one launch (start us, length us, event | category | flops | bytes accessed | tf_op | source)
XLA Modules:
  0.0 57.8 jit_solution(13441673582452021237)
XLA Ops:
  0.0 4.0 %collective-permute-start.3 = (bf16[8,8192]{1,0:T(8,128)(2,1)}, bf16[8,8192]{1,0:T(8,128)(2,1)S(1)}, u32[]{:S(2)}, u32[]{:S(2)}) collective-permute-start(bf16[8,8192]{1,0:T(8,128)(2,1)} %param.5), channel_id=1, source_target_pairs={{0,8},{1,9},{2,10},{3,11},{4,12},{5,13},{6,14},{7,15},{8,0},{9,1},... | collective-permute-start | bytes 393224 | tf_op jit(solution)/shard_map/ppermute | solution.py:161
  4.0 2.5 %collective-permute-start.2 = (bf16[8,8192]{1,0:T(8,128)(2,1)}, bf16[8,8192]{1,0:T(8,128)(2,1)S(1)}, u32[]{:S(2)}, u32[]{:S(2)}) collective-permute-start(bf16[8,8192]{1,0:T(8,128)(2,1)} %param.5), channel_id=1, source_target_pairs={{0,6},{1,7},{2,4},{3,5},{4,2},{5,3},{6,0},{7,1},{8,14},{9,15},{10,... | collective-permute-start | bytes 393224 | tf_op jit(solution)/shard_map/ppermute | solution.py:161
  6.6 0.5 collective-permute-start.1
  7.1 0.4 collective-permute-start
  7.5 0.0 collective-permute-start.7
  7.5 0.9 %constant_dynamic-update-slice_fusion.11 = bf16[128,8192]{1,0:T(8,128)(2,1)S(1)} fusion(bf16[8,8192]{1,0:T(8,128)(2,1)} %param.5), kind=kLoop, calls=%fused_computation.19 | loop fusion | bytes 262144
  8.5 4.2 %shard_map.55 = (bf16[448,8192]{1,0:T(8,128)(2,1)S(1)}, bf16[224,8192]{1,0:T(8,128)(2,1)S(1)}) custom-call(bf16[224,8192]{1,0:T(8,128)(2,1)} %bitcast.4, bf16[224,8192]{1,0:T(8,128)(2,1)} %bitcast.5, bf16[224,8192]{1,0:T(8,128)(2,1)} %down_hbm.1), custom_call_target="tpu_custom_call" | custom-call | bytes 11010048 | tf_op jit(solution)/shard_map/pallas_call | solution.py:34
  12.7 0.0 collective-permute-done.2
  12.7 0.2 collective-permute-done.1
  12.9 1.7 %collective-permute-done = bf16[8,8192]{1,0:T(8,128)(2,1)S(1)} collective-permute-done((bf16[8,8192]{1,0:T(8,128)(2,1)}, bf16[8,8192]{1,0:T(8,128)(2,1)S(1)}, u32[]{:S(2)}, u32[]{:S(2)}) %collective-permute-start) | collective-permute-done | bytes 131104 | tf_op jit(solution)/shard_map/ppermute | solution.py:161
  14.6 0.1 collective-permute-start.8
  14.7 0.0 collective-permute-done.3
  14.7 1.5 %collective-permute-start.6 = (bf16[8,8192]{1,0:T(8,128)(2,1)S(1)}, bf16[8,8192]{1,0:T(8,128)(2,1)S(1)}, u32[]{:S(2)}, u32[]{:S(2)}) collective-permute-start(bf16[8,8192]{1,0:T(8,128)(2,1)S(1)} %collective-permute-done.3), channel_id=1, source_target_pairs={{0,6},{1,7},{2,4},{3,5},{4,2},{5,3},{6,0},{7,1},{8,14},{9,15},{10,... | collective-permute-start | bytes 393224 | tf_op jit(solution)/shard_map/ppermute | solution.py:161
  16.2 0.6 %collective-permute-start.5 = (bf16[8,8192]{1,0:T(8,128)(2,1)S(1)}, bf16[8,8192]{1,0:T(8,128)(2,1)S(1)}, u32[]{:S(2)}, u32[]{:S(2)}) collective-permute-start(bf16[8,8192]{1,0:T(8,128)(2,1)S(1)} %collective-permute-done.3), channel_id=1, source_target_pairs={{0,2},{1,3},{2,0},{3,1},{4,6},{5,7},{6,4},{7,5},{8,10},{9,11},{10,... | collective-permute-start | bytes 393224 | tf_op jit(solution)/shard_map/ppermute | solution.py:161
  16.8 1.4 %collective-permute-start.4 = (bf16[8,8192]{1,0:T(8,128)(2,1)S(1)}, bf16[8,8192]{1,0:T(8,128)(2,1)S(1)}, u32[]{:S(2)}, u32[]{:S(2)}) collective-permute-start(bf16[8,8192]{1,0:T(8,128)(2,1)S(1)} %collective-permute-done.3), channel_id=1, source_target_pairs={{0,4},{1,5},{2,6},{3,7},{4,0},{5,1},{6,2},{7,3},{8,12},{9,13},{10,... | collective-permute-start | bytes 393224 | tf_op jit(solution)/shard_map/ppermute | solution.py:161
  18.4 3.7 %collective-permute-done.6 = bf16[8,8192]{1,0:T(8,128)(2,1)S(1)} collective-permute-done((bf16[8,8192]{1,0:T(8,128)(2,1)S(1)}, bf16[8,8192]{1,0:T(8,128)(2,1)S(1)}, u32[]{:S(2)}, u32[]{:S(2)}) %collective-permute-start.6) | collective-permute-done | bytes 131104 | tf_op jit(solution)/shard_map/ppermute | solution.py:161
  22.0 0.0 collective-permute-start.9
  22.0 2.3 %collective-permute-done.5 = bf16[8,8192]{1,0:T(8,128)(2,1)S(1)} collective-permute-done((bf16[8,8192]{1,0:T(8,128)(2,1)S(1)}, bf16[8,8192]{1,0:T(8,128)(2,1)S(1)}, u32[]{:S(2)}, u32[]{:S(2)}) %collective-permute-start.5) | collective-permute-done | bytes 131104 | tf_op jit(solution)/shard_map/ppermute | solution.py:161
  24.3 0.0 collective-permute-done.4
  24.4 0.1 collective-permute-start.10
  24.5 0.0 collective-permute-done.7
  24.6 0.0 collective-permute-done.8
  24.6 0.0 collective-permute-done.9
  24.6 1.5 %collective-permute-done.10 = bf16[24,8192]{1,0:T(8,128)(2,1)S(1)} collective-permute-done((bf16[24,8192]{1,0:T(8,128)(2,1)S(1)}, bf16[24,8192]{1,0:T(8,128)(2,1)S(1)}, u32[]{:S(2)}, u32[]{:S(2)}) %collective-permute-start.10) | collective-permute-done | bytes 393248 | tf_op jit(solution)/shard_map/ppermute | solution.py:161
  26.2 3.4 %shard_map.56.hidden_ref = bf16[128,224]{1,0:T(8,128)(2,1)S(1)} custom-call(bf16[448,8192]{1,0:T(8,128)(2,1)S(1)} %get-tuple-element.11.weights_ref, bf16[128,8192]{1,0:T(8,128)(2,1)S(1)} %constant_dynamic-update-slice_fusion.rows_ref), custom_call_target="tpu_custom_call" | custom-call | flops 939524096 | bytes 7340032 | tf_op jit(solution)/shard_map/pallas_call | solution.py:68
  29.6 2.7 %shard_map.58 = (f32[32,8192]{1,0:T(8,128)S(1)}, bf16[32,8192]{1,0:T(8,128)(2,1)S(1)}) custom-call(bf16[128,224]{1,0:T(8,128)(2,1)S(1)} %shard_map.56.hidden_ref, bf16[224,8192]{1,0:T(8,128)(2,1)S(1)} %get-tuple-element.12.down_ref), custom_call_target="tpu_custom_call" | custom-call | flops 234881024 | bytes 3670016 | tf_op jit(solution)/shard_map/pallas_call | solution.py:98
  32.3 0.2 collective-permute-start.15
  32.5 2.7 %shard_map.57 = (f32[32,8192]{1,0:T(8,128)S(1)}, bf16[32,8192]{1,0:T(8,128)(2,1)S(1)}) custom-call(bf16[128,224]{1,0:T(8,128)(2,1)S(1)} %shard_map.56.hidden_ref, bf16[224,8192]{1,0:T(8,128)(2,1)S(1)} %get-tuple-element.12.down_ref), custom_call_target="tpu_custom_call" | custom-call | flops 234881024 | bytes 3670016 | tf_op jit(solution)/shard_map/pallas_call | solution.py:98
  35.1 0.4 collective-permute-start.11
  35.6 0.0 collective-permute-done.15
  35.6 0.1 fusion.3
  35.7 0.7 %collective-permute-start.16 = (bf16[8,8192]{1,0:T(8,128)(2,1)S(1)}, bf16[8,8192]{1,0:T(8,128)(2,1)S(1)}, u32[]{:S(2)}, u32[]{:S(2)}) collective-permute-start(bf16[8,8192]{1,0:T(8,128)(2,1)S(1)} %get-tuple-element.21), channel_id=1, source_target_pairs={{0,4},{1,5},{2,6},{3,7},{4,0},{5,1},{6,2},{7,3},{8,12},{9,13},{10,... | collective-permute-start | bytes 393224 | tf_op jit(solution)/shard_map/ppermute | solution.py:161
  36.4 1.5 %collective-permute-start.18 = (bf16[8,8192]{1,0:T(8,128)(2,1)S(1)}, bf16[8,8192]{1,0:T(8,128)(2,1)S(1)}, u32[]{:S(2)}, u32[]{:S(2)}) collective-permute-start(bf16[8,8192]{1,0:T(8,128)(2,1)S(1)} %get-tuple-element.22), channel_id=1, source_target_pairs={{0,6},{1,7},{2,4},{3,5},{4,2},{5,3},{6,0},{7,1},{8,14},{9,15},{10,... | collective-permute-start | bytes 393224 | tf_op jit(solution)/shard_map/ppermute | solution.py:161
  37.9 1.4 %collective-permute-start.17 = (bf16[8,8192]{1,0:T(8,128)(2,1)S(1)}, bf16[8,8192]{1,0:T(8,128)(2,1)S(1)}, u32[]{:S(2)}, u32[]{:S(2)}) collective-permute-start(bf16[8,8192]{1,0:T(8,128)(2,1)S(1)} %get-tuple-element.23), channel_id=1, source_target_pairs={{0,2},{1,3},{2,0},{3,1},{4,6},{5,7},{6,4},{7,5},{8,10},{9,11},{10,... | collective-permute-start | bytes 393224 | tf_op jit(solution)/shard_map/ppermute | solution.py:161
  39.3 0.0 collective-permute-done.11
  39.3 0.0 copy-start
  39.3 0.1 fusion.4
  39.5 1.5 %collective-permute-start.14 = (bf16[8,8192]{1,0:T(8,128)(2,1)S(1)}, bf16[8,8192]{1,0:T(8,128)(2,1)S(1)}, u32[]{:S(2)}, u32[]{:S(2)}) collective-permute-start(bf16[8,8192]{1,0:T(8,128)(2,1)S(1)} %get-tuple-element.24), channel_id=1, source_target_pairs={{0,6},{1,7},{2,4},{3,5},{4,2},{5,3},{6,0},{7,1},{8,14},{9,15},{10,... | collective-permute-start | bytes 393224 | tf_op jit(solution)/shard_map/ppermute | solution.py:161
  41.0 0.6 %collective-permute-start.13 = (bf16[8,8192]{1,0:T(8,128)(2,1)S(1)}, bf16[8,8192]{1,0:T(8,128)(2,1)S(1)}, u32[]{:S(2)}, u32[]{:S(2)}) collective-permute-start(bf16[8,8192]{1,0:T(8,128)(2,1)S(1)} %get-tuple-element.25), channel_id=1, source_target_pairs={{0,2},{1,3},{2,0},{3,1},{4,6},{5,7},{6,4},{7,5},{8,10},{9,11},{10,... | collective-permute-start | bytes 393224 | tf_op jit(solution)/shard_map/ppermute | solution.py:161
  41.6 0.6 collective-permute-done.16
  42.2 0.9 %collective-permute-start.12 = (bf16[8,8192]{1,0:T(8,128)(2,1)S(1)}, bf16[8,8192]{1,0:T(8,128)(2,1)S(1)}, u32[]{:S(2)}, u32[]{:S(2)}) collective-permute-start(bf16[8,8192]{1,0:T(8,128)(2,1)S(1)} %get-tuple-element.26), channel_id=1, source_target_pairs={{0,4},{1,5},{2,6},{3,7},{4,0},{5,1},{6,2},{7,3},{8,12},{9,13},{10,... | collective-permute-start | bytes 393224 | tf_op jit(solution)/shard_map/ppermute | solution.py:161
  43.0 2.1 %collective-permute-done.18 = bf16[8,8192]{1,0:T(8,128)(2,1)S(1)} collective-permute-done((bf16[8,8192]{1,0:T(8,128)(2,1)S(1)}, bf16[8,8192]{1,0:T(8,128)(2,1)S(1)}, u32[]{:S(2)}, u32[]{:S(2)}) %collective-permute-start.18) | collective-permute-done | bytes 131104 | tf_op jit(solution)/shard_map/ppermute | solution.py:161
  45.1 4.4 %collective-permute-done.17 = bf16[8,8192]{1,0:T(8,128)(2,1)S(1)} collective-permute-done((bf16[8,8192]{1,0:T(8,128)(2,1)S(1)}, bf16[8,8192]{1,0:T(8,128)(2,1)S(1)}, u32[]{:S(2)}, u32[]{:S(2)}) %collective-permute-start.17) | collective-permute-done | bytes 131104 | tf_op jit(solution)/shard_map/ppermute | solution.py:161
  49.5 0.1 fusion.2
  49.5 1.4 %collective-permute-start.19 = (bf16[8,8192]{1,0:T(8,128)(2,1)S(1)}, bf16[8,8192]{1,0:T(8,128)(2,1)S(1)}, u32[]{:S(2)}, u32[]{:S(2)}) collective-permute-start(bf16[8,8192]{1,0:T(8,128)(2,1)S(1)} %fusion.2), channel_id=1, source_target_pairs={{0,8},{1,9},{2,10},{3,11},{4,12},{5,13},{6,14},{7,15},{8,0},{9,1},... | collective-permute-start | bytes 393224 | tf_op jit(solution)/shard_map/ppermute | solution.py:161
  51.0 0.0 collective-permute-done.14.refs_3_
  51.0 0.3 collective-permute-done.13.refs_2_
  51.3 0.0 collective-permute-done.12.refs_1_
  51.3 5.6 %collective-permute-done.19.refs_4_ = bf16[8,8192]{1,0:T(8,128)(2,1)S(1)} collective-permute-done((bf16[8,8192]{1,0:T(8,128)(2,1)S(1)}, bf16[8,8192]{1,0:T(8,128)(2,1)S(1)}, u32[]{:S(2)}, u32[]{:S(2)}) %collective-permute-start.19) | collective-permute-done | bytes 131104 | tf_op jit(solution)/shard_map/ppermute | solution.py:161
  56.9 0.0 copy-done
  56.9 0.9 %shard_map.59 = bf16[8,8192]{1,0:T(8,128)(2,1)} custom-call(f32[8,8192]{1,0:T(8,128)S(1)} %slice.42.refs_0_, bf16[8,8192]{1,0:T(8,128)(2,1)S(1)} %collective-permute-done.12.refs_1_, bf16[8,8192]{1,0:T(8,128)(2,1)S(1)} %collective-permute-done.13.refs_2_, bf16[8,8192]{1,0:T(8,128)(2,1)S(1)} %collective-permute-done.14.refs_3_, ...), custom_call_target="tpu_custom_call" | custom-call | tf_op jit(solution)/shard_map/pallas_call | solution.py:139
  (16 shorter events, 0.3 us)
Async XLA Ops:
  0.0 14.7 %collective-permute-start.3 = (bf16[8,8192]{1,0:T(8,128)(2,1)}, bf16[8,8192]{1,0:T(8,128)(2,1)S(1)}, u32[]{:S(2)}, u32[]{:S(2)}) collective-permute-start(bf16[8,8192]{1,0:T(8,128)(2,1)} %param.5), channel_id=1, source_target_pairs={{0,8},{1,9},{2,10},{3,11},{4,12},{5,13},{6,14},{7,15},{8,0},{9,1},... | collective-permute-start | bytes 393224 | tf_op jit(solution)/shard_map/ppermute | solution.py:161
  4.0 8.7 %collective-permute-start.2 = (bf16[8,8192]{1,0:T(8,128)(2,1)}, bf16[8,8192]{1,0:T(8,128)(2,1)S(1)}, u32[]{:S(2)}, u32[]{:S(2)}) collective-permute-start(bf16[8,8192]{1,0:T(8,128)(2,1)} %param.5), channel_id=1, source_target_pairs={{0,6},{1,7},{2,4},{3,5},{4,2},{5,3},{6,0},{7,1},{8,14},{9,15},{10,... | collective-permute-start | bytes 393224 | tf_op jit(solution)/shard_map/ppermute | solution.py:161
  6.6 6.3 %collective-permute-start.1 = (bf16[8,8192]{1,0:T(8,128)(2,1)}, bf16[8,8192]{1,0:T(8,128)(2,1)S(1)}, u32[]{:S(2)}, u32[]{:S(2)}) collective-permute-start(bf16[8,8192]{1,0:T(8,128)(2,1)} %param.5), channel_id=1, source_target_pairs={{0,2},{1,3},{2,0},{3,1},{4,6},{5,7},{6,4},{7,5},{8,10},{9,11},{10,... | collective-permute-start | bytes 393224 | tf_op jit(solution)/shard_map/ppermute | solution.py:161
  7.1 7.5 %collective-permute-start = (bf16[8,8192]{1,0:T(8,128)(2,1)}, bf16[8,8192]{1,0:T(8,128)(2,1)S(1)}, u32[]{:S(2)}, u32[]{:S(2)}) collective-permute-start(bf16[8,8192]{1,0:T(8,128)(2,1)} %param.5), channel_id=1, source_target_pairs={{0,4},{1,5},{2,6},{3,7},{4,0},{5,1},{6,2},{7,3},{8,12},{9,13},{10,... | collective-permute-start | bytes 393224 | tf_op jit(solution)/shard_map/ppermute | solution.py:161
  7.5 17.0 %collective-permute-start.7 = (bf16[8,8192]{1,0:T(8,128)(2,1)}, bf16[8,8192]{1,0:T(8,128)(2,1)S(1)}, u32[]{:S(2)}, u32[]{:S(2)}) collective-permute-start(bf16[8,8192]{1,0:T(8,128)(2,1)} %param.5), channel_id=1, source_target_pairs={{0,1},{1,0},{2,3},{3,2},{4,5},{5,4},{6,7},{7,6},{8,9},{9,8},{10,11... | collective-permute-start | bytes 393224 | tf_op jit(solution)/shard_map/ppermute | solution.py:161
  14.6 9.9 %collective-permute-start.8 = (bf16[24,8192]{1,0:T(8,128)(2,1)S(1)}, bf16[24,8192]{1,0:T(8,128)(2,1)S(1)}, u32[]{:S(2)}, u32[]{:S(2)}) collective-permute-start(bf16[24,8192]{1,0:T(8,128)(2,1)S(1)} %pad_maximum_fusion), channel_id=1, source_target_pairs={{0,1},{1,0},{2,3},{3,2},{4,5},{5,4},{6,7},{7,6},{8,9},{9,8},{10,11... | collective-permute-start | bytes 1179656 | tf_op jit(solution)/shard_map/ppermute | solution.py:161
  14.7 7.3 %collective-permute-start.6 = (bf16[8,8192]{1,0:T(8,128)(2,1)S(1)}, bf16[8,8192]{1,0:T(8,128)(2,1)S(1)}, u32[]{:S(2)}, u32[]{:S(2)}) collective-permute-start(bf16[8,8192]{1,0:T(8,128)(2,1)S(1)} %collective-permute-done.3), channel_id=1, source_target_pairs={{0,6},{1,7},{2,4},{3,5},{4,2},{5,3},{6,0},{7,1},{8,14},{9,15},{10,... | collective-permute-start | bytes 393224 | tf_op jit(solution)/shard_map/ppermute | solution.py:161
  16.2 8.1 %collective-permute-start.5 = (bf16[8,8192]{1,0:T(8,128)(2,1)S(1)}, bf16[8,8192]{1,0:T(8,128)(2,1)S(1)}, u32[]{:S(2)}, u32[]{:S(2)}) collective-permute-start(bf16[8,8192]{1,0:T(8,128)(2,1)S(1)} %collective-permute-done.3), channel_id=1, source_target_pairs={{0,2},{1,3},{2,0},{3,1},{4,6},{5,7},{6,4},{7,5},{8,10},{9,11},{10,... | collective-permute-start | bytes 393224 | tf_op jit(solution)/shard_map/ppermute | solution.py:161
  16.8 7.5 %collective-permute-start.4 = (bf16[8,8192]{1,0:T(8,128)(2,1)S(1)}, bf16[8,8192]{1,0:T(8,128)(2,1)S(1)}, u32[]{:S(2)}, u32[]{:S(2)}) collective-permute-start(bf16[8,8192]{1,0:T(8,128)(2,1)S(1)} %collective-permute-done.3), channel_id=1, source_target_pairs={{0,4},{1,5},{2,6},{3,7},{4,0},{5,1},{6,2},{7,3},{8,12},{9,13},{10,... | collective-permute-start | bytes 393224 | tf_op jit(solution)/shard_map/ppermute | solution.py:161
  22.0 2.6 %collective-permute-start.9 = (bf16[8,8192]{1,0:T(8,128)(2,1)S(1)}, bf16[8,8192]{1,0:T(8,128)(2,1)S(1)}, u32[]{:S(2)}, u32[]{:S(2)}) collective-permute-start(bf16[8,8192]{1,0:T(8,128)(2,1)S(1)} %collective-permute-done.3), channel_id=1, source_target_pairs={{0,1},{1,0},{2,3},{3,2},{4,5},{5,4},{6,7},{7,6},{8,9},{9,8},{10,11... | collective-permute-start | bytes 393224 | tf_op jit(solution)/shard_map/ppermute | solution.py:161
  24.4 1.8 %collective-permute-start.10 = (bf16[24,8192]{1,0:T(8,128)(2,1)S(1)}, bf16[24,8192]{1,0:T(8,128)(2,1)S(1)}, u32[]{:S(2)}, u32[]{:S(2)}) collective-permute-start(bf16[24,8192]{1,0:T(8,128)(2,1)S(1)} %pad_maximum_fusion.1), channel_id=1, source_target_pairs={{0,1},{1,0},{2,3},{3,2},{4,5},{5,4},{6,7},{7,6},{8,9},{9,8},{10,11... | collective-permute-start | bytes 1179656 | tf_op jit(solution)/shard_map/ppermute | solution.py:161
  32.3 3.3 %collective-permute-start.15 = (bf16[32,8192]{1,0:T(8,128)(2,1)S(1)}, bf16[32,8192]{1,0:T(8,128)(2,1)S(1)}, u32[]{:S(2)}, u32[]{:S(2)}) collective-permute-start(bf16[32,8192]{1,0:T(8,128)(2,1)S(1)} %get-tuple-element.16), channel_id=1, source_target_pairs={{0,1},{1,0},{2,3},{3,2},{4,5},{5,4},{6,7},{7,6},{8,9},{9,8},{10,11... | collective-permute-start | bytes 1572872 | tf_op jit(solution)/shard_map/ppermute | solution.py:161
  35.1 4.2 %collective-permute-start.11 = (bf16[32,8192]{1,0:T(8,128)(2,1)S(1)}, bf16[32,8192]{1,0:T(8,128)(2,1)S(1)}, u32[]{:S(2)}, u32[]{:S(2)}) collective-permute-start(bf16[32,8192]{1,0:T(8,128)(2,1)S(1)} %get-tuple-element.14), channel_id=1, source_target_pairs={{0,1},{1,0},{2,3},{3,2},{4,5},{5,4},{6,7},{7,6},{8,9},{9,8},{10,11... | collective-permute-start | bytes 1572872 | tf_op jit(solution)/shard_map/ppermute | solution.py:161
  35.7 6.4 %collective-permute-start.16 = (bf16[8,8192]{1,0:T(8,128)(2,1)S(1)}, bf16[8,8192]{1,0:T(8,128)(2,1)S(1)}, u32[]{:S(2)}, u32[]{:S(2)}) collective-permute-start(bf16[8,8192]{1,0:T(8,128)(2,1)S(1)} %get-tuple-element.21), channel_id=1, source_target_pairs={{0,4},{1,5},{2,6},{3,7},{4,0},{5,1},{6,2},{7,3},{8,12},{9,13},{10,... | collective-permute-start | bytes 393224 | tf_op jit(solution)/shard_map/ppermute | solution.py:161
  36.4 8.7 %collective-permute-start.18 = (bf16[8,8192]{1,0:T(8,128)(2,1)S(1)}, bf16[8,8192]{1,0:T(8,128)(2,1)S(1)}, u32[]{:S(2)}, u32[]{:S(2)}) collective-permute-start(bf16[8,8192]{1,0:T(8,128)(2,1)S(1)} %get-tuple-element.22), channel_id=1, source_target_pairs={{0,6},{1,7},{2,4},{3,5},{4,2},{5,3},{6,0},{7,1},{8,14},{9,15},{10,... | collective-permute-start | bytes 393224 | tf_op jit(solution)/shard_map/ppermute | solution.py:161
  37.9 11.6 %collective-permute-start.17 = (bf16[8,8192]{1,0:T(8,128)(2,1)S(1)}, bf16[8,8192]{1,0:T(8,128)(2,1)S(1)}, u32[]{:S(2)}, u32[]{:S(2)}) collective-permute-start(bf16[8,8192]{1,0:T(8,128)(2,1)S(1)} %get-tuple-element.23), channel_id=1, source_target_pairs={{0,2},{1,3},{2,0},{3,1},{4,6},{5,7},{6,4},{7,5},{8,10},{9,11},{10,... | collective-permute-start | bytes 393224 | tf_op jit(solution)/shard_map/ppermute | solution.py:161
  39.3 17.6 %copy-start = (s32[8192]{0:T(1024)S(1)}, s32[8192]{0:T(1024)}, u32[]{:S(2)}) copy-start(s32[8192]{0:T(1024)} %param.9) | copy-start | bytes 98308
  39.5 11.5 %collective-permute-start.14 = (bf16[8,8192]{1,0:T(8,128)(2,1)S(1)}, bf16[8,8192]{1,0:T(8,128)(2,1)S(1)}, u32[]{:S(2)}, u32[]{:S(2)}) collective-permute-start(bf16[8,8192]{1,0:T(8,128)(2,1)S(1)} %get-tuple-element.24), channel_id=1, source_target_pairs={{0,6},{1,7},{2,4},{3,5},{4,2},{5,3},{6,0},{7,1},{8,14},{9,15},{10,... | collective-permute-start | bytes 393224 | tf_op jit(solution)/shard_map/ppermute | solution.py:161
  41.0 10.3 %collective-permute-start.13 = (bf16[8,8192]{1,0:T(8,128)(2,1)S(1)}, bf16[8,8192]{1,0:T(8,128)(2,1)S(1)}, u32[]{:S(2)}, u32[]{:S(2)}) collective-permute-start(bf16[8,8192]{1,0:T(8,128)(2,1)S(1)} %get-tuple-element.25), channel_id=1, source_target_pairs={{0,2},{1,3},{2,0},{3,1},{4,6},{5,7},{6,4},{7,5},{8,10},{9,11},{10,... | collective-permute-start | bytes 393224 | tf_op jit(solution)/shard_map/ppermute | solution.py:161
  42.2 9.1 %collective-permute-start.12 = (bf16[8,8192]{1,0:T(8,128)(2,1)S(1)}, bf16[8,8192]{1,0:T(8,128)(2,1)S(1)}, u32[]{:S(2)}, u32[]{:S(2)}) collective-permute-start(bf16[8,8192]{1,0:T(8,128)(2,1)S(1)} %get-tuple-element.26), channel_id=1, source_target_pairs={{0,4},{1,5},{2,6},{3,7},{4,0},{5,1},{6,2},{7,3},{8,12},{9,13},{10,... | collective-permute-start | bytes 393224 | tf_op jit(solution)/shard_map/ppermute | solution.py:161
  49.5 7.3 %collective-permute-start.19 = (bf16[8,8192]{1,0:T(8,128)(2,1)S(1)}, bf16[8,8192]{1,0:T(8,128)(2,1)S(1)}, u32[]{:S(2)}, u32[]{:S(2)}) collective-permute-start(bf16[8,8192]{1,0:T(8,128)(2,1)S(1)} %fusion.2), channel_id=1, source_target_pairs={{0,8},{1,9},{2,10},{3,11},{4,12},{5,13},{6,14},{7,15},{8,0},{9,1},... | collective-permute-start | bytes 393224 | tf_op jit(solution)/shard_map/ppermute | solution.py:161

commit v6 on v5

v6 whole, which is shorter than its diff:
```python
import functools
import math

import jax
import jax.numpy as jnp
from jax import lax
from jax.experimental import pallas as pl
from jax.experimental.pallas import tpu as pltpu
from jax.sharding import PartitionSpec as P

BLOCK = 128
NT = (((1,), (1,)), ((), ()))


def vmem():
    return pl.BlockSpec(memory_space=pltpu.VMEM)


def fetch_kernel(gate_hbm, up_hbm, down_hbm, _, gate_up_ref, down_ref, sems):
    units = gate_hbm.shape[0]
    copies = [
        pltpu.make_async_copy(gate_hbm, gate_up_ref.at[:units], sems.at[0]),
        pltpu.make_async_copy(up_hbm, gate_up_ref.at[units:], sems.at[1]),
        pltpu.make_async_copy(down_hbm, down_ref, sems.at[2]),
    ]
    for copy in copies:
        copy.start()
    for copy in copies:
        copy.wait()


def fetch(gate_w, up_w, down_w, after):
    units, features = gate_w.shape
    return pl.pallas_call(
        fetch_kernel,
        out_shape=(
            jax.ShapeDtypeStruct((2 * units, features), gate_w.dtype),
            jax.ShapeDtypeStruct(down_w.shape, down_w.dtype),
        ),
        in_specs=[pl.BlockSpec(memory_space=pltpu.HBM)] * 3 + [pl.BlockSpec(memory_space=pl.ANY)],
        out_specs=(vmem(),) * 2,
        scratch_shapes=[pltpu.SemaphoreType.DMA((3,))],
        cost_estimate=pl.CostEstimate(flops=0, bytes_accessed=6 * units * features, transcendentals=0),
        compiler_params=pltpu.CompilerParams(vmem_limit_bytes=24 << 20),
    )(*(pltpu.with_memory_space_constraint(w, pltpu.HBM) for w in (gate_w, up_w, down_w)), after)


def product(weights_ref, start, here_ref, there_ref):
    width = here_ref.shape[1]
    tile = math.gcd(width, 1024)
    total = None
    for first in range(0, width, tile):
        rows = jnp.concatenate([here_ref[:, first : first + tile], there_ref[:, first : first + tile]])
        span = weights_ref[:, start + first : start + first + tile]
        part = lax.dot_general(rows, span, NT, preferred_element_type=jnp.float32)
        total = part if total is None else total + part
    return total


def sums_kernel(weights_ref, here_ref, there_ref, sums_ref):
    sums_ref[...] = product(weights_ref, 0, here_ref, there_ref)


def hidden_kernel(weights_ref, here_ref, there_ref, sums_ref, hidden_ref):
    total = sums_ref[...] + product(weights_ref, here_ref.shape[1], here_ref, there_ref)
    units = total.shape[1] // 2
    gate = total[:, :units]
    hidden_ref[...] = (gate / (1.0 + jnp.exp(-gate)) * total[:, units:]).astype(jnp.bfloat16)


def hidden_units(weights, halves):
    units, width = weights.shape[0] // 2, halves[0][0].shape[1]
    count = 2 * halves[0][0].shape[0]
    cost = pl.CostEstimate(
        flops=4 * units * count * width, bytes_accessed=4 * units * width, transcendentals=0
    )
    params = pltpu.CompilerParams(vmem_limit_bytes=24 << 20)
    sums = pl.pallas_call(
        sums_kernel,
        out_shape=jax.ShapeDtypeStruct((count, 2 * units), jnp.float32),
        in_specs=[vmem()] * 3,
        out_specs=vmem(),
        cost_estimate=cost,
        compiler_params=params,
    )(weights, *halves[0])
    return pl.pallas_call(
        hidden_kernel,
        out_shape=jax.ShapeDtypeStruct((count, units), jnp.bfloat16),
        in_specs=[vmem()] * 4,
        out_specs=vmem(),
        cost_estimate=cost,
        compiler_params=params,
    )(weights, *halves[1], sums)


def down_kernel(hidden_ref, down_ref, keep_ref, near_ref, far_ref):
    half, features = keep_ref.shape
    near = near_ref.shape[0]
    tile = math.gcd(features, 512)
    for first in range(0, features, tile):
        here = slice(first, first + tile)
        part = jnp.dot(hidden_ref[...], down_ref[:, here], preferred_element_type=jnp.float32)
        keep_ref[:, here] = part[:half]
        near_ref[:, here] = part[half : half + near].astype(jnp.bfloat16)
        far_ref[:, here] = part[half + near :].astype(jnp.bfloat16)


def down(hidden, down_w, near):
    units, features = down_w.shape
    count = hidden.shape[0]
    half = count // 2
    return pl.pallas_call(
        down_kernel,
        out_shape=(
            jax.ShapeDtypeStruct((half, features), jnp.float32),
            jax.ShapeDtypeStruct((near, features), jnp.bfloat16),
            jax.ShapeDtypeStruct((half - near, features), jnp.bfloat16),
        ),
        in_specs=[vmem()] * 2,
        out_specs=(vmem(),) * 3,
        cost_estimate=pl.CostEstimate(
            flops=2 * count * units * features, bytes_accessed=2 * units * features, transcendentals=0
        ),
        compiler_params=pltpu.CompilerParams(vmem_limit_bytes=24 << 20),
    )(hidden, down_w)


def rotate_kernel(count, *refs):
    total_ref, *arrived = refs[: count + 1]
    sign_ref, out_ref = refs[count + 1 :]
    rows, features = total_ref.shape
    common = lax.broadcasted_iota(jnp.int32, (BLOCK, BLOCK), 0) & lax.broadcasted_iota(
        jnp.int32, (BLOCK, BLOCK), 1
    )
    for shift in (4, 2, 1):
        common = common ^ (common >> shift)
    flips = (1 - 2 * (common & 1)).astype(jnp.float32).astype(jnp.bfloat16)
    scale = 1.0 / math.sqrt(BLOCK)
    value = total_ref[...]
    for piece in arrived:
        value = value + piece[...].astype(jnp.float32)
    value = value * sign_ref[...].astype(jnp.float32)
    value = jnp.concatenate([value[:, b : b + BLOCK] for b in range(0, features, BLOCK)])
    high = value.astype(jnp.bfloat16)
    low = (value - high.astype(jnp.float32)).astype(jnp.bfloat16)
    turned = jnp.dot(high, flips, preferred_element_type=jnp.float32)
    turned = (turned + jnp.dot(low, flips, preferred_element_type=jnp.float32)) * scale
    for b in range(features // BLOCK):
        out_ref[:, b * BLOCK : (b + 1) * BLOCK] = turned[b * rows : (b + 1) * rows].astype(jnp.bfloat16)


def rotate(total, arrived, signs):
    features = signs.shape[0]
    return pl.pallas_call(
        functools.partial(rotate_kernel, len(arrived)),
        out_shape=jax.ShapeDtypeStruct(total.shape, jnp.bfloat16),
        in_specs=[vmem()] * (len(arrived) + 2),
        out_specs=vmem(),
        compiler_params=pltpu.CompilerParams(vmem_limit_bytes=16 << 20),
    )(total, *arrived, signs.reshape(1, features))


def solution(mesh):
    members = mesh.shape["gx"]
    assert members & (members - 1) == 0 and members >= 16

    square = ((4, 2), (2, 4), (6, 6))
    far = []
    mask = members // 2
    while mask > 4:
        far.append((mask, mask))
        mask //= 2
    others = members // 8 - 1

    def swap(value, masks):
        return lax.ppermute(value, "gx", [(i, i ^ masks[i % 2]) for i in range(members)])

    def on_device(tokens, gate_weight, up_weight, down_weight, sign_pattern):
        rows, features = tokens.shape

        away = []
        for masks in far:
            away.append(swap(jnp.concatenate([tokens] + away), masks))
        away = jnp.concatenate(away)
        first = [swap(tokens, m) for m in square] + [away]
        second = [swap(away, m) for m in square[::-1]]
        gate_up_w, down_w = fetch(gate_weight.T, up_weight.T, down_weight, away)
        gate_up_w, *gathered = lax.optimization_barrier((gate_up_w, *first, *second))
        gathered = [tokens, *gathered]
        halves = []
        for part in (slice(None, features // 2), slice(features // 2, None)):
            half = jnp.concatenate([piece[:, part] for piece in gathered])
            halves.append((half, swap(half, (1, 1))))
        hidden = hidden_units(gate_up_w, halves)

        near = 4 * rows
        keep, near_send, far_send = down(hidden, down_w, near)

        far_there, near_send = lax.optimization_barrier((swap(far_send, (1, 1)), near_send))
        near_there = swap(near_send, (1, 1))
        total = keep[near:] + far_there.astype(jnp.float32)
        count = others * rows
        leave = total[count:].astype(jnp.bfloat16)
        arrived = [swap(leave[k * count : (k + 1) * count], m) for k, m in enumerate(square[::-1])]
        near_there, arrived[0] = lax.optimization_barrier((near_there, arrived[0]))
        total = total[:count]
        for piece in arrived:
            total = total + piece.astype(jnp.float32)
        arrived = []
        for masks in reversed(far):
            split = total.shape[0] // 2 // rows * rows
            piece = swap(total[split:].astype(jnp.bfloat16), masks)
            arrived.append(piece[:rows])
            total = total[:split] + piece[rows:].astype(jnp.float32)

        total = keep[:near] + near_there.astype(jnp.float32)
        total = total[: 2 * rows] + swap(total[2 * rows :].astype(jnp.bfloat16), square[1]).astype(jnp.float32)
        arrived.append(swap(total[rows:].astype(jnp.bfloat16), square[0]))
        return rotate(total[:rows], arrived, sign_pattern)

    placed = (P(("groups", "gx"), None), P(None, "gx"), P(None, "gx"), P("gx", None), P())
    return jax.shard_map(
        on_device, mesh=mesh, in_specs=placed, out_specs=P(("groups", "gx"), None), check_vma=False
    )
```

time: 58 us -> 49.6 us (0.86)
  Pallas kernels: 13.9 us -> 8.36 us
  waiting for transfers between devices: 22.4 us -> 19.4 us
    pallas_call x2, Pallas kernels: 5.36 us -> 1.92 us  [the longest x1 1.21 us: hidden_units(): pl.pallas_call(sums_kernel, out_shape=jax.ShapeDtypeStruct((count, 2 * un...]
    ppermute x20 -> x17, waiting for transfers between devices: 22.4 us -> 19.4 us  [swap(): lax.ppermute(value, 'gx', [(i, i ^ masks[i % 2]) for i in range(members)])]
    pallas_call x1, Pallas kernels: 3.36 us -> 1.3 us  [hidden_units(): pl.pallas_call(hidden_kernel, out_shape=jax.ShapeDtypeStruct((count, unit...]
    ppermute x20 -> x17, starting transfers between devices: 19.8 us -> 20 us  [swap(): lax.ppermute(value, 'gx', [(i, i ^ masks[i % 2]) for i in range(members)])]
  transfers between devices with their start and end apart: 20 -> 17, of which waited for: 10 -> 9; matrix products, arithmetic and copies ran while one was open for 3% -> 3% of each run, Pallas kernels for 12% -> 11%
where the time goes in v6:
time: 49.6 us; the launch traced here: 49.4 us
  starting transfers between devices  20 us (40%)
  waiting for transfers between devices  19.4 us (39%)
  Pallas kernels  8.36 us (17%)
  local copies, waits for them, and re-layouts  1.06 us (2%)
    ppermute x17, starting transfers between devices, swap(): lax.ppermute(value, 'gx', [(i, i ^ masks[i % 2]) for i in range(members)])  20 us
    ppermute x17, waiting for transfers between devices, swap(): lax.ppermute(value, 'gx', [(i, i ^ masks[i % 2]) for i in range(members)])  19.4 us
    pallas_call x1, Pallas kernels, fetch(): pl.pallas_call(fetch_kernel, out_shape=(jax.ShapeDtypeStruct((2 * units,...  4.23 us
    pallas_call x1, Pallas kernels, hidden_units(): pl.pallas_call(hidden_kernel, out_shape=jax.ShapeDtypeStruct((count, unit...  1.3 us
    pallas_call x1, Pallas kernels, hidden_units(): pl.pallas_call(sums_kernel, out_shape=jax.ShapeDtypeStruct((count, 2 * un...  1.21 us
  transfers between devices with their start and end apart: 17, of which 9 were waited for; matrix products, arithmetic and copies ran while one was open for 3% of the time, Pallas kernels for 11%

profile of v6, /device:TPU:0, one launch (start us, length us, event | category | flops | bytes accessed | tf_op | source)
XLA Modules:
  0.0 49.4 jit_solution(17964329392521666393)
XLA Ops:
  0.0 4.0 %collective-permute-start = (bf16[8,8192]{1,0:T(8,128)(2,1)}, bf16[8,8192]{1,0:T(8,128)(2,1)S(1)}, u32[]{:S(2)}, u32[]{:S(2)}) collective-permute-start(bf16[8,8192]{1,0:T(8,128)(2,1)} %param.5), channel_id=1, source_target_pairs={{0,8},{1,9},{2,10},{3,11},{4,12},{5,13},{6,14},{7,15},{8,0},{9,1},... | collective-permute-start | bytes 393224 | tf_op jit(solution)/shard_map/ppermute | solution.py:176
  4.0 1.5 %collective-permute-start.2 = (bf16[8,8192]{1,0:T(8,128)(2,1)}, bf16[8,8192]{1,0:T(8,128)(2,1)S(1)}, u32[]{:S(2)}, u32[]{:S(2)}) collective-permute-start(bf16[8,8192]{1,0:T(8,128)(2,1)} %param.5), channel_id=1, source_target_pairs={{0,2},{1,5},{2,0},{3,7},{4,6},{5,1},{6,4},{7,3},{8,10},{9,13},{10,... | collective-permute-start | bytes 393224 | tf_op jit(solution)/shard_map/ppermute | solution.py:176
  5.6 1.6 %collective-permute-start.1 = (bf16[8,8192]{1,0:T(8,128)(2,1)}, bf16[8,8192]{1,0:T(8,128)(2,1)S(1)}, u32[]{:S(2)}, u32[]{:S(2)}) collective-permute-start(bf16[8,8192]{1,0:T(8,128)(2,1)} %param.5), channel_id=1, source_target_pairs={{0,4},{1,3},{2,6},{3,1},{4,0},{5,7},{6,2},{7,5},{8,12},{9,11},{10,... | collective-permute-start | bytes 393224 | tf_op jit(solution)/shard_map/ppermute | solution.py:176
  7.1 0.4 collective-permute-start.3
  7.5 3.1 %collective-permute-done._ = bf16[8,8192]{1,0:T(8,128)(2,1)S(1)} collective-permute-done((bf16[8,8192]{1,0:T(8,128)(2,1)}, bf16[8,8192]{1,0:T(8,128)(2,1)S(1)}, u32[]{:S(2)}, u32[]{:S(2)}) %collective-permute-start) | collective-permute-done | bytes 131104 | tf_op jit(solution)/shard_map/ppermute | solution.py:176
  10.6 0.8 %collective-permute-start.6 = (bf16[8,8192]{1,0:T(8,128)(2,1)S(1)}, bf16[8,8192]{1,0:T(8,128)(2,1)S(1)}, u32[]{:S(2)}, u32[]{:S(2)}) collective-permute-start(bf16[8,8192]{1,0:T(8,128)(2,1)S(1)} %collective-permute-done._), channel_id=1, source_target_pairs={{0,4},{1,3},{2,6},{3,1},{4,0},{5,7},{6,2},{7,5},{8,12},{9,11},{10,... | collective-permute-start | bytes 393224 | tf_op jit(solution)/shard_map/ppermute | solution.py:176
  11.4 1.5 %collective-permute-start.5 = (bf16[8,8192]{1,0:T(8,128)(2,1)S(1)}, bf16[8,8192]{1,0:T(8,128)(2,1)S(1)}, u32[]{:S(2)}, u32[]{:S(2)}) collective-permute-start(bf16[8,8192]{1,0:T(8,128)(2,1)S(1)} %collective-permute-done._), channel_id=1, source_target_pairs={{0,2},{1,5},{2,0},{3,7},{4,6},{5,1},{6,4},{7,3},{8,10},{9,13},{10,... | collective-permute-start | bytes 393224 | tf_op jit(solution)/shard_map/ppermute | solution.py:176
  12.9 0.0 collective-permute-done.2
  12.9 1.2 %collective-permute-start.4 = (bf16[8,8192]{1,0:T(8,128)(2,1)S(1)}, bf16[8,8192]{1,0:T(8,128)(2,1)S(1)}, u32[]{:S(2)}, u32[]{:S(2)}) collective-permute-start(bf16[8,8192]{1,0:T(8,128)(2,1)S(1)} %collective-permute-done._), channel_id=1, source_target_pairs={{0,6},{1,7},{2,4},{3,5},{4,2},{5,3},{6,0},{7,1},{8,14},{9,15},{10,... | collective-permute-start | bytes 393224 | tf_op jit(solution)/shard_map/ppermute | solution.py:176
  14.1 0.9 %slice_dynamic-update-slice_fusion.7 = (bf16[64,4096]{1,0:T(8,128)(2,1)S(1)}, bf16[64,4096]{1,0:T(8,128)(2,1)S(1)}) fusion(bf16[8,8192]{1,0:T(8,128)(2,1)} %param.5), kind=kLoop, calls=%fused_computation.16 | loop fusion | bytes 262144
  15.0 4.2 %shard_map.55 = (bf16[448,8192]{1,0:T(8,128)(2,1)S(1)}, bf16[224,8192]{1,0:T(8,128)(2,1)S(1)}) custom-call(bf16[224,8192]{1,0:T(8,128)(2,1)} %bitcast.4, bf16[224,8192]{1,0:T(8,128)(2,1)} %bitcast.5, bf16[224,8192]{1,0:T(8,128)(2,1)} %down_hbm.1, bf16[8,8192]{1,0:T(8,128)(2,1)S(1)} %collective-permute-done._), custom_call_target="tpu_custom_call" | custom-call | bytes 11010048 | tf_op jit(solution)/shard_map/pallas_call | solution.py:34
  19.3 0.0 collective-permute-done.1
  19.3 0.0 collective-permute-done.3
  19.3 0.0 collective-permute-done.6
  19.3 0.0 collective-permute-done.5
  19.3 1.3 %collective-permute-done.4 = bf16[8,8192]{1,0:T(8,128)(2,1)S(1)} collective-permute-done((bf16[8,8192]{1,0:T(8,128)(2,1)S(1)}, bf16[8,8192]{1,0:T(8,128)(2,1)S(1)}, u32[]{:S(2)}, u32[]{:S(2)}) %collective-permute-start.4) | collective-permute-done | bytes 131104 | tf_op jit(solution)/shard_map/ppermute | solution.py:176
  20.7 0.1 collective-permute-start.8
  20.8 0.5 %collective-permute-start.7 = (bf16[64,4096]{1,0:T(8,128)(2,1)S(1)}, bf16[64,4096]{1,0:T(8,128)(2,1)S(1)}, u32[]{:S(2)}, u32[]{:S(2)}) collective-permute-start(bf16[64,4096]{1,0:T(8,128)(2,1)S(1)} %get-tuple-element.45.here_ref), channel_id=1, source_target_pairs={{0,1},{1,0},{2,3},{3,2},{4,5},{5,4},{6,7},{7,6},{8,9},{9,8},{10,11... | collective-permute-start | bytes 1572872 | tf_op jit(solution)/shard_map/ppermute | solution.py:176
  21.3 1.4 %collective-permute-done.8.there_ref = bf16[64,4096]{1,0:T(8,128)(2,1)S(1)} collective-permute-done((bf16[64,4096]{1,0:T(8,128)(2,1)S(1)}, bf16[64,4096]{1,0:T(8,128)(2,1)S(1)}, u32[]{:S(2)}, u32[]{:S(2)}) %collective-permute-start.8) | collective-permute-done | bytes 524320 | tf_op jit(solution)/shard_map/ppermute | solution.py:176
  22.7 1.2 %shard_map.56.sums_ref = f32[128,448]{1,0:T(8,128)S(1)} custom-call(bf16[448,8192]{1,0:T(8,128)(2,1)S(1)} %get-tuple-element.23.weights_ref, bf16[64,4096]{1,0:T(8,128)(2,1)S(1)} %get-tuple-element.44.here_ref, bf16[64,4096]{1,0:T(8,128)(2,1)S(1)} %collective-permute-done.8.there_ref), custom_call_target="tpu_custom_call" | custom-call | flops 469762048 | bytes 3670016 | tf_op jit(solution)/shard_map/pallas_call | solution.py:78
  23.9 0.0 collective-permute-done.7.there_ref
  23.9 1.3 %shard_map.57.hidden_ref = bf16[128,224]{1,0:T(8,128)(2,1)S(1)} custom-call(bf16[448,8192]{1,0:T(8,128)(2,1)S(1)} %get-tuple-element.23.weights_ref, bf16[64,4096]{1,0:T(8,128)(2,1)S(1)} %get-tuple-element.45.here_ref, bf16[64,4096]{1,0:T(8,128)(2,1)S(1)} %collective-permute-done.7.there_ref, f32[128,448]{1,0:T(8,128)S(1)} %shard_map.56.sums_ref), custom_call_target="tpu_custom_call" | custom-call | flops 469762048 | bytes 3670016 | tf_op jit(solution)/shard_map/pallas_call | solution.py:86
  25.2 0.7 %shard_map.58 = (f32[64,8192]{1,0:T(8,128)S(1)}, bf16[32,8192]{1,0:T(8,128)(2,1)S(1)}, bf16[32,8192]{1,0:T(8,128)(2,1)S(1)}) custom-call(bf16[128,224]{1,0:T(8,128)(2,1)S(1)} %shard_map.57.hidden_ref, bf16[224,8192]{1,0:T(8,128)(2,1)S(1)} %get-tuple-element.31.down_ref), custom_call_target="tpu_custom_call" | custom-call | flops 469762048 | bytes 3670016 | tf_op jit(solution)/shard_map/pallas_call | solution.py:112
  25.9 0.2 collective-permute-start.9
  26.1 1.8 %collective-permute-done.9 = bf16[32,8192]{1,0:T(8,128)(2,1)S(1)} collective-permute-done((bf16[32,8192]{1,0:T(8,128)(2,1)S(1)}, bf16[32,8192]{1,0:T(8,128)(2,1)S(1)}, u32[]{:S(2)}, u32[]{:S(2)}) %collective-permute-start.9) | collective-permute-done | bytes 524320 | tf_op jit(solution)/shard_map/ppermute | solution.py:176
  27.9 0.1 collective-permute-start.10
  28.0 0.1 fusion.3
  28.2 0.0 copy-start
  28.2 1.0 %collective-permute-start.11 = (bf16[8,8192]{1,0:T(8,128)(2,1)S(1)}, bf16[8,8192]{1,0:T(8,128)(2,1)S(1)}, u32[]{:S(2)}, u32[]{:S(2)}) collective-permute-start(bf16[8,8192]{1,0:T(8,128)(2,1)S(1)} %get-tuple-element.43), channel_id=1, source_target_pairs={{0,6},{1,7},{2,4},{3,5},{4,2},{5,3},{6,0},{7,1},{8,14},{9,15},{10,... | collective-permute-start | bytes 393224 | tf_op jit(solution)/shard_map/ppermute | solution.py:176
  29.2 1.7 %collective-permute-start.13 = (bf16[8,8192]{1,0:T(8,128)(2,1)S(1)}, bf16[8,8192]{1,0:T(8,128)(2,1)S(1)}, u32[]{:S(2)}, u32[]{:S(2)}) collective-permute-start(bf16[8,8192]{1,0:T(8,128)(2,1)S(1)} %get-tuple-element.41), channel_id=1, source_target_pairs={{0,2},{1,5},{2,0},{3,7},{4,6},{5,1},{6,4},{7,3},{8,10},{9,13},{10,... | collective-permute-start | bytes 393224 | tf_op jit(solution)/shard_map/ppermute | solution.py:176
  30.9 0.9 %collective-permute-start.14 = (bf16[8,8192]{1,0:T(8,128)(2,1)S(1)}, bf16[8,8192]{1,0:T(8,128)(2,1)S(1)}, u32[]{:S(2)}, u32[]{:S(2)}) collective-permute-start(bf16[8,8192]{1,0:T(8,128)(2,1)S(1)} %get-tuple-element.42), channel_id=1, source_target_pairs={{0,4},{1,3},{2,6},{3,1},{4,0},{5,7},{6,2},{7,5},{8,12},{9,11},{10,... | collective-permute-start | bytes 393224 | tf_op jit(solution)/shard_map/ppermute | solution.py:176
  31.8 3.7 %collective-permute-done.11 = bf16[8,8192]{1,0:T(8,128)(2,1)S(1)} collective-permute-done((bf16[8,8192]{1,0:T(8,128)(2,1)S(1)}, bf16[8,8192]{1,0:T(8,128)(2,1)S(1)}, u32[]{:S(2)}, u32[]{:S(2)}) %collective-permute-start.11) | collective-permute-done | bytes 131104 | tf_op jit(solution)/shard_map/ppermute | solution.py:176
  35.5 0.0 collective-permute-done.10
  35.5 0.1 convert_add_fusion
  35.6 0.8 %collective-permute-start.12 = (bf16[16,8192]{1,0:T(8,128)(2,1)S(1)}, bf16[16,8192]{1,0:T(8,128)(2,1)S(1)}, u32[]{:S(2)}, u32[]{:S(2)}) collective-permute-start(bf16[16,8192]{1,0:T(8,128)(2,1)S(1)} %slice.147), channel_id=1, source_target_pairs={{0,2},{1,5},{2,0},{3,7},{4,6},{5,1},{6,4},{7,3},{8,10},{9,13},{10,... | collective-permute-start | bytes 786440 | tf_op jit(solution)/shard_map/ppermute | solution.py:176
  36.4 1.3 %collective-permute-done.13 = bf16[8,8192]{1,0:T(8,128)(2,1)S(1)} collective-permute-done((bf16[8,8192]{1,0:T(8,128)(2,1)S(1)}, bf16[8,8192]{1,0:T(8,128)(2,1)S(1)}, u32[]{:S(2)}, u32[]{:S(2)}) %collective-permute-start.13) | collective-permute-done | bytes 131104 | tf_op jit(solution)/shard_map/ppermute | solution.py:176
  37.7 0.0 collective-permute-done.14
  37.7 0.1 fusion.2
  37.8 2.6 %collective-permute-start.15 = (bf16[8,8192]{1,0:T(8,128)(2,1)S(1)}, bf16[8,8192]{1,0:T(8,128)(2,1)S(1)}, u32[]{:S(2)}, u32[]{:S(2)}) collective-permute-start(bf16[8,8192]{1,0:T(8,128)(2,1)S(1)} %fusion.2), channel_id=1, source_target_pairs={{0,8},{1,9},{2,10},{3,11},{4,12},{5,13},{6,14},{7,15},{8,0},{9,1},... | collective-permute-start | bytes 393224 | tf_op jit(solution)/shard_map/ppermute | solution.py:176
  40.4 1.7 %collective-permute-done.12 = bf16[16,8192]{1,0:T(8,128)(2,1)S(1)} collective-permute-done((bf16[16,8192]{1,0:T(8,128)(2,1)S(1)}, bf16[16,8192]{1,0:T(8,128)(2,1)S(1)}, u32[]{:S(2)}, u32[]{:S(2)}) %collective-permute-start.12) | collective-permute-done | bytes 262176 | tf_op jit(solution)/shard_map/ppermute | solution.py:176
  42.1 0.1 slice_add_fusion
  42.2 1.2 %collective-permute-start.16 = (bf16[8,8192]{1,0:T(8,128)(2,1)S(1)}, bf16[8,8192]{1,0:T(8,128)(2,1)S(1)}, u32[]{:S(2)}, u32[]{:S(2)}) collective-permute-start(bf16[8,8192]{1,0:T(8,128)(2,1)S(1)} %slice.148), channel_id=1, source_target_pairs={{0,4},{1,3},{2,6},{3,1},{4,0},{5,7},{6,2},{7,5},{8,12},{9,11},{10,... | collective-permute-start | bytes 393224 | tf_op jit(solution)/shard_map/ppermute | solution.py:176
  43.4 3.8 %collective-permute-done.15.refs_1_ = bf16[8,8192]{1,0:T(8,128)(2,1)S(1)} collective-permute-done((bf16[8,8192]{1,0:T(8,128)(2,1)S(1)}, bf16[8,8192]{1,0:T(8,128)(2,1)S(1)}, u32[]{:S(2)}, u32[]{:S(2)}) %collective-permute-start.15) | collective-permute-done | bytes 131104 | tf_op jit(solution)/shard_map/ppermute | solution.py:176
  47.2 1.3 %collective-permute-done.16.refs_2_ = bf16[8,8192]{1,0:T(8,128)(2,1)S(1)} collective-permute-done((bf16[8,8192]{1,0:T(8,128)(2,1)S(1)}, bf16[8,8192]{1,0:T(8,128)(2,1)S(1)}, u32[]{:S(2)}, u32[]{:S(2)}) %collective-permute-start.16) | collective-permute-done | bytes 131104 | tf_op jit(solution)/shard_map/ppermute | solution.py:176
  48.5 0.0 copy-done
  48.5 0.9 %shard_map.59 = bf16[8,8192]{1,0:T(8,128)(2,1)} custom-call(f32[8,8192]{1,0:T(8,128)S(1)} %slice.114.refs_0_, bf16[8,8192]{1,0:T(8,128)(2,1)S(1)} %collective-permute-done.15.refs_1_, bf16[8,8192]{1,0:T(8,128)(2,1)S(1)} %collective-permute-done.16.refs_2_, s32[1,8192]{1,0:T(1,128)S(1)} %bitcast.3), custom_call_target="tpu_custom_call" | custom-call | tf_op jit(solution)/shard_map/pallas_call | solution.py:154
  (11 shorter events, 0.2 us)
Async XLA Ops:
  0.0 10.6 %collective-permute-start = (bf16[8,8192]{1,0:T(8,128)(2,1)}, bf16[8,8192]{1,0:T(8,128)(2,1)S(1)}, u32[]{:S(2)}, u32[]{:S(2)}) collective-permute-start(bf16[8,8192]{1,0:T(8,128)(2,1)} %param.5), channel_id=1, source_target_pairs={{0,8},{1,9},{2,10},{3,11},{4,12},{5,13},{6,14},{7,15},{8,0},{9,1},... | collective-permute-start | bytes 393224 | tf_op jit(solution)/shard_map/ppermute | solution.py:176
  4.0 8.9 %collective-permute-start.2 = (bf16[8,8192]{1,0:T(8,128)(2,1)}, bf16[8,8192]{1,0:T(8,128)(2,1)S(1)}, u32[]{:S(2)}, u32[]{:S(2)}) collective-permute-start(bf16[8,8192]{1,0:T(8,128)(2,1)} %param.5), channel_id=1, source_target_pairs={{0,2},{1,5},{2,0},{3,7},{4,6},{5,1},{6,4},{7,3},{8,10},{9,13},{10,... | collective-permute-start | bytes 393224 | tf_op jit(solution)/shard_map/ppermute | solution.py:176
  5.6 13.7 %collective-permute-start.1 = (bf16[8,8192]{1,0:T(8,128)(2,1)}, bf16[8,8192]{1,0:T(8,128)(2,1)S(1)}, u32[]{:S(2)}, u32[]{:S(2)}) collective-permute-start(bf16[8,8192]{1,0:T(8,128)(2,1)} %param.5), channel_id=1, source_target_pairs={{0,4},{1,3},{2,6},{3,1},{4,0},{5,7},{6,2},{7,5},{8,12},{9,11},{10,... | collective-permute-start | bytes 393224 | tf_op jit(solution)/shard_map/ppermute | solution.py:176
  7.1 12.1 %collective-permute-start.3 = (bf16[8,8192]{1,0:T(8,128)(2,1)}, bf16[8,8192]{1,0:T(8,128)(2,1)S(1)}, u32[]{:S(2)}, u32[]{:S(2)}) collective-permute-start(bf16[8,8192]{1,0:T(8,128)(2,1)} %param.5), channel_id=1, source_target_pairs={{0,6},{1,7},{2,4},{3,5},{4,2},{5,3},{6,0},{7,1},{8,14},{9,15},{10,... | collective-permute-start | bytes 393224 | tf_op jit(solution)/shard_map/ppermute | solution.py:176
  10.6 8.6 %collective-permute-start.6 = (bf16[8,8192]{1,0:T(8,128)(2,1)S(1)}, bf16[8,8192]{1,0:T(8,128)(2,1)S(1)}, u32[]{:S(2)}, u32[]{:S(2)}) collective-permute-start(bf16[8,8192]{1,0:T(8,128)(2,1)S(1)} %collective-permute-done._), channel_id=1, source_target_pairs={{0,4},{1,3},{2,6},{3,1},{4,0},{5,7},{6,2},{7,5},{8,12},{9,11},{10,... | collective-permute-start | bytes 393224 | tf_op jit(solution)/shard_map/ppermute | solution.py:176
  11.4 7.9 %collective-permute-start.5 = (bf16[8,8192]{1,0:T(8,128)(2,1)S(1)}, bf16[8,8192]{1,0:T(8,128)(2,1)S(1)}, u32[]{:S(2)}, u32[]{:S(2)}) collective-permute-start(bf16[8,8192]{1,0:T(8,128)(2,1)S(1)} %collective-permute-done._), channel_id=1, source_target_pairs={{0,2},{1,5},{2,0},{3,7},{4,6},{5,1},{6,4},{7,3},{8,10},{9,13},{10,... | collective-permute-start | bytes 393224 | tf_op jit(solution)/shard_map/ppermute | solution.py:176
  12.9 7.6 %collective-permute-start.4 = (bf16[8,8192]{1,0:T(8,128)(2,1)S(1)}, bf16[8,8192]{1,0:T(8,128)(2,1)S(1)}, u32[]{:S(2)}, u32[]{:S(2)}) collective-permute-start(bf16[8,8192]{1,0:T(8,128)(2,1)S(1)} %collective-permute-done._), channel_id=1, source_target_pairs={{0,6},{1,7},{2,4},{3,5},{4,2},{5,3},{6,0},{7,1},{8,14},{9,15},{10,... | collective-permute-start | bytes 393224 | tf_op jit(solution)/shard_map/ppermute | solution.py:176
  20.7 2.0 %collective-permute-start.8 = (bf16[64,4096]{1,0:T(8,128)(2,1)S(1)}, bf16[64,4096]{1,0:T(8,128)(2,1)S(1)}, u32[]{:S(2)}, u32[]{:S(2)}) collective-permute-start(bf16[64,4096]{1,0:T(8,128)(2,1)S(1)} %get-tuple-element.44.here_ref), channel_id=1, source_target_pairs={{0,1},{1,0},{2,3},{3,2},{4,5},{5,4},{6,7},{7,6},{8,9},{9,8},{10,11... | collective-permute-start | bytes 1572872 | tf_op jit(solution)/shard_map/ppermute | solution.py:176
  20.8 3.1 %collective-permute-start.7 = (bf16[64,4096]{1,0:T(8,128)(2,1)S(1)}, bf16[64,4096]{1,0:T(8,128)(2,1)S(1)}, u32[]{:S(2)}, u32[]{:S(2)}) collective-permute-start(bf16[64,4096]{1,0:T(8,128)(2,1)S(1)} %get-tuple-element.45.here_ref), channel_id=1, source_target_pairs={{0,1},{1,0},{2,3},{3,2},{4,5},{5,4},{6,7},{7,6},{8,9},{9,8},{10,11... | collective-permute-start | bytes 1572872 | tf_op jit(solution)/shard_map/ppermute | solution.py:176
  25.9 2.0 %collective-permute-start.9 = (bf16[32,8192]{1,0:T(8,128)(2,1)S(1)}, bf16[32,8192]{1,0:T(8,128)(2,1)S(1)}, u32[]{:S(2)}, u32[]{:S(2)}) collective-permute-start(bf16[32,8192]{1,0:T(8,128)(2,1)S(1)} %get-tuple-element.33), channel_id=1, source_target_pairs={{0,1},{1,0},{2,3},{3,2},{4,5},{5,4},{6,7},{7,6},{8,9},{9,8},{10,11... | collective-permute-start | bytes 1572872 | tf_op jit(solution)/shard_map/ppermute | solution.py:176
  27.9 7.6 %collective-permute-start.10 = (bf16[32,8192]{1,0:T(8,128)(2,1)S(1)}, bf16[32,8192]{1,0:T(8,128)(2,1)S(1)}, u32[]{:S(2)}, u32[]{:S(2)}) collective-permute-start(bf16[32,8192]{1,0:T(8,128)(2,1)S(1)} %get-tuple-element.35), channel_id=1, source_target_pairs={{0,1},{1,0},{2,3},{3,2},{4,5},{5,4},{6,7},{7,6},{8,9},{9,8},{10,11... | collective-permute-start | bytes 1572872 | tf_op jit(solution)/shard_map/ppermute | solution.py:176
  28.2 20.3 %copy-start = (s32[8192]{0:T(1024)S(1)}, s32[8192]{0:T(1024)}, u32[]{:S(2)}) copy-start(s32[8192]{0:T(1024)} %param.9) | copy-start | bytes 98308
  28.2 7.3 %collective-permute-start.11 = (bf16[8,8192]{1,0:T(8,128)(2,1)S(1)}, bf16[8,8192]{1,0:T(8,128)(2,1)S(1)}, u32[]{:S(2)}, u32[]{:S(2)}) collective-permute-start(bf16[8,8192]{1,0:T(8,128)(2,1)S(1)} %get-tuple-element.43), channel_id=1, source_target_pairs={{0,6},{1,7},{2,4},{3,5},{4,2},{5,3},{6,0},{7,1},{8,14},{9,15},{10,... | collective-permute-start | bytes 393224 | tf_op jit(solution)/shard_map/ppermute | solution.py:176
  29.2 8.6 %collective-permute-start.13 = (bf16[8,8192]{1,0:T(8,128)(2,1)S(1)}, bf16[8,8192]{1,0:T(8,128)(2,1)S(1)}, u32[]{:S(2)}, u32[]{:S(2)}) collective-permute-start(bf16[8,8192]{1,0:T(8,128)(2,1)S(1)} %get-tuple-element.41), channel_id=1, source_target_pairs={{0,2},{1,5},{2,0},{3,7},{4,6},{5,1},{6,4},{7,3},{8,10},{9,13},{10,... | collective-permute-start | bytes 393224 | tf_op jit(solution)/shard_map/ppermute | solution.py:176
  30.9 6.9 %collective-permute-start.14 = (bf16[8,8192]{1,0:T(8,128)(2,1)S(1)}, bf16[8,8192]{1,0:T(8,128)(2,1)S(1)}, u32[]{:S(2)}, u32[]{:S(2)}) collective-permute-start(bf16[8,8192]{1,0:T(8,128)(2,1)S(1)} %get-tuple-element.42), channel_id=1, source_target_pairs={{0,4},{1,3},{2,6},{3,1},{4,0},{5,7},{6,2},{7,5},{8,12},{9,11},{10,... | collective-permute-start | bytes 393224 | tf_op jit(solution)/shard_map/ppermute | solution.py:176
  35.6 6.4 %collective-permute-start.12 = (bf16[16,8192]{1,0:T(8,128)(2,1)S(1)}, bf16[16,8192]{1,0:T(8,128)(2,1)S(1)}, u32[]{:S(2)}, u32[]{:S(2)}) collective-permute-start(bf16[16,8192]{1,0:T(8,128)(2,1)S(1)} %slice.147), channel_id=1, source_target_pairs={{0,2},{1,5},{2,0},{3,7},{4,6},{5,1},{6,4},{7,3},{8,10},{9,13},{10,... | collective-permute-start | bytes 786440 | tf_op jit(solution)/shard_map/ppermute | solution.py:176
  37.8 9.4 %collective-permute-start.15 = (bf16[8,8192]{1,0:T(8,128)(2,1)S(1)}, bf16[8,8192]{1,0:T(8,128)(2,1)S(1)}, u32[]{:S(2)}, u32[]{:S(2)}) collective-permute-start(bf16[8,8192]{1,0:T(8,128)(2,1)S(1)} %fusion.2), channel_id=1, source_target_pairs={{0,8},{1,9},{2,10},{3,11},{4,12},{5,13},{6,14},{7,15},{8,0},{9,1},... | collective-permute-start | bytes 393224 | tf_op jit(solution)/shard_map/ppermute | solution.py:176
  42.2 6.3 %collective-permute-start.16 = (bf16[8,8192]{1,0:T(8,128)(2,1)S(1)}, bf16[8,8192]{1,0:T(8,128)(2,1)S(1)}, u32[]{:S(2)}, u32[]{:S(2)}) collective-permute-start(bf16[8,8192]{1,0:T(8,128)(2,1)S(1)} %slice.148), channel_id=1, source_target_pairs={{0,4},{1,3},{2,6},{3,1},{4,0},{5,7},{6,2},{7,5},{8,12},{9,11},{10,... | collective-permute-start | bytes 393224 | tf_op jit(solution)/shard_map/ppermute | solution.py:176

commit v7 on v6

v7 whole, which is shorter than its diff:
```python
import functools
import math

import jax
import jax.numpy as jnp
from jax import lax
from jax.experimental import pallas as pl
from jax.experimental.pallas import tpu as pltpu
from jax.sharding import PartitionSpec as P

BLOCK = 128
PIECES = 4
SPANS = 4
NT = (((1,), (1,)), ((), ()))


def vmem():
    return pl.BlockSpec(memory_space=pltpu.VMEM)


def fetch_kernel(gate_hbm, up_hbm, down_hbm, _, gate_up_ref, down_ref, sems):
    units = gate_hbm.shape[0]
    copies = [
        pltpu.make_async_copy(gate_hbm, gate_up_ref.at[:units], sems.at[0]),
        pltpu.make_async_copy(up_hbm, gate_up_ref.at[units:], sems.at[1]),
        pltpu.make_async_copy(down_hbm, down_ref, sems.at[2]),
    ]
    for copy in copies:
        copy.start()
    for copy in copies:
        copy.wait()


def fetch(gate_w, up_w, down_w, after):
    units, features = gate_w.shape
    return pl.pallas_call(
        fetch_kernel,
        out_shape=(
            jax.ShapeDtypeStruct((2 * units, features), gate_w.dtype),
            jax.ShapeDtypeStruct(down_w.shape, down_w.dtype),
        ),
        in_specs=[pl.BlockSpec(memory_space=pltpu.HBM)] * 3 + [pl.BlockSpec(memory_space=pl.ANY)],
        out_specs=(vmem(),) * 2,
        scratch_shapes=[pltpu.SemaphoreType.DMA((3,))],
        cost_estimate=pl.CostEstimate(flops=0, bytes_accessed=6 * units * features, transcendentals=0),
        compiler_params=pltpu.CompilerParams(vmem_limit_bytes=24 << 20),
    )(*(pltpu.with_memory_space_constraint(w, pltpu.HBM) for w in (gate_w, up_w, down_w)), after)


def hidden_kernel(start, last, weights_ref, here_ref, there_ref, *refs):
    *sums, out_ref = refs
    width = here_ref.shape[1]
    tile = math.gcd(width, 1024)
    total = sums[0][...] if sums else None
    for first in range(0, width, tile):
        rows = jnp.concatenate([here_ref[:, first : first + tile], there_ref[:, first : first + tile]])
        span = weights_ref[:, start + first : start + first + tile]
        part = lax.dot_general(rows, span, NT, preferred_element_type=jnp.float32)
        total = part if total is None else total + part
    if last:
        units = total.shape[1] // 2
        gate = total[:, :units]
        total = gate / (1.0 + jnp.exp(-gate)) * total[:, units:]
    out_ref[...] = total.astype(out_ref.dtype)


def hidden_units(weights, spans):
    units, width = weights.shape[0] // 2, spans[0][0].shape[1]
    count = 2 * spans[0][0].shape[0]
    sums = ()
    for k, span in enumerate(spans):
        last = k == len(spans) - 1
        shape = ((count, units), jnp.bfloat16) if last else ((count, 2 * units), jnp.float32)
        sums = (
            pl.pallas_call(
                functools.partial(hidden_kernel, k * width, last),
                out_shape=jax.ShapeDtypeStruct(*shape),
                in_specs=[vmem()] * (3 + len(sums)),
                out_specs=vmem(),
                cost_estimate=pl.CostEstimate(
                    flops=4 * units * count * width, bytes_accessed=4 * units * width, transcendentals=0
                ),
                compiler_params=pltpu.CompilerParams(vmem_limit_bytes=24 << 20),
            )(weights, *span, *sums),
        )
    return sums[0]


def down_kernel(hidden_ref, down_ref, *outs):
    features = down_ref.shape[1]
    tile = math.gcd(features, 512)
    for first in range(0, features, tile):
        here = slice(first, first + tile)
        part = jnp.dot(hidden_ref[...], down_ref[:, here], preferred_element_type=jnp.float32)
        row = 0
        for out in outs:
            out[:, here] = part[row : row + out.shape[0]].astype(out.dtype)
            row += out.shape[0]


def down(hidden, down_w, counts):
    units, features = down_w.shape
    return pl.pallas_call(
        down_kernel,
        out_shape=[jax.ShapeDtypeStruct((count, features), jnp.float32) for count in counts]
        + [jax.ShapeDtypeStruct((count, features), jnp.bfloat16) for count in counts],
        in_specs=[vmem()] * 2,
        out_specs=[vmem()] * (2 * len(counts)),
        cost_estimate=pl.CostEstimate(
            flops=2 * hidden.size * features, bytes_accessed=2 * units * features, transcendentals=0
        ),
        compiler_params=pltpu.CompilerParams(vmem_limit_bytes=24 << 20),
    )(hidden, down_w)


def rotate_kernel(count, *refs):
    total_ref, *arrived = refs[: count + 1]
    sign_ref, out_ref, turned_ref, sems = refs[count + 1 :]
    rows, features = total_ref.shape
    common = lax.broadcasted_iota(jnp.int32, (BLOCK, BLOCK), 0) & lax.broadcasted_iota(
        jnp.int32, (BLOCK, BLOCK), 1
    )
    for shift in (4, 2, 1):
        common = common ^ (common >> shift)
    flips = (1 - 2 * (common & 1)).astype(jnp.float32).astype(jnp.bfloat16)
    scale = 1.0 / math.sqrt(BLOCK)
    width = features // PIECES
    copies = []
    for k in range(PIECES):
        here = slice(k * width, (k + 1) * width)
        value = total_ref[:, here]
        for piece in arrived:
            value = value + piece[:, here].astype(jnp.float32)
        value = value * sign_ref[:, here].astype(jnp.float32)
        value = jnp.concatenate([value[:, b : b + BLOCK] for b in range(0, width, BLOCK)])
        high = value.astype(jnp.bfloat16)
        low = (value - high.astype(jnp.float32)).astype(jnp.bfloat16)
        turned = jnp.dot(high, flips, preferred_element_type=jnp.float32)
        turned = (turned + jnp.dot(low, flips, preferred_element_type=jnp.float32)) * scale
        for b in range(width // BLOCK):
            first = k * width + b * BLOCK
            turned_ref[:, first : first + BLOCK] = turned[b * rows : (b + 1) * rows].astype(jnp.bfloat16)
        copies.append(pltpu.make_async_copy(turned_ref.at[:, here], out_ref.at[:, here], sems.at[k]))
        copies[-1].start()
    for copy in copies:
        copy.wait()


def rotate(total, arrived, signs):
    features = signs.shape[0]
    return pl.pallas_call(
        functools.partial(rotate_kernel, len(arrived)),
        out_shape=jax.ShapeDtypeStruct(total.shape, jnp.bfloat16),
        in_specs=[vmem()] * (len(arrived) + 2),
        out_specs=pl.BlockSpec(memory_space=pl.ANY),
        scratch_shapes=[pltpu.VMEM(total.shape, jnp.bfloat16), pltpu.SemaphoreType.DMA((PIECES,))],
        compiler_params=pltpu.CompilerParams(vmem_limit_bytes=16 << 20),
    )(total, *arrived, signs.reshape(1, features))


def solution(mesh):
    members = mesh.shape["gx"]
    assert members & (members - 1) == 0 and members >= 16

    square = ((4, 2), (2, 4), (6, 6))
    far = []
    mask = members // 2
    while mask > 4:
        far.append((mask, mask))
        mask //= 2
    others = members // 8 - 1

    def swap(value, masks):
        return lax.ppermute(value, "gx", [(i, i ^ masks[i % 2]) for i in range(members)])

    def on_device(tokens, gate_weight, up_weight, down_weight, sign_pattern):
        rows, features = tokens.shape

        away = []
        for masks in far:
            away.append(swap(jnp.concatenate([tokens] + away), masks))
        away = jnp.concatenate(away)
        near = [swap(tokens, m) for m in square]
        there = [swap(away, m) for m in square]
        gate_up_w, down_w = fetch(gate_weight.T, up_weight.T, down_weight, away)
        gate_up_w, *near, there[0], there[1], there[2] = lax.optimization_barrier((gate_up_w, *near, *there))
        gathered = [tokens, *near, there[2], away, *there[:2]]
        spans = []
        width = features // SPANS
        for k in range(SPANS):
            span = jnp.concatenate([piece[:, k * width : (k + 1) * width] for piece in gathered])
            spans.append((span, swap(span, (1, 1))))
        hidden = hidden_units(gate_up_w, spans)

        count = others * rows
        own, diagonal, rest, *sends = down(hidden, down_w, (4 * rows, count, 3 * count))
        diagonal = diagonal + swap(sends[1], (1, 1)).astype(jnp.float32)
        diagonal = swap(diagonal.astype(jnp.bfloat16), square[2])
        rest_there, sends[0] = lax.optimization_barrier((swap(sends[2], (1, 1)), sends[0]))
        rest = rest + rest_there.astype(jnp.float32)
        leave = rest[count:].astype(jnp.bfloat16)
        total = rest[:count]
        for piece in (diagonal, swap(leave[:count], square[0]), swap(leave[count:], square[1])):
            total = total + piece.astype(jnp.float32)
        arrived = []
        for masks in reversed(far):
            split = total.shape[0] // 2 // rows * rows
            piece = swap(total[split:].astype(jnp.bfloat16), masks)
            arrived.append(piece[:rows])
            total = total[:split] + piece[rows:].astype(jnp.float32)

        own = own + swap(sends[0], (1, 1)).astype(jnp.float32)
        own = own[: 2 * rows] + swap(own[2 * rows :].astype(jnp.bfloat16), square[1]).astype(jnp.float32)
        arrived.append(swap(own[rows:].astype(jnp.bfloat16), square[0]))
        return rotate(own[:rows], arrived, sign_pattern)

    placed = (P(("groups", "gx"), None), P(None, "gx"), P(None, "gx"), P("gx", None), P())
    return jax.shard_map(
        on_device, mesh=mesh, in_specs=placed, out_specs=P(("groups", "gx"), None), check_vma=False
    )
```

time: 49.6 us -> 47.8 us (0.964)
  waiting for transfers between devices: 19.4 us -> 17.1 us
    ppermute x17 -> x20, waiting for transfers between devices: 19.4 us -> 17.1 us  [swap(): lax.ppermute(value, 'gx', [(i, i ^ masks[i % 2]) for i in range(members)])]
    ppermute x17 -> x20, starting transfers between devices: 20 us -> 20.4 us  [swap(): lax.ppermute(value, 'gx', [(i, i ^ masks[i % 2]) for i in range(members)])]
    pallas_call x3 -> x5, Pallas kernels: 3.22 us -> 3.48 us  [the longest x4 2.77 us: hidden_units(): pl.pallas_call(functools.partial(hidden_kernel, k * width, last), out_sha...]
  transfers between devices with their start and end apart: 17 -> 20, of which waited for: 9 -> 10; matrix products, arithmetic and copies ran while one was open for 3% -> 3% of each run, Pallas kernels for 11% -> 13%
where the time goes in v7:
time: 47.8 us; the launch traced here: 47.6 us
  starting transfers between devices  20.4 us (43%)
  waiting for transfers between devices  17.1 us (36%)
  Pallas kernels  8.63 us (18%)
  local copies, waits for them, and re-layouts  0.99 us (2%)
    ppermute x20, starting transfers between devices, swap(): lax.ppermute(value, 'gx', [(i, i ^ masks[i % 2]) for i in range(members)])  20.4 us
    ppermute x20, waiting for transfers between devices, swap(): lax.ppermute(value, 'gx', [(i, i ^ masks[i % 2]) for i in range(members)])  17.1 us
    pallas_call x1, Pallas kernels, fetch(): pl.pallas_call(fetch_kernel, out_shape=(jax.ShapeDtypeStruct((2 * units,...  4.23 us
    pallas_call x4, Pallas kernels, hidden_units(): pl.pallas_call(functools.partial(hidden_kernel, k * width, last), out_sha...  2.77 us
  transfers between devices with their start and end apart: 20, of which 10 were waited for; matrix products, arithmetic and copies ran while one was open for 3% of the time, Pallas kernels for 13%

profile of v7, /device:TPU:0, one launch (start us, length us, event | category | flops | bytes accessed | tf_op | source)
XLA Modules:
  0.0 47.6 jit_solution(17379709622500256773)
XLA Ops:
  0.0 4.0 %collective-permute-start = (bf16[8,8192]{1,0:T(8,128)(2,1)}, bf16[8,8192]{1,0:T(8,128)(2,1)S(1)}, u32[]{:S(2)}, u32[]{:S(2)}) collective-permute-start(bf16[8,8192]{1,0:T(8,128)(2,1)} %param.5), channel_id=1, source_target_pairs={{0,8},{1,9},{2,10},{3,11},{4,12},{5,13},{6,14},{7,15},{8,0},{9,1},... | collective-permute-start | bytes 393224 | tf_op jit(solution)/shard_map/ppermute | solution.py:174
  4.0 1.5 %collective-permute-start.2 = (bf16[8,8192]{1,0:T(8,128)(2,1)}, bf16[8,8192]{1,0:T(8,128)(2,1)S(1)}, u32[]{:S(2)}, u32[]{:S(2)}) collective-permute-start(bf16[8,8192]{1,0:T(8,128)(2,1)} %param.5), channel_id=1, source_target_pairs={{0,2},{1,5},{2,0},{3,7},{4,6},{5,1},{6,4},{7,3},{8,10},{9,13},{10,... | collective-permute-start | bytes 393224 | tf_op jit(solution)/shard_map/ppermute | solution.py:174
  5.6 1.6 %collective-permute-start.1 = (bf16[8,8192]{1,0:T(8,128)(2,1)}, bf16[8,8192]{1,0:T(8,128)(2,1)S(1)}, u32[]{:S(2)}, u32[]{:S(2)}) collective-permute-start(bf16[8,8192]{1,0:T(8,128)(2,1)} %param.5), channel_id=1, source_target_pairs={{0,4},{1,3},{2,6},{3,1},{4,0},{5,7},{6,2},{7,5},{8,12},{9,11},{10,... | collective-permute-start | bytes 393224 | tf_op jit(solution)/shard_map/ppermute | solution.py:174
  7.1 0.4 collective-permute-start.3
  7.5 3.1 %collective-permute-done._ = bf16[8,8192]{1,0:T(8,128)(2,1)S(1)} collective-permute-done((bf16[8,8192]{1,0:T(8,128)(2,1)}, bf16[8,8192]{1,0:T(8,128)(2,1)S(1)}, u32[]{:S(2)}, u32[]{:S(2)}) %collective-permute-start) | collective-permute-done | bytes 131104 | tf_op jit(solution)/shard_map/ppermute | solution.py:174
  10.6 1.7 %collective-permute-start.6 = (bf16[8,8192]{1,0:T(8,128)(2,1)S(1)}, bf16[8,8192]{1,0:T(8,128)(2,1)S(1)}, u32[]{:S(2)}, u32[]{:S(2)}) collective-permute-start(bf16[8,8192]{1,0:T(8,128)(2,1)S(1)} %collective-permute-done._), channel_id=1, source_target_pairs={{0,6},{1,7},{2,4},{3,5},{4,2},{5,3},{6,0},{7,1},{8,14},{9,15},{10,... | collective-permute-start | bytes 393224 | tf_op jit(solution)/shard_map/ppermute | solution.py:174
  12.4 0.5 %collective-permute-start.5 = (bf16[8,8192]{1,0:T(8,128)(2,1)S(1)}, bf16[8,8192]{1,0:T(8,128)(2,1)S(1)}, u32[]{:S(2)}, u32[]{:S(2)}) collective-permute-start(bf16[8,8192]{1,0:T(8,128)(2,1)S(1)} %collective-permute-done._), channel_id=1, source_target_pairs={{0,2},{1,5},{2,0},{3,7},{4,6},{5,1},{6,4},{7,3},{8,10},{9,13},{10,... | collective-permute-start | bytes 393224 | tf_op jit(solution)/shard_map/ppermute | solution.py:174
  12.9 0.0 collective-permute-done.2
  12.9 1.2 %collective-permute-start.4 = (bf16[8,8192]{1,0:T(8,128)(2,1)S(1)}, bf16[8,8192]{1,0:T(8,128)(2,1)S(1)}, u32[]{:S(2)}, u32[]{:S(2)}) collective-permute-start(bf16[8,8192]{1,0:T(8,128)(2,1)S(1)} %collective-permute-done._), channel_id=1, source_target_pairs={{0,4},{1,3},{2,6},{3,1},{4,0},{5,7},{6,2},{7,5},{8,12},{9,11},{10,... | collective-permute-start | bytes 393224 | tf_op jit(solution)/shard_map/ppermute | solution.py:174
  14.1 0.8 %constant_dynamic-update-slice_fusion.31 = (bf16[64,2048]{1,0:T(8,128)(2,1)S(1)}, bf16[64,2048]{1,0:T(8,128)(2,1)S(1)}, bf16[64,2048]{1,0:T(8,128)(2,1)S(1)}, bf16[64,2048]{1,0:T(8,128)(2,1)S(1)}) fusion(bf16[8,8192]{1,0:T(8,128)(2,1)} %param.5), kind=kLoop, calls=%fused_computation.41 | loop fusion | bytes 262144
  15.0 4.2 %shard_map.55 = (bf16[448,8192]{1,0:T(8,128)(2,1)S(1)}, bf16[224,8192]{1,0:T(8,128)(2,1)S(1)}) custom-call(bf16[224,8192]{1,0:T(8,128)(2,1)} %bitcast.4, bf16[224,8192]{1,0:T(8,128)(2,1)} %bitcast.5, bf16[224,8192]{1,0:T(8,128)(2,1)} %down_hbm.1, bf16[8,8192]{1,0:T(8,128)(2,1)S(1)} %collective-permute-done._), custom_call_target="tpu_custom_call" | custom-call | bytes 11010048 | tf_op jit(solution)/shard_map/pallas_call | solution.py:36
  19.2 0.0 collective-permute-done.1
  19.2 0.0 collective-permute-done.3
  19.2 0.0 collective-permute-done.6
  19.2 1.3 %collective-permute-done.5 = bf16[8,8192]{1,0:T(8,128)(2,1)S(1)} collective-permute-done((bf16[8,8192]{1,0:T(8,128)(2,1)S(1)}, bf16[8,8192]{1,0:T(8,128)(2,1)S(1)}, u32[]{:S(2)}, u32[]{:S(2)}) %collective-permute-start.5) | collective-permute-done | bytes 131104 | tf_op jit(solution)/shard_map/ppermute | solution.py:174
  20.6 0.0 collective-permute-done.4
  20.7 0.1 collective-permute-start.10
  20.8 0.5 %collective-permute-start.9 = (bf16[64,2048]{1,0:T(8,128)(2,1)S(1)}, bf16[64,2048]{1,0:T(8,128)(2,1)S(1)}, u32[]{:S(2)}, u32[]{:S(2)}) collective-permute-start(bf16[64,2048]{1,0:T(8,128)(2,1)S(1)} %get-tuple-element.44.here_ref), channel_id=1, source_target_pairs={{0,1},{1,0},{2,3},{3,2},{4,5},{5,4},{6,7},{7,6},{8,9},{9,8},{10,11... | collective-permute-start | bytes 786440 | tf_op jit(solution)/shard_map/ppermute | solution.py:174
  21.3 0.1 collective-permute-start.8
  21.4 0.4 collective-permute-start.7
  21.8 0.5 %collective-permute-done.10.there_ref = bf16[64,2048]{1,0:T(8,128)(2,1)S(1)} collective-permute-done((bf16[64,2048]{1,0:T(8,128)(2,1)S(1)}, bf16[64,2048]{1,0:T(8,128)(2,1)S(1)}, u32[]{:S(2)}, u32[]{:S(2)}) %collective-permute-start.10) | collective-permute-done | bytes 262176 | tf_op jit(solution)/shard_map/ppermute | solution.py:174
  22.3 0.7 %shard_map.56.refs_0_ = f32[128,448]{1,0:T(8,128)S(1)} custom-call(bf16[448,8192]{1,0:T(8,128)(2,1)S(1)} %get-tuple-element.23.weights_ref, bf16[64,2048]{1,0:T(8,128)(2,1)S(1)} %get-tuple-element.43.here_ref, bf16[64,2048]{1,0:T(8,128)(2,1)S(1)} %collective-permute-done.10.there_ref), custom_call_target="tpu_custom_call" | custom-call | flops 234881024 | bytes 1835008 | tf_op jit(solution)/shard_map/pallas_call | solution.py:75
  23.0 0.0 collective-permute-done.9.there_ref
  23.0 0.7 %shard_map.57.refs_0_ = f32[128,448]{1,0:T(8,128)S(1)} custom-call(bf16[448,8192]{1,0:T(8,128)(2,1)S(1)} %get-tuple-element.23.weights_ref, bf16[64,2048]{1,0:T(8,128)(2,1)S(1)} %get-tuple-element.44.here_ref, bf16[64,2048]{1,0:T(8,128)(2,1)S(1)} %collective-permute-done.9.there_ref, f32[128,448]{1,0:T(8,128)S(1)} %shard_map.56.refs_0_), custom_call_target="tpu_custom_call" | custom-call | flops 234881024 | bytes 1835008 | tf_op jit(solution)/shard_map/pallas_call | solution.py:75
  23.7 0.0 collective-permute-done.8.there_ref
  23.7 0.7 %shard_map.58.refs_0_ = f32[128,448]{1,0:T(8,128)S(1)} custom-call(bf16[448,8192]{1,0:T(8,128)(2,1)S(1)} %get-tuple-element.23.weights_ref, bf16[64,2048]{1,0:T(8,128)(2,1)S(1)} %get-tuple-element.45.here_ref, bf16[64,2048]{1,0:T(8,128)(2,1)S(1)} %collective-permute-done.8.there_ref, f32[128,448]{1,0:T(8,128)S(1)} %shard_map.57.refs_0_), custom_call_target="tpu_custom_call" | custom-call | flops 234881024 | bytes 1835008 | tf_op jit(solution)/shard_map/pallas_call | solution.py:75
  24.4 0.0 collective-permute-done.7.there_ref
  24.4 0.8 %shard_map.59.hidden_ref = bf16[128,224]{1,0:T(8,128)(2,1)S(1)} custom-call(bf16[448,8192]{1,0:T(8,128)(2,1)S(1)} %get-tuple-element.23.weights_ref, bf16[64,2048]{1,0:T(8,128)(2,1)S(1)} %get-tuple-element.46.here_ref, bf16[64,2048]{1,0:T(8,128)(2,1)S(1)} %collective-permute-done.7.there_ref, f32[128,448]{1,0:T(8,128)S(1)} %shard_map.58.refs_0_), custom_call_target="tpu_custom_call" | custom-call | flops 234881024 | bytes 1835008 | tf_op jit(solution)/shard_map/pallas_call | solution.py:75
  25.1 0.7 %shard_map.60 = (f32[32,8192]{1,0:T(8,128)S(1)}, f32[8,8192]{1,0:T(8,128)S(1)}, f32[24,8192]{1,0:T(8,128)S(1)}, bf16[32,8192]{1,0:T(8,128)(2,1)S(1)}, bf16[8,819...) custom-call(bf16[128,224]{1,0:T(8,128)(2,1)S(1)} %shard_map.59.hidden_ref, bf16[224,8192]{1,0:T(8,128)(2,1)S(1)} %get-tuple-element.30.down_ref), custom_call_target="tpu_custom_call" | custom-call | flops 469762048 | bytes 3670016 | tf_op jit(solution)/shard_map/pallas_call | solution.py:103
  25.9 0.2 collective-permute-start.14
  26.1 0.4 collective-permute-start.11
  26.4 0.8 %collective-permute-done.14 = bf16[8,8192]{1,0:T(8,128)(2,1)S(1)} collective-permute-done((bf16[8,8192]{1,0:T(8,128)(2,1)S(1)}, bf16[8,8192]{1,0:T(8,128)(2,1)S(1)}, u32[]{:S(2)}, u32[]{:S(2)}) %collective-permute-start.14) | collective-permute-done | bytes 131104 | tf_op jit(solution)/shard_map/ppermute | solution.py:174
  27.3 1.2 %collective-permute-start.15 = (bf16[8,8192]{1,0:T(8,128)(2,1)S(1)}, bf16[8,8192]{1,0:T(8,128)(2,1)S(1)}, u32[]{:S(2)}, u32[]{:S(2)}) collective-permute-start(bf16[8,8192]{1,0:T(8,128)(2,1)S(1)} %add_convert_fusion), channel_id=1, source_target_pairs={{0,6},{1,7},{2,4},{3,5},{4,2},{5,3},{6,0},{7,1},{8,14},{9,15},{10,... | collective-permute-start | bytes 393224 | tf_op jit(solution)/shard_map/ppermute | solution.py:174
  28.5 0.0 collective-permute-done.11
  28.5 0.0 collective-permute-start.12
  28.5 0.1 fusion.3
  28.6 0.0 copy-start
  28.6 1.2 %collective-permute-start.16 = (bf16[8,8192]{1,0:T(8,128)(2,1)S(1)}, bf16[8,8192]{1,0:T(8,128)(2,1)S(1)}, u32[]{:S(2)}, u32[]{:S(2)}) collective-permute-start(bf16[8,8192]{1,0:T(8,128)(2,1)S(1)} %get-tuple-element.41), channel_id=1, source_target_pairs={{0,4},{1,3},{2,6},{3,1},{4,0},{5,7},{6,2},{7,5},{8,12},{9,11},{10,... | collective-permute-start | bytes 393224 | tf_op jit(solution)/shard_map/ppermute | solution.py:174
  29.8 1.3 %collective-permute-start.17 = (bf16[8,8192]{1,0:T(8,128)(2,1)S(1)}, bf16[8,8192]{1,0:T(8,128)(2,1)S(1)}, u32[]{:S(2)}, u32[]{:S(2)}) collective-permute-start(bf16[8,8192]{1,0:T(8,128)(2,1)S(1)} %get-tuple-element.42), channel_id=1, source_target_pairs={{0,2},{1,5},{2,0},{3,7},{4,6},{5,1},{6,4},{7,3},{8,10},{9,13},{10,... | collective-permute-start | bytes 393224 | tf_op jit(solution)/shard_map/ppermute | solution.py:174
  31.1 0.0 collective-permute-done.12
  31.1 0.1 convert_add_fusion
  31.2 0.9 %collective-permute-start.13 = (bf16[16,8192]{1,0:T(8,128)(2,1)S(1)}, bf16[16,8192]{1,0:T(8,128)(2,1)S(1)}, u32[]{:S(2)}, u32[]{:S(2)}) collective-permute-start(bf16[16,8192]{1,0:T(8,128)(2,1)S(1)} %slice.215), channel_id=1, source_target_pairs={{0,2},{1,5},{2,0},{3,7},{4,6},{5,1},{6,4},{7,3},{8,10},{9,13},{10,... | collective-permute-start | bytes 786440 | tf_op jit(solution)/shard_map/ppermute | solution.py:174
  32.1 2.6 %collective-permute-done.15 = bf16[8,8192]{1,0:T(8,128)(2,1)S(1)} collective-permute-done((bf16[8,8192]{1,0:T(8,128)(2,1)S(1)}, bf16[8,8192]{1,0:T(8,128)(2,1)S(1)}, u32[]{:S(2)}, u32[]{:S(2)}) %collective-permute-start.15) | collective-permute-done | bytes 131104 | tf_op jit(solution)/shard_map/ppermute | solution.py:174
  34.6 1.4 %collective-permute-done.16 = bf16[8,8192]{1,0:T(8,128)(2,1)S(1)} collective-permute-done((bf16[8,8192]{1,0:T(8,128)(2,1)S(1)}, bf16[8,8192]{1,0:T(8,128)(2,1)S(1)}, u32[]{:S(2)}, u32[]{:S(2)}) %collective-permute-start.16) | collective-permute-done | bytes 131104 | tf_op jit(solution)/shard_map/ppermute | solution.py:174
  36.0 0.7 %collective-permute-done.17 = bf16[8,8192]{1,0:T(8,128)(2,1)S(1)} collective-permute-done((bf16[8,8192]{1,0:T(8,128)(2,1)S(1)}, bf16[8,8192]{1,0:T(8,128)(2,1)S(1)}, u32[]{:S(2)}, u32[]{:S(2)}) %collective-permute-start.17) | collective-permute-done | bytes 131104 | tf_op jit(solution)/shard_map/ppermute | solution.py:174
  36.6 0.1 fusion.2
  36.7 1.7 %collective-permute-start.18 = (bf16[8,8192]{1,0:T(8,128)(2,1)S(1)}, bf16[8,8192]{1,0:T(8,128)(2,1)S(1)}, u32[]{:S(2)}, u32[]{:S(2)}) collective-permute-start(bf16[8,8192]{1,0:T(8,128)(2,1)S(1)} %fusion.2), channel_id=1, source_target_pairs={{0,8},{1,9},{2,10},{3,11},{4,12},{5,13},{6,14},{7,15},{8,0},{9,1},... | collective-permute-start | bytes 393224 | tf_op jit(solution)/shard_map/ppermute | solution.py:174
  38.4 1.0 %collective-permute-done.13 = bf16[16,8192]{1,0:T(8,128)(2,1)S(1)} collective-permute-done((bf16[16,8192]{1,0:T(8,128)(2,1)S(1)}, bf16[16,8192]{1,0:T(8,128)(2,1)S(1)}, u32[]{:S(2)}, u32[]{:S(2)}) %collective-permute-start.13) | collective-permute-done | bytes 262176 | tf_op jit(solution)/shard_map/ppermute | solution.py:174
  39.4 0.1 slice_add_fusion
  39.5 1.5 %collective-permute-start.19 = (bf16[8,8192]{1,0:T(8,128)(2,1)S(1)}, bf16[8,8192]{1,0:T(8,128)(2,1)S(1)}, u32[]{:S(2)}, u32[]{:S(2)}) collective-permute-start(bf16[8,8192]{1,0:T(8,128)(2,1)S(1)} %slice.216), channel_id=1, source_target_pairs={{0,4},{1,3},{2,6},{3,1},{4,0},{5,7},{6,2},{7,5},{8,12},{9,11},{10,... | collective-permute-start | bytes 393224 | tf_op jit(solution)/shard_map/ppermute | solution.py:174
  41.1 4.9 %collective-permute-done.18.refs_1_ = bf16[8,8192]{1,0:T(8,128)(2,1)S(1)} collective-permute-done((bf16[8,8192]{1,0:T(8,128)(2,1)S(1)}, bf16[8,8192]{1,0:T(8,128)(2,1)S(1)}, u32[]{:S(2)}, u32[]{:S(2)}) %collective-permute-start.18) | collective-permute-done | bytes 131104 | tf_op jit(solution)/shard_map/ppermute | solution.py:174
  45.9 0.7 %collective-permute-done.19.refs_2_ = bf16[8,8192]{1,0:T(8,128)(2,1)S(1)} collective-permute-done((bf16[8,8192]{1,0:T(8,128)(2,1)S(1)}, bf16[8,8192]{1,0:T(8,128)(2,1)S(1)}, u32[]{:S(2)}, u32[]{:S(2)}) %collective-permute-start.19) | collective-permute-done | bytes 131104 | tf_op jit(solution)/shard_map/ppermute | solution.py:174
  46.7 0.0 copy-done
  46.7 0.9 %shard_map.61 = bf16[8,8192]{1,0:T(8,128)(2,1)} custom-call(f32[8,8192]{1,0:T(8,128)S(1)} %slice.168.refs_0_, bf16[8,8192]{1,0:T(8,128)(2,1)S(1)} %collective-permute-done.18.refs_1_, bf16[8,8192]{1,0:T(8,128)(2,1)S(1)} %collective-permute-done.19.refs_2_, s32[1,8192]{1,0:T(1,128)S(1)} %bitcast.3), custom_call_target="tpu_custom_call" | custom-call | tf_op jit(solution)/shard_map/pallas_call | solution.py:151
  (12 shorter events, 0.2 us)
Async XLA Ops:
  0.0 10.6 %collective-permute-start = (bf16[8,8192]{1,0:T(8,128)(2,1)}, bf16[8,8192]{1,0:T(8,128)(2,1)S(1)}, u32[]{:S(2)}, u32[]{:S(2)}) collective-permute-start(bf16[8,8192]{1,0:T(8,128)(2,1)} %param.5), channel_id=1, source_target_pairs={{0,8},{1,9},{2,10},{3,11},{4,12},{5,13},{6,14},{7,15},{8,0},{9,1},... | collective-permute-start | bytes 393224 | tf_op jit(solution)/shard_map/ppermute | solution.py:174
  4.0 8.9 %collective-permute-start.2 = (bf16[8,8192]{1,0:T(8,128)(2,1)}, bf16[8,8192]{1,0:T(8,128)(2,1)S(1)}, u32[]{:S(2)}, u32[]{:S(2)}) collective-permute-start(bf16[8,8192]{1,0:T(8,128)(2,1)} %param.5), channel_id=1, source_target_pairs={{0,2},{1,5},{2,0},{3,7},{4,6},{5,1},{6,4},{7,3},{8,10},{9,13},{10,... | collective-permute-start | bytes 393224 | tf_op jit(solution)/shard_map/ppermute | solution.py:174
  5.6 13.6 %collective-permute-start.1 = (bf16[8,8192]{1,0:T(8,128)(2,1)}, bf16[8,8192]{1,0:T(8,128)(2,1)S(1)}, u32[]{:S(2)}, u32[]{:S(2)}) collective-permute-start(bf16[8,8192]{1,0:T(8,128)(2,1)} %param.5), channel_id=1, source_target_pairs={{0,4},{1,3},{2,6},{3,1},{4,0},{5,7},{6,2},{7,5},{8,12},{9,11},{10,... | collective-permute-start | bytes 393224 | tf_op jit(solution)/shard_map/ppermute | solution.py:174
  7.1 12.1 %collective-permute-start.3 = (bf16[8,8192]{1,0:T(8,128)(2,1)}, bf16[8,8192]{1,0:T(8,128)(2,1)S(1)}, u32[]{:S(2)}, u32[]{:S(2)}) collective-permute-start(bf16[8,8192]{1,0:T(8,128)(2,1)} %param.5), channel_id=1, source_target_pairs={{0,6},{1,7},{2,4},{3,5},{4,2},{5,3},{6,0},{7,1},{8,14},{9,15},{10,... | collective-permute-start | bytes 393224 | tf_op jit(solution)/shard_map/ppermute | solution.py:174
  10.6 8.6 %collective-permute-start.6 = (bf16[8,8192]{1,0:T(8,128)(2,1)S(1)}, bf16[8,8192]{1,0:T(8,128)(2,1)S(1)}, u32[]{:S(2)}, u32[]{:S(2)}) collective-permute-start(bf16[8,8192]{1,0:T(8,128)(2,1)S(1)} %collective-permute-done._), channel_id=1, source_target_pairs={{0,6},{1,7},{2,4},{3,5},{4,2},{5,3},{6,0},{7,1},{8,14},{9,15},{10,... | collective-permute-start | bytes 393224 | tf_op jit(solution)/shard_map/ppermute | solution.py:174
  12.4 8.2 %collective-permute-start.5 = (bf16[8,8192]{1,0:T(8,128)(2,1)S(1)}, bf16[8,8192]{1,0:T(8,128)(2,1)S(1)}, u32[]{:S(2)}, u32[]{:S(2)}) collective-permute-start(bf16[8,8192]{1,0:T(8,128)(2,1)S(1)} %collective-permute-done._), channel_id=1, source_target_pairs={{0,2},{1,5},{2,0},{3,7},{4,6},{5,1},{6,4},{7,3},{8,10},{9,13},{10,... | collective-permute-start | bytes 393224 | tf_op jit(solution)/shard_map/ppermute | solution.py:174
  12.9 7.7 %collective-permute-start.4 = (bf16[8,8192]{1,0:T(8,128)(2,1)S(1)}, bf16[8,8192]{1,0:T(8,128)(2,1)S(1)}, u32[]{:S(2)}, u32[]{:S(2)}) collective-permute-start(bf16[8,8192]{1,0:T(8,128)(2,1)S(1)} %collective-permute-done._), channel_id=1, source_target_pairs={{0,4},{1,3},{2,6},{3,1},{4,0},{5,7},{6,2},{7,5},{8,12},{9,11},{10,... | collective-permute-start | bytes 393224 | tf_op jit(solution)/shard_map/ppermute | solution.py:174
  20.7 1.6 %collective-permute-start.10 = (bf16[64,2048]{1,0:T(8,128)(2,1)S(1)}, bf16[64,2048]{1,0:T(8,128)(2,1)S(1)}, u32[]{:S(2)}, u32[]{:S(2)}) collective-permute-start(bf16[64,2048]{1,0:T(8,128)(2,1)S(1)} %get-tuple-element.43.here_ref), channel_id=1, source_target_pairs={{0,1},{1,0},{2,3},{3,2},{4,5},{5,4},{6,7},{7,6},{8,9},{9,8},{10,11... | collective-permute-start | bytes 786440 | tf_op jit(solution)/shard_map/ppermute | solution.py:174
  20.8 2.2 %collective-permute-start.9 = (bf16[64,2048]{1,0:T(8,128)(2,1)S(1)}, bf16[64,2048]{1,0:T(8,128)(2,1)S(1)}, u32[]{:S(2)}, u32[]{:S(2)}) collective-permute-start(bf16[64,2048]{1,0:T(8,128)(2,1)S(1)} %get-tuple-element.44.here_ref), channel_id=1, source_target_pairs={{0,1},{1,0},{2,3},{3,2},{4,5},{5,4},{6,7},{7,6},{8,9},{9,8},{10,11... | collective-permute-start | bytes 786440 | tf_op jit(solution)/shard_map/ppermute | solution.py:174
  21.3 2.4 %collective-permute-start.8 = (bf16[64,2048]{1,0:T(8,128)(2,1)S(1)}, bf16[64,2048]{1,0:T(8,128)(2,1)S(1)}, u32[]{:S(2)}, u32[]{:S(2)}) collective-permute-start(bf16[64,2048]{1,0:T(8,128)(2,1)S(1)} %get-tuple-element.45.here_ref), channel_id=1, source_target_pairs={{0,1},{1,0},{2,3},{3,2},{4,5},{5,4},{6,7},{7,6},{8,9},{9,8},{10,11... | collective-permute-start | bytes 786440 | tf_op jit(solution)/shard_map/ppermute | solution.py:174
  21.4 3.0 %collective-permute-start.7 = (bf16[64,2048]{1,0:T(8,128)(2,1)S(1)}, bf16[64,2048]{1,0:T(8,128)(2,1)S(1)}, u32[]{:S(2)}, u32[]{:S(2)}) collective-permute-start(bf16[64,2048]{1,0:T(8,128)(2,1)S(1)} %get-tuple-element.46.here_ref), channel_id=1, source_target_pairs={{0,1},{1,0},{2,3},{3,2},{4,5},{5,4},{6,7},{7,6},{8,9},{9,8},{10,11... | collective-permute-start | bytes 786440 | tf_op jit(solution)/shard_map/ppermute | solution.py:174
  25.9 1.4 %collective-permute-start.14 = (bf16[8,8192]{1,0:T(8,128)(2,1)S(1)}, bf16[8,8192]{1,0:T(8,128)(2,1)S(1)}, u32[]{:S(2)}, u32[]{:S(2)}) collective-permute-start(bf16[8,8192]{1,0:T(8,128)(2,1)S(1)} %get-tuple-element.38), channel_id=1, source_target_pairs={{0,1},{1,0},{2,3},{3,2},{4,5},{5,4},{6,7},{7,6},{8,9},{9,8},{10,11... | collective-permute-start | bytes 393224 | tf_op jit(solution)/shard_map/ppermute | solution.py:174
  26.1 2.4 %collective-permute-start.11 = (bf16[24,8192]{1,0:T(8,128)(2,1)S(1)}, bf16[24,8192]{1,0:T(8,128)(2,1)S(1)}, u32[]{:S(2)}, u32[]{:S(2)}) collective-permute-start(bf16[24,8192]{1,0:T(8,128)(2,1)S(1)} %get-tuple-element.32), channel_id=1, source_target_pairs={{0,1},{1,0},{2,3},{3,2},{4,5},{5,4},{6,7},{7,6},{8,9},{9,8},{10,11... | collective-permute-start | bytes 1179656 | tf_op jit(solution)/shard_map/ppermute | solution.py:174
  27.3 7.3 %collective-permute-start.15 = (bf16[8,8192]{1,0:T(8,128)(2,1)S(1)}, bf16[8,8192]{1,0:T(8,128)(2,1)S(1)}, u32[]{:S(2)}, u32[]{:S(2)}) collective-permute-start(bf16[8,8192]{1,0:T(8,128)(2,1)S(1)} %add_convert_fusion), channel_id=1, source_target_pairs={{0,6},{1,7},{2,4},{3,5},{4,2},{5,3},{6,0},{7,1},{8,14},{9,15},{10,... | collective-permute-start | bytes 393224 | tf_op jit(solution)/shard_map/ppermute | solution.py:174
  28.5 2.6 %collective-permute-start.12 = (bf16[32,8192]{1,0:T(8,128)(2,1)S(1)}, bf16[32,8192]{1,0:T(8,128)(2,1)S(1)}, u32[]{:S(2)}, u32[]{:S(2)}) collective-permute-start(bf16[32,8192]{1,0:T(8,128)(2,1)S(1)} %get-tuple-element.34), channel_id=1, source_target_pairs={{0,1},{1,0},{2,3},{3,2},{4,5},{5,4},{6,7},{7,6},{8,9},{9,8},{10,11... | collective-permute-start | bytes 1572872 | tf_op jit(solution)/shard_map/ppermute | solution.py:174
  28.6 18.1 %copy-start = (s32[8192]{0:T(1024)S(1)}, s32[8192]{0:T(1024)}, u32[]{:S(2)}) copy-start(s32[8192]{0:T(1024)} %param.9) | copy-start | bytes 98308
  28.6 7.4 %collective-permute-start.16 = (bf16[8,8192]{1,0:T(8,128)(2,1)S(1)}, bf16[8,8192]{1,0:T(8,128)(2,1)S(1)}, u32[]{:S(2)}, u32[]{:S(2)}) collective-permute-start(bf16[8,8192]{1,0:T(8,128)(2,1)S(1)} %get-tuple-element.41), channel_id=1, source_target_pairs={{0,4},{1,3},{2,6},{3,1},{4,0},{5,7},{6,2},{7,5},{8,12},{9,11},{10,... | collective-permute-start | bytes 393224 | tf_op jit(solution)/shard_map/ppermute | solution.py:174
  29.8 6.9 %collective-permute-start.17 = (bf16[8,8192]{1,0:T(8,128)(2,1)S(1)}, bf16[8,8192]{1,0:T(8,128)(2,1)S(1)}, u32[]{:S(2)}, u32[]{:S(2)}) collective-permute-start(bf16[8,8192]{1,0:T(8,128)(2,1)S(1)} %get-tuple-element.42), channel_id=1, source_target_pairs={{0,2},{1,5},{2,0},{3,7},{4,6},{5,1},{6,4},{7,3},{8,10},{9,13},{10,... | collective-permute-start | bytes 393224 | tf_op jit(solution)/shard_map/ppermute | solution.py:174
  31.2 8.2 %collective-permute-start.13 = (bf16[16,8192]{1,0:T(8,128)(2,1)S(1)}, bf16[16,8192]{1,0:T(8,128)(2,1)S(1)}, u32[]{:S(2)}, u32[]{:S(2)}) collective-permute-start(bf16[16,8192]{1,0:T(8,128)(2,1)S(1)} %slice.215), channel_id=1, source_target_pairs={{0,2},{1,5},{2,0},{3,7},{4,6},{5,1},{6,4},{7,3},{8,10},{9,13},{10,... | collective-permute-start | bytes 786440 | tf_op jit(solution)/shard_map/ppermute | solution.py:174
  36.7 9.2 %collective-permute-start.18 = (bf16[8,8192]{1,0:T(8,128)(2,1)S(1)}, bf16[8,8192]{1,0:T(8,128)(2,1)S(1)}, u32[]{:S(2)}, u32[]{:S(2)}) collective-permute-start(bf16[8,8192]{1,0:T(8,128)(2,1)S(1)} %fusion.2), channel_id=1, source_target_pairs={{0,8},{1,9},{2,10},{3,11},{4,12},{5,13},{6,14},{7,15},{8,0},{9,1},... | collective-permute-start | bytes 393224 | tf_op jit(solution)/shard_map/ppermute | solution.py:174
  39.5 7.1 %collective-permute-start.19 = (bf16[8,8192]{1,0:T(8,128)(2,1)S(1)}, bf16[8,8192]{1,0:T(8,128)(2,1)S(1)}, u32[]{:S(2)}, u32[]{:S(2)}) collective-permute-start(bf16[8,8192]{1,0:T(8,128)(2,1)S(1)} %slice.216), channel_id=1, source_target_pairs={{0,4},{1,3},{2,6},{3,1},{4,0},{5,7},{6,2},{7,5},{8,12},{9,11},{10,... | collective-permute-start | bytes 393224 | tf_op jit(solution)/shard_map/ppermute | solution.py:174

commit v8 on v7

--- a/solution.py
+++ b/solution.py
@@ -9,8 +9,8 @@
 from jax.sharding import PartitionSpec as P
 
 BLOCK = 128
-PIECES = 4
-SPANS = 4
+PIECES = 2
+SPANS = (6, 5, 5)
 NT = (((1,), (1,)), ((), ()))
 
 
@@ -50,7 +50,7 @@
 def hidden_kernel(start, last, weights_ref, here_ref, there_ref, *refs):
     *sums, out_ref = refs
     width = here_ref.shape[1]
-    tile = math.gcd(width, 1024)
+    tile = math.gcd(width, 512)
     total = sums[0][...] if sums else None
     for first in range(0, width, tile):
         rows = jnp.concatenate([here_ref[:, first : first + tile], there_ref[:, first : first + tile]])
@@ -65,15 +65,16 @@
 
 
 def hidden_units(weights, spans):
-    units, width = weights.shape[0] // 2, spans[0][0].shape[1]
+    units, features = weights.shape[0] // 2, weights.shape[1]
     count = 2 * spans[0][0].shape[0]
-    sums = ()
-    for k, span in enumerate(spans):
-        last = k == len(spans) - 1
+    sums, start = (), 0
+    for span in spans:
+        width = span[0].shape[1]
+        last = start + width == features
         shape = ((count, units), jnp.bfloat16) if last else ((count, 2 * units), jnp.float32)
         sums = (
             pl.pallas_call(
-                functools.partial(hidden_kernel, k * width, last),
+                functools.partial(hidden_kernel, start, last),
                 out_shape=jax.ShapeDtypeStruct(*shape),
                 in_specs=[vmem()] * (3 + len(sums)),
                 out_specs=vmem(),
@@ -83,6 +84,7 @@
                 compiler_params=pltpu.CompilerParams(vmem_limit_bytes=24 << 20),
             )(weights, *span, *sums),
         )
+        start += width
     return sums[0]
 
 
@@ -113,16 +115,19 @@
     )(hidden, down_w)
 
 
+def signs_twice():
+    index = jnp.arange(BLOCK, dtype=jnp.int32)
+    common = index[:, None] & index[None, :]
+    for shift in (4, 2, 1):
+        common = common ^ (common >> shift)
+    signs = (1 - 2 * (common & 1)).astype(jnp.bfloat16)
+    return jnp.concatenate([signs, signs])
+
+
 def rotate_kernel(count, *refs):
     total_ref, *arrived = refs[: count + 1]
-    sign_ref, out_ref, turned_ref, sems = refs[count + 1 :]
+    sign_ref, matrix_ref, out_ref, turned_ref, sems = refs[count + 1 :]
     rows, features = total_ref.shape
-    common = lax.broadcasted_iota(jnp.int32, (BLOCK, BLOCK), 0) & lax.broadcasted_iota(
-        jnp.int32, (BLOCK, BLOCK), 1
-    )
-    for shift in (4, 2, 1):
-        common = common ^ (common >> shift)
-    flips = (1 - 2 * (common & 1)).astype(jnp.float32).astype(jnp.bfloat16)
     scale = 1.0 / math.sqrt(BLOCK)
     width = features // PIECES
     copies = []
@@ -135,8 +140,8 @@
         value = jnp.concatenate([value[:, b : b + BLOCK] for b in range(0, width, BLOCK)])
         high = value.astype(jnp.bfloat16)
         low = (value - high.astype(jnp.float32)).astype(jnp.bfloat16)
-        turned = jnp.dot(high, flips, preferred_element_type=jnp.float32)
-        turned = (turned + jnp.dot(low, flips, preferred_element_type=jnp.float32)) * scale
+        both = jnp.concatenate([high, low], axis=1)
+        turned = jnp.dot(both, matrix_ref[...], preferred_element_type=jnp.float32) * scale
         for b in range(width // BLOCK):
             first = k * width + b * BLOCK
             turned_ref[:, first : first + BLOCK] = turned[b * rows : (b + 1) * rows].astype(jnp.bfloat16)
@@ -147,15 +152,14 @@
 
 
 def rotate(total, arrived, signs):
-    features = signs.shape[0]
     return pl.pallas_call(
         functools.partial(rotate_kernel, len(arrived)),
         out_shape=jax.ShapeDtypeStruct(total.shape, jnp.bfloat16),
-        in_specs=[vmem()] * (len(arrived) + 2),
+        in_specs=[vmem()] * (len(arrived) + 3),
         out_specs=pl.BlockSpec(memory_space=pl.ANY),
         scratch_shapes=[pltpu.VMEM(total.shape, jnp.bfloat16), pltpu.SemaphoreType.DMA((PIECES,))],
         compiler_params=pltpu.CompilerParams(vmem_limit_bytes=16 << 20),
-    )(total, *arrived, signs.reshape(1, features))
+    )(total, *arrived, signs.reshape(1, -1), signs_twice())
 
 
 def solution(mesh):
@@ -184,17 +188,19 @@
         there = [swap(away, m) for m in square]
         gate_up_w, down_w = fetch(gate_weight.T, up_weight.T, down_weight, away)
         gate_up_w, *near, there[0], there[1], there[2] = lax.optimization_barrier((gate_up_w, *near, *there))
-        gathered = [tokens, *near, there[2], away, *there[:2]]
-        spans = []
-        width = features // SPANS
-        for k in range(SPANS):
-            span = jnp.concatenate([piece[:, k * width : (k + 1) * width] for piece in gathered])
+        gathered = [tokens, near[1], near[0], near[2], there[2], away, *there[:2]]
+        spans, start = [], 0
+        for share in SPANS:
+            end = start + features * share // sum(SPANS)
+            span = jnp.concatenate([piece[:, start:end] for piece in gathered])
             spans.append((span, swap(span, (1, 1))))
+            start = end
         hidden = hidden_units(gate_up_w, spans)
 
         count = others * rows
         own, diagonal, rest, *sends = down(hidden, down_w, (4 * rows, count, 3 * count))
-        diagonal = diagonal + swap(sends[1], (1, 1)).astype(jnp.float32)
+        there, sends[2] = lax.optimization_barrier((swap(sends[1], (1, 1)), sends[2]))
+        diagonal = diagonal + there.astype(jnp.float32)
         diagonal = swap(diagonal.astype(jnp.bfloat16), square[2])
         rest_there, sends[0] = lax.optimization_barrier((swap(sends[2], (1, 1)), sends[0]))
         rest = rest + rest_there.astype(jnp.float32)
@@ -210,8 +216,8 @@
             total = total[:split] + piece[rows:].astype(jnp.float32)
 
         own = own + swap(sends[0], (1, 1)).astype(jnp.float32)
-        own = own[: 2 * rows] + swap(own[2 * rows :].astype(jnp.bfloat16), square[1]).astype(jnp.float32)
-        arrived.append(swap(own[rows:].astype(jnp.bfloat16), square[0]))
+        own = own[: 2 * rows] + swap(own[2 * rows :].astype(jnp.bfloat16), square[0]).astype(jnp.float32)
+        arrived.append(swap(own[rows:].astype(jnp.bfloat16), square[1]))
         return rotate(own[:rows], arrived, sign_pattern)
 
     placed = (P(("groups", "gx"), None), P(None, "gx"), P(None, "gx"), P("gx", None), P())

time: 47.8 us -> 47 us (0.983)
  waiting for transfers between devices: 17.1 us -> 15.4 us
  local copies, waits for them, and re-layouts: 0.99 us -> 1.81 us
    ppermute x20 -> x19, waiting for transfers between devices: 17.1 us -> 15.4 us  [swap(): lax.ppermute(value, 'gx', [(i, i ^ masks[i % 2]) for i in range(members)])]
    unnamed x9 -> x16, local copies, waits for them, and re-layouts: 0.89 us -> 1.71 us
    pallas_call x4 -> x3, Pallas kernels: 2.77 us -> 2.67 us  [hidden_units(): pl.pallas_call(functools.partial(hidden_kernel, start, last), out_shape=j...]
    ppermute x20 -> x19, starting transfers between devices: 20.4 us -> 20.4 us  [swap(): lax.ppermute(value, 'gx', [(i, i ^ masks[i % 2]) for i in range(members)])]
  transfers between devices with their start and end apart: 20 -> 19, of which waited for: 10 -> 10; matrix products, arithmetic and copies ran while one was open for 3% -> 5% of each run, Pallas kernels for 13% -> 13%
where the time goes in v8:
time: 47 us; the launch traced here: 46.8 us
  starting transfers between devices  20.4 us (43%)
  waiting for transfers between devices  15.4 us (33%)
  Pallas kernels  8.52 us (18%)
  local copies, waits for them, and re-layouts  1.81 us (4%)
    ppermute x19, starting transfers between devices, swap(): lax.ppermute(value, 'gx', [(i, i ^ masks[i % 2]) for i in range(members)])  20.4 us
    ppermute x19, waiting for transfers between devices, swap(): lax.ppermute(value, 'gx', [(i, i ^ masks[i % 2]) for i in range(members)])  15.4 us
    pallas_call x1, Pallas kernels, fetch(): pl.pallas_call(fetch_kernel, out_shape=(jax.ShapeDtypeStruct((2 * units,...  4.23 us
    pallas_call x3, Pallas kernels, hidden_units(): pl.pallas_call(functools.partial(hidden_kernel, start, last), out_shape=j...  2.67 us
    unnamed x16, local copies, waits for them, and re-layouts  1.71 us
  transfers between devices with their start and end apart: 19, of which 10 were waited for; matrix products, arithmetic and copies ran while one was open for 5% of the time, Pallas kernels for 13%

profile of v8, /device:TPU:0, one launch (start us, length us, event | category | flops | bytes accessed | tf_op | source)
XLA Modules:
  0.0 46.8 jit_solution(8726488103532824991)
XLA Ops:
  0.0 4.0 %collective-permute-start = (bf16[8,8192]{1,0:T(8,128)(2,1)}, bf16[8,8192]{1,0:T(8,128)(2,1)S(1)}, u32[]{:S(2)}, u32[]{:S(2)}) collective-permute-start(bf16[8,8192]{1,0:T(8,128)(2,1)} %param.5), channel_id=1, source_target_pairs={{0,8},{1,9},{2,10},{3,11},{4,12},{5,13},{6,14},{7,15},{8,0},{9,1},... | collective-permute-start | bytes 393224 | tf_op jit(solution)/shard_map/ppermute | solution.py:178
  4.0 1.6 %collective-permute-start.1 = (bf16[8,8192]{1,0:T(8,128)(2,1)}, bf16[8,8192]{1,0:T(8,128)(2,1)S(1)}, u32[]{:S(2)}, u32[]{:S(2)}) collective-permute-start(bf16[8,8192]{1,0:T(8,128)(2,1)} %param.5), channel_id=1, source_target_pairs={{0,4},{1,3},{2,6},{3,1},{4,0},{5,7},{6,2},{7,5},{8,12},{9,11},{10,... | collective-permute-start | bytes 393224 | tf_op jit(solution)/shard_map/ppermute | solution.py:178
  5.6 1.5 %collective-permute-start.2 = (bf16[8,8192]{1,0:T(8,128)(2,1)}, bf16[8,8192]{1,0:T(8,128)(2,1)S(1)}, u32[]{:S(2)}, u32[]{:S(2)}) collective-permute-start(bf16[8,8192]{1,0:T(8,128)(2,1)} %param.5), channel_id=1, source_target_pairs={{0,2},{1,5},{2,0},{3,7},{4,6},{5,1},{6,4},{7,3},{8,10},{9,13},{10,... | collective-permute-start | bytes 393224 | tf_op jit(solution)/shard_map/ppermute | solution.py:178
  7.1 0.4 collective-permute-start.3
  7.5 0.8 %constant_dynamic-update-slice_fusion.15 = (bf16[64,2560]{1,0:T(8,128)(2,1)S(1)}, bf16[64,2560]{1,0:T(8,128)(2,1)S(1)}) fusion(bf16[8,8192]{1,0:T(8,128)(2,1)} %param.5), kind=kLoop, calls=%fused_computation.33 | loop fusion | bytes 163840
  8.3 2.3 %collective-permute-done._ = bf16[8,8192]{1,0:T(8,128)(2,1)S(1)} collective-permute-done((bf16[8,8192]{1,0:T(8,128)(2,1)}, bf16[8,8192]{1,0:T(8,128)(2,1)S(1)}, u32[]{:S(2)}, u32[]{:S(2)}) %collective-permute-start) | collective-permute-done | bytes 131104 | tf_op jit(solution)/shard_map/ppermute | solution.py:178
  10.7 0.8 %collective-permute-start.4 = (bf16[8,8192]{1,0:T(8,128)(2,1)S(1)}, bf16[8,8192]{1,0:T(8,128)(2,1)S(1)}, u32[]{:S(2)}, u32[]{:S(2)}) collective-permute-start(bf16[8,8192]{1,0:T(8,128)(2,1)S(1)} %collective-permute-done._), channel_id=1, source_target_pairs={{0,4},{1,3},{2,6},{3,1},{4,0},{5,7},{6,2},{7,5},{8,12},{9,11},{10,... | collective-permute-start | bytes 393224 | tf_op jit(solution)/shard_map/ppermute | solution.py:178
  11.4 1.5 %collective-permute-start.5 = (bf16[8,8192]{1,0:T(8,128)(2,1)S(1)}, bf16[8,8192]{1,0:T(8,128)(2,1)S(1)}, u32[]{:S(2)}, u32[]{:S(2)}) collective-permute-start(bf16[8,8192]{1,0:T(8,128)(2,1)S(1)} %collective-permute-done._), channel_id=1, source_target_pairs={{0,2},{1,5},{2,0},{3,7},{4,6},{5,1},{6,4},{7,3},{8,10},{9,13},{10,... | collective-permute-start | bytes 393224 | tf_op jit(solution)/shard_map/ppermute | solution.py:178
  12.9 0.0 collective-permute-done.1
  12.9 1.5 %collective-permute-start.6 = (bf16[8,8192]{1,0:T(8,128)(2,1)S(1)}, bf16[8,8192]{1,0:T(8,128)(2,1)S(1)}, u32[]{:S(2)}, u32[]{:S(2)}) collective-permute-start(bf16[8,8192]{1,0:T(8,128)(2,1)S(1)} %collective-permute-done._), channel_id=1, source_target_pairs={{0,6},{1,7},{2,4},{3,5},{4,2},{5,3},{6,0},{7,1},{8,14},{9,15},{10,... | collective-permute-start | bytes 393224 | tf_op jit(solution)/shard_map/ppermute | solution.py:178
  14.4 0.8 %constant_dynamic-update-slice_fusion.23 = bf16[64,3072]{1,0:T(8,128)(2,1)S(1)} fusion(bf16[8,8192]{1,0:T(8,128)(2,1)} %param.5), kind=kLoop, calls=%fused_computation.41 | loop fusion | bytes 98304
  15.2 4.2 %shard_map.55 = (bf16[448,8192]{1,0:T(8,128)(2,1)S(1)}, bf16[224,8192]{1,0:T(8,128)(2,1)S(1)}) custom-call(bf16[224,8192]{1,0:T(8,128)(2,1)} %bitcast.4, bf16[224,8192]{1,0:T(8,128)(2,1)} %bitcast.5, bf16[224,8192]{1,0:T(8,128)(2,1)} %down_hbm.1, bf16[8,8192]{1,0:T(8,128)(2,1)S(1)} %collective-permute-done._), custom_call_target="tpu_custom_call" | custom-call | bytes 11010048 | tf_op jit(solution)/shard_map/pallas_call | solution.py:36
  19.4 0.0 collective-permute-done.2
  19.4 0.0 collective-permute-done.3
  19.5 0.0 collective-permute-done.4
  19.5 0.0 collective-permute-done.5
  19.5 1.0 %collective-permute-done.6 = bf16[8,8192]{1,0:T(8,128)(2,1)S(1)} collective-permute-done((bf16[8,8192]{1,0:T(8,128)(2,1)S(1)}, bf16[8,8192]{1,0:T(8,128)(2,1)S(1)}, u32[]{:S(2)}, u32[]{:S(2)}) %collective-permute-start.6) | collective-permute-done | bytes 131104 | tf_op jit(solution)/shard_map/ppermute | solution.py:178
  20.6 0.1 collective-permute-start.9
  20.8 0.5 %collective-permute-start.8 = (bf16[64,2560]{1,0:T(8,128)(2,1)S(1)}, bf16[64,2560]{1,0:T(8,128)(2,1)S(1)}, u32[]{:S(2)}, u32[]{:S(2)}) collective-permute-start(bf16[64,2560]{1,0:T(8,128)(2,1)S(1)} %get-tuple-element.47.here_ref), channel_id=1, source_target_pairs={{0,1},{1,0},{2,3},{3,2},{4,5},{5,4},{6,7},{7,6},{8,9},{9,8},{10,11... | collective-permute-start | bytes 983048 | tf_op jit(solution)/shard_map/ppermute | solution.py:178
  21.3 0.1 collective-permute-start.7
  21.4 1.0 %collective-permute-done.9.there_ref = bf16[64,3072]{1,0:T(8,128)(2,1)S(1)} collective-permute-done((bf16[64,3072]{1,0:T(8,128)(2,1)S(1)}, bf16[64,3072]{1,0:T(8,128)(2,1)S(1)}, u32[]{:S(2)}, u32[]{:S(2)}) %collective-permute-start.9) | collective-permute-done | bytes 393248 | tf_op jit(solution)/shard_map/ppermute | solution.py:178
  22.4 1.0 %shard_map.56.refs_0_ = f32[128,448]{1,0:T(8,128)S(1)} custom-call(bf16[448,8192]{1,0:T(8,128)(2,1)S(1)} %get-tuple-element.25.weights_ref, bf16[64,3072]{1,0:T(8,128)(2,1)S(1)} %constant_dynamic-update-slice_fusion.16.here_ref, bf16[64,3072]{1,0:T(8,128)(2,1)S(1)} %collective-permute-done.9.there_ref), custom_call_target="tpu_custom_call" | custom-call | flops 352321536 | bytes 2752512 | tf_op jit(solution)/shard_map/pallas_call | solution.py:76
  23.4 0.0 collective-permute-done.8.there_ref
  23.4 0.8 %shard_map.57.refs_0_ = f32[128,448]{1,0:T(8,128)S(1)} custom-call(bf16[448,8192]{1,0:T(8,128)(2,1)S(1)} %get-tuple-element.25.weights_ref, bf16[64,2560]{1,0:T(8,128)(2,1)S(1)} %get-tuple-element.47.here_ref, bf16[64,2560]{1,0:T(8,128)(2,1)S(1)} %collective-permute-done.8.there_ref, f32[128,448]{1,0:T(8,128)S(1)} %shard_map.56.refs_0_), custom_call_target="tpu_custom_call" | custom-call | flops 293601280 | bytes 2293760 | tf_op jit(solution)/shard_map/pallas_call | solution.py:76
  24.2 0.0 collective-permute-done.7.there_ref
  24.2 0.9 %shard_map.58.hidden_ref = bf16[128,224]{1,0:T(8,128)(2,1)S(1)} custom-call(bf16[448,8192]{1,0:T(8,128)(2,1)S(1)} %get-tuple-element.25.weights_ref, bf16[64,2560]{1,0:T(8,128)(2,1)S(1)} %get-tuple-element.48.here_ref, bf16[64,2560]{1,0:T(8,128)(2,1)S(1)} %collective-permute-done.7.there_ref, f32[128,448]{1,0:T(8,128)S(1)} %shard_map.57.refs_0_), custom_call_target="tpu_custom_call" | custom-call | flops 293601280 | bytes 2293760 | tf_op jit(solution)/shard_map/pallas_call | solution.py:76
  25.1 0.7 %shard_map.59 = (f32[32,8192]{1,0:T(8,128)S(1)}, f32[8,8192]{1,0:T(8,128)S(1)}, f32[24,8192]{1,0:T(8,128)S(1)}, bf16[32,8192]{1,0:T(8,128)(2,1)S(1)}, bf16[8,819...) custom-call(bf16[128,224]{1,0:T(8,128)(2,1)S(1)} %shard_map.58.hidden_ref, bf16[224,8192]{1,0:T(8,128)(2,1)S(1)} %get-tuple-element.32.down_ref), custom_call_target="tpu_custom_call" | custom-call | flops 469762048 | bytes 3670016 | tf_op jit(solution)/shard_map/pallas_call | solution.py:105
  25.8 0.2 collective-permute-start.10
  26.0 1.2 %collective-permute-done.10 = bf16[8,8192]{1,0:T(8,128)(2,1)S(1)} collective-permute-done((bf16[8,8192]{1,0:T(8,128)(2,1)S(1)}, bf16[8,8192]{1,0:T(8,128)(2,1)S(1)}, u32[]{:S(2)}, u32[]{:S(2)}) %collective-permute-start.10) | collective-permute-done | bytes 131104 | tf_op jit(solution)/shard_map/ppermute | solution.py:178
  27.2 0.1 collective-permute-start.11
  27.4 1.2 %collective-permute-start.14 = (bf16[8,8192]{1,0:T(8,128)(2,1)S(1)}, bf16[8,8192]{1,0:T(8,128)(2,1)S(1)}, u32[]{:S(2)}, u32[]{:S(2)}) collective-permute-start(bf16[8,8192]{1,0:T(8,128)(2,1)S(1)} %add_convert_fusion), channel_id=1, source_target_pairs={{0,6},{1,7},{2,4},{3,5},{4,2},{5,3},{6,0},{7,1},{8,14},{9,15},{10,... | collective-permute-start | bytes 393224 | tf_op jit(solution)/shard_map/ppermute | solution.py:178
  28.6 0.3 collective-permute-done.11
  29.0 0.1 collective-permute-start.12
  29.1 0.1 fusion.7
  29.2 0.0 copy-start
  29.2 1.5 %collective-permute-start.15 = (bf16[8,8192]{1,0:T(8,128)(2,1)S(1)}, bf16[8,8192]{1,0:T(8,128)(2,1)S(1)}, u32[]{:S(2)}, u32[]{:S(2)}) collective-permute-start(bf16[8,8192]{1,0:T(8,128)(2,1)S(1)} %get-tuple-element.45), channel_id=1, source_target_pairs={{0,4},{1,3},{2,6},{3,1},{4,0},{5,7},{6,2},{7,5},{8,12},{9,11},{10,... | collective-permute-start | bytes 393224 | tf_op jit(solution)/shard_map/ppermute | solution.py:178
  30.7 0.5 %collective-permute-start.16 = (bf16[8,8192]{1,0:T(8,128)(2,1)S(1)}, bf16[8,8192]{1,0:T(8,128)(2,1)S(1)}, u32[]{:S(2)}, u32[]{:S(2)}) collective-permute-start(bf16[8,8192]{1,0:T(8,128)(2,1)S(1)} %get-tuple-element.46), channel_id=1, source_target_pairs={{0,2},{1,5},{2,0},{3,7},{4,6},{5,1},{6,4},{7,3},{8,10},{9,13},{10,... | collective-permute-start | bytes 393224 | tf_op jit(solution)/shard_map/ppermute | solution.py:178
  31.2 0.0 collective-permute-done.12
  31.2 0.1 convert_add_fusion
  31.4 1.6 %collective-permute-start.13 = (bf16[16,8192]{1,0:T(8,128)(2,1)S(1)}, bf16[16,8192]{1,0:T(8,128)(2,1)S(1)}, u32[]{:S(2)}, u32[]{:S(2)}) collective-permute-start(bf16[16,8192]{1,0:T(8,128)(2,1)S(1)} %slice.174), channel_id=1, source_target_pairs={{0,4},{1,3},{2,6},{3,1},{4,0},{5,7},{6,2},{7,5},{8,12},{9,11},{10,... | collective-permute-start | bytes 786440 | tf_op jit(solution)/shard_map/ppermute | solution.py:178
  33.0 1.7 %collective-permute-done.14 = bf16[8,8192]{1,0:T(8,128)(2,1)S(1)} collective-permute-done((bf16[8,8192]{1,0:T(8,128)(2,1)S(1)}, bf16[8,8192]{1,0:T(8,128)(2,1)S(1)}, u32[]{:S(2)}, u32[]{:S(2)}) %collective-permute-start.14) | collective-permute-done | bytes 131104 | tf_op jit(solution)/shard_map/ppermute | solution.py:178
  34.7 2.3 %collective-permute-done.15 = bf16[8,8192]{1,0:T(8,128)(2,1)S(1)} collective-permute-done((bf16[8,8192]{1,0:T(8,128)(2,1)S(1)}, bf16[8,8192]{1,0:T(8,128)(2,1)S(1)}, u32[]{:S(2)}, u32[]{:S(2)}) %collective-permute-start.15) | collective-permute-done | bytes 131104 | tf_op jit(solution)/shard_map/ppermute | solution.py:178
  37.0 0.4 collective-permute-done.16
  37.4 0.1 fusion.2
  37.4 2.0 %collective-permute-start.17 = (bf16[8,8192]{1,0:T(8,128)(2,1)S(1)}, bf16[8,8192]{1,0:T(8,128)(2,1)S(1)}, u32[]{:S(2)}, u32[]{:S(2)}) collective-permute-start(bf16[8,8192]{1,0:T(8,128)(2,1)S(1)} %fusion.2), channel_id=1, source_target_pairs={{0,8},{1,9},{2,10},{3,11},{4,12},{5,13},{6,14},{7,15},{8,0},{9,1},... | collective-permute-start | bytes 393224 | tf_op jit(solution)/shard_map/ppermute | solution.py:178
  39.4 0.4 collective-permute-done.13
  39.8 0.1 slice_add_fusion
  39.9 1.1 %collective-permute-start.18 = (bf16[8,8192]{1,0:T(8,128)(2,1)S(1)}, bf16[8,8192]{1,0:T(8,128)(2,1)S(1)}, u32[]{:S(2)}, u32[]{:S(2)}) collective-permute-start(bf16[8,8192]{1,0:T(8,128)(2,1)S(1)} %slice.175), channel_id=1, source_target_pairs={{0,2},{1,5},{2,0},{3,7},{4,6},{5,1},{6,4},{7,3},{8,10},{9,13},{10,... | collective-permute-start | bytes 393224 | tf_op jit(solution)/shard_map/ppermute | solution.py:178
  41.1 4.8 %collective-permute-done.17.refs_1_ = bf16[8,8192]{1,0:T(8,128)(2,1)S(1)} collective-permute-done((bf16[8,8192]{1,0:T(8,128)(2,1)S(1)}, bf16[8,8192]{1,0:T(8,128)(2,1)S(1)}, u32[]{:S(2)}, u32[]{:S(2)}) %collective-permute-start.17) | collective-permute-done | bytes 131104 | tf_op jit(solution)/shard_map/ppermute | solution.py:178
  45.9 0.0 collective-permute-done.18.refs_2_
  45.9 0.0 copy-done
  45.9 0.9 %shard_map.60 = bf16[8,8192]{1,0:T(8,128)(2,1)} custom-call(f32[8,8192]{1,0:T(8,128)S(1)} %slice.135.refs_0_, bf16[8,8192]{1,0:T(8,128)(2,1)S(1)} %collective-permute-done.17.refs_1_, bf16[8,8192]{1,0:T(8,128)(2,1)S(1)} %collective-permute-done.18.refs_2_, s32[1,8192]{1,0:T(1,128)S(1)} %bitcast.3, bf16[256,128]{1,0:T(8,128)(2,1)S(1)} %pad_maximum_fusion.refs_4_), custom_call_target="tpu_custom_call" | custom-call | tf_op jit(solution)/shard_map/pallas_call | solution.py:155
  (21 shorter events, 0.2 us)
Async XLA Ops:
  0.0 10.7 %collective-permute-start = (bf16[8,8192]{1,0:T(8,128)(2,1)}, bf16[8,8192]{1,0:T(8,128)(2,1)S(1)}, u32[]{:S(2)}, u32[]{:S(2)}) collective-permute-start(bf16[8,8192]{1,0:T(8,128)(2,1)} %param.5), channel_id=1, source_target_pairs={{0,8},{1,9},{2,10},{3,11},{4,12},{5,13},{6,14},{7,15},{8,0},{9,1},... | collective-permute-start | bytes 393224 | tf_op jit(solution)/shard_map/ppermute | solution.py:178
  4.0 8.9 %collective-permute-start.1 = (bf16[8,8192]{1,0:T(8,128)(2,1)}, bf16[8,8192]{1,0:T(8,128)(2,1)S(1)}, u32[]{:S(2)}, u32[]{:S(2)}) collective-permute-start(bf16[8,8192]{1,0:T(8,128)(2,1)} %param.5), channel_id=1, source_target_pairs={{0,4},{1,3},{2,6},{3,1},{4,0},{5,7},{6,2},{7,5},{8,12},{9,11},{10,... | collective-permute-start | bytes 393224 | tf_op jit(solution)/shard_map/ppermute | solution.py:178
  5.6 13.8 %collective-permute-start.2 = (bf16[8,8192]{1,0:T(8,128)(2,1)}, bf16[8,8192]{1,0:T(8,128)(2,1)S(1)}, u32[]{:S(2)}, u32[]{:S(2)}) collective-permute-start(bf16[8,8192]{1,0:T(8,128)(2,1)} %param.5), channel_id=1, source_target_pairs={{0,2},{1,5},{2,0},{3,7},{4,6},{5,1},{6,4},{7,3},{8,10},{9,13},{10,... | collective-permute-start | bytes 393224 | tf_op jit(solution)/shard_map/ppermute | solution.py:178
  7.1 12.3 %collective-permute-start.3 = (bf16[8,8192]{1,0:T(8,128)(2,1)}, bf16[8,8192]{1,0:T(8,128)(2,1)S(1)}, u32[]{:S(2)}, u32[]{:S(2)}) collective-permute-start(bf16[8,8192]{1,0:T(8,128)(2,1)} %param.5), channel_id=1, source_target_pairs={{0,6},{1,7},{2,4},{3,5},{4,2},{5,3},{6,0},{7,1},{8,14},{9,15},{10,... | collective-permute-start | bytes 393224 | tf_op jit(solution)/shard_map/ppermute | solution.py:178
  10.7 8.8 %collective-permute-start.4 = (bf16[8,8192]{1,0:T(8,128)(2,1)S(1)}, bf16[8,8192]{1,0:T(8,128)(2,1)S(1)}, u32[]{:S(2)}, u32[]{:S(2)}) collective-permute-start(bf16[8,8192]{1,0:T(8,128)(2,1)S(1)} %collective-permute-done._), channel_id=1, source_target_pairs={{0,4},{1,3},{2,6},{3,1},{4,0},{5,7},{6,2},{7,5},{8,12},{9,11},{10,... | collective-permute-start | bytes 393224 | tf_op jit(solution)/shard_map/ppermute | solution.py:178
  11.4 8.0 %collective-permute-start.5 = (bf16[8,8192]{1,0:T(8,128)(2,1)S(1)}, bf16[8,8192]{1,0:T(8,128)(2,1)S(1)}, u32[]{:S(2)}, u32[]{:S(2)}) collective-permute-start(bf16[8,8192]{1,0:T(8,128)(2,1)S(1)} %collective-permute-done._), channel_id=1, source_target_pairs={{0,2},{1,5},{2,0},{3,7},{4,6},{5,1},{6,4},{7,3},{8,10},{9,13},{10,... | collective-permute-start | bytes 393224 | tf_op jit(solution)/shard_map/ppermute | solution.py:178
  12.9 7.6 %collective-permute-start.6 = (bf16[8,8192]{1,0:T(8,128)(2,1)S(1)}, bf16[8,8192]{1,0:T(8,128)(2,1)S(1)}, u32[]{:S(2)}, u32[]{:S(2)}) collective-permute-start(bf16[8,8192]{1,0:T(8,128)(2,1)S(1)} %collective-permute-done._), channel_id=1, source_target_pairs={{0,6},{1,7},{2,4},{3,5},{4,2},{5,3},{6,0},{7,1},{8,14},{9,15},{10,... | collective-permute-start | bytes 393224 | tf_op jit(solution)/shard_map/ppermute | solution.py:178
  20.6 1.8 %collective-permute-start.9 = (bf16[64,3072]{1,0:T(8,128)(2,1)S(1)}, bf16[64,3072]{1,0:T(8,128)(2,1)S(1)}, u32[]{:S(2)}, u32[]{:S(2)}) collective-permute-start(bf16[64,3072]{1,0:T(8,128)(2,1)S(1)} %constant_dynamic-update-slice_fusion.16.here_ref), channel_id=1, source_target_pairs={{0,1},{1,0},{2,3},{3,2},{4,5},{5,4},{6,7},{7,6},{8,9},{9,8},{10,11... | collective-permute-start | bytes 1179656 | tf_op jit(solution)/shard_map/ppermute | solution.py:178
  20.8 2.6 %collective-permute-start.8 = (bf16[64,2560]{1,0:T(8,128)(2,1)S(1)}, bf16[64,2560]{1,0:T(8,128)(2,1)S(1)}, u32[]{:S(2)}, u32[]{:S(2)}) collective-permute-start(bf16[64,2560]{1,0:T(8,128)(2,1)S(1)} %get-tuple-element.47.here_ref), channel_id=1, source_target_pairs={{0,1},{1,0},{2,3},{3,2},{4,5},{5,4},{6,7},{7,6},{8,9},{9,8},{10,11... | collective-permute-start | bytes 983048 | tf_op jit(solution)/shard_map/ppermute | solution.py:178
  21.3 2.9 %collective-permute-start.7 = (bf16[64,2560]{1,0:T(8,128)(2,1)S(1)}, bf16[64,2560]{1,0:T(8,128)(2,1)S(1)}, u32[]{:S(2)}, u32[]{:S(2)}) collective-permute-start(bf16[64,2560]{1,0:T(8,128)(2,1)S(1)} %get-tuple-element.48.here_ref), channel_id=1, source_target_pairs={{0,1},{1,0},{2,3},{3,2},{4,5},{5,4},{6,7},{7,6},{8,9},{9,8},{10,11... | collective-permute-start | bytes 983048 | tf_op jit(solution)/shard_map/ppermute | solution.py:178
  25.8 1.4 %collective-permute-start.10 = (bf16[8,8192]{1,0:T(8,128)(2,1)S(1)}, bf16[8,8192]{1,0:T(8,128)(2,1)S(1)}, u32[]{:S(2)}, u32[]{:S(2)}) collective-permute-start(bf16[8,8192]{1,0:T(8,128)(2,1)S(1)} %get-tuple-element.34), channel_id=1, source_target_pairs={{0,1},{1,0},{2,3},{3,2},{4,5},{5,4},{6,7},{7,6},{8,9},{9,8},{10,11... | collective-permute-start | bytes 393224 | tf_op jit(solution)/shard_map/ppermute | solution.py:178
  27.2 1.7 %collective-permute-start.11 = (bf16[24,8192]{1,0:T(8,128)(2,1)S(1)}, bf16[24,8192]{1,0:T(8,128)(2,1)S(1)}, u32[]{:S(2)}, u32[]{:S(2)}) collective-permute-start(bf16[24,8192]{1,0:T(8,128)(2,1)S(1)} %get-tuple-element.36), channel_id=1, source_target_pairs={{0,1},{1,0},{2,3},{3,2},{4,5},{5,4},{6,7},{7,6},{8,9},{9,8},{10,11... | collective-permute-start | bytes 1179656 | tf_op jit(solution)/shard_map/ppermute | solution.py:178
  27.4 7.3 %collective-permute-start.14 = (bf16[8,8192]{1,0:T(8,128)(2,1)S(1)}, bf16[8,8192]{1,0:T(8,128)(2,1)S(1)}, u32[]{:S(2)}, u32[]{:S(2)}) collective-permute-start(bf16[8,8192]{1,0:T(8,128)(2,1)S(1)} %add_convert_fusion), channel_id=1, source_target_pairs={{0,6},{1,7},{2,4},{3,5},{4,2},{5,3},{6,0},{7,1},{8,14},{9,15},{10,... | collective-permute-start | bytes 393224 | tf_op jit(solution)/shard_map/ppermute | solution.py:178
  29.0 2.3 %collective-permute-start.12 = (bf16[32,8192]{1,0:T(8,128)(2,1)S(1)}, bf16[32,8192]{1,0:T(8,128)(2,1)S(1)}, u32[]{:S(2)}, u32[]{:S(2)}) collective-permute-start(bf16[32,8192]{1,0:T(8,128)(2,1)S(1)} %get-tuple-element.38), channel_id=1, source_target_pairs={{0,1},{1,0},{2,3},{3,2},{4,5},{5,4},{6,7},{7,6},{8,9},{9,8},{10,11... | collective-permute-start | bytes 1572872 | tf_op jit(solution)/shard_map/ppermute | solution.py:178
  29.2 16.7 %copy-start = (s32[8192]{0:T(1024)S(1)}, s32[8192]{0:T(1024)}, u32[]{:S(2)}) copy-start(s32[8192]{0:T(1024)} %param.9) | copy-start | bytes 98308
  29.2 7.8 %collective-permute-start.15 = (bf16[8,8192]{1,0:T(8,128)(2,1)S(1)}, bf16[8,8192]{1,0:T(8,128)(2,1)S(1)}, u32[]{:S(2)}, u32[]{:S(2)}) collective-permute-start(bf16[8,8192]{1,0:T(8,128)(2,1)S(1)} %get-tuple-element.45), channel_id=1, source_target_pairs={{0,4},{1,3},{2,6},{3,1},{4,0},{5,7},{6,2},{7,5},{8,12},{9,11},{10,... | collective-permute-start | bytes 393224 | tf_op jit(solution)/shard_map/ppermute | solution.py:178
  30.7 6.7 %collective-permute-start.16 = (bf16[8,8192]{1,0:T(8,128)(2,1)S(1)}, bf16[8,8192]{1,0:T(8,128)(2,1)S(1)}, u32[]{:S(2)}, u32[]{:S(2)}) collective-permute-start(bf16[8,8192]{1,0:T(8,128)(2,1)S(1)} %get-tuple-element.46), channel_id=1, source_target_pairs={{0,2},{1,5},{2,0},{3,7},{4,6},{5,1},{6,4},{7,3},{8,10},{9,13},{10,... | collective-permute-start | bytes 393224 | tf_op jit(solution)/shard_map/ppermute | solution.py:178
  31.4 8.4 %collective-permute-start.13 = (bf16[16,8192]{1,0:T(8,128)(2,1)S(1)}, bf16[16,8192]{1,0:T(8,128)(2,1)S(1)}, u32[]{:S(2)}, u32[]{:S(2)}) collective-permute-start(bf16[16,8192]{1,0:T(8,128)(2,1)S(1)} %slice.174), channel_id=1, source_target_pairs={{0,4},{1,3},{2,6},{3,1},{4,0},{5,7},{6,2},{7,5},{8,12},{9,11},{10,... | collective-permute-start | bytes 786440 | tf_op jit(solution)/shard_map/ppermute | solution.py:178
  37.4 8.5 %collective-permute-start.17 = (bf16[8,8192]{1,0:T(8,128)(2,1)S(1)}, bf16[8,8192]{1,0:T(8,128)(2,1)S(1)}, u32[]{:S(2)}, u32[]{:S(2)}) collective-permute-start(bf16[8,8192]{1,0:T(8,128)(2,1)S(1)} %fusion.2), channel_id=1, source_target_pairs={{0,8},{1,9},{2,10},{3,11},{4,12},{5,13},{6,14},{7,15},{8,0},{9,1},... | collective-permute-start | bytes 393224 | tf_op jit(solution)/shard_map/ppermute | solution.py:178
  39.9 6.0 %collective-permute-start.18 = (bf16[8,8192]{1,0:T(8,128)(2,1)S(1)}, bf16[8,8192]{1,0:T(8,128)(2,1)S(1)}, u32[]{:S(2)}, u32[]{:S(2)}) collective-permute-start(bf16[8,8192]{1,0:T(8,128)(2,1)S(1)} %slice.175), channel_id=1, source_target_pairs={{0,2},{1,5},{2,0},{3,7},{4,6},{5,1},{6,4},{7,3},{8,10},{9,13},{10,... | collective-permute-start | bytes 393224 | tf_op jit(solution)/shard_map/ppermute | solution.py:178

commit v9 on v8

--- a/solution.py
+++ b/solution.py
@@ -47,15 +47,14 @@
     )(*(pltpu.with_memory_space_constraint(w, pltpu.HBM) for w in (gate_w, up_w, down_w)), after)
 
 
-def hidden_kernel(start, last, weights_ref, here_ref, there_ref, *refs):
+def hidden_kernel(start, last, weights_ref, rows_ref, *refs):
     *sums, out_ref = refs
-    width = here_ref.shape[1]
+    width = rows_ref.shape[1]
     tile = math.gcd(width, 512)
     total = sums[0][...] if sums else None
     for first in range(0, width, tile):
-        rows = jnp.concatenate([here_ref[:, first : first + tile], there_ref[:, first : first + tile]])
         span = weights_ref[:, start + first : start + first + tile]
-        part = lax.dot_general(rows, span, NT, preferred_element_type=jnp.float32)
+        part = lax.dot_general(rows_ref[:, first : first + tile], span, NT, preferred_element_type=jnp.float32)
         total = part if total is None else total + part
     if last:
         units = total.shape[1] // 2
@@ -66,53 +65,54 @@
 
 def hidden_units(weights, spans):
     units, features = weights.shape[0] // 2, weights.shape[1]
-    count = 2 * spans[0][0].shape[0]
+    count = spans[0].shape[0]
     sums, start = (), 0
     for span in spans:
-        width = span[0].shape[1]
+        width = span.shape[1]
         last = start + width == features
         shape = ((count, units), jnp.bfloat16) if last else ((count, 2 * units), jnp.float32)
         sums = (
             pl.pallas_call(
                 functools.partial(hidden_kernel, start, last),
                 out_shape=jax.ShapeDtypeStruct(*shape),
-                in_specs=[vmem()] * (3 + len(sums)),
+                in_specs=[vmem()] * (2 + len(sums)),
                 out_specs=vmem(),
                 cost_estimate=pl.CostEstimate(
                     flops=4 * units * count * width, bytes_accessed=4 * units * width, transcendentals=0
                 ),
                 compiler_params=pltpu.CompilerParams(vmem_limit_bytes=24 << 20),
-            )(weights, *span, *sums),
+            )(weights, span, *sums),
         )
         start += width
     return sums[0]
 
 
-def down_kernel(hidden_ref, down_ref, *outs):
+def down_kernel(here_ref, there_ref, down_ref, *outs):
     features = down_ref.shape[1]
+    hidden = jnp.concatenate([here_ref[...], there_ref[...]])
     tile = math.gcd(features, 512)
     for first in range(0, features, tile):
         here = slice(first, first + tile)
-        part = jnp.dot(hidden_ref[...], down_ref[:, here], preferred_element_type=jnp.float32)
+        part = jnp.dot(hidden, down_ref[:, here], preferred_element_type=jnp.float32)
         row = 0
         for out in outs:
             out[:, here] = part[row : row + out.shape[0]].astype(out.dtype)
             row += out.shape[0]
 
 
-def down(hidden, down_w, counts):
+def down(here, there, down_w, counts):
     units, features = down_w.shape
     return pl.pallas_call(
         down_kernel,
         out_shape=[jax.ShapeDtypeStruct((count, features), jnp.float32) for count in counts]
         + [jax.ShapeDtypeStruct((count, features), jnp.bfloat16) for count in counts],
-        in_specs=[vmem()] * 2,
+        in_specs=[vmem()] * 3,
         out_specs=[vmem()] * (2 * len(counts)),
         cost_estimate=pl.CostEstimate(
-            flops=2 * hidden.size * features, bytes_accessed=2 * units * features, transcendentals=0
+            flops=4 * here.size * features, bytes_accessed=2 * units * features, transcendentals=0
         ),
         compiler_params=pltpu.CompilerParams(vmem_limit_bytes=24 << 20),
-    )(hidden, down_w)
+    )(here, there, down_w)
 
 
 def signs_twice():
@@ -193,14 +193,14 @@
         for share in SPANS:
             end = start + features * share // sum(SPANS)
             span = jnp.concatenate([piece[:, start:end] for piece in gathered])
-            spans.append((span, swap(span, (1, 1))))
+            spans.append(span)
             start = end
-        hidden = hidden_units(gate_up_w, spans)
+        here = hidden_units(gate_up_w, spans)
+        there = hidden_units(gate_up_w, [swap(span, (1, 1)) for span in spans])
 
         count = others * rows
-        own, diagonal, rest, *sends = down(hidden, down_w, (4 * rows, count, 3 * count))
-        there, sends[2] = lax.optimization_barrier((swap(sends[1], (1, 1)), sends[2]))
-        diagonal = diagonal + there.astype(jnp.float32)
+        own, diagonal, rest, *sends = down(here, there, down_w, (4 * rows, count, 3 * count))
+        diagonal = diagonal + swap(sends[1], (1, 1)).astype(jnp.float32)
         diagonal = swap(diagonal.astype(jnp.bfloat16), square[2])
         rest_there, sends[0] = lax.optimization_barrier((swap(sends[2], (1, 1)), sends[0]))
         rest = rest + rest_there.astype(jnp.float32)

time: 47 us -> 48.9 us (1.040)
  Pallas kernels: 8.52 us -> 11 us
  waiting for transfers between devices: 15.4 us -> 14.7 us
    pallas_call x3 -> x6, Pallas kernels: 2.67 us -> 5.16 us  [hidden_units(): pl.pallas_call(functools.partial(hidden_kernel, start, last), out_shape=j...]
    ppermute x19, waiting for transfers between devices: 15.4 us -> 14.7 us  [swap(): lax.ppermute(value, 'gx', [(i, i ^ masks[i % 2]) for i in range(members)])]
  transfers between devices with their start and end apart: 19 -> 19, of which waited for: 10 -> 8; matrix products, arithmetic and copies ran while one was open for 5% -> 4% of each run, Pallas kernels for 13% -> 18%
where the time goes in v9:
time: 48.9 us; the launch traced here: 48.7 us
  starting transfers between devices  20.5 us (42%)
  waiting for transfers between devices  14.7 us (30%)
  Pallas kernels  11 us (22%)
  local copies, waits for them, and re-layouts  1.81 us (4%)
    ppermute x19, starting transfers between devices, swap(): lax.ppermute(value, 'gx', [(i, i ^ masks[i % 2]) for i in range(members)])  20.5 us
    ppermute x19, waiting for transfers between devices, swap(): lax.ppermute(value, 'gx', [(i, i ^ masks[i % 2]) for i in range(members)])  14.7 us
    pallas_call x6, Pallas kernels, hidden_units(): pl.pallas_call(functools.partial(hidden_kernel, start, last), out_shape=j...  5.16 us
    pallas_call x1, Pallas kernels, fetch(): pl.pallas_call(fetch_kernel, out_shape=(jax.ShapeDtypeStruct((2 * units,...  4.23 us
    unnamed x16, local copies, waits for them, and re-layouts  1.71 us
  transfers between devices with their start and end apart: 19, of which 8 were waited for; matrix products, arithmetic and copies ran while one was open for 4% of the time, Pallas kernels for 18%

profile of v9, /device:TPU:0, one launch (start us, length us, event | category | flops | bytes accessed | tf_op | source)
XLA Modules:
  0.0 48.7 jit_solution(5459995589575453631)
XLA Ops:
  0.0 4.0 %collective-permute-start = (bf16[8,8192]{1,0:T(8,128)(2,1)}, bf16[8,8192]{1,0:T(8,128)(2,1)S(1)}, u32[]{:S(2)}, u32[]{:S(2)}) collective-permute-start(bf16[8,8192]{1,0:T(8,128)(2,1)} %param.5), channel_id=1, source_target_pairs={{0,8},{1,9},{2,10},{3,11},{4,12},{5,13},{6,14},{7,15},{8,0},{9,1},... | collective-permute-start | bytes 393224 | tf_op jit(solution)/shard_map/ppermute | solution.py:178
  4.0 1.6 %collective-permute-start.1 = (bf16[8,8192]{1,0:T(8,128)(2,1)}, bf16[8,8192]{1,0:T(8,128)(2,1)S(1)}, u32[]{:S(2)}, u32[]{:S(2)}) collective-permute-start(bf16[8,8192]{1,0:T(8,128)(2,1)} %param.5), channel_id=1, source_target_pairs={{0,4},{1,3},{2,6},{3,1},{4,0},{5,7},{6,2},{7,5},{8,12},{9,11},{10,... | collective-permute-start | bytes 393224 | tf_op jit(solution)/shard_map/ppermute | solution.py:178
  5.6 1.5 %collective-permute-start.2 = (bf16[8,8192]{1,0:T(8,128)(2,1)}, bf16[8,8192]{1,0:T(8,128)(2,1)S(1)}, u32[]{:S(2)}, u32[]{:S(2)}) collective-permute-start(bf16[8,8192]{1,0:T(8,128)(2,1)} %param.5), channel_id=1, source_target_pairs={{0,2},{1,5},{2,0},{3,7},{4,6},{5,1},{6,4},{7,3},{8,10},{9,13},{10,... | collective-permute-start | bytes 393224 | tf_op jit(solution)/shard_map/ppermute | solution.py:178
  7.1 0.4 collective-permute-start.3
  7.5 0.8 %constant_dynamic-update-slice_fusion.15 = (bf16[64,2560]{1,0:T(8,128)(2,1)S(1)}, bf16[64,2560]{1,0:T(8,128)(2,1)S(1)}) fusion(bf16[8,8192]{1,0:T(8,128)(2,1)} %param.5), kind=kLoop, calls=%fused_computation.33 | loop fusion | bytes 163840
  8.3 2.3 %collective-permute-done._ = bf16[8,8192]{1,0:T(8,128)(2,1)S(1)} collective-permute-done((bf16[8,8192]{1,0:T(8,128)(2,1)}, bf16[8,8192]{1,0:T(8,128)(2,1)S(1)}, u32[]{:S(2)}, u32[]{:S(2)}) %collective-permute-start) | collective-permute-done | bytes 131104 | tf_op jit(solution)/shard_map/ppermute | solution.py:178
  10.7 0.8 %collective-permute-start.4 = (bf16[8,8192]{1,0:T(8,128)(2,1)S(1)}, bf16[8,8192]{1,0:T(8,128)(2,1)S(1)}, u32[]{:S(2)}, u32[]{:S(2)}) collective-permute-start(bf16[8,8192]{1,0:T(8,128)(2,1)S(1)} %collective-permute-done._), channel_id=1, source_target_pairs={{0,4},{1,3},{2,6},{3,1},{4,0},{5,7},{6,2},{7,5},{8,12},{9,11},{10,... | collective-permute-start | bytes 393224 | tf_op jit(solution)/shard_map/ppermute | solution.py:178
  11.4 1.5 %collective-permute-start.5 = (bf16[8,8192]{1,0:T(8,128)(2,1)S(1)}, bf16[8,8192]{1,0:T(8,128)(2,1)S(1)}, u32[]{:S(2)}, u32[]{:S(2)}) collective-permute-start(bf16[8,8192]{1,0:T(8,128)(2,1)S(1)} %collective-permute-done._), channel_id=1, source_target_pairs={{0,2},{1,5},{2,0},{3,7},{4,6},{5,1},{6,4},{7,3},{8,10},{9,13},{10,... | collective-permute-start | bytes 393224 | tf_op jit(solution)/shard_map/ppermute | solution.py:178
  12.9 0.0 collective-permute-done.1
  12.9 1.5 %collective-permute-start.6 = (bf16[8,8192]{1,0:T(8,128)(2,1)S(1)}, bf16[8,8192]{1,0:T(8,128)(2,1)S(1)}, u32[]{:S(2)}, u32[]{:S(2)}) collective-permute-start(bf16[8,8192]{1,0:T(8,128)(2,1)S(1)} %collective-permute-done._), channel_id=1, source_target_pairs={{0,6},{1,7},{2,4},{3,5},{4,2},{5,3},{6,0},{7,1},{8,14},{9,15},{10,... | collective-permute-start | bytes 393224 | tf_op jit(solution)/shard_map/ppermute | solution.py:178
  14.4 0.8 %constant_dynamic-update-slice_fusion.23 = bf16[64,3072]{1,0:T(8,128)(2,1)S(1)} fusion(bf16[8,8192]{1,0:T(8,128)(2,1)} %param.5), kind=kLoop, calls=%fused_computation.41 | loop fusion | bytes 98304
  15.2 4.2 %shard_map.55 = (bf16[448,8192]{1,0:T(8,128)(2,1)S(1)}, bf16[224,8192]{1,0:T(8,128)(2,1)S(1)}) custom-call(bf16[224,8192]{1,0:T(8,128)(2,1)} %bitcast.4, bf16[224,8192]{1,0:T(8,128)(2,1)} %bitcast.5, bf16[224,8192]{1,0:T(8,128)(2,1)} %down_hbm.1, bf16[8,8192]{1,0:T(8,128)(2,1)S(1)} %collective-permute-done._), custom_call_target="tpu_custom_call" | custom-call | bytes 11010048 | tf_op jit(solution)/shard_map/pallas_call | solution.py:36
  19.4 0.0 collective-permute-done.2
  19.4 0.0 collective-permute-done.3
  19.5 0.0 collective-permute-done.4
  19.5 0.0 collective-permute-done.5
  19.5 1.0 %collective-permute-done.6 = bf16[8,8192]{1,0:T(8,128)(2,1)S(1)} collective-permute-done((bf16[8,8192]{1,0:T(8,128)(2,1)S(1)}, bf16[8,8192]{1,0:T(8,128)(2,1)S(1)}, u32[]{:S(2)}, u32[]{:S(2)}) %collective-permute-start.6) | collective-permute-done | bytes 131104 | tf_op jit(solution)/shard_map/ppermute | solution.py:178
  20.6 0.1 collective-permute-start.9
  20.8 0.5 %collective-permute-start.8 = (bf16[64,2560]{1,0:T(8,128)(2,1)S(1)}, bf16[64,2560]{1,0:T(8,128)(2,1)S(1)}, u32[]{:S(2)}, u32[]{:S(2)}) collective-permute-start(bf16[64,2560]{1,0:T(8,128)(2,1)S(1)} %get-tuple-element.43.rows_ref), channel_id=1, source_target_pairs={{0,1},{1,0},{2,3},{3,2},{4,5},{5,4},{6,7},{7,6},{8,9},{9,8},{10,11... | collective-permute-start | bytes 983048 | tf_op jit(solution)/shard_map/ppermute | solution.py:178
  21.3 0.1 collective-permute-start.7
  21.4 0.9 %shard_map.56.refs_0_ = f32[64,448]{1,0:T(8,128)S(1)} custom-call(bf16[448,8192]{1,0:T(8,128)(2,1)S(1)} %get-tuple-element.23.weights_ref, bf16[64,3072]{1,0:T(8,128)(2,1)S(1)} %constant_dynamic-update-slice_fusion.16.rows_ref), custom_call_target="tpu_custom_call" | custom-call | flops 176160768 | bytes 2752512 | tf_op jit(solution)/shard_map/pallas_call | solution.py:75
  22.4 0.8 %shard_map.57.refs_0_ = f32[64,448]{1,0:T(8,128)S(1)} custom-call(bf16[448,8192]{1,0:T(8,128)(2,1)S(1)} %get-tuple-element.23.weights_ref, bf16[64,2560]{1,0:T(8,128)(2,1)S(1)} %get-tuple-element.43.rows_ref, f32[64,448]{1,0:T(8,128)S(1)} %shard_map.56.refs_0_), custom_call_target="tpu_custom_call" | custom-call | flops 146800640 | bytes 2293760 | tf_op jit(solution)/shard_map/pallas_call | solution.py:75
  23.1 0.9 %shard_map.58.here_ref = bf16[64,224]{1,0:T(8,128)(2,1)S(1)} custom-call(bf16[448,8192]{1,0:T(8,128)(2,1)S(1)} %get-tuple-element.23.weights_ref, bf16[64,2560]{1,0:T(8,128)(2,1)S(1)} %get-tuple-element.44.rows_ref, f32[64,448]{1,0:T(8,128)S(1)} %shard_map.57.refs_0_), custom_call_target="tpu_custom_call" | custom-call | flops 146800640 | bytes 2293760 | tf_op jit(solution)/shard_map/pallas_call | solution.py:75
  24.0 0.0 collective-permute-done.9.rows_ref
  24.0 0.9 %shard_map.59.refs_0_ = f32[64,448]{1,0:T(8,128)S(1)} custom-call(bf16[448,8192]{1,0:T(8,128)(2,1)S(1)} %get-tuple-element.23.weights_ref, bf16[64,3072]{1,0:T(8,128)(2,1)S(1)} %collective-permute-done.9.rows_ref), custom_call_target="tpu_custom_call" | custom-call | flops 176160768 | bytes 2752512 | tf_op jit(solution)/shard_map/pallas_call | solution.py:75
  25.0 0.0 collective-permute-done.8.rows_ref
  25.0 0.8 %shard_map.60.refs_0_ = f32[64,448]{1,0:T(8,128)S(1)} custom-call(bf16[448,8192]{1,0:T(8,128)(2,1)S(1)} %get-tuple-element.23.weights_ref, bf16[64,2560]{1,0:T(8,128)(2,1)S(1)} %collective-permute-done.8.rows_ref, f32[64,448]{1,0:T(8,128)S(1)} %shard_map.59.refs_0_), custom_call_target="tpu_custom_call" | custom-call | flops 146800640 | bytes 2293760 | tf_op jit(solution)/shard_map/pallas_call | solution.py:75
  25.8 0.0 collective-permute-done.7.rows_ref
  25.8 0.9 %shard_map.61.there_ref = bf16[64,224]{1,0:T(8,128)(2,1)S(1)} custom-call(bf16[448,8192]{1,0:T(8,128)(2,1)S(1)} %get-tuple-element.23.weights_ref, bf16[64,2560]{1,0:T(8,128)(2,1)S(1)} %collective-permute-done.7.rows_ref, f32[64,448]{1,0:T(8,128)S(1)} %shard_map.60.refs_0_), custom_call_target="tpu_custom_call" | custom-call | flops 146800640 | bytes 2293760 | tf_op jit(solution)/shard_map/pallas_call | solution.py:75
  26.6 0.7 %shard_map.62 = (f32[32,8192]{1,0:T(8,128)S(1)}, f32[8,8192]{1,0:T(8,128)S(1)}, f32[24,8192]{1,0:T(8,128)S(1)}, bf16[32,8192]{1,0:T(8,128)(2,1)S(1)}, bf16[8,819...) custom-call(bf16[64,224]{1,0:T(8,128)(2,1)S(1)} %shard_map.58.here_ref, bf16[64,224]{1,0:T(8,128)(2,1)S(1)} %shard_map.61.there_ref, ...), custom_call_target="tpu_custom_call" | custom-call | flops 469762048 | bytes 3670016 | tf_op jit(solution)/shard_map/pallas_call | solution.py:105
  27.4 0.5 %collective-permute-start.13 = (bf16[8,8192]{1,0:T(8,128)(2,1)S(1)}, bf16[8,8192]{1,0:T(8,128)(2,1)S(1)}, u32[]{:S(2)}, u32[]{:S(2)}) collective-permute-start(bf16[8,8192]{1,0:T(8,128)(2,1)S(1)} %get-tuple-element.38), channel_id=1, source_target_pairs={{0,1},{1,0},{2,3},{3,2},{4,5},{5,4},{6,7},{7,6},{8,9},{9,8},{10,11... | collective-permute-start | bytes 393224 | tf_op jit(solution)/shard_map/ppermute | solution.py:178
  27.9 0.1 collective-permute-start.10
  27.9 0.9 %collective-permute-done.13 = bf16[8,8192]{1,0:T(8,128)(2,1)S(1)} collective-permute-done((bf16[8,8192]{1,0:T(8,128)(2,1)S(1)}, bf16[8,8192]{1,0:T(8,128)(2,1)S(1)}, u32[]{:S(2)}, u32[]{:S(2)}) %collective-permute-start.13) | collective-permute-done | bytes 131104 | tf_op jit(solution)/shard_map/ppermute | solution.py:178
  28.9 1.2 %collective-permute-start.14 = (bf16[8,8192]{1,0:T(8,128)(2,1)S(1)}, bf16[8,8192]{1,0:T(8,128)(2,1)S(1)}, u32[]{:S(2)}, u32[]{:S(2)}) collective-permute-start(bf16[8,8192]{1,0:T(8,128)(2,1)S(1)} %add_convert_fusion), channel_id=1, source_target_pairs={{0,6},{1,7},{2,4},{3,5},{4,2},{5,3},{6,0},{7,1},{8,14},{9,15},{10,... | collective-permute-start | bytes 393224 | tf_op jit(solution)/shard_map/ppermute | solution.py:178
  30.1 0.0 collective-permute-done.10
  30.1 0.1 collective-permute-start.11
  30.2 0.1 fusion.7
  30.3 0.0 copy-start
  30.3 1.5 %collective-permute-start.16 = (bf16[8,8192]{1,0:T(8,128)(2,1)S(1)}, bf16[8,8192]{1,0:T(8,128)(2,1)S(1)}, u32[]{:S(2)}, u32[]{:S(2)}) collective-permute-start(bf16[8,8192]{1,0:T(8,128)(2,1)S(1)} %get-tuple-element.42), channel_id=1, source_target_pairs={{0,2},{1,5},{2,0},{3,7},{4,6},{5,1},{6,4},{7,3},{8,10},{9,13},{10,... | collective-permute-start | bytes 393224 | tf_op jit(solution)/shard_map/ppermute | solution.py:178
  31.8 0.9 %collective-permute-start.15 = (bf16[8,8192]{1,0:T(8,128)(2,1)S(1)}, bf16[8,8192]{1,0:T(8,128)(2,1)S(1)}, u32[]{:S(2)}, u32[]{:S(2)}) collective-permute-start(bf16[8,8192]{1,0:T(8,128)(2,1)S(1)} %get-tuple-element.41), channel_id=1, source_target_pairs={{0,4},{1,3},{2,6},{3,1},{4,0},{5,7},{6,2},{7,5},{8,12},{9,11},{10,... | collective-permute-start | bytes 393224 | tf_op jit(solution)/shard_map/ppermute | solution.py:178
  32.7 0.0 collective-permute-done.11
  32.7 0.1 convert_add_fusion
  32.8 1.2 %collective-permute-start.12 = (bf16[16,8192]{1,0:T(8,128)(2,1)S(1)}, bf16[16,8192]{1,0:T(8,128)(2,1)S(1)}, u32[]{:S(2)}, u32[]{:S(2)}) collective-permute-start(bf16[16,8192]{1,0:T(8,128)(2,1)S(1)} %slice.174), channel_id=1, source_target_pairs={{0,4},{1,3},{2,6},{3,1},{4,0},{5,7},{6,2},{7,5},{8,12},{9,11},{10,... | collective-permute-start | bytes 786440 | tf_op jit(solution)/shard_map/ppermute | solution.py:178
  34.1 2.1 %collective-permute-done.14 = bf16[8,8192]{1,0:T(8,128)(2,1)S(1)} collective-permute-done((bf16[8,8192]{1,0:T(8,128)(2,1)S(1)}, bf16[8,8192]{1,0:T(8,128)(2,1)S(1)}, u32[]{:S(2)}, u32[]{:S(2)}) %collective-permute-start.14) | collective-permute-done | bytes 131104 | tf_op jit(solution)/shard_map/ppermute | solution.py:178
  36.2 2.1 %collective-permute-done.16 = bf16[8,8192]{1,0:T(8,128)(2,1)S(1)} collective-permute-done((bf16[8,8192]{1,0:T(8,128)(2,1)S(1)}, bf16[8,8192]{1,0:T(8,128)(2,1)S(1)}, u32[]{:S(2)}, u32[]{:S(2)}) %collective-permute-start.16) | collective-permute-done | bytes 131104 | tf_op jit(solution)/shard_map/ppermute | solution.py:178
  38.3 0.1 collective-permute-done.15
  38.5 0.1 fusion.2
  38.5 2.1 %collective-permute-start.17 = (bf16[8,8192]{1,0:T(8,128)(2,1)S(1)}, bf16[8,8192]{1,0:T(8,128)(2,1)S(1)}, u32[]{:S(2)}, u32[]{:S(2)}) collective-permute-start(bf16[8,8192]{1,0:T(8,128)(2,1)S(1)} %fusion.2), channel_id=1, source_target_pairs={{0,8},{1,9},{2,10},{3,11},{4,12},{5,13},{6,14},{7,15},{8,0},{9,1},... | collective-permute-start | bytes 393224 | tf_op jit(solution)/shard_map/ppermute | solution.py:178
  40.6 0.6 %collective-permute-done.12 = bf16[16,8192]{1,0:T(8,128)(2,1)S(1)} collective-permute-done((bf16[16,8192]{1,0:T(8,128)(2,1)S(1)}, bf16[16,8192]{1,0:T(8,128)(2,1)S(1)}, u32[]{:S(2)}, u32[]{:S(2)}) %collective-permute-start.12) | collective-permute-done | bytes 262176 | tf_op jit(solution)/shard_map/ppermute | solution.py:178
  41.3 0.1 slice_add_fusion
  41.4 0.9 %collective-permute-start.18 = (bf16[8,8192]{1,0:T(8,128)(2,1)S(1)}, bf16[8,8192]{1,0:T(8,128)(2,1)S(1)}, u32[]{:S(2)}, u32[]{:S(2)}) collective-permute-start(bf16[8,8192]{1,0:T(8,128)(2,1)S(1)} %slice.175), channel_id=1, source_target_pairs={{0,2},{1,5},{2,0},{3,7},{4,6},{5,1},{6,4},{7,3},{8,10},{9,13},{10,... | collective-permute-start | bytes 393224 | tf_op jit(solution)/shard_map/ppermute | solution.py:178
  42.4 5.4 %collective-permute-done.17.refs_1_ = bf16[8,8192]{1,0:T(8,128)(2,1)S(1)} collective-permute-done((bf16[8,8192]{1,0:T(8,128)(2,1)S(1)}, bf16[8,8192]{1,0:T(8,128)(2,1)S(1)}, u32[]{:S(2)}, u32[]{:S(2)}) %collective-permute-start.17) | collective-permute-done | bytes 131104 | tf_op jit(solution)/shard_map/ppermute | solution.py:178
  47.8 0.0 collective-permute-done.18.refs_2_
  47.8 0.0 copy-done
  47.8 0.9 %shard_map.63 = bf16[8,8192]{1,0:T(8,128)(2,1)} custom-call(f32[8,8192]{1,0:T(8,128)S(1)} %slice.135.refs_0_, bf16[8,8192]{1,0:T(8,128)(2,1)S(1)} %collective-permute-done.17.refs_1_, bf16[8,8192]{1,0:T(8,128)(2,1)S(1)} %collective-permute-done.18.refs_2_, s32[1,8192]{1,0:T(1,128)S(1)} %bitcast.3, bf16[256,128]{1,0:T(8,128)(2,1)S(1)} %pad_maximum_fusion.refs_4_), custom_call_target="tpu_custom_call" | custom-call | tf_op jit(solution)/shard_map/pallas_call | solution.py:155
  (21 shorter events, 0.2 us)
Async XLA Ops:
  0.0 10.7 %collective-permute-start = (bf16[8,8192]{1,0:T(8,128)(2,1)}, bf16[8,8192]{1,0:T(8,128)(2,1)S(1)}, u32[]{:S(2)}, u32[]{:S(2)}) collective-permute-start(bf16[8,8192]{1,0:T(8,128)(2,1)} %param.5), channel_id=1, source_target_pairs={{0,8},{1,9},{2,10},{3,11},{4,12},{5,13},{6,14},{7,15},{8,0},{9,1},... | collective-permute-start | bytes 393224 | tf_op jit(solution)/shard_map/ppermute | solution.py:178
  4.0 8.9 %collective-permute-start.1 = (bf16[8,8192]{1,0:T(8,128)(2,1)}, bf16[8,8192]{1,0:T(8,128)(2,1)S(1)}, u32[]{:S(2)}, u32[]{:S(2)}) collective-permute-start(bf16[8,8192]{1,0:T(8,128)(2,1)} %param.5), channel_id=1, source_target_pairs={{0,4},{1,3},{2,6},{3,1},{4,0},{5,7},{6,2},{7,5},{8,12},{9,11},{10,... | collective-permute-start | bytes 393224 | tf_op jit(solution)/shard_map/ppermute | solution.py:178
  5.6 13.8 %collective-permute-start.2 = (bf16[8,8192]{1,0:T(8,128)(2,1)}, bf16[8,8192]{1,0:T(8,128)(2,1)S(1)}, u32[]{:S(2)}, u32[]{:S(2)}) collective-permute-start(bf16[8,8192]{1,0:T(8,128)(2,1)} %param.5), channel_id=1, source_target_pairs={{0,2},{1,5},{2,0},{3,7},{4,6},{5,1},{6,4},{7,3},{8,10},{9,13},{10,... | collective-permute-start | bytes 393224 | tf_op jit(solution)/shard_map/ppermute | solution.py:178
  7.1 12.3 %collective-permute-start.3 = (bf16[8,8192]{1,0:T(8,128)(2,1)}, bf16[8,8192]{1,0:T(8,128)(2,1)S(1)}, u32[]{:S(2)}, u32[]{:S(2)}) collective-permute-start(bf16[8,8192]{1,0:T(8,128)(2,1)} %param.5), channel_id=1, source_target_pairs={{0,6},{1,7},{2,4},{3,5},{4,2},{5,3},{6,0},{7,1},{8,14},{9,15},{10,... | collective-permute-start | bytes 393224 | tf_op jit(solution)/shard_map/ppermute | solution.py:178
  10.7 8.8 %collective-permute-start.4 = (bf16[8,8192]{1,0:T(8,128)(2,1)S(1)}, bf16[8,8192]{1,0:T(8,128)(2,1)S(1)}, u32[]{:S(2)}, u32[]{:S(2)}) collective-permute-start(bf16[8,8192]{1,0:T(8,128)(2,1)S(1)} %collective-permute-done._), channel_id=1, source_target_pairs={{0,4},{1,3},{2,6},{3,1},{4,0},{5,7},{6,2},{7,5},{8,12},{9,11},{10,... | collective-permute-start | bytes 393224 | tf_op jit(solution)/shard_map/ppermute | solution.py:178
  11.4 8.0 %collective-permute-start.5 = (bf16[8,8192]{1,0:T(8,128)(2,1)S(1)}, bf16[8,8192]{1,0:T(8,128)(2,1)S(1)}, u32[]{:S(2)}, u32[]{:S(2)}) collective-permute-start(bf16[8,8192]{1,0:T(8,128)(2,1)S(1)} %collective-permute-done._), channel_id=1, source_target_pairs={{0,2},{1,5},{2,0},{3,7},{4,6},{5,1},{6,4},{7,3},{8,10},{9,13},{10,... | collective-permute-start | bytes 393224 | tf_op jit(solution)/shard_map/ppermute | solution.py:178
  12.9 7.6 %collective-permute-start.6 = (bf16[8,8192]{1,0:T(8,128)(2,1)S(1)}, bf16[8,8192]{1,0:T(8,128)(2,1)S(1)}, u32[]{:S(2)}, u32[]{:S(2)}) collective-permute-start(bf16[8,8192]{1,0:T(8,128)(2,1)S(1)} %collective-permute-done._), channel_id=1, source_target_pairs={{0,6},{1,7},{2,4},{3,5},{4,2},{5,3},{6,0},{7,1},{8,14},{9,15},{10,... | collective-permute-start | bytes 393224 | tf_op jit(solution)/shard_map/ppermute | solution.py:178
  20.6 3.4 %collective-permute-start.9 = (bf16[64,3072]{1,0:T(8,128)(2,1)S(1)}, bf16[64,3072]{1,0:T(8,128)(2,1)S(1)}, u32[]{:S(2)}, u32[]{:S(2)}) collective-permute-start(bf16[64,3072]{1,0:T(8,128)(2,1)S(1)} %constant_dynamic-update-slice_fusion.16.rows_ref), channel_id=1, source_target_pairs={{0,1},{1,0},{2,3},{3,2},{4,5},{5,4},{6,7},{7,6},{8,9},{9,8},{10,11... | collective-permute-start | bytes 1179656 | tf_op jit(solution)/shard_map/ppermute | solution.py:178
  20.8 4.2 %collective-permute-start.8 = (bf16[64,2560]{1,0:T(8,128)(2,1)S(1)}, bf16[64,2560]{1,0:T(8,128)(2,1)S(1)}, u32[]{:S(2)}, u32[]{:S(2)}) collective-permute-start(bf16[64,2560]{1,0:T(8,128)(2,1)S(1)} %get-tuple-element.43.rows_ref), channel_id=1, source_target_pairs={{0,1},{1,0},{2,3},{3,2},{4,5},{5,4},{6,7},{7,6},{8,9},{9,8},{10,11... | collective-permute-start | bytes 983048 | tf_op jit(solution)/shard_map/ppermute | solution.py:178
  21.3 4.4 %collective-permute-start.7 = (bf16[64,2560]{1,0:T(8,128)(2,1)S(1)}, bf16[64,2560]{1,0:T(8,128)(2,1)S(1)}, u32[]{:S(2)}, u32[]{:S(2)}) collective-permute-start(bf16[64,2560]{1,0:T(8,128)(2,1)S(1)} %get-tuple-element.44.rows_ref), channel_id=1, source_target_pairs={{0,1},{1,0},{2,3},{3,2},{4,5},{5,4},{6,7},{7,6},{8,9},{9,8},{10,11... | collective-permute-start | bytes 983048 | tf_op jit(solution)/shard_map/ppermute | solution.py:178
  27.4 1.5 %collective-permute-start.13 = (bf16[8,8192]{1,0:T(8,128)(2,1)S(1)}, bf16[8,8192]{1,0:T(8,128)(2,1)S(1)}, u32[]{:S(2)}, u32[]{:S(2)}) collective-permute-start(bf16[8,8192]{1,0:T(8,128)(2,1)S(1)} %get-tuple-element.38), channel_id=1, source_target_pairs={{0,1},{1,0},{2,3},{3,2},{4,5},{5,4},{6,7},{7,6},{8,9},{9,8},{10,11... | collective-permute-start | bytes 393224 | tf_op jit(solution)/shard_map/ppermute | solution.py:178
  27.9 2.2 %collective-permute-start.10 = (bf16[24,8192]{1,0:T(8,128)(2,1)S(1)}, bf16[24,8192]{1,0:T(8,128)(2,1)S(1)}, u32[]{:S(2)}, u32[]{:S(2)}) collective-permute-start(bf16[24,8192]{1,0:T(8,128)(2,1)S(1)} %get-tuple-element.32), channel_id=1, source_target_pairs={{0,1},{1,0},{2,3},{3,2},{4,5},{5,4},{6,7},{7,6},{8,9},{9,8},{10,11... | collective-permute-start | bytes 1179656 | tf_op jit(solution)/shard_map/ppermute | solution.py:178
  28.9 7.3 %collective-permute-start.14 = (bf16[8,8192]{1,0:T(8,128)(2,1)S(1)}, bf16[8,8192]{1,0:T(8,128)(2,1)S(1)}, u32[]{:S(2)}, u32[]{:S(2)}) collective-permute-start(bf16[8,8192]{1,0:T(8,128)(2,1)S(1)} %add_convert_fusion), channel_id=1, source_target_pairs={{0,6},{1,7},{2,4},{3,5},{4,2},{5,3},{6,0},{7,1},{8,14},{9,15},{10,... | collective-permute-start | bytes 393224 | tf_op jit(solution)/shard_map/ppermute | solution.py:178
  30.1 2.6 %collective-permute-start.11 = (bf16[32,8192]{1,0:T(8,128)(2,1)S(1)}, bf16[32,8192]{1,0:T(8,128)(2,1)S(1)}, u32[]{:S(2)}, u32[]{:S(2)}) collective-permute-start(bf16[32,8192]{1,0:T(8,128)(2,1)S(1)} %get-tuple-element.34), channel_id=1, source_target_pairs={{0,1},{1,0},{2,3},{3,2},{4,5},{5,4},{6,7},{7,6},{8,9},{9,8},{10,11... | collective-permute-start | bytes 1572872 | tf_op jit(solution)/shard_map/ppermute | solution.py:178
  30.3 17.5 %copy-start = (s32[8192]{0:T(1024)S(1)}, s32[8192]{0:T(1024)}, u32[]{:S(2)}) copy-start(s32[8192]{0:T(1024)} %param.9) | copy-start | bytes 98308
  30.3 8.0 %collective-permute-start.16 = (bf16[8,8192]{1,0:T(8,128)(2,1)S(1)}, bf16[8,8192]{1,0:T(8,128)(2,1)S(1)}, u32[]{:S(2)}, u32[]{:S(2)}) collective-permute-start(bf16[8,8192]{1,0:T(8,128)(2,1)S(1)} %get-tuple-element.42), channel_id=1, source_target_pairs={{0,2},{1,5},{2,0},{3,7},{4,6},{5,1},{6,4},{7,3},{8,10},{9,13},{10,... | collective-permute-start | bytes 393224 | tf_op jit(solution)/shard_map/ppermute | solution.py:178
  31.8 6.6 %collective-permute-start.15 = (bf16[8,8192]{1,0:T(8,128)(2,1)S(1)}, bf16[8,8192]{1,0:T(8,128)(2,1)S(1)}, u32[]{:S(2)}, u32[]{:S(2)}) collective-permute-start(bf16[8,8192]{1,0:T(8,128)(2,1)S(1)} %get-tuple-element.41), channel_id=1, source_target_pairs={{0,4},{1,3},{2,6},{3,1},{4,0},{5,7},{6,2},{7,5},{8,12},{9,11},{10,... | collective-permute-start | bytes 393224 | tf_op jit(solution)/shard_map/ppermute | solution.py:178
  32.8 8.4 %collective-permute-start.12 = (bf16[16,8192]{1,0:T(8,128)(2,1)S(1)}, bf16[16,8192]{1,0:T(8,128)(2,1)S(1)}, u32[]{:S(2)}, u32[]{:S(2)}) collective-permute-start(bf16[16,8192]{1,0:T(8,128)(2,1)S(1)} %slice.174), channel_id=1, source_target_pairs={{0,4},{1,3},{2,6},{3,1},{4,0},{5,7},{6,2},{7,5},{8,12},{9,11},{10,... | collective-permute-start | bytes 786440 | tf_op jit(solution)/shard_map/ppermute | solution.py:178
  38.5 9.2 %collective-permute-start.17 = (bf16[8,8192]{1,0:T(8,128)(2,1)S(1)}, bf16[8,8192]{1,0:T(8,128)(2,1)S(1)}, u32[]{:S(2)}, u32[]{:S(2)}) collective-permute-start(bf16[8,8192]{1,0:T(8,128)(2,1)S(1)} %fusion.2), channel_id=1, source_target_pairs={{0,8},{1,9},{2,10},{3,11},{4,12},{5,13},{6,14},{7,15},{8,0},{9,1},... | collective-permute-start | bytes 393224 | tf_op jit(solution)/shard_map/ppermute | solution.py:178
  41.4 6.4 %collective-permute-start.18 = (bf16[8,8192]{1,0:T(8,128)(2,1)S(1)}, bf16[8,8192]{1,0:T(8,128)(2,1)S(1)}, u32[]{:S(2)}, u32[]{:S(2)}) collective-permute-start(bf16[8,8192]{1,0:T(8,128)(2,1)S(1)} %slice.175), channel_id=1, source_target_pairs={{0,2},{1,5},{2,0},{3,7},{4,6},{5,1},{6,4},{7,3},{8,10},{9,13},{10,... | collective-permute-start | bytes 393224 | tf_op jit(solution)/shard_map/ppermute | solution.py:178

commit v10 on v8

--- a/solution.py
+++ b/solution.py
@@ -10,7 +10,8 @@
 
 BLOCK = 128
 PIECES = 2
-SPANS = (6, 5, 5)
+SPANS = 2
+TURNS = 8
 NT = (((1,), (1,)), ((), ()))
 
 
@@ -18,72 +19,93 @@
     return pl.BlockSpec(memory_space=pltpu.VMEM)
 
 
-def fetch_kernel(gate_hbm, up_hbm, down_hbm, _, gate_up_ref, down_ref, sems):
-    units = gate_hbm.shape[0]
-    copies = [
-        pltpu.make_async_copy(gate_hbm, gate_up_ref.at[:units], sems.at[0]),
-        pltpu.make_async_copy(up_hbm, gate_up_ref.at[units:], sems.at[1]),
-        pltpu.make_async_copy(down_hbm, down_ref, sems.at[2]),
-    ]
-    for copy in copies:
-        copy.start()
-    for copy in copies:
-        copy.wait()
-
-
-def fetch(gate_w, up_w, down_w, after):
+def turn_kernel(gate_hbm, up_hbm, _, gate_ref, up_ref, staged, sems):
+    tile = staged.shape[2] // sems.shape[1]
+    copies = []
+    for k in range(sems.shape[1]):
+        here = slice(k * tile, (k + 1) * tile)
+        for j, source in enumerate((gate_hbm, up_hbm)):
+            copies.append(
+                pltpu.make_async_copy(source.at[:, here], staged.at[j, :, here], sems.at[j, k])
+            )
+            copies[-1].start()
+    for k in range(sems.shape[1]):
+        here = slice(k * tile, (k + 1) * tile)
+        for j, out in enumerate((gate_ref, up_ref)):
+            copies[2 * k + j].wait()
+            out[here, :] = staged[j, :, here].T
+
+
+def turn(gate_w, up_w, after):
     units, features = gate_w.shape
+    shape = jax.ShapeDtypeStruct((features, units), gate_w.dtype)
+    return pl.pallas_call(
+        turn_kernel,
+        out_shape=(shape, shape),
+        in_specs=[pl.BlockSpec(memory_space=pltpu.HBM)] * 2 + [pl.BlockSpec(memory_space=pl.ANY)],
+        out_specs=(vmem(), vmem()),
+        scratch_shapes=[
+            pltpu.VMEM((2, units, features), gate_w.dtype),
+            pltpu.SemaphoreType.DMA((2, TURNS)),
+        ],
+        cost_estimate=pl.CostEstimate(flops=0, bytes_accessed=4 * units * features, transcendentals=0),
+        compiler_params=pltpu.CompilerParams(vmem_limit_bytes=24 << 20),
+    )(*(pltpu.with_memory_space_constraint(w, pltpu.HBM) for w in (gate_w, up_w)), after)
+
+
+def fetch_kernel(down_hbm, down_ref, sem):
+    copy = pltpu.make_async_copy(down_hbm, down_ref, sem)
+    copy.start()
+    copy.wait()
+
+
+def fetch(down_w):
     return pl.pallas_call(
         fetch_kernel,
-        out_shape=(
-            jax.ShapeDtypeStruct((2 * units, features), gate_w.dtype),
-            jax.ShapeDtypeStruct(down_w.shape, down_w.dtype),
-        ),
-        in_specs=[pl.BlockSpec(memory_space=pltpu.HBM)] * 3 + [pl.BlockSpec(memory_space=pl.ANY)],
-        out_specs=(vmem(),) * 2,
-        scratch_shapes=[pltpu.SemaphoreType.DMA((3,))],
-        cost_estimate=pl.CostEstimate(flops=0, bytes_accessed=6 * units * features, transcendentals=0),
-        compiler_params=pltpu.CompilerParams(vmem_limit_bytes=24 << 20),
-    )(*(pltpu.with_memory_space_constraint(w, pltpu.HBM) for w in (gate_w, up_w, down_w)), after)
-
-
-def hidden_kernel(start, last, weights_ref, here_ref, there_ref, *refs):
-    *sums, out_ref = refs
-    width = here_ref.shape[1]
-    tile = math.gcd(width, 512)
-    total = sums[0][...] if sums else None
+        out_shape=jax.ShapeDtypeStruct(down_w.shape, down_w.dtype),
+        in_specs=[pl.BlockSpec(memory_space=pltpu.HBM)],
+        out_specs=vmem(),
+        scratch_shapes=[pltpu.SemaphoreType.DMA],
+        cost_estimate=pl.CostEstimate(flops=0, bytes_accessed=2 * down_w.size, transcendentals=0),
+        compiler_params=pltpu.CompilerParams(vmem_limit_bytes=4 << 20),
+    )(pltpu.with_memory_space_constraint(down_w, pltpu.HBM))
+
+
+def hidden_kernel(start, last, *refs):
+    gate_ref, up_ref, near_here, near_there, far_here, far_there, *refs = refs
+    sums, outs = refs[: len(refs) - (1 if last else 2)], refs[-1 if last else -2 :]
+    width = far_here.shape[1]
+    tile = math.gcd(width, 1024)
+    gate, up = (ref[...] for ref in sums) if sums else (0.0, 0.0)
     for first in range(0, width, tile):
-        rows = jnp.concatenate([here_ref[:, first : first + tile], there_ref[:, first : first + tile]])
-        span = weights_ref[:, start + first : start + first + tile]
-        part = lax.dot_general(rows, span, NT, preferred_element_type=jnp.float32)
-        total = part if total is None else total + part
+        here, there = slice(first, first + tile), slice(start + first, start + first + tile)
+        rows = jnp.concatenate([near_here[:, there], far_here[:, here], near_there[:, there], far_there[:, here]])
+        gate = gate + jnp.dot(rows, gate_ref[there, :], preferred_element_type=jnp.float32)
+        up = up + jnp.dot(rows, up_ref[there, :], preferred_element_type=jnp.float32)
     if last:
-        units = total.shape[1] // 2
-        gate = total[:, :units]
-        total = gate / (1.0 + jnp.exp(-gate)) * total[:, units:]
-    out_ref[...] = total.astype(out_ref.dtype)
-
-
-def hidden_units(weights, spans):
-    units, features = weights.shape[0] // 2, weights.shape[1]
-    count = 2 * spans[0][0].shape[0]
+        outs[0][...] = (gate / (1.0 + jnp.exp(-gate)) * up).astype(jnp.bfloat16)
+    else:
+        outs[0][...], outs[1][...] = gate, up
+
+
+def hidden_units(gate_w, up_w, near, spans):
+    features, units = gate_w.shape
+    count = 2 * (near[0].shape[0] + spans[0][0].shape[0])
     sums, start = (), 0
     for span in spans:
         width = span[0].shape[1]
         last = start + width == features
-        shape = ((count, units), jnp.bfloat16) if last else ((count, 2 * units), jnp.float32)
-        sums = (
-            pl.pallas_call(
-                functools.partial(hidden_kernel, start, last),
-                out_shape=jax.ShapeDtypeStruct(*shape),
-                in_specs=[vmem()] * (3 + len(sums)),
-                out_specs=vmem(),
-                cost_estimate=pl.CostEstimate(
-                    flops=4 * units * count * width, bytes_accessed=4 * units * width, transcendentals=0
-                ),
-                compiler_params=pltpu.CompilerParams(vmem_limit_bytes=24 << 20),
-            )(weights, *span, *sums),
-        )
+        total = jax.ShapeDtypeStruct((count, units), jnp.float32)
+        sums = pl.pallas_call(
+            functools.partial(hidden_kernel, start, last),
+            out_shape=(jax.ShapeDtypeStruct((count, units), jnp.bfloat16),) if last else (total, total),
+            in_specs=[vmem()] * (6 + len(sums)),
+            out_specs=(vmem(),) * (1 if last else 2),
+            cost_estimate=pl.CostEstimate(
+                flops=4 * units * count * width, bytes_accessed=4 * units * width, transcendentals=0
+            ),
+            compiler_params=pltpu.CompilerParams(vmem_limit_bytes=24 << 20),
+        )(gate_w, up_w, *near, *span, *sums)
         start += width
     return sums[0]
 
@@ -185,22 +207,27 @@
             away.append(swap(jnp.concatenate([tokens] + away), masks))
         away = jnp.concatenate(away)
         near = [swap(tokens, m) for m in square]
-        there = [swap(away, m) for m in square]
-        gate_up_w, down_w = fetch(gate_weight.T, up_weight.T, down_weight, away)
-        gate_up_w, *near, there[0], there[1], there[2] = lax.optimization_barrier((gate_up_w, *near, *there))
-        gathered = [tokens, near[1], near[0], near[2], there[2], away, *there[:2]]
-        spans, start = [], 0
-        for share in SPANS:
-            end = start + features * share // sum(SPANS)
-            span = jnp.concatenate([piece[:, start:end] for piece in gathered])
+        down_w = fetch(down_weight)
+        away, down_w = lax.optimization_barrier((away, down_w))
+        there = [swap(away, m) for m in square[:2]]
+        away, near[0] = lax.optimization_barrier((away, near[0]))
+        there.append(swap(away, square[2]))
+        gate_w, up_w = turn(gate_weight.T, up_weight.T, away)
+        there[0], *near = lax.optimization_barrier((there[0], *near))
+        near = jnp.concatenate([tokens, near[1], near[0], near[2]])
+        near_there = swap(near, (1, 1))
+        gate_w, up_w, near, *there[1:] = lax.optimization_barrier((gate_w, up_w, near, *there[1:]))
+        far_rows = [there[2], away, *there[:2]]
+        spans = []
+        width = features // SPANS
+        for k in range(SPANS):
+            span = jnp.concatenate([piece[:, k * width : (k + 1) * width] for piece in far_rows])
             spans.append((span, swap(span, (1, 1))))
-            start = end
-        hidden = hidden_units(gate_up_w, spans)
+        hidden = hidden_units(gate_w, up_w, (near, near_there), spans)
 
         count = others * rows
         own, diagonal, rest, *sends = down(hidden, down_w, (4 * rows, count, 3 * count))
-        there, sends[2] = lax.optimization_barrier((swap(sends[1], (1, 1)), sends[2]))
-        diagonal = diagonal + there.astype(jnp.float32)
+        diagonal = diagonal + swap(sends[1], (1, 1)).astype(jnp.float32)
         diagonal = swap(diagonal.astype(jnp.bfloat16), square[2])
         rest_there, sends[0] = lax.optimization_barrier((swap(sends[2], (1, 1)), sends[0]))
         rest = rest + rest_there.astype(jnp.float32)

time: 47 us -> 45.1 us (0.960)
  waiting for transfers between devices: 15.4 us -> 13.5 us
  Pallas kernels: 8.52 us -> 9.42 us
  local copies, waits for them, and re-layouts: 1.81 us -> 1.11 us
    ppermute x19, waiting for transfers between devices: 15.4 us -> 13.5 us  [swap(): lax.ppermute(value, 'gx', [(i, i ^ masks[i % 2]) for i in range(members)])]
    pallas_call x4, Pallas kernels: 6.9 us -> 7.81 us  [the longest x1 4.31 us: turn(): pl.pallas_call(turn_kernel, out_shape=(shape, shape), in_specs=[pl.BlockS...]
    unnamed x16 -> x5, local copies, waits for them, and re-layouts: 1.71 us -> 0.97 us
  transfers between devices with their start and end apart: 19 -> 19, of which waited for: 10 -> 9; matrix products, arithmetic and copies ran while one was open for 5% -> 3% of each run, Pallas kernels for 13% -> 16%
where the time goes in v10:
time: 45.1 us; the launch traced here: 44.9 us
  starting transfers between devices  20.2 us (45%)
  waiting for transfers between devices  13.5 us (30%)
  Pallas kernels  9.42 us (21%)
  local copies, waits for them, and re-layouts  1.11 us (2%)
    ppermute x19, starting transfers between devices, swap(): lax.ppermute(value, 'gx', [(i, i ^ masks[i % 2]) for i in range(members)])  20.2 us
    ppermute x19, waiting for transfers between devices, swap(): lax.ppermute(value, 'gx', [(i, i ^ masks[i % 2]) for i in range(members)])  13.5 us
    pallas_call x1, Pallas kernels, turn(): pl.pallas_call(turn_kernel, out_shape=(shape, shape), in_specs=[pl.BlockS...  4.31 us
    pallas_call x1, Pallas kernels, fetch(): pl.pallas_call(fetch_kernel, out_shape=jax.ShapeDtypeStruct(down_w.shape,...  2.05 us
    pallas_call x2, Pallas kernels, hidden_units(): pl.pallas_call(functools.partial(hidden_kernel, start, last), out_shape=(...  1.45 us
    unnamed x5, local copies, waits for them, and re-layouts  0.97 us
  transfers between devices with their start and end apart: 19, of which 9 were waited for; matrix products, arithmetic and copies ran while one was open for 3% of the time, Pallas kernels for 16%

profile of v10, /device:TPU:0, one launch (start us, length us, event | category | flops | bytes accessed | tf_op | source)
XLA Modules:
  0.0 44.9 jit_solution(5770797763032941747)
XLA Ops:
  0.0 4.0 %collective-permute-start = (bf16[8,8192]{1,0:T(8,128)(2,1)}, bf16[8,8192]{1,0:T(8,128)(2,1)S(1)}, u32[]{:S(2)}, u32[]{:S(2)}) collective-permute-start(bf16[8,8192]{1,0:T(8,128)(2,1)} %param.5), channel_id=1, source_target_pairs={{0,8},{1,9},{2,10},{3,11},{4,12},{5,13},{6,14},{7,15},{8,0},{9,1},... | collective-permute-start | bytes 393224 | tf_op jit(solution)/shard_map/ppermute | solution.py:200
  4.0 1.6 %collective-permute-start.1 = (bf16[8,8192]{1,0:T(8,128)(2,1)}, bf16[8,8192]{1,0:T(8,128)(2,1)S(1)}, u32[]{:S(2)}, u32[]{:S(2)}) collective-permute-start(bf16[8,8192]{1,0:T(8,128)(2,1)} %param.5), channel_id=1, source_target_pairs={{0,4},{1,3},{2,6},{3,1},{4,0},{5,7},{6,2},{7,5},{8,12},{9,11},{10,... | collective-permute-start | bytes 393224 | tf_op jit(solution)/shard_map/ppermute | solution.py:200
  5.6 1.5 %collective-permute-start.3 = (bf16[8,8192]{1,0:T(8,128)(2,1)}, bf16[8,8192]{1,0:T(8,128)(2,1)S(1)}, u32[]{:S(2)}, u32[]{:S(2)}) collective-permute-start(bf16[8,8192]{1,0:T(8,128)(2,1)} %param.5), channel_id=1, source_target_pairs={{0,2},{1,5},{2,0},{3,7},{4,6},{5,1},{6,4},{7,3},{8,10},{9,13},{10,... | collective-permute-start | bytes 393224 | tf_op jit(solution)/shard_map/ppermute | solution.py:200
  7.1 0.4 collective-permute-start.4
  7.5 0.9 %constant_dynamic-update-slice_fusion.3 = bf16[32,8192]{1,0:T(8,128)(2,1)S(1)} fusion(bf16[8,8192]{1,0:T(8,128)(2,1)} %param.5), kind=kLoop, calls=%fused_computation.23 | loop fusion | bytes 262144
  8.5 2.0 %shard_map.55.down_ref = bf16[224,8192]{1,0:T(8,128)(2,1)S(1)} custom-call(bf16[224,8192]{1,0:T(8,128)(2,1)} %down_hbm.1), custom_call_target="tpu_custom_call" | custom-call | bytes 3670016 | tf_op jit(solution)/shard_map/pallas_call | solution.py:63
  10.5 0.1 collective-permute-done._
  10.7 1.5 %collective-permute-start.2 = (bf16[8,8192]{1,0:T(8,128)(2,1)S(1)}, bf16[8,8192]{1,0:T(8,128)(2,1)S(1)}, u32[]{:S(2)}, u32[]{:S(2)}) collective-permute-start(bf16[8,8192]{1,0:T(8,128)(2,1)S(1)} %collective-permute-done._), channel_id=1, source_target_pairs={{0,4},{1,3},{2,6},{3,1},{4,0},{5,7},{6,2},{7,5},{8,12},{9,11},{10,... | collective-permute-start | bytes 393224 | tf_op jit(solution)/shard_map/ppermute | solution.py:200
  12.2 1.5 %collective-permute-start.5 = (bf16[8,8192]{1,0:T(8,128)(2,1)S(1)}, bf16[8,8192]{1,0:T(8,128)(2,1)S(1)}, u32[]{:S(2)}, u32[]{:S(2)}) collective-permute-start(bf16[8,8192]{1,0:T(8,128)(2,1)S(1)} %collective-permute-done._), channel_id=1, source_target_pairs={{0,2},{1,5},{2,0},{3,7},{4,6},{5,1},{6,4},{7,3},{8,10},{9,13},{10,... | collective-permute-start | bytes 393224 | tf_op jit(solution)/shard_map/ppermute | solution.py:200
  13.7 0.0 collective-permute-done.1
  13.7 0.7 %collective-permute-start.6 = (bf16[8,8192]{1,0:T(8,128)(2,1)S(1)}, bf16[8,8192]{1,0:T(8,128)(2,1)S(1)}, u32[]{:S(2)}, u32[]{:S(2)}) collective-permute-start(bf16[8,8192]{1,0:T(8,128)(2,1)S(1)} %collective-permute-done._), channel_id=1, source_target_pairs={{0,6},{1,7},{2,4},{3,5},{4,2},{5,3},{6,0},{7,1},{8,14},{9,15},{10,... | collective-permute-start | bytes 393224 | tf_op jit(solution)/shard_map/ppermute | solution.py:200
  14.4 4.3 %shard_map.56 = (bf16[8192,224]{1,0:T(8,128)(2,1)S(1)}, bf16[8192,224]{1,0:T(8,128)(2,1)S(1)}) custom-call(bf16[224,8192]{1,0:T(8,128)(2,1)} %bitcast.4, bf16[224,8192]{1,0:T(8,128)(2,1)} %bitcast.5, bf16[8,8192]{1,0:T(8,128)(2,1)S(1)} %collective-permute-done._), custom_call_target="tpu_custom_call" | custom-call | bytes 7340032 | tf_op jit(solution)/shard_map/pallas_call | solution.py:42
  18.7 0.0 collective-permute-done.3
  18.7 0.0 collective-permute-done.4
  18.8 0.0 collective-permute-done.2
  18.8 0.1 collective-permute-start.7
  18.9 1.6 %collective-permute-done.6 = bf16[8,8192]{1,0:T(8,128)(2,1)S(1)} collective-permute-done((bf16[8,8192]{1,0:T(8,128)(2,1)S(1)}, bf16[8,8192]{1,0:T(8,128)(2,1)S(1)}, u32[]{:S(2)}, u32[]{:S(2)}) %collective-permute-start.6) | collective-permute-done | bytes 131104 | tf_op jit(solution)/shard_map/ppermute | solution.py:200
  20.5 0.0 collective-permute-done.5
  20.6 0.1 collective-permute-start.9
  20.7 0.6 %collective-permute-start.8 = (bf16[32,4096]{1,0:T(8,128)(2,1)S(1)}, bf16[32,4096]{1,0:T(8,128)(2,1)S(1)}, u32[]{:S(2)}, u32[]{:S(2)}) collective-permute-start(bf16[32,4096]{1,0:T(8,128)(2,1)S(1)} %pad_maximum_fusion.refs_4_), channel_id=1, source_target_pairs={{0,1},{1,0},{2,3},{3,2},{4,5},{5,4},{6,7},{7,6},{8,9},{9,8},{10,11... | collective-permute-start | bytes 786440 | tf_op jit(solution)/shard_map/ppermute | solution.py:200
  21.2 0.9 %collective-permute-done.9.refs_5_ = bf16[32,4096]{1,0:T(8,128)(2,1)S(1)} collective-permute-done((bf16[32,4096]{1,0:T(8,128)(2,1)S(1)}, bf16[32,4096]{1,0:T(8,128)(2,1)S(1)}, u32[]{:S(2)}, u32[]{:S(2)}) %collective-permute-start.9) | collective-permute-done | bytes 262176 | tf_op jit(solution)/shard_map/ppermute | solution.py:200
  22.2 0.0 collective-permute-done.7.refs_3_
  22.2 0.7 %shard_map.57 = (f32[128,224]{1,0:T(8,128)S(1)}, f32[128,224]{1,0:T(8,128)S(1)}) custom-call(bf16[8192,224]{1,0:T(8,128)(2,1)S(1)} %get-tuple-element.38.refs_0_, bf16[8192,224]{1,0:T(8,128)(2,1)S(1)} %get-tuple-element.39.refs_1_, bf16[32,8192]{1,0:T(8,128)(2,1)S(1)} %constant_dynamic-update-slice_fusion.refs_2_, ...), custom_call_target="tpu_custom_call" | custom-call | flops 469762048 | bytes 3670016 | tf_op jit(solution)/shard_map/pallas_call | solution.py:99
  22.9 0.0 collective-permute-done.8.refs_5_
  22.9 0.7 %shard_map.58.hidden_ref = bf16[128,224]{1,0:T(8,128)(2,1)S(1)} custom-call(bf16[8192,224]{1,0:T(8,128)(2,1)S(1)} %get-tuple-element.38.refs_0_, bf16[8192,224]{1,0:T(8,128)(2,1)S(1)} %get-tuple-element.39.refs_1_, bf16[32,8192]{1,0:T(8,128)(2,1)S(1)} %constant_dynamic-update-slice_fusion.refs_2_, bf16[32,8192]{1,0:T(8,128)(2,1)S(1)} %collective-permute-done.7.refs_3_, ...), custom_call_target="tpu_custom_call" | custom-call | flops 469762048 | bytes 3670016 | tf_op jit(solution)/shard_map/pallas_call | solution.py:99
  23.7 0.7 %shard_map.59 = (f32[32,8192]{1,0:T(8,128)S(1)}, f32[8,8192]{1,0:T(8,128)S(1)}, f32[24,8192]{1,0:T(8,128)S(1)}, bf16[32,8192]{1,0:T(8,128)(2,1)S(1)}, bf16[8,819...) custom-call(bf16[128,224]{1,0:T(8,128)(2,1)S(1)} %shard_map.58.hidden_ref, bf16[224,8192]{1,0:T(8,128)(2,1)S(1)} %shard_map.55.down_ref), custom_call_target="tpu_custom_call" | custom-call | flops 469762048 | bytes 3670016 | tf_op jit(solution)/shard_map/pallas_call | solution.py:127
  24.4 0.2 collective-permute-start.13
  24.6 0.4 collective-permute-start.10
  25.0 0.8 %collective-permute-done.13 = bf16[8,8192]{1,0:T(8,128)(2,1)S(1)} collective-permute-done((bf16[8,8192]{1,0:T(8,128)(2,1)S(1)}, bf16[8,8192]{1,0:T(8,128)(2,1)S(1)}, u32[]{:S(2)}, u32[]{:S(2)}) %collective-permute-start.13) | collective-permute-done | bytes 131104 | tf_op jit(solution)/shard_map/ppermute | solution.py:200
  25.8 1.4 %collective-permute-start.14 = (bf16[8,8192]{1,0:T(8,128)(2,1)S(1)}, bf16[8,8192]{1,0:T(8,128)(2,1)S(1)}, u32[]{:S(2)}, u32[]{:S(2)}) collective-permute-start(bf16[8,8192]{1,0:T(8,128)(2,1)S(1)} %add_convert_fusion), channel_id=1, source_target_pairs={{0,6},{1,7},{2,4},{3,5},{4,2},{5,3},{6,0},{7,1},{8,14},{9,15},{10,... | collective-permute-start | bytes 393224 | tf_op jit(solution)/shard_map/ppermute | solution.py:200
  27.2 0.0 collective-permute-done.10
  27.2 0.0 collective-permute-start.11
  27.2 0.1 fusion.7
  27.3 0.0 copy-start
  27.3 1.7 %collective-permute-start.15 = (bf16[8,8192]{1,0:T(8,128)(2,1)S(1)}, bf16[8,8192]{1,0:T(8,128)(2,1)S(1)}, u32[]{:S(2)}, u32[]{:S(2)}) collective-permute-start(bf16[8,8192]{1,0:T(8,128)(2,1)S(1)} %get-tuple-element.57), channel_id=1, source_target_pairs={{0,4},{1,3},{2,6},{3,1},{4,0},{5,7},{6,2},{7,5},{8,12},{9,11},{10,... | collective-permute-start | bytes 393224 | tf_op jit(solution)/shard_map/ppermute | solution.py:200
  29.0 0.5 %collective-permute-start.16 = (bf16[8,8192]{1,0:T(8,128)(2,1)S(1)}, bf16[8,8192]{1,0:T(8,128)(2,1)S(1)}, u32[]{:S(2)}, u32[]{:S(2)}) collective-permute-start(bf16[8,8192]{1,0:T(8,128)(2,1)S(1)} %get-tuple-element.58), channel_id=1, source_target_pairs={{0,2},{1,5},{2,0},{3,7},{4,6},{5,1},{6,4},{7,3},{8,10},{9,13},{10,... | collective-permute-start | bytes 393224 | tf_op jit(solution)/shard_map/ppermute | solution.py:200
  29.6 0.0 collective-permute-done.11
  29.6 0.1 convert_add_fusion
  29.7 1.2 %collective-permute-start.12 = (bf16[16,8192]{1,0:T(8,128)(2,1)S(1)}, bf16[16,8192]{1,0:T(8,128)(2,1)S(1)}, u32[]{:S(2)}, u32[]{:S(2)}) collective-permute-start(bf16[16,8192]{1,0:T(8,128)(2,1)S(1)} %slice.83), channel_id=1, source_target_pairs={{0,4},{1,3},{2,6},{3,1},{4,0},{5,7},{6,2},{7,5},{8,12},{9,11},{10,... | collective-permute-start | bytes 786440 | tf_op jit(solution)/shard_map/ppermute | solution.py:200
  31.0 2.0 %collective-permute-done.14 = bf16[8,8192]{1,0:T(8,128)(2,1)S(1)} collective-permute-done((bf16[8,8192]{1,0:T(8,128)(2,1)S(1)}, bf16[8,8192]{1,0:T(8,128)(2,1)S(1)}, u32[]{:S(2)}, u32[]{:S(2)}) %collective-permute-start.14) | collective-permute-done | bytes 131104 | tf_op jit(solution)/shard_map/ppermute | solution.py:200
  33.0 2.2 %collective-permute-done.15 = bf16[8,8192]{1,0:T(8,128)(2,1)S(1)} collective-permute-done((bf16[8,8192]{1,0:T(8,128)(2,1)S(1)}, bf16[8,8192]{1,0:T(8,128)(2,1)S(1)}, u32[]{:S(2)}, u32[]{:S(2)}) %collective-permute-start.15) | collective-permute-done | bytes 131104 | tf_op jit(solution)/shard_map/ppermute | solution.py:200
  35.2 0.5 %collective-permute-done.16 = bf16[8,8192]{1,0:T(8,128)(2,1)S(1)} collective-permute-done((bf16[8,8192]{1,0:T(8,128)(2,1)S(1)}, bf16[8,8192]{1,0:T(8,128)(2,1)S(1)}, u32[]{:S(2)}, u32[]{:S(2)}) %collective-permute-start.16) | collective-permute-done | bytes 131104 | tf_op jit(solution)/shard_map/ppermute | solution.py:200
  35.7 0.1 fusion.2
  35.7 1.9 %collective-permute-start.17 = (bf16[8,8192]{1,0:T(8,128)(2,1)S(1)}, bf16[8,8192]{1,0:T(8,128)(2,1)S(1)}, u32[]{:S(2)}, u32[]{:S(2)}) collective-permute-start(bf16[8,8192]{1,0:T(8,128)(2,1)S(1)} %fusion.2), channel_id=1, source_target_pairs={{0,8},{1,9},{2,10},{3,11},{4,12},{5,13},{6,14},{7,15},{8,0},{9,1},... | collective-permute-start | bytes 393224 | tf_op jit(solution)/shard_map/ppermute | solution.py:200
  37.6 0.4 collective-permute-done.12
  38.0 0.1 slice_add_fusion
  38.1 1.0 %collective-permute-start.18 = (bf16[8,8192]{1,0:T(8,128)(2,1)S(1)}, bf16[8,8192]{1,0:T(8,128)(2,1)S(1)}, u32[]{:S(2)}, u32[]{:S(2)}) collective-permute-start(bf16[8,8192]{1,0:T(8,128)(2,1)S(1)} %slice.84), channel_id=1, source_target_pairs={{0,2},{1,5},{2,0},{3,7},{4,6},{5,1},{6,4},{7,3},{8,10},{9,13},{10,... | collective-permute-start | bytes 393224 | tf_op jit(solution)/shard_map/ppermute | solution.py:200
  39.1 4.9 %collective-permute-done.17.refs_1_ = bf16[8,8192]{1,0:T(8,128)(2,1)S(1)} collective-permute-done((bf16[8,8192]{1,0:T(8,128)(2,1)S(1)}, bf16[8,8192]{1,0:T(8,128)(2,1)S(1)}, u32[]{:S(2)}, u32[]{:S(2)}) %collective-permute-start.17) | collective-permute-done | bytes 131104 | tf_op jit(solution)/shard_map/ppermute | solution.py:200
  44.0 0.0 collective-permute-done.18.refs_2_
  44.0 0.0 copy-done
  44.0 0.9 %shard_map.60 = bf16[8,8192]{1,0:T(8,128)(2,1)} custom-call(f32[8,8192]{1,0:T(8,128)S(1)} %slice.68.refs_0_, bf16[8,8192]{1,0:T(8,128)(2,1)S(1)} %collective-permute-done.17.refs_1_, bf16[8,8192]{1,0:T(8,128)(2,1)S(1)} %collective-permute-done.18.refs_2_, s32[1,8192]{1,0:T(1,128)S(1)} %bitcast.3, bf16[256,128]{1,0:T(8,128)(2,1)S(1)} %pad_maximum_fusion.2.refs_4_), custom_call_target="tpu_custom_call" | custom-call | tf_op jit(solution)/shard_map/pallas_call | solution.py:177
  (15 shorter events, 0.3 us)
Async XLA Ops:
  0.0 10.7 %collective-permute-start = (bf16[8,8192]{1,0:T(8,128)(2,1)}, bf16[8,8192]{1,0:T(8,128)(2,1)S(1)}, u32[]{:S(2)}, u32[]{:S(2)}) collective-permute-start(bf16[8,8192]{1,0:T(8,128)(2,1)} %param.5), channel_id=1, source_target_pairs={{0,8},{1,9},{2,10},{3,11},{4,12},{5,13},{6,14},{7,15},{8,0},{9,1},... | collective-permute-start | bytes 393224 | tf_op jit(solution)/shard_map/ppermute | solution.py:200
  4.0 9.7 %collective-permute-start.1 = (bf16[8,8192]{1,0:T(8,128)(2,1)}, bf16[8,8192]{1,0:T(8,128)(2,1)S(1)}, u32[]{:S(2)}, u32[]{:S(2)}) collective-permute-start(bf16[8,8192]{1,0:T(8,128)(2,1)} %param.5), channel_id=1, source_target_pairs={{0,4},{1,3},{2,6},{3,1},{4,0},{5,7},{6,2},{7,5},{8,12},{9,11},{10,... | collective-permute-start | bytes 393224 | tf_op jit(solution)/shard_map/ppermute | solution.py:200
  5.6 13.1 %collective-permute-start.3 = (bf16[8,8192]{1,0:T(8,128)(2,1)}, bf16[8,8192]{1,0:T(8,128)(2,1)S(1)}, u32[]{:S(2)}, u32[]{:S(2)}) collective-permute-start(bf16[8,8192]{1,0:T(8,128)(2,1)} %param.5), channel_id=1, source_target_pairs={{0,2},{1,5},{2,0},{3,7},{4,6},{5,1},{6,4},{7,3},{8,10},{9,13},{10,... | collective-permute-start | bytes 393224 | tf_op jit(solution)/shard_map/ppermute | solution.py:200
  7.1 11.6 %collective-permute-start.4 = (bf16[8,8192]{1,0:T(8,128)(2,1)}, bf16[8,8192]{1,0:T(8,128)(2,1)S(1)}, u32[]{:S(2)}, u32[]{:S(2)}) collective-permute-start(bf16[8,8192]{1,0:T(8,128)(2,1)} %param.5), channel_id=1, source_target_pairs={{0,6},{1,7},{2,4},{3,5},{4,2},{5,3},{6,0},{7,1},{8,14},{9,15},{10,... | collective-permute-start | bytes 393224 | tf_op jit(solution)/shard_map/ppermute | solution.py:200
  10.7 8.1 %collective-permute-start.2 = (bf16[8,8192]{1,0:T(8,128)(2,1)S(1)}, bf16[8,8192]{1,0:T(8,128)(2,1)S(1)}, u32[]{:S(2)}, u32[]{:S(2)}) collective-permute-start(bf16[8,8192]{1,0:T(8,128)(2,1)S(1)} %collective-permute-done._), channel_id=1, source_target_pairs={{0,4},{1,3},{2,6},{3,1},{4,0},{5,7},{6,2},{7,5},{8,12},{9,11},{10,... | collective-permute-start | bytes 393224 | tf_op jit(solution)/shard_map/ppermute | solution.py:200
  12.2 8.3 %collective-permute-start.5 = (bf16[8,8192]{1,0:T(8,128)(2,1)S(1)}, bf16[8,8192]{1,0:T(8,128)(2,1)S(1)}, u32[]{:S(2)}, u32[]{:S(2)}) collective-permute-start(bf16[8,8192]{1,0:T(8,128)(2,1)S(1)} %collective-permute-done._), channel_id=1, source_target_pairs={{0,2},{1,5},{2,0},{3,7},{4,6},{5,1},{6,4},{7,3},{8,10},{9,13},{10,... | collective-permute-start | bytes 393224 | tf_op jit(solution)/shard_map/ppermute | solution.py:200
  13.7 6.8 %collective-permute-start.6 = (bf16[8,8192]{1,0:T(8,128)(2,1)S(1)}, bf16[8,8192]{1,0:T(8,128)(2,1)S(1)}, u32[]{:S(2)}, u32[]{:S(2)}) collective-permute-start(bf16[8,8192]{1,0:T(8,128)(2,1)S(1)} %collective-permute-done._), channel_id=1, source_target_pairs={{0,6},{1,7},{2,4},{3,5},{4,2},{5,3},{6,0},{7,1},{8,14},{9,15},{10,... | collective-permute-start | bytes 393224 | tf_op jit(solution)/shard_map/ppermute | solution.py:200
  18.8 3.4 %collective-permute-start.7 = (bf16[32,8192]{1,0:T(8,128)(2,1)S(1)}, bf16[32,8192]{1,0:T(8,128)(2,1)S(1)}, u32[]{:S(2)}, u32[]{:S(2)}) collective-permute-start(bf16[32,8192]{1,0:T(8,128)(2,1)S(1)} %constant_dynamic-update-slice_fusion.refs_2_), channel_id=1, source_target_pairs={{0,1},{1,0},{2,3},{3,2},{4,5},{5,4},{6,7},{7,6},{8,9},{9,8},{10,11... | collective-permute-start | bytes 1572872 | tf_op jit(solution)/shard_map/ppermute | solution.py:200
  20.6 1.6 %collective-permute-start.9 = (bf16[32,4096]{1,0:T(8,128)(2,1)S(1)}, bf16[32,4096]{1,0:T(8,128)(2,1)S(1)}, u32[]{:S(2)}, u32[]{:S(2)}) collective-permute-start(bf16[32,4096]{1,0:T(8,128)(2,1)S(1)} %pad_maximum_fusion.1.refs_4_), channel_id=1, source_target_pairs={{0,1},{1,0},{2,3},{3,2},{4,5},{5,4},{6,7},{7,6},{8,9},{9,8},{10,11... | collective-permute-start | bytes 786440 | tf_op jit(solution)/shard_map/ppermute | solution.py:200
  20.7 2.2 %collective-permute-start.8 = (bf16[32,4096]{1,0:T(8,128)(2,1)S(1)}, bf16[32,4096]{1,0:T(8,128)(2,1)S(1)}, u32[]{:S(2)}, u32[]{:S(2)}) collective-permute-start(bf16[32,4096]{1,0:T(8,128)(2,1)S(1)} %pad_maximum_fusion.refs_4_), channel_id=1, source_target_pairs={{0,1},{1,0},{2,3},{3,2},{4,5},{5,4},{6,7},{7,6},{8,9},{9,8},{10,11... | collective-permute-start | bytes 786440 | tf_op jit(solution)/shard_map/ppermute | solution.py:200
  24.4 1.4 %collective-permute-start.13 = (bf16[8,8192]{1,0:T(8,128)(2,1)S(1)}, bf16[8,8192]{1,0:T(8,128)(2,1)S(1)}, u32[]{:S(2)}, u32[]{:S(2)}) collective-permute-start(bf16[8,8192]{1,0:T(8,128)(2,1)S(1)} %get-tuple-element.54), channel_id=1, source_target_pairs={{0,1},{1,0},{2,3},{3,2},{4,5},{5,4},{6,7},{7,6},{8,9},{9,8},{10,11... | collective-permute-start | bytes 393224 | tf_op jit(solution)/shard_map/ppermute | solution.py:200
  24.6 2.6 %collective-permute-start.10 = (bf16[24,8192]{1,0:T(8,128)(2,1)S(1)}, bf16[24,8192]{1,0:T(8,128)(2,1)S(1)}, u32[]{:S(2)}, u32[]{:S(2)}) collective-permute-start(bf16[24,8192]{1,0:T(8,128)(2,1)S(1)} %get-tuple-element.48), channel_id=1, source_target_pairs={{0,1},{1,0},{2,3},{3,2},{4,5},{5,4},{6,7},{7,6},{8,9},{9,8},{10,11... | collective-permute-start | bytes 1179656 | tf_op jit(solution)/shard_map/ppermute | solution.py:200
  25.8 7.2 %collective-permute-start.14 = (bf16[8,8192]{1,0:T(8,128)(2,1)S(1)}, bf16[8,8192]{1,0:T(8,128)(2,1)S(1)}, u32[]{:S(2)}, u32[]{:S(2)}) collective-permute-start(bf16[8,8192]{1,0:T(8,128)(2,1)S(1)} %add_convert_fusion), channel_id=1, source_target_pairs={{0,6},{1,7},{2,4},{3,5},{4,2},{5,3},{6,0},{7,1},{8,14},{9,15},{10,... | collective-permute-start | bytes 393224 | tf_op jit(solution)/shard_map/ppermute | solution.py:200
  27.2 2.4 %collective-permute-start.11 = (bf16[32,8192]{1,0:T(8,128)(2,1)S(1)}, bf16[32,8192]{1,0:T(8,128)(2,1)S(1)}, u32[]{:S(2)}, u32[]{:S(2)}) collective-permute-start(bf16[32,8192]{1,0:T(8,128)(2,1)S(1)} %get-tuple-element.50), channel_id=1, source_target_pairs={{0,1},{1,0},{2,3},{3,2},{4,5},{5,4},{6,7},{7,6},{8,9},{9,8},{10,11... | collective-permute-start | bytes 1572872 | tf_op jit(solution)/shard_map/ppermute | solution.py:200
  27.3 16.7 %copy-start = (s32[8192]{0:T(1024)S(1)}, s32[8192]{0:T(1024)}, u32[]{:S(2)}) copy-start(s32[8192]{0:T(1024)} %param.9) | copy-start | bytes 98308
  27.3 7.9 %collective-permute-start.15 = (bf16[8,8192]{1,0:T(8,128)(2,1)S(1)}, bf16[8,8192]{1,0:T(8,128)(2,1)S(1)}, u32[]{:S(2)}, u32[]{:S(2)}) collective-permute-start(bf16[8,8192]{1,0:T(8,128)(2,1)S(1)} %get-tuple-element.57), channel_id=1, source_target_pairs={{0,4},{1,3},{2,6},{3,1},{4,0},{5,7},{6,2},{7,5},{8,12},{9,11},{10,... | collective-permute-start | bytes 393224 | tf_op jit(solution)/shard_map/ppermute | solution.py:200
  29.0 6.6 %collective-permute-start.16 = (bf16[8,8192]{1,0:T(8,128)(2,1)S(1)}, bf16[8,8192]{1,0:T(8,128)(2,1)S(1)}, u32[]{:S(2)}, u32[]{:S(2)}) collective-permute-start(bf16[8,8192]{1,0:T(8,128)(2,1)S(1)} %get-tuple-element.58), channel_id=1, source_target_pairs={{0,2},{1,5},{2,0},{3,7},{4,6},{5,1},{6,4},{7,3},{8,10},{9,13},{10,... | collective-permute-start | bytes 393224 | tf_op jit(solution)/shard_map/ppermute | solution.py:200
  29.7 8.3 %collective-permute-start.12 = (bf16[16,8192]{1,0:T(8,128)(2,1)S(1)}, bf16[16,8192]{1,0:T(8,128)(2,1)S(1)}, u32[]{:S(2)}, u32[]{:S(2)}) collective-permute-start(bf16[16,8192]{1,0:T(8,128)(2,1)S(1)} %slice.83), channel_id=1, source_target_pairs={{0,4},{1,3},{2,6},{3,1},{4,0},{5,7},{6,2},{7,5},{8,12},{9,11},{10,... | collective-permute-start | bytes 786440 | tf_op jit(solution)/shard_map/ppermute | solution.py:200
  35.7 8.3 %collective-permute-start.17 = (bf16[8,8192]{1,0:T(8,128)(2,1)S(1)}, bf16[8,8192]{1,0:T(8,128)(2,1)S(1)}, u32[]{:S(2)}, u32[]{:S(2)}) collective-permute-start(bf16[8,8192]{1,0:T(8,128)(2,1)S(1)} %fusion.2), channel_id=1, source_target_pairs={{0,8},{1,9},{2,10},{3,11},{4,12},{5,13},{6,14},{7,15},{8,0},{9,1},... | collective-permute-start | bytes 393224 | tf_op jit(solution)/shard_map/ppermute | solution.py:200
  38.1 5.9 %collective-permute-start.18 = (bf16[8,8192]{1,0:T(8,128)(2,1)S(1)}, bf16[8,8192]{1,0:T(8,128)(2,1)S(1)}, u32[]{:S(2)}, u32[]{:S(2)}) collective-permute-start(bf16[8,8192]{1,0:T(8,128)(2,1)S(1)} %slice.84), channel_id=1, source_target_pairs={{0,2},{1,5},{2,0},{3,7},{4,6},{5,1},{6,4},{7,3},{8,10},{9,13},{10,... | collective-permute-start | bytes 393224 | tf_op jit(solution)/shard_map/ppermute | solution.py:200

commit v11 on v10

--- a/solution.py
+++ b/solution.py
@@ -19,7 +19,7 @@
     return pl.BlockSpec(memory_space=pltpu.VMEM)
 
 
-def turn_kernel(gate_hbm, up_hbm, _, gate_ref, up_ref, staged, sems):
+def load_kernel(gate_hbm, up_hbm, down_hbm, _, gate_ref, up_ref, down_ref, staged, sems, down_sem):
     tile = staged.shape[2] // sems.shape[1]
     copies = []
     for k in range(sems.shape[1]):
@@ -29,46 +29,32 @@
                 pltpu.make_async_copy(source.at[:, here], staged.at[j, :, here], sems.at[j, k])
             )
             copies[-1].start()
+    down_copy = pltpu.make_async_copy(down_hbm, down_ref, down_sem)
+    down_copy.start()
     for k in range(sems.shape[1]):
         here = slice(k * tile, (k + 1) * tile)
         for j, out in enumerate((gate_ref, up_ref)):
             copies[2 * k + j].wait()
             out[here, :] = staged[j, :, here].T
-
-
-def turn(gate_w, up_w, after):
+    down_copy.wait()
+
+
+def load(gate_w, up_w, down_w, after):
     units, features = gate_w.shape
     shape = jax.ShapeDtypeStruct((features, units), gate_w.dtype)
     return pl.pallas_call(
-        turn_kernel,
-        out_shape=(shape, shape),
-        in_specs=[pl.BlockSpec(memory_space=pltpu.HBM)] * 2 + [pl.BlockSpec(memory_space=pl.ANY)],
-        out_specs=(vmem(), vmem()),
+        load_kernel,
+        out_shape=(shape, shape, jax.ShapeDtypeStruct(down_w.shape, down_w.dtype)),
+        in_specs=[pl.BlockSpec(memory_space=pltpu.HBM)] * 3 + [pl.BlockSpec(memory_space=pl.ANY)],
+        out_specs=(vmem(),) * 3,
         scratch_shapes=[
             pltpu.VMEM((2, units, features), gate_w.dtype),
             pltpu.SemaphoreType.DMA((2, TURNS)),
+            pltpu.SemaphoreType.DMA,
         ],
-        cost_estimate=pl.CostEstimate(flops=0, bytes_accessed=4 * units * features, transcendentals=0),
+        cost_estimate=pl.CostEstimate(flops=0, bytes_accessed=6 * units * features, transcendentals=0),
         compiler_params=pltpu.CompilerParams(vmem_limit_bytes=24 << 20),
-    )(*(pltpu.with_memory_space_constraint(w, pltpu.HBM) for w in (gate_w, up_w)), after)
-
-
-def fetch_kernel(down_hbm, down_ref, sem):
-    copy = pltpu.make_async_copy(down_hbm, down_ref, sem)
-    copy.start()
-    copy.wait()
-
-
-def fetch(down_w):
-    return pl.pallas_call(
-        fetch_kernel,
-        out_shape=jax.ShapeDtypeStruct(down_w.shape, down_w.dtype),
-        in_specs=[pl.BlockSpec(memory_space=pltpu.HBM)],
-        out_specs=vmem(),
-        scratch_shapes=[pltpu.SemaphoreType.DMA],
-        cost_estimate=pl.CostEstimate(flops=0, bytes_accessed=2 * down_w.size, transcendentals=0),
-        compiler_params=pltpu.CompilerParams(vmem_limit_bytes=4 << 20),
-    )(pltpu.with_memory_space_constraint(down_w, pltpu.HBM))
+    )(*(pltpu.with_memory_space_constraint(w, pltpu.HBM) for w in (gate_w, up_w, down_w)), after)
 
 
 def hidden_kernel(start, last, *refs):
@@ -110,22 +96,23 @@
     return sums[0]
 
 
-def down_kernel(hidden_ref, down_ref, *outs):
-    features = down_ref.shape[1]
+def down_kernel(spans, hidden_ref, down_ref, *outs):
+    half, features = hidden_ref.shape[0] // 2, down_ref.shape[1]
     tile = math.gcd(features, 512)
     for first in range(0, features, tile):
         here = slice(first, first + tile)
         part = jnp.dot(hidden_ref[...], down_ref[:, here], preferred_element_type=jnp.float32)
-        row = 0
-        for out in outs:
-            out[:, here] = part[row : row + out.shape[0]].astype(out.dtype)
-            row += out.shape[0]
-
-
-def down(hidden, down_w, counts):
+        for k, out in enumerate(outs):
+            begin = 0 if k < len(spans) else half
+            rows = [part[begin + first : begin + last] for first, last in spans[k % len(spans)]]
+            out[:, here] = jnp.concatenate(rows).astype(out.dtype)
+
+
+def down(hidden, down_w, spans):
     units, features = down_w.shape
+    counts = [sum(last - first for first, last in span) for span in spans]
     return pl.pallas_call(
-        down_kernel,
+        functools.partial(down_kernel, spans),
         out_shape=[jax.ShapeDtypeStruct((count, features), jnp.float32) for count in counts]
         + [jax.ShapeDtypeStruct((count, features), jnp.bfloat16) for count in counts],
         in_specs=[vmem()] * 2,
@@ -206,27 +193,30 @@
         for masks in far:
             away.append(swap(jnp.concatenate([tokens] + away), masks))
         away = jnp.concatenate(away)
-        near = [swap(tokens, m) for m in square]
-        down_w = fetch(down_weight)
-        away, down_w = lax.optimization_barrier((away, down_w))
-        there = [swap(away, m) for m in square[:2]]
-        away, near[0] = lax.optimization_barrier((away, near[0]))
-        there.append(swap(away, square[2]))
-        gate_w, up_w = turn(gate_weight.T, up_weight.T, away)
-        there[0], *near = lax.optimization_barrier((there[0], *near))
-        near = jnp.concatenate([tokens, near[1], near[0], near[2]])
-        near_there = swap(near, (1, 1))
-        gate_w, up_w, near, *there[1:] = lax.optimization_barrier((gate_w, up_w, near, *there[1:]))
-        far_rows = [there[2], away, *there[:2]]
+        near = [swap(tokens, m) for m in square[:2]]
+        gate_w, up_w, down_w = load(gate_weight.T, up_weight.T, down_weight, away)
+        first = swap(away, square[0])
+        both = swap(jnp.concatenate([away, near[0]]), square[1])
+        diagonal = swap(away, square[2])
+        first, *near = lax.optimization_barrier((first, *near))
+        early = jnp.concatenate([tokens, near[1], near[0], away])
+        early_there = swap(early, (1, 1))
+        gate_w, up_w, early, both, diagonal = lax.optimization_barrier((gate_w, up_w, early, both, diagonal))
+        count = others * rows
+        late = [both[count:], diagonal, first, both[:count]]
         spans = []
         width = features // SPANS
         for k in range(SPANS):
-            span = jnp.concatenate([piece[:, k * width : (k + 1) * width] for piece in far_rows])
+            span = jnp.concatenate([piece[:, k * width : (k + 1) * width] for piece in late])
             spans.append((span, swap(span, (1, 1))))
-        hidden = hidden_units(gate_w, up_w, (near, near_there), spans)
-
-        count = others * rows
-        own, diagonal, rest, *sends = down(hidden, down_w, (4 * rows, count, 3 * count))
+        hidden = hidden_units(gate_w, up_w, (early, early_there), spans)
+
+        a, b = 3 * rows, 3 * rows + count
+        own_rows = ((0, a), (b, b + rows))
+        rest_rows = ((a, b), (b + rows + count, b + rows + 3 * count))
+        own, diagonal, rest, *sends = down(
+            hidden, down_w, (own_rows, ((b + rows, b + rows + count),), rest_rows)
+        )
         diagonal = diagonal + swap(sends[1], (1, 1)).astype(jnp.float32)
         diagonal = swap(diagonal.astype(jnp.bfloat16), square[2])
         rest_there, sends[0] = lax.optimization_barrier((swap(sends[2], (1, 1)), sends[0]))

time: 45.1 us -> 46.2 us (1.024)
  waiting for transfers between devices: 13.5 us -> 17.2 us
  Pallas kernels: 9.42 us -> 7.48 us
  starting transfers between devices: 20.2 us -> 19.7 us
    ppermute x19 -> x18, waiting for transfers between devices: 13.5 us -> 17.2 us  [swap(): lax.ppermute(value, 'gx', [(i, i ^ masks[i % 2]) for i in range(members)])]
    pallas_call x3 -> x2, Pallas kernels: 7.08 us -> 5.14 us  [the longest x1 4.43 us: load(): pl.pallas_call(load_kernel, out_shape=(shape, shape, jax.ShapeDtypeStruct...]
    ppermute x19 -> x18, starting transfers between devices: 20.2 us -> 19.7 us  [swap(): lax.ppermute(value, 'gx', [(i, i ^ masks[i % 2]) for i in range(members)])]
  transfers between devices with their start and end apart: 19 -> 18, of which waited for: 9 -> 10; matrix products, arithmetic and copies ran while one was open for 3% -> 3% of each run, Pallas kernels for 16% -> 11%
where the time goes in v11:
time: 46.2 us; the launch traced here: 46.1 us
  starting transfers between devices  19.7 us (43%)
  waiting for transfers between devices  17.2 us (37%)
  Pallas kernels  7.48 us (16%)
  local copies, waits for them, and re-layouts  1.11 us (2%)
    ppermute x18, starting transfers between devices, swap(): lax.ppermute(value, 'gx', [(i, i ^ masks[i % 2]) for i in range(members)])  19.7 us
    ppermute x18, waiting for transfers between devices, swap(): lax.ppermute(value, 'gx', [(i, i ^ masks[i % 2]) for i in range(members)])  17.2 us
    pallas_call x1, Pallas kernels, load(): pl.pallas_call(load_kernel, out_shape=(shape, shape, jax.ShapeDtypeStruct...  4.43 us
    pallas_call x2, Pallas kernels, hidden_units(): pl.pallas_call(functools.partial(hidden_kernel, start, last), out_shape=(...  1.45 us
    unnamed x5, local copies, waits for them, and re-layouts  0.97 us
  transfers between devices with their start and end apart: 18, of which 10 were waited for; matrix products, arithmetic and copies ran while one was open for 3% of the time, Pallas kernels for 11%

profile of v11, /device:TPU:0, one launch (start us, length us, event | category | flops | bytes accessed | tf_op | source)
XLA Modules:
  0.0 46.1 jit_solution(5213312045628459599)
XLA Ops:
  0.0 4.0 %collective-permute-start = (bf16[8,8192]{1,0:T(8,128)(2,1)}, bf16[8,8192]{1,0:T(8,128)(2,1)S(1)}, u32[]{:S(2)}, u32[]{:S(2)}) collective-permute-start(bf16[8,8192]{1,0:T(8,128)(2,1)} %param.5), channel_id=1, source_target_pairs={{0,8},{1,9},{2,10},{3,11},{4,12},{5,13},{6,14},{7,15},{8,0},{9,1},... | collective-permute-start | bytes 393224 | tf_op jit(solution)/shard_map/ppermute | solution.py:187
  4.0 1.6 %collective-permute-start.2 = (bf16[8,8192]{1,0:T(8,128)(2,1)}, bf16[8,8192]{1,0:T(8,128)(2,1)S(1)}, u32[]{:S(2)}, u32[]{:S(2)}) collective-permute-start(bf16[8,8192]{1,0:T(8,128)(2,1)} %param.5), channel_id=1, source_target_pairs={{0,4},{1,3},{2,6},{3,1},{4,0},{5,7},{6,2},{7,5},{8,12},{9,11},{10,... | collective-permute-start | bytes 393224 | tf_op jit(solution)/shard_map/ppermute | solution.py:187
  5.6 1.5 %collective-permute-start.3 = (bf16[8,8192]{1,0:T(8,128)(2,1)}, bf16[8,8192]{1,0:T(8,128)(2,1)S(1)}, u32[]{:S(2)}, u32[]{:S(2)}) collective-permute-start(bf16[8,8192]{1,0:T(8,128)(2,1)} %param.5), channel_id=1, source_target_pairs={{0,2},{1,5},{2,0},{3,7},{4,6},{5,1},{6,4},{7,3},{8,10},{9,13},{10,... | collective-permute-start | bytes 393224 | tf_op jit(solution)/shard_map/ppermute | solution.py:187
  7.1 0.9 %constant_dynamic-update-slice_fusion.3 = bf16[32,8192]{1,0:T(8,128)(2,1)S(1)} fusion(bf16[8,8192]{1,0:T(8,128)(2,1)} %param.5), kind=kLoop, calls=%fused_computation.24 | loop fusion | bytes 262144
  8.1 2.6 %collective-permute-done._ = bf16[8,8192]{1,0:T(8,128)(2,1)S(1)} collective-permute-done((bf16[8,8192]{1,0:T(8,128)(2,1)}, bf16[8,8192]{1,0:T(8,128)(2,1)S(1)}, u32[]{:S(2)}, u32[]{:S(2)}) %collective-permute-start) | collective-permute-done | bytes 131104 | tf_op jit(solution)/shard_map/ppermute | solution.py:187
  10.7 0.8 %collective-permute-start.1 = (bf16[8,8192]{1,0:T(8,128)(2,1)S(1)}, bf16[8,8192]{1,0:T(8,128)(2,1)S(1)}, u32[]{:S(2)}, u32[]{:S(2)}) collective-permute-start(bf16[8,8192]{1,0:T(8,128)(2,1)S(1)} %collective-permute-done._), channel_id=1, source_target_pairs={{0,4},{1,3},{2,6},{3,1},{4,0},{5,7},{6,2},{7,5},{8,12},{9,11},{10,... | collective-permute-start | bytes 393224 | tf_op jit(solution)/shard_map/ppermute | solution.py:187
  11.4 0.7 %collective-permute-done.2 = bf16[8,8192]{1,0:T(8,128)(2,1)S(1)} collective-permute-done((bf16[8,8192]{1,0:T(8,128)(2,1)}, bf16[8,8192]{1,0:T(8,128)(2,1)S(1)}, u32[]{:S(2)}, u32[]{:S(2)}) %collective-permute-start.2) | collective-permute-done | bytes 131104 | tf_op jit(solution)/shard_map/ppermute | solution.py:187
  12.1 0.9 %collective-permute-start.4 = (bf16[16,8192]{1,0:T(8,128)(2,1)S(1)}, bf16[16,8192]{1,0:T(8,128)(2,1)S(1)}, u32[]{:S(2)}, u32[]{:S(2)}) collective-permute-start(bf16[16,8192]{1,0:T(8,128)(2,1)S(1)} %pad_maximum_fusion), channel_id=1, source_target_pairs={{0,2},{1,5},{2,0},{3,7},{4,6},{5,1},{6,4},{7,3},{8,10},{9,13},{10,... | collective-permute-start | bytes 786440 | tf_op jit(solution)/shard_map/ppermute | solution.py:187
  13.0 1.2 %collective-permute-start.5 = (bf16[8,8192]{1,0:T(8,128)(2,1)S(1)}, bf16[8,8192]{1,0:T(8,128)(2,1)S(1)}, u32[]{:S(2)}, u32[]{:S(2)}) collective-permute-start(bf16[8,8192]{1,0:T(8,128)(2,1)S(1)} %collective-permute-done._), channel_id=1, source_target_pairs={{0,6},{1,7},{2,4},{3,5},{4,2},{5,3},{6,0},{7,1},{8,14},{9,15},{10,... | collective-permute-start | bytes 393224 | tf_op jit(solution)/shard_map/ppermute | solution.py:187
  14.2 4.4 %shard_map.55 = (bf16[8192,224]{1,0:T(8,128)(2,1)S(1)}, bf16[8192,224]{1,0:T(8,128)(2,1)S(1)}, bf16[224,8192]{1,0:T(8,128)(2,1)S(1)}) custom-call(bf16[224,8192]{1,0:T(8,128)(2,1)} %bitcast.4, bf16[224,8192]{1,0:T(8,128)(2,1)} %bitcast.5, bf16[224,8192]{1,0:T(8,128)(2,1)} %down_hbm.1, bf16[8,8192]{1,0:T(8,128)(2,1)S(1)} %collective-permute-done._), custom_call_target="tpu_custom_call" | custom-call | bytes 11010048 | tf_op jit(solution)/shard_map/pallas_call | solution.py:45
  18.7 0.0 collective-permute-done.3
  18.7 0.0 collective-permute-done.1
  18.8 0.1 collective-permute-start.6
  18.9 1.8 %collective-permute-done.5 = bf16[8,8192]{1,0:T(8,128)(2,1)S(1)} collective-permute-done((bf16[8,8192]{1,0:T(8,128)(2,1)S(1)}, bf16[8,8192]{1,0:T(8,128)(2,1)S(1)}, u32[]{:S(2)}, u32[]{:S(2)}) %collective-permute-start.5) | collective-permute-done | bytes 131104 | tf_op jit(solution)/shard_map/ppermute | solution.py:187
  20.7 0.7 %collective-permute-done.4 = bf16[16,8192]{1,0:T(8,128)(2,1)S(1)} collective-permute-done((bf16[16,8192]{1,0:T(8,128)(2,1)S(1)}, bf16[16,8192]{1,0:T(8,128)(2,1)S(1)}, u32[]{:S(2)}, u32[]{:S(2)}) %collective-permute-start.4) | collective-permute-done | bytes 262176 | tf_op jit(solution)/shard_map/ppermute | solution.py:187
  21.4 0.1 collective-permute-start.8
  21.5 0.6 %collective-permute-start.7 = (bf16[32,4096]{1,0:T(8,128)(2,1)S(1)}, bf16[32,4096]{1,0:T(8,128)(2,1)S(1)}, u32[]{:S(2)}, u32[]{:S(2)}) collective-permute-start(bf16[32,4096]{1,0:T(8,128)(2,1)S(1)} %pad_maximum_fusion.1.refs_4_), channel_id=1, source_target_pairs={{0,1},{1,0},{2,3},{3,2},{4,5},{5,4},{6,7},{7,6},{8,9},{9,8},{10,11... | collective-permute-start | bytes 786440 | tf_op jit(solution)/shard_map/ppermute | solution.py:187
  22.1 0.9 %collective-permute-done.8.refs_5_ = bf16[32,4096]{1,0:T(8,128)(2,1)S(1)} collective-permute-done((bf16[32,4096]{1,0:T(8,128)(2,1)S(1)}, bf16[32,4096]{1,0:T(8,128)(2,1)S(1)}, u32[]{:S(2)}, u32[]{:S(2)}) %collective-permute-start.8) | collective-permute-done | bytes 262176 | tf_op jit(solution)/shard_map/ppermute | solution.py:187
  23.0 0.0 collective-permute-done.6.refs_3_
  23.0 0.7 %shard_map.56 = (f32[128,224]{1,0:T(8,128)S(1)}, f32[128,224]{1,0:T(8,128)S(1)}) custom-call(bf16[8192,224]{1,0:T(8,128)(2,1)S(1)} %get-tuple-element.30.refs_0_, bf16[8192,224]{1,0:T(8,128)(2,1)S(1)} %get-tuple-element.31.refs_1_, bf16[32,8192]{1,0:T(8,128)(2,1)S(1)} %constant_dynamic-update-slice_fusion.refs_2_, ...), custom_call_target="tpu_custom_call" | custom-call | flops 469762048 | bytes 3670016 | tf_op jit(solution)/shard_map/pallas_call | solution.py:85
  23.7 0.0 collective-permute-done.7.refs_5_
  23.7 0.7 %shard_map.57.hidden_ref = bf16[128,224]{1,0:T(8,128)(2,1)S(1)} custom-call(bf16[8192,224]{1,0:T(8,128)(2,1)S(1)} %get-tuple-element.30.refs_0_, bf16[8192,224]{1,0:T(8,128)(2,1)S(1)} %get-tuple-element.31.refs_1_, bf16[32,8192]{1,0:T(8,128)(2,1)S(1)} %constant_dynamic-update-slice_fusion.refs_2_, bf16[32,8192]{1,0:T(8,128)(2,1)S(1)} %collective-permute-done.6.refs_3_, ...), custom_call_target="tpu_custom_call" | custom-call | flops 469762048 | bytes 3670016 | tf_op jit(solution)/shard_map/pallas_call | solution.py:85
  24.5 0.7 %shard_map.58 = (f32[32,8192]{1,0:T(8,128)S(1)}, f32[8,8192]{1,0:T(8,128)S(1)}, f32[24,8192]{1,0:T(8,128)S(1)}, bf16[32,8192]{1,0:T(8,128)(2,1)S(1)}, bf16[8,819...) custom-call(bf16[128,224]{1,0:T(8,128)(2,1)S(1)} %shard_map.57.hidden_ref, bf16[224,8192]{1,0:T(8,128)(2,1)S(1)} %get-tuple-element.38.down_ref), custom_call_target="tpu_custom_call" | custom-call | flops 469762048 | bytes 3670016 | tf_op jit(solution)/shard_map/pallas_call | solution.py:114
  25.2 0.2 collective-permute-start.12
  25.4 0.4 collective-permute-start.9
  25.8 0.8 %collective-permute-done.12 = bf16[8,8192]{1,0:T(8,128)(2,1)S(1)} collective-permute-done((bf16[8,8192]{1,0:T(8,128)(2,1)S(1)}, bf16[8,8192]{1,0:T(8,128)(2,1)S(1)}, u32[]{:S(2)}, u32[]{:S(2)}) %collective-permute-start.12) | collective-permute-done | bytes 131104 | tf_op jit(solution)/shard_map/ppermute | solution.py:187
  26.6 1.1 %collective-permute-start.13 = (bf16[8,8192]{1,0:T(8,128)(2,1)S(1)}, bf16[8,8192]{1,0:T(8,128)(2,1)S(1)}, u32[]{:S(2)}, u32[]{:S(2)}) collective-permute-start(bf16[8,8192]{1,0:T(8,128)(2,1)S(1)} %add_convert_fusion), channel_id=1, source_target_pairs={{0,6},{1,7},{2,4},{3,5},{4,2},{5,3},{6,0},{7,1},{8,14},{9,15},{10,... | collective-permute-start | bytes 393224 | tf_op jit(solution)/shard_map/ppermute | solution.py:187
  27.8 0.0 collective-permute-done.9
  27.8 0.1 collective-permute-start.10
  27.9 0.1 fusion.7
  28.0 0.0 copy-start
  28.0 1.2 %collective-permute-start.14 = (bf16[8,8192]{1,0:T(8,128)(2,1)S(1)}, bf16[8,8192]{1,0:T(8,128)(2,1)S(1)}, u32[]{:S(2)}, u32[]{:S(2)}) collective-permute-start(bf16[8,8192]{1,0:T(8,128)(2,1)S(1)} %get-tuple-element.49), channel_id=1, source_target_pairs={{0,4},{1,3},{2,6},{3,1},{4,0},{5,7},{6,2},{7,5},{8,12},{9,11},{10,... | collective-permute-start | bytes 393224 | tf_op jit(solution)/shard_map/ppermute | solution.py:187
  29.2 1.2 %collective-permute-start.15 = (bf16[8,8192]{1,0:T(8,128)(2,1)S(1)}, bf16[8,8192]{1,0:T(8,128)(2,1)S(1)}, u32[]{:S(2)}, u32[]{:S(2)}) collective-permute-start(bf16[8,8192]{1,0:T(8,128)(2,1)S(1)} %get-tuple-element.50), channel_id=1, source_target_pairs={{0,2},{1,5},{2,0},{3,7},{4,6},{5,1},{6,4},{7,3},{8,10},{9,13},{10,... | collective-permute-start | bytes 393224 | tf_op jit(solution)/shard_map/ppermute | solution.py:187
  30.4 0.0 collective-permute-done.10
  30.4 0.1 convert_add_fusion
  30.5 0.6 %collective-permute-start.11 = (bf16[16,8192]{1,0:T(8,128)(2,1)S(1)}, bf16[16,8192]{1,0:T(8,128)(2,1)S(1)}, u32[]{:S(2)}, u32[]{:S(2)}) collective-permute-start(bf16[16,8192]{1,0:T(8,128)(2,1)S(1)} %slice.89), channel_id=1, source_target_pairs={{0,4},{1,3},{2,6},{3,1},{4,0},{5,7},{6,2},{7,5},{8,12},{9,11},{10,... | collective-permute-start | bytes 786440 | tf_op jit(solution)/shard_map/ppermute | solution.py:187
  31.1 2.8 %collective-permute-done.13 = bf16[8,8192]{1,0:T(8,128)(2,1)S(1)} collective-permute-done((bf16[8,8192]{1,0:T(8,128)(2,1)S(1)}, bf16[8,8192]{1,0:T(8,128)(2,1)S(1)}, u32[]{:S(2)}, u32[]{:S(2)}) %collective-permute-start.13) | collective-permute-done | bytes 131104 | tf_op jit(solution)/shard_map/ppermute | solution.py:187
  34.0 1.4 %collective-permute-done.14 = bf16[8,8192]{1,0:T(8,128)(2,1)S(1)} collective-permute-done((bf16[8,8192]{1,0:T(8,128)(2,1)S(1)}, bf16[8,8192]{1,0:T(8,128)(2,1)S(1)}, u32[]{:S(2)}, u32[]{:S(2)}) %collective-permute-start.14) | collective-permute-done | bytes 131104 | tf_op jit(solution)/shard_map/ppermute | solution.py:187
  35.3 0.8 %collective-permute-done.15 = bf16[8,8192]{1,0:T(8,128)(2,1)S(1)} collective-permute-done((bf16[8,8192]{1,0:T(8,128)(2,1)S(1)}, bf16[8,8192]{1,0:T(8,128)(2,1)S(1)}, u32[]{:S(2)}, u32[]{:S(2)}) %collective-permute-start.15) | collective-permute-done | bytes 131104 | tf_op jit(solution)/shard_map/ppermute | solution.py:187
  36.2 0.1 fusion.2
  36.2 2.8 %collective-permute-start.16 = (bf16[8,8192]{1,0:T(8,128)(2,1)S(1)}, bf16[8,8192]{1,0:T(8,128)(2,1)S(1)}, u32[]{:S(2)}, u32[]{:S(2)}) collective-permute-start(bf16[8,8192]{1,0:T(8,128)(2,1)S(1)} %fusion.2), channel_id=1, source_target_pairs={{0,8},{1,9},{2,10},{3,11},{4,12},{5,13},{6,14},{7,15},{8,0},{9,1},... | collective-permute-start | bytes 393224 | tf_op jit(solution)/shard_map/ppermute | solution.py:187
  39.0 0.0 collective-permute-done.11
  39.0 0.1 slice_add_fusion
  39.1 1.4 %collective-permute-start.17 = (bf16[8,8192]{1,0:T(8,128)(2,1)S(1)}, bf16[8,8192]{1,0:T(8,128)(2,1)S(1)}, u32[]{:S(2)}, u32[]{:S(2)}) collective-permute-start(bf16[8,8192]{1,0:T(8,128)(2,1)S(1)} %slice.90), channel_id=1, source_target_pairs={{0,2},{1,5},{2,0},{3,7},{4,6},{5,1},{6,4},{7,3},{8,10},{9,13},{10,... | collective-permute-start | bytes 393224 | tf_op jit(solution)/shard_map/ppermute | solution.py:187
  40.5 4.6 %collective-permute-done.16.refs_1_ = bf16[8,8192]{1,0:T(8,128)(2,1)S(1)} collective-permute-done((bf16[8,8192]{1,0:T(8,128)(2,1)S(1)}, bf16[8,8192]{1,0:T(8,128)(2,1)S(1)}, u32[]{:S(2)}, u32[]{:S(2)}) %collective-permute-start.16) | collective-permute-done | bytes 131104 | tf_op jit(solution)/shard_map/ppermute | solution.py:187
  45.2 0.0 collective-permute-done.17.refs_2_
  45.2 0.0 copy-done
  45.2 0.9 %shard_map.59 = bf16[8,8192]{1,0:T(8,128)(2,1)} custom-call(f32[8,8192]{1,0:T(8,128)S(1)} %slice.74.refs_0_, bf16[8,8192]{1,0:T(8,128)(2,1)S(1)} %collective-permute-done.16.refs_1_, bf16[8,8192]{1,0:T(8,128)(2,1)S(1)} %collective-permute-done.17.refs_2_, s32[1,8192]{1,0:T(1,128)S(1)} %bitcast.3, bf16[256,128]{1,0:T(8,128)(2,1)S(1)} %pad_maximum_fusion.3.refs_4_), custom_call_target="tpu_custom_call" | custom-call | tf_op jit(solution)/shard_map/pallas_call | solution.py:164
  (15 shorter events, 0.3 us)
Async XLA Ops:
  0.0 10.7 %collective-permute-start = (bf16[8,8192]{1,0:T(8,128)(2,1)}, bf16[8,8192]{1,0:T(8,128)(2,1)S(1)}, u32[]{:S(2)}, u32[]{:S(2)}) collective-permute-start(bf16[8,8192]{1,0:T(8,128)(2,1)} %param.5), channel_id=1, source_target_pairs={{0,8},{1,9},{2,10},{3,11},{4,12},{5,13},{6,14},{7,15},{8,0},{9,1},... | collective-permute-start | bytes 393224 | tf_op jit(solution)/shard_map/ppermute | solution.py:187
  4.0 8.0 %collective-permute-start.2 = (bf16[8,8192]{1,0:T(8,128)(2,1)}, bf16[8,8192]{1,0:T(8,128)(2,1)S(1)}, u32[]{:S(2)}, u32[]{:S(2)}) collective-permute-start(bf16[8,8192]{1,0:T(8,128)(2,1)} %param.5), channel_id=1, source_target_pairs={{0,4},{1,3},{2,6},{3,1},{4,0},{5,7},{6,2},{7,5},{8,12},{9,11},{10,... | collective-permute-start | bytes 393224 | tf_op jit(solution)/shard_map/ppermute | solution.py:187
  5.6 13.1 %collective-permute-start.3 = (bf16[8,8192]{1,0:T(8,128)(2,1)}, bf16[8,8192]{1,0:T(8,128)(2,1)S(1)}, u32[]{:S(2)}, u32[]{:S(2)}) collective-permute-start(bf16[8,8192]{1,0:T(8,128)(2,1)} %param.5), channel_id=1, source_target_pairs={{0,2},{1,5},{2,0},{3,7},{4,6},{5,1},{6,4},{7,3},{8,10},{9,13},{10,... | collective-permute-start | bytes 393224 | tf_op jit(solution)/shard_map/ppermute | solution.py:187
  10.7 8.0 %collective-permute-start.1 = (bf16[8,8192]{1,0:T(8,128)(2,1)S(1)}, bf16[8,8192]{1,0:T(8,128)(2,1)S(1)}, u32[]{:S(2)}, u32[]{:S(2)}) collective-permute-start(bf16[8,8192]{1,0:T(8,128)(2,1)S(1)} %collective-permute-done._), channel_id=1, source_target_pairs={{0,4},{1,3},{2,6},{3,1},{4,0},{5,7},{6,2},{7,5},{8,12},{9,11},{10,... | collective-permute-start | bytes 393224 | tf_op jit(solution)/shard_map/ppermute | solution.py:187
  12.1 9.2 %collective-permute-start.4 = (bf16[16,8192]{1,0:T(8,128)(2,1)S(1)}, bf16[16,8192]{1,0:T(8,128)(2,1)S(1)}, u32[]{:S(2)}, u32[]{:S(2)}) collective-permute-start(bf16[16,8192]{1,0:T(8,128)(2,1)S(1)} %pad_maximum_fusion), channel_id=1, source_target_pairs={{0,2},{1,5},{2,0},{3,7},{4,6},{5,1},{6,4},{7,3},{8,10},{9,13},{10,... | collective-permute-start | bytes 786440 | tf_op jit(solution)/shard_map/ppermute | solution.py:187
  13.0 7.7 %collective-permute-start.5 = (bf16[8,8192]{1,0:T(8,128)(2,1)S(1)}, bf16[8,8192]{1,0:T(8,128)(2,1)S(1)}, u32[]{:S(2)}, u32[]{:S(2)}) collective-permute-start(bf16[8,8192]{1,0:T(8,128)(2,1)S(1)} %collective-permute-done._), channel_id=1, source_target_pairs={{0,6},{1,7},{2,4},{3,5},{4,2},{5,3},{6,0},{7,1},{8,14},{9,15},{10,... | collective-permute-start | bytes 393224 | tf_op jit(solution)/shard_map/ppermute | solution.py:187
  18.8 4.2 %collective-permute-start.6 = (bf16[32,8192]{1,0:T(8,128)(2,1)S(1)}, bf16[32,8192]{1,0:T(8,128)(2,1)S(1)}, u32[]{:S(2)}, u32[]{:S(2)}) collective-permute-start(bf16[32,8192]{1,0:T(8,128)(2,1)S(1)} %constant_dynamic-update-slice_fusion.refs_2_), channel_id=1, source_target_pairs={{0,1},{1,0},{2,3},{3,2},{4,5},{5,4},{6,7},{7,6},{8,9},{9,8},{10,11... | collective-permute-start | bytes 1572872 | tf_op jit(solution)/shard_map/ppermute | solution.py:187
  21.4 1.6 %collective-permute-start.8 = (bf16[32,4096]{1,0:T(8,128)(2,1)S(1)}, bf16[32,4096]{1,0:T(8,128)(2,1)S(1)}, u32[]{:S(2)}, u32[]{:S(2)}) collective-permute-start(bf16[32,4096]{1,0:T(8,128)(2,1)S(1)} %pad_maximum_fusion.2.refs_4_), channel_id=1, source_target_pairs={{0,1},{1,0},{2,3},{3,2},{4,5},{5,4},{6,7},{7,6},{8,9},{9,8},{10,11... | collective-permute-start | bytes 786440 | tf_op jit(solution)/shard_map/ppermute | solution.py:187
  21.5 2.2 %collective-permute-start.7 = (bf16[32,4096]{1,0:T(8,128)(2,1)S(1)}, bf16[32,4096]{1,0:T(8,128)(2,1)S(1)}, u32[]{:S(2)}, u32[]{:S(2)}) collective-permute-start(bf16[32,4096]{1,0:T(8,128)(2,1)S(1)} %pad_maximum_fusion.1.refs_4_), channel_id=1, source_target_pairs={{0,1},{1,0},{2,3},{3,2},{4,5},{5,4},{6,7},{7,6},{8,9},{9,8},{10,11... | collective-permute-start | bytes 786440 | tf_op jit(solution)/shard_map/ppermute | solution.py:187
  25.2 1.4 %collective-permute-start.12 = (bf16[8,8192]{1,0:T(8,128)(2,1)S(1)}, bf16[8,8192]{1,0:T(8,128)(2,1)S(1)}, u32[]{:S(2)}, u32[]{:S(2)}) collective-permute-start(bf16[8,8192]{1,0:T(8,128)(2,1)S(1)} %get-tuple-element.46), channel_id=1, source_target_pairs={{0,1},{1,0},{2,3},{3,2},{4,5},{5,4},{6,7},{7,6},{8,9},{9,8},{10,11... | collective-permute-start | bytes 393224 | tf_op jit(solution)/shard_map/ppermute | solution.py:187
  25.4 2.4 %collective-permute-start.9 = (bf16[24,8192]{1,0:T(8,128)(2,1)S(1)}, bf16[24,8192]{1,0:T(8,128)(2,1)S(1)}, u32[]{:S(2)}, u32[]{:S(2)}) collective-permute-start(bf16[24,8192]{1,0:T(8,128)(2,1)S(1)} %get-tuple-element.40), channel_id=1, source_target_pairs={{0,1},{1,0},{2,3},{3,2},{4,5},{5,4},{6,7},{7,6},{8,9},{9,8},{10,11... | collective-permute-start | bytes 1179656 | tf_op jit(solution)/shard_map/ppermute | solution.py:187
  26.6 7.3 %collective-permute-start.13 = (bf16[8,8192]{1,0:T(8,128)(2,1)S(1)}, bf16[8,8192]{1,0:T(8,128)(2,1)S(1)}, u32[]{:S(2)}, u32[]{:S(2)}) collective-permute-start(bf16[8,8192]{1,0:T(8,128)(2,1)S(1)} %add_convert_fusion), channel_id=1, source_target_pairs={{0,6},{1,7},{2,4},{3,5},{4,2},{5,3},{6,0},{7,1},{8,14},{9,15},{10,... | collective-permute-start | bytes 393224 | tf_op jit(solution)/shard_map/ppermute | solution.py:187
  27.8 2.6 %collective-permute-start.10 = (bf16[32,8192]{1,0:T(8,128)(2,1)S(1)}, bf16[32,8192]{1,0:T(8,128)(2,1)S(1)}, u32[]{:S(2)}, u32[]{:S(2)}) collective-permute-start(bf16[32,8192]{1,0:T(8,128)(2,1)S(1)} %get-tuple-element.42), channel_id=1, source_target_pairs={{0,1},{1,0},{2,3},{3,2},{4,5},{5,4},{6,7},{7,6},{8,9},{9,8},{10,11... | collective-permute-start | bytes 1572872 | tf_op jit(solution)/shard_map/ppermute | solution.py:187
  28.0 17.2 %copy-start = (s32[8192]{0:T(1024)S(1)}, s32[8192]{0:T(1024)}, u32[]{:S(2)}) copy-start(s32[8192]{0:T(1024)} %param.9) | copy-start | bytes 98308
  28.0 7.4 %collective-permute-start.14 = (bf16[8,8192]{1,0:T(8,128)(2,1)S(1)}, bf16[8,8192]{1,0:T(8,128)(2,1)S(1)}, u32[]{:S(2)}, u32[]{:S(2)}) collective-permute-start(bf16[8,8192]{1,0:T(8,128)(2,1)S(1)} %get-tuple-element.49), channel_id=1, source_target_pairs={{0,4},{1,3},{2,6},{3,1},{4,0},{5,7},{6,2},{7,5},{8,12},{9,11},{10,... | collective-permute-start | bytes 393224 | tf_op jit(solution)/shard_map/ppermute | solution.py:187
  29.2 7.0 %collective-permute-start.15 = (bf16[8,8192]{1,0:T(8,128)(2,1)S(1)}, bf16[8,8192]{1,0:T(8,128)(2,1)S(1)}, u32[]{:S(2)}, u32[]{:S(2)}) collective-permute-start(bf16[8,8192]{1,0:T(8,128)(2,1)S(1)} %get-tuple-element.50), channel_id=1, source_target_pairs={{0,2},{1,5},{2,0},{3,7},{4,6},{5,1},{6,4},{7,3},{8,10},{9,13},{10,... | collective-permute-start | bytes 393224 | tf_op jit(solution)/shard_map/ppermute | solution.py:187
  30.5 8.5 %collective-permute-start.11 = (bf16[16,8192]{1,0:T(8,128)(2,1)S(1)}, bf16[16,8192]{1,0:T(8,128)(2,1)S(1)}, u32[]{:S(2)}, u32[]{:S(2)}) collective-permute-start(bf16[16,8192]{1,0:T(8,128)(2,1)S(1)} %slice.89), channel_id=1, source_target_pairs={{0,4},{1,3},{2,6},{3,1},{4,0},{5,7},{6,2},{7,5},{8,12},{9,11},{10,... | collective-permute-start | bytes 786440 | tf_op jit(solution)/shard_map/ppermute | solution.py:187
  36.2 8.9 %collective-permute-start.16 = (bf16[8,8192]{1,0:T(8,128)(2,1)S(1)}, bf16[8,8192]{1,0:T(8,128)(2,1)S(1)}, u32[]{:S(2)}, u32[]{:S(2)}) collective-permute-start(bf16[8,8192]{1,0:T(8,128)(2,1)S(1)} %fusion.2), channel_id=1, source_target_pairs={{0,8},{1,9},{2,10},{3,11},{4,12},{5,13},{6,14},{7,15},{8,0},{9,1},... | collective-permute-start | bytes 393224 | tf_op jit(solution)/shard_map/ppermute | solution.py:187
  39.1 6.1 %collective-permute-start.17 = (bf16[8,8192]{1,0:T(8,128)(2,1)S(1)}, bf16[8,8192]{1,0:T(8,128)(2,1)S(1)}, u32[]{:S(2)}, u32[]{:S(2)}) collective-permute-start(bf16[8,8192]{1,0:T(8,128)(2,1)S(1)} %slice.90), channel_id=1, source_target_pairs={{0,2},{1,5},{2,0},{3,7},{4,6},{5,1},{6,4},{7,3},{8,10},{9,13},{10,... | collective-permute-start | bytes 393224 | tf_op jit(solution)/shard_map/ppermute | solution.py:187

commit v12 on v11

--- a/solution.py
+++ b/solution.py
@@ -59,7 +59,7 @@
 
 def hidden_kernel(start, last, *refs):
     gate_ref, up_ref, near_here, near_there, far_here, far_there, *refs = refs
-    sums, outs = refs[: len(refs) - (1 if last else 2)], refs[-1 if last else -2 :]
+    sums, outs = refs[:-2], refs[-2:]
     width = far_here.shape[1]
     tile = math.gcd(width, 1024)
     gate, up = (ref[...] for ref in sums) if sums else (0.0, 0.0)
@@ -69,7 +69,9 @@
         gate = gate + jnp.dot(rows, gate_ref[there, :], preferred_element_type=jnp.float32)
         up = up + jnp.dot(rows, up_ref[there, :], preferred_element_type=jnp.float32)
     if last:
-        outs[0][...] = (gate / (1.0 + jnp.exp(-gate)) * up).astype(jnp.bfloat16)
+        hidden = (gate / (1.0 + jnp.exp(-gate)) * up).astype(jnp.bfloat16)
+        half = outs[0].shape[0]
+        outs[0][...], outs[1][...] = hidden[:half], hidden[half:]
     else:
         outs[0][...], outs[1][...] = gate, up
 
@@ -81,47 +83,47 @@
     for span in spans:
         width = span[0].shape[1]
         last = start + width == features
-        total = jax.ShapeDtypeStruct((count, units), jnp.float32)
+        out = ((count // 2, units), jnp.bfloat16) if last else ((count, units), jnp.float32)
         sums = pl.pallas_call(
             functools.partial(hidden_kernel, start, last),
-            out_shape=(jax.ShapeDtypeStruct((count, units), jnp.bfloat16),) if last else (total, total),
+            out_shape=(jax.ShapeDtypeStruct(*out),) * 2,
             in_specs=[vmem()] * (6 + len(sums)),
-            out_specs=(vmem(),) * (1 if last else 2),
+            out_specs=(vmem(),) * 2,
             cost_estimate=pl.CostEstimate(
                 flops=4 * units * count * width, bytes_accessed=4 * units * width, transcendentals=0
             ),
             compiler_params=pltpu.CompilerParams(vmem_limit_bytes=24 << 20),
         )(gate_w, up_w, *near, *span, *sums)
         start += width
-    return sums[0]
-
-
-def down_kernel(spans, hidden_ref, down_ref, *outs):
-    half, features = hidden_ref.shape[0] // 2, down_ref.shape[1]
+    return sums
+
+
+def down_kernel(count, hidden_ref, down_ref, *refs):
+    before, outs = refs[:count], refs[count:]
+    features = down_ref.shape[1]
     tile = math.gcd(features, 512)
     for first in range(0, features, tile):
         here = slice(first, first + tile)
         part = jnp.dot(hidden_ref[...], down_ref[:, here], preferred_element_type=jnp.float32)
+        row = 0
         for k, out in enumerate(outs):
-            begin = 0 if k < len(spans) else half
-            rows = [part[begin + first : begin + last] for first, last in spans[k % len(spans)]]
-            out[:, here] = jnp.concatenate(rows).astype(out.dtype)
-
-
-def down(hidden, down_w, spans):
+            rows = part[row : row + out.shape[0]]
+            row += out.shape[0]
+            out[:, here] = (before[k][:, here] + rows if before else rows).astype(out.dtype)
+
+
+def down(hidden, down_w, outs, before=()):
     units, features = down_w.shape
-    counts = [sum(last - first for first, last in span) for span in spans]
     return pl.pallas_call(
-        functools.partial(down_kernel, spans),
-        out_shape=[jax.ShapeDtypeStruct((count, features), jnp.float32) for count in counts]
-        + [jax.ShapeDtypeStruct((count, features), jnp.bfloat16) for count in counts],
-        in_specs=[vmem()] * 2,
-        out_specs=[vmem()] * (2 * len(counts)),
+        functools.partial(down_kernel, len(before)),
+        out_shape=[jax.ShapeDtypeStruct((count, features), kind) for count, kind in outs],
+        in_specs=[vmem()] * (2 + len(before)),
+        out_specs=[vmem()] * len(outs),
         cost_estimate=pl.CostEstimate(
             flops=2 * hidden.size * features, bytes_accessed=2 * units * features, transcendentals=0
         ),
         compiler_params=pltpu.CompilerParams(vmem_limit_bytes=24 << 20),
-    )(hidden, down_w)
+    )(hidden, down_w, *before)
 
 
 def signs_twice():
@@ -193,37 +195,33 @@
         for masks in far:
             away.append(swap(jnp.concatenate([tokens] + away), masks))
         away = jnp.concatenate(away)
-        near = [swap(tokens, m) for m in square[:2]]
+        near = [swap(tokens, m) for m in square]
+        there = [None] * 3
+        for k, arrived in ((1, None), (2, 1), (0, 0)):
+            if arrived is not None:
+                away, near[arrived] = lax.optimization_barrier((away, near[arrived]))
+            there[k] = swap(away, square[k])
+        down_there = swap(down_weight, (1, 1))
         gate_w, up_w, down_w = load(gate_weight.T, up_weight.T, down_weight, away)
-        first = swap(away, square[0])
-        both = swap(jnp.concatenate([away, near[0]]), square[1])
-        diagonal = swap(away, square[2])
-        first, *near = lax.optimization_barrier((first, *near))
-        early = jnp.concatenate([tokens, near[1], near[0], away])
-        early_there = swap(early, (1, 1))
-        gate_w, up_w, early, both, diagonal = lax.optimization_barrier((gate_w, up_w, early, both, diagonal))
-        count = others * rows
-        late = [both[count:], diagonal, first, both[:count]]
+        there[1], *near = lax.optimization_barrier((there[1], *near))
+        near = jnp.concatenate([tokens, near[1], near[0], near[2]])
+        near_there = swap(near, (1, 1))
+        gate_w, up_w, near, there[0], there[2] = lax.optimization_barrier((gate_w, up_w, near, there[0], there[2]))
+        far_rows = [there[2], away, *there[:2]]
         spans = []
         width = features // SPANS
         for k in range(SPANS):
-            span = jnp.concatenate([piece[:, k * width : (k + 1) * width] for piece in late])
+            span = jnp.concatenate([piece[:, k * width : (k + 1) * width] for piece in far_rows])
             spans.append((span, swap(span, (1, 1))))
-        hidden = hidden_units(gate_w, up_w, (early, early_there), spans)
-
-        a, b = 3 * rows, 3 * rows + count
-        own_rows = ((0, a), (b, b + rows))
-        rest_rows = ((a, b), (b + rows + count, b + rows + 3 * count))
-        own, diagonal, rest, *sends = down(
-            hidden, down_w, (own_rows, ((b + rows, b + rows + count),), rest_rows)
-        )
-        diagonal = diagonal + swap(sends[1], (1, 1)).astype(jnp.float32)
-        diagonal = swap(diagonal.astype(jnp.bfloat16), square[2])
-        rest_there, sends[0] = lax.optimization_barrier((swap(sends[2], (1, 1)), sends[0]))
-        rest = rest + rest_there.astype(jnp.float32)
-        leave = rest[count:].astype(jnp.bfloat16)
-        total = rest[:count]
-        for piece in (diagonal, swap(leave[:count], square[0]), swap(leave[count:], square[1])):
+        mine, theirs = hidden_units(gate_w, up_w, (near, near_there), spans)
+
+        count = others * rows
+        wide, narrow = jnp.float32, jnp.bfloat16
+        counts = (4 * rows, count, count, count, count)
+        sums = down(mine, down_w, [(n, wide) for n in counts])
+        kinds = (wide, narrow, wide, narrow, narrow)
+        own, diagonal, total, *leave = down(swap(theirs, (1, 1)), down_there, list(zip(counts, kinds)), sums)
+        for piece in (swap(diagonal, square[2]), swap(leave[0], square[0]), swap(leave[1], square[1])):
             total = total + piece.astype(jnp.float32)
         arrived = []
         for masks in reversed(far):
@@ -232,7 +230,6 @@
             arrived.append(piece[:rows])
             total = total[:split] + piece[rows:].astype(jnp.float32)
 
-        own = own + swap(sends[0], (1, 1)).astype(jnp.float32)
         own = own[: 2 * rows] + swap(own[2 * rows :].astype(jnp.bfloat16), square[0]).astype(jnp.float32)
         arrived.append(swap(own[rows:].astype(jnp.bfloat16), square[1]))
         return rotate(own[:rows], arrived, sign_pattern)

time: 46.2 us -> 45.9 us (level)
  waiting for transfers between devices: 17.2 us -> 16 us
  Pallas kernels: 7.48 us -> 8.34 us
    ppermute x18, waiting for transfers between devices: 17.2 us -> 16 us  [swap(): lax.ppermute(value, 'gx', [(i, i ^ masks[i % 2]) for i in range(members)])]
    pallas_call x1 -> x2, Pallas kernels: 0.71 us -> 1.57 us  [down(): pl.pallas_call(functools.partial(down_kernel, len(before)), out_shape=[ja...]
  transfers between devices with their start and end apart: 18 -> 18, of which waited for: 10 -> 11; matrix products, arithmetic and copies ran while one was open for 3% -> 3% of each run, Pallas kernels for 11% -> 15%
where the time goes in v12:
time: 45.9 us; the launch traced here: 45.8 us
  starting transfers between devices  19.9 us (43%)
  waiting for transfers between devices  16 us (35%)
  Pallas kernels  8.34 us (18%)
  local copies, waits for them, and re-layouts  1.08 us (2%)
    ppermute x18, starting transfers between devices, swap(): lax.ppermute(value, 'gx', [(i, i ^ masks[i % 2]) for i in range(members)])  19.9 us
    ppermute x18, waiting for transfers between devices, swap(): lax.ppermute(value, 'gx', [(i, i ^ masks[i % 2]) for i in range(members)])  16 us
    pallas_call x1, Pallas kernels, load(): pl.pallas_call(load_kernel, out_shape=(shape, shape, jax.ShapeDtypeStruct...  4.44 us
    pallas_call x2, Pallas kernels, down(): pl.pallas_call(functools.partial(down_kernel, len(before)), out_shape=[ja...  1.57 us
    pallas_call x2, Pallas kernels, hidden_units(): pl.pallas_call(functools.partial(hidden_kernel, start, last), out_shape=(...  1.45 us
    unnamed x5, local copies, waits for them, and re-layouts  0.97 us
  transfers between devices with their start and end apart: 18, of which 11 were waited for; matrix products, arithmetic and copies ran while one was open for 3% of the time, Pallas kernels for 15%

profile of v12, /device:TPU:0, one launch (start us, length us, event | category | flops | bytes accessed | tf_op | source)
XLA Modules:
  0.0 45.8 jit_solution(12970625914519023833)
XLA Ops:
  0.0 4.0 %collective-permute-start = (bf16[8,8192]{1,0:T(8,128)(2,1)}, bf16[8,8192]{1,0:T(8,128)(2,1)S(1)}, u32[]{:S(2)}, u32[]{:S(2)}) collective-permute-start(bf16[8,8192]{1,0:T(8,128)(2,1)} %param.5), channel_id=1, source_target_pairs={{0,8},{1,9},{2,10},{3,11},{4,12},{5,13},{6,14},{7,15},{8,0},{9,1},... | collective-permute-start | bytes 393224 | tf_op jit(solution)/shard_map/ppermute | solution.py:189
  4.0 1.5 %collective-permute-start.1 = (bf16[8,8192]{1,0:T(8,128)(2,1)}, bf16[8,8192]{1,0:T(8,128)(2,1)S(1)}, u32[]{:S(2)}, u32[]{:S(2)}) collective-permute-start(bf16[8,8192]{1,0:T(8,128)(2,1)} %param.5), channel_id=1, source_target_pairs={{0,2},{1,5},{2,0},{3,7},{4,6},{5,1},{6,4},{7,3},{8,10},{9,13},{10,... | collective-permute-start | bytes 393224 | tf_op jit(solution)/shard_map/ppermute | solution.py:189
  5.6 1.6 %collective-permute-start.2 = (bf16[8,8192]{1,0:T(8,128)(2,1)}, bf16[8,8192]{1,0:T(8,128)(2,1)S(1)}, u32[]{:S(2)}, u32[]{:S(2)}) collective-permute-start(bf16[8,8192]{1,0:T(8,128)(2,1)} %param.5), channel_id=1, source_target_pairs={{0,4},{1,3},{2,6},{3,1},{4,0},{5,7},{6,2},{7,5},{8,12},{9,11},{10,... | collective-permute-start | bytes 393224 | tf_op jit(solution)/shard_map/ppermute | solution.py:189
  7.1 0.4 collective-permute-start.4
  7.5 0.0 collective-permute-start.11
  7.5 0.9 %constant_dynamic-update-slice_fusion.3 = bf16[32,8192]{1,0:T(8,128)(2,1)S(1)} fusion(bf16[8,8192]{1,0:T(8,128)(2,1)} %param.5), kind=kLoop, calls=%fused_computation.17 | loop fusion | bytes 262144
  8.5 2.2 %collective-permute-done._ = bf16[8,8192]{1,0:T(8,128)(2,1)S(1)} collective-permute-done((bf16[8,8192]{1,0:T(8,128)(2,1)}, bf16[8,8192]{1,0:T(8,128)(2,1)S(1)}, u32[]{:S(2)}, u32[]{:S(2)}) %collective-permute-start) | collective-permute-done | bytes 131104 | tf_op jit(solution)/shard_map/ppermute | solution.py:189
  10.6 0.1 collective-permute-done.1
  10.7 1.7 %collective-permute-start.6 = (bf16[8,8192]{1,0:T(8,128)(2,1)S(1)}, bf16[8,8192]{1,0:T(8,128)(2,1)S(1)}, u32[]{:S(2)}, u32[]{:S(2)}) collective-permute-start(bf16[8,8192]{1,0:T(8,128)(2,1)S(1)} %collective-permute-done._), channel_id=1, source_target_pairs={{0,6},{1,7},{2,4},{3,5},{4,2},{5,3},{6,0},{7,1},{8,14},{9,15},{10,... | collective-permute-start | bytes 393224 | tf_op jit(solution)/shard_map/ppermute | solution.py:189
  12.4 0.5 %collective-permute-done.2 = bf16[8,8192]{1,0:T(8,128)(2,1)S(1)} collective-permute-done((bf16[8,8192]{1,0:T(8,128)(2,1)}, bf16[8,8192]{1,0:T(8,128)(2,1)S(1)}, u32[]{:S(2)}, u32[]{:S(2)}) %collective-permute-start.2) | collective-permute-done | bytes 131104 | tf_op jit(solution)/shard_map/ppermute | solution.py:189
  12.9 1.4 %collective-permute-start.5 = (bf16[8,8192]{1,0:T(8,128)(2,1)S(1)}, bf16[8,8192]{1,0:T(8,128)(2,1)S(1)}, u32[]{:S(2)}, u32[]{:S(2)}) collective-permute-start(bf16[8,8192]{1,0:T(8,128)(2,1)S(1)} %collective-permute-done._), channel_id=1, source_target_pairs={{0,4},{1,3},{2,6},{3,1},{4,0},{5,7},{6,2},{7,5},{8,12},{9,11},{10,... | collective-permute-start | bytes 393224 | tf_op jit(solution)/shard_map/ppermute | solution.py:189
  14.3 0.7 %collective-permute-start.3 = (bf16[8,8192]{1,0:T(8,128)(2,1)S(1)}, bf16[8,8192]{1,0:T(8,128)(2,1)S(1)}, u32[]{:S(2)}, u32[]{:S(2)}) collective-permute-start(bf16[8,8192]{1,0:T(8,128)(2,1)S(1)} %collective-permute-done._), channel_id=1, source_target_pairs={{0,2},{1,5},{2,0},{3,7},{4,6},{5,1},{6,4},{7,3},{8,10},{9,13},{10,... | collective-permute-start | bytes 393224 | tf_op jit(solution)/shard_map/ppermute | solution.py:189
  15.0 4.4 %shard_map.55 = (bf16[8192,224]{1,0:T(8,128)(2,1)S(1)}, bf16[8192,224]{1,0:T(8,128)(2,1)S(1)}, bf16[224,8192]{1,0:T(8,128)(2,1)S(1)}) custom-call(bf16[224,8192]{1,0:T(8,128)(2,1)} %bitcast.4, bf16[224,8192]{1,0:T(8,128)(2,1)} %bitcast.5, bf16[224,8192]{1,0:T(8,128)(2,1)} %down_hbm.1, bf16[8,8192]{1,0:T(8,128)(2,1)S(1)} %collective-permute-done._), custom_call_target="tpu_custom_call" | custom-call | bytes 11010048 | tf_op jit(solution)/shard_map/pallas_call | solution.py:45
  19.4 0.0 collective-permute-done.4
  19.4 1.1 %collective-permute-done.3 = bf16[8,8192]{1,0:T(8,128)(2,1)S(1)} collective-permute-done((bf16[8,8192]{1,0:T(8,128)(2,1)S(1)}, bf16[8,8192]{1,0:T(8,128)(2,1)S(1)}, u32[]{:S(2)}, u32[]{:S(2)}) %collective-permute-start.3) | collective-permute-done | bytes 131104 | tf_op jit(solution)/shard_map/ppermute | solution.py:189
  20.6 0.1 collective-permute-start.7
  20.7 0.0 collective-permute-done.5
  20.7 0.0 collective-permute-done.6
  20.8 0.5 %collective-permute-start.9 = (bf16[32,4096]{1,0:T(8,128)(2,1)S(1)}, bf16[32,4096]{1,0:T(8,128)(2,1)S(1)}, u32[]{:S(2)}, u32[]{:S(2)}) collective-permute-start(bf16[32,4096]{1,0:T(8,128)(2,1)S(1)} %pad_maximum_fusion.1.refs_4_), channel_id=1, source_target_pairs={{0,1},{1,0},{2,3},{3,2},{4,5},{5,4},{6,7},{7,6},{8,9},{9,8},{10,11... | collective-permute-start | bytes 786440 | tf_op jit(solution)/shard_map/ppermute | solution.py:189
  21.4 0.1 collective-permute-start.8
  21.5 1.5 %collective-permute-done.9.refs_5_ = bf16[32,4096]{1,0:T(8,128)(2,1)S(1)} collective-permute-done((bf16[32,4096]{1,0:T(8,128)(2,1)S(1)}, bf16[32,4096]{1,0:T(8,128)(2,1)S(1)}, u32[]{:S(2)}, u32[]{:S(2)}) %collective-permute-start.9) | collective-permute-done | bytes 262176 | tf_op jit(solution)/shard_map/ppermute | solution.py:189
  23.0 0.0 collective-permute-done.7.refs_3_
  23.0 0.7 %shard_map.56 = (f32[128,224]{1,0:T(8,128)S(1)}, f32[128,224]{1,0:T(8,128)S(1)}) custom-call(bf16[8192,224]{1,0:T(8,128)(2,1)S(1)} %get-tuple-element.44.refs_0_, bf16[8192,224]{1,0:T(8,128)(2,1)S(1)} %get-tuple-element.45.refs_1_, bf16[32,8192]{1,0:T(8,128)(2,1)S(1)} %constant_dynamic-update-slice_fusion.refs_2_, ...), custom_call_target="tpu_custom_call" | custom-call | flops 469762048 | bytes 3670016 | tf_op jit(solution)/shard_map/pallas_call | solution.py:87
  23.7 0.0 collective-permute-done.8.refs_5_
  23.7 0.7 %shard_map.57 = (bf16[64,224]{1,0:T(8,128)(2,1)S(1)}, bf16[64,224]{1,0:T(8,128)(2,1)S(1)}) custom-call(bf16[8192,224]{1,0:T(8,128)(2,1)S(1)} %get-tuple-element.44.refs_0_, bf16[8192,224]{1,0:T(8,128)(2,1)S(1)} %get-tuple-element.45.refs_1_, bf16[32,8192]{1,0:T(8,128)(2,1)S(1)} %constant_dynamic-update-slice_fusion.refs_2_, ...), custom_call_target="tpu_custom_call" | custom-call | flops 469762048 | bytes 3670016 | tf_op jit(solution)/shard_map/pallas_call | solution.py:87
  24.4 0.2 collective-permute-start.10
  24.7 0.8 %shard_map.58 = (f32[32,8192]{1,0:T(8,128)S(1)}, f32[8,8192]{1,0:T(8,128)S(1)}, f32[8,8192]{1,0:T(8,128)S(1)}, f32[8,8192]{1,0:T(8,128)S(1)}, f32[8,8192]{1,0:T(8,128)S(1)}) custom-call(bf16[64,224]{1,0:T(8,128)(2,1)S(1)} %get-tuple-element.53.hidden_ref, bf16[224,8192]{1,0:T(8,128)(2,1)S(1)} %get-tuple-element.54.down_ref), custom_call_target="tpu_custom_call" | custom-call | flops 234881024 | bytes 3670016 | tf_op jit(solution)/shard_map/pallas_call | solution.py:117
  25.4 0.3 collective-permute-done.10.hidden_ref
  25.7 0.0 collective-permute-done.11.down_ref
  25.7 0.0 copy-start
  25.7 0.8 %shard_map.59 = (f32[32,8192]{1,0:T(8,128)S(1)}, bf16[8,8192]{1,0:T(8,128)(2,1)S(1)}, f32[8,8192]{1,0:T(8,128)S(1)}, bf16[8,8192]{1,0:T(8,128)(2,1)S(1)}, bf16[8,8192]{1,0:T(8,128)(2,1)S(1)}) custom-call(bf16[64,224]{1,0:T(8,128)(2,1)S(1)} %collective-permute-done.10.hidden_ref, bf16[224,8192]{1,0:T(8,128)(2,1)S(1)} %collective-permute-done.11.down_ref, ...), custom_call_target="tpu_custom_call" | custom-call | flops 234881024 | bytes 3670016 | tf_op jit(solution)/shard_map/pallas_call | solution.py:117
  26.5 1.1 %collective-permute-start.13 = (bf16[8,8192]{1,0:T(8,128)(2,1)S(1)}, bf16[8,8192]{1,0:T(8,128)(2,1)S(1)}, u32[]{:S(2)}, u32[]{:S(2)}) collective-permute-start(bf16[8,8192]{1,0:T(8,128)(2,1)S(1)} %get-tuple-element.62), channel_id=1, source_target_pairs={{0,6},{1,7},{2,4},{3,5},{4,2},{5,3},{6,0},{7,1},{8,14},{9,15},{10,... | collective-permute-start | bytes 393224 | tf_op jit(solution)/shard_map/ppermute | solution.py:189
  27.6 1.1 %collective-permute-start.14 = (bf16[8,8192]{1,0:T(8,128)(2,1)S(1)}, bf16[8,8192]{1,0:T(8,128)(2,1)S(1)}, u32[]{:S(2)}, u32[]{:S(2)}) collective-permute-start(bf16[8,8192]{1,0:T(8,128)(2,1)S(1)} %get-tuple-element.63), channel_id=1, source_target_pairs={{0,4},{1,3},{2,6},{3,1},{4,0},{5,7},{6,2},{7,5},{8,12},{9,11},{10,... | collective-permute-start | bytes 393224 | tf_op jit(solution)/shard_map/ppermute | solution.py:189
  28.8 1.3 %collective-permute-start.15 = (bf16[8,8192]{1,0:T(8,128)(2,1)S(1)}, bf16[8,8192]{1,0:T(8,128)(2,1)S(1)}, u32[]{:S(2)}, u32[]{:S(2)}) collective-permute-start(bf16[8,8192]{1,0:T(8,128)(2,1)S(1)} %get-tuple-element.64), channel_id=1, source_target_pairs={{0,2},{1,5},{2,0},{3,7},{4,6},{5,1},{6,4},{7,3},{8,10},{9,13},{10,... | collective-permute-start | bytes 393224 | tf_op jit(solution)/shard_map/ppermute | solution.py:189
  30.1 1.2 %collective-permute-start.12 = (bf16[16,8192]{1,0:T(8,128)(2,1)S(1)}, bf16[16,8192]{1,0:T(8,128)(2,1)S(1)}, u32[]{:S(2)}, u32[]{:S(2)}) collective-permute-start(bf16[16,8192]{1,0:T(8,128)(2,1)S(1)} %slice.56), channel_id=1, source_target_pairs={{0,4},{1,3},{2,6},{3,1},{4,0},{5,7},{6,2},{7,5},{8,12},{9,11},{10,... | collective-permute-start | bytes 786440 | tf_op jit(solution)/shard_map/ppermute | solution.py:189
  31.3 2.6 %collective-permute-done.13 = bf16[8,8192]{1,0:T(8,128)(2,1)S(1)} collective-permute-done((bf16[8,8192]{1,0:T(8,128)(2,1)S(1)}, bf16[8,8192]{1,0:T(8,128)(2,1)S(1)}, u32[]{:S(2)}, u32[]{:S(2)}) %collective-permute-start.13) | collective-permute-done | bytes 131104 | tf_op jit(solution)/shard_map/ppermute | solution.py:189
  33.9 1.3 %collective-permute-done.14 = bf16[8,8192]{1,0:T(8,128)(2,1)S(1)} collective-permute-done((bf16[8,8192]{1,0:T(8,128)(2,1)S(1)}, bf16[8,8192]{1,0:T(8,128)(2,1)S(1)}, u32[]{:S(2)}, u32[]{:S(2)}) %collective-permute-start.14) | collective-permute-done | bytes 131104 | tf_op jit(solution)/shard_map/ppermute | solution.py:189
  35.1 0.8 %collective-permute-done.15 = bf16[8,8192]{1,0:T(8,128)(2,1)S(1)} collective-permute-done((bf16[8,8192]{1,0:T(8,128)(2,1)S(1)}, bf16[8,8192]{1,0:T(8,128)(2,1)S(1)}, u32[]{:S(2)}, u32[]{:S(2)}) %collective-permute-start.15) | collective-permute-done | bytes 131104 | tf_op jit(solution)/shard_map/ppermute | solution.py:189
  35.9 0.1 add_convert_fusion
  36.0 1.6 %collective-permute-start.16 = (bf16[8,8192]{1,0:T(8,128)(2,1)S(1)}, bf16[8,8192]{1,0:T(8,128)(2,1)S(1)}, u32[]{:S(2)}, u32[]{:S(2)}) collective-permute-start(bf16[8,8192]{1,0:T(8,128)(2,1)S(1)} %add_convert_fusion), channel_id=1, source_target_pairs={{0,8},{1,9},{2,10},{3,11},{4,12},{5,13},{6,14},{7,15},{8,0},{9,1},... | collective-permute-start | bytes 393224 | tf_op jit(solution)/shard_map/ppermute | solution.py:189
  37.6 0.3 collective-permute-done.12
  38.0 1.4 %collective-permute-start.17 = (bf16[8,8192]{1,0:T(8,128)(2,1)S(1)}, bf16[8,8192]{1,0:T(8,128)(2,1)S(1)}, u32[]{:S(2)}, u32[]{:S(2)}) collective-permute-start(bf16[8,8192]{1,0:T(8,128)(2,1)S(1)} %slice.57), channel_id=1, source_target_pairs={{0,2},{1,5},{2,0},{3,7},{4,6},{5,1},{6,4},{7,3},{8,10},{9,13},{10,... | collective-permute-start | bytes 393224 | tf_op jit(solution)/shard_map/ppermute | solution.py:189
  39.5 5.4 %collective-permute-done.16.refs_1_ = bf16[8,8192]{1,0:T(8,128)(2,1)S(1)} collective-permute-done((bf16[8,8192]{1,0:T(8,128)(2,1)S(1)}, bf16[8,8192]{1,0:T(8,128)(2,1)S(1)}, u32[]{:S(2)}, u32[]{:S(2)}) %collective-permute-start.16) | collective-permute-done | bytes 131104 | tf_op jit(solution)/shard_map/ppermute | solution.py:189
  44.9 0.0 collective-permute-done.17.refs_2_
  44.9 0.0 copy-done
  44.9 0.9 %shard_map.60 = bf16[8,8192]{1,0:T(8,128)(2,1)} custom-call(f32[8,8192]{1,0:T(8,128)S(1)} %slice.51.refs_0_, bf16[8,8192]{1,0:T(8,128)(2,1)S(1)} %collective-permute-done.16.refs_1_, bf16[8,8192]{1,0:T(8,128)(2,1)S(1)} %collective-permute-done.17.refs_2_, s32[1,8192]{1,0:T(1,128)S(1)} %bitcast.3, bf16[256,128]{1,0:T(8,128)(2,1)S(1)} %pad_maximum_fusion.2.refs_4_), custom_call_target="tpu_custom_call" | custom-call | tf_op jit(solution)/shard_map/pallas_call | solution.py:166
  (14 shorter events, 0.3 us)
Async XLA Ops:
  0.0 10.6 %collective-permute-start = (bf16[8,8192]{1,0:T(8,128)(2,1)}, bf16[8,8192]{1,0:T(8,128)(2,1)S(1)}, u32[]{:S(2)}, u32[]{:S(2)}) collective-permute-start(bf16[8,8192]{1,0:T(8,128)(2,1)} %param.5), channel_id=1, source_target_pairs={{0,8},{1,9},{2,10},{3,11},{4,12},{5,13},{6,14},{7,15},{8,0},{9,1},... | collective-permute-start | bytes 393224 | tf_op jit(solution)/shard_map/ppermute | solution.py:189
  4.0 6.7 %collective-permute-start.1 = (bf16[8,8192]{1,0:T(8,128)(2,1)}, bf16[8,8192]{1,0:T(8,128)(2,1)S(1)}, u32[]{:S(2)}, u32[]{:S(2)}) collective-permute-start(bf16[8,8192]{1,0:T(8,128)(2,1)} %param.5), channel_id=1, source_target_pairs={{0,2},{1,5},{2,0},{3,7},{4,6},{5,1},{6,4},{7,3},{8,10},{9,13},{10,... | collective-permute-start | bytes 393224 | tf_op jit(solution)/shard_map/ppermute | solution.py:189
  5.6 7.4 %collective-permute-start.2 = (bf16[8,8192]{1,0:T(8,128)(2,1)}, bf16[8,8192]{1,0:T(8,128)(2,1)S(1)}, u32[]{:S(2)}, u32[]{:S(2)}) collective-permute-start(bf16[8,8192]{1,0:T(8,128)(2,1)} %param.5), channel_id=1, source_target_pairs={{0,4},{1,3},{2,6},{3,1},{4,0},{5,7},{6,2},{7,5},{8,12},{9,11},{10,... | collective-permute-start | bytes 393224 | tf_op jit(solution)/shard_map/ppermute | solution.py:189
  7.1 12.3 %collective-permute-start.4 = (bf16[8,8192]{1,0:T(8,128)(2,1)}, bf16[8,8192]{1,0:T(8,128)(2,1)S(1)}, u32[]{:S(2)}, u32[]{:S(2)}) collective-permute-start(bf16[8,8192]{1,0:T(8,128)(2,1)} %param.5), channel_id=1, source_target_pairs={{0,6},{1,7},{2,4},{3,5},{4,2},{5,3},{6,0},{7,1},{8,14},{9,15},{10,... | collective-permute-start | bytes 393224 | tf_op jit(solution)/shard_map/ppermute | solution.py:189
  7.5 18.2 %collective-permute-start.11 = (bf16[224,8192]{1,0:T(8,128)(2,1)}, bf16[224,8192]{1,0:T(8,128)(2,1)S(1)}, u32[]{:S(2)}, u32[]{:S(2)}) collective-permute-start(bf16[224,8192]{1,0:T(8,128)(2,1)} %down_hbm.1), channel_id=1, source_target_pairs={{0,1},{1,0},{2,3},{3,2},{4,5},{5,4},{6,7},{7,6},{8,9},{9,8},{10,11... | collective-permute-start | bytes 11010056 | tf_op jit(solution)/shard_map/ppermute | solution.py:189
  10.7 10.0 %collective-permute-start.6 = (bf16[8,8192]{1,0:T(8,128)(2,1)S(1)}, bf16[8,8192]{1,0:T(8,128)(2,1)S(1)}, u32[]{:S(2)}, u32[]{:S(2)}) collective-permute-start(bf16[8,8192]{1,0:T(8,128)(2,1)S(1)} %collective-permute-done._), channel_id=1, source_target_pairs={{0,6},{1,7},{2,4},{3,5},{4,2},{5,3},{6,0},{7,1},{8,14},{9,15},{10,... | collective-permute-start | bytes 393224 | tf_op jit(solution)/shard_map/ppermute | solution.py:189
  12.9 7.8 %collective-permute-start.5 = (bf16[8,8192]{1,0:T(8,128)(2,1)S(1)}, bf16[8,8192]{1,0:T(8,128)(2,1)S(1)}, u32[]{:S(2)}, u32[]{:S(2)}) collective-permute-start(bf16[8,8192]{1,0:T(8,128)(2,1)S(1)} %collective-permute-done._), channel_id=1, source_target_pairs={{0,4},{1,3},{2,6},{3,1},{4,0},{5,7},{6,2},{7,5},{8,12},{9,11},{10,... | collective-permute-start | bytes 393224 | tf_op jit(solution)/shard_map/ppermute | solution.py:189
  14.3 6.3 %collective-permute-start.3 = (bf16[8,8192]{1,0:T(8,128)(2,1)S(1)}, bf16[8,8192]{1,0:T(8,128)(2,1)S(1)}, u32[]{:S(2)}, u32[]{:S(2)}) collective-permute-start(bf16[8,8192]{1,0:T(8,128)(2,1)S(1)} %collective-permute-done._), channel_id=1, source_target_pairs={{0,2},{1,5},{2,0},{3,7},{4,6},{5,1},{6,4},{7,3},{8,10},{9,13},{10,... | collective-permute-start | bytes 393224 | tf_op jit(solution)/shard_map/ppermute | solution.py:189
  20.6 2.4 %collective-permute-start.7 = (bf16[32,8192]{1,0:T(8,128)(2,1)S(1)}, bf16[32,8192]{1,0:T(8,128)(2,1)S(1)}, u32[]{:S(2)}, u32[]{:S(2)}) collective-permute-start(bf16[32,8192]{1,0:T(8,128)(2,1)S(1)} %constant_dynamic-update-slice_fusion.refs_2_), channel_id=1, source_target_pairs={{0,1},{1,0},{2,3},{3,2},{4,5},{5,4},{6,7},{7,6},{8,9},{9,8},{10,11... | collective-permute-start | bytes 1572872 | tf_op jit(solution)/shard_map/ppermute | solution.py:189
  20.8 2.2 %collective-permute-start.9 = (bf16[32,4096]{1,0:T(8,128)(2,1)S(1)}, bf16[32,4096]{1,0:T(8,128)(2,1)S(1)}, u32[]{:S(2)}, u32[]{:S(2)}) collective-permute-start(bf16[32,4096]{1,0:T(8,128)(2,1)S(1)} %pad_maximum_fusion.1.refs_4_), channel_id=1, source_target_pairs={{0,1},{1,0},{2,3},{3,2},{4,5},{5,4},{6,7},{7,6},{8,9},{9,8},{10,11... | collective-permute-start | bytes 786440 | tf_op jit(solution)/shard_map/ppermute | solution.py:189
  21.4 2.3 %collective-permute-start.8 = (bf16[32,4096]{1,0:T(8,128)(2,1)S(1)}, bf16[32,4096]{1,0:T(8,128)(2,1)S(1)}, u32[]{:S(2)}, u32[]{:S(2)}) collective-permute-start(bf16[32,4096]{1,0:T(8,128)(2,1)S(1)} %pad_maximum_fusion.refs_4_), channel_id=1, source_target_pairs={{0,1},{1,0},{2,3},{3,2},{4,5},{5,4},{6,7},{7,6},{8,9},{9,8},{10,11... | collective-permute-start | bytes 786440 | tf_op jit(solution)/shard_map/ppermute | solution.py:189
  24.4 1.3 %collective-permute-start.10 = (bf16[64,224]{1,0:T(8,128)(2,1)S(1)}, bf16[64,224]{1,0:T(8,128)(2,1)S(1)}, u32[]{:S(2)}, u32[]{:S(2)}) collective-permute-start(bf16[64,224]{1,0:T(8,128)(2,1)S(1)} %get-tuple-element.52), channel_id=1, source_target_pairs={{0,1},{1,0},{2,3},{3,2},{4,5},{5,4},{6,7},{7,6},{8,9},{9,8},{10,11... | collective-permute-start | bytes 86024 | tf_op jit(solution)/shard_map/ppermute | solution.py:189
  25.7 19.1 %copy-start = (s32[8192]{0:T(1024)S(1)}, s32[8192]{0:T(1024)}, u32[]{:S(2)}) copy-start(s32[8192]{0:T(1024)} %param.9) | copy-start | bytes 98308
  26.5 7.3 %collective-permute-start.13 = (bf16[8,8192]{1,0:T(8,128)(2,1)S(1)}, bf16[8,8192]{1,0:T(8,128)(2,1)S(1)}, u32[]{:S(2)}, u32[]{:S(2)}) collective-permute-start(bf16[8,8192]{1,0:T(8,128)(2,1)S(1)} %get-tuple-element.62), channel_id=1, source_target_pairs={{0,6},{1,7},{2,4},{3,5},{4,2},{5,3},{6,0},{7,1},{8,14},{9,15},{10,... | collective-permute-start | bytes 393224 | tf_op jit(solution)/shard_map/ppermute | solution.py:189
  27.6 7.5 %collective-permute-start.14 = (bf16[8,8192]{1,0:T(8,128)(2,1)S(1)}, bf16[8,8192]{1,0:T(8,128)(2,1)S(1)}, u32[]{:S(2)}, u32[]{:S(2)}) collective-permute-start(bf16[8,8192]{1,0:T(8,128)(2,1)S(1)} %get-tuple-element.63), channel_id=1, source_target_pairs={{0,4},{1,3},{2,6},{3,1},{4,0},{5,7},{6,2},{7,5},{8,12},{9,11},{10,... | collective-permute-start | bytes 393224 | tf_op jit(solution)/shard_map/ppermute | solution.py:189
  28.8 7.2 %collective-permute-start.15 = (bf16[8,8192]{1,0:T(8,128)(2,1)S(1)}, bf16[8,8192]{1,0:T(8,128)(2,1)S(1)}, u32[]{:S(2)}, u32[]{:S(2)}) collective-permute-start(bf16[8,8192]{1,0:T(8,128)(2,1)S(1)} %get-tuple-element.64), channel_id=1, source_target_pairs={{0,2},{1,5},{2,0},{3,7},{4,6},{5,1},{6,4},{7,3},{8,10},{9,13},{10,... | collective-permute-start | bytes 393224 | tf_op jit(solution)/shard_map/ppermute | solution.py:189
  30.1 7.8 %collective-permute-start.12 = (bf16[16,8192]{1,0:T(8,128)(2,1)S(1)}, bf16[16,8192]{1,0:T(8,128)(2,1)S(1)}, u32[]{:S(2)}, u32[]{:S(2)}) collective-permute-start(bf16[16,8192]{1,0:T(8,128)(2,1)S(1)} %slice.56), channel_id=1, source_target_pairs={{0,4},{1,3},{2,6},{3,1},{4,0},{5,7},{6,2},{7,5},{8,12},{9,11},{10,... | collective-permute-start | bytes 786440 | tf_op jit(solution)/shard_map/ppermute | solution.py:189
  36.0 8.9 %collective-permute-start.16 = (bf16[8,8192]{1,0:T(8,128)(2,1)S(1)}, bf16[8,8192]{1,0:T(8,128)(2,1)S(1)}, u32[]{:S(2)}, u32[]{:S(2)}) collective-permute-start(bf16[8,8192]{1,0:T(8,128)(2,1)S(1)} %add_convert_fusion), channel_id=1, source_target_pairs={{0,8},{1,9},{2,10},{3,11},{4,12},{5,13},{6,14},{7,15},{8,0},{9,1},... | collective-permute-start | bytes 393224 | tf_op jit(solution)/shard_map/ppermute | solution.py:189
  38.0 6.9 %collective-permute-start.17 = (bf16[8,8192]{1,0:T(8,128)(2,1)S(1)}, bf16[8,8192]{1,0:T(8,128)(2,1)S(1)}, u32[]{:S(2)}, u32[]{:S(2)}) collective-permute-start(bf16[8,8192]{1,0:T(8,128)(2,1)S(1)} %slice.57), channel_id=1, source_target_pairs={{0,2},{1,5},{2,0},{3,7},{4,6},{5,1},{6,4},{7,3},{8,10},{9,13},{10,... | collective-permute-start | bytes 393224 | tf_op jit(solution)/shard_map/ppermute | solution.py:189

commit v13 on v10

--- a/solution.py
+++ b/solution.py
@@ -12,6 +12,7 @@
 PIECES = 2
 SPANS = 2
 TURNS = 8
+FIRST, SECOND, THIRD = (8, 4), (4, 2), (2, 8)
 NT = (((1,), (1,)), ((), ()))
 
 
@@ -19,56 +20,49 @@
     return pl.BlockSpec(memory_space=pltpu.VMEM)
 
 
-def turn_kernel(gate_hbm, up_hbm, _, gate_ref, up_ref, staged, sems):
-    tile = staged.shape[2] // sems.shape[1]
+def load_kernel(turned, *refs):
+    count = len(turned)
+    sources, outs = refs[:count], refs[count + 1 : 2 * count + 1]
+    staged, sems = refs[2 * count + 1 :]
+    tile = staged.shape[1] // (sems.shape[0] - 1)
     copies = []
-    for k in range(sems.shape[1]):
-        here = slice(k * tile, (k + 1) * tile)
-        for j, source in enumerate((gate_hbm, up_hbm)):
-            copies.append(
-                pltpu.make_async_copy(source.at[:, here], staged.at[j, :, here], sems.at[j, k])
-            )
-            copies[-1].start()
-    for k in range(sems.shape[1]):
-        here = slice(k * tile, (k + 1) * tile)
-        for j, out in enumerate((gate_ref, up_ref)):
-            copies[2 * k + j].wait()
-            out[here, :] = staged[j, :, here].T
-
-
-def turn(gate_w, up_w, after):
-    units, features = gate_w.shape
-    shape = jax.ShapeDtypeStruct((features, units), gate_w.dtype)
+    for source, out, turn in zip(sources, outs, turned):
+        if not turn:
+            continue
+        for k in range(sems.shape[0] - 1):
+            here = slice(k * tile, (k + 1) * tile)
+            copies.append((pltpu.make_async_copy(source.at[:, here], staged.at[:, here], sems.at[k]), out, here))
+    others = [
+        pltpu.make_async_copy(source, out, sems.at[sems.shape[0] - 1])
+        for source, out, turn in zip(sources, outs, turned)
+        if not turn
+    ]
+    for copy, _, _ in copies:
+        copy.start()
+    for copy in others:
+        copy.start()
+    for copy, out, here in copies:
+        copy.wait()
+        out[here, :] = staged[:, here].T
+    for copy in others:
+        copy.wait()
+
+
+def load(weights, turned, after):
+    shapes = [w.shape[::-1] if turn else w.shape for w, turn in zip(weights, turned)]
+    size = sum(w.size for w in weights)
     return pl.pallas_call(
-        turn_kernel,
-        out_shape=(shape, shape),
-        in_specs=[pl.BlockSpec(memory_space=pltpu.HBM)] * 2 + [pl.BlockSpec(memory_space=pl.ANY)],
-        out_specs=(vmem(), vmem()),
+        functools.partial(load_kernel, turned),
+        out_shape=[jax.ShapeDtypeStruct(shape, weights[0].dtype) for shape in shapes],
+        in_specs=[pl.BlockSpec(memory_space=pltpu.HBM)] * len(weights) + [pl.BlockSpec(memory_space=pl.ANY)],
+        out_specs=[vmem()] * len(weights),
         scratch_shapes=[
-            pltpu.VMEM((2, units, features), gate_w.dtype),
-            pltpu.SemaphoreType.DMA((2, TURNS)),
+            pltpu.VMEM(weights[0].shape, weights[0].dtype),
+            pltpu.SemaphoreType.DMA((TURNS + 1,)),
         ],
-        cost_estimate=pl.CostEstimate(flops=0, bytes_accessed=4 * units * features, transcendentals=0),
-        compiler_params=pltpu.CompilerParams(vmem_limit_bytes=24 << 20),
-    )(*(pltpu.with_memory_space_constraint(w, pltpu.HBM) for w in (gate_w, up_w)), after)
-
-
-def fetch_kernel(down_hbm, down_ref, sem):
-    copy = pltpu.make_async_copy(down_hbm, down_ref, sem)
-    copy.start()
-    copy.wait()
-
-
-def fetch(down_w):
-    return pl.pallas_call(
-        fetch_kernel,
-        out_shape=jax.ShapeDtypeStruct(down_w.shape, down_w.dtype),
-        in_specs=[pl.BlockSpec(memory_space=pltpu.HBM)],
-        out_specs=vmem(),
-        scratch_shapes=[pltpu.SemaphoreType.DMA],
-        cost_estimate=pl.CostEstimate(flops=0, bytes_accessed=2 * down_w.size, transcendentals=0),
-        compiler_params=pltpu.CompilerParams(vmem_limit_bytes=4 << 20),
-    )(pltpu.with_memory_space_constraint(down_w, pltpu.HBM))
+        cost_estimate=pl.CostEstimate(flops=0, bytes_accessed=4 * size, transcendentals=0),
+        compiler_params=pltpu.CompilerParams(vmem_limit_bytes=16 << 20),
+    )(*(pltpu.with_memory_space_constraint(w, pltpu.HBM) for w in weights), after)
 
 
 def hidden_kernel(start, last, *refs):
@@ -188,64 +182,78 @@
     members = mesh.shape["gx"]
     assert members & (members - 1) == 0 and members >= 16
 
-    square = ((4, 2), (2, 4), (6, 6))
-    far = []
+    wide = []
     mask = members // 2
-    while mask > 4:
-        far.append((mask, mask))
+    while mask > 8:
+        wide.append((mask, mask))
         mask //= 2
-    others = members // 8 - 1
 
     def swap(value, masks):
-        return lax.ppermute(value, "gx", [(i, i ^ masks[i % 2]) for i in range(members)])
+        pairs = [(i, i ^ masks[i % 2]) for i in range(members) if masks[i % 2] is not None]
+        return lax.ppermute(value, "gx", pairs)
+
+    def narrow(value):
+        return value.astype(jnp.bfloat16)
 
     def on_device(tokens, gate_weight, up_weight, down_weight, sign_pattern):
-        rows, features = tokens.shape
-
-        away = []
-        for masks in far:
-            away.append(swap(jnp.concatenate([tokens] + away), masks))
-        away = jnp.concatenate(away)
-        near = [swap(tokens, m) for m in square]
-        down_w = fetch(down_weight)
-        away, down_w = lax.optimization_barrier((away, down_w))
-        there = [swap(away, m) for m in square[:2]]
-        away, near[0] = lax.optimization_barrier((away, near[0]))
-        there.append(swap(away, square[2]))
-        gate_w, up_w = turn(gate_weight.T, up_weight.T, away)
-        there[0], *near = lax.optimization_barrier((there[0], *near))
-        near = jnp.concatenate([tokens, near[1], near[0], near[2]])
-        near_there = swap(near, (1, 1))
-        gate_w, up_w, near, *there[1:] = lax.optimization_barrier((gate_w, up_w, near, *there[1:]))
-        far_rows = [there[2], away, *there[:2]]
+        features = tokens.shape[1]
+        own = tokens
+        for masks in wide:
+            own = jnp.concatenate([own, swap(own, masks)])
+        rows = own.shape[0]
+
+        one, two, three = swap(own, FIRST), swap(own, SECOND), swap(own, THIRD)
+        four, five, six = swap(one, (4, 2)), swap(one, (2, None)), swap(one, (6, None))
+        beside = swap(two, (2, None))
+        (gate_w,) = load((gate_weight.T,), (True,), one)
+        gate_w, three, four, five, six, beside = lax.optimization_barrier((gate_w, three, four, five, six, beside))
+        seven, eight, nine = swap(three, (None, 4)), swap(three, (None, 2)), swap(three, (None, 6))
+        up_w, down_w = load((up_weight.T, down_weight), (True, False), three)
+        up_w, beside, seven, eight, nine = lax.optimization_barrier((up_w, beside, seven, eight, nine))
+        early = jnp.concatenate([own, one, two, three])
+        early_there = swap(early, (1, 1))
         spans = []
         width = features // SPANS
         for k in range(SPANS):
-            span = jnp.concatenate([piece[:, k * width : (k + 1) * width] for piece in far_rows])
+            here = slice(k * width, (k + 1) * width)
+            pieces = [five[:, here] + eight[:, here], six[:, here] + nine[:, here], beside[:, here] + seven[:, here]]
+            span = jnp.concatenate([four[:, here]] + pieces)
             spans.append((span, swap(span, (1, 1))))
-        hidden = hidden_units(gate_w, up_w, (near, near_there), spans)
-
-        count = others * rows
-        own, diagonal, rest, *sends = down(hidden, down_w, (4 * rows, count, 3 * count))
-        diagonal = diagonal + swap(sends[1], (1, 1)).astype(jnp.float32)
-        diagonal = swap(diagonal.astype(jnp.bfloat16), square[2])
+        hidden = hidden_units(gate_w, up_w, (early, early_there), spans)
+
+        near, last, rest, *sends = down(hidden, down_w, (4 * rows, rows, 3 * rows))
+        last = narrow(last + swap(sends[1], (1, 1)).astype(jnp.float32))
         rest_there, sends[0] = lax.optimization_barrier((swap(sends[2], (1, 1)), sends[0]))
-        rest = rest + rest_there.astype(jnp.float32)
-        leave = rest[count:].astype(jnp.bfloat16)
-        total = rest[:count]
-        for piece in (diagonal, swap(leave[:count], square[0]), swap(leave[count:], square[1])):
-            total = total + piece.astype(jnp.float32)
-        arrived = []
-        for masks in reversed(far):
-            split = total.shape[0] // 2 // rows * rows
-            piece = swap(total[split:].astype(jnp.bfloat16), masks)
-            arrived.append(piece[:rows])
-            total = total[:split] + piece[rows:].astype(jnp.float32)
-
-        own = own + swap(sends[0], (1, 1)).astype(jnp.float32)
-        own = own[: 2 * rows] + swap(own[2 * rows :].astype(jnp.bfloat16), square[0]).astype(jnp.float32)
-        arrived.append(swap(own[rows:].astype(jnp.bfloat16), square[1]))
-        return rotate(own[:rows], arrived, sign_pattern)
+        rest = narrow(rest + rest_there.astype(jnp.float32))
+        both, diagonal, seven = (rest[k * rows : (k + 1) * rows] for k in range(3))
+        near_there = swap(sends[0], (1, 1))
+        a, b, c, g = swap(last, (4, 2)), swap(both, (2, None)), swap(diagonal, (6, None)), swap(seven, (2, None))
+        e = swap(both, (None, 2))
+        a, diagonal = lax.optimization_barrier((a, diagonal))
+        f = swap(diagonal, (None, 6))
+        b, seven = lax.optimization_barrier((b, seven))
+        d = swap(seven, (None, 4))
+        near = near + near_there.astype(jnp.float32)
+        one = near[rows : 2 * rows]
+        for piece in (a, b, c):
+            one = one + piece.astype(jnp.float32)
+        one, near = lax.optimization_barrier((narrow(one), near))
+        own, _, two, three = (near[k * rows : (k + 1) * rows] for k in range(4))
+        for piece in (d, e, f):
+            three = three + piece.astype(jnp.float32)
+        three, g = lax.optimization_barrier((narrow(three), g))
+        two = narrow(two + g.astype(jnp.float32))
+        arrived = [swap(one, FIRST), swap(two, SECOND), swap(three, THIRD)]
+        for k in (2, 0):
+            own, arrived[k] = lax.optimization_barrier((own, arrived[k]))
+            own = own + arrived[k].astype(jnp.float32)
+        own, *arrived = lax.optimization_barrier((own, arrived[1]))
+        if wide:
+            own = own + arrived.pop().astype(jnp.float32)
+        for masks in reversed(wide):
+            half = own.shape[0] // 2
+            own = own[:half] + swap(narrow(own[half:]), masks).astype(jnp.float32)
+        return rotate(own, arrived, sign_pattern)
 
     placed = (P(("groups", "gx"), None), P(None, "gx"), P(None, "gx"), P("gx", None), P())
     return jax.shard_map(

time: 45.1 us -> 64.7 us (1.43)
  starting transfers between devices: 20.2 us -> 41.9 us
  waiting for transfers between devices: 13.5 us -> 11.5 us
    ppermute x19 -> x26, starting transfers between devices: 20.2 us -> 41.9 us  [swap(): return lax.ppermute(value, 'gx', pairs)]
    ppermute x19 -> x26, waiting for transfers between devices: 13.5 us -> 11.5 us  [swap(): return lax.ppermute(value, 'gx', pairs)]
  transfers between devices with their start and end apart: 19 -> 26, of which waited for: 9 -> 8; matrix products, arithmetic and copies ran while one was open for 3% -> 2% of each run, Pallas kernels for 16% -> 10%
where the time goes in v13:
time: 64.7 us; the launch traced here: 64.3 us
  starting transfers between devices  41.9 us (65%)
  waiting for transfers between devices  11.5 us (18%)
  Pallas kernels  8.99 us (14%)
  local copies, waits for them, and re-layouts  1.02 us (2%)
    ppermute x26, starting transfers between devices, swap(): return lax.ppermute(value, 'gx', pairs)  41.9 us
    ppermute x26, waiting for transfers between devices, swap(): return lax.ppermute(value, 'gx', pairs)  11.5 us
    pallas_call x2, Pallas kernels, load(): pl.pallas_call(functools.partial(load_kernel, turned), out_shape=[jax.Sha...  5.95 us
    pallas_call x2, Pallas kernels, hidden_units(): pl.pallas_call(functools.partial(hidden_kernel, start, last), out_shape=(...  1.45 us
  transfers between devices with their start and end apart: 26, of which 8 were waited for; matrix products, arithmetic and copies ran while one was open for 2% of the time, Pallas kernels for 10%

profile of v13, /device:TPU:0, one launch (start us, length us, event | category | flops | bytes accessed | tf_op | source)
XLA Modules:
  0.0 64.3 jit_solution(11043466220501543166)
XLA Ops:
  0.0 4.0 %collective-permute-start = (bf16[8,8192]{1,0:T(8,128)(2,1)}, bf16[8,8192]{1,0:T(8,128)(2,1)S(1)}, u32[]{:S(2)}, u32[]{:S(2)}) collective-permute-start(bf16[8,8192]{1,0:T(8,128)(2,1)} %param.5), channel_id=1, source_target_pairs={{0,8},{1,5},{2,10},{3,7},{4,12},{5,1},{6,14},{7,3},{8,0},{9,13},{1... | collective-permute-start | bytes 393224 | tf_op jit(solution)/shard_map/ppermute | solution.py:193
  4.0 1.6 %collective-permute-start.5 = (bf16[8,8192]{1,0:T(8,128)(2,1)}, bf16[8,8192]{1,0:T(8,128)(2,1)S(1)}, u32[]{:S(2)}, u32[]{:S(2)}) collective-permute-start(bf16[8,8192]{1,0:T(8,128)(2,1)} %param.5), channel_id=1, source_target_pairs={{0,4},{1,3},{2,6},{3,1},{4,0},{5,7},{6,2},{7,5},{8,12},{9,11},{10,... | collective-permute-start | bytes 393224 | tf_op jit(solution)/shard_map/ppermute | solution.py:193
  5.6 1.5 %collective-permute-start.1 = (bf16[8,8192]{1,0:T(8,128)(2,1)}, bf16[8,8192]{1,0:T(8,128)(2,1)S(1)}, u32[]{:S(2)}, u32[]{:S(2)}) collective-permute-start(bf16[8,8192]{1,0:T(8,128)(2,1)} %param.5), channel_id=1, source_target_pairs={{0,2},{1,9},{2,0},{3,11},{4,6},{5,13},{6,4},{7,15},{8,10},{9,1},{1... | collective-permute-start | bytes 393224 | tf_op jit(solution)/shard_map/ppermute | solution.py:193
  7.1 0.9 %constant_dynamic-update-slice_fusion.3 = bf16[32,8192]{1,0:T(8,128)(2,1)S(1)} fusion(bf16[8,8192]{1,0:T(8,128)(2,1)} %param.5), kind=kLoop, calls=%fused_computation.30 | loop fusion | bytes 262144
  8.1 0.0 collective-permute-done.refs_1_
  8.1 4.4 %collective-permute-start.2 = (bf16[8,8192]{1,0:T(8,128)(2,1)S(1)}, bf16[8,8192]{1,0:T(8,128)(2,1)S(1)}, u32[]{:S(2)}, u32[]{:S(2)}) collective-permute-start(bf16[8,8192]{1,0:T(8,128)(2,1)S(1)} %collective-permute-done.refs_1_), channel_id=1, source_target_pairs={{0,4},{1,3},{2,6},{3,1},{4,0},{5,7},{6,2},{7,5},{8,12},{9,11},{10,... | collective-permute-start | bytes 393224 | tf_op jit(solution)/shard_map/ppermute | solution.py:193
  12.5 2.8 %collective-permute-start.3 = (bf16[8,8192]{1,0:T(8,128)(2,1)S(1)}, bf16[8,8192]{1,0:T(8,128)(2,1)S(1)}, u32[]{:S(2)}, u32[]{:S(2)}) collective-permute-start(bf16[8,8192]{1,0:T(8,128)(2,1)S(1)} %collective-permute-done.refs_1_), channel_id=1, source_target_pairs={{0,2},{2,0},{4,6},{6,4},{8,10},{10,8},{12,14},{14,12},{16,18},{18,... | collective-permute-start | bytes 393224 | tf_op jit(solution)/shard_map/ppermute | solution.py:193
  15.3 2.9 %collective-permute-start.4 = (bf16[8,8192]{1,0:T(8,128)(2,1)S(1)}, bf16[8,8192]{1,0:T(8,128)(2,1)S(1)}, u32[]{:S(2)}, u32[]{:S(2)}) collective-permute-start(bf16[8,8192]{1,0:T(8,128)(2,1)S(1)} %collective-permute-done.refs_1_), channel_id=1, source_target_pairs={{0,6},{2,4},{4,2},{6,0},{8,14},{10,12},{12,10},{14,8},{16,22},{18,... | collective-permute-start | bytes 393224 | tf_op jit(solution)/shard_map/ppermute | solution.py:193
  18.2 0.0 collective-permute-done.5
  18.2 3.9 %collective-permute-start.6 = (bf16[8,8192]{1,0:T(8,128)(2,1)S(1)}, bf16[8,8192]{1,0:T(8,128)(2,1)S(1)}, u32[]{:S(2)}, u32[]{:S(2)}) collective-permute-start(bf16[8,8192]{1,0:T(8,128)(2,1)S(1)} %collective-permute-done.5), channel_id=1, source_target_pairs={{0,2},{2,0},{4,6},{6,4},{8,10},{10,8},{12,14},{14,12},{16,18},{18,... | collective-permute-start | bytes 393224 | tf_op jit(solution)/shard_map/ppermute | solution.py:193
  22.2 2.7 %shard_map.55.refs_0_ = bf16[8192,224]{1,0:T(8,128)(2,1)S(1)} custom-call(bf16[224,8192]{1,0:T(8,128)(2,1)} %bitcast.5, bf16[8,8192]{1,0:T(8,128)(2,1)S(1)} %collective-permute-done.refs_1_), custom_call_target="tpu_custom_call" | custom-call | bytes 7340032 | tf_op jit(solution)/shard_map/pallas_call | solution.py:54
  24.9 0.0 collective-permute-done.1.refs_2_
  24.9 0.0 collective-permute-done.2
  24.9 0.0 collective-permute-done.3
  24.9 0.0 collective-permute-done.4
  24.9 0.9 %collective-permute-done.6 = bf16[8,8192]{1,0:T(8,128)(2,1)S(1)} collective-permute-done((bf16[8,8192]{1,0:T(8,128)(2,1)S(1)}, bf16[8,8192]{1,0:T(8,128)(2,1)S(1)}, u32[]{:S(2)}, u32[]{:S(2)}) %collective-permute-start.6) | collective-permute-done | bytes 131104 | tf_op jit(solution)/shard_map/ppermute | solution.py:193
  25.9 0.7 %collective-permute-start.7 = (bf16[8,8192]{1,0:T(8,128)(2,1)S(1)}, bf16[8,8192]{1,0:T(8,128)(2,1)S(1)}, u32[]{:S(2)}, u32[]{:S(2)}) collective-permute-start(bf16[8,8192]{1,0:T(8,128)(2,1)S(1)} %collective-permute-done.1.refs_2_), channel_id=1, source_target_pairs={{1,5},{3,7},{5,1},{7,3},{9,13},{11,15},{13,9},{15,11},{17,21},{19,... | collective-permute-start | bytes 393224 | tf_op jit(solution)/shard_map/ppermute | solution.py:193
  26.6 0.7 %collective-permute-start.8 = (bf16[8,8192]{1,0:T(8,128)(2,1)S(1)}, bf16[8,8192]{1,0:T(8,128)(2,1)S(1)}, u32[]{:S(2)}, u32[]{:S(2)}) collective-permute-start(bf16[8,8192]{1,0:T(8,128)(2,1)S(1)} %collective-permute-done.1.refs_2_), channel_id=1, source_target_pairs={{1,3},{3,1},{5,7},{7,5},{9,11},{11,9},{13,15},{15,13},{17,19},{19,... | collective-permute-start | bytes 393224 | tf_op jit(solution)/shard_map/ppermute | solution.py:193
  27.2 0.7 %collective-permute-start.9 = (bf16[8,8192]{1,0:T(8,128)(2,1)S(1)}, bf16[8,8192]{1,0:T(8,128)(2,1)S(1)}, u32[]{:S(2)}, u32[]{:S(2)}) collective-permute-start(bf16[8,8192]{1,0:T(8,128)(2,1)S(1)} %collective-permute-done.1.refs_2_), channel_id=1, source_target_pairs={{1,7},{3,5},{5,3},{7,1},{9,15},{11,13},{13,11},{15,9},{17,23},{19,... | collective-permute-start | bytes 393224 | tf_op jit(solution)/shard_map/ppermute | solution.py:193
  27.9 0.1 collective-permute-start.10
  28.0 3.3 %shard_map.56 = (bf16[8192,224]{1,0:T(8,128)(2,1)S(1)}, bf16[224,8192]{1,0:T(8,128)(2,1)S(1)}) custom-call(bf16[224,8192]{1,0:T(8,128)(2,1)} %bitcast.4, bf16[224,8192]{1,0:T(8,128)(2,1)} %refs_1_.1, bf16[8,8192]{1,0:T(8,128)(2,1)S(1)} %collective-permute-done.1.refs_2_), custom_call_target="tpu_custom_call" | custom-call | bytes 14680064 | tf_op jit(solution)/shard_map/pallas_call | solution.py:54
  31.3 0.0 collective-permute-done.7
  31.3 0.0 collective-permute-done.8
  31.3 0.0 collective-permute-done.9
  31.4 0.6 collective-permute-start.12
  32.0 0.1 collective-permute-start.11
  32.1 1.1 %collective-permute-done.12.refs_5_ = bf16[32,4096]{1,0:T(8,128)(2,1)S(1)} collective-permute-done((bf16[32,4096]{1,0:T(8,128)(2,1)S(1)}, bf16[32,4096]{1,0:T(8,128)(2,1)S(1)}, u32[]{:S(2)}, u32[]{:S(2)}) %collective-permute-start.12) | collective-permute-done | bytes 262176 | tf_op jit(solution)/shard_map/ppermute | solution.py:193
  33.1 0.0 collective-permute-done.10.refs_3_
  33.1 0.7 %shard_map.57 = (f32[128,224]{1,0:T(8,128)S(1)}, f32[128,224]{1,0:T(8,128)S(1)}) custom-call(bf16[8192,224]{1,0:T(8,128)(2,1)S(1)} %shard_map.55.refs_0_, bf16[8192,224]{1,0:T(8,128)(2,1)S(1)} %get-tuple-element.46.refs_1_, bf16[32,8192]{1,0:T(8,128)(2,1)S(1)} %constant_dynamic-update-slice_fusion.refs_2_, ...), custom_call_target="tpu_custom_call" | custom-call | flops 469762048 | bytes 3670016 | tf_op jit(solution)/shard_map/pallas_call | solution.py:93
  33.9 0.0 collective-permute-done.11.refs_5_
  33.9 0.7 %shard_map.58.hidden_ref = bf16[128,224]{1,0:T(8,128)(2,1)S(1)} custom-call(bf16[8192,224]{1,0:T(8,128)(2,1)S(1)} %shard_map.55.refs_0_, bf16[8192,224]{1,0:T(8,128)(2,1)S(1)} %get-tuple-element.46.refs_1_, bf16[32,8192]{1,0:T(8,128)(2,1)S(1)} %constant_dynamic-update-slice_fusion.refs_2_, bf16[32,8192]{1,0:T(8,128)(2,1)S(1)} %collective-permute-done.10.refs_3_, ...), custom_call_target="tpu_custom_call" | custom-call | flops 469762048 | bytes 3670016 | tf_op jit(solution)/shard_map/pallas_call | solution.py:93
  34.6 0.7 %shard_map.59 = (f32[32,8192]{1,0:T(8,128)S(1)}, f32[8,8192]{1,0:T(8,128)S(1)}, f32[24,8192]{1,0:T(8,128)S(1)}, bf16[32,8192]{1,0:T(8,128)(2,1)S(1)}, bf16[8,819...) custom-call(bf16[128,224]{1,0:T(8,128)(2,1)S(1)} %shard_map.58.hidden_ref, bf16[224,8192]{1,0:T(8,128)(2,1)S(1)} %get-tuple-element.56.down_ref), custom_call_target="tpu_custom_call" | custom-call | flops 469762048 | bytes 3670016 | tf_op jit(solution)/shard_map/pallas_call | solution.py:121
  35.3 0.4 collective-permute-start.15
  35.8 0.1 collective-permute-start.13
  35.9 0.8 %collective-permute-done.15 = bf16[8,8192]{1,0:T(8,128)(2,1)S(1)} collective-permute-done((bf16[8,8192]{1,0:T(8,128)(2,1)S(1)}, bf16[8,8192]{1,0:T(8,128)(2,1)S(1)}, u32[]{:S(2)}, u32[]{:S(2)}) %collective-permute-start.15) | collective-permute-done | bytes 131104 | tf_op jit(solution)/shard_map/ppermute | solution.py:193
  36.8 1.6 %collective-permute-start.16 = (bf16[8,8192]{1,0:T(8,128)(2,1)S(1)}, bf16[8,8192]{1,0:T(8,128)(2,1)S(1)}, u32[]{:S(2)}, u32[]{:S(2)}) collective-permute-start(bf16[8,8192]{1,0:T(8,128)(2,1)S(1)} %add_convert_fusion.3), channel_id=1, source_target_pairs={{0,4},{1,3},{2,6},{3,1},{4,0},{5,7},{6,2},{7,5},{8,12},{9,11},{10,... | collective-permute-start | bytes 393224 | tf_op jit(solution)/shard_map/ppermute | solution.py:193
  38.4 0.0 collective-permute-done.13
  38.4 0.0 collective-permute-start.14
  38.4 0.1 add_convert_fusion
  38.5 0.0 copy-start
  38.5 2.5 %collective-permute-start.17 = (bf16[8,8192]{1,0:T(8,128)(2,1)S(1)}, bf16[8,8192]{1,0:T(8,128)(2,1)S(1)}, u32[]{:S(2)}, u32[]{:S(2)}) collective-permute-start(bf16[8,8192]{1,0:T(8,128)(2,1)S(1)} %get-tuple-element.82), channel_id=1, source_target_pairs={{0,2},{2,0},{4,6},{6,4},{8,10},{10,8},{12,14},{14,12},{16,18},{18,... | collective-permute-start | bytes 393224 | tf_op jit(solution)/shard_map/ppermute | solution.py:193
  41.1 0.7 %collective-permute-start.20 = (bf16[8,8192]{1,0:T(8,128)(2,1)S(1)}, bf16[8,8192]{1,0:T(8,128)(2,1)S(1)}, u32[]{:S(2)}, u32[]{:S(2)}) collective-permute-start(bf16[8,8192]{1,0:T(8,128)(2,1)S(1)} %get-tuple-element.82), channel_id=1, source_target_pairs={{1,3},{3,1},{5,7},{7,5},{9,11},{11,9},{13,15},{15,13},{17,19},{19,... | collective-permute-start | bytes 393224 | tf_op jit(solution)/shard_map/ppermute | solution.py:193
  41.7 3.6 %collective-permute-start.18 = (bf16[8,8192]{1,0:T(8,128)(2,1)S(1)}, bf16[8,8192]{1,0:T(8,128)(2,1)S(1)}, u32[]{:S(2)}, u32[]{:S(2)}) collective-permute-start(bf16[8,8192]{1,0:T(8,128)(2,1)S(1)} %get-tuple-element.69), channel_id=1, source_target_pairs={{0,6},{2,4},{4,2},{6,0},{8,14},{10,12},{12,10},{14,8},{16,22},{18,... | collective-permute-start | bytes 393224 | tf_op jit(solution)/shard_map/ppermute | solution.py:193
  45.4 0.0 collective-permute-done.16
  45.4 0.7 %collective-permute-start.21 = (bf16[8,8192]{1,0:T(8,128)(2,1)S(1)}, bf16[8,8192]{1,0:T(8,128)(2,1)S(1)}, u32[]{:S(2)}, u32[]{:S(2)}) collective-permute-start(bf16[8,8192]{1,0:T(8,128)(2,1)S(1)} %get-tuple-element.69), channel_id=1, source_target_pairs={{1,7},{3,5},{5,3},{7,1},{9,15},{11,13},{13,11},{15,9},{17,23},{19,... | collective-permute-start | bytes 393224 | tf_op jit(solution)/shard_map/ppermute | solution.py:193
  46.1 0.5 collective-permute-done.17
  46.5 2.7 %collective-permute-start.22 = (bf16[8,8192]{1,0:T(8,128)(2,1)S(1)}, bf16[8,8192]{1,0:T(8,128)(2,1)S(1)}, u32[]{:S(2)}, u32[]{:S(2)}) collective-permute-start(bf16[8,8192]{1,0:T(8,128)(2,1)S(1)} %get-tuple-element.68), channel_id=1, source_target_pairs={{0,2},{2,0},{4,6},{6,4},{8,10},{10,8},{12,14},{14,12},{16,18},{18,... | collective-permute-start | bytes 393224 | tf_op jit(solution)/shard_map/ppermute | solution.py:193
  49.3 0.0 collective-permute-done.14
  49.3 0.7 %collective-permute-start.19 = (bf16[8,8192]{1,0:T(8,128)(2,1)S(1)}, bf16[8,8192]{1,0:T(8,128)(2,1)S(1)}, u32[]{:S(2)}, u32[]{:S(2)}) collective-permute-start(bf16[8,8192]{1,0:T(8,128)(2,1)S(1)} %get-tuple-element.68), channel_id=1, source_target_pairs={{1,5},{3,7},{5,1},{7,3},{9,13},{11,15},{13,9},{15,11},{17,21},{19,... | collective-permute-start | bytes 393224 | tf_op jit(solution)/shard_map/ppermute | solution.py:193
  50.0 0.1 convert_add_fusion
  50.1 0.5 collective-permute-done.18
  50.6 0.1 fusion.2
  50.7 0.0 collective-permute-done.21
  50.7 0.0 collective-permute-done.20
  50.7 0.0 collective-permute-done.19
  50.7 0.1 add_convert_fusion.2
  50.8 2.6 %collective-permute-done.22 = bf16[8,8192]{1,0:T(8,128)(2,1)S(1)} collective-permute-done((bf16[8,8192]{1,0:T(8,128)(2,1)S(1)}, bf16[8,8192]{1,0:T(8,128)(2,1)S(1)}, u32[]{:S(2)}, u32[]{:S(2)}) %collective-permute-start.22) | collective-permute-done | bytes 131104 | tf_op jit(solution)/shard_map/ppermute | solution.py:193
  53.4 0.8 %collective-permute-start.23 = (bf16[8,8192]{1,0:T(8,128)(2,1)S(1)}, bf16[8,8192]{1,0:T(8,128)(2,1)S(1)}, u32[]{:S(2)}, u32[]{:S(2)}) collective-permute-start(bf16[8,8192]{1,0:T(8,128)(2,1)S(1)} %add_convert_fusion.2), channel_id=1, source_target_pairs={{0,2},{1,9},{2,0},{3,11},{4,6},{5,13},{6,4},{7,15},{8,10},{9,1},{1... | collective-permute-start | bytes 393224 | tf_op jit(solution)/shard_map/ppermute | solution.py:193
  54.3 3.2 %collective-permute-start.24 = (bf16[8,8192]{1,0:T(8,128)(2,1)S(1)}, bf16[8,8192]{1,0:T(8,128)(2,1)S(1)}, u32[]{:S(2)}, u32[]{:S(2)}) collective-permute-start(bf16[8,8192]{1,0:T(8,128)(2,1)S(1)} %fusion.2), channel_id=1, source_target_pairs={{0,8},{1,5},{2,10},{3,7},{4,12},{5,1},{6,14},{7,3},{8,0},{9,13},{1... | collective-permute-start | bytes 393224 | tf_op jit(solution)/shard_map/ppermute | solution.py:193
  57.5 0.9 %collective-permute-start.25 = (bf16[8,8192]{1,0:T(8,128)(2,1)S(1)}, bf16[8,8192]{1,0:T(8,128)(2,1)S(1)}, u32[]{:S(2)}, u32[]{:S(2)}) collective-permute-start(bf16[8,8192]{1,0:T(8,128)(2,1)S(1)} %get-tuple-element.79), channel_id=1, source_target_pairs={{0,4},{1,3},{2,6},{3,1},{4,0},{5,7},{6,2},{7,5},{8,12},{9,11},{10,... | collective-permute-start | bytes 393224 | tf_op jit(solution)/shard_map/ppermute | solution.py:193
  58.4 0.0 collective-permute-done.23
  58.4 4.0 %collective-permute-done.24 = bf16[8,8192]{1,0:T(8,128)(2,1)S(1)} collective-permute-done((bf16[8,8192]{1,0:T(8,128)(2,1)S(1)}, bf16[8,8192]{1,0:T(8,128)(2,1)S(1)}, u32[]{:S(2)}, u32[]{:S(2)}) %collective-permute-start.24) | collective-permute-done | bytes 131104 | tf_op jit(solution)/shard_map/ppermute | solution.py:193
  62.4 1.0 %collective-permute-done.25.refs_1_ = bf16[8,8192]{1,0:T(8,128)(2,1)S(1)} collective-permute-done((bf16[8,8192]{1,0:T(8,128)(2,1)S(1)}, bf16[8,8192]{1,0:T(8,128)(2,1)S(1)}, u32[]{:S(2)}, u32[]{:S(2)}) %collective-permute-start.25) | collective-permute-done | bytes 131104 | tf_op jit(solution)/shard_map/ppermute | solution.py:193
  63.4 0.9 %shard_map.60 = bf16[8,8192]{1,0:T(8,128)(2,1)} custom-call(f32[8,8192]{1,0:T(8,128)S(1)} %convert_add_fusion.1.refs_0_, bf16[8,8192]{1,0:T(8,128)(2,1)S(1)} %collective-permute-done.25.refs_1_, s32[1,8192]{1,0:T(1,128)S(1)} %bitcast.3, bf16[256,128]{1,0:T(8,128)(2,1)S(1)} %pad_maximum_fusion.2.refs_3_), custom_call_target="tpu_custom_call" | custom-call | tf_op jit(solution)/shard_map/pallas_call | solution.py:171
  (16 shorter events, 0.3 us)
Async XLA Ops:
  0.0 8.1 %collective-permute-start = (bf16[8,8192]{1,0:T(8,128)(2,1)}, bf16[8,8192]{1,0:T(8,128)(2,1)S(1)}, u32[]{:S(2)}, u32[]{:S(2)}) collective-permute-start(bf16[8,8192]{1,0:T(8,128)(2,1)} %param.5), channel_id=1, source_target_pairs={{0,8},{1,5},{2,10},{3,7},{4,12},{5,1},{6,14},{7,3},{8,0},{9,13},{1... | collective-permute-start | bytes 393224 | tf_op jit(solution)/shard_map/ppermute | solution.py:193
  4.0 14.2 %collective-permute-start.5 = (bf16[8,8192]{1,0:T(8,128)(2,1)}, bf16[8,8192]{1,0:T(8,128)(2,1)S(1)}, u32[]{:S(2)}, u32[]{:S(2)}) collective-permute-start(bf16[8,8192]{1,0:T(8,128)(2,1)} %param.5), channel_id=1, source_target_pairs={{0,4},{1,3},{2,6},{3,1},{4,0},{5,7},{6,2},{7,5},{8,12},{9,11},{10,... | collective-permute-start | bytes 393224 | tf_op jit(solution)/shard_map/ppermute | solution.py:193
  5.6 19.3 %collective-permute-start.1 = (bf16[8,8192]{1,0:T(8,128)(2,1)}, bf16[8,8192]{1,0:T(8,128)(2,1)S(1)}, u32[]{:S(2)}, u32[]{:S(2)}) collective-permute-start(bf16[8,8192]{1,0:T(8,128)(2,1)} %param.5), channel_id=1, source_target_pairs={{0,2},{1,9},{2,0},{3,11},{4,6},{5,13},{6,4},{7,15},{8,10},{9,1},{1... | collective-permute-start | bytes 393224 | tf_op jit(solution)/shard_map/ppermute | solution.py:193
  8.1 16.8 %collective-permute-start.2 = (bf16[8,8192]{1,0:T(8,128)(2,1)S(1)}, bf16[8,8192]{1,0:T(8,128)(2,1)S(1)}, u32[]{:S(2)}, u32[]{:S(2)}) collective-permute-start(bf16[8,8192]{1,0:T(8,128)(2,1)S(1)} %collective-permute-done.refs_1_), channel_id=1, source_target_pairs={{0,4},{1,3},{2,6},{3,1},{4,0},{5,7},{6,2},{7,5},{8,12},{9,11},{10,... | collective-permute-start | bytes 393224 | tf_op jit(solution)/shard_map/ppermute | solution.py:193
  12.5 12.4 %collective-permute-start.3 = (bf16[8,8192]{1,0:T(8,128)(2,1)S(1)}, bf16[8,8192]{1,0:T(8,128)(2,1)S(1)}, u32[]{:S(2)}, u32[]{:S(2)}) collective-permute-start(bf16[8,8192]{1,0:T(8,128)(2,1)S(1)} %collective-permute-done.refs_1_), channel_id=1, source_target_pairs={{0,2},{2,0},{4,6},{6,4},{8,10},{10,8},{12,14},{14,12},{16,18},{18,... | collective-permute-start | bytes 393224 | tf_op jit(solution)/shard_map/ppermute | solution.py:193
  15.3 9.6 %collective-permute-start.4 = (bf16[8,8192]{1,0:T(8,128)(2,1)S(1)}, bf16[8,8192]{1,0:T(8,128)(2,1)S(1)}, u32[]{:S(2)}, u32[]{:S(2)}) collective-permute-start(bf16[8,8192]{1,0:T(8,128)(2,1)S(1)} %collective-permute-done.refs_1_), channel_id=1, source_target_pairs={{0,6},{2,4},{4,2},{6,0},{8,14},{10,12},{12,10},{14,8},{16,22},{18,... | collective-permute-start | bytes 393224 | tf_op jit(solution)/shard_map/ppermute | solution.py:193
  18.2 7.6 %collective-permute-start.6 = (bf16[8,8192]{1,0:T(8,128)(2,1)S(1)}, bf16[8,8192]{1,0:T(8,128)(2,1)S(1)}, u32[]{:S(2)}, u32[]{:S(2)}) collective-permute-start(bf16[8,8192]{1,0:T(8,128)(2,1)S(1)} %collective-permute-done.5), channel_id=1, source_target_pairs={{0,2},{2,0},{4,6},{6,4},{8,10},{10,8},{12,14},{14,12},{16,18},{18,... | collective-permute-start | bytes 393224 | tf_op jit(solution)/shard_map/ppermute | solution.py:193
  25.9 5.4 %collective-permute-start.7 = (bf16[8,8192]{1,0:T(8,128)(2,1)S(1)}, bf16[8,8192]{1,0:T(8,128)(2,1)S(1)}, u32[]{:S(2)}, u32[]{:S(2)}) collective-permute-start(bf16[8,8192]{1,0:T(8,128)(2,1)S(1)} %collective-permute-done.1.refs_2_), channel_id=1, source_target_pairs={{1,5},{3,7},{5,1},{7,3},{9,13},{11,15},{13,9},{15,11},{17,21},{19,... | collective-permute-start | bytes 393224 | tf_op jit(solution)/shard_map/ppermute | solution.py:193
  26.6 4.8 %collective-permute-start.8 = (bf16[8,8192]{1,0:T(8,128)(2,1)S(1)}, bf16[8,8192]{1,0:T(8,128)(2,1)S(1)}, u32[]{:S(2)}, u32[]{:S(2)}) collective-permute-start(bf16[8,8192]{1,0:T(8,128)(2,1)S(1)} %collective-permute-done.1.refs_2_), channel_id=1, source_target_pairs={{1,3},{3,1},{5,7},{7,5},{9,11},{11,9},{13,15},{15,13},{17,19},{19,... | collective-permute-start | bytes 393224 | tf_op jit(solution)/shard_map/ppermute | solution.py:193
  27.2 4.1 %collective-permute-start.9 = (bf16[8,8192]{1,0:T(8,128)(2,1)S(1)}, bf16[8,8192]{1,0:T(8,128)(2,1)S(1)}, u32[]{:S(2)}, u32[]{:S(2)}) collective-permute-start(bf16[8,8192]{1,0:T(8,128)(2,1)S(1)} %collective-permute-done.1.refs_2_), channel_id=1, source_target_pairs={{1,7},{3,5},{5,3},{7,1},{9,15},{11,13},{13,11},{15,9},{17,23},{19,... | collective-permute-start | bytes 393224 | tf_op jit(solution)/shard_map/ppermute | solution.py:193
  27.9 5.2 %collective-permute-start.10 = (bf16[32,8192]{1,0:T(8,128)(2,1)S(1)}, bf16[32,8192]{1,0:T(8,128)(2,1)S(1)}, u32[]{:S(2)}, u32[]{:S(2)}) collective-permute-start(bf16[32,8192]{1,0:T(8,128)(2,1)S(1)} %constant_dynamic-update-slice_fusion.refs_2_), channel_id=1, source_target_pairs={{0,1},{1,0},{2,3},{3,2},{4,5},{5,4},{6,7},{7,6},{8,9},{9,8},{10,11... | collective-permute-start | bytes 1572872 | tf_op jit(solution)/shard_map/ppermute | solution.py:193
  31.4 1.7 %collective-permute-start.12 = (bf16[32,4096]{1,0:T(8,128)(2,1)S(1)}, bf16[32,4096]{1,0:T(8,128)(2,1)S(1)}, u32[]{:S(2)}, u32[]{:S(2)}) collective-permute-start(bf16[32,4096]{1,0:T(8,128)(2,1)S(1)} %pad_maximum_fusion.1.refs_4_), channel_id=1, source_target_pairs={{0,1},{1,0},{2,3},{3,2},{4,5},{5,4},{6,7},{7,6},{8,9},{9,8},{10,11... | collective-permute-start | bytes 786440 | tf_op jit(solution)/shard_map/ppermute | solution.py:193
  32.0 1.9 %collective-permute-start.11 = (bf16[32,4096]{1,0:T(8,128)(2,1)S(1)}, bf16[32,4096]{1,0:T(8,128)(2,1)S(1)}, u32[]{:S(2)}, u32[]{:S(2)}) collective-permute-start(bf16[32,4096]{1,0:T(8,128)(2,1)S(1)} %pad_maximum_fusion.refs_4_), channel_id=1, source_target_pairs={{0,1},{1,0},{2,3},{3,2},{4,5},{5,4},{6,7},{7,6},{8,9},{9,8},{10,11... | collective-permute-start | bytes 786440 | tf_op jit(solution)/shard_map/ppermute | solution.py:193
  35.3 1.4 %collective-permute-start.15 = (bf16[8,8192]{1,0:T(8,128)(2,1)S(1)}, bf16[8,8192]{1,0:T(8,128)(2,1)S(1)}, u32[]{:S(2)}, u32[]{:S(2)}) collective-permute-start(bf16[8,8192]{1,0:T(8,128)(2,1)S(1)} %get-tuple-element.62), channel_id=1, source_target_pairs={{0,1},{1,0},{2,3},{3,2},{4,5},{5,4},{6,7},{7,6},{8,9},{9,8},{10,11... | collective-permute-start | bytes 393224 | tf_op jit(solution)/shard_map/ppermute | solution.py:193
  35.8 2.6 %collective-permute-start.13 = (bf16[24,8192]{1,0:T(8,128)(2,1)S(1)}, bf16[24,8192]{1,0:T(8,128)(2,1)S(1)}, u32[]{:S(2)}, u32[]{:S(2)}) collective-permute-start(bf16[24,8192]{1,0:T(8,128)(2,1)S(1)} %get-tuple-element.58), channel_id=1, source_target_pairs={{0,1},{1,0},{2,3},{3,2},{4,5},{5,4},{6,7},{7,6},{8,9},{9,8},{10,11... | collective-permute-start | bytes 1179656 | tf_op jit(solution)/shard_map/ppermute | solution.py:193
  36.8 8.6 %collective-permute-start.16 = (bf16[8,8192]{1,0:T(8,128)(2,1)S(1)}, bf16[8,8192]{1,0:T(8,128)(2,1)S(1)}, u32[]{:S(2)}, u32[]{:S(2)}) collective-permute-start(bf16[8,8192]{1,0:T(8,128)(2,1)S(1)} %add_convert_fusion.3), channel_id=1, source_target_pairs={{0,4},{1,3},{2,6},{3,1},{4,0},{5,7},{6,2},{7,5},{8,12},{9,11},{10,... | collective-permute-start | bytes 393224 | tf_op jit(solution)/shard_map/ppermute | solution.py:193
  38.4 10.9 %collective-permute-start.14 = (bf16[32,8192]{1,0:T(8,128)(2,1)S(1)}, bf16[32,8192]{1,0:T(8,128)(2,1)S(1)}, u32[]{:S(2)}, u32[]{:S(2)}) collective-permute-start(bf16[32,8192]{1,0:T(8,128)(2,1)S(1)} %get-tuple-element.60), channel_id=1, source_target_pairs={{0,1},{1,0},{2,3},{3,2},{4,5},{5,4},{6,7},{7,6},{8,9},{9,8},{10,11... | collective-permute-start | bytes 1572872 | tf_op jit(solution)/shard_map/ppermute | solution.py:193
  38.5 24.9 %copy-start = (s32[8192]{0:T(1024)S(1)}, s32[8192]{0:T(1024)}, u32[]{:S(2)}) copy-start(s32[8192]{0:T(1024)} %param.9) | copy-start | bytes 98308
  38.5 8.0 %collective-permute-start.17 = (bf16[8,8192]{1,0:T(8,128)(2,1)S(1)}, bf16[8,8192]{1,0:T(8,128)(2,1)S(1)}, u32[]{:S(2)}, u32[]{:S(2)}) collective-permute-start(bf16[8,8192]{1,0:T(8,128)(2,1)S(1)} %get-tuple-element.82), channel_id=1, source_target_pairs={{0,2},{2,0},{4,6},{6,4},{8,10},{10,8},{12,14},{14,12},{16,18},{18,... | collective-permute-start | bytes 393224 | tf_op jit(solution)/shard_map/ppermute | solution.py:193
  41.1 9.6 %collective-permute-start.20 = (bf16[8,8192]{1,0:T(8,128)(2,1)S(1)}, bf16[8,8192]{1,0:T(8,128)(2,1)S(1)}, u32[]{:S(2)}, u32[]{:S(2)}) collective-permute-start(bf16[8,8192]{1,0:T(8,128)(2,1)S(1)} %get-tuple-element.82), channel_id=1, source_target_pairs={{1,3},{3,1},{5,7},{7,5},{9,11},{11,9},{13,15},{15,13},{17,19},{19,... | collective-permute-start | bytes 393224 | tf_op jit(solution)/shard_map/ppermute | solution.py:193
  41.7 8.9 %collective-permute-start.18 = (bf16[8,8192]{1,0:T(8,128)(2,1)S(1)}, bf16[8,8192]{1,0:T(8,128)(2,1)S(1)}, u32[]{:S(2)}, u32[]{:S(2)}) collective-permute-start(bf16[8,8192]{1,0:T(8,128)(2,1)S(1)} %get-tuple-element.69), channel_id=1, source_target_pairs={{0,6},{2,4},{4,2},{6,0},{8,14},{10,12},{12,10},{14,8},{16,22},{18,... | collective-permute-start | bytes 393224 | tf_op jit(solution)/shard_map/ppermute | solution.py:193
  45.4 5.3 %collective-permute-start.21 = (bf16[8,8192]{1,0:T(8,128)(2,1)S(1)}, bf16[8,8192]{1,0:T(8,128)(2,1)S(1)}, u32[]{:S(2)}, u32[]{:S(2)}) collective-permute-start(bf16[8,8192]{1,0:T(8,128)(2,1)S(1)} %get-tuple-element.69), channel_id=1, source_target_pairs={{1,7},{3,5},{5,3},{7,1},{9,15},{11,13},{13,11},{15,9},{17,23},{19,... | collective-permute-start | bytes 393224 | tf_op jit(solution)/shard_map/ppermute | solution.py:193
  46.5 6.8 %collective-permute-start.22 = (bf16[8,8192]{1,0:T(8,128)(2,1)S(1)}, bf16[8,8192]{1,0:T(8,128)(2,1)S(1)}, u32[]{:S(2)}, u32[]{:S(2)}) collective-permute-start(bf16[8,8192]{1,0:T(8,128)(2,1)S(1)} %get-tuple-element.68), channel_id=1, source_target_pairs={{0,2},{2,0},{4,6},{6,4},{8,10},{10,8},{12,14},{14,12},{16,18},{18,... | collective-permute-start | bytes 393224 | tf_op jit(solution)/shard_map/ppermute | solution.py:193
  49.3 1.4 %collective-permute-start.19 = (bf16[8,8192]{1,0:T(8,128)(2,1)S(1)}, bf16[8,8192]{1,0:T(8,128)(2,1)S(1)}, u32[]{:S(2)}, u32[]{:S(2)}) collective-permute-start(bf16[8,8192]{1,0:T(8,128)(2,1)S(1)} %get-tuple-element.68), channel_id=1, source_target_pairs={{1,5},{3,7},{5,1},{7,3},{9,13},{11,15},{13,9},{15,11},{17,21},{19,... | collective-permute-start | bytes 393224 | tf_op jit(solution)/shard_map/ppermute | solution.py:193
  53.4 5.0 %collective-permute-start.23 = (bf16[8,8192]{1,0:T(8,128)(2,1)S(1)}, bf16[8,8192]{1,0:T(8,128)(2,1)S(1)}, u32[]{:S(2)}, u32[]{:S(2)}) collective-permute-start(bf16[8,8192]{1,0:T(8,128)(2,1)S(1)} %add_convert_fusion.2), channel_id=1, source_target_pairs={{0,2},{1,9},{2,0},{3,11},{4,6},{5,13},{6,4},{7,15},{8,10},{9,1},{1... | collective-permute-start | bytes 393224 | tf_op jit(solution)/shard_map/ppermute | solution.py:193
  54.3 8.1 %collective-permute-start.24 = (bf16[8,8192]{1,0:T(8,128)(2,1)S(1)}, bf16[8,8192]{1,0:T(8,128)(2,1)S(1)}, u32[]{:S(2)}, u32[]{:S(2)}) collective-permute-start(bf16[8,8192]{1,0:T(8,128)(2,1)S(1)} %fusion.2), channel_id=1, source_target_pairs={{0,8},{1,5},{2,10},{3,7},{4,12},{5,1},{6,14},{7,3},{8,0},{9,13},{1... | collective-permute-start | bytes 393224 | tf_op jit(solution)/shard_map/ppermute | solution.py:193
  57.5 5.9 %collective-permute-start.25 = (bf16[8,8192]{1,0:T(8,128)(2,1)S(1)}, bf16[8,8192]{1,0:T(8,128)(2,1)S(1)}, u32[]{:S(2)}, u32[]{:S(2)}) collective-permute-start(bf16[8,8192]{1,0:T(8,128)(2,1)S(1)} %get-tuple-element.79), channel_id=1, source_target_pairs={{0,4},{1,3},{2,6},{3,1},{4,0},{5,7},{6,2},{7,5},{8,12},{9,11},{10,... | collective-permute-start | bytes 393224 | tf_op jit(solution)/shard_map/ppermute | solution.py:193

commit v14 on v13

--- a/solution.py
+++ b/solution.py
@@ -189,25 +189,25 @@
         mask //= 2
 
     def swap(value, masks):
-        pairs = [(i, i ^ masks[i % 2]) for i in range(members) if masks[i % 2] is not None]
-        return lax.ppermute(value, "gx", pairs)
+        return lax.ppermute(value, "gx", [(i, i ^ masks[i % 2]) for i in range(members)])
 
     def narrow(value):
         return value.astype(jnp.bfloat16)
 
     def on_device(tokens, gate_weight, up_weight, down_weight, sign_pattern):
         features = tokens.shape[1]
+        even = lax.axis_index("gx") % 2 == 0
         own = tokens
         for masks in wide:
             own = jnp.concatenate([own, swap(own, masks)])
         rows = own.shape[0]
 
         one, two, three = swap(own, FIRST), swap(own, SECOND), swap(own, THIRD)
-        four, five, six = swap(one, (4, 2)), swap(one, (2, None)), swap(one, (6, None))
-        beside = swap(two, (2, None))
+        four, five, six = swap(one, (4, 2)), swap(one, (2, 0)), swap(one, (6, 0))
+        beside = swap(two, (2, 0))
         (gate_w,) = load((gate_weight.T,), (True,), one)
         gate_w, three, four, five, six, beside = lax.optimization_barrier((gate_w, three, four, five, six, beside))
-        seven, eight, nine = swap(three, (None, 4)), swap(three, (None, 2)), swap(three, (None, 6))
+        seven, eight, nine = swap(three, (0, 4)), swap(three, (0, 2)), swap(three, (0, 6))
         up_w, down_w = load((up_weight.T, down_weight), (True, False), three)
         up_w, beside, seven, eight, nine = lax.optimization_barrier((up_w, beside, seven, eight, nine))
         early = jnp.concatenate([own, one, two, three])
@@ -216,7 +216,8 @@
         width = features // SPANS
         for k in range(SPANS):
             here = slice(k * width, (k + 1) * width)
-            pieces = [five[:, here] + eight[:, here], six[:, here] + nine[:, here], beside[:, here] + seven[:, here]]
+            pairs = ((five, eight), (six, nine), (beside, seven))
+            pieces = [jnp.where(even, a[:, here], b[:, here]) for a, b in pairs]
             span = jnp.concatenate([four[:, here]] + pieces)
             spans.append((span, swap(span, (1, 1))))
         hidden = hidden_units(gate_w, up_w, (early, early_there), spans)
@@ -227,22 +228,22 @@
         rest = narrow(rest + rest_there.astype(jnp.float32))
         both, diagonal, seven = (rest[k * rows : (k + 1) * rows] for k in range(3))
         near_there = swap(sends[0], (1, 1))
-        a, b, c, g = swap(last, (4, 2)), swap(both, (2, None)), swap(diagonal, (6, None)), swap(seven, (2, None))
-        e = swap(both, (None, 2))
+        a, b, c, g = swap(last, (4, 2)), swap(both, (2, 0)), swap(diagonal, (6, 0)), swap(seven, (2, 0))
+        e = swap(both, (0, 2))
         a, diagonal = lax.optimization_barrier((a, diagonal))
-        f = swap(diagonal, (None, 6))
+        f = swap(diagonal, (0, 6))
         b, seven = lax.optimization_barrier((b, seven))
-        d = swap(seven, (None, 4))
+        d = swap(seven, (0, 4))
         near = near + near_there.astype(jnp.float32)
         one = near[rows : 2 * rows]
-        for piece in (a, b, c):
-            one = one + piece.astype(jnp.float32)
+        one = one + a.astype(jnp.float32)
+        one = one + jnp.where(even, b.astype(jnp.float32) + c.astype(jnp.float32), 0.0)
         one, near = lax.optimization_barrier((narrow(one), near))
         own, _, two, three = (near[k * rows : (k + 1) * rows] for k in range(4))
-        for piece in (d, e, f):
-            three = three + piece.astype(jnp.float32)
+        there = d.astype(jnp.float32) + e.astype(jnp.float32) + f.astype(jnp.float32)
+        three = three + jnp.where(even, 0.0, there)
         three, g = lax.optimization_barrier((narrow(three), g))
-        two = narrow(two + g.astype(jnp.float32))
+        two = narrow(two + jnp.where(even, g.astype(jnp.float32), 0.0))
         arrived = [swap(one, FIRST), swap(two, SECOND), swap(three, THIRD)]
         for k in (2, 0):
             own, arrived[k] = lax.optimization_barrier((own, arrived[k]))
@@ -255,7 +256,7 @@
             own = own[:half] + swap(narrow(own[half:]), masks).astype(jnp.float32)
         return rotate(own, arrived, sign_pattern)
 
-    placed = (P(("groups", "gx"), None), P(None, "gx"), P(None, "gx"), P("gx", None), P())
+    placed = (P(("groups", "gx"), 0), P(0, "gx"), P(0, "gx"), P("gx", 0), P())
     return jax.shard_map(
-        on_device, mesh=mesh, in_specs=placed, out_specs=P(("groups", "gx"), None), check_vma=False
+        on_device, mesh=mesh, in_specs=placed, out_specs=P(("groups", "gx"), 0), check_vma=False
     )

time: 64.7 us -> 64.7 us (level)
  no operation moved by 1% of the time
where the time goes in v14:
time: 64.7 us; the launch traced here: 64.3 us
  starting transfers between devices  41.8 us (65%)
  waiting for transfers between devices  11.5 us (18%)
  Pallas kernels  8.99 us (14%)
  local copies, waits for them, and re-layouts  1.02 us (2%)
    ppermute x26, starting transfers between devices, swap(): lax.ppermute(value, 'gx', [(i, i ^ masks[i % 2]) for i in range(members)])  41.8 us
    ppermute x26, waiting for transfers between devices, swap(): lax.ppermute(value, 'gx', [(i, i ^ masks[i % 2]) for i in range(members)])  11.5 us
    pallas_call x2, Pallas kernels, load(): pl.pallas_call(functools.partial(load_kernel, turned), out_shape=[jax.Sha...  5.95 us
    pallas_call x2, Pallas kernels, hidden_units(): pl.pallas_call(functools.partial(hidden_kernel, start, last), out_shape=(...  1.44 us
  transfers between devices with their start and end apart: 26, of which 8 were waited for; matrix products, arithmetic and copies ran while one was open for 2% of the time, Pallas kernels for 10%

profile of v14, /device:TPU:0, one launch (start us, length us, event | category | flops | bytes accessed | tf_op | source)
XLA Modules:
  0.0 64.3 jit_solution(3755114020036657970)
XLA Ops:
  0.0 4.0 %collective-permute-start = (bf16[8,8192]{1,0:T(8,128)(2,1)}, bf16[8,8192]{1,0:T(8,128)(2,1)S(1)}, u32[]{:S(2)}, u32[]{:S(2)}) collective-permute-start(bf16[8,8192]{1,0:T(8,128)(2,1)} %param.5), channel_id=1, source_target_pairs={{0,8},{1,5},{2,10},{3,7},{4,12},{5,1},{6,14},{7,3},{8,0},{9,13},{1... | collective-permute-start | bytes 393224 | tf_op jit(solution)/shard_map/ppermute | solution.py:192
  4.0 1.6 %collective-permute-start.5 = (bf16[8,8192]{1,0:T(8,128)(2,1)}, bf16[8,8192]{1,0:T(8,128)(2,1)S(1)}, u32[]{:S(2)}, u32[]{:S(2)}) collective-permute-start(bf16[8,8192]{1,0:T(8,128)(2,1)} %param.5), channel_id=1, source_target_pairs={{0,4},{1,3},{2,6},{3,1},{4,0},{5,7},{6,2},{7,5},{8,12},{9,11},{10,... | collective-permute-start | bytes 393224 | tf_op jit(solution)/shard_map/ppermute | solution.py:192
  5.6 1.5 %collective-permute-start.1 = (bf16[8,8192]{1,0:T(8,128)(2,1)}, bf16[8,8192]{1,0:T(8,128)(2,1)S(1)}, u32[]{:S(2)}, u32[]{:S(2)}) collective-permute-start(bf16[8,8192]{1,0:T(8,128)(2,1)} %param.5), channel_id=1, source_target_pairs={{0,2},{1,9},{2,0},{3,11},{4,6},{5,13},{6,4},{7,15},{8,10},{9,1},{1... | collective-permute-start | bytes 393224 | tf_op jit(solution)/shard_map/ppermute | solution.py:192
  7.1 0.9 %constant_dynamic-update-slice_fusion.3 = bf16[32,8192]{1,0:T(8,128)(2,1)S(1)} fusion(bf16[8,8192]{1,0:T(8,128)(2,1)} %param.5), kind=kLoop, calls=%fused_computation.29 | loop fusion | bytes 262144
  8.1 0.0 collective-permute-done.refs_1_
  8.1 4.4 %collective-permute-start.2 = (bf16[8,8192]{1,0:T(8,128)(2,1)S(1)}, bf16[8,8192]{1,0:T(8,128)(2,1)S(1)}, u32[]{:S(2)}, u32[]{:S(2)}) collective-permute-start(bf16[8,8192]{1,0:T(8,128)(2,1)S(1)} %collective-permute-done.refs_1_), channel_id=1, source_target_pairs={{0,4},{1,3},{2,6},{3,1},{4,0},{5,7},{6,2},{7,5},{8,12},{9,11},{10,... | collective-permute-start | bytes 393224 | tf_op jit(solution)/shard_map/ppermute | solution.py:192
  12.5 2.8 %collective-permute-start.3 = (bf16[8,8192]{1,0:T(8,128)(2,1)S(1)}, bf16[8,8192]{1,0:T(8,128)(2,1)S(1)}, u32[]{:S(2)}, u32[]{:S(2)}) collective-permute-start(bf16[8,8192]{1,0:T(8,128)(2,1)S(1)} %collective-permute-done.refs_1_), channel_id=1, source_target_pairs={{0,2},{1,1},{2,0},{3,3},{4,6},{5,5},{6,4},{7,7},{8,10},{9,9},{10,8... | collective-permute-start | bytes 393224 | tf_op jit(solution)/shard_map/ppermute | solution.py:192
  15.3 2.9 %collective-permute-start.4 = (bf16[8,8192]{1,0:T(8,128)(2,1)S(1)}, bf16[8,8192]{1,0:T(8,128)(2,1)S(1)}, u32[]{:S(2)}, u32[]{:S(2)}) collective-permute-start(bf16[8,8192]{1,0:T(8,128)(2,1)S(1)} %collective-permute-done.refs_1_), channel_id=1, source_target_pairs={{0,6},{1,1},{2,4},{3,3},{4,2},{5,5},{6,0},{7,7},{8,14},{9,9},{10,1... | collective-permute-start | bytes 393224 | tf_op jit(solution)/shard_map/ppermute | solution.py:192
  18.2 0.0 collective-permute-done.5
  18.2 3.9 %collective-permute-start.6 = (bf16[8,8192]{1,0:T(8,128)(2,1)S(1)}, bf16[8,8192]{1,0:T(8,128)(2,1)S(1)}, u32[]{:S(2)}, u32[]{:S(2)}) collective-permute-start(bf16[8,8192]{1,0:T(8,128)(2,1)S(1)} %collective-permute-done.5), channel_id=1, source_target_pairs={{0,2},{1,1},{2,0},{3,3},{4,6},{5,5},{6,4},{7,7},{8,10},{9,9},{10,8... | collective-permute-start | bytes 393224 | tf_op jit(solution)/shard_map/ppermute | solution.py:192
  22.2 2.7 %shard_map.55.refs_0_ = bf16[8192,224]{1,0:T(8,128)(2,1)S(1)} custom-call(bf16[224,8192]{1,0:T(8,128)(2,1)} %bitcast.5, bf16[8,8192]{1,0:T(8,128)(2,1)S(1)} %collective-permute-done.refs_1_), custom_call_target="tpu_custom_call" | custom-call | bytes 7340032 | tf_op jit(solution)/shard_map/pallas_call | solution.py:54
  24.9 0.0 collective-permute-done.1.refs_2_
  24.9 0.0 collective-permute-done.2
  24.9 0.0 collective-permute-done.3
  24.9 0.0 collective-permute-done.4
  24.9 0.9 %collective-permute-done.6 = bf16[8,8192]{1,0:T(8,128)(2,1)S(1)} collective-permute-done((bf16[8,8192]{1,0:T(8,128)(2,1)S(1)}, bf16[8,8192]{1,0:T(8,128)(2,1)S(1)}, u32[]{:S(2)}, u32[]{:S(2)}) %collective-permute-start.6) | collective-permute-done | bytes 131104 | tf_op jit(solution)/shard_map/ppermute | solution.py:192
  25.9 0.7 %collective-permute-start.7 = (bf16[8,8192]{1,0:T(8,128)(2,1)S(1)}, bf16[8,8192]{1,0:T(8,128)(2,1)S(1)}, u32[]{:S(2)}, u32[]{:S(2)}) collective-permute-start(bf16[8,8192]{1,0:T(8,128)(2,1)S(1)} %collective-permute-done.1.refs_2_), channel_id=1, source_target_pairs={{0,0},{1,5},{2,2},{3,7},{4,4},{5,1},{6,6},{7,3},{8,8},{9,13},{10,1... | collective-permute-start | bytes 393224 | tf_op jit(solution)/shard_map/ppermute | solution.py:192
  26.6 0.7 %collective-permute-start.8 = (bf16[8,8192]{1,0:T(8,128)(2,1)S(1)}, bf16[8,8192]{1,0:T(8,128)(2,1)S(1)}, u32[]{:S(2)}, u32[]{:S(2)}) collective-permute-start(bf16[8,8192]{1,0:T(8,128)(2,1)S(1)} %collective-permute-done.1.refs_2_), channel_id=1, source_target_pairs={{0,0},{1,3},{2,2},{3,1},{4,4},{5,7},{6,6},{7,5},{8,8},{9,11},{10,1... | collective-permute-start | bytes 393224 | tf_op jit(solution)/shard_map/ppermute | solution.py:192
  27.2 0.7 %collective-permute-start.9 = (bf16[8,8192]{1,0:T(8,128)(2,1)S(1)}, bf16[8,8192]{1,0:T(8,128)(2,1)S(1)}, u32[]{:S(2)}, u32[]{:S(2)}) collective-permute-start(bf16[8,8192]{1,0:T(8,128)(2,1)S(1)} %collective-permute-done.1.refs_2_), channel_id=1, source_target_pairs={{0,0},{1,7},{2,2},{3,5},{4,4},{5,3},{6,6},{7,1},{8,8},{9,15},{10,1... | collective-permute-start | bytes 393224 | tf_op jit(solution)/shard_map/ppermute | solution.py:192
  27.9 0.1 collective-permute-start.10
  28.0 3.3 %shard_map.56 = (bf16[8192,224]{1,0:T(8,128)(2,1)S(1)}, bf16[224,8192]{1,0:T(8,128)(2,1)S(1)}) custom-call(bf16[224,8192]{1,0:T(8,128)(2,1)} %bitcast.4, bf16[224,8192]{1,0:T(8,128)(2,1)} %refs_1_.1, bf16[8,8192]{1,0:T(8,128)(2,1)S(1)} %collective-permute-done.1.refs_2_), custom_call_target="tpu_custom_call" | custom-call | bytes 14680064 | tf_op jit(solution)/shard_map/pallas_call | solution.py:54
  31.3 0.0 collective-permute-done.7
  31.3 0.0 collective-permute-done.8
  31.3 0.0 collective-permute-done.9
  31.4 0.6 collective-permute-start.12
  32.0 0.1 collective-permute-start.11
  32.1 1.1 %collective-permute-done.12.refs_5_ = bf16[32,4096]{1,0:T(8,128)(2,1)S(1)} collective-permute-done((bf16[32,4096]{1,0:T(8,128)(2,1)S(1)}, bf16[32,4096]{1,0:T(8,128)(2,1)S(1)}, u32[]{:S(2)}, u32[]{:S(2)}) %collective-permute-start.12) | collective-permute-done | bytes 262176 | tf_op jit(solution)/shard_map/ppermute | solution.py:192
  33.1 0.0 collective-permute-done.10.refs_3_
  33.2 0.7 %shard_map.57 = (f32[128,224]{1,0:T(8,128)S(1)}, f32[128,224]{1,0:T(8,128)S(1)}) custom-call(bf16[8192,224]{1,0:T(8,128)(2,1)S(1)} %shard_map.55.refs_0_, bf16[8192,224]{1,0:T(8,128)(2,1)S(1)} %get-tuple-element.46.refs_1_, bf16[32,8192]{1,0:T(8,128)(2,1)S(1)} %constant_dynamic-update-slice_fusion.refs_2_, ...), custom_call_target="tpu_custom_call" | custom-call | flops 469762048 | bytes 3670016 | tf_op jit(solution)/shard_map/pallas_call | solution.py:93
  33.9 0.0 collective-permute-done.11.refs_5_
  33.9 0.7 %shard_map.58.hidden_ref = bf16[128,224]{1,0:T(8,128)(2,1)S(1)} custom-call(bf16[8192,224]{1,0:T(8,128)(2,1)S(1)} %shard_map.55.refs_0_, bf16[8192,224]{1,0:T(8,128)(2,1)S(1)} %get-tuple-element.46.refs_1_, bf16[32,8192]{1,0:T(8,128)(2,1)S(1)} %constant_dynamic-update-slice_fusion.refs_2_, bf16[32,8192]{1,0:T(8,128)(2,1)S(1)} %collective-permute-done.10.refs_3_, ...), custom_call_target="tpu_custom_call" | custom-call | flops 469762048 | bytes 3670016 | tf_op jit(solution)/shard_map/pallas_call | solution.py:93
  34.6 0.7 %shard_map.59 = (f32[32,8192]{1,0:T(8,128)S(1)}, f32[8,8192]{1,0:T(8,128)S(1)}, f32[24,8192]{1,0:T(8,128)S(1)}, bf16[32,8192]{1,0:T(8,128)(2,1)S(1)}, bf16[8,819...) custom-call(bf16[128,224]{1,0:T(8,128)(2,1)S(1)} %shard_map.58.hidden_ref, bf16[224,8192]{1,0:T(8,128)(2,1)S(1)} %get-tuple-element.56.down_ref), custom_call_target="tpu_custom_call" | custom-call | flops 469762048 | bytes 3670016 | tf_op jit(solution)/shard_map/pallas_call | solution.py:121
  35.3 0.4 collective-permute-start.15
  35.8 0.1 collective-permute-start.13
  35.9 0.9 %collective-permute-done.15 = bf16[8,8192]{1,0:T(8,128)(2,1)S(1)} collective-permute-done((bf16[8,8192]{1,0:T(8,128)(2,1)S(1)}, bf16[8,8192]{1,0:T(8,128)(2,1)S(1)}, u32[]{:S(2)}, u32[]{:S(2)}) %collective-permute-start.15) | collective-permute-done | bytes 131104 | tf_op jit(solution)/shard_map/ppermute | solution.py:192
  36.8 1.6 %collective-permute-start.16 = (bf16[8,8192]{1,0:T(8,128)(2,1)S(1)}, bf16[8,8192]{1,0:T(8,128)(2,1)S(1)}, u32[]{:S(2)}, u32[]{:S(2)}) collective-permute-start(bf16[8,8192]{1,0:T(8,128)(2,1)S(1)} %add_convert_fusion.3), channel_id=1, source_target_pairs={{0,4},{1,3},{2,6},{3,1},{4,0},{5,7},{6,2},{7,5},{8,12},{9,11},{10,... | collective-permute-start | bytes 393224 | tf_op jit(solution)/shard_map/ppermute | solution.py:192
  38.4 0.0 collective-permute-done.13
  38.4 0.0 collective-permute-start.14
  38.4 0.1 add_convert_fusion
  38.5 0.0 copy-start
  38.5 2.5 %collective-permute-start.17 = (bf16[8,8192]{1,0:T(8,128)(2,1)S(1)}, bf16[8,8192]{1,0:T(8,128)(2,1)S(1)}, u32[]{:S(2)}, u32[]{:S(2)}) collective-permute-start(bf16[8,8192]{1,0:T(8,128)(2,1)S(1)} %get-tuple-element.82), channel_id=1, source_target_pairs={{0,2},{1,1},{2,0},{3,3},{4,6},{5,5},{6,4},{7,7},{8,10},{9,9},{10,8... | collective-permute-start | bytes 393224 | tf_op jit(solution)/shard_map/ppermute | solution.py:192
  41.1 0.7 %collective-permute-start.20 = (bf16[8,8192]{1,0:T(8,128)(2,1)S(1)}, bf16[8,8192]{1,0:T(8,128)(2,1)S(1)}, u32[]{:S(2)}, u32[]{:S(2)}) collective-permute-start(bf16[8,8192]{1,0:T(8,128)(2,1)S(1)} %get-tuple-element.82), channel_id=1, source_target_pairs={{0,0},{1,3},{2,2},{3,1},{4,4},{5,7},{6,6},{7,5},{8,8},{9,11},{10,1... | collective-permute-start | bytes 393224 | tf_op jit(solution)/shard_map/ppermute | solution.py:192
  41.7 3.6 %collective-permute-start.18 = (bf16[8,8192]{1,0:T(8,128)(2,1)S(1)}, bf16[8,8192]{1,0:T(8,128)(2,1)S(1)}, u32[]{:S(2)}, u32[]{:S(2)}) collective-permute-start(bf16[8,8192]{1,0:T(8,128)(2,1)S(1)} %get-tuple-element.69), channel_id=1, source_target_pairs={{0,6},{1,1},{2,4},{3,3},{4,2},{5,5},{6,0},{7,7},{8,14},{9,9},{10,1... | collective-permute-start | bytes 393224 | tf_op jit(solution)/shard_map/ppermute | solution.py:192
  45.4 0.0 collective-permute-done.16
  45.4 0.7 %collective-permute-start.21 = (bf16[8,8192]{1,0:T(8,128)(2,1)S(1)}, bf16[8,8192]{1,0:T(8,128)(2,1)S(1)}, u32[]{:S(2)}, u32[]{:S(2)}) collective-permute-start(bf16[8,8192]{1,0:T(8,128)(2,1)S(1)} %get-tuple-element.69), channel_id=1, source_target_pairs={{0,0},{1,7},{2,2},{3,5},{4,4},{5,3},{6,6},{7,1},{8,8},{9,15},{10,1... | collective-permute-start | bytes 393224 | tf_op jit(solution)/shard_map/ppermute | solution.py:192
  46.1 0.5 collective-permute-done.17
  46.5 2.7 %collective-permute-start.22 = (bf16[8,8192]{1,0:T(8,128)(2,1)S(1)}, bf16[8,8192]{1,0:T(8,128)(2,1)S(1)}, u32[]{:S(2)}, u32[]{:S(2)}) collective-permute-start(bf16[8,8192]{1,0:T(8,128)(2,1)S(1)} %get-tuple-element.68), channel_id=1, source_target_pairs={{0,2},{1,1},{2,0},{3,3},{4,6},{5,5},{6,4},{7,7},{8,10},{9,9},{10,8... | collective-permute-start | bytes 393224 | tf_op jit(solution)/shard_map/ppermute | solution.py:192
  49.3 0.0 collective-permute-done.14
  49.3 0.7 %collective-permute-start.19 = (bf16[8,8192]{1,0:T(8,128)(2,1)S(1)}, bf16[8,8192]{1,0:T(8,128)(2,1)S(1)}, u32[]{:S(2)}, u32[]{:S(2)}) collective-permute-start(bf16[8,8192]{1,0:T(8,128)(2,1)S(1)} %get-tuple-element.68), channel_id=1, source_target_pairs={{0,0},{1,5},{2,2},{3,7},{4,4},{5,1},{6,6},{7,3},{8,8},{9,13},{10,1... | collective-permute-start | bytes 393224 | tf_op jit(solution)/shard_map/ppermute | solution.py:192
  50.0 0.1 convert_add_fusion
  50.1 0.5 collective-permute-done.18
  50.6 0.1 fusion.1
  50.7 0.0 collective-permute-done.21
  50.7 0.0 collective-permute-done.20
  50.7 0.0 collective-permute-done.19
  50.7 0.1 add_convert_fusion.2
  50.8 2.6 %collective-permute-done.22 = bf16[8,8192]{1,0:T(8,128)(2,1)S(1)} collective-permute-done((bf16[8,8192]{1,0:T(8,128)(2,1)S(1)}, bf16[8,8192]{1,0:T(8,128)(2,1)S(1)}, u32[]{:S(2)}, u32[]{:S(2)}) %collective-permute-start.22) | collective-permute-done | bytes 131104 | tf_op jit(solution)/shard_map/ppermute | solution.py:192
  53.4 0.8 %collective-permute-start.23 = (bf16[8,8192]{1,0:T(8,128)(2,1)S(1)}, bf16[8,8192]{1,0:T(8,128)(2,1)S(1)}, u32[]{:S(2)}, u32[]{:S(2)}) collective-permute-start(bf16[8,8192]{1,0:T(8,128)(2,1)S(1)} %add_convert_fusion.2), channel_id=1, source_target_pairs={{0,2},{1,9},{2,0},{3,11},{4,6},{5,13},{6,4},{7,15},{8,10},{9,1},{1... | collective-permute-start | bytes 393224 | tf_op jit(solution)/shard_map/ppermute | solution.py:192
  54.3 3.2 %collective-permute-start.24 = (bf16[8,8192]{1,0:T(8,128)(2,1)S(1)}, bf16[8,8192]{1,0:T(8,128)(2,1)S(1)}, u32[]{:S(2)}, u32[]{:S(2)}) collective-permute-start(bf16[8,8192]{1,0:T(8,128)(2,1)S(1)} %fusion.1), channel_id=1, source_target_pairs={{0,8},{1,5},{2,10},{3,7},{4,12},{5,1},{6,14},{7,3},{8,0},{9,13},{1... | collective-permute-start | bytes 393224 | tf_op jit(solution)/shard_map/ppermute | solution.py:192
  57.5 0.8 %collective-permute-start.25 = (bf16[8,8192]{1,0:T(8,128)(2,1)S(1)}, bf16[8,8192]{1,0:T(8,128)(2,1)S(1)}, u32[]{:S(2)}, u32[]{:S(2)}) collective-permute-start(bf16[8,8192]{1,0:T(8,128)(2,1)S(1)} %get-tuple-element.79), channel_id=1, source_target_pairs={{0,4},{1,3},{2,6},{3,1},{4,0},{5,7},{6,2},{7,5},{8,12},{9,11},{10,... | collective-permute-start | bytes 393224 | tf_op jit(solution)/shard_map/ppermute | solution.py:192
  58.4 0.0 collective-permute-done.23
  58.4 4.0 %collective-permute-done.24 = bf16[8,8192]{1,0:T(8,128)(2,1)S(1)} collective-permute-done((bf16[8,8192]{1,0:T(8,128)(2,1)S(1)}, bf16[8,8192]{1,0:T(8,128)(2,1)S(1)}, u32[]{:S(2)}, u32[]{:S(2)}) %collective-permute-start.24) | collective-permute-done | bytes 131104 | tf_op jit(solution)/shard_map/ppermute | solution.py:192
  62.5 1.0 %collective-permute-done.25.refs_1_ = bf16[8,8192]{1,0:T(8,128)(2,1)S(1)} collective-permute-done((bf16[8,8192]{1,0:T(8,128)(2,1)S(1)}, bf16[8,8192]{1,0:T(8,128)(2,1)S(1)}, u32[]{:S(2)}, u32[]{:S(2)}) %collective-permute-start.25) | collective-permute-done | bytes 131104 | tf_op jit(solution)/shard_map/ppermute | solution.py:192
  63.4 0.9 %shard_map.60 = bf16[8,8192]{1,0:T(8,128)(2,1)} custom-call(f32[8,8192]{1,0:T(8,128)S(1)} %convert_add_fusion.1.refs_0_, bf16[8,8192]{1,0:T(8,128)(2,1)S(1)} %collective-permute-done.25.refs_1_, s32[1,8192]{1,0:T(1,128)S(1)} %bitcast.3, bf16[256,128]{1,0:T(8,128)(2,1)S(1)} %pad_maximum_fusion.2.refs_3_), custom_call_target="tpu_custom_call" | custom-call | tf_op jit(solution)/shard_map/pallas_call | solution.py:171
  (16 shorter events, 0.3 us)
Async XLA Ops:
  0.0 8.1 %collective-permute-start = (bf16[8,8192]{1,0:T(8,128)(2,1)}, bf16[8,8192]{1,0:T(8,128)(2,1)S(1)}, u32[]{:S(2)}, u32[]{:S(2)}) collective-permute-start(bf16[8,8192]{1,0:T(8,128)(2,1)} %param.5), channel_id=1, source_target_pairs={{0,8},{1,5},{2,10},{3,7},{4,12},{5,1},{6,14},{7,3},{8,0},{9,13},{1... | collective-permute-start | bytes 393224 | tf_op jit(solution)/shard_map/ppermute | solution.py:192
  4.0 14.2 %collective-permute-start.5 = (bf16[8,8192]{1,0:T(8,128)(2,1)}, bf16[8,8192]{1,0:T(8,128)(2,1)S(1)}, u32[]{:S(2)}, u32[]{:S(2)}) collective-permute-start(bf16[8,8192]{1,0:T(8,128)(2,1)} %param.5), channel_id=1, source_target_pairs={{0,4},{1,3},{2,6},{3,1},{4,0},{5,7},{6,2},{7,5},{8,12},{9,11},{10,... | collective-permute-start | bytes 393224 | tf_op jit(solution)/shard_map/ppermute | solution.py:192
  5.6 19.3 %collective-permute-start.1 = (bf16[8,8192]{1,0:T(8,128)(2,1)}, bf16[8,8192]{1,0:T(8,128)(2,1)S(1)}, u32[]{:S(2)}, u32[]{:S(2)}) collective-permute-start(bf16[8,8192]{1,0:T(8,128)(2,1)} %param.5), channel_id=1, source_target_pairs={{0,2},{1,9},{2,0},{3,11},{4,6},{5,13},{6,4},{7,15},{8,10},{9,1},{1... | collective-permute-start | bytes 393224 | tf_op jit(solution)/shard_map/ppermute | solution.py:192
  8.1 16.8 %collective-permute-start.2 = (bf16[8,8192]{1,0:T(8,128)(2,1)S(1)}, bf16[8,8192]{1,0:T(8,128)(2,1)S(1)}, u32[]{:S(2)}, u32[]{:S(2)}) collective-permute-start(bf16[8,8192]{1,0:T(8,128)(2,1)S(1)} %collective-permute-done.refs_1_), channel_id=1, source_target_pairs={{0,4},{1,3},{2,6},{3,1},{4,0},{5,7},{6,2},{7,5},{8,12},{9,11},{10,... | collective-permute-start | bytes 393224 | tf_op jit(solution)/shard_map/ppermute | solution.py:192
  12.5 12.4 %collective-permute-start.3 = (bf16[8,8192]{1,0:T(8,128)(2,1)S(1)}, bf16[8,8192]{1,0:T(8,128)(2,1)S(1)}, u32[]{:S(2)}, u32[]{:S(2)}) collective-permute-start(bf16[8,8192]{1,0:T(8,128)(2,1)S(1)} %collective-permute-done.refs_1_), channel_id=1, source_target_pairs={{0,2},{1,1},{2,0},{3,3},{4,6},{5,5},{6,4},{7,7},{8,10},{9,9},{10,8... | collective-permute-start | bytes 393224 | tf_op jit(solution)/shard_map/ppermute | solution.py:192
  15.3 9.6 %collective-permute-start.4 = (bf16[8,8192]{1,0:T(8,128)(2,1)S(1)}, bf16[8,8192]{1,0:T(8,128)(2,1)S(1)}, u32[]{:S(2)}, u32[]{:S(2)}) collective-permute-start(bf16[8,8192]{1,0:T(8,128)(2,1)S(1)} %collective-permute-done.refs_1_), channel_id=1, source_target_pairs={{0,6},{1,1},{2,4},{3,3},{4,2},{5,5},{6,0},{7,7},{8,14},{9,9},{10,1... | collective-permute-start | bytes 393224 | tf_op jit(solution)/shard_map/ppermute | solution.py:192
  18.2 7.6 %collective-permute-start.6 = (bf16[8,8192]{1,0:T(8,128)(2,1)S(1)}, bf16[8,8192]{1,0:T(8,128)(2,1)S(1)}, u32[]{:S(2)}, u32[]{:S(2)}) collective-permute-start(bf16[8,8192]{1,0:T(8,128)(2,1)S(1)} %collective-permute-done.5), channel_id=1, source_target_pairs={{0,2},{1,1},{2,0},{3,3},{4,6},{5,5},{6,4},{7,7},{8,10},{9,9},{10,8... | collective-permute-start | bytes 393224 | tf_op jit(solution)/shard_map/ppermute | solution.py:192
  25.9 5.4 %collective-permute-start.7 = (bf16[8,8192]{1,0:T(8,128)(2,1)S(1)}, bf16[8,8192]{1,0:T(8,128)(2,1)S(1)}, u32[]{:S(2)}, u32[]{:S(2)}) collective-permute-start(bf16[8,8192]{1,0:T(8,128)(2,1)S(1)} %collective-permute-done.1.refs_2_), channel_id=1, source_target_pairs={{0,0},{1,5},{2,2},{3,7},{4,4},{5,1},{6,6},{7,3},{8,8},{9,13},{10,1... | collective-permute-start | bytes 393224 | tf_op jit(solution)/shard_map/ppermute | solution.py:192
  26.6 4.8 %collective-permute-start.8 = (bf16[8,8192]{1,0:T(8,128)(2,1)S(1)}, bf16[8,8192]{1,0:T(8,128)(2,1)S(1)}, u32[]{:S(2)}, u32[]{:S(2)}) collective-permute-start(bf16[8,8192]{1,0:T(8,128)(2,1)S(1)} %collective-permute-done.1.refs_2_), channel_id=1, source_target_pairs={{0,0},{1,3},{2,2},{3,1},{4,4},{5,7},{6,6},{7,5},{8,8},{9,11},{10,1... | collective-permute-start | bytes 393224 | tf_op jit(solution)/shard_map/ppermute | solution.py:192
  27.2 4.1 %collective-permute-start.9 = (bf16[8,8192]{1,0:T(8,128)(2,1)S(1)}, bf16[8,8192]{1,0:T(8,128)(2,1)S(1)}, u32[]{:S(2)}, u32[]{:S(2)}) collective-permute-start(bf16[8,8192]{1,0:T(8,128)(2,1)S(1)} %collective-permute-done.1.refs_2_), channel_id=1, source_target_pairs={{0,0},{1,7},{2,2},{3,5},{4,4},{5,3},{6,6},{7,1},{8,8},{9,15},{10,1... | collective-permute-start | bytes 393224 | tf_op jit(solution)/shard_map/ppermute | solution.py:192
  27.9 5.2 %collective-permute-start.10 = (bf16[32,8192]{1,0:T(8,128)(2,1)S(1)}, bf16[32,8192]{1,0:T(8,128)(2,1)S(1)}, u32[]{:S(2)}, u32[]{:S(2)}) collective-permute-start(bf16[32,8192]{1,0:T(8,128)(2,1)S(1)} %constant_dynamic-update-slice_fusion.refs_2_), channel_id=1, source_target_pairs={{0,1},{1,0},{2,3},{3,2},{4,5},{5,4},{6,7},{7,6},{8,9},{9,8},{10,11... | collective-permute-start | bytes 1572872 | tf_op jit(solution)/shard_map/ppermute | solution.py:192
  31.4 1.7 %collective-permute-start.12 = (bf16[32,4096]{1,0:T(8,128)(2,1)S(1)}, bf16[32,4096]{1,0:T(8,128)(2,1)S(1)}, u32[]{:S(2)}, u32[]{:S(2)}) collective-permute-start(bf16[32,4096]{1,0:T(8,128)(2,1)S(1)} %pad_maximum_fusion.1.refs_4_), channel_id=1, source_target_pairs={{0,1},{1,0},{2,3},{3,2},{4,5},{5,4},{6,7},{7,6},{8,9},{9,8},{10,11... | collective-permute-start | bytes 786440 | tf_op jit(solution)/shard_map/ppermute | solution.py:192
  32.0 1.9 %collective-permute-start.11 = (bf16[32,4096]{1,0:T(8,128)(2,1)S(1)}, bf16[32,4096]{1,0:T(8,128)(2,1)S(1)}, u32[]{:S(2)}, u32[]{:S(2)}) collective-permute-start(bf16[32,4096]{1,0:T(8,128)(2,1)S(1)} %pad_maximum_fusion.refs_4_), channel_id=1, source_target_pairs={{0,1},{1,0},{2,3},{3,2},{4,5},{5,4},{6,7},{7,6},{8,9},{9,8},{10,11... | collective-permute-start | bytes 786440 | tf_op jit(solution)/shard_map/ppermute | solution.py:192
  35.3 1.4 %collective-permute-start.15 = (bf16[8,8192]{1,0:T(8,128)(2,1)S(1)}, bf16[8,8192]{1,0:T(8,128)(2,1)S(1)}, u32[]{:S(2)}, u32[]{:S(2)}) collective-permute-start(bf16[8,8192]{1,0:T(8,128)(2,1)S(1)} %get-tuple-element.62), channel_id=1, source_target_pairs={{0,1},{1,0},{2,3},{3,2},{4,5},{5,4},{6,7},{7,6},{8,9},{9,8},{10,11... | collective-permute-start | bytes 393224 | tf_op jit(solution)/shard_map/ppermute | solution.py:192
  35.8 2.6 %collective-permute-start.13 = (bf16[24,8192]{1,0:T(8,128)(2,1)S(1)}, bf16[24,8192]{1,0:T(8,128)(2,1)S(1)}, u32[]{:S(2)}, u32[]{:S(2)}) collective-permute-start(bf16[24,8192]{1,0:T(8,128)(2,1)S(1)} %get-tuple-element.58), channel_id=1, source_target_pairs={{0,1},{1,0},{2,3},{3,2},{4,5},{5,4},{6,7},{7,6},{8,9},{9,8},{10,11... | collective-permute-start | bytes 1179656 | tf_op jit(solution)/shard_map/ppermute | solution.py:192
  36.8 8.6 %collective-permute-start.16 = (bf16[8,8192]{1,0:T(8,128)(2,1)S(1)}, bf16[8,8192]{1,0:T(8,128)(2,1)S(1)}, u32[]{:S(2)}, u32[]{:S(2)}) collective-permute-start(bf16[8,8192]{1,0:T(8,128)(2,1)S(1)} %add_convert_fusion.3), channel_id=1, source_target_pairs={{0,4},{1,3},{2,6},{3,1},{4,0},{5,7},{6,2},{7,5},{8,12},{9,11},{10,... | collective-permute-start | bytes 393224 | tf_op jit(solution)/shard_map/ppermute | solution.py:192
  38.4 10.9 %collective-permute-start.14 = (bf16[32,8192]{1,0:T(8,128)(2,1)S(1)}, bf16[32,8192]{1,0:T(8,128)(2,1)S(1)}, u32[]{:S(2)}, u32[]{:S(2)}) collective-permute-start(bf16[32,8192]{1,0:T(8,128)(2,1)S(1)} %get-tuple-element.60), channel_id=1, source_target_pairs={{0,1},{1,0},{2,3},{3,2},{4,5},{5,4},{6,7},{7,6},{8,9},{9,8},{10,11... | collective-permute-start | bytes 1572872 | tf_op jit(solution)/shard_map/ppermute | solution.py:192
  38.5 25.0 %copy-start = (s32[8192]{0:T(1024)S(1)}, s32[8192]{0:T(1024)}, u32[]{:S(2)}) copy-start(s32[8192]{0:T(1024)} %param.9) | copy-start | bytes 98308
  38.5 8.0 %collective-permute-start.17 = (bf16[8,8192]{1,0:T(8,128)(2,1)S(1)}, bf16[8,8192]{1,0:T(8,128)(2,1)S(1)}, u32[]{:S(2)}, u32[]{:S(2)}) collective-permute-start(bf16[8,8192]{1,0:T(8,128)(2,1)S(1)} %get-tuple-element.82), channel_id=1, source_target_pairs={{0,2},{1,1},{2,0},{3,3},{4,6},{5,5},{6,4},{7,7},{8,10},{9,9},{10,8... | collective-permute-start | bytes 393224 | tf_op jit(solution)/shard_map/ppermute | solution.py:192
  41.1 9.6 %collective-permute-start.20 = (bf16[8,8192]{1,0:T(8,128)(2,1)S(1)}, bf16[8,8192]{1,0:T(8,128)(2,1)S(1)}, u32[]{:S(2)}, u32[]{:S(2)}) collective-permute-start(bf16[8,8192]{1,0:T(8,128)(2,1)S(1)} %get-tuple-element.82), channel_id=1, source_target_pairs={{0,0},{1,3},{2,2},{3,1},{4,4},{5,7},{6,6},{7,5},{8,8},{9,11},{10,1... | collective-permute-start | bytes 393224 | tf_op jit(solution)/shard_map/ppermute | solution.py:192
  41.7 8.9 %collective-permute-start.18 = (bf16[8,8192]{1,0:T(8,128)(2,1)S(1)}, bf16[8,8192]{1,0:T(8,128)(2,1)S(1)}, u32[]{:S(2)}, u32[]{:S(2)}) collective-permute-start(bf16[8,8192]{1,0:T(8,128)(2,1)S(1)} %get-tuple-element.69), channel_id=1, source_target_pairs={{0,6},{1,1},{2,4},{3,3},{4,2},{5,5},{6,0},{7,7},{8,14},{9,9},{10,1... | collective-permute-start | bytes 393224 | tf_op jit(solution)/shard_map/ppermute | solution.py:192
  45.4 5.3 %collective-permute-start.21 = (bf16[8,8192]{1,0:T(8,128)(2,1)S(1)}, bf16[8,8192]{1,0:T(8,128)(2,1)S(1)}, u32[]{:S(2)}, u32[]{:S(2)}) collective-permute-start(bf16[8,8192]{1,0:T(8,128)(2,1)S(1)} %get-tuple-element.69), channel_id=1, source_target_pairs={{0,0},{1,7},{2,2},{3,5},{4,4},{5,3},{6,6},{7,1},{8,8},{9,15},{10,1... | collective-permute-start | bytes 393224 | tf_op jit(solution)/shard_map/ppermute | solution.py:192
  46.5 6.8 %collective-permute-start.22 = (bf16[8,8192]{1,0:T(8,128)(2,1)S(1)}, bf16[8,8192]{1,0:T(8,128)(2,1)S(1)}, u32[]{:S(2)}, u32[]{:S(2)}) collective-permute-start(bf16[8,8192]{1,0:T(8,128)(2,1)S(1)} %get-tuple-element.68), channel_id=1, source_target_pairs={{0,2},{1,1},{2,0},{3,3},{4,6},{5,5},{6,4},{7,7},{8,10},{9,9},{10,8... | collective-permute-start | bytes 393224 | tf_op jit(solution)/shard_map/ppermute | solution.py:192
  49.3 1.4 %collective-permute-start.19 = (bf16[8,8192]{1,0:T(8,128)(2,1)S(1)}, bf16[8,8192]{1,0:T(8,128)(2,1)S(1)}, u32[]{:S(2)}, u32[]{:S(2)}) collective-permute-start(bf16[8,8192]{1,0:T(8,128)(2,1)S(1)} %get-tuple-element.68), channel_id=1, source_target_pairs={{0,0},{1,5},{2,2},{3,7},{4,4},{5,1},{6,6},{7,3},{8,8},{9,13},{10,1... | collective-permute-start | bytes 393224 | tf_op jit(solution)/shard_map/ppermute | solution.py:192
  53.4 5.0 %collective-permute-start.23 = (bf16[8,8192]{1,0:T(8,128)(2,1)S(1)}, bf16[8,8192]{1,0:T(8,128)(2,1)S(1)}, u32[]{:S(2)}, u32[]{:S(2)}) collective-permute-start(bf16[8,8192]{1,0:T(8,128)(2,1)S(1)} %add_convert_fusion.2), channel_id=1, source_target_pairs={{0,2},{1,9},{2,0},{3,11},{4,6},{5,13},{6,4},{7,15},{8,10},{9,1},{1... | collective-permute-start | bytes 393224 | tf_op jit(solution)/shard_map/ppermute | solution.py:192
  54.3 8.2 %collective-permute-start.24 = (bf16[8,8192]{1,0:T(8,128)(2,1)S(1)}, bf16[8,8192]{1,0:T(8,128)(2,1)S(1)}, u32[]{:S(2)}, u32[]{:S(2)}) collective-permute-start(bf16[8,8192]{1,0:T(8,128)(2,1)S(1)} %fusion.1), channel_id=1, source_target_pairs={{0,8},{1,5},{2,10},{3,7},{4,12},{5,1},{6,14},{7,3},{8,0},{9,13},{1... | collective-permute-start | bytes 393224 | tf_op jit(solution)/shard_map/ppermute | solution.py:192
  57.5 5.9 %collective-permute-start.25 = (bf16[8,8192]{1,0:T(8,128)(2,1)S(1)}, bf16[8,8192]{1,0:T(8,128)(2,1)S(1)}, u32[]{:S(2)}, u32[]{:S(2)}) collective-permute-start(bf16[8,8192]{1,0:T(8,128)(2,1)S(1)} %get-tuple-element.79), channel_id=1, source_target_pairs={{0,4},{1,3},{2,6},{3,1},{4,0},{5,7},{6,2},{7,5},{8,12},{9,11},{10,... | collective-permute-start | bytes 393224 | tf_op jit(solution)/shard_map/ppermute | solution.py:192

commit v15 on v10

--- a/solution.py
+++ b/solution.py
@@ -19,7 +19,7 @@
     return pl.BlockSpec(memory_space=pltpu.VMEM)
 
 
-def turn_kernel(gate_hbm, up_hbm, _, gate_ref, up_ref, staged, sems):
+def load_kernel(gate_hbm, up_hbm, down_hbm, _, gate_ref, up_ref, down_ref, staged, sems, down_sem):
     tile = staged.shape[2] // sems.shape[1]
     copies = []
     for k in range(sems.shape[1]):
@@ -29,46 +29,32 @@
                 pltpu.make_async_copy(source.at[:, here], staged.at[j, :, here], sems.at[j, k])
             )
             copies[-1].start()
+    down_copy = pltpu.make_async_copy(down_hbm, down_ref, down_sem)
+    down_copy.start()
     for k in range(sems.shape[1]):
         here = slice(k * tile, (k + 1) * tile)
         for j, out in enumerate((gate_ref, up_ref)):
             copies[2 * k + j].wait()
             out[here, :] = staged[j, :, here].T
-
-
-def turn(gate_w, up_w, after):
+    down_copy.wait()
+
+
+def load(gate_w, up_w, down_w, after):
     units, features = gate_w.shape
     shape = jax.ShapeDtypeStruct((features, units), gate_w.dtype)
     return pl.pallas_call(
-        turn_kernel,
-        out_shape=(shape, shape),
-        in_specs=[pl.BlockSpec(memory_space=pltpu.HBM)] * 2 + [pl.BlockSpec(memory_space=pl.ANY)],
-        out_specs=(vmem(), vmem()),
+        load_kernel,
+        out_shape=(shape, shape, jax.ShapeDtypeStruct(down_w.shape, down_w.dtype)),
+        in_specs=[pl.BlockSpec(memory_space=pltpu.HBM)] * 3 + [pl.BlockSpec(memory_space=pl.ANY)],
+        out_specs=(vmem(),) * 3,
         scratch_shapes=[
             pltpu.VMEM((2, units, features), gate_w.dtype),
             pltpu.SemaphoreType.DMA((2, TURNS)),
+            pltpu.SemaphoreType.DMA,
         ],
-        cost_estimate=pl.CostEstimate(flops=0, bytes_accessed=4 * units * features, transcendentals=0),
+        cost_estimate=pl.CostEstimate(flops=0, bytes_accessed=6 * units * features, transcendentals=0),
         compiler_params=pltpu.CompilerParams(vmem_limit_bytes=24 << 20),
-    )(*(pltpu.with_memory_space_constraint(w, pltpu.HBM) for w in (gate_w, up_w)), after)
-
-
-def fetch_kernel(down_hbm, down_ref, sem):
-    copy = pltpu.make_async_copy(down_hbm, down_ref, sem)
-    copy.start()
-    copy.wait()
-
-
-def fetch(down_w):
-    return pl.pallas_call(
-        fetch_kernel,
-        out_shape=jax.ShapeDtypeStruct(down_w.shape, down_w.dtype),
-        in_specs=[pl.BlockSpec(memory_space=pltpu.HBM)],
-        out_specs=vmem(),
-        scratch_shapes=[pltpu.SemaphoreType.DMA],
-        cost_estimate=pl.CostEstimate(flops=0, bytes_accessed=2 * down_w.size, transcendentals=0),
-        compiler_params=pltpu.CompilerParams(vmem_limit_bytes=4 << 20),
-    )(pltpu.with_memory_space_constraint(down_w, pltpu.HBM))
+    )(*(pltpu.with_memory_space_constraint(w, pltpu.HBM) for w in (gate_w, up_w, down_w)), after)
 
 
 def hidden_kernel(start, last, *refs):
@@ -188,12 +174,13 @@
     members = mesh.shape["gx"]
     assert members & (members - 1) == 0 and members >= 16
 
-    square = ((4, 2), (2, 4), (6, 6))
     far = []
     mask = members // 2
-    while mask > 4:
+    while mask > 8:
         far.append((mask, mask))
         mask //= 2
+    far.append((8, 4))
+    square = ((4, 2), (2, 8), (6, 10))
     others = members // 8 - 1
 
     def swap(value, masks):
@@ -207,12 +194,10 @@
             away.append(swap(jnp.concatenate([tokens] + away), masks))
         away = jnp.concatenate(away)
         near = [swap(tokens, m) for m in square]
-        down_w = fetch(down_weight)
-        away, down_w = lax.optimization_barrier((away, down_w))
         there = [swap(away, m) for m in square[:2]]
         away, near[0] = lax.optimization_barrier((away, near[0]))
         there.append(swap(away, square[2]))
-        gate_w, up_w = turn(gate_weight.T, up_weight.T, away)
+        gate_w, up_w, down_w = load(gate_weight.T, up_weight.T, down_weight, away)
         there[0], *near = lax.optimization_barrier((there[0], *near))
         near = jnp.concatenate([tokens, near[1], near[0], near[2]])
         near_there = swap(near, (1, 1))

time: 45.1 us -> 52.7 us (1.17)
  the two profiles are of different devices: /device:TPU:0 before, /device:TPU:5 now
where the time goes in v15:
time: 52.7 us; the launch traced here: 52.6 us
  starting transfers between devices  31.4 us (60%)
  waiting for transfers between devices  11.9 us (23%)
  Pallas kernels  7.5 us (14%)
  local copies, waits for them, and re-layouts  1.11 us (2%)
    ppermute x19, starting transfers between devices, swap(): lax.ppermute(value, 'gx', [(i, i ^ masks[i % 2]) for i in range(members)])  31.4 us
    ppermute x19, waiting for transfers between devices, swap(): lax.ppermute(value, 'gx', [(i, i ^ masks[i % 2]) for i in range(members)])  11.9 us
    pallas_call x1, Pallas kernels, load(): pl.pallas_call(load_kernel, out_shape=(shape, shape, jax.ShapeDtypeStruct...  4.44 us
    pallas_call x2, Pallas kernels, hidden_units(): pl.pallas_call(functools.partial(hidden_kernel, start, last), out_shape=(...  1.45 us
  transfers between devices with their start and end apart: 19, of which 6 were waited for; matrix products, arithmetic and copies ran while one was open for 3% of the time, Pallas kernels for 10%

profile of v15, /device:TPU:5, one launch (start us, length us, event | category | flops | bytes accessed | tf_op | source)
XLA Modules:
  0.0 52.6 jit_solution(4576488777861979562)
XLA Ops:
  0.0 1.3 %collective-permute-start = (bf16[8,8192]{1,0:T(8,128)(2,1)}, bf16[8,8192]{1,0:T(8,128)(2,1)S(1)}, u32[]{:S(2)}, u32[]{:S(2)}) collective-permute-start(bf16[8,8192]{1,0:T(8,128)(2,1)} %param.5), channel_id=1, source_target_pairs={{0,8},{1,5},{2,10},{3,7},{4,12},{5,1},{6,14},{7,3},{8,0},{9,13},{1... | collective-permute-start | bytes 393224 | tf_op jit(solution)/shard_map/ppermute | solution.py:187
  1.3 0.2 collective-permute-start.1
  1.5 2.3 %collective-permute-start.3 = (bf16[8,8192]{1,0:T(8,128)(2,1)}, bf16[8,8192]{1,0:T(8,128)(2,1)S(1)}, u32[]{:S(2)}, u32[]{:S(2)}) collective-permute-start(bf16[8,8192]{1,0:T(8,128)(2,1)} %param.5), channel_id=1, source_target_pairs={{0,2},{1,9},{2,0},{3,11},{4,6},{5,13},{6,4},{7,15},{8,10},{9,1},{1... | collective-permute-start | bytes 393224 | tf_op jit(solution)/shard_map/ppermute | solution.py:187
  3.8 1.0 %collective-permute-start.4 = (bf16[8,8192]{1,0:T(8,128)(2,1)}, bf16[8,8192]{1,0:T(8,128)(2,1)S(1)}, u32[]{:S(2)}, u32[]{:S(2)}) collective-permute-start(bf16[8,8192]{1,0:T(8,128)(2,1)} %param.5), channel_id=1, source_target_pairs={{0,6},{1,11},{2,4},{3,9},{4,2},{5,15},{6,0},{7,13},{8,14},{9,3},{1... | collective-permute-start | bytes 393224 | tf_op jit(solution)/shard_map/ppermute | solution.py:187
  4.8 0.9 %constant_dynamic-update-slice_fusion.3 = bf16[32,8192]{1,0:T(8,128)(2,1)S(1)} fusion(bf16[8,8192]{1,0:T(8,128)(2,1)} %param.5), kind=kLoop, calls=%fused_computation.23 | loop fusion | bytes 262144
  5.8 0.0 collective-permute-done._
  5.8 0.0 collective-permute-done.1
  5.8 2.3 %collective-permute-start.6 = (bf16[8,8192]{1,0:T(8,128)(2,1)S(1)}, bf16[8,8192]{1,0:T(8,128)(2,1)S(1)}, u32[]{:S(2)}, u32[]{:S(2)}) collective-permute-start(bf16[8,8192]{1,0:T(8,128)(2,1)S(1)} %collective-permute-done._), channel_id=1, source_target_pairs={{0,6},{1,11},{2,4},{3,9},{4,2},{5,15},{6,0},{7,13},{8,14},{9,3},{1... | collective-permute-start | bytes 393224 | tf_op jit(solution)/shard_map/ppermute | solution.py:187
  8.1 1.2 %collective-permute-start.2 = (bf16[8,8192]{1,0:T(8,128)(2,1)S(1)}, bf16[8,8192]{1,0:T(8,128)(2,1)S(1)}, u32[]{:S(2)}, u32[]{:S(2)}) collective-permute-start(bf16[8,8192]{1,0:T(8,128)(2,1)S(1)} %collective-permute-done._), channel_id=1, source_target_pairs={{0,4},{1,3},{2,6},{3,1},{4,0},{5,7},{6,2},{7,5},{8,12},{9,11},{10,... | collective-permute-start | bytes 393224 | tf_op jit(solution)/shard_map/ppermute | solution.py:187
  9.4 4.4 %shard_map.55 = (bf16[8192,224]{1,0:T(8,128)(2,1)S(1)}, bf16[8192,224]{1,0:T(8,128)(2,1)S(1)}, bf16[224,8192]{1,0:T(8,128)(2,1)S(1)}) custom-call(bf16[224,8192]{1,0:T(8,128)(2,1)} %bitcast.4, bf16[224,8192]{1,0:T(8,128)(2,1)} %bitcast.5, bf16[224,8192]{1,0:T(8,128)(2,1)} %down_hbm.1, bf16[8,8192]{1,0:T(8,128)(2,1)S(1)} %collective-permute-done._), custom_call_target="tpu_custom_call" | custom-call | bytes 11010048 | tf_op jit(solution)/shard_map/pallas_call | solution.py:45
  13.8 0.1 collective-permute-start.5
  14.0 0.0 collective-permute-done.3
  14.0 0.0 collective-permute-done.4
  14.0 0.4 collective-permute-done.2
  14.4 5.9 %collective-permute-start.7 = (bf16[32,8192]{1,0:T(8,128)(2,1)S(1)}, bf16[32,8192]{1,0:T(8,128)(2,1)S(1)}, u32[]{:S(2)}, u32[]{:S(2)}) collective-permute-start(bf16[32,8192]{1,0:T(8,128)(2,1)S(1)} %constant_dynamic-update-slice_fusion.refs_2_), channel_id=1, source_target_pairs={{0,1},{1,0},{2,3},{3,2},{4,5},{5,4},{6,7},{7,6},{8,9},{9,8},{10,11... | collective-permute-start | bytes 1572872 | tf_op jit(solution)/shard_map/ppermute | solution.py:187
  20.3 0.0 collective-permute-done.6
  20.4 0.0 collective-permute-done.5
  20.4 3.0 %collective-permute-start.9 = (bf16[32,4096]{1,0:T(8,128)(2,1)S(1)}, bf16[32,4096]{1,0:T(8,128)(2,1)S(1)}, u32[]{:S(2)}, u32[]{:S(2)}) collective-permute-start(bf16[32,4096]{1,0:T(8,128)(2,1)S(1)} %pad_maximum_fusion.1.refs_4_), channel_id=1, source_target_pairs={{0,1},{1,0},{2,3},{3,2},{4,5},{5,4},{6,7},{7,6},{8,9},{9,8},{10,11... | collective-permute-start | bytes 786440 | tf_op jit(solution)/shard_map/ppermute | solution.py:187
  23.5 0.1 collective-permute-start.8
  23.6 1.1 %collective-permute-done.9.refs_5_ = bf16[32,4096]{1,0:T(8,128)(2,1)S(1)} collective-permute-done((bf16[32,4096]{1,0:T(8,128)(2,1)S(1)}, bf16[32,4096]{1,0:T(8,128)(2,1)S(1)}, u32[]{:S(2)}, u32[]{:S(2)}) %collective-permute-start.9) | collective-permute-done | bytes 262176 | tf_op jit(solution)/shard_map/ppermute | solution.py:187
  24.6 0.0 collective-permute-done.7.refs_3_
  24.6 0.7 %shard_map.56 = (f32[128,224]{1,0:T(8,128)S(1)}, f32[128,224]{1,0:T(8,128)S(1)}) custom-call(bf16[8192,224]{1,0:T(8,128)(2,1)S(1)} %get-tuple-element.36.refs_0_, bf16[8192,224]{1,0:T(8,128)(2,1)S(1)} %get-tuple-element.37.refs_1_, bf16[32,8192]{1,0:T(8,128)(2,1)S(1)} %constant_dynamic-update-slice_fusion.refs_2_, ...), custom_call_target="tpu_custom_call" | custom-call | flops 469762048 | bytes 3670016 | tf_op jit(solution)/shard_map/pallas_call | solution.py:85
  25.3 0.0 collective-permute-done.8.refs_5_
  25.4 0.7 %shard_map.57.hidden_ref = bf16[128,224]{1,0:T(8,128)(2,1)S(1)} custom-call(bf16[8192,224]{1,0:T(8,128)(2,1)S(1)} %get-tuple-element.36.refs_0_, bf16[8192,224]{1,0:T(8,128)(2,1)S(1)} %get-tuple-element.37.refs_1_, bf16[32,8192]{1,0:T(8,128)(2,1)S(1)} %constant_dynamic-update-slice_fusion.refs_2_, bf16[32,8192]{1,0:T(8,128)(2,1)S(1)} %collective-permute-done.7.refs_3_, ...), custom_call_target="tpu_custom_call" | custom-call | flops 469762048 | bytes 3670016 | tf_op jit(solution)/shard_map/pallas_call | solution.py:85
  26.1 0.7 %shard_map.58 = (f32[32,8192]{1,0:T(8,128)S(1)}, f32[8,8192]{1,0:T(8,128)S(1)}, f32[24,8192]{1,0:T(8,128)S(1)}, bf16[32,8192]{1,0:T(8,128)(2,1)S(1)}, bf16[8,819...) custom-call(bf16[128,224]{1,0:T(8,128)(2,1)S(1)} %shard_map.57.hidden_ref, bf16[224,8192]{1,0:T(8,128)(2,1)S(1)} %get-tuple-element.44.down_ref), custom_call_target="tpu_custom_call" | custom-call | flops 469762048 | bytes 3670016 | tf_op jit(solution)/shard_map/pallas_call | solution.py:113
  26.8 0.4 collective-permute-start.13
  27.3 0.2 collective-permute-start.10
  27.4 0.8 %collective-permute-done.13 = bf16[8,8192]{1,0:T(8,128)(2,1)S(1)} collective-permute-done((bf16[8,8192]{1,0:T(8,128)(2,1)S(1)}, bf16[8,8192]{1,0:T(8,128)(2,1)S(1)}, u32[]{:S(2)}, u32[]{:S(2)}) %collective-permute-start.13) | collective-permute-done | bytes 131104 | tf_op jit(solution)/shard_map/ppermute | solution.py:187
  28.3 4.7 %collective-permute-start.14 = (bf16[8,8192]{1,0:T(8,128)(2,1)S(1)}, bf16[8,8192]{1,0:T(8,128)(2,1)S(1)}, u32[]{:S(2)}, u32[]{:S(2)}) collective-permute-start(bf16[8,8192]{1,0:T(8,128)(2,1)S(1)} %add_convert_fusion), channel_id=1, source_target_pairs={{0,6},{1,11},{2,4},{3,9},{4,2},{5,15},{6,0},{7,13},{8,14},{9,3},{1... | collective-permute-start | bytes 393224 | tf_op jit(solution)/shard_map/ppermute | solution.py:187
  33.0 0.0 collective-permute-done.10
  33.0 0.0 collective-permute-start.11
  33.0 0.1 fusion.7
  33.1 0.0 copy-start
  33.2 0.3 collective-permute-start.15
  33.5 2.2 %collective-permute-start.16 = (bf16[8,8192]{1,0:T(8,128)(2,1)S(1)}, bf16[8,8192]{1,0:T(8,128)(2,1)S(1)}, u32[]{:S(2)}, u32[]{:S(2)}) collective-permute-start(bf16[8,8192]{1,0:T(8,128)(2,1)S(1)} %get-tuple-element.56), channel_id=1, source_target_pairs={{0,2},{1,9},{2,0},{3,11},{4,6},{5,13},{6,4},{7,15},{8,10},{9,1},{1... | collective-permute-start | bytes 393224 | tf_op jit(solution)/shard_map/ppermute | solution.py:187
  35.7 0.0 collective-permute-done.11
  35.7 0.1 convert_add_fusion
  35.8 1.5 %collective-permute-start.12 = (bf16[16,8192]{1,0:T(8,128)(2,1)S(1)}, bf16[16,8192]{1,0:T(8,128)(2,1)S(1)}, u32[]{:S(2)}, u32[]{:S(2)}) collective-permute-start(bf16[16,8192]{1,0:T(8,128)(2,1)S(1)} %slice.83), channel_id=1, source_target_pairs={{0,4},{1,3},{2,6},{3,1},{4,0},{5,7},{6,2},{7,5},{8,12},{9,11},{10,... | collective-permute-start | bytes 786440 | tf_op jit(solution)/shard_map/ppermute | solution.py:187
  37.3 0.0 collective-permute-done.14
  37.3 0.0 collective-permute-done.15
  37.3 1.4 %collective-permute-done.16 = bf16[8,8192]{1,0:T(8,128)(2,1)S(1)} collective-permute-done((bf16[8,8192]{1,0:T(8,128)(2,1)S(1)}, bf16[8,8192]{1,0:T(8,128)(2,1)S(1)}, u32[]{:S(2)}, u32[]{:S(2)}) %collective-permute-start.16) | collective-permute-done | bytes 131104 | tf_op jit(solution)/shard_map/ppermute | solution.py:187
  38.7 0.1 fusion.2
  38.8 2.4 %collective-permute-start.17 = (bf16[8,8192]{1,0:T(8,128)(2,1)S(1)}, bf16[8,8192]{1,0:T(8,128)(2,1)S(1)}, u32[]{:S(2)}, u32[]{:S(2)}) collective-permute-start(bf16[8,8192]{1,0:T(8,128)(2,1)S(1)} %fusion.2), channel_id=1, source_target_pairs={{0,8},{1,5},{2,10},{3,7},{4,12},{5,1},{6,14},{7,3},{8,0},{9,13},{1... | collective-permute-start | bytes 393224 | tf_op jit(solution)/shard_map/ppermute | solution.py:187
  41.2 1.4 %collective-permute-done.12 = bf16[16,8192]{1,0:T(8,128)(2,1)S(1)} collective-permute-done((bf16[16,8192]{1,0:T(8,128)(2,1)S(1)}, bf16[16,8192]{1,0:T(8,128)(2,1)S(1)}, u32[]{:S(2)}, u32[]{:S(2)}) %collective-permute-start.12) | collective-permute-done | bytes 262176 | tf_op jit(solution)/shard_map/ppermute | solution.py:187
  42.6 0.1 slice_add_fusion
  42.6 2.2 %collective-permute-start.18 = (bf16[8,8192]{1,0:T(8,128)(2,1)S(1)}, bf16[8,8192]{1,0:T(8,128)(2,1)S(1)}, u32[]{:S(2)}, u32[]{:S(2)}) collective-permute-start(bf16[8,8192]{1,0:T(8,128)(2,1)S(1)} %slice.84), channel_id=1, source_target_pairs={{0,2},{1,9},{2,0},{3,11},{4,6},{5,13},{6,4},{7,15},{8,10},{9,1},{1... | collective-permute-start | bytes 393224 | tf_op jit(solution)/shard_map/ppermute | solution.py:187
  44.9 0.0 collective-permute-done.17.refs_1_
  44.9 6.8 %collective-permute-done.18.refs_2_ = bf16[8,8192]{1,0:T(8,128)(2,1)S(1)} collective-permute-done((bf16[8,8192]{1,0:T(8,128)(2,1)S(1)}, bf16[8,8192]{1,0:T(8,128)(2,1)S(1)}, u32[]{:S(2)}, u32[]{:S(2)}) %collective-permute-start.18) | collective-permute-done | bytes 131104 | tf_op jit(solution)/shard_map/ppermute | solution.py:187
  51.7 0.0 copy-done
  51.7 0.9 %shard_map.59 = bf16[8,8192]{1,0:T(8,128)(2,1)} custom-call(f32[8,8192]{1,0:T(8,128)S(1)} %slice.68.refs_0_, bf16[8,8192]{1,0:T(8,128)(2,1)S(1)} %collective-permute-done.17.refs_1_, bf16[8,8192]{1,0:T(8,128)(2,1)S(1)} %collective-permute-done.18.refs_2_, s32[1,8192]{1,0:T(1,128)S(1)} %bitcast.3, bf16[256,128]{1,0:T(8,128)(2,1)S(1)} %pad_maximum_fusion.2.refs_4_), custom_call_target="tpu_custom_call" | custom-call | tf_op jit(solution)/shard_map/pallas_call | solution.py:163
  (15 shorter events, 0.3 us)
Async XLA Ops:
  0.0 5.8 %collective-permute-start = (bf16[8,8192]{1,0:T(8,128)(2,1)}, bf16[8,8192]{1,0:T(8,128)(2,1)S(1)}, u32[]{:S(2)}, u32[]{:S(2)}) collective-permute-start(bf16[8,8192]{1,0:T(8,128)(2,1)} %param.5), channel_id=1, source_target_pairs={{0,8},{1,5},{2,10},{3,7},{4,12},{5,1},{6,14},{7,3},{8,0},{9,13},{1... | collective-permute-start | bytes 393224 | tf_op jit(solution)/shard_map/ppermute | solution.py:187
  1.3 4.5 %collective-permute-start.1 = (bf16[8,8192]{1,0:T(8,128)(2,1)}, bf16[8,8192]{1,0:T(8,128)(2,1)S(1)}, u32[]{:S(2)}, u32[]{:S(2)}) collective-permute-start(bf16[8,8192]{1,0:T(8,128)(2,1)} %param.5), channel_id=1, source_target_pairs={{0,4},{1,3},{2,6},{3,1},{4,0},{5,7},{6,2},{7,5},{8,12},{9,11},{10,... | collective-permute-start | bytes 393224 | tf_op jit(solution)/shard_map/ppermute | solution.py:187
  1.5 12.4 %collective-permute-start.3 = (bf16[8,8192]{1,0:T(8,128)(2,1)}, bf16[8,8192]{1,0:T(8,128)(2,1)S(1)}, u32[]{:S(2)}, u32[]{:S(2)}) collective-permute-start(bf16[8,8192]{1,0:T(8,128)(2,1)} %param.5), channel_id=1, source_target_pairs={{0,2},{1,9},{2,0},{3,11},{4,6},{5,13},{6,4},{7,15},{8,10},{9,1},{1... | collective-permute-start | bytes 393224 | tf_op jit(solution)/shard_map/ppermute | solution.py:187
  3.8 10.1 %collective-permute-start.4 = (bf16[8,8192]{1,0:T(8,128)(2,1)}, bf16[8,8192]{1,0:T(8,128)(2,1)S(1)}, u32[]{:S(2)}, u32[]{:S(2)}) collective-permute-start(bf16[8,8192]{1,0:T(8,128)(2,1)} %param.5), channel_id=1, source_target_pairs={{0,6},{1,11},{2,4},{3,9},{4,2},{5,15},{6,0},{7,13},{8,14},{9,3},{1... | collective-permute-start | bytes 393224 | tf_op jit(solution)/shard_map/ppermute | solution.py:187
  5.8 14.5 %collective-permute-start.6 = (bf16[8,8192]{1,0:T(8,128)(2,1)S(1)}, bf16[8,8192]{1,0:T(8,128)(2,1)S(1)}, u32[]{:S(2)}, u32[]{:S(2)}) collective-permute-start(bf16[8,8192]{1,0:T(8,128)(2,1)S(1)} %collective-permute-done._), channel_id=1, source_target_pairs={{0,6},{1,11},{2,4},{3,9},{4,2},{5,15},{6,0},{7,13},{8,14},{9,3},{1... | collective-permute-start | bytes 393224 | tf_op jit(solution)/shard_map/ppermute | solution.py:187
  8.1 6.2 %collective-permute-start.2 = (bf16[8,8192]{1,0:T(8,128)(2,1)S(1)}, bf16[8,8192]{1,0:T(8,128)(2,1)S(1)}, u32[]{:S(2)}, u32[]{:S(2)}) collective-permute-start(bf16[8,8192]{1,0:T(8,128)(2,1)S(1)} %collective-permute-done._), channel_id=1, source_target_pairs={{0,4},{1,3},{2,6},{3,1},{4,0},{5,7},{6,2},{7,5},{8,12},{9,11},{10,... | collective-permute-start | bytes 393224 | tf_op jit(solution)/shard_map/ppermute | solution.py:187
  13.8 6.5 %collective-permute-start.5 = (bf16[8,8192]{1,0:T(8,128)(2,1)S(1)}, bf16[8,8192]{1,0:T(8,128)(2,1)S(1)}, u32[]{:S(2)}, u32[]{:S(2)}) collective-permute-start(bf16[8,8192]{1,0:T(8,128)(2,1)S(1)} %collective-permute-done._), channel_id=1, source_target_pairs={{0,2},{1,9},{2,0},{3,11},{4,6},{5,13},{6,4},{7,15},{8,10},{9,1},{1... | collective-permute-start | bytes 393224 | tf_op jit(solution)/shard_map/ppermute | solution.py:187
  14.4 10.2 %collective-permute-start.7 = (bf16[32,8192]{1,0:T(8,128)(2,1)S(1)}, bf16[32,8192]{1,0:T(8,128)(2,1)S(1)}, u32[]{:S(2)}, u32[]{:S(2)}) collective-permute-start(bf16[32,8192]{1,0:T(8,128)(2,1)S(1)} %constant_dynamic-update-slice_fusion.refs_2_), channel_id=1, source_target_pairs={{0,1},{1,0},{2,3},{3,2},{4,5},{5,4},{6,7},{7,6},{8,9},{9,8},{10,11... | collective-permute-start | bytes 1572872 | tf_op jit(solution)/shard_map/ppermute | solution.py:187
  20.4 4.2 %collective-permute-start.9 = (bf16[32,4096]{1,0:T(8,128)(2,1)S(1)}, bf16[32,4096]{1,0:T(8,128)(2,1)S(1)}, u32[]{:S(2)}, u32[]{:S(2)}) collective-permute-start(bf16[32,4096]{1,0:T(8,128)(2,1)S(1)} %pad_maximum_fusion.1.refs_4_), channel_id=1, source_target_pairs={{0,1},{1,0},{2,3},{3,2},{4,5},{5,4},{6,7},{7,6},{8,9},{9,8},{10,11... | collective-permute-start | bytes 786440 | tf_op jit(solution)/shard_map/ppermute | solution.py:187
  23.5 1.9 %collective-permute-start.8 = (bf16[32,4096]{1,0:T(8,128)(2,1)S(1)}, bf16[32,4096]{1,0:T(8,128)(2,1)S(1)}, u32[]{:S(2)}, u32[]{:S(2)}) collective-permute-start(bf16[32,4096]{1,0:T(8,128)(2,1)S(1)} %pad_maximum_fusion.refs_4_), channel_id=1, source_target_pairs={{0,1},{1,0},{2,3},{3,2},{4,5},{5,4},{6,7},{7,6},{8,9},{9,8},{10,11... | collective-permute-start | bytes 786440 | tf_op jit(solution)/shard_map/ppermute | solution.py:187
  26.8 1.4 %collective-permute-start.13 = (bf16[8,8192]{1,0:T(8,128)(2,1)S(1)}, bf16[8,8192]{1,0:T(8,128)(2,1)S(1)}, u32[]{:S(2)}, u32[]{:S(2)}) collective-permute-start(bf16[8,8192]{1,0:T(8,128)(2,1)S(1)} %get-tuple-element.52), channel_id=1, source_target_pairs={{0,1},{1,0},{2,3},{3,2},{4,5},{5,4},{6,7},{7,6},{8,9},{9,8},{10,11... | collective-permute-start | bytes 393224 | tf_op jit(solution)/shard_map/ppermute | solution.py:187
  27.3 5.8 %collective-permute-start.10 = (bf16[24,8192]{1,0:T(8,128)(2,1)S(1)}, bf16[24,8192]{1,0:T(8,128)(2,1)S(1)}, u32[]{:S(2)}, u32[]{:S(2)}) collective-permute-start(bf16[24,8192]{1,0:T(8,128)(2,1)S(1)} %get-tuple-element.46), channel_id=1, source_target_pairs={{0,1},{1,0},{2,3},{3,2},{4,5},{5,4},{6,7},{7,6},{8,9},{9,8},{10,11... | collective-permute-start | bytes 1179656 | tf_op jit(solution)/shard_map/ppermute | solution.py:187
  28.3 9.0 %collective-permute-start.14 = (bf16[8,8192]{1,0:T(8,128)(2,1)S(1)}, bf16[8,8192]{1,0:T(8,128)(2,1)S(1)}, u32[]{:S(2)}, u32[]{:S(2)}) collective-permute-start(bf16[8,8192]{1,0:T(8,128)(2,1)S(1)} %add_convert_fusion), channel_id=1, source_target_pairs={{0,6},{1,11},{2,4},{3,9},{4,2},{5,15},{6,0},{7,13},{8,14},{9,3},{1... | collective-permute-start | bytes 393224 | tf_op jit(solution)/shard_map/ppermute | solution.py:187
  33.0 2.7 %collective-permute-start.11 = (bf16[32,8192]{1,0:T(8,128)(2,1)S(1)}, bf16[32,8192]{1,0:T(8,128)(2,1)S(1)}, u32[]{:S(2)}, u32[]{:S(2)}) collective-permute-start(bf16[32,8192]{1,0:T(8,128)(2,1)S(1)} %get-tuple-element.48), channel_id=1, source_target_pairs={{0,1},{1,0},{2,3},{3,2},{4,5},{5,4},{6,7},{7,6},{8,9},{9,8},{10,11... | collective-permute-start | bytes 1572872 | tf_op jit(solution)/shard_map/ppermute | solution.py:187
  33.1 18.6 %copy-start = (s32[8192]{0:T(1024)S(1)}, s32[8192]{0:T(1024)}, u32[]{:S(2)}) copy-start(s32[8192]{0:T(1024)} %param.9) | copy-start | bytes 98308
  33.2 4.2 %collective-permute-start.15 = (bf16[8,8192]{1,0:T(8,128)(2,1)S(1)}, bf16[8,8192]{1,0:T(8,128)(2,1)S(1)}, u32[]{:S(2)}, u32[]{:S(2)}) collective-permute-start(bf16[8,8192]{1,0:T(8,128)(2,1)S(1)} %get-tuple-element.55), channel_id=1, source_target_pairs={{0,4},{1,3},{2,6},{3,1},{4,0},{5,7},{6,2},{7,5},{8,12},{9,11},{10,... | collective-permute-start | bytes 393224 | tf_op jit(solution)/shard_map/ppermute | solution.py:187
  33.5 5.3 %collective-permute-start.16 = (bf16[8,8192]{1,0:T(8,128)(2,1)S(1)}, bf16[8,8192]{1,0:T(8,128)(2,1)S(1)}, u32[]{:S(2)}, u32[]{:S(2)}) collective-permute-start(bf16[8,8192]{1,0:T(8,128)(2,1)S(1)} %get-tuple-element.56), channel_id=1, source_target_pairs={{0,2},{1,9},{2,0},{3,11},{4,6},{5,13},{6,4},{7,15},{8,10},{9,1},{1... | collective-permute-start | bytes 393224 | tf_op jit(solution)/shard_map/ppermute | solution.py:187
  35.8 6.7 %collective-permute-start.12 = (bf16[16,8192]{1,0:T(8,128)(2,1)S(1)}, bf16[16,8192]{1,0:T(8,128)(2,1)S(1)}, u32[]{:S(2)}, u32[]{:S(2)}) collective-permute-start(bf16[16,8192]{1,0:T(8,128)(2,1)S(1)} %slice.83), channel_id=1, source_target_pairs={{0,4},{1,3},{2,6},{3,1},{4,0},{5,7},{6,2},{7,5},{8,12},{9,11},{10,... | collective-permute-start | bytes 786440 | tf_op jit(solution)/shard_map/ppermute | solution.py:187
  38.8 6.1 %collective-permute-start.17 = (bf16[8,8192]{1,0:T(8,128)(2,1)S(1)}, bf16[8,8192]{1,0:T(8,128)(2,1)S(1)}, u32[]{:S(2)}, u32[]{:S(2)}) collective-permute-start(bf16[8,8192]{1,0:T(8,128)(2,1)S(1)} %fusion.2), channel_id=1, source_target_pairs={{0,8},{1,5},{2,10},{3,7},{4,12},{5,1},{6,14},{7,3},{8,0},{9,13},{1... | collective-permute-start | bytes 393224 | tf_op jit(solution)/shard_map/ppermute | solution.py:187
  42.6 9.1 %collective-permute-start.18 = (bf16[8,8192]{1,0:T(8,128)(2,1)S(1)}, bf16[8,8192]{1,0:T(8,128)(2,1)S(1)}, u32[]{:S(2)}, u32[]{:S(2)}) collective-permute-start(bf16[8,8192]{1,0:T(8,128)(2,1)S(1)} %slice.84), channel_id=1, source_target_pairs={{0,2},{1,9},{2,0},{3,11},{4,6},{5,13},{6,4},{7,15},{8,10},{9,1},{1... | collective-permute-start | bytes 393224 | tf_op jit(solution)/shard_map/ppermute | solution.py:187

commit v16 on v15

--- a/solution.py
+++ b/solution.py
@@ -174,13 +174,12 @@
     members = mesh.shape["gx"]
     assert members & (members - 1) == 0 and members >= 16
 
+    square = ((4, 2), (2, 4), (6, 6))
     far = []
     mask = members // 2
-    while mask > 8:
+    while mask > 4:
         far.append((mask, mask))
         mask //= 2
-    far.append((8, 4))
-    square = ((4, 2), (2, 8), (6, 10))
     others = members // 8 - 1
 
     def swap(value, masks):
@@ -194,6 +193,7 @@
             away.append(swap(jnp.concatenate([tokens] + away), masks))
         away = jnp.concatenate(away)
         near = [swap(tokens, m) for m in square]
+        away, sign_pattern = lax.optimization_barrier((away, sign_pattern))
         there = [swap(away, m) for m in square[:2]]
         away, near[0] = lax.optimization_barrier((away, near[0]))
         there.append(swap(away, square[2]))

time: 52.7 us -> 45 us (0.85)
  the two profiles are of different devices: /device:TPU:5 before, /device:TPU:0 now
where the time goes in v16:
time: 45 us; the launch traced here: 44.8 us
  starting transfers between devices  20.2 us (45%)
  waiting for transfers between devices  15.4 us (34%)
  Pallas kernels  7.5 us (17%)
  local copies, waits for them, and re-layouts  1.11 us (2%)
    ppermute x19, starting transfers between devices, swap(): lax.ppermute(value, 'gx', [(i, i ^ masks[i % 2]) for i in range(members)])  20.2 us
    ppermute x19, waiting for transfers between devices, swap(): lax.ppermute(value, 'gx', [(i, i ^ masks[i % 2]) for i in range(members)])  15.4 us
    pallas_call x1, Pallas kernels, load(): pl.pallas_call(load_kernel, out_shape=(shape, shape, jax.ShapeDtypeStruct...  4.44 us
    pallas_call x2, Pallas kernels, hidden_units(): pl.pallas_call(functools.partial(hidden_kernel, start, last), out_shape=(...  1.45 us
    unnamed x5, local copies, waits for them, and re-layouts  0.97 us
  transfers between devices with their start and end apart: 19, of which 9 were waited for; matrix products, arithmetic and copies ran while one was open for 3% of the time, Pallas kernels for 11%

profile of v16, /device:TPU:0, one launch (start us, length us, event | category | flops | bytes accessed | tf_op | source)
XLA Modules:
  0.0 44.8 jit_solution(12773518888987253155)
XLA Ops:
  0.0 4.0 %collective-permute-start = (bf16[8,8192]{1,0:T(8,128)(2,1)}, bf16[8,8192]{1,0:T(8,128)(2,1)S(1)}, u32[]{:S(2)}, u32[]{:S(2)}) collective-permute-start(bf16[8,8192]{1,0:T(8,128)(2,1)} %param.5), channel_id=1, source_target_pairs={{0,8},{1,9},{2,10},{3,11},{4,12},{5,13},{6,14},{7,15},{8,0},{9,1},... | collective-permute-start | bytes 393224 | tf_op jit(solution)/shard_map/ppermute | solution.py:186
  4.0 1.6 %collective-permute-start.1 = (bf16[8,8192]{1,0:T(8,128)(2,1)}, bf16[8,8192]{1,0:T(8,128)(2,1)S(1)}, u32[]{:S(2)}, u32[]{:S(2)}) collective-permute-start(bf16[8,8192]{1,0:T(8,128)(2,1)} %param.5), channel_id=1, source_target_pairs={{0,4},{1,3},{2,6},{3,1},{4,0},{5,7},{6,2},{7,5},{8,12},{9,11},{10,... | collective-permute-start | bytes 393224 | tf_op jit(solution)/shard_map/ppermute | solution.py:186
  5.6 1.5 %collective-permute-start.3 = (bf16[8,8192]{1,0:T(8,128)(2,1)}, bf16[8,8192]{1,0:T(8,128)(2,1)S(1)}, u32[]{:S(2)}, u32[]{:S(2)}) collective-permute-start(bf16[8,8192]{1,0:T(8,128)(2,1)} %param.5), channel_id=1, source_target_pairs={{0,2},{1,5},{2,0},{3,7},{4,6},{5,1},{6,4},{7,3},{8,10},{9,13},{10,... | collective-permute-start | bytes 393224 | tf_op jit(solution)/shard_map/ppermute | solution.py:186
  7.1 0.4 collective-permute-start.4
  7.5 0.9 %constant_dynamic-update-slice_fusion.3 = bf16[32,8192]{1,0:T(8,128)(2,1)S(1)} fusion(bf16[8,8192]{1,0:T(8,128)(2,1)} %param.5), kind=kLoop, calls=%fused_computation.23 | loop fusion | bytes 262144
  8.5 2.2 %collective-permute-done._ = bf16[8,8192]{1,0:T(8,128)(2,1)S(1)} collective-permute-done((bf16[8,8192]{1,0:T(8,128)(2,1)}, bf16[8,8192]{1,0:T(8,128)(2,1)S(1)}, u32[]{:S(2)}, u32[]{:S(2)}) %collective-permute-start) | collective-permute-done | bytes 131104 | tf_op jit(solution)/shard_map/ppermute | solution.py:186
  10.7 0.8 %collective-permute-start.2 = (bf16[8,8192]{1,0:T(8,128)(2,1)S(1)}, bf16[8,8192]{1,0:T(8,128)(2,1)S(1)}, u32[]{:S(2)}, u32[]{:S(2)}) collective-permute-start(bf16[8,8192]{1,0:T(8,128)(2,1)S(1)} %collective-permute-done._), channel_id=1, source_target_pairs={{0,4},{1,3},{2,6},{3,1},{4,0},{5,7},{6,2},{7,5},{8,12},{9,11},{10,... | collective-permute-start | bytes 393224 | tf_op jit(solution)/shard_map/ppermute | solution.py:186
  11.4 1.5 %collective-permute-start.5 = (bf16[8,8192]{1,0:T(8,128)(2,1)S(1)}, bf16[8,8192]{1,0:T(8,128)(2,1)S(1)}, u32[]{:S(2)}, u32[]{:S(2)}) collective-permute-start(bf16[8,8192]{1,0:T(8,128)(2,1)S(1)} %collective-permute-done._), channel_id=1, source_target_pairs={{0,2},{1,5},{2,0},{3,7},{4,6},{5,1},{6,4},{7,3},{8,10},{9,13},{10,... | collective-permute-start | bytes 393224 | tf_op jit(solution)/shard_map/ppermute | solution.py:186
  12.9 0.0 collective-permute-done.1
  12.9 1.5 %collective-permute-start.6 = (bf16[8,8192]{1,0:T(8,128)(2,1)S(1)}, bf16[8,8192]{1,0:T(8,128)(2,1)S(1)}, u32[]{:S(2)}, u32[]{:S(2)}) collective-permute-start(bf16[8,8192]{1,0:T(8,128)(2,1)S(1)} %collective-permute-done._), channel_id=1, source_target_pairs={{0,6},{1,7},{2,4},{3,5},{4,2},{5,3},{6,0},{7,1},{8,14},{9,15},{10,... | collective-permute-start | bytes 393224 | tf_op jit(solution)/shard_map/ppermute | solution.py:186
  14.4 4.4 %shard_map.55 = (bf16[8192,224]{1,0:T(8,128)(2,1)S(1)}, bf16[8192,224]{1,0:T(8,128)(2,1)S(1)}, bf16[224,8192]{1,0:T(8,128)(2,1)S(1)}) custom-call(bf16[224,8192]{1,0:T(8,128)(2,1)} %bitcast.4, bf16[224,8192]{1,0:T(8,128)(2,1)} %bitcast.5, bf16[224,8192]{1,0:T(8,128)(2,1)} %down_hbm.1, bf16[8,8192]{1,0:T(8,128)(2,1)S(1)} %collective-permute-done._), custom_call_target="tpu_custom_call" | custom-call | bytes 11010048 | tf_op jit(solution)/shard_map/pallas_call | solution.py:45
  18.9 0.0 collective-permute-done.3
  18.9 0.0 collective-permute-done.4
  18.9 0.0 collective-permute-done.2
  18.9 0.1 collective-permute-start.7
  19.0 1.5 %collective-permute-done.6 = bf16[8,8192]{1,0:T(8,128)(2,1)S(1)} collective-permute-done((bf16[8,8192]{1,0:T(8,128)(2,1)S(1)}, bf16[8,8192]{1,0:T(8,128)(2,1)S(1)}, u32[]{:S(2)}, u32[]{:S(2)}) %collective-permute-start.6) | collective-permute-done | bytes 131104 | tf_op jit(solution)/shard_map/ppermute | solution.py:186
  20.5 0.0 collective-permute-done.5
  20.6 0.1 collective-permute-start.9
  20.7 0.6 %collective-permute-start.8 = (bf16[32,4096]{1,0:T(8,128)(2,1)S(1)}, bf16[32,4096]{1,0:T(8,128)(2,1)S(1)}, u32[]{:S(2)}, u32[]{:S(2)}) collective-permute-start(bf16[32,4096]{1,0:T(8,128)(2,1)S(1)} %pad_maximum_fusion.refs_4_), channel_id=1, source_target_pairs={{0,1},{1,0},{2,3},{3,2},{4,5},{5,4},{6,7},{7,6},{8,9},{9,8},{10,11... | collective-permute-start | bytes 786440 | tf_op jit(solution)/shard_map/ppermute | solution.py:186
  21.2 0.9 %collective-permute-done.9.refs_5_ = bf16[32,4096]{1,0:T(8,128)(2,1)S(1)} collective-permute-done((bf16[32,4096]{1,0:T(8,128)(2,1)S(1)}, bf16[32,4096]{1,0:T(8,128)(2,1)S(1)}, u32[]{:S(2)}, u32[]{:S(2)}) %collective-permute-start.9) | collective-permute-done | bytes 262176 | tf_op jit(solution)/shard_map/ppermute | solution.py:186
  22.2 0.0 collective-permute-done.7.refs_3_
  22.2 0.7 %shard_map.56 = (f32[128,224]{1,0:T(8,128)S(1)}, f32[128,224]{1,0:T(8,128)S(1)}) custom-call(bf16[8192,224]{1,0:T(8,128)(2,1)S(1)} %get-tuple-element.39.refs_0_, bf16[8192,224]{1,0:T(8,128)(2,1)S(1)} %get-tuple-element.40.refs_1_, bf16[32,8192]{1,0:T(8,128)(2,1)S(1)} %constant_dynamic-update-slice_fusion.refs_2_, ...), custom_call_target="tpu_custom_call" | custom-call | flops 469762048 | bytes 3670016 | tf_op jit(solution)/shard_map/pallas_call | solution.py:85
  22.9 0.0 collective-permute-done.8.refs_5_
  22.9 0.7 %shard_map.57.hidden_ref = bf16[128,224]{1,0:T(8,128)(2,1)S(1)} custom-call(bf16[8192,224]{1,0:T(8,128)(2,1)S(1)} %get-tuple-element.39.refs_0_, bf16[8192,224]{1,0:T(8,128)(2,1)S(1)} %get-tuple-element.40.refs_1_, bf16[32,8192]{1,0:T(8,128)(2,1)S(1)} %constant_dynamic-update-slice_fusion.refs_2_, bf16[32,8192]{1,0:T(8,128)(2,1)S(1)} %collective-permute-done.7.refs_3_, ...), custom_call_target="tpu_custom_call" | custom-call | flops 469762048 | bytes 3670016 | tf_op jit(solution)/shard_map/pallas_call | solution.py:85
  23.7 0.7 %shard_map.58 = (f32[32,8192]{1,0:T(8,128)S(1)}, f32[8,8192]{1,0:T(8,128)S(1)}, f32[24,8192]{1,0:T(8,128)S(1)}, bf16[32,8192]{1,0:T(8,128)(2,1)S(1)}, bf16[8,819...) custom-call(bf16[128,224]{1,0:T(8,128)(2,1)S(1)} %shard_map.57.hidden_ref, bf16[224,8192]{1,0:T(8,128)(2,1)S(1)} %get-tuple-element.47.down_ref), custom_call_target="tpu_custom_call" | custom-call | flops 469762048 | bytes 3670016 | tf_op jit(solution)/shard_map/pallas_call | solution.py:113
  24.4 0.2 collective-permute-start.13
  24.6 0.4 collective-permute-start.10
  25.0 0.8 %collective-permute-done.13 = bf16[8,8192]{1,0:T(8,128)(2,1)S(1)} collective-permute-done((bf16[8,8192]{1,0:T(8,128)(2,1)S(1)}, bf16[8,8192]{1,0:T(8,128)(2,1)S(1)}, u32[]{:S(2)}, u32[]{:S(2)}) %collective-permute-start.13) | collective-permute-done | bytes 131104 | tf_op jit(solution)/shard_map/ppermute | solution.py:186
  25.8 1.2 %collective-permute-start.14 = (bf16[8,8192]{1,0:T(8,128)(2,1)S(1)}, bf16[8,8192]{1,0:T(8,128)(2,1)S(1)}, u32[]{:S(2)}, u32[]{:S(2)}) collective-permute-start(bf16[8,8192]{1,0:T(8,128)(2,1)S(1)} %add_convert_fusion), channel_id=1, source_target_pairs={{0,6},{1,7},{2,4},{3,5},{4,2},{5,3},{6,0},{7,1},{8,14},{9,15},{10,... | collective-permute-start | bytes 393224 | tf_op jit(solution)/shard_map/ppermute | solution.py:186
  27.0 0.0 collective-permute-done.10
  27.0 0.0 collective-permute-start.11
  27.0 0.1 fusion.7
  27.1 0.0 copy-start
  27.2 1.9 %collective-permute-start.15 = (bf16[8,8192]{1,0:T(8,128)(2,1)S(1)}, bf16[8,8192]{1,0:T(8,128)(2,1)S(1)}, u32[]{:S(2)}, u32[]{:S(2)}) collective-permute-start(bf16[8,8192]{1,0:T(8,128)(2,1)S(1)} %get-tuple-element.59), channel_id=1, source_target_pairs={{0,4},{1,3},{2,6},{3,1},{4,0},{5,7},{6,2},{7,5},{8,12},{9,11},{10,... | collective-permute-start | bytes 393224 | tf_op jit(solution)/shard_map/ppermute | solution.py:186
  29.1 0.5 %collective-permute-start.16 = (bf16[8,8192]{1,0:T(8,128)(2,1)S(1)}, bf16[8,8192]{1,0:T(8,128)(2,1)S(1)}, u32[]{:S(2)}, u32[]{:S(2)}) collective-permute-start(bf16[8,8192]{1,0:T(8,128)(2,1)S(1)} %get-tuple-element.60), channel_id=1, source_target_pairs={{0,2},{1,5},{2,0},{3,7},{4,6},{5,1},{6,4},{7,3},{8,10},{9,13},{10,... | collective-permute-start | bytes 393224 | tf_op jit(solution)/shard_map/ppermute | solution.py:186
  29.6 0.0 collective-permute-done.11
  29.6 0.1 convert_add_fusion
  29.7 1.3 %collective-permute-start.12 = (bf16[16,8192]{1,0:T(8,128)(2,1)S(1)}, bf16[16,8192]{1,0:T(8,128)(2,1)S(1)}, u32[]{:S(2)}, u32[]{:S(2)}) collective-permute-start(bf16[16,8192]{1,0:T(8,128)(2,1)S(1)} %slice.83), channel_id=1, source_target_pairs={{0,4},{1,3},{2,6},{3,1},{4,0},{5,7},{6,2},{7,5},{8,12},{9,11},{10,... | collective-permute-start | bytes 786440 | tf_op jit(solution)/shard_map/ppermute | solution.py:186
  31.0 2.1 %collective-permute-done.14 = bf16[8,8192]{1,0:T(8,128)(2,1)S(1)} collective-permute-done((bf16[8,8192]{1,0:T(8,128)(2,1)S(1)}, bf16[8,8192]{1,0:T(8,128)(2,1)S(1)}, u32[]{:S(2)}, u32[]{:S(2)}) %collective-permute-start.14) | collective-permute-done | bytes 131104 | tf_op jit(solution)/shard_map/ppermute | solution.py:186
  33.0 2.2 %collective-permute-done.15 = bf16[8,8192]{1,0:T(8,128)(2,1)S(1)} collective-permute-done((bf16[8,8192]{1,0:T(8,128)(2,1)S(1)}, bf16[8,8192]{1,0:T(8,128)(2,1)S(1)}, u32[]{:S(2)}, u32[]{:S(2)}) %collective-permute-start.15) | collective-permute-done | bytes 131104 | tf_op jit(solution)/shard_map/ppermute | solution.py:186
  35.2 0.5 %collective-permute-done.16 = bf16[8,8192]{1,0:T(8,128)(2,1)S(1)} collective-permute-done((bf16[8,8192]{1,0:T(8,128)(2,1)S(1)}, bf16[8,8192]{1,0:T(8,128)(2,1)S(1)}, u32[]{:S(2)}, u32[]{:S(2)}) %collective-permute-start.16) | collective-permute-done | bytes 131104 | tf_op jit(solution)/shard_map/ppermute | solution.py:186
  35.7 0.1 fusion.2
  35.8 1.8 %collective-permute-start.17 = (bf16[8,8192]{1,0:T(8,128)(2,1)S(1)}, bf16[8,8192]{1,0:T(8,128)(2,1)S(1)}, u32[]{:S(2)}, u32[]{:S(2)}) collective-permute-start(bf16[8,8192]{1,0:T(8,128)(2,1)S(1)} %fusion.2), channel_id=1, source_target_pairs={{0,8},{1,9},{2,10},{3,11},{4,12},{5,13},{6,14},{7,15},{8,0},{9,1},... | collective-permute-start | bytes 393224 | tf_op jit(solution)/shard_map/ppermute | solution.py:186
  37.6 0.4 collective-permute-done.12
  38.0 0.1 slice_add_fusion
  38.1 0.9 %collective-permute-start.18 = (bf16[8,8192]{1,0:T(8,128)(2,1)S(1)}, bf16[8,8192]{1,0:T(8,128)(2,1)S(1)}, u32[]{:S(2)}, u32[]{:S(2)}) collective-permute-start(bf16[8,8192]{1,0:T(8,128)(2,1)S(1)} %slice.84), channel_id=1, source_target_pairs={{0,2},{1,5},{2,0},{3,7},{4,6},{5,1},{6,4},{7,3},{8,10},{9,13},{10,... | collective-permute-start | bytes 393224 | tf_op jit(solution)/shard_map/ppermute | solution.py:186
  39.1 4.8 %collective-permute-done.17.refs_1_ = bf16[8,8192]{1,0:T(8,128)(2,1)S(1)} collective-permute-done((bf16[8,8192]{1,0:T(8,128)(2,1)S(1)}, bf16[8,8192]{1,0:T(8,128)(2,1)S(1)}, u32[]{:S(2)}, u32[]{:S(2)}) %collective-permute-start.17) | collective-permute-done | bytes 131104 | tf_op jit(solution)/shard_map/ppermute | solution.py:186
  43.9 0.0 collective-permute-done.18.refs_2_
  44.0 0.0 copy-done
  44.0 0.9 %shard_map.59 = bf16[8,8192]{1,0:T(8,128)(2,1)} custom-call(f32[8,8192]{1,0:T(8,128)S(1)} %slice.68.refs_0_, bf16[8,8192]{1,0:T(8,128)(2,1)S(1)} %collective-permute-done.17.refs_1_, bf16[8,8192]{1,0:T(8,128)(2,1)S(1)} %collective-permute-done.18.refs_2_, s32[1,8192]{1,0:T(1,128)S(1)} %bitcast.3, bf16[256,128]{1,0:T(8,128)(2,1)S(1)} %pad_maximum_fusion.2.refs_4_), custom_call_target="tpu_custom_call" | custom-call | tf_op jit(solution)/shard_map/pallas_call | solution.py:163
  (15 shorter events, 0.3 us)
Async XLA Ops:
  0.0 10.7 %collective-permute-start = (bf16[8,8192]{1,0:T(8,128)(2,1)}, bf16[8,8192]{1,0:T(8,128)(2,1)S(1)}, u32[]{:S(2)}, u32[]{:S(2)}) collective-permute-start(bf16[8,8192]{1,0:T(8,128)(2,1)} %param.5), channel_id=1, source_target_pairs={{0,8},{1,9},{2,10},{3,11},{4,12},{5,13},{6,14},{7,15},{8,0},{9,1},... | collective-permute-start | bytes 393224 | tf_op jit(solution)/shard_map/ppermute | solution.py:186
  4.0 8.9 %collective-permute-start.1 = (bf16[8,8192]{1,0:T(8,128)(2,1)}, bf16[8,8192]{1,0:T(8,128)(2,1)S(1)}, u32[]{:S(2)}, u32[]{:S(2)}) collective-permute-start(bf16[8,8192]{1,0:T(8,128)(2,1)} %param.5), channel_id=1, source_target_pairs={{0,4},{1,3},{2,6},{3,1},{4,0},{5,7},{6,2},{7,5},{8,12},{9,11},{10,... | collective-permute-start | bytes 393224 | tf_op jit(solution)/shard_map/ppermute | solution.py:186
  5.6 13.2 %collective-permute-start.3 = (bf16[8,8192]{1,0:T(8,128)(2,1)}, bf16[8,8192]{1,0:T(8,128)(2,1)S(1)}, u32[]{:S(2)}, u32[]{:S(2)}) collective-permute-start(bf16[8,8192]{1,0:T(8,128)(2,1)} %param.5), channel_id=1, source_target_pairs={{0,2},{1,5},{2,0},{3,7},{4,6},{5,1},{6,4},{7,3},{8,10},{9,13},{10,... | collective-permute-start | bytes 393224 | tf_op jit(solution)/shard_map/ppermute | solution.py:186
  7.1 11.7 %collective-permute-start.4 = (bf16[8,8192]{1,0:T(8,128)(2,1)}, bf16[8,8192]{1,0:T(8,128)(2,1)S(1)}, u32[]{:S(2)}, u32[]{:S(2)}) collective-permute-start(bf16[8,8192]{1,0:T(8,128)(2,1)} %param.5), channel_id=1, source_target_pairs={{0,6},{1,7},{2,4},{3,5},{4,2},{5,3},{6,0},{7,1},{8,14},{9,15},{10,... | collective-permute-start | bytes 393224 | tf_op jit(solution)/shard_map/ppermute | solution.py:186
  10.7 8.2 %collective-permute-start.2 = (bf16[8,8192]{1,0:T(8,128)(2,1)S(1)}, bf16[8,8192]{1,0:T(8,128)(2,1)S(1)}, u32[]{:S(2)}, u32[]{:S(2)}) collective-permute-start(bf16[8,8192]{1,0:T(8,128)(2,1)S(1)} %collective-permute-done._), channel_id=1, source_target_pairs={{0,4},{1,3},{2,6},{3,1},{4,0},{5,7},{6,2},{7,5},{8,12},{9,11},{10,... | collective-permute-start | bytes 393224 | tf_op jit(solution)/shard_map/ppermute | solution.py:186
  11.4 9.1 %collective-permute-start.5 = (bf16[8,8192]{1,0:T(8,128)(2,1)S(1)}, bf16[8,8192]{1,0:T(8,128)(2,1)S(1)}, u32[]{:S(2)}, u32[]{:S(2)}) collective-permute-start(bf16[8,8192]{1,0:T(8,128)(2,1)S(1)} %collective-permute-done._), channel_id=1, source_target_pairs={{0,2},{1,5},{2,0},{3,7},{4,6},{5,1},{6,4},{7,3},{8,10},{9,13},{10,... | collective-permute-start | bytes 393224 | tf_op jit(solution)/shard_map/ppermute | solution.py:186
  12.9 7.6 %collective-permute-start.6 = (bf16[8,8192]{1,0:T(8,128)(2,1)S(1)}, bf16[8,8192]{1,0:T(8,128)(2,1)S(1)}, u32[]{:S(2)}, u32[]{:S(2)}) collective-permute-start(bf16[8,8192]{1,0:T(8,128)(2,1)S(1)} %collective-permute-done._), channel_id=1, source_target_pairs={{0,6},{1,7},{2,4},{3,5},{4,2},{5,3},{6,0},{7,1},{8,14},{9,15},{10,... | collective-permute-start | bytes 393224 | tf_op jit(solution)/shard_map/ppermute | solution.py:186
  18.9 3.2 %collective-permute-start.7 = (bf16[32,8192]{1,0:T(8,128)(2,1)S(1)}, bf16[32,8192]{1,0:T(8,128)(2,1)S(1)}, u32[]{:S(2)}, u32[]{:S(2)}) collective-permute-start(bf16[32,8192]{1,0:T(8,128)(2,1)S(1)} %constant_dynamic-update-slice_fusion.refs_2_), channel_id=1, source_target_pairs={{0,1},{1,0},{2,3},{3,2},{4,5},{5,4},{6,7},{7,6},{8,9},{9,8},{10,11... | collective-permute-start | bytes 1572872 | tf_op jit(solution)/shard_map/ppermute | solution.py:186
  20.6 1.6 %collective-permute-start.9 = (bf16[32,4096]{1,0:T(8,128)(2,1)S(1)}, bf16[32,4096]{1,0:T(8,128)(2,1)S(1)}, u32[]{:S(2)}, u32[]{:S(2)}) collective-permute-start(bf16[32,4096]{1,0:T(8,128)(2,1)S(1)} %pad_maximum_fusion.1.refs_4_), channel_id=1, source_target_pairs={{0,1},{1,0},{2,3},{3,2},{4,5},{5,4},{6,7},{7,6},{8,9},{9,8},{10,11... | collective-permute-start | bytes 786440 | tf_op jit(solution)/shard_map/ppermute | solution.py:186
  20.7 2.2 %collective-permute-start.8 = (bf16[32,4096]{1,0:T(8,128)(2,1)S(1)}, bf16[32,4096]{1,0:T(8,128)(2,1)S(1)}, u32[]{:S(2)}, u32[]{:S(2)}) collective-permute-start(bf16[32,4096]{1,0:T(8,128)(2,1)S(1)} %pad_maximum_fusion.refs_4_), channel_id=1, source_target_pairs={{0,1},{1,0},{2,3},{3,2},{4,5},{5,4},{6,7},{7,6},{8,9},{9,8},{10,11... | collective-permute-start | bytes 786440 | tf_op jit(solution)/shard_map/ppermute | solution.py:186
  24.4 1.4 %collective-permute-start.13 = (bf16[8,8192]{1,0:T(8,128)(2,1)S(1)}, bf16[8,8192]{1,0:T(8,128)(2,1)S(1)}, u32[]{:S(2)}, u32[]{:S(2)}) collective-permute-start(bf16[8,8192]{1,0:T(8,128)(2,1)S(1)} %get-tuple-element.55), channel_id=1, source_target_pairs={{0,1},{1,0},{2,3},{3,2},{4,5},{5,4},{6,7},{7,6},{8,9},{9,8},{10,11... | collective-permute-start | bytes 393224 | tf_op jit(solution)/shard_map/ppermute | solution.py:186
  24.6 2.5 %collective-permute-start.10 = (bf16[24,8192]{1,0:T(8,128)(2,1)S(1)}, bf16[24,8192]{1,0:T(8,128)(2,1)S(1)}, u32[]{:S(2)}, u32[]{:S(2)}) collective-permute-start(bf16[24,8192]{1,0:T(8,128)(2,1)S(1)} %get-tuple-element.49), channel_id=1, source_target_pairs={{0,1},{1,0},{2,3},{3,2},{4,5},{5,4},{6,7},{7,6},{8,9},{9,8},{10,11... | collective-permute-start | bytes 1179656 | tf_op jit(solution)/shard_map/ppermute | solution.py:186
  25.8 7.2 %collective-permute-start.14 = (bf16[8,8192]{1,0:T(8,128)(2,1)S(1)}, bf16[8,8192]{1,0:T(8,128)(2,1)S(1)}, u32[]{:S(2)}, u32[]{:S(2)}) collective-permute-start(bf16[8,8192]{1,0:T(8,128)(2,1)S(1)} %add_convert_fusion), channel_id=1, source_target_pairs={{0,6},{1,7},{2,4},{3,5},{4,2},{5,3},{6,0},{7,1},{8,14},{9,15},{10,... | collective-permute-start | bytes 393224 | tf_op jit(solution)/shard_map/ppermute | solution.py:186
  27.0 2.5 %collective-permute-start.11 = (bf16[32,8192]{1,0:T(8,128)(2,1)S(1)}, bf16[32,8192]{1,0:T(8,128)(2,1)S(1)}, u32[]{:S(2)}, u32[]{:S(2)}) collective-permute-start(bf16[32,8192]{1,0:T(8,128)(2,1)S(1)} %get-tuple-element.51), channel_id=1, source_target_pairs={{0,1},{1,0},{2,3},{3,2},{4,5},{5,4},{6,7},{7,6},{8,9},{9,8},{10,11... | collective-permute-start | bytes 1572872 | tf_op jit(solution)/shard_map/ppermute | solution.py:186
  27.1 16.8 %copy-start = (s32[8192]{0:T(1024)S(1)}, s32[8192]{0:T(1024)}, u32[]{:S(2)}) copy-start(s32[8192]{0:T(1024)} %param.9) | copy-start | bytes 98308
  27.2 8.0 %collective-permute-start.15 = (bf16[8,8192]{1,0:T(8,128)(2,1)S(1)}, bf16[8,8192]{1,0:T(8,128)(2,1)S(1)}, u32[]{:S(2)}, u32[]{:S(2)}) collective-permute-start(bf16[8,8192]{1,0:T(8,128)(2,1)S(1)} %get-tuple-element.59), channel_id=1, source_target_pairs={{0,4},{1,3},{2,6},{3,1},{4,0},{5,7},{6,2},{7,5},{8,12},{9,11},{10,... | collective-permute-start | bytes 393224 | tf_op jit(solution)/shard_map/ppermute | solution.py:186
  29.1 6.6 %collective-permute-start.16 = (bf16[8,8192]{1,0:T(8,128)(2,1)S(1)}, bf16[8,8192]{1,0:T(8,128)(2,1)S(1)}, u32[]{:S(2)}, u32[]{:S(2)}) collective-permute-start(bf16[8,8192]{1,0:T(8,128)(2,1)S(1)} %get-tuple-element.60), channel_id=1, source_target_pairs={{0,2},{1,5},{2,0},{3,7},{4,6},{5,1},{6,4},{7,3},{8,10},{9,13},{10,... | collective-permute-start | bytes 393224 | tf_op jit(solution)/shard_map/ppermute | solution.py:186
  29.7 8.3 %collective-permute-start.12 = (bf16[16,8192]{1,0:T(8,128)(2,1)S(1)}, bf16[16,8192]{1,0:T(8,128)(2,1)S(1)}, u32[]{:S(2)}, u32[]{:S(2)}) collective-permute-start(bf16[16,8192]{1,0:T(8,128)(2,1)S(1)} %slice.83), channel_id=1, source_target_pairs={{0,4},{1,3},{2,6},{3,1},{4,0},{5,7},{6,2},{7,5},{8,12},{9,11},{10,... | collective-permute-start | bytes 786440 | tf_op jit(solution)/shard_map/ppermute | solution.py:186
  35.8 8.2 %collective-permute-start.17 = (bf16[8,8192]{1,0:T(8,128)(2,1)S(1)}, bf16[8,8192]{1,0:T(8,128)(2,1)S(1)}, u32[]{:S(2)}, u32[]{:S(2)}) collective-permute-start(bf16[8,8192]{1,0:T(8,128)(2,1)S(1)} %fusion.2), channel_id=1, source_target_pairs={{0,8},{1,9},{2,10},{3,11},{4,12},{5,13},{6,14},{7,15},{8,0},{9,1},... | collective-permute-start | bytes 393224 | tf_op jit(solution)/shard_map/ppermute | solution.py:186
  38.1 5.8 %collective-permute-start.18 = (bf16[8,8192]{1,0:T(8,128)(2,1)S(1)}, bf16[8,8192]{1,0:T(8,128)(2,1)S(1)}, u32[]{:S(2)}, u32[]{:S(2)}) collective-permute-start(bf16[8,8192]{1,0:T(8,128)(2,1)S(1)} %slice.84), channel_id=1, source_target_pairs={{0,2},{1,5},{2,0},{3,7},{4,6},{5,1},{6,4},{7,3},{8,10},{9,13},{10,... | collective-permute-start | bytes 393224 | tf_op jit(solution)/shard_map/ppermute | solution.py:186

commit v17 on v16

--- a/solution.py
+++ b/solution.py
@@ -177,20 +177,26 @@
     square = ((4, 2), (2, 4), (6, 6))
     far = []
     mask = members // 2
-    while mask > 4:
+    while mask > 8:
         far.append((mask, mask))
         mask //= 2
+    far.append((12, 8))
     others = members // 8 - 1
 
     def swap(value, masks):
         return lax.ppermute(value, "gx", [(i, i ^ masks[i % 2]) for i in range(members)])
 
+    def swap_far(value, masks):
+        firsts = range(0, mesh.shape["groups"] * members, members)
+        pairs = [(g + i, g + (i ^ masks[g // members % 2])) for g in firsts for i in range(members)]
+        return lax.ppermute(value, ("groups", "gx"), pairs)
+
     def on_device(tokens, gate_weight, up_weight, down_weight, sign_pattern):
         rows, features = tokens.shape
 
         away = []
         for masks in far:
-            away.append(swap(jnp.concatenate([tokens] + away), masks))
+            away.append(swap_far(jnp.concatenate([tokens] + away), masks))
         away = jnp.concatenate(away)
         near = [swap(tokens, m) for m in square]
         away, sign_pattern = lax.optimization_barrier((away, sign_pattern))
@@ -223,7 +229,7 @@
         arrived = []
         for masks in reversed(far):
             split = total.shape[0] // 2 // rows * rows
-            piece = swap(total[split:].astype(jnp.bfloat16), masks)
+            piece = swap_far(total[split:].astype(jnp.bfloat16), masks)
             arrived.append(piece[:rows])
             total = total[:split] + piece[rows:].astype(jnp.float32)
 

time: 45 us -> 45.1 us (level)
  starting transfers between devices: 20.2 us -> 24.4 us
  waiting for transfers between devices: 15.4 us -> 11.4 us
    ppermute x19 -> x17, waiting for transfers between devices: 15.4 us -> 6.59 us  [swap(): lax.ppermute(value, 'gx', [(i, i ^ masks[i % 2]) for i in range(members)])]
    ppermute x0 -> x2, starting transfers between devices: none -> 7.41 us  [swap_far(): return lax.ppermute(value, ('groups', 'gx'), pairs)]
    ppermute x0 -> x2, waiting for transfers between devices: none -> 4.82 us  [swap_far(): return lax.ppermute(value, ('groups', 'gx'), pairs)]
    ppermute x19 -> x17, starting transfers between devices: 20.2 us -> 17 us  [swap(): lax.ppermute(value, 'gx', [(i, i ^ masks[i % 2]) for i in range(members)])]
  transfers between devices with their start and end apart: 19 -> 19, of which waited for: 9 -> 8; matrix products, arithmetic and copies ran while one was open for 3% -> 3% of each run, Pallas kernels for 11% -> 11%
where the time goes in v17:
time: 45.1 us; the launch traced here: 45 us
  starting transfers between devices  24.4 us (54%)
  waiting for transfers between devices  11.4 us (25%)
  Pallas kernels  7.5 us (17%)
  local copies, waits for them, and re-layouts  1.11 us (2%)
    ppermute x17, starting transfers between devices, swap(): lax.ppermute(value, 'gx', [(i, i ^ masks[i % 2]) for i in range(members)])  17 us
    ppermute x2, starting transfers between devices, swap_far(): return lax.ppermute(value, ('groups', 'gx'), pairs)  7.41 us
    ppermute x17, waiting for transfers between devices, swap(): lax.ppermute(value, 'gx', [(i, i ^ masks[i % 2]) for i in range(members)])  6.59 us
    ppermute x2, waiting for transfers between devices, swap_far(): return lax.ppermute(value, ('groups', 'gx'), pairs)  4.82 us
    pallas_call x1, Pallas kernels, load(): pl.pallas_call(load_kernel, out_shape=(shape, shape, jax.ShapeDtypeStruct...  4.44 us
    pallas_call x2, Pallas kernels, hidden_units(): pl.pallas_call(functools.partial(hidden_kernel, start, last), out_shape=(...  1.45 us
    unnamed x5, local copies, waits for them, and re-layouts  0.97 us
  transfers between devices with their start and end apart: 19, of which 8 were waited for; matrix products, arithmetic and copies ran while one was open for 3% of the time, Pallas kernels for 11%

profile of v17, /device:TPU:0, one launch (start us, length us, event | category | flops | bytes accessed | tf_op | source)
XLA Modules:
  0.0 45.0 jit_solution(5536651861387504530)
XLA Ops:
  0.0 5.0 %collective-permute-start = (bf16[8,8192]{1,0:T(8,128)(2,1)}, bf16[8,8192]{1,0:T(8,128)(2,1)S(1)}, u32[]{:S(2)}, u32[]{:S(2)}) collective-permute-start(bf16[8,8192]{1,0:T(8,128)(2,1)} %param.5), channel_id=1, source_target_pairs={{0,12},{1,13},{2,14},{3,15},{4,8},{5,9},{6,10},{7,11},{8,4},{9,5},... | collective-permute-start | bytes 393224 | tf_op jit(solution)/shard_map/ppermute | solution.py:192
  5.0 0.0 collective-permute-start.1
  5.1 1.5 %collective-permute-start.3 = (bf16[8,8192]{1,0:T(8,128)(2,1)}, bf16[8,8192]{1,0:T(8,128)(2,1)S(1)}, u32[]{:S(2)}, u32[]{:S(2)}) collective-permute-start(bf16[8,8192]{1,0:T(8,128)(2,1)} %param.5), channel_id=1, source_target_pairs={{0,2},{1,5},{2,0},{3,7},{4,6},{5,1},{6,4},{7,3},{8,10},{9,13},{10,... | collective-permute-start | bytes 393224 | tf_op jit(solution)/shard_map/ppermute | solution.py:187
  6.6 2.0 %collective-permute-start.4 = (bf16[8,8192]{1,0:T(8,128)(2,1)}, bf16[8,8192]{1,0:T(8,128)(2,1)S(1)}, u32[]{:S(2)}, u32[]{:S(2)}) collective-permute-start(bf16[8,8192]{1,0:T(8,128)(2,1)} %param.5), channel_id=1, source_target_pairs={{0,6},{1,7},{2,4},{3,5},{4,2},{5,3},{6,0},{7,1},{8,14},{9,15},{10,... | collective-permute-start | bytes 393224 | tf_op jit(solution)/shard_map/ppermute | solution.py:187
  8.5 0.9 %constant_dynamic-update-slice_fusion.3 = bf16[32,8192]{1,0:T(8,128)(2,1)S(1)} fusion(bf16[8,8192]{1,0:T(8,128)(2,1)} %param.5), kind=kLoop, calls=%fused_computation.23 | loop fusion | bytes 262144
  9.5 0.1 collective-permute-done._
  9.6 1.6 %collective-permute-start.2 = (bf16[8,8192]{1,0:T(8,128)(2,1)S(1)}, bf16[8,8192]{1,0:T(8,128)(2,1)S(1)}, u32[]{:S(2)}, u32[]{:S(2)}) collective-permute-start(bf16[8,8192]{1,0:T(8,128)(2,1)S(1)} %collective-permute-done._), channel_id=1, source_target_pairs={{0,4},{1,3},{2,6},{3,1},{4,0},{5,7},{6,2},{7,5},{8,12},{9,11},{10,... | collective-permute-start | bytes 393224 | tf_op jit(solution)/shard_map/ppermute | solution.py:187
  11.3 1.5 %collective-permute-start.5 = (bf16[8,8192]{1,0:T(8,128)(2,1)S(1)}, bf16[8,8192]{1,0:T(8,128)(2,1)S(1)}, u32[]{:S(2)}, u32[]{:S(2)}) collective-permute-start(bf16[8,8192]{1,0:T(8,128)(2,1)S(1)} %collective-permute-done._), channel_id=1, source_target_pairs={{0,2},{1,5},{2,0},{3,7},{4,6},{5,1},{6,4},{7,3},{8,10},{9,13},{10,... | collective-permute-start | bytes 393224 | tf_op jit(solution)/shard_map/ppermute | solution.py:187
  12.8 0.0 collective-permute-done.1
  12.8 2.6 %collective-permute-start.6 = (bf16[8,8192]{1,0:T(8,128)(2,1)S(1)}, bf16[8,8192]{1,0:T(8,128)(2,1)S(1)}, u32[]{:S(2)}, u32[]{:S(2)}) collective-permute-start(bf16[8,8192]{1,0:T(8,128)(2,1)S(1)} %collective-permute-done._), channel_id=1, source_target_pairs={{0,6},{1,7},{2,4},{3,5},{4,2},{5,3},{6,0},{7,1},{8,14},{9,15},{10,... | collective-permute-start | bytes 393224 | tf_op jit(solution)/shard_map/ppermute | solution.py:187
  15.4 4.4 %shard_map.55 = (bf16[8192,224]{1,0:T(8,128)(2,1)S(1)}, bf16[8192,224]{1,0:T(8,128)(2,1)S(1)}, bf16[224,8192]{1,0:T(8,128)(2,1)S(1)}) custom-call(bf16[224,8192]{1,0:T(8,128)(2,1)} %bitcast.4, bf16[224,8192]{1,0:T(8,128)(2,1)} %bitcast.5, bf16[224,8192]{1,0:T(8,128)(2,1)} %down_hbm.1, bf16[8,8192]{1,0:T(8,128)(2,1)S(1)} %collective-permute-done._), custom_call_target="tpu_custom_call" | custom-call | bytes 11010048 | tf_op jit(solution)/shard_map/pallas_call | solution.py:45
  19.9 0.0 collective-permute-done.3
  19.9 0.0 collective-permute-done.4
  19.9 0.0 collective-permute-done.2
  20.0 0.1 collective-permute-start.7
  20.0 1.0 %collective-permute-done.6 = bf16[8,8192]{1,0:T(8,128)(2,1)S(1)} collective-permute-done((bf16[8,8192]{1,0:T(8,128)(2,1)S(1)}, bf16[8,8192]{1,0:T(8,128)(2,1)S(1)}, u32[]{:S(2)}, u32[]{:S(2)}) %collective-permute-start.6) | collective-permute-done | bytes 131104 | tf_op jit(solution)/shard_map/ppermute | solution.py:187
  21.0 0.0 collective-permute-done.5
  21.1 0.1 collective-permute-start.9
  21.2 0.6 %collective-permute-start.8 = (bf16[32,4096]{1,0:T(8,128)(2,1)S(1)}, bf16[32,4096]{1,0:T(8,128)(2,1)S(1)}, u32[]{:S(2)}, u32[]{:S(2)}) collective-permute-start(bf16[32,4096]{1,0:T(8,128)(2,1)S(1)} %pad_maximum_fusion.refs_4_), channel_id=1, source_target_pairs={{0,1},{1,0},{2,3},{3,2},{4,5},{5,4},{6,7},{7,6},{8,9},{9,8},{10,11... | collective-permute-start | bytes 786440 | tf_op jit(solution)/shard_map/ppermute | solution.py:187
  21.8 0.9 %collective-permute-done.9.refs_5_ = bf16[32,4096]{1,0:T(8,128)(2,1)S(1)} collective-permute-done((bf16[32,4096]{1,0:T(8,128)(2,1)S(1)}, bf16[32,4096]{1,0:T(8,128)(2,1)S(1)}, u32[]{:S(2)}, u32[]{:S(2)}) %collective-permute-start.9) | collective-permute-done | bytes 262176 | tf_op jit(solution)/shard_map/ppermute | solution.py:187
  22.7 0.0 collective-permute-done.7.refs_3_
  22.7 0.7 %shard_map.56 = (f32[128,224]{1,0:T(8,128)S(1)}, f32[128,224]{1,0:T(8,128)S(1)}) custom-call(bf16[8192,224]{1,0:T(8,128)(2,1)S(1)} %get-tuple-element.39.refs_0_, bf16[8192,224]{1,0:T(8,128)(2,1)S(1)} %get-tuple-element.40.refs_1_, bf16[32,8192]{1,0:T(8,128)(2,1)S(1)} %constant_dynamic-update-slice_fusion.refs_2_, ...), custom_call_target="tpu_custom_call" | custom-call | flops 469762048 | bytes 3670016 | tf_op jit(solution)/shard_map/pallas_call | solution.py:85
  23.4 0.0 collective-permute-done.8.refs_5_
  23.5 0.7 %shard_map.57.hidden_ref = bf16[128,224]{1,0:T(8,128)(2,1)S(1)} custom-call(bf16[8192,224]{1,0:T(8,128)(2,1)S(1)} %get-tuple-element.39.refs_0_, bf16[8192,224]{1,0:T(8,128)(2,1)S(1)} %get-tuple-element.40.refs_1_, bf16[32,8192]{1,0:T(8,128)(2,1)S(1)} %constant_dynamic-update-slice_fusion.refs_2_, bf16[32,8192]{1,0:T(8,128)(2,1)S(1)} %collective-permute-done.7.refs_3_, ...), custom_call_target="tpu_custom_call" | custom-call | flops 469762048 | bytes 3670016 | tf_op jit(solution)/shard_map/pallas_call | solution.py:85
  24.2 0.7 %shard_map.58 = (f32[32,8192]{1,0:T(8,128)S(1)}, f32[8,8192]{1,0:T(8,128)S(1)}, f32[24,8192]{1,0:T(8,128)S(1)}, bf16[32,8192]{1,0:T(8,128)(2,1)S(1)}, bf16[8,819...) custom-call(bf16[128,224]{1,0:T(8,128)(2,1)S(1)} %shard_map.57.hidden_ref, bf16[224,8192]{1,0:T(8,128)(2,1)S(1)} %get-tuple-element.47.down_ref), custom_call_target="tpu_custom_call" | custom-call | flops 469762048 | bytes 3670016 | tf_op jit(solution)/shard_map/pallas_call | solution.py:113
  24.9 0.2 collective-permute-start.13
  25.1 0.4 collective-permute-start.10
  25.5 0.8 %collective-permute-done.13 = bf16[8,8192]{1,0:T(8,128)(2,1)S(1)} collective-permute-done((bf16[8,8192]{1,0:T(8,128)(2,1)S(1)}, bf16[8,8192]{1,0:T(8,128)(2,1)S(1)}, u32[]{:S(2)}, u32[]{:S(2)}) %collective-permute-start.13) | collective-permute-done | bytes 131104 | tf_op jit(solution)/shard_map/ppermute | solution.py:187
  26.4 1.7 %collective-permute-start.14 = (bf16[8,8192]{1,0:T(8,128)(2,1)S(1)}, bf16[8,8192]{1,0:T(8,128)(2,1)S(1)}, u32[]{:S(2)}, u32[]{:S(2)}) collective-permute-start(bf16[8,8192]{1,0:T(8,128)(2,1)S(1)} %add_convert_fusion), channel_id=1, source_target_pairs={{0,6},{1,7},{2,4},{3,5},{4,2},{5,3},{6,0},{7,1},{8,14},{9,15},{10,... | collective-permute-start | bytes 393224 | tf_op jit(solution)/shard_map/ppermute | solution.py:187
  28.0 0.0 collective-permute-done.10
  28.1 0.0 collective-permute-start.11
  28.1 0.1 fusion.7
  28.1 0.0 copy-start
  28.2 0.9 %collective-permute-start.15 = (bf16[8,8192]{1,0:T(8,128)(2,1)S(1)}, bf16[8,8192]{1,0:T(8,128)(2,1)S(1)}, u32[]{:S(2)}, u32[]{:S(2)}) collective-permute-start(bf16[8,8192]{1,0:T(8,128)(2,1)S(1)} %get-tuple-element.59), channel_id=1, source_target_pairs={{0,4},{1,3},{2,6},{3,1},{4,0},{5,7},{6,2},{7,5},{8,12},{9,11},{10,... | collective-permute-start | bytes 393224 | tf_op jit(solution)/shard_map/ppermute | solution.py:187
  29.1 1.0 %collective-permute-start.16 = (bf16[8,8192]{1,0:T(8,128)(2,1)S(1)}, bf16[8,8192]{1,0:T(8,128)(2,1)S(1)}, u32[]{:S(2)}, u32[]{:S(2)}) collective-permute-start(bf16[8,8192]{1,0:T(8,128)(2,1)S(1)} %get-tuple-element.60), channel_id=1, source_target_pairs={{0,2},{1,5},{2,0},{3,7},{4,6},{5,1},{6,4},{7,3},{8,10},{9,13},{10,... | collective-permute-start | bytes 393224 | tf_op jit(solution)/shard_map/ppermute | solution.py:187
  30.1 0.0 collective-permute-done.11
  30.1 0.1 convert_add_fusion
  30.3 1.8 %collective-permute-start.12 = (bf16[16,8192]{1,0:T(8,128)(2,1)S(1)}, bf16[16,8192]{1,0:T(8,128)(2,1)S(1)}, u32[]{:S(2)}, u32[]{:S(2)}) collective-permute-start(bf16[16,8192]{1,0:T(8,128)(2,1)S(1)} %slice.83), channel_id=1, source_target_pairs={{0,4},{1,3},{2,6},{3,1},{4,0},{5,7},{6,2},{7,5},{8,12},{9,11},{10,... | collective-permute-start | bytes 786440 | tf_op jit(solution)/shard_map/ppermute | solution.py:187
  32.0 1.2 %collective-permute-done.14 = bf16[8,8192]{1,0:T(8,128)(2,1)S(1)} collective-permute-done((bf16[8,8192]{1,0:T(8,128)(2,1)S(1)}, bf16[8,8192]{1,0:T(8,128)(2,1)S(1)}, u32[]{:S(2)}, u32[]{:S(2)}) %collective-permute-start.14) | collective-permute-done | bytes 131104 | tf_op jit(solution)/shard_map/ppermute | solution.py:187
  33.2 1.5 %collective-permute-done.15 = bf16[8,8192]{1,0:T(8,128)(2,1)S(1)} collective-permute-done((bf16[8,8192]{1,0:T(8,128)(2,1)S(1)}, bf16[8,8192]{1,0:T(8,128)(2,1)S(1)}, u32[]{:S(2)}, u32[]{:S(2)}) %collective-permute-start.15) | collective-permute-done | bytes 131104 | tf_op jit(solution)/shard_map/ppermute | solution.py:187
  34.6 1.2 %collective-permute-done.16 = bf16[8,8192]{1,0:T(8,128)(2,1)S(1)} collective-permute-done((bf16[8,8192]{1,0:T(8,128)(2,1)S(1)}, bf16[8,8192]{1,0:T(8,128)(2,1)S(1)}, u32[]{:S(2)}, u32[]{:S(2)}) %collective-permute-start.16) | collective-permute-done | bytes 131104 | tf_op jit(solution)/shard_map/ppermute | solution.py:187
  35.8 0.1 fusion.2
  35.8 2.4 %collective-permute-start.17 = (bf16[8,8192]{1,0:T(8,128)(2,1)S(1)}, bf16[8,8192]{1,0:T(8,128)(2,1)S(1)}, u32[]{:S(2)}, u32[]{:S(2)}) collective-permute-start(bf16[8,8192]{1,0:T(8,128)(2,1)S(1)} %fusion.2), channel_id=1, source_target_pairs={{0,12},{1,13},{2,14},{3,15},{4,8},{5,9},{6,10},{7,11},{8,4},{9,5},... | collective-permute-start | bytes 393224 | tf_op jit(solution)/shard_map/ppermute | solution.py:192
  38.2 0.0 collective-permute-done.12
  38.2 0.1 slice_add_fusion
  38.3 1.0 %collective-permute-start.18 = (bf16[8,8192]{1,0:T(8,128)(2,1)S(1)}, bf16[8,8192]{1,0:T(8,128)(2,1)S(1)}, u32[]{:S(2)}, u32[]{:S(2)}) collective-permute-start(bf16[8,8192]{1,0:T(8,128)(2,1)S(1)} %slice.84), channel_id=1, source_target_pairs={{0,2},{1,5},{2,0},{3,7},{4,6},{5,1},{6,4},{7,3},{8,10},{9,13},{10,... | collective-permute-start | bytes 393224 | tf_op jit(solution)/shard_map/ppermute | solution.py:187
  39.4 4.7 %collective-permute-done.17.refs_1_ = bf16[8,8192]{1,0:T(8,128)(2,1)S(1)} collective-permute-done((bf16[8,8192]{1,0:T(8,128)(2,1)S(1)}, bf16[8,8192]{1,0:T(8,128)(2,1)S(1)}, u32[]{:S(2)}, u32[]{:S(2)}) %collective-permute-start.17) | collective-permute-done | bytes 131104 | tf_op jit(solution)/shard_map/ppermute | solution.py:192
  44.1 0.0 collective-permute-done.18.refs_2_
  44.1 0.0 copy-done
  44.1 0.9 %shard_map.59 = bf16[8,8192]{1,0:T(8,128)(2,1)} custom-call(f32[8,8192]{1,0:T(8,128)S(1)} %slice.68.refs_0_, bf16[8,8192]{1,0:T(8,128)(2,1)S(1)} %collective-permute-done.17.refs_1_, bf16[8,8192]{1,0:T(8,128)(2,1)S(1)} %collective-permute-done.18.refs_2_, s32[1,8192]{1,0:T(1,128)S(1)} %bitcast.3, bf16[256,128]{1,0:T(8,128)(2,1)S(1)} %pad_maximum_fusion.2.refs_4_), custom_call_target="tpu_custom_call" | custom-call | tf_op jit(solution)/shard_map/pallas_call | solution.py:163
  (15 shorter events, 0.3 us)
Async XLA Ops:
  0.0 9.6 %collective-permute-start = (bf16[8,8192]{1,0:T(8,128)(2,1)}, bf16[8,8192]{1,0:T(8,128)(2,1)S(1)}, u32[]{:S(2)}, u32[]{:S(2)}) collective-permute-start(bf16[8,8192]{1,0:T(8,128)(2,1)} %param.5), channel_id=1, source_target_pairs={{0,12},{1,13},{2,14},{3,15},{4,8},{5,9},{6,10},{7,11},{8,4},{9,5},... | collective-permute-start | bytes 393224 | tf_op jit(solution)/shard_map/ppermute | solution.py:192
  5.0 7.8 %collective-permute-start.1 = (bf16[8,8192]{1,0:T(8,128)(2,1)}, bf16[8,8192]{1,0:T(8,128)(2,1)S(1)}, u32[]{:S(2)}, u32[]{:S(2)}) collective-permute-start(bf16[8,8192]{1,0:T(8,128)(2,1)} %param.5), channel_id=1, source_target_pairs={{0,4},{1,3},{2,6},{3,1},{4,0},{5,7},{6,2},{7,5},{8,12},{9,11},{10,... | collective-permute-start | bytes 393224 | tf_op jit(solution)/shard_map/ppermute | solution.py:187
  5.1 14.8 %collective-permute-start.3 = (bf16[8,8192]{1,0:T(8,128)(2,1)}, bf16[8,8192]{1,0:T(8,128)(2,1)S(1)}, u32[]{:S(2)}, u32[]{:S(2)}) collective-permute-start(bf16[8,8192]{1,0:T(8,128)(2,1)} %param.5), channel_id=1, source_target_pairs={{0,2},{1,5},{2,0},{3,7},{4,6},{5,1},{6,4},{7,3},{8,10},{9,13},{10,... | collective-permute-start | bytes 393224 | tf_op jit(solution)/shard_map/ppermute | solution.py:187
  6.6 13.3 %collective-permute-start.4 = (bf16[8,8192]{1,0:T(8,128)(2,1)}, bf16[8,8192]{1,0:T(8,128)(2,1)S(1)}, u32[]{:S(2)}, u32[]{:S(2)}) collective-permute-start(bf16[8,8192]{1,0:T(8,128)(2,1)} %param.5), channel_id=1, source_target_pairs={{0,6},{1,7},{2,4},{3,5},{4,2},{5,3},{6,0},{7,1},{8,14},{9,15},{10,... | collective-permute-start | bytes 393224 | tf_op jit(solution)/shard_map/ppermute | solution.py:187
  9.6 10.3 %collective-permute-start.2 = (bf16[8,8192]{1,0:T(8,128)(2,1)S(1)}, bf16[8,8192]{1,0:T(8,128)(2,1)S(1)}, u32[]{:S(2)}, u32[]{:S(2)}) collective-permute-start(bf16[8,8192]{1,0:T(8,128)(2,1)S(1)} %collective-permute-done._), channel_id=1, source_target_pairs={{0,4},{1,3},{2,6},{3,1},{4,0},{5,7},{6,2},{7,5},{8,12},{9,11},{10,... | collective-permute-start | bytes 393224 | tf_op jit(solution)/shard_map/ppermute | solution.py:187
  11.3 9.8 %collective-permute-start.5 = (bf16[8,8192]{1,0:T(8,128)(2,1)S(1)}, bf16[8,8192]{1,0:T(8,128)(2,1)S(1)}, u32[]{:S(2)}, u32[]{:S(2)}) collective-permute-start(bf16[8,8192]{1,0:T(8,128)(2,1)S(1)} %collective-permute-done._), channel_id=1, source_target_pairs={{0,2},{1,5},{2,0},{3,7},{4,6},{5,1},{6,4},{7,3},{8,10},{9,13},{10,... | collective-permute-start | bytes 393224 | tf_op jit(solution)/shard_map/ppermute | solution.py:187
  12.8 8.2 %collective-permute-start.6 = (bf16[8,8192]{1,0:T(8,128)(2,1)S(1)}, bf16[8,8192]{1,0:T(8,128)(2,1)S(1)}, u32[]{:S(2)}, u32[]{:S(2)}) collective-permute-start(bf16[8,8192]{1,0:T(8,128)(2,1)S(1)} %collective-permute-done._), channel_id=1, source_target_pairs={{0,6},{1,7},{2,4},{3,5},{4,2},{5,3},{6,0},{7,1},{8,14},{9,15},{10,... | collective-permute-start | bytes 393224 | tf_op jit(solution)/shard_map/ppermute | solution.py:187
  20.0 2.8 %collective-permute-start.7 = (bf16[32,8192]{1,0:T(8,128)(2,1)S(1)}, bf16[32,8192]{1,0:T(8,128)(2,1)S(1)}, u32[]{:S(2)}, u32[]{:S(2)}) collective-permute-start(bf16[32,8192]{1,0:T(8,128)(2,1)S(1)} %constant_dynamic-update-slice_fusion.refs_2_), channel_id=1, source_target_pairs={{0,1},{1,0},{2,3},{3,2},{4,5},{5,4},{6,7},{7,6},{8,9},{9,8},{10,11... | collective-permute-start | bytes 1572872 | tf_op jit(solution)/shard_map/ppermute | solution.py:187
  21.1 1.6 %collective-permute-start.9 = (bf16[32,4096]{1,0:T(8,128)(2,1)S(1)}, bf16[32,4096]{1,0:T(8,128)(2,1)S(1)}, u32[]{:S(2)}, u32[]{:S(2)}) collective-permute-start(bf16[32,4096]{1,0:T(8,128)(2,1)S(1)} %pad_maximum_fusion.1.refs_4_), channel_id=1, source_target_pairs={{0,1},{1,0},{2,3},{3,2},{4,5},{5,4},{6,7},{7,6},{8,9},{9,8},{10,11... | collective-permute-start | bytes 786440 | tf_op jit(solution)/shard_map/ppermute | solution.py:187
  21.2 2.2 %collective-permute-start.8 = (bf16[32,4096]{1,0:T(8,128)(2,1)S(1)}, bf16[32,4096]{1,0:T(8,128)(2,1)S(1)}, u32[]{:S(2)}, u32[]{:S(2)}) collective-permute-start(bf16[32,4096]{1,0:T(8,128)(2,1)S(1)} %pad_maximum_fusion.refs_4_), channel_id=1, source_target_pairs={{0,1},{1,0},{2,3},{3,2},{4,5},{5,4},{6,7},{7,6},{8,9},{9,8},{10,11... | collective-permute-start | bytes 786440 | tf_op jit(solution)/shard_map/ppermute | solution.py:187
  24.9 1.4 %collective-permute-start.13 = (bf16[8,8192]{1,0:T(8,128)(2,1)S(1)}, bf16[8,8192]{1,0:T(8,128)(2,1)S(1)}, u32[]{:S(2)}, u32[]{:S(2)}) collective-permute-start(bf16[8,8192]{1,0:T(8,128)(2,1)S(1)} %get-tuple-element.55), channel_id=1, source_target_pairs={{0,1},{1,0},{2,3},{3,2},{4,5},{5,4},{6,7},{7,6},{8,9},{9,8},{10,11... | collective-permute-start | bytes 393224 | tf_op jit(solution)/shard_map/ppermute | solution.py:187
  25.1 2.9 %collective-permute-start.10 = (bf16[24,8192]{1,0:T(8,128)(2,1)S(1)}, bf16[24,8192]{1,0:T(8,128)(2,1)S(1)}, u32[]{:S(2)}, u32[]{:S(2)}) collective-permute-start(bf16[24,8192]{1,0:T(8,128)(2,1)S(1)} %get-tuple-element.49), channel_id=1, source_target_pairs={{0,1},{1,0},{2,3},{3,2},{4,5},{5,4},{6,7},{7,6},{8,9},{9,8},{10,11... | collective-permute-start | bytes 1179656 | tf_op jit(solution)/shard_map/ppermute | solution.py:187
  26.4 6.8 %collective-permute-start.14 = (bf16[8,8192]{1,0:T(8,128)(2,1)S(1)}, bf16[8,8192]{1,0:T(8,128)(2,1)S(1)}, u32[]{:S(2)}, u32[]{:S(2)}) collective-permute-start(bf16[8,8192]{1,0:T(8,128)(2,1)S(1)} %add_convert_fusion), channel_id=1, source_target_pairs={{0,6},{1,7},{2,4},{3,5},{4,2},{5,3},{6,0},{7,1},{8,14},{9,15},{10,... | collective-permute-start | bytes 393224 | tf_op jit(solution)/shard_map/ppermute | solution.py:187
  28.1 2.1 %collective-permute-start.11 = (bf16[32,8192]{1,0:T(8,128)(2,1)S(1)}, bf16[32,8192]{1,0:T(8,128)(2,1)S(1)}, u32[]{:S(2)}, u32[]{:S(2)}) collective-permute-start(bf16[32,8192]{1,0:T(8,128)(2,1)S(1)} %get-tuple-element.51), channel_id=1, source_target_pairs={{0,1},{1,0},{2,3},{3,2},{4,5},{5,4},{6,7},{7,6},{8,9},{9,8},{10,11... | collective-permute-start | bytes 1572872 | tf_op jit(solution)/shard_map/ppermute | solution.py:187
  28.1 16.0 %copy-start = (s32[8192]{0:T(1024)S(1)}, s32[8192]{0:T(1024)}, u32[]{:S(2)}) copy-start(s32[8192]{0:T(1024)} %param.9) | copy-start | bytes 98308
  28.2 6.5 %collective-permute-start.15 = (bf16[8,8192]{1,0:T(8,128)(2,1)S(1)}, bf16[8,8192]{1,0:T(8,128)(2,1)S(1)}, u32[]{:S(2)}, u32[]{:S(2)}) collective-permute-start(bf16[8,8192]{1,0:T(8,128)(2,1)S(1)} %get-tuple-element.59), channel_id=1, source_target_pairs={{0,4},{1,3},{2,6},{3,1},{4,0},{5,7},{6,2},{7,5},{8,12},{9,11},{10,... | collective-permute-start | bytes 393224 | tf_op jit(solution)/shard_map/ppermute | solution.py:187
  29.1 6.7 %collective-permute-start.16 = (bf16[8,8192]{1,0:T(8,128)(2,1)S(1)}, bf16[8,8192]{1,0:T(8,128)(2,1)S(1)}, u32[]{:S(2)}, u32[]{:S(2)}) collective-permute-start(bf16[8,8192]{1,0:T(8,128)(2,1)S(1)} %get-tuple-element.60), channel_id=1, source_target_pairs={{0,2},{1,5},{2,0},{3,7},{4,6},{5,1},{6,4},{7,3},{8,10},{9,13},{10,... | collective-permute-start | bytes 393224 | tf_op jit(solution)/shard_map/ppermute | solution.py:187
  30.3 8.0 %collective-permute-start.12 = (bf16[16,8192]{1,0:T(8,128)(2,1)S(1)}, bf16[16,8192]{1,0:T(8,128)(2,1)S(1)}, u32[]{:S(2)}, u32[]{:S(2)}) collective-permute-start(bf16[16,8192]{1,0:T(8,128)(2,1)S(1)} %slice.83), channel_id=1, source_target_pairs={{0,4},{1,3},{2,6},{3,1},{4,0},{5,7},{6,2},{7,5},{8,12},{9,11},{10,... | collective-permute-start | bytes 786440 | tf_op jit(solution)/shard_map/ppermute | solution.py:187
  35.8 8.2 %collective-permute-start.17 = (bf16[8,8192]{1,0:T(8,128)(2,1)S(1)}, bf16[8,8192]{1,0:T(8,128)(2,1)S(1)}, u32[]{:S(2)}, u32[]{:S(2)}) collective-permute-start(bf16[8,8192]{1,0:T(8,128)(2,1)S(1)} %fusion.2), channel_id=1, source_target_pairs={{0,12},{1,13},{2,14},{3,15},{4,8},{5,9},{6,10},{7,11},{8,4},{9,5},... | collective-permute-start | bytes 393224 | tf_op jit(solution)/shard_map/ppermute | solution.py:192
  38.3 5.8 %collective-permute-start.18 = (bf16[8,8192]{1,0:T(8,128)(2,1)S(1)}, bf16[8,8192]{1,0:T(8,128)(2,1)S(1)}, u32[]{:S(2)}, u32[]{:S(2)}) collective-permute-start(bf16[8,8192]{1,0:T(8,128)(2,1)S(1)} %slice.84), channel_id=1, source_target_pairs={{0,2},{1,5},{2,0},{3,7},{4,6},{5,1},{6,4},{7,3},{8,10},{9,13},{10,... | collective-permute-start | bytes 393224 | tf_op jit(solution)/shard_map/ppermute | solution.py:187

commit v18 on v11

--- a/solution.py
+++ b/solution.py
@@ -9,7 +9,6 @@
 from jax.sharding import PartitionSpec as P
 
 BLOCK = 128
-PIECES = 2
 SPANS = 2
 TURNS = 8
 NT = (((1,), (1,)), ((), ()))
@@ -135,29 +134,19 @@
 
 def rotate_kernel(count, *refs):
     total_ref, *arrived = refs[: count + 1]
-    sign_ref, matrix_ref, out_ref, turned_ref, sems = refs[count + 1 :]
+    sign_ref, matrix_ref, out_ref = refs[count + 1 :]
     rows, features = total_ref.shape
-    scale = 1.0 / math.sqrt(BLOCK)
-    width = features // PIECES
-    copies = []
-    for k in range(PIECES):
-        here = slice(k * width, (k + 1) * width)
-        value = total_ref[:, here]
-        for piece in arrived:
-            value = value + piece[:, here].astype(jnp.float32)
-        value = value * sign_ref[:, here].astype(jnp.float32)
-        value = jnp.concatenate([value[:, b : b + BLOCK] for b in range(0, width, BLOCK)])
-        high = value.astype(jnp.bfloat16)
-        low = (value - high.astype(jnp.float32)).astype(jnp.bfloat16)
-        both = jnp.concatenate([high, low], axis=1)
-        turned = jnp.dot(both, matrix_ref[...], preferred_element_type=jnp.float32) * scale
-        for b in range(width // BLOCK):
-            first = k * width + b * BLOCK
-            turned_ref[:, first : first + BLOCK] = turned[b * rows : (b + 1) * rows].astype(jnp.bfloat16)
-        copies.append(pltpu.make_async_copy(turned_ref.at[:, here], out_ref.at[:, here], sems.at[k]))
-        copies[-1].start()
-    for copy in copies:
-        copy.wait()
+    value = total_ref[...]
+    for piece in arrived:
+        value = value + piece[...].astype(jnp.float32)
+    value = value * sign_ref[...].astype(jnp.float32)
+    value = jnp.concatenate([value[:, b : b + BLOCK] for b in range(0, features, BLOCK)])
+    high = value.astype(jnp.bfloat16)
+    low = (value - high.astype(jnp.float32)).astype(jnp.bfloat16)
+    both = jnp.concatenate([high, low], axis=1)
+    turned = jnp.dot(both, matrix_ref[...], preferred_element_type=jnp.float32) * (1.0 / math.sqrt(BLOCK))
+    for b in range(features // BLOCK):
+        out_ref[:, b * BLOCK : (b + 1) * BLOCK] = turned[b * rows : (b + 1) * rows].astype(jnp.bfloat16)
 
 
 def rotate(total, arrived, signs):
@@ -165,8 +154,7 @@
         functools.partial(rotate_kernel, len(arrived)),
         out_shape=jax.ShapeDtypeStruct(total.shape, jnp.bfloat16),
         in_specs=[vmem()] * (len(arrived) + 3),
-        out_specs=pl.BlockSpec(memory_space=pl.ANY),
-        scratch_shapes=[pltpu.VMEM(total.shape, jnp.bfloat16), pltpu.SemaphoreType.DMA((PIECES,))],
+        out_specs=vmem(),
         compiler_params=pltpu.CompilerParams(vmem_limit_bytes=16 << 20),
     )(total, *arrived, signs.reshape(1, -1), signs_twice())
 
@@ -193,29 +181,29 @@
         for masks in far:
             away.append(swap(jnp.concatenate([tokens] + away), masks))
         away = jnp.concatenate(away)
-        near = [swap(tokens, m) for m in square[:2]]
+        near = [swap(tokens, m) for m in square]
+        away, sign_pattern = lax.optimization_barrier((away, sign_pattern))
+        there = [swap(away, m) for m in square[:2]]
+        away, near[0] = lax.optimization_barrier((away, near[0]))
+        there.append(swap(away, square[2]))
         gate_w, up_w, down_w = load(gate_weight.T, up_weight.T, down_weight, away)
-        first = swap(away, square[0])
-        both = swap(jnp.concatenate([away, near[0]]), square[1])
-        diagonal = swap(away, square[2])
-        first, *near = lax.optimization_barrier((first, *near))
-        early = jnp.concatenate([tokens, near[1], near[0], away])
+        there[0], *near = lax.optimization_barrier((there[0], *near))
+        early = jnp.concatenate([tokens, near[1], near[0], near[2], away, there[0]])
         early_there = swap(early, (1, 1))
-        gate_w, up_w, early, both, diagonal = lax.optimization_barrier((gate_w, up_w, early, both, diagonal))
-        count = others * rows
-        late = [both[count:], diagonal, first, both[:count]]
+        gate_w, up_w, early, *there[1:] = lax.optimization_barrier((gate_w, up_w, early, *there[1:]))
         spans = []
         width = features // SPANS
         for k in range(SPANS):
-            span = jnp.concatenate([piece[:, k * width : (k + 1) * width] for piece in late])
+            span = jnp.concatenate([piece[:, k * width : (k + 1) * width] for piece in there[:0:-1]])
             spans.append((span, swap(span, (1, 1))))
         hidden = hidden_units(gate_w, up_w, (early, early_there), spans)
 
-        a, b = 3 * rows, 3 * rows + count
-        own_rows = ((0, a), (b, b + rows))
-        rest_rows = ((a, b), (b + rows + count, b + rows + 3 * count))
+        count = others * rows
+        ends = [4 * rows + k * count for k in range(5)]
         own, diagonal, rest, *sends = down(
-            hidden, down_w, (own_rows, ((b + rows, b + rows + count),), rest_rows)
+            hidden,
+            down_w,
+            (((0, ends[0]),), ((ends[2], ends[3]),), ((ends[0], ends[2]), (ends[3], ends[4]))),
         )
         diagonal = diagonal + swap(sends[1], (1, 1)).astype(jnp.float32)
         diagonal = swap(diagonal.astype(jnp.bfloat16), square[2])

time: 46.2 us -> 45.6 us (0.987)
  waiting for transfers between devices: 17.2 us -> 15 us
  starting transfers between devices: 19.7 us -> 21.3 us
    ppermute x18 -> x19, waiting for transfers between devices: 17.2 us -> 15 us  [swap(): lax.ppermute(value, 'gx', [(i, i ^ masks[i % 2]) for i in range(members)])]
    ppermute x18 -> x19, starting transfers between devices: 19.7 us -> 21.3 us  [swap(): lax.ppermute(value, 'gx', [(i, i ^ masks[i % 2]) for i in range(members)])]
    unnamed x5 -> x7, local copies, waits for them, and re-layouts: 0.97 us -> 0.96 us
  transfers between devices with their start and end apart: 18 -> 19, of which waited for: 10 -> 8; matrix products, arithmetic and copies ran while one was open for 3% -> 3% of each run, Pallas kernels for 11% -> 11%
where the time goes in v18:
time: 45.6 us; the launch traced here: 45.4 us
  starting transfers between devices  21.3 us (47%)
  waiting for transfers between devices  15 us (33%)
  Pallas kernels  7.5 us (16%)
  local copies, waits for them, and re-layouts  1.07 us (2%)
    ppermute x19, starting transfers between devices, swap(): lax.ppermute(value, 'gx', [(i, i ^ masks[i % 2]) for i in range(members)])  21.3 us
    ppermute x19, waiting for transfers between devices, swap(): lax.ppermute(value, 'gx', [(i, i ^ masks[i % 2]) for i in range(members)])  15 us
    pallas_call x1, Pallas kernels, load(): pl.pallas_call(load_kernel, out_shape=(shape, shape, jax.ShapeDtypeStruct...  4.43 us
    pallas_call x2, Pallas kernels, hidden_units(): pl.pallas_call(functools.partial(hidden_kernel, start, last), out_shape=(...  1.45 us
    unnamed x7, local copies, waits for them, and re-layouts  0.96 us
  transfers between devices with their start and end apart: 19, of which 8 were waited for; matrix products, arithmetic and copies ran while one was open for 3% of the time, Pallas kernels for 11%

profile of v18, /device:TPU:0, one launch (start us, length us, event | category | flops | bytes accessed | tf_op | source)
XLA Modules:
  0.0 45.4 jit_solution(1312303270366083470)
XLA Ops:
  0.0 4.0 %collective-permute-start = (bf16[8,8192]{1,0:T(8,128)(2,1)}, bf16[8,8192]{1,0:T(8,128)(2,1)S(1)}, u32[]{:S(2)}, u32[]{:S(2)}) collective-permute-start(bf16[8,8192]{1,0:T(8,128)(2,1)} %param.5), channel_id=1, source_target_pairs={{0,8},{1,9},{2,10},{3,11},{4,12},{5,13},{6,14},{7,15},{8,0},{9,1},... | collective-permute-start | bytes 393224 | tf_op jit(solution)/shard_map/ppermute | solution.py:175
  4.0 1.6 %collective-permute-start.1 = (bf16[8,8192]{1,0:T(8,128)(2,1)}, bf16[8,8192]{1,0:T(8,128)(2,1)S(1)}, u32[]{:S(2)}, u32[]{:S(2)}) collective-permute-start(bf16[8,8192]{1,0:T(8,128)(2,1)} %param.5), channel_id=1, source_target_pairs={{0,4},{1,3},{2,6},{3,1},{4,0},{5,7},{6,2},{7,5},{8,12},{9,11},{10,... | collective-permute-start | bytes 393224 | tf_op jit(solution)/shard_map/ppermute | solution.py:175
  5.6 1.5 %collective-permute-start.3 = (bf16[8,8192]{1,0:T(8,128)(2,1)}, bf16[8,8192]{1,0:T(8,128)(2,1)S(1)}, u32[]{:S(2)}, u32[]{:S(2)}) collective-permute-start(bf16[8,8192]{1,0:T(8,128)(2,1)} %param.5), channel_id=1, source_target_pairs={{0,2},{1,5},{2,0},{3,7},{4,6},{5,1},{6,4},{7,3},{8,10},{9,13},{10,... | collective-permute-start | bytes 393224 | tf_op jit(solution)/shard_map/ppermute | solution.py:175
  7.1 0.4 collective-permute-start.4
  7.5 3.1 %collective-permute-done._ = bf16[8,8192]{1,0:T(8,128)(2,1)S(1)} collective-permute-done((bf16[8,8192]{1,0:T(8,128)(2,1)}, bf16[8,8192]{1,0:T(8,128)(2,1)S(1)}, u32[]{:S(2)}, u32[]{:S(2)}) %collective-permute-start) | collective-permute-done | bytes 131104 | tf_op jit(solution)/shard_map/ppermute | solution.py:175
  10.7 0.8 %collective-permute-start.2 = (bf16[8,8192]{1,0:T(8,128)(2,1)S(1)}, bf16[8,8192]{1,0:T(8,128)(2,1)S(1)}, u32[]{:S(2)}, u32[]{:S(2)}) collective-permute-start(bf16[8,8192]{1,0:T(8,128)(2,1)S(1)} %collective-permute-done._), channel_id=1, source_target_pairs={{0,4},{1,3},{2,6},{3,1},{4,0},{5,7},{6,2},{7,5},{8,12},{9,11},{10,... | collective-permute-start | bytes 393224 | tf_op jit(solution)/shard_map/ppermute | solution.py:175
  11.4 0.9 %constant_dynamic-update-slice_fusion.5 = bf16[48,8192]{1,0:T(8,128)(2,1)S(1)} fusion(bf16[8,8192]{1,0:T(8,128)(2,1)} %param.5), kind=kLoop, calls=%fused_computation.25 | loop fusion | bytes 262144
  12.3 1.6 %collective-permute-start.5 = (bf16[8,8192]{1,0:T(8,128)(2,1)S(1)}, bf16[8,8192]{1,0:T(8,128)(2,1)S(1)}, u32[]{:S(2)}, u32[]{:S(2)}) collective-permute-start(bf16[8,8192]{1,0:T(8,128)(2,1)S(1)} %collective-permute-done._), channel_id=1, source_target_pairs={{0,2},{1,5},{2,0},{3,7},{4,6},{5,1},{6,4},{7,3},{8,10},{9,13},{10,... | collective-permute-start | bytes 393224 | tf_op jit(solution)/shard_map/ppermute | solution.py:175
  13.9 0.0 collective-permute-done.1
  13.9 1.2 %collective-permute-start.6 = (bf16[8,8192]{1,0:T(8,128)(2,1)S(1)}, bf16[8,8192]{1,0:T(8,128)(2,1)S(1)}, u32[]{:S(2)}, u32[]{:S(2)}) collective-permute-start(bf16[8,8192]{1,0:T(8,128)(2,1)S(1)} %collective-permute-done._), channel_id=1, source_target_pairs={{0,6},{1,7},{2,4},{3,5},{4,2},{5,3},{6,0},{7,1},{8,14},{9,15},{10,... | collective-permute-start | bytes 393224 | tf_op jit(solution)/shard_map/ppermute | solution.py:175
  15.1 4.4 %shard_map.55 = (bf16[8192,224]{1,0:T(8,128)(2,1)S(1)}, bf16[8192,224]{1,0:T(8,128)(2,1)S(1)}, bf16[224,8192]{1,0:T(8,128)(2,1)S(1)}) custom-call(bf16[224,8192]{1,0:T(8,128)(2,1)} %bitcast.4, bf16[224,8192]{1,0:T(8,128)(2,1)} %bitcast.5, bf16[224,8192]{1,0:T(8,128)(2,1)} %down_hbm.1, bf16[8,8192]{1,0:T(8,128)(2,1)S(1)} %collective-permute-done._), custom_call_target="tpu_custom_call" | custom-call | bytes 11010048 | tf_op jit(solution)/shard_map/pallas_call | solution.py:44
  19.6 0.0 collective-permute-done.3
  19.6 0.0 collective-permute-done.4
  19.6 0.0 collective-permute-done.2
  19.7 0.1 collective-permute-start.7
  19.8 0.8 %collective-permute-done.6 = bf16[8,8192]{1,0:T(8,128)(2,1)S(1)} collective-permute-done((bf16[8,8192]{1,0:T(8,128)(2,1)S(1)}, bf16[8,8192]{1,0:T(8,128)(2,1)S(1)}, u32[]{:S(2)}, u32[]{:S(2)}) %collective-permute-start.6) | collective-permute-done | bytes 131104 | tf_op jit(solution)/shard_map/ppermute | solution.py:175
  20.6 0.0 collective-permute-done.5
  20.6 0.1 collective-permute-start.9
  20.7 0.6 %collective-permute-start.8 = (bf16[16,4096]{1,0:T(8,128)(2,1)S(1)}, bf16[16,4096]{1,0:T(8,128)(2,1)S(1)}, u32[]{:S(2)}, u32[]{:S(2)}) collective-permute-start(bf16[16,4096]{1,0:T(8,128)(2,1)S(1)} %pad_maximum_fusion.refs_4_), channel_id=1, source_target_pairs={{0,1},{1,0},{2,3},{3,2},{4,5},{5,4},{6,7},{7,6},{8,9},{9,8},{10,11... | collective-permute-start | bytes 393224 | tf_op jit(solution)/shard_map/ppermute | solution.py:175
  21.3 1.0 %collective-permute-done.9.refs_5_ = bf16[16,4096]{1,0:T(8,128)(2,1)S(1)} collective-permute-done((bf16[16,4096]{1,0:T(8,128)(2,1)S(1)}, bf16[16,4096]{1,0:T(8,128)(2,1)S(1)}, u32[]{:S(2)}, u32[]{:S(2)}) %collective-permute-start.9) | collective-permute-done | bytes 131104 | tf_op jit(solution)/shard_map/ppermute | solution.py:175
  22.2 0.0 collective-permute-done.7.refs_3_
  22.2 0.7 %shard_map.56 = (f32[128,224]{1,0:T(8,128)S(1)}, f32[128,224]{1,0:T(8,128)S(1)}) custom-call(bf16[8192,224]{1,0:T(8,128)(2,1)S(1)} %get-tuple-element.40.refs_0_, bf16[8192,224]{1,0:T(8,128)(2,1)S(1)} %get-tuple-element.41.refs_1_, bf16[48,8192]{1,0:T(8,128)(2,1)S(1)} %constant_dynamic-update-slice_fusion.refs_2_, ...), custom_call_target="tpu_custom_call" | custom-call | flops 469762048 | bytes 3670016 | tf_op jit(solution)/shard_map/pallas_call | solution.py:84
  23.0 0.0 collective-permute-done.8.refs_5_
  23.0 0.7 %shard_map.57.hidden_ref = bf16[128,224]{1,0:T(8,128)(2,1)S(1)} custom-call(bf16[8192,224]{1,0:T(8,128)(2,1)S(1)} %get-tuple-element.40.refs_0_, bf16[8192,224]{1,0:T(8,128)(2,1)S(1)} %get-tuple-element.41.refs_1_, bf16[48,8192]{1,0:T(8,128)(2,1)S(1)} %constant_dynamic-update-slice_fusion.refs_2_, bf16[48,8192]{1,0:T(8,128)(2,1)S(1)} %collective-permute-done.7.refs_3_, ...), custom_call_target="tpu_custom_call" | custom-call | flops 469762048 | bytes 3670016 | tf_op jit(solution)/shard_map/pallas_call | solution.py:84
  23.7 0.7 %shard_map.58 = (f32[32,8192]{1,0:T(8,128)S(1)}, f32[8,8192]{1,0:T(8,128)S(1)}, f32[24,8192]{1,0:T(8,128)S(1)}, bf16[32,8192]{1,0:T(8,128)(2,1)S(1)}, bf16[8,819...) custom-call(bf16[128,224]{1,0:T(8,128)(2,1)S(1)} %shard_map.57.hidden_ref, bf16[224,8192]{1,0:T(8,128)(2,1)S(1)} %get-tuple-element.47.down_ref), custom_call_target="tpu_custom_call" | custom-call | flops 469762048 | bytes 3670016 | tf_op jit(solution)/shard_map/pallas_call | solution.py:113
  24.4 0.2 collective-permute-start.13
  24.6 0.4 collective-permute-start.10
  25.0 0.8 %collective-permute-done.13 = bf16[8,8192]{1,0:T(8,128)(2,1)S(1)} collective-permute-done((bf16[8,8192]{1,0:T(8,128)(2,1)S(1)}, bf16[8,8192]{1,0:T(8,128)(2,1)S(1)}, u32[]{:S(2)}, u32[]{:S(2)}) %collective-permute-start.13) | collective-permute-done | bytes 131104 | tf_op jit(solution)/shard_map/ppermute | solution.py:175
  25.9 1.8 %collective-permute-start.14 = (bf16[8,8192]{1,0:T(8,128)(2,1)S(1)}, bf16[8,8192]{1,0:T(8,128)(2,1)S(1)}, u32[]{:S(2)}, u32[]{:S(2)}) collective-permute-start(bf16[8,8192]{1,0:T(8,128)(2,1)S(1)} %add_convert_fusion), channel_id=1, source_target_pairs={{0,6},{1,7},{2,4},{3,5},{4,2},{5,3},{6,0},{7,1},{8,14},{9,15},{10,... | collective-permute-start | bytes 393224 | tf_op jit(solution)/shard_map/ppermute | solution.py:175
  27.7 0.0 collective-permute-done.10
  27.7 0.0 collective-permute-start.11
  27.7 0.1 fusion.7
  27.8 0.0 copy-start
  27.8 1.4 %collective-permute-start.15 = (bf16[8,8192]{1,0:T(8,128)(2,1)S(1)}, bf16[8,8192]{1,0:T(8,128)(2,1)S(1)}, u32[]{:S(2)}, u32[]{:S(2)}) collective-permute-start(bf16[8,8192]{1,0:T(8,128)(2,1)S(1)} %get-tuple-element.59), channel_id=1, source_target_pairs={{0,4},{1,3},{2,6},{3,1},{4,0},{5,7},{6,2},{7,5},{8,12},{9,11},{10,... | collective-permute-start | bytes 393224 | tf_op jit(solution)/shard_map/ppermute | solution.py:175
  29.2 0.5 %collective-permute-start.16 = (bf16[8,8192]{1,0:T(8,128)(2,1)S(1)}, bf16[8,8192]{1,0:T(8,128)(2,1)S(1)}, u32[]{:S(2)}, u32[]{:S(2)}) collective-permute-start(bf16[8,8192]{1,0:T(8,128)(2,1)S(1)} %get-tuple-element.60), channel_id=1, source_target_pairs={{0,2},{1,5},{2,0},{3,7},{4,6},{5,1},{6,4},{7,3},{8,10},{9,13},{10,... | collective-permute-start | bytes 393224 | tf_op jit(solution)/shard_map/ppermute | solution.py:175
  29.6 0.0 collective-permute-done.11
  29.6 0.1 convert_add_fusion
  29.8 1.3 %collective-permute-start.12 = (bf16[16,8192]{1,0:T(8,128)(2,1)S(1)}, bf16[16,8192]{1,0:T(8,128)(2,1)S(1)}, u32[]{:S(2)}, u32[]{:S(2)}) collective-permute-start(bf16[16,8192]{1,0:T(8,128)(2,1)S(1)} %slice.67), channel_id=1, source_target_pairs={{0,4},{1,3},{2,6},{3,1},{4,0},{5,7},{6,2},{7,5},{8,12},{9,11},{10,... | collective-permute-start | bytes 786440 | tf_op jit(solution)/shard_map/ppermute | solution.py:175
  31.1 1.5 %collective-permute-done.14 = bf16[8,8192]{1,0:T(8,128)(2,1)S(1)} collective-permute-done((bf16[8,8192]{1,0:T(8,128)(2,1)S(1)}, bf16[8,8192]{1,0:T(8,128)(2,1)S(1)}, u32[]{:S(2)}, u32[]{:S(2)}) %collective-permute-start.14) | collective-permute-done | bytes 131104 | tf_op jit(solution)/shard_map/ppermute | solution.py:175
  32.6 2.7 %collective-permute-done.15 = bf16[8,8192]{1,0:T(8,128)(2,1)S(1)} collective-permute-done((bf16[8,8192]{1,0:T(8,128)(2,1)S(1)}, bf16[8,8192]{1,0:T(8,128)(2,1)S(1)}, u32[]{:S(2)}, u32[]{:S(2)}) %collective-permute-start.15) | collective-permute-done | bytes 131104 | tf_op jit(solution)/shard_map/ppermute | solution.py:175
  35.3 0.2 collective-permute-done.16
  35.5 0.1 fusion.2
  35.6 2.6 %collective-permute-start.17 = (bf16[8,8192]{1,0:T(8,128)(2,1)S(1)}, bf16[8,8192]{1,0:T(8,128)(2,1)S(1)}, u32[]{:S(2)}, u32[]{:S(2)}) collective-permute-start(bf16[8,8192]{1,0:T(8,128)(2,1)S(1)} %fusion.2), channel_id=1, source_target_pairs={{0,8},{1,9},{2,10},{3,11},{4,12},{5,13},{6,14},{7,15},{8,0},{9,1},... | collective-permute-start | bytes 393224 | tf_op jit(solution)/shard_map/ppermute | solution.py:175
  38.2 0.0 collective-permute-done.12
  38.2 0.1 slice_add_fusion
  38.3 1.4 %collective-permute-start.18 = (bf16[8,8192]{1,0:T(8,128)(2,1)S(1)}, bf16[8,8192]{1,0:T(8,128)(2,1)S(1)}, u32[]{:S(2)}, u32[]{:S(2)}) collective-permute-start(bf16[8,8192]{1,0:T(8,128)(2,1)S(1)} %slice.68), channel_id=1, source_target_pairs={{0,2},{1,5},{2,0},{3,7},{4,6},{5,1},{6,4},{7,3},{8,10},{9,13},{10,... | collective-permute-start | bytes 393224 | tf_op jit(solution)/shard_map/ppermute | solution.py:175
  39.8 4.8 %collective-permute-done.17.refs_1_ = bf16[8,8192]{1,0:T(8,128)(2,1)S(1)} collective-permute-done((bf16[8,8192]{1,0:T(8,128)(2,1)S(1)}, bf16[8,8192]{1,0:T(8,128)(2,1)S(1)}, u32[]{:S(2)}, u32[]{:S(2)}) %collective-permute-start.17) | collective-permute-done | bytes 131104 | tf_op jit(solution)/shard_map/ppermute | solution.py:175
  44.5 0.0 collective-permute-done.18.refs_2_
  44.5 0.0 copy-done
  44.5 0.9 %shard_map.59 = bf16[8,8192]{1,0:T(8,128)(2,1)} custom-call(f32[8,8192]{1,0:T(8,128)S(1)} %slice.52.refs_0_, bf16[8,8192]{1,0:T(8,128)(2,1)S(1)} %collective-permute-done.17.refs_1_, bf16[8,8192]{1,0:T(8,128)(2,1)S(1)} %collective-permute-done.18.refs_2_, s32[1,8192]{1,0:T(1,128)S(1)} %bitcast.3, bf16[256,128]{1,0:T(8,128)(2,1)S(1)} %pad_maximum_fusion.2.refs_4_), custom_call_target="tpu_custom_call" | custom-call | tf_op jit(solution)/shard_map/pallas_call | solution.py:153
  (15 shorter events, 0.2 us)
Async XLA Ops:
  0.0 10.7 %collective-permute-start = (bf16[8,8192]{1,0:T(8,128)(2,1)}, bf16[8,8192]{1,0:T(8,128)(2,1)S(1)}, u32[]{:S(2)}, u32[]{:S(2)}) collective-permute-start(bf16[8,8192]{1,0:T(8,128)(2,1)} %param.5), channel_id=1, source_target_pairs={{0,8},{1,9},{2,10},{3,11},{4,12},{5,13},{6,14},{7,15},{8,0},{9,1},... | collective-permute-start | bytes 393224 | tf_op jit(solution)/shard_map/ppermute | solution.py:175
  4.0 9.9 %collective-permute-start.1 = (bf16[8,8192]{1,0:T(8,128)(2,1)}, bf16[8,8192]{1,0:T(8,128)(2,1)S(1)}, u32[]{:S(2)}, u32[]{:S(2)}) collective-permute-start(bf16[8,8192]{1,0:T(8,128)(2,1)} %param.5), channel_id=1, source_target_pairs={{0,4},{1,3},{2,6},{3,1},{4,0},{5,7},{6,2},{7,5},{8,12},{9,11},{10,... | collective-permute-start | bytes 393224 | tf_op jit(solution)/shard_map/ppermute | solution.py:175
  5.6 14.0 %collective-permute-start.3 = (bf16[8,8192]{1,0:T(8,128)(2,1)}, bf16[8,8192]{1,0:T(8,128)(2,1)S(1)}, u32[]{:S(2)}, u32[]{:S(2)}) collective-permute-start(bf16[8,8192]{1,0:T(8,128)(2,1)} %param.5), channel_id=1, source_target_pairs={{0,2},{1,5},{2,0},{3,7},{4,6},{5,1},{6,4},{7,3},{8,10},{9,13},{10,... | collective-permute-start | bytes 393224 | tf_op jit(solution)/shard_map/ppermute | solution.py:175
  7.1 12.4 %collective-permute-start.4 = (bf16[8,8192]{1,0:T(8,128)(2,1)}, bf16[8,8192]{1,0:T(8,128)(2,1)S(1)}, u32[]{:S(2)}, u32[]{:S(2)}) collective-permute-start(bf16[8,8192]{1,0:T(8,128)(2,1)} %param.5), channel_id=1, source_target_pairs={{0,6},{1,7},{2,4},{3,5},{4,2},{5,3},{6,0},{7,1},{8,14},{9,15},{10,... | collective-permute-start | bytes 393224 | tf_op jit(solution)/shard_map/ppermute | solution.py:175
  10.7 8.9 %collective-permute-start.2 = (bf16[8,8192]{1,0:T(8,128)(2,1)S(1)}, bf16[8,8192]{1,0:T(8,128)(2,1)S(1)}, u32[]{:S(2)}, u32[]{:S(2)}) collective-permute-start(bf16[8,8192]{1,0:T(8,128)(2,1)S(1)} %collective-permute-done._), channel_id=1, source_target_pairs={{0,4},{1,3},{2,6},{3,1},{4,0},{5,7},{6,2},{7,5},{8,12},{9,11},{10,... | collective-permute-start | bytes 393224 | tf_op jit(solution)/shard_map/ppermute | solution.py:175
  12.3 8.2 %collective-permute-start.5 = (bf16[8,8192]{1,0:T(8,128)(2,1)S(1)}, bf16[8,8192]{1,0:T(8,128)(2,1)S(1)}, u32[]{:S(2)}, u32[]{:S(2)}) collective-permute-start(bf16[8,8192]{1,0:T(8,128)(2,1)S(1)} %collective-permute-done._), channel_id=1, source_target_pairs={{0,2},{1,5},{2,0},{3,7},{4,6},{5,1},{6,4},{7,3},{8,10},{9,13},{10,... | collective-permute-start | bytes 393224 | tf_op jit(solution)/shard_map/ppermute | solution.py:175
  13.9 6.6 %collective-permute-start.6 = (bf16[8,8192]{1,0:T(8,128)(2,1)S(1)}, bf16[8,8192]{1,0:T(8,128)(2,1)S(1)}, u32[]{:S(2)}, u32[]{:S(2)}) collective-permute-start(bf16[8,8192]{1,0:T(8,128)(2,1)S(1)} %collective-permute-done._), channel_id=1, source_target_pairs={{0,6},{1,7},{2,4},{3,5},{4,2},{5,3},{6,0},{7,1},{8,14},{9,15},{10,... | collective-permute-start | bytes 393224 | tf_op jit(solution)/shard_map/ppermute | solution.py:175
  19.7 2.5 %collective-permute-start.7 = (bf16[48,8192]{1,0:T(8,128)(2,1)S(1)}, bf16[48,8192]{1,0:T(8,128)(2,1)S(1)}, u32[]{:S(2)}, u32[]{:S(2)}) collective-permute-start(bf16[48,8192]{1,0:T(8,128)(2,1)S(1)} %constant_dynamic-update-slice_fusion.refs_2_), channel_id=1, source_target_pairs={{0,1},{1,0},{2,3},{3,2},{4,5},{5,4},{6,7},{7,6},{8,9},{9,8},{10,11... | collective-permute-start | bytes 2359304 | tf_op jit(solution)/shard_map/ppermute | solution.py:175
  20.6 1.6 %collective-permute-start.9 = (bf16[16,4096]{1,0:T(8,128)(2,1)S(1)}, bf16[16,4096]{1,0:T(8,128)(2,1)S(1)}, u32[]{:S(2)}, u32[]{:S(2)}) collective-permute-start(bf16[16,4096]{1,0:T(8,128)(2,1)S(1)} %pad_maximum_fusion.1.refs_4_), channel_id=1, source_target_pairs={{0,1},{1,0},{2,3},{3,2},{4,5},{5,4},{6,7},{7,6},{8,9},{9,8},{10,11... | collective-permute-start | bytes 393224 | tf_op jit(solution)/shard_map/ppermute | solution.py:175
  20.7 2.3 %collective-permute-start.8 = (bf16[16,4096]{1,0:T(8,128)(2,1)S(1)}, bf16[16,4096]{1,0:T(8,128)(2,1)S(1)}, u32[]{:S(2)}, u32[]{:S(2)}) collective-permute-start(bf16[16,4096]{1,0:T(8,128)(2,1)S(1)} %pad_maximum_fusion.refs_4_), channel_id=1, source_target_pairs={{0,1},{1,0},{2,3},{3,2},{4,5},{5,4},{6,7},{7,6},{8,9},{9,8},{10,11... | collective-permute-start | bytes 393224 | tf_op jit(solution)/shard_map/ppermute | solution.py:175
  24.4 1.4 %collective-permute-start.13 = (bf16[8,8192]{1,0:T(8,128)(2,1)S(1)}, bf16[8,8192]{1,0:T(8,128)(2,1)S(1)}, u32[]{:S(2)}, u32[]{:S(2)}) collective-permute-start(bf16[8,8192]{1,0:T(8,128)(2,1)S(1)} %get-tuple-element.55), channel_id=1, source_target_pairs={{0,1},{1,0},{2,3},{3,2},{4,5},{5,4},{6,7},{7,6},{8,9},{9,8},{10,11... | collective-permute-start | bytes 393224 | tf_op jit(solution)/shard_map/ppermute | solution.py:175
  24.6 3.1 %collective-permute-start.10 = (bf16[24,8192]{1,0:T(8,128)(2,1)S(1)}, bf16[24,8192]{1,0:T(8,128)(2,1)S(1)}, u32[]{:S(2)}, u32[]{:S(2)}) collective-permute-start(bf16[24,8192]{1,0:T(8,128)(2,1)S(1)} %get-tuple-element.49), channel_id=1, source_target_pairs={{0,1},{1,0},{2,3},{3,2},{4,5},{5,4},{6,7},{7,6},{8,9},{9,8},{10,11... | collective-permute-start | bytes 1179656 | tf_op jit(solution)/shard_map/ppermute | solution.py:175
  25.9 6.7 %collective-permute-start.14 = (bf16[8,8192]{1,0:T(8,128)(2,1)S(1)}, bf16[8,8192]{1,0:T(8,128)(2,1)S(1)}, u32[]{:S(2)}, u32[]{:S(2)}) collective-permute-start(bf16[8,8192]{1,0:T(8,128)(2,1)S(1)} %add_convert_fusion), channel_id=1, source_target_pairs={{0,6},{1,7},{2,4},{3,5},{4,2},{5,3},{6,0},{7,1},{8,14},{9,15},{10,... | collective-permute-start | bytes 393224 | tf_op jit(solution)/shard_map/ppermute | solution.py:175
  27.7 2.0 %collective-permute-start.11 = (bf16[32,8192]{1,0:T(8,128)(2,1)S(1)}, bf16[32,8192]{1,0:T(8,128)(2,1)S(1)}, u32[]{:S(2)}, u32[]{:S(2)}) collective-permute-start(bf16[32,8192]{1,0:T(8,128)(2,1)S(1)} %get-tuple-element.51), channel_id=1, source_target_pairs={{0,1},{1,0},{2,3},{3,2},{4,5},{5,4},{6,7},{7,6},{8,9},{9,8},{10,11... | collective-permute-start | bytes 1572872 | tf_op jit(solution)/shard_map/ppermute | solution.py:175
  27.8 16.7 %copy-start = (s32[8192]{0:T(1024)S(1)}, s32[8192]{0:T(1024)}, u32[]{:S(2)}) copy-start(s32[8192]{0:T(1024)} %param.9) | copy-start | bytes 98308
  27.8 7.5 %collective-permute-start.15 = (bf16[8,8192]{1,0:T(8,128)(2,1)S(1)}, bf16[8,8192]{1,0:T(8,128)(2,1)S(1)}, u32[]{:S(2)}, u32[]{:S(2)}) collective-permute-start(bf16[8,8192]{1,0:T(8,128)(2,1)S(1)} %get-tuple-element.59), channel_id=1, source_target_pairs={{0,4},{1,3},{2,6},{3,1},{4,0},{5,7},{6,2},{7,5},{8,12},{9,11},{10,... | collective-permute-start | bytes 393224 | tf_op jit(solution)/shard_map/ppermute | solution.py:175
  29.2 6.4 %collective-permute-start.16 = (bf16[8,8192]{1,0:T(8,128)(2,1)S(1)}, bf16[8,8192]{1,0:T(8,128)(2,1)S(1)}, u32[]{:S(2)}, u32[]{:S(2)}) collective-permute-start(bf16[8,8192]{1,0:T(8,128)(2,1)S(1)} %get-tuple-element.60), channel_id=1, source_target_pairs={{0,2},{1,5},{2,0},{3,7},{4,6},{5,1},{6,4},{7,3},{8,10},{9,13},{10,... | collective-permute-start | bytes 393224 | tf_op jit(solution)/shard_map/ppermute | solution.py:175
  29.8 8.4 %collective-permute-start.12 = (bf16[16,8192]{1,0:T(8,128)(2,1)S(1)}, bf16[16,8192]{1,0:T(8,128)(2,1)S(1)}, u32[]{:S(2)}, u32[]{:S(2)}) collective-permute-start(bf16[16,8192]{1,0:T(8,128)(2,1)S(1)} %slice.67), channel_id=1, source_target_pairs={{0,4},{1,3},{2,6},{3,1},{4,0},{5,7},{6,2},{7,5},{8,12},{9,11},{10,... | collective-permute-start | bytes 786440 | tf_op jit(solution)/shard_map/ppermute | solution.py:175
  35.6 8.9 %collective-permute-start.17 = (bf16[8,8192]{1,0:T(8,128)(2,1)S(1)}, bf16[8,8192]{1,0:T(8,128)(2,1)S(1)}, u32[]{:S(2)}, u32[]{:S(2)}) collective-permute-start(bf16[8,8192]{1,0:T(8,128)(2,1)S(1)} %fusion.2), channel_id=1, source_target_pairs={{0,8},{1,9},{2,10},{3,11},{4,12},{5,13},{6,14},{7,15},{8,0},{9,1},... | collective-permute-start | bytes 393224 | tf_op jit(solution)/shard_map/ppermute | solution.py:175
  38.3 6.2 %collective-permute-start.18 = (bf16[8,8192]{1,0:T(8,128)(2,1)S(1)}, bf16[8,8192]{1,0:T(8,128)(2,1)S(1)}, u32[]{:S(2)}, u32[]{:S(2)}) collective-permute-start(bf16[8,8192]{1,0:T(8,128)(2,1)S(1)} %slice.68), channel_id=1, source_target_pairs={{0,2},{1,5},{2,0},{3,7},{4,6},{5,1},{6,4},{7,3},{8,10},{9,13},{10,... | collective-permute-start | bytes 393224 | tf_op jit(solution)/shard_map/ppermute | solution.py:175

commit v19 on v16

--- a/solution.py
+++ b/solution.py
@@ -9,7 +9,7 @@
 from jax.sharding import PartitionSpec as P
 
 BLOCK = 128
-PIECES = 2
+PARTS = (9, 7)
 SPANS = 2
 TURNS = 8
 NT = (((1,), (1,)), ((), ()))
@@ -132,42 +132,33 @@
     return jnp.concatenate([signs, signs])
 
 
-def rotate_kernel(count, *refs):
-    total_ref, *arrived = refs[: count + 1]
-    sign_ref, matrix_ref, out_ref, turned_ref, sems = refs[count + 1 :]
-    rows, features = total_ref.shape
-    scale = 1.0 / math.sqrt(BLOCK)
-    width = features // PIECES
-    copies = []
-    for k in range(PIECES):
-        here = slice(k * width, (k + 1) * width)
-        value = total_ref[:, here]
-        for piece in arrived:
-            value = value + piece[:, here].astype(jnp.float32)
-        value = value * sign_ref[:, here].astype(jnp.float32)
-        value = jnp.concatenate([value[:, b : b + BLOCK] for b in range(0, width, BLOCK)])
-        high = value.astype(jnp.bfloat16)
-        low = (value - high.astype(jnp.float32)).astype(jnp.bfloat16)
-        both = jnp.concatenate([high, low], axis=1)
-        turned = jnp.dot(both, matrix_ref[...], preferred_element_type=jnp.float32) * scale
-        for b in range(width // BLOCK):
-            first = k * width + b * BLOCK
-            turned_ref[:, first : first + BLOCK] = turned[b * rows : (b + 1) * rows].astype(jnp.bfloat16)
-        copies.append(pltpu.make_async_copy(turned_ref.at[:, here], out_ref.at[:, here], sems.at[k]))
-        copies[-1].start()
-    for copy in copies:
-        copy.wait()
+def rotate_kernel(counts, *refs):
+    total_ref, *refs = refs
+    value = total_ref[...]
+    rows, features = value.shape
+    for count in counts:
+        parts, refs = refs[:count], refs[count:]
+        value = value + jnp.concatenate([part[...] for part in parts], axis=1).astype(jnp.float32)
+    sign_ref, matrix_ref, out_ref = refs
+    value = value * sign_ref[...].astype(jnp.float32)
+    value = jnp.concatenate([value[:, b : b + BLOCK] for b in range(0, features, BLOCK)])
+    high = value.astype(jnp.bfloat16)
+    low = (value - high.astype(jnp.float32)).astype(jnp.bfloat16)
+    both = jnp.concatenate([high, low], axis=1)
+    turned = jnp.dot(both, matrix_ref[...], preferred_element_type=jnp.float32) * (1.0 / math.sqrt(BLOCK))
+    for b in range(features // BLOCK):
+        out_ref[:, b * BLOCK : (b + 1) * BLOCK] = turned[b * rows : (b + 1) * rows].astype(jnp.bfloat16)
 
 
 def rotate(total, arrived, signs):
+    pieces = [piece for parts in arrived for piece in parts]
     return pl.pallas_call(
-        functools.partial(rotate_kernel, len(arrived)),
+        functools.partial(rotate_kernel, [len(parts) for parts in arrived]),
         out_shape=jax.ShapeDtypeStruct(total.shape, jnp.bfloat16),
-        in_specs=[vmem()] * (len(arrived) + 3),
-        out_specs=pl.BlockSpec(memory_space=pl.ANY),
-        scratch_shapes=[pltpu.VMEM(total.shape, jnp.bfloat16), pltpu.SemaphoreType.DMA((PIECES,))],
+        in_specs=[vmem()] * (len(pieces) + 3),
+        out_specs=vmem(),
         compiler_params=pltpu.CompilerParams(vmem_limit_bytes=16 << 20),
-    )(total, *arrived, signs.reshape(1, -1), signs_twice())
+    )(total, *pieces, signs.reshape(1, -1), signs_twice())
 
 
 def solution(mesh):
@@ -213,23 +204,29 @@
         count = others * rows
         own, diagonal, rest, *sends = down(hidden, down_w, (4 * rows, count, 3 * count))
         diagonal = diagonal + swap(sends[1], (1, 1)).astype(jnp.float32)
-        diagonal = swap(diagonal.astype(jnp.bfloat16), square[2])
+        diagonal = diagonal.astype(jnp.bfloat16)
         rest_there, sends[0] = lax.optimization_barrier((swap(sends[2], (1, 1)), sends[0]))
         rest = rest + rest_there.astype(jnp.float32)
         leave = rest[count:].astype(jnp.bfloat16)
-        total = rest[:count]
-        for piece in (diagonal, swap(leave[:count], square[0]), swap(leave[count:], square[1])):
-            total = total + piece.astype(jnp.float32)
-        arrived = []
-        for masks in reversed(far):
-            split = total.shape[0] // 2 // rows * rows
-            piece = swap(total[split:].astype(jnp.bfloat16), masks)
-            arrived.append(piece[:rows])
-            total = total[:split] + piece[rows:].astype(jnp.float32)
+
+        arrived, start = [], 0
+        for share in PARTS:
+            part = slice(start, start + features * share // sum(PARTS))
+            start = part.stop
+            total = rest[:count, part]
+            for masks, piece in zip(square[::-1], (diagonal, leave[count:], leave[:count])):
+                total = total + swap(piece[:, part], masks).astype(jnp.float32)
+            arrived.append([])
+            for masks in reversed(far):
+                split = total.shape[0] // 2 // rows * rows
+                piece = swap(total[split:].astype(jnp.bfloat16), masks)
+                arrived[-1].append(piece[:rows])
+                total = total[:split] + piece[rows:].astype(jnp.float32)
+        arrived = list(zip(*arrived))
 
         own = own + swap(sends[0], (1, 1)).astype(jnp.float32)
         own = own[: 2 * rows] + swap(own[2 * rows :].astype(jnp.bfloat16), square[0]).astype(jnp.float32)
-        arrived.append(swap(own[rows:].astype(jnp.bfloat16), square[1]))
+        arrived.append([swap(own[rows:].astype(jnp.bfloat16), square[1])])
         return rotate(own[:rows], arrived, sign_pattern)
 
     placed = (P(("groups", "gx"), None), P(None, "gx"), P(None, "gx"), P("gx", None), P())

time: 45 us -> 49.9 us (1.11)
  starting transfers between devices: 20.2 us -> 26.4 us
  waiting for transfers between devices: 15.4 us -> 14.1 us
    ppermute x19 -> x23, starting transfers between devices: 20.2 us -> 26.4 us  [swap(): lax.ppermute(value, 'gx', [(i, i ^ masks[i % 2]) for i in range(members)])]
    ppermute x19 -> x23, waiting for transfers between devices: 15.4 us -> 14.1 us  [swap(): lax.ppermute(value, 'gx', [(i, i ^ masks[i % 2]) for i in range(members)])]
  transfers between devices with their start and end apart: 19 -> 23, of which waited for: 9 -> 8; matrix products, arithmetic and copies ran while one was open for 3% -> 3% of each run, Pallas kernels for 11% -> 10%
where the time goes in v19:
time: 49.9 us; the launch traced here: 49.8 us
  starting transfers between devices  26.4 us (53%)
  waiting for transfers between devices  14.1 us (28%)
  Pallas kernels  7.51 us (15%)
  local copies, waits for them, and re-layouts  1.12 us (2%)
    ppermute x23, starting transfers between devices, swap(): lax.ppermute(value, 'gx', [(i, i ^ masks[i % 2]) for i in range(members)])  26.4 us
    ppermute x23, waiting for transfers between devices, swap(): lax.ppermute(value, 'gx', [(i, i ^ masks[i % 2]) for i in range(members)])  14.1 us
    pallas_call x1, Pallas kernels, load(): pl.pallas_call(load_kernel, out_shape=(shape, shape, jax.ShapeDtypeStruct...  4.44 us
    pallas_call x2, Pallas kernels, hidden_units(): pl.pallas_call(functools.partial(hidden_kernel, start, last), out_shape=(...  1.45 us
  transfers between devices with their start and end apart: 23, of which 8 were waited for; matrix products, arithmetic and copies ran while one was open for 3% of the time, Pallas kernels for 10%

profile of v19, /device:TPU:0, one launch (start us, length us, event | category | flops | bytes accessed | tf_op | source)
XLA Modules:
  0.0 49.8 jit_solution(11072174905991579161)
XLA Ops:
  0.0 4.0 %collective-permute-start = (bf16[8,8192]{1,0:T(8,128)(2,1)}, bf16[8,8192]{1,0:T(8,128)(2,1)S(1)}, u32[]{:S(2)}, u32[]{:S(2)}) collective-permute-start(bf16[8,8192]{1,0:T(8,128)(2,1)} %param.5), channel_id=1, source_target_pairs={{0,8},{1,9},{2,10},{3,11},{4,12},{5,13},{6,14},{7,15},{8,0},{9,1},... | collective-permute-start | bytes 393224 | tf_op jit(solution)/shard_map/ppermute | solution.py:177
  4.0 1.6 %collective-permute-start.1 = (bf16[8,8192]{1,0:T(8,128)(2,1)}, bf16[8,8192]{1,0:T(8,128)(2,1)S(1)}, u32[]{:S(2)}, u32[]{:S(2)}) collective-permute-start(bf16[8,8192]{1,0:T(8,128)(2,1)} %param.5), channel_id=1, source_target_pairs={{0,4},{1,3},{2,6},{3,1},{4,0},{5,7},{6,2},{7,5},{8,12},{9,11},{10,... | collective-permute-start | bytes 393224 | tf_op jit(solution)/shard_map/ppermute | solution.py:177
  5.6 1.5 %collective-permute-start.3 = (bf16[8,8192]{1,0:T(8,128)(2,1)}, bf16[8,8192]{1,0:T(8,128)(2,1)S(1)}, u32[]{:S(2)}, u32[]{:S(2)}) collective-permute-start(bf16[8,8192]{1,0:T(8,128)(2,1)} %param.5), channel_id=1, source_target_pairs={{0,2},{1,5},{2,0},{3,7},{4,6},{5,1},{6,4},{7,3},{8,10},{9,13},{10,... | collective-permute-start | bytes 393224 | tf_op jit(solution)/shard_map/ppermute | solution.py:177
  7.1 0.4 collective-permute-start.4
  7.5 0.9 %constant_dynamic-update-slice_fusion.3 = bf16[32,8192]{1,0:T(8,128)(2,1)S(1)} fusion(bf16[8,8192]{1,0:T(8,128)(2,1)} %param.5), kind=kLoop, calls=%fused_computation.27 | loop fusion | bytes 262144
  8.5 2.2 %collective-permute-done._ = bf16[8,8192]{1,0:T(8,128)(2,1)S(1)} collective-permute-done((bf16[8,8192]{1,0:T(8,128)(2,1)}, bf16[8,8192]{1,0:T(8,128)(2,1)S(1)}, u32[]{:S(2)}, u32[]{:S(2)}) %collective-permute-start) | collective-permute-done | bytes 131104 | tf_op jit(solution)/shard_map/ppermute | solution.py:177
  10.7 0.8 %collective-permute-start.2 = (bf16[8,8192]{1,0:T(8,128)(2,1)S(1)}, bf16[8,8192]{1,0:T(8,128)(2,1)S(1)}, u32[]{:S(2)}, u32[]{:S(2)}) collective-permute-start(bf16[8,8192]{1,0:T(8,128)(2,1)S(1)} %collective-permute-done._), channel_id=1, source_target_pairs={{0,4},{1,3},{2,6},{3,1},{4,0},{5,7},{6,2},{7,5},{8,12},{9,11},{10,... | collective-permute-start | bytes 393224 | tf_op jit(solution)/shard_map/ppermute | solution.py:177
  11.4 1.5 %collective-permute-start.5 = (bf16[8,8192]{1,0:T(8,128)(2,1)S(1)}, bf16[8,8192]{1,0:T(8,128)(2,1)S(1)}, u32[]{:S(2)}, u32[]{:S(2)}) collective-permute-start(bf16[8,8192]{1,0:T(8,128)(2,1)S(1)} %collective-permute-done._), channel_id=1, source_target_pairs={{0,2},{1,5},{2,0},{3,7},{4,6},{5,1},{6,4},{7,3},{8,10},{9,13},{10,... | collective-permute-start | bytes 393224 | tf_op jit(solution)/shard_map/ppermute | solution.py:177
  12.9 0.0 collective-permute-done.1
  12.9 1.5 %collective-permute-start.6 = (bf16[8,8192]{1,0:T(8,128)(2,1)S(1)}, bf16[8,8192]{1,0:T(8,128)(2,1)S(1)}, u32[]{:S(2)}, u32[]{:S(2)}) collective-permute-start(bf16[8,8192]{1,0:T(8,128)(2,1)S(1)} %collective-permute-done._), channel_id=1, source_target_pairs={{0,6},{1,7},{2,4},{3,5},{4,2},{5,3},{6,0},{7,1},{8,14},{9,15},{10,... | collective-permute-start | bytes 393224 | tf_op jit(solution)/shard_map/ppermute | solution.py:177
  14.4 4.4 %shard_map.55 = (bf16[8192,224]{1,0:T(8,128)(2,1)S(1)}, bf16[8192,224]{1,0:T(8,128)(2,1)S(1)}, bf16[224,8192]{1,0:T(8,128)(2,1)S(1)}) custom-call(bf16[224,8192]{1,0:T(8,128)(2,1)} %bitcast.4, bf16[224,8192]{1,0:T(8,128)(2,1)} %bitcast.5, bf16[224,8192]{1,0:T(8,128)(2,1)} %down_hbm.1, bf16[8,8192]{1,0:T(8,128)(2,1)S(1)} %collective-permute-done._), custom_call_target="tpu_custom_call" | custom-call | bytes 11010048 | tf_op jit(solution)/shard_map/pallas_call | solution.py:45
  18.9 0.0 collective-permute-done.3
  18.9 0.0 collective-permute-done.4
  18.9 0.0 collective-permute-done.2
  18.9 0.1 collective-permute-start.7
  19.0 1.5 %collective-permute-done.6 = bf16[8,8192]{1,0:T(8,128)(2,1)S(1)} collective-permute-done((bf16[8,8192]{1,0:T(8,128)(2,1)S(1)}, bf16[8,8192]{1,0:T(8,128)(2,1)S(1)}, u32[]{:S(2)}, u32[]{:S(2)}) %collective-permute-start.6) | collective-permute-done | bytes 131104 | tf_op jit(solution)/shard_map/ppermute | solution.py:177
  20.5 0.0 collective-permute-done.5
  20.6 0.1 collective-permute-start.9
  20.7 0.6 %collective-permute-start.8 = (bf16[32,4096]{1,0:T(8,128)(2,1)S(1)}, bf16[32,4096]{1,0:T(8,128)(2,1)S(1)}, u32[]{:S(2)}, u32[]{:S(2)}) collective-permute-start(bf16[32,4096]{1,0:T(8,128)(2,1)S(1)} %pad_maximum_fusion.refs_4_), channel_id=1, source_target_pairs={{0,1},{1,0},{2,3},{3,2},{4,5},{5,4},{6,7},{7,6},{8,9},{9,8},{10,11... | collective-permute-start | bytes 786440 | tf_op jit(solution)/shard_map/ppermute | solution.py:177
  21.2 0.9 %collective-permute-done.9.refs_5_ = bf16[32,4096]{1,0:T(8,128)(2,1)S(1)} collective-permute-done((bf16[32,4096]{1,0:T(8,128)(2,1)S(1)}, bf16[32,4096]{1,0:T(8,128)(2,1)S(1)}, u32[]{:S(2)}, u32[]{:S(2)}) %collective-permute-start.9) | collective-permute-done | bytes 262176 | tf_op jit(solution)/shard_map/ppermute | solution.py:177
  22.2 0.0 collective-permute-done.7.refs_3_
  22.2 0.7 %shard_map.56 = (f32[128,224]{1,0:T(8,128)S(1)}, f32[128,224]{1,0:T(8,128)S(1)}) custom-call(bf16[8192,224]{1,0:T(8,128)(2,1)S(1)} %get-tuple-element.39.refs_0_, bf16[8192,224]{1,0:T(8,128)(2,1)S(1)} %get-tuple-element.40.refs_1_, bf16[32,8192]{1,0:T(8,128)(2,1)S(1)} %constant_dynamic-update-slice_fusion.refs_2_, ...), custom_call_target="tpu_custom_call" | custom-call | flops 469762048 | bytes 3670016 | tf_op jit(solution)/shard_map/pallas_call | solution.py:85
  22.9 0.0 collective-permute-done.8.refs_5_
  22.9 0.7 %shard_map.57.hidden_ref = bf16[128,224]{1,0:T(8,128)(2,1)S(1)} custom-call(bf16[8192,224]{1,0:T(8,128)(2,1)S(1)} %get-tuple-element.39.refs_0_, bf16[8192,224]{1,0:T(8,128)(2,1)S(1)} %get-tuple-element.40.refs_1_, bf16[32,8192]{1,0:T(8,128)(2,1)S(1)} %constant_dynamic-update-slice_fusion.refs_2_, bf16[32,8192]{1,0:T(8,128)(2,1)S(1)} %collective-permute-done.7.refs_3_, ...), custom_call_target="tpu_custom_call" | custom-call | flops 469762048 | bytes 3670016 | tf_op jit(solution)/shard_map/pallas_call | solution.py:85
  23.7 0.7 %shard_map.58 = (f32[32,8192]{1,0:T(8,128)S(1)}, f32[8,8192]{1,0:T(8,128)S(1)}, f32[24,8192]{1,0:T(8,128)S(1)}, bf16[32,8192]{1,0:T(8,128)(2,1)S(1)}, bf16[8,819...) custom-call(bf16[128,224]{1,0:T(8,128)(2,1)S(1)} %shard_map.57.hidden_ref, bf16[224,8192]{1,0:T(8,128)(2,1)S(1)} %get-tuple-element.47.down_ref), custom_call_target="tpu_custom_call" | custom-call | flops 469762048 | bytes 3670016 | tf_op jit(solution)/shard_map/pallas_call | solution.py:113
  24.4 0.2 collective-permute-start.13
  24.6 0.5 collective-permute-start.10
  25.1 0.7 %collective-permute-done.13 = bf16[8,8192]{1,0:T(8,128)(2,1)S(1)} collective-permute-done((bf16[8,8192]{1,0:T(8,128)(2,1)S(1)}, bf16[8,8192]{1,0:T(8,128)(2,1)S(1)}, u32[]{:S(2)}, u32[]{:S(2)}) %collective-permute-start.13) | collective-permute-done | bytes 131104 | tf_op jit(solution)/shard_map/ppermute | solution.py:177
  25.9 1.2 %collective-permute-start.18 = (bf16[8,3584]{1,0:T(8,128)(2,1)S(1)}, bf16[8,3584]{1,0:T(8,128)(2,1)S(1)}, u32[]{:S(2)}, u32[]{:S(2)}) collective-permute-start(bf16[8,3584]{1,0:T(8,128)(2,1)S(1)} %slice.104), channel_id=1, source_target_pairs={{0,6},{1,7},{2,4},{3,5},{4,2},{5,3},{6,0},{7,1},{8,14},{9,15},{10,... | collective-permute-start | bytes 172040 | tf_op jit(solution)/shard_map/ppermute | solution.py:177
  27.1 1.8 %collective-permute-start.14 = (bf16[8,4608]{1,0:T(8,128)(2,1)S(1)}, bf16[8,4608]{1,0:T(8,128)(2,1)S(1)}, u32[]{:S(2)}, u32[]{:S(2)}) collective-permute-start(bf16[8,4608]{1,0:T(8,128)(2,1)S(1)} %slice.100), channel_id=1, source_target_pairs={{0,6},{1,7},{2,4},{3,5},{4,2},{5,3},{6,0},{7,1},{8,14},{9,15},{10,... | collective-permute-start | bytes 221192 | tf_op jit(solution)/shard_map/ppermute | solution.py:177
  28.9 0.0 collective-permute-done.10
  28.9 0.1 fusion.10
  28.9 0.0 copy-start
  29.0 0.1 collective-permute-start.11
  29.1 1.6 %collective-permute-start.19 = (bf16[8,3584]{1,0:T(8,128)(2,1)S(1)}, bf16[8,3584]{1,0:T(8,128)(2,1)S(1)}, u32[]{:S(2)}, u32[]{:S(2)}) collective-permute-start(bf16[8,3584]{1,0:T(8,128)(2,1)S(1)} %get-tuple-element.59), channel_id=1, source_target_pairs={{0,2},{1,5},{2,0},{3,7},{4,6},{5,1},{6,4},{7,3},{8,10},{9,13},{10,... | collective-permute-start | bytes 172040 | tf_op jit(solution)/shard_map/ppermute | solution.py:177
  30.6 0.2 collective-permute-start.20
  30.8 0.1 collective-permute-done.11
  30.9 1.5 %collective-permute-start.15 = (bf16[8,4608]{1,0:T(8,128)(2,1)S(1)}, bf16[8,4608]{1,0:T(8,128)(2,1)S(1)}, u32[]{:S(2)}, u32[]{:S(2)}) collective-permute-start(bf16[8,4608]{1,0:T(8,128)(2,1)S(1)} %get-tuple-element.61), channel_id=1, source_target_pairs={{0,2},{1,5},{2,0},{3,7},{4,6},{5,1},{6,4},{7,3},{8,10},{9,13},{10,... | collective-permute-start | bytes 221192 | tf_op jit(solution)/shard_map/ppermute | solution.py:177
  32.5 0.1 convert_add_fusion
  32.6 0.0 collective-permute-done.18
  32.6 0.8 %collective-permute-start.16 = (bf16[8,4608]{1,0:T(8,128)(2,1)S(1)}, bf16[8,4608]{1,0:T(8,128)(2,1)S(1)}, u32[]{:S(2)}, u32[]{:S(2)}) collective-permute-start(bf16[8,4608]{1,0:T(8,128)(2,1)S(1)} %get-tuple-element.62), channel_id=1, source_target_pairs={{0,4},{1,3},{2,6},{3,1},{4,0},{5,7},{6,2},{7,5},{8,12},{9,11},{10,... | collective-permute-start | bytes 221192 | tf_op jit(solution)/shard_map/ppermute | solution.py:177
  33.4 0.2 collective-permute-done.19
  33.6 1.9 %collective-permute-start.12 = (bf16[16,8192]{1,0:T(8,128)(2,1)S(1)}, bf16[16,8192]{1,0:T(8,128)(2,1)S(1)}, u32[]{:S(2)}, u32[]{:S(2)}) collective-permute-start(bf16[16,8192]{1,0:T(8,128)(2,1)S(1)} %slice.125), channel_id=1, source_target_pairs={{0,4},{1,3},{2,6},{3,1},{4,0},{5,7},{6,2},{7,5},{8,12},{9,11},{10,... | collective-permute-start | bytes 786440 | tf_op jit(solution)/shard_map/ppermute | solution.py:177
  35.5 0.0 collective-permute-done.20
  35.6 1.9 %collective-permute-start.21 = (bf16[8,3584]{1,0:T(8,128)(2,1)S(1)}, bf16[8,3584]{1,0:T(8,128)(2,1)S(1)}, u32[]{:S(2)}, u32[]{:S(2)}) collective-permute-start(bf16[8,3584]{1,0:T(8,128)(2,1)S(1)} %fusion.5), channel_id=1, source_target_pairs={{0,8},{1,9},{2,10},{3,11},{4,12},{5,13},{6,14},{7,15},{8,0},{9,1},... | collective-permute-start | bytes 172040 | tf_op jit(solution)/shard_map/ppermute | solution.py:177
  37.5 3.7 %collective-permute-done.12 = bf16[16,8192]{1,0:T(8,128)(2,1)S(1)} collective-permute-done((bf16[16,8192]{1,0:T(8,128)(2,1)S(1)}, bf16[16,8192]{1,0:T(8,128)(2,1)S(1)}, u32[]{:S(2)}, u32[]{:S(2)}) %collective-permute-start.12) | collective-permute-done | bytes 262176 | tf_op jit(solution)/shard_map/ppermute | solution.py:177
  41.3 1.8 %collective-permute-start.22 = (bf16[8,8192]{1,0:T(8,128)(2,1)S(1)}, bf16[8,8192]{1,0:T(8,128)(2,1)S(1)}, u32[]{:S(2)}, u32[]{:S(2)}) collective-permute-start(bf16[8,8192]{1,0:T(8,128)(2,1)S(1)} %slice.126), channel_id=1, source_target_pairs={{0,2},{1,5},{2,0},{3,7},{4,6},{5,1},{6,4},{7,3},{8,10},{9,13},{10,... | collective-permute-start | bytes 393224 | tf_op jit(solution)/shard_map/ppermute | solution.py:177
  43.0 0.0 collective-permute-done.14
  43.0 0.0 collective-permute-done.15
  43.0 0.0 collective-permute-done.16
  43.1 1.1 %collective-permute-start.17 = (bf16[8,4608]{1,0:T(8,128)(2,1)S(1)}, bf16[8,4608]{1,0:T(8,128)(2,1)S(1)}, u32[]{:S(2)}, u32[]{:S(2)}) collective-permute-start(bf16[8,4608]{1,0:T(8,128)(2,1)S(1)} %fusion.2), channel_id=1, source_target_pairs={{0,8},{1,9},{2,10},{3,11},{4,12},{5,13},{6,14},{7,15},{8,0},{9,1},... | collective-permute-start | bytes 221192 | tf_op jit(solution)/shard_map/ppermute | solution.py:177
  44.2 0.0 collective-permute-done.21.refs_2_
  44.2 4.6 %collective-permute-done.17.refs_1_ = bf16[8,4608]{1,0:T(8,128)(2,1)S(1)} collective-permute-done((bf16[8,4608]{1,0:T(8,128)(2,1)S(1)}, bf16[8,4608]{1,0:T(8,128)(2,1)S(1)}, u32[]{:S(2)}, u32[]{:S(2)}) %collective-permute-start.17) | collective-permute-done | bytes 73760 | tf_op jit(solution)/shard_map/ppermute | solution.py:177
  48.9 0.0 collective-permute-done.22.refs_3_
  48.9 0.0 copy-done
  48.9 0.9 %shard_map.59 = bf16[8,8192]{1,0:T(8,128)(2,1)} custom-call(f32[8,8192]{1,0:T(8,128)S(1)} %slice.98.refs_0_, bf16[8,4608]{1,0:T(8,128)(2,1)S(1)} %collective-permute-done.17.refs_1_, bf16[8,3584]{1,0:T(8,128)(2,1)S(1)} %collective-permute-done.21.refs_2_, bf16[8,8192]{1,0:T(8,128)(2,1)S(1)} %collective-permute-done.22.refs_3_, s32[1,8192]{1,0:T(1,128)S(1)} %bitcast.3, ...), custom_call_target="tpu_custom_call" | custom-call | tf_op jit(solution)/shard_map/pallas_call | solution.py:155
  (21 shorter events, 0.4 us)
Async XLA Ops:
  0.0 10.7 %collective-permute-start = (bf16[8,8192]{1,0:T(8,128)(2,1)}, bf16[8,8192]{1,0:T(8,128)(2,1)S(1)}, u32[]{:S(2)}, u32[]{:S(2)}) collective-permute-start(bf16[8,8192]{1,0:T(8,128)(2,1)} %param.5), channel_id=1, source_target_pairs={{0,8},{1,9},{2,10},{3,11},{4,12},{5,13},{6,14},{7,15},{8,0},{9,1},... | collective-permute-start | bytes 393224 | tf_op jit(solution)/shard_map/ppermute | solution.py:177
  4.0 8.9 %collective-permute-start.1 = (bf16[8,8192]{1,0:T(8,128)(2,1)}, bf16[8,8192]{1,0:T(8,128)(2,1)S(1)}, u32[]{:S(2)}, u32[]{:S(2)}) collective-permute-start(bf16[8,8192]{1,0:T(8,128)(2,1)} %param.5), channel_id=1, source_target_pairs={{0,4},{1,3},{2,6},{3,1},{4,0},{5,7},{6,2},{7,5},{8,12},{9,11},{10,... | collective-permute-start | bytes 393224 | tf_op jit(solution)/shard_map/ppermute | solution.py:177
  5.6 13.2 %collective-permute-start.3 = (bf16[8,8192]{1,0:T(8,128)(2,1)}, bf16[8,8192]{1,0:T(8,128)(2,1)S(1)}, u32[]{:S(2)}, u32[]{:S(2)}) collective-permute-start(bf16[8,8192]{1,0:T(8,128)(2,1)} %param.5), channel_id=1, source_target_pairs={{0,2},{1,5},{2,0},{3,7},{4,6},{5,1},{6,4},{7,3},{8,10},{9,13},{10,... | collective-permute-start | bytes 393224 | tf_op jit(solution)/shard_map/ppermute | solution.py:177
  7.1 11.7 %collective-permute-start.4 = (bf16[8,8192]{1,0:T(8,128)(2,1)}, bf16[8,8192]{1,0:T(8,128)(2,1)S(1)}, u32[]{:S(2)}, u32[]{:S(2)}) collective-permute-start(bf16[8,8192]{1,0:T(8,128)(2,1)} %param.5), channel_id=1, source_target_pairs={{0,6},{1,7},{2,4},{3,5},{4,2},{5,3},{6,0},{7,1},{8,14},{9,15},{10,... | collective-permute-start | bytes 393224 | tf_op jit(solution)/shard_map/ppermute | solution.py:177
  10.7 8.2 %collective-permute-start.2 = (bf16[8,8192]{1,0:T(8,128)(2,1)S(1)}, bf16[8,8192]{1,0:T(8,128)(2,1)S(1)}, u32[]{:S(2)}, u32[]{:S(2)}) collective-permute-start(bf16[8,8192]{1,0:T(8,128)(2,1)S(1)} %collective-permute-done._), channel_id=1, source_target_pairs={{0,4},{1,3},{2,6},{3,1},{4,0},{5,7},{6,2},{7,5},{8,12},{9,11},{10,... | collective-permute-start | bytes 393224 | tf_op jit(solution)/shard_map/ppermute | solution.py:177
  11.4 9.1 %collective-permute-start.5 = (bf16[8,8192]{1,0:T(8,128)(2,1)S(1)}, bf16[8,8192]{1,0:T(8,128)(2,1)S(1)}, u32[]{:S(2)}, u32[]{:S(2)}) collective-permute-start(bf16[8,8192]{1,0:T(8,128)(2,1)S(1)} %collective-permute-done._), channel_id=1, source_target_pairs={{0,2},{1,5},{2,0},{3,7},{4,6},{5,1},{6,4},{7,3},{8,10},{9,13},{10,... | collective-permute-start | bytes 393224 | tf_op jit(solution)/shard_map/ppermute | solution.py:177
  12.9 7.6 %collective-permute-start.6 = (bf16[8,8192]{1,0:T(8,128)(2,1)S(1)}, bf16[8,8192]{1,0:T(8,128)(2,1)S(1)}, u32[]{:S(2)}, u32[]{:S(2)}) collective-permute-start(bf16[8,8192]{1,0:T(8,128)(2,1)S(1)} %collective-permute-done._), channel_id=1, source_target_pairs={{0,6},{1,7},{2,4},{3,5},{4,2},{5,3},{6,0},{7,1},{8,14},{9,15},{10,... | collective-permute-start | bytes 393224 | tf_op jit(solution)/shard_map/ppermute | solution.py:177
  18.9 3.2 %collective-permute-start.7 = (bf16[32,8192]{1,0:T(8,128)(2,1)S(1)}, bf16[32,8192]{1,0:T(8,128)(2,1)S(1)}, u32[]{:S(2)}, u32[]{:S(2)}) collective-permute-start(bf16[32,8192]{1,0:T(8,128)(2,1)S(1)} %constant_dynamic-update-slice_fusion.refs_2_), channel_id=1, source_target_pairs={{0,1},{1,0},{2,3},{3,2},{4,5},{5,4},{6,7},{7,6},{8,9},{9,8},{10,11... | collective-permute-start | bytes 1572872 | tf_op jit(solution)/shard_map/ppermute | solution.py:177
  20.6 1.6 %collective-permute-start.9 = (bf16[32,4096]{1,0:T(8,128)(2,1)S(1)}, bf16[32,4096]{1,0:T(8,128)(2,1)S(1)}, u32[]{:S(2)}, u32[]{:S(2)}) collective-permute-start(bf16[32,4096]{1,0:T(8,128)(2,1)S(1)} %pad_maximum_fusion.1.refs_4_), channel_id=1, source_target_pairs={{0,1},{1,0},{2,3},{3,2},{4,5},{5,4},{6,7},{7,6},{8,9},{9,8},{10,11... | collective-permute-start | bytes 786440 | tf_op jit(solution)/shard_map/ppermute | solution.py:177
  20.7 2.2 %collective-permute-start.8 = (bf16[32,4096]{1,0:T(8,128)(2,1)S(1)}, bf16[32,4096]{1,0:T(8,128)(2,1)S(1)}, u32[]{:S(2)}, u32[]{:S(2)}) collective-permute-start(bf16[32,4096]{1,0:T(8,128)(2,1)S(1)} %pad_maximum_fusion.refs_4_), channel_id=1, source_target_pairs={{0,1},{1,0},{2,3},{3,2},{4,5},{5,4},{6,7},{7,6},{8,9},{9,8},{10,11... | collective-permute-start | bytes 786440 | tf_op jit(solution)/shard_map/ppermute | solution.py:177
  24.4 1.4 %collective-permute-start.13 = (bf16[8,8192]{1,0:T(8,128)(2,1)S(1)}, bf16[8,8192]{1,0:T(8,128)(2,1)S(1)}, u32[]{:S(2)}, u32[]{:S(2)}) collective-permute-start(bf16[8,8192]{1,0:T(8,128)(2,1)S(1)} %get-tuple-element.55), channel_id=1, source_target_pairs={{0,1},{1,0},{2,3},{3,2},{4,5},{5,4},{6,7},{7,6},{8,9},{9,8},{10,11... | collective-permute-start | bytes 393224 | tf_op jit(solution)/shard_map/ppermute | solution.py:177
  24.6 4.2 %collective-permute-start.10 = (bf16[24,8192]{1,0:T(8,128)(2,1)S(1)}, bf16[24,8192]{1,0:T(8,128)(2,1)S(1)}, u32[]{:S(2)}, u32[]{:S(2)}) collective-permute-start(bf16[24,8192]{1,0:T(8,128)(2,1)S(1)} %get-tuple-element.49), channel_id=1, source_target_pairs={{0,1},{1,0},{2,3},{3,2},{4,5},{5,4},{6,7},{7,6},{8,9},{9,8},{10,11... | collective-permute-start | bytes 1179656 | tf_op jit(solution)/shard_map/ppermute | solution.py:177
  25.9 6.7 %collective-permute-start.18 = (bf16[8,3584]{1,0:T(8,128)(2,1)S(1)}, bf16[8,3584]{1,0:T(8,128)(2,1)S(1)}, u32[]{:S(2)}, u32[]{:S(2)}) collective-permute-start(bf16[8,3584]{1,0:T(8,128)(2,1)S(1)} %slice.104), channel_id=1, source_target_pairs={{0,6},{1,7},{2,4},{3,5},{4,2},{5,3},{6,0},{7,1},{8,14},{9,15},{10,... | collective-permute-start | bytes 172040 | tf_op jit(solution)/shard_map/ppermute | solution.py:177
  27.1 16.0 %collective-permute-start.14 = (bf16[8,4608]{1,0:T(8,128)(2,1)S(1)}, bf16[8,4608]{1,0:T(8,128)(2,1)S(1)}, u32[]{:S(2)}, u32[]{:S(2)}) collective-permute-start(bf16[8,4608]{1,0:T(8,128)(2,1)S(1)} %slice.100), channel_id=1, source_target_pairs={{0,6},{1,7},{2,4},{3,5},{4,2},{5,3},{6,0},{7,1},{8,14},{9,15},{10,... | collective-permute-start | bytes 221192 | tf_op jit(solution)/shard_map/ppermute | solution.py:177
  28.9 19.9 %copy-start = (s32[8192]{0:T(1024)S(1)}, s32[8192]{0:T(1024)}, u32[]{:S(2)}) copy-start(s32[8192]{0:T(1024)} %param.9) | copy-start | bytes 98308
  29.0 2.0 %collective-permute-start.11 = (bf16[32,8192]{1,0:T(8,128)(2,1)S(1)}, bf16[32,8192]{1,0:T(8,128)(2,1)S(1)}, u32[]{:S(2)}, u32[]{:S(2)}) collective-permute-start(bf16[32,8192]{1,0:T(8,128)(2,1)S(1)} %get-tuple-element.51), channel_id=1, source_target_pairs={{0,1},{1,0},{2,3},{3,2},{4,5},{5,4},{6,7},{7,6},{8,9},{9,8},{10,11... | collective-permute-start | bytes 1572872 | tf_op jit(solution)/shard_map/ppermute | solution.py:177
  29.1 4.5 %collective-permute-start.19 = (bf16[8,3584]{1,0:T(8,128)(2,1)S(1)}, bf16[8,3584]{1,0:T(8,128)(2,1)S(1)}, u32[]{:S(2)}, u32[]{:S(2)}) collective-permute-start(bf16[8,3584]{1,0:T(8,128)(2,1)S(1)} %get-tuple-element.59), channel_id=1, source_target_pairs={{0,2},{1,5},{2,0},{3,7},{4,6},{5,1},{6,4},{7,3},{8,10},{9,13},{10,... | collective-permute-start | bytes 172040 | tf_op jit(solution)/shard_map/ppermute | solution.py:177
  30.6 4.9 %collective-permute-start.20 = (bf16[8,3584]{1,0:T(8,128)(2,1)S(1)}, bf16[8,3584]{1,0:T(8,128)(2,1)S(1)}, u32[]{:S(2)}, u32[]{:S(2)}) collective-permute-start(bf16[8,3584]{1,0:T(8,128)(2,1)S(1)} %get-tuple-element.60), channel_id=1, source_target_pairs={{0,4},{1,3},{2,6},{3,1},{4,0},{5,7},{6,2},{7,5},{8,12},{9,11},{10,... | collective-permute-start | bytes 172040 | tf_op jit(solution)/shard_map/ppermute | solution.py:177
  30.9 12.1 %collective-permute-start.15 = (bf16[8,4608]{1,0:T(8,128)(2,1)S(1)}, bf16[8,4608]{1,0:T(8,128)(2,1)S(1)}, u32[]{:S(2)}, u32[]{:S(2)}) collective-permute-start(bf16[8,4608]{1,0:T(8,128)(2,1)S(1)} %get-tuple-element.61), channel_id=1, source_target_pairs={{0,2},{1,5},{2,0},{3,7},{4,6},{5,1},{6,4},{7,3},{8,10},{9,13},{10,... | collective-permute-start | bytes 221192 | tf_op jit(solution)/shard_map/ppermute | solution.py:177
  32.6 10.4 %collective-permute-start.16 = (bf16[8,4608]{1,0:T(8,128)(2,1)S(1)}, bf16[8,4608]{1,0:T(8,128)(2,1)S(1)}, u32[]{:S(2)}, u32[]{:S(2)}) collective-permute-start(bf16[8,4608]{1,0:T(8,128)(2,1)S(1)} %get-tuple-element.62), channel_id=1, source_target_pairs={{0,4},{1,3},{2,6},{3,1},{4,0},{5,7},{6,2},{7,5},{8,12},{9,11},{10,... | collective-permute-start | bytes 221192 | tf_op jit(solution)/shard_map/ppermute | solution.py:177
  33.6 7.6 %collective-permute-start.12 = (bf16[16,8192]{1,0:T(8,128)(2,1)S(1)}, bf16[16,8192]{1,0:T(8,128)(2,1)S(1)}, u32[]{:S(2)}, u32[]{:S(2)}) collective-permute-start(bf16[16,8192]{1,0:T(8,128)(2,1)S(1)} %slice.125), channel_id=1, source_target_pairs={{0,4},{1,3},{2,6},{3,1},{4,0},{5,7},{6,2},{7,5},{8,12},{9,11},{10,... | collective-permute-start | bytes 786440 | tf_op jit(solution)/shard_map/ppermute | solution.py:177
  35.6 8.6 %collective-permute-start.21 = (bf16[8,3584]{1,0:T(8,128)(2,1)S(1)}, bf16[8,3584]{1,0:T(8,128)(2,1)S(1)}, u32[]{:S(2)}, u32[]{:S(2)}) collective-permute-start(bf16[8,3584]{1,0:T(8,128)(2,1)S(1)} %fusion.5), channel_id=1, source_target_pairs={{0,8},{1,9},{2,10},{3,11},{4,12},{5,13},{6,14},{7,15},{8,0},{9,1},... | collective-permute-start | bytes 172040 | tf_op jit(solution)/shard_map/ppermute | solution.py:177
  41.3 7.6 %collective-permute-start.22 = (bf16[8,8192]{1,0:T(8,128)(2,1)S(1)}, bf16[8,8192]{1,0:T(8,128)(2,1)S(1)}, u32[]{:S(2)}, u32[]{:S(2)}) collective-permute-start(bf16[8,8192]{1,0:T(8,128)(2,1)S(1)} %slice.126), channel_id=1, source_target_pairs={{0,2},{1,5},{2,0},{3,7},{4,6},{5,1},{6,4},{7,3},{8,10},{9,13},{10,... | collective-permute-start | bytes 393224 | tf_op jit(solution)/shard_map/ppermute | solution.py:177
  43.1 5.8 %collective-permute-start.17 = (bf16[8,4608]{1,0:T(8,128)(2,1)S(1)}, bf16[8,4608]{1,0:T(8,128)(2,1)S(1)}, u32[]{:S(2)}, u32[]{:S(2)}) collective-permute-start(bf16[8,4608]{1,0:T(8,128)(2,1)S(1)} %fusion.2), channel_id=1, source_target_pairs={{0,8},{1,9},{2,10},{3,11},{4,12},{5,13},{6,14},{7,15},{8,0},{9,1},... | collective-permute-start | bytes 221192 | tf_op jit(solution)/shard_map/ppermute | solution.py:177

commit v20 on v18

--- a/solution.py
+++ b/solution.py
@@ -188,7 +188,7 @@
         there.append(swap(away, square[2]))
         gate_w, up_w, down_w = load(gate_weight.T, up_weight.T, down_weight, away)
         there[0], *near = lax.optimization_barrier((there[0], *near))
-        early = jnp.concatenate([tokens, near[1], near[0], near[2], away, there[0]])
+        early = jnp.concatenate([near[1], near[0], near[2], away, there[0], tokens])
         early_there = swap(early, (1, 1))
         gate_w, up_w, early, *there[1:] = lax.optimization_barrier((gate_w, up_w, early, *there[1:]))
         spans = []
@@ -199,12 +199,11 @@
         hidden = hidden_units(gate_w, up_w, (early, early_there), spans)
 
         count = others * rows
-        ends = [4 * rows + k * count for k in range(5)]
-        own, diagonal, rest, *sends = down(
-            hidden,
-            down_w,
-            (((0, ends[0]),), ((ends[2], ends[3]),), ((ends[0], ends[2]), (ends[3], ends[4]))),
-        )
+        ends = [3 * rows, 3 * rows + count, 3 * rows + 2 * count, 4 * rows + 2 * count]
+        ends += [ends[3] + count, ends[3] + 2 * count]
+        own_rows = ((ends[2], ends[3]), (0, ends[0]))
+        rest_rows = ((ends[0], ends[2]), (ends[4], ends[5]))
+        own, diagonal, rest, *sends = down(hidden, down_w, (own_rows, ((ends[3], ends[4]),), rest_rows))
         diagonal = diagonal + swap(sends[1], (1, 1)).astype(jnp.float32)
         diagonal = swap(diagonal.astype(jnp.bfloat16), square[2])
         rest_there, sends[0] = lax.optimization_barrier((swap(sends[2], (1, 1)), sends[0]))

time: 45.6 us -> 44.8 us (0.982)
  starting transfers between devices: 21.3 us -> 20.2 us
  waiting for transfers between devices: 15 us -> 16.1 us
  local copies, waits for them, and re-layouts: 1.07 us -> 0.18 us
    ppermute x19, waiting for transfers between devices: 15 us -> 16.1 us  [swap(): lax.ppermute(value, 'gx', [(i, i ^ masks[i % 2]) for i in range(members)])]
    ppermute x19, starting transfers between devices: 21.3 us -> 20.2 us  [swap(): lax.ppermute(value, 'gx', [(i, i ^ masks[i % 2]) for i in range(members)])]
    unnamed x7 -> x9, local copies, waits for them, and re-layouts: 0.96 us -> 0.06 us
  transfers between devices with their start and end apart: 19 -> 19, of which waited for: 8 -> 9; matrix products, arithmetic and copies ran while one was open for 3% -> 1% of each run, Pallas kernels for 11% -> 12%
where the time goes in v20:
time: 44.8 us; the launch traced here: 44.6 us
  starting transfers between devices  20.2 us (45%)
  waiting for transfers between devices  16.1 us (36%)
  Pallas kernels  7.51 us (17%)
    ppermute x19, starting transfers between devices, swap(): lax.ppermute(value, 'gx', [(i, i ^ masks[i % 2]) for i in range(members)])  20.2 us
    ppermute x19, waiting for transfers between devices, swap(): lax.ppermute(value, 'gx', [(i, i ^ masks[i % 2]) for i in range(members)])  16.1 us
    pallas_call x1, Pallas kernels, load(): pl.pallas_call(load_kernel, out_shape=(shape, shape, jax.ShapeDtypeStruct...  4.46 us
    pallas_call x2, Pallas kernels, hidden_units(): pl.pallas_call(functools.partial(hidden_kernel, start, last), out_shape=(...  1.45 us
  transfers between devices with their start and end apart: 19, of which 9 were waited for; matrix products, arithmetic and copies ran while one was open for 1% of the time, Pallas kernels for 12%

profile of v20, /device:TPU:0, one launch (start us, length us, event | category | flops | bytes accessed | tf_op | source)
XLA Modules:
  0.0 44.6 jit_solution(1411517006758957762)
XLA Ops:
  0.0 4.0 %collective-permute-start = (bf16[8,8192]{1,0:T(8,128)(2,1)}, bf16[8,8192]{1,0:T(8,128)(2,1)S(1)}, u32[]{:S(2)}, u32[]{:S(2)}) collective-permute-start(bf16[8,8192]{1,0:T(8,128)(2,1)} %param.5), channel_id=1, source_target_pairs={{0,8},{1,9},{2,10},{3,11},{4,12},{5,13},{6,14},{7,15},{8,0},{9,1},... | collective-permute-start | bytes 393224 | tf_op jit(solution)/shard_map/ppermute | solution.py:175
  4.0 1.6 %collective-permute-start.1 = (bf16[8,8192]{1,0:T(8,128)(2,1)}, bf16[8,8192]{1,0:T(8,128)(2,1)S(1)}, u32[]{:S(2)}, u32[]{:S(2)}) collective-permute-start(bf16[8,8192]{1,0:T(8,128)(2,1)} %param.5), channel_id=1, source_target_pairs={{0,4},{1,3},{2,6},{3,1},{4,0},{5,7},{6,2},{7,5},{8,12},{9,11},{10,... | collective-permute-start | bytes 393224 | tf_op jit(solution)/shard_map/ppermute | solution.py:175
  5.6 1.5 %collective-permute-start.3 = (bf16[8,8192]{1,0:T(8,128)(2,1)}, bf16[8,8192]{1,0:T(8,128)(2,1)S(1)}, u32[]{:S(2)}, u32[]{:S(2)}) collective-permute-start(bf16[8,8192]{1,0:T(8,128)(2,1)} %param.5), channel_id=1, source_target_pairs={{0,2},{1,5},{2,0},{3,7},{4,6},{5,1},{6,4},{7,3},{8,10},{9,13},{10,... | collective-permute-start | bytes 393224 | tf_op jit(solution)/shard_map/ppermute | solution.py:175
  7.1 0.4 collective-permute-start.4
  7.5 3.1 %collective-permute-done._ = bf16[8,8192]{1,0:T(8,128)(2,1)S(1)} collective-permute-done((bf16[8,8192]{1,0:T(8,128)(2,1)}, bf16[8,8192]{1,0:T(8,128)(2,1)S(1)}, u32[]{:S(2)}, u32[]{:S(2)}) %collective-permute-start) | collective-permute-done | bytes 131104 | tf_op jit(solution)/shard_map/ppermute | solution.py:175
  10.7 0.8 %collective-permute-start.2 = (bf16[8,8192]{1,0:T(8,128)(2,1)S(1)}, bf16[8,8192]{1,0:T(8,128)(2,1)S(1)}, u32[]{:S(2)}, u32[]{:S(2)}) collective-permute-start(bf16[8,8192]{1,0:T(8,128)(2,1)S(1)} %collective-permute-done._), channel_id=1, source_target_pairs={{0,4},{1,3},{2,6},{3,1},{4,0},{5,7},{6,2},{7,5},{8,12},{9,11},{10,... | collective-permute-start | bytes 393224 | tf_op jit(solution)/shard_map/ppermute | solution.py:175
  11.4 1.5 %collective-permute-start.5 = (bf16[8,8192]{1,0:T(8,128)(2,1)S(1)}, bf16[8,8192]{1,0:T(8,128)(2,1)S(1)}, u32[]{:S(2)}, u32[]{:S(2)}) collective-permute-start(bf16[8,8192]{1,0:T(8,128)(2,1)S(1)} %collective-permute-done._), channel_id=1, source_target_pairs={{0,2},{1,5},{2,0},{3,7},{4,6},{5,1},{6,4},{7,3},{8,10},{9,13},{10,... | collective-permute-start | bytes 393224 | tf_op jit(solution)/shard_map/ppermute | solution.py:175
  12.9 0.0 collective-permute-done.1
  12.9 1.5 %collective-permute-start.6 = (bf16[8,8192]{1,0:T(8,128)(2,1)S(1)}, bf16[8,8192]{1,0:T(8,128)(2,1)S(1)}, u32[]{:S(2)}, u32[]{:S(2)}) collective-permute-start(bf16[8,8192]{1,0:T(8,128)(2,1)S(1)} %collective-permute-done._), channel_id=1, source_target_pairs={{0,6},{1,7},{2,4},{3,5},{4,2},{5,3},{6,0},{7,1},{8,14},{9,15},{10,... | collective-permute-start | bytes 393224 | tf_op jit(solution)/shard_map/ppermute | solution.py:175
  14.4 0.0 copy-start.1
  14.4 4.5 %shard_map.55 = (bf16[8192,224]{1,0:T(8,128)(2,1)S(1)}, bf16[8192,224]{1,0:T(8,128)(2,1)S(1)}, bf16[224,8192]{1,0:T(8,128)(2,1)S(1)}) custom-call(bf16[224,8192]{1,0:T(8,128)(2,1)} %bitcast.4, bf16[224,8192]{1,0:T(8,128)(2,1)} %bitcast.5, bf16[224,8192]{1,0:T(8,128)(2,1)} %down_hbm.1, bf16[8,8192]{1,0:T(8,128)(2,1)S(1)} %collective-permute-done._), custom_call_target="tpu_custom_call" | custom-call | bytes 11010048 | tf_op jit(solution)/shard_map/pallas_call | solution.py:44
  18.9 0.0 collective-permute-done.3
  18.9 0.0 collective-permute-done.4
  18.9 0.0 collective-permute-done.2
  19.0 0.0 copy-done.1
  19.0 0.1 collective-permute-start.7
  19.1 1.4 %collective-permute-done.6 = bf16[8,8192]{1,0:T(8,128)(2,1)S(1)} collective-permute-done((bf16[8,8192]{1,0:T(8,128)(2,1)S(1)}, bf16[8,8192]{1,0:T(8,128)(2,1)S(1)}, u32[]{:S(2)}, u32[]{:S(2)}) %collective-permute-start.6) | collective-permute-done | bytes 131104 | tf_op jit(solution)/shard_map/ppermute | solution.py:175
  20.5 0.0 collective-permute-done.5
  20.6 0.1 collective-permute-start.9
  20.7 0.6 %collective-permute-start.8 = (bf16[16,4096]{1,0:T(8,128)(2,1)S(1)}, bf16[16,4096]{1,0:T(8,128)(2,1)S(1)}, u32[]{:S(2)}, u32[]{:S(2)}) collective-permute-start(bf16[16,4096]{1,0:T(8,128)(2,1)S(1)} %pad_maximum_fusion.refs_4_), channel_id=1, source_target_pairs={{0,1},{1,0},{2,3},{3,2},{4,5},{5,4},{6,7},{7,6},{8,9},{9,8},{10,11... | collective-permute-start | bytes 393224 | tf_op jit(solution)/shard_map/ppermute | solution.py:175
  21.2 0.8 %collective-permute-done.9.refs_5_ = bf16[16,4096]{1,0:T(8,128)(2,1)S(1)} collective-permute-done((bf16[16,4096]{1,0:T(8,128)(2,1)S(1)}, bf16[16,4096]{1,0:T(8,128)(2,1)S(1)}, u32[]{:S(2)}, u32[]{:S(2)}) %collective-permute-start.9) | collective-permute-done | bytes 131104 | tf_op jit(solution)/shard_map/ppermute | solution.py:175
  22.0 0.0 collective-permute-done.7.refs_3_
  22.0 0.7 %shard_map.56 = (f32[128,224]{1,0:T(8,128)S(1)}, f32[128,224]{1,0:T(8,128)S(1)}) custom-call(bf16[8192,224]{1,0:T(8,128)(2,1)S(1)} %get-tuple-element.40.refs_0_, bf16[8192,224]{1,0:T(8,128)(2,1)S(1)} %get-tuple-element.41.refs_1_, bf16[48,8192]{1,0:T(8,128)(2,1)S(1)} %constant_dynamic-update-slice_fusion.refs_2_, ...), custom_call_target="tpu_custom_call" | custom-call | flops 469762048 | bytes 3670016 | tf_op jit(solution)/shard_map/pallas_call | solution.py:84
  22.7 0.0 collective-permute-done.8.refs_5_
  22.7 0.7 %shard_map.57.hidden_ref = bf16[128,224]{1,0:T(8,128)(2,1)S(1)} custom-call(bf16[8192,224]{1,0:T(8,128)(2,1)S(1)} %get-tuple-element.40.refs_0_, bf16[8192,224]{1,0:T(8,128)(2,1)S(1)} %get-tuple-element.41.refs_1_, bf16[48,8192]{1,0:T(8,128)(2,1)S(1)} %constant_dynamic-update-slice_fusion.refs_2_, bf16[48,8192]{1,0:T(8,128)(2,1)S(1)} %collective-permute-done.7.refs_3_, ...), custom_call_target="tpu_custom_call" | custom-call | flops 469762048 | bytes 3670016 | tf_op jit(solution)/shard_map/pallas_call | solution.py:84
  23.4 0.7 %shard_map.58 = (f32[32,8192]{1,0:T(8,128)S(1)}, f32[8,8192]{1,0:T(8,128)S(1)}, f32[24,8192]{1,0:T(8,128)S(1)}, bf16[32,8192]{1,0:T(8,128)(2,1)S(1)}, bf16[8,819...) custom-call(bf16[128,224]{1,0:T(8,128)(2,1)S(1)} %shard_map.57.hidden_ref, bf16[224,8192]{1,0:T(8,128)(2,1)S(1)} %get-tuple-element.47.down_ref), custom_call_target="tpu_custom_call" | custom-call | flops 469762048 | bytes 3670016 | tf_op jit(solution)/shard_map/pallas_call | solution.py:113
  24.2 0.2 collective-permute-start.13
  24.4 0.4 collective-permute-start.10
  24.7 0.8 %collective-permute-done.13 = bf16[8,8192]{1,0:T(8,128)(2,1)S(1)} collective-permute-done((bf16[8,8192]{1,0:T(8,128)(2,1)S(1)}, bf16[8,8192]{1,0:T(8,128)(2,1)S(1)}, u32[]{:S(2)}, u32[]{:S(2)}) %collective-permute-start.13) | collective-permute-done | bytes 131104 | tf_op jit(solution)/shard_map/ppermute | solution.py:175
  25.6 1.2 %collective-permute-start.14 = (bf16[8,8192]{1,0:T(8,128)(2,1)S(1)}, bf16[8,8192]{1,0:T(8,128)(2,1)S(1)}, u32[]{:S(2)}, u32[]{:S(2)}) collective-permute-start(bf16[8,8192]{1,0:T(8,128)(2,1)S(1)} %add_convert_fusion), channel_id=1, source_target_pairs={{0,6},{1,7},{2,4},{3,5},{4,2},{5,3},{6,0},{7,1},{8,14},{9,15},{10,... | collective-permute-start | bytes 393224 | tf_op jit(solution)/shard_map/ppermute | solution.py:175
  26.8 0.0 collective-permute-done.10
  26.8 0.0 collective-permute-start.11
  26.8 0.1 fusion.7
  26.9 0.0 copy-start
  26.9 1.9 %collective-permute-start.15 = (bf16[8,8192]{1,0:T(8,128)(2,1)S(1)}, bf16[8,8192]{1,0:T(8,128)(2,1)S(1)}, u32[]{:S(2)}, u32[]{:S(2)}) collective-permute-start(bf16[8,8192]{1,0:T(8,128)(2,1)S(1)} %get-tuple-element.59), channel_id=1, source_target_pairs={{0,4},{1,3},{2,6},{3,1},{4,0},{5,7},{6,2},{7,5},{8,12},{9,11},{10,... | collective-permute-start | bytes 393224 | tf_op jit(solution)/shard_map/ppermute | solution.py:175
  28.8 0.5 %collective-permute-start.16 = (bf16[8,8192]{1,0:T(8,128)(2,1)S(1)}, bf16[8,8192]{1,0:T(8,128)(2,1)S(1)}, u32[]{:S(2)}, u32[]{:S(2)}) collective-permute-start(bf16[8,8192]{1,0:T(8,128)(2,1)S(1)} %get-tuple-element.60), channel_id=1, source_target_pairs={{0,2},{1,5},{2,0},{3,7},{4,6},{5,1},{6,4},{7,3},{8,10},{9,13},{10,... | collective-permute-start | bytes 393224 | tf_op jit(solution)/shard_map/ppermute | solution.py:175
  29.4 0.0 collective-permute-done.11
  29.4 0.1 convert_add_fusion
  29.5 1.3 %collective-permute-start.12 = (bf16[16,8192]{1,0:T(8,128)(2,1)S(1)}, bf16[16,8192]{1,0:T(8,128)(2,1)S(1)}, u32[]{:S(2)}, u32[]{:S(2)}) collective-permute-start(bf16[16,8192]{1,0:T(8,128)(2,1)S(1)} %slice.67), channel_id=1, source_target_pairs={{0,4},{1,3},{2,6},{3,1},{4,0},{5,7},{6,2},{7,5},{8,12},{9,11},{10,... | collective-permute-start | bytes 786440 | tf_op jit(solution)/shard_map/ppermute | solution.py:175
  30.8 2.1 %collective-permute-done.14 = bf16[8,8192]{1,0:T(8,128)(2,1)S(1)} collective-permute-done((bf16[8,8192]{1,0:T(8,128)(2,1)S(1)}, bf16[8,8192]{1,0:T(8,128)(2,1)S(1)}, u32[]{:S(2)}, u32[]{:S(2)}) %collective-permute-start.14) | collective-permute-done | bytes 131104 | tf_op jit(solution)/shard_map/ppermute | solution.py:175
  32.8 2.1 %collective-permute-done.15 = bf16[8,8192]{1,0:T(8,128)(2,1)S(1)} collective-permute-done((bf16[8,8192]{1,0:T(8,128)(2,1)S(1)}, bf16[8,8192]{1,0:T(8,128)(2,1)S(1)}, u32[]{:S(2)}, u32[]{:S(2)}) %collective-permute-start.15) | collective-permute-done | bytes 131104 | tf_op jit(solution)/shard_map/ppermute | solution.py:175
  35.0 0.5 %collective-permute-done.16 = bf16[8,8192]{1,0:T(8,128)(2,1)S(1)} collective-permute-done((bf16[8,8192]{1,0:T(8,128)(2,1)S(1)}, bf16[8,8192]{1,0:T(8,128)(2,1)S(1)}, u32[]{:S(2)}, u32[]{:S(2)}) %collective-permute-start.16) | collective-permute-done | bytes 131104 | tf_op jit(solution)/shard_map/ppermute | solution.py:175
  35.5 0.1 fusion.2
  35.5 1.8 %collective-permute-start.17 = (bf16[8,8192]{1,0:T(8,128)(2,1)S(1)}, bf16[8,8192]{1,0:T(8,128)(2,1)S(1)}, u32[]{:S(2)}, u32[]{:S(2)}) collective-permute-start(bf16[8,8192]{1,0:T(8,128)(2,1)S(1)} %fusion.2), channel_id=1, source_target_pairs={{0,8},{1,9},{2,10},{3,11},{4,12},{5,13},{6,14},{7,15},{8,0},{9,1},... | collective-permute-start | bytes 393224 | tf_op jit(solution)/shard_map/ppermute | solution.py:175
  37.4 0.4 collective-permute-done.12
  37.8 0.1 slice_add_fusion
  37.9 1.0 %collective-permute-start.18 = (bf16[8,8192]{1,0:T(8,128)(2,1)S(1)}, bf16[8,8192]{1,0:T(8,128)(2,1)S(1)}, u32[]{:S(2)}, u32[]{:S(2)}) collective-permute-start(bf16[8,8192]{1,0:T(8,128)(2,1)S(1)} %slice.68), channel_id=1, source_target_pairs={{0,2},{1,5},{2,0},{3,7},{4,6},{5,1},{6,4},{7,3},{8,10},{9,13},{10,... | collective-permute-start | bytes 393224 | tf_op jit(solution)/shard_map/ppermute | solution.py:175
  38.9 4.8 %collective-permute-done.17.refs_1_ = bf16[8,8192]{1,0:T(8,128)(2,1)S(1)} collective-permute-done((bf16[8,8192]{1,0:T(8,128)(2,1)S(1)}, bf16[8,8192]{1,0:T(8,128)(2,1)S(1)}, u32[]{:S(2)}, u32[]{:S(2)}) %collective-permute-start.17) | collective-permute-done | bytes 131104 | tf_op jit(solution)/shard_map/ppermute | solution.py:175
  43.7 0.0 collective-permute-done.18.refs_2_
  43.7 0.0 copy-done
  43.7 0.9 %shard_map.59 = bf16[8,8192]{1,0:T(8,128)(2,1)} custom-call(f32[8,8192]{1,0:T(8,128)S(1)} %slice.52.refs_0_, bf16[8,8192]{1,0:T(8,128)(2,1)S(1)} %collective-permute-done.17.refs_1_, bf16[8,8192]{1,0:T(8,128)(2,1)S(1)} %collective-permute-done.18.refs_2_, s32[1,8192]{1,0:T(1,128)S(1)} %bitcast.3, bf16[256,128]{1,0:T(8,128)(2,1)S(1)} %pad_maximum_fusion.2.refs_4_), custom_call_target="tpu_custom_call" | custom-call | tf_op jit(solution)/shard_map/pallas_call | solution.py:153
  (16 shorter events, 0.3 us)
Async XLA Ops:
  0.0 10.7 %collective-permute-start = (bf16[8,8192]{1,0:T(8,128)(2,1)}, bf16[8,8192]{1,0:T(8,128)(2,1)S(1)}, u32[]{:S(2)}, u32[]{:S(2)}) collective-permute-start(bf16[8,8192]{1,0:T(8,128)(2,1)} %param.5), channel_id=1, source_target_pairs={{0,8},{1,9},{2,10},{3,11},{4,12},{5,13},{6,14},{7,15},{8,0},{9,1},... | collective-permute-start | bytes 393224 | tf_op jit(solution)/shard_map/ppermute | solution.py:175
  4.0 8.9 %collective-permute-start.1 = (bf16[8,8192]{1,0:T(8,128)(2,1)}, bf16[8,8192]{1,0:T(8,128)(2,1)S(1)}, u32[]{:S(2)}, u32[]{:S(2)}) collective-permute-start(bf16[8,8192]{1,0:T(8,128)(2,1)} %param.5), channel_id=1, source_target_pairs={{0,4},{1,3},{2,6},{3,1},{4,0},{5,7},{6,2},{7,5},{8,12},{9,11},{10,... | collective-permute-start | bytes 393224 | tf_op jit(solution)/shard_map/ppermute | solution.py:175
  5.6 13.3 %collective-permute-start.3 = (bf16[8,8192]{1,0:T(8,128)(2,1)}, bf16[8,8192]{1,0:T(8,128)(2,1)S(1)}, u32[]{:S(2)}, u32[]{:S(2)}) collective-permute-start(bf16[8,8192]{1,0:T(8,128)(2,1)} %param.5), channel_id=1, source_target_pairs={{0,2},{1,5},{2,0},{3,7},{4,6},{5,1},{6,4},{7,3},{8,10},{9,13},{10,... | collective-permute-start | bytes 393224 | tf_op jit(solution)/shard_map/ppermute | solution.py:175
  7.1 11.7 %collective-permute-start.4 = (bf16[8,8192]{1,0:T(8,128)(2,1)}, bf16[8,8192]{1,0:T(8,128)(2,1)S(1)}, u32[]{:S(2)}, u32[]{:S(2)}) collective-permute-start(bf16[8,8192]{1,0:T(8,128)(2,1)} %param.5), channel_id=1, source_target_pairs={{0,6},{1,7},{2,4},{3,5},{4,2},{5,3},{6,0},{7,1},{8,14},{9,15},{10,... | collective-permute-start | bytes 393224 | tf_op jit(solution)/shard_map/ppermute | solution.py:175
  10.7 8.2 %collective-permute-start.2 = (bf16[8,8192]{1,0:T(8,128)(2,1)S(1)}, bf16[8,8192]{1,0:T(8,128)(2,1)S(1)}, u32[]{:S(2)}, u32[]{:S(2)}) collective-permute-start(bf16[8,8192]{1,0:T(8,128)(2,1)S(1)} %collective-permute-done._), channel_id=1, source_target_pairs={{0,4},{1,3},{2,6},{3,1},{4,0},{5,7},{6,2},{7,5},{8,12},{9,11},{10,... | collective-permute-start | bytes 393224 | tf_op jit(solution)/shard_map/ppermute | solution.py:175
  11.4 9.1 %collective-permute-start.5 = (bf16[8,8192]{1,0:T(8,128)(2,1)S(1)}, bf16[8,8192]{1,0:T(8,128)(2,1)S(1)}, u32[]{:S(2)}, u32[]{:S(2)}) collective-permute-start(bf16[8,8192]{1,0:T(8,128)(2,1)S(1)} %collective-permute-done._), channel_id=1, source_target_pairs={{0,2},{1,5},{2,0},{3,7},{4,6},{5,1},{6,4},{7,3},{8,10},{9,13},{10,... | collective-permute-start | bytes 393224 | tf_op jit(solution)/shard_map/ppermute | solution.py:175
  12.9 7.6 %collective-permute-start.6 = (bf16[8,8192]{1,0:T(8,128)(2,1)S(1)}, bf16[8,8192]{1,0:T(8,128)(2,1)S(1)}, u32[]{:S(2)}, u32[]{:S(2)}) collective-permute-start(bf16[8,8192]{1,0:T(8,128)(2,1)S(1)} %collective-permute-done._), channel_id=1, source_target_pairs={{0,6},{1,7},{2,4},{3,5},{4,2},{5,3},{6,0},{7,1},{8,14},{9,15},{10,... | collective-permute-start | bytes 393224 | tf_op jit(solution)/shard_map/ppermute | solution.py:175
  14.4 4.6 %copy-start.1 = (bf16[8,8192]{1,0:T(8,128)(2,1)S(1)}, bf16[8,8192]{1,0:T(8,128)(2,1)}, u32[]{:S(2)}) copy-start(bf16[8,8192]{1,0:T(8,128)(2,1)} %param.5) | copy-start | bytes 393220
  19.0 3.0 %collective-permute-start.7 = (bf16[48,8192]{1,0:T(8,128)(2,1)S(1)}, bf16[48,8192]{1,0:T(8,128)(2,1)S(1)}, u32[]{:S(2)}, u32[]{:S(2)}) collective-permute-start(bf16[48,8192]{1,0:T(8,128)(2,1)S(1)} %constant_dynamic-update-slice_fusion.refs_2_), channel_id=1, source_target_pairs={{0,1},{1,0},{2,3},{3,2},{4,5},{5,4},{6,7},{7,6},{8,9},{9,8},{10,11... | collective-permute-start | bytes 2359304 | tf_op jit(solution)/shard_map/ppermute | solution.py:175
  20.6 1.4 %collective-permute-start.9 = (bf16[16,4096]{1,0:T(8,128)(2,1)S(1)}, bf16[16,4096]{1,0:T(8,128)(2,1)S(1)}, u32[]{:S(2)}, u32[]{:S(2)}) collective-permute-start(bf16[16,4096]{1,0:T(8,128)(2,1)S(1)} %pad_maximum_fusion.1.refs_4_), channel_id=1, source_target_pairs={{0,1},{1,0},{2,3},{3,2},{4,5},{5,4},{6,7},{7,6},{8,9},{9,8},{10,11... | collective-permute-start | bytes 393224 | tf_op jit(solution)/shard_map/ppermute | solution.py:175
  20.7 2.0 %collective-permute-start.8 = (bf16[16,4096]{1,0:T(8,128)(2,1)S(1)}, bf16[16,4096]{1,0:T(8,128)(2,1)S(1)}, u32[]{:S(2)}, u32[]{:S(2)}) collective-permute-start(bf16[16,4096]{1,0:T(8,128)(2,1)S(1)} %pad_maximum_fusion.refs_4_), channel_id=1, source_target_pairs={{0,1},{1,0},{2,3},{3,2},{4,5},{5,4},{6,7},{7,6},{8,9},{9,8},{10,11... | collective-permute-start | bytes 393224 | tf_op jit(solution)/shard_map/ppermute | solution.py:175
  24.2 1.4 %collective-permute-start.13 = (bf16[8,8192]{1,0:T(8,128)(2,1)S(1)}, bf16[8,8192]{1,0:T(8,128)(2,1)S(1)}, u32[]{:S(2)}, u32[]{:S(2)}) collective-permute-start(bf16[8,8192]{1,0:T(8,128)(2,1)S(1)} %get-tuple-element.55), channel_id=1, source_target_pairs={{0,1},{1,0},{2,3},{3,2},{4,5},{5,4},{6,7},{7,6},{8,9},{9,8},{10,11... | collective-permute-start | bytes 393224 | tf_op jit(solution)/shard_map/ppermute | solution.py:175
  24.4 2.4 %collective-permute-start.10 = (bf16[24,8192]{1,0:T(8,128)(2,1)S(1)}, bf16[24,8192]{1,0:T(8,128)(2,1)S(1)}, u32[]{:S(2)}, u32[]{:S(2)}) collective-permute-start(bf16[24,8192]{1,0:T(8,128)(2,1)S(1)} %get-tuple-element.49), channel_id=1, source_target_pairs={{0,1},{1,0},{2,3},{3,2},{4,5},{5,4},{6,7},{7,6},{8,9},{9,8},{10,11... | collective-permute-start | bytes 1179656 | tf_op jit(solution)/shard_map/ppermute | solution.py:175
  25.6 7.2 %collective-permute-start.14 = (bf16[8,8192]{1,0:T(8,128)(2,1)S(1)}, bf16[8,8192]{1,0:T(8,128)(2,1)S(1)}, u32[]{:S(2)}, u32[]{:S(2)}) collective-permute-start(bf16[8,8192]{1,0:T(8,128)(2,1)S(1)} %add_convert_fusion), channel_id=1, source_target_pairs={{0,6},{1,7},{2,4},{3,5},{4,2},{5,3},{6,0},{7,1},{8,14},{9,15},{10,... | collective-permute-start | bytes 393224 | tf_op jit(solution)/shard_map/ppermute | solution.py:175
  26.8 2.5 %collective-permute-start.11 = (bf16[32,8192]{1,0:T(8,128)(2,1)S(1)}, bf16[32,8192]{1,0:T(8,128)(2,1)S(1)}, u32[]{:S(2)}, u32[]{:S(2)}) collective-permute-start(bf16[32,8192]{1,0:T(8,128)(2,1)S(1)} %get-tuple-element.51), channel_id=1, source_target_pairs={{0,1},{1,0},{2,3},{3,2},{4,5},{5,4},{6,7},{7,6},{8,9},{9,8},{10,11... | collective-permute-start | bytes 1572872 | tf_op jit(solution)/shard_map/ppermute | solution.py:175
  26.9 16.8 %copy-start = (s32[8192]{0:T(1024)S(1)}, s32[8192]{0:T(1024)}, u32[]{:S(2)}) copy-start(s32[8192]{0:T(1024)} %param.9) | copy-start | bytes 98308
  26.9 8.0 %collective-permute-start.15 = (bf16[8,8192]{1,0:T(8,128)(2,1)S(1)}, bf16[8,8192]{1,0:T(8,128)(2,1)S(1)}, u32[]{:S(2)}, u32[]{:S(2)}) collective-permute-start(bf16[8,8192]{1,0:T(8,128)(2,1)S(1)} %get-tuple-element.59), channel_id=1, source_target_pairs={{0,4},{1,3},{2,6},{3,1},{4,0},{5,7},{6,2},{7,5},{8,12},{9,11},{10,... | collective-permute-start | bytes 393224 | tf_op jit(solution)/shard_map/ppermute | solution.py:175
  28.8 6.6 %collective-permute-start.16 = (bf16[8,8192]{1,0:T(8,128)(2,1)S(1)}, bf16[8,8192]{1,0:T(8,128)(2,1)S(1)}, u32[]{:S(2)}, u32[]{:S(2)}) collective-permute-start(bf16[8,8192]{1,0:T(8,128)(2,1)S(1)} %get-tuple-element.60), channel_id=1, source_target_pairs={{0,2},{1,5},{2,0},{3,7},{4,6},{5,1},{6,4},{7,3},{8,10},{9,13},{10,... | collective-permute-start | bytes 393224 | tf_op jit(solution)/shard_map/ppermute | solution.py:175
  29.5 8.3 %collective-permute-start.12 = (bf16[16,8192]{1,0:T(8,128)(2,1)S(1)}, bf16[16,8192]{1,0:T(8,128)(2,1)S(1)}, u32[]{:S(2)}, u32[]{:S(2)}) collective-permute-start(bf16[16,8192]{1,0:T(8,128)(2,1)S(1)} %slice.67), channel_id=1, source_target_pairs={{0,4},{1,3},{2,6},{3,1},{4,0},{5,7},{6,2},{7,5},{8,12},{9,11},{10,... | collective-permute-start | bytes 786440 | tf_op jit(solution)/shard_map/ppermute | solution.py:175
  35.5 8.2 %collective-permute-start.17 = (bf16[8,8192]{1,0:T(8,128)(2,1)S(1)}, bf16[8,8192]{1,0:T(8,128)(2,1)S(1)}, u32[]{:S(2)}, u32[]{:S(2)}) collective-permute-start(bf16[8,8192]{1,0:T(8,128)(2,1)S(1)} %fusion.2), channel_id=1, source_target_pairs={{0,8},{1,9},{2,10},{3,11},{4,12},{5,13},{6,14},{7,15},{8,0},{9,1},... | collective-permute-start | bytes 393224 | tf_op jit(solution)/shard_map/ppermute | solution.py:175
  37.9 5.9 %collective-permute-start.18 = (bf16[8,8192]{1,0:T(8,128)(2,1)S(1)}, bf16[8,8192]{1,0:T(8,128)(2,1)S(1)}, u32[]{:S(2)}, u32[]{:S(2)}) collective-permute-start(bf16[8,8192]{1,0:T(8,128)(2,1)S(1)} %slice.68), channel_id=1, source_target_pairs={{0,2},{1,5},{2,0},{3,7},{4,6},{5,1},{6,4},{7,3},{8,10},{9,13},{10,... | collective-permute-start | bytes 393224 | tf_op jit(solution)/shard_map/ppermute | solution.py:175

commit v21 on v20

--- a/solution.py
+++ b/solution.py
@@ -10,6 +10,7 @@
 
 BLOCK = 128
 SPANS = 2
+PARTS, ORDER = (9, 7), (0, 1)
 TURNS = 8
 NT = (((1,), (1,)), ((), ()))
 
@@ -132,13 +133,14 @@
     return jnp.concatenate([signs, signs])
 
 
-def rotate_kernel(count, *refs):
-    total_ref, *arrived = refs[: count + 1]
-    sign_ref, matrix_ref, out_ref = refs[count + 1 :]
-    rows, features = total_ref.shape
+def rotate_kernel(counts, *refs):
+    total_ref, *refs = refs
     value = total_ref[...]
-    for piece in arrived:
-        value = value + piece[...].astype(jnp.float32)
+    rows, features = value.shape
+    for count in counts:
+        parts, refs = refs[:count], refs[count:]
+        value = value + jnp.concatenate([part[...] for part in parts], axis=1).astype(jnp.float32)
+    sign_ref, matrix_ref, out_ref = refs
     value = value * sign_ref[...].astype(jnp.float32)
     value = jnp.concatenate([value[:, b : b + BLOCK] for b in range(0, features, BLOCK)])
     high = value.astype(jnp.bfloat16)
@@ -150,13 +152,14 @@
 
 
 def rotate(total, arrived, signs):
+    pieces = [piece for parts in arrived for piece in parts]
     return pl.pallas_call(
-        functools.partial(rotate_kernel, len(arrived)),
+        functools.partial(rotate_kernel, [len(parts) for parts in arrived]),
         out_shape=jax.ShapeDtypeStruct(total.shape, jnp.bfloat16),
-        in_specs=[vmem()] * (len(arrived) + 3),
+        in_specs=[vmem()] * (len(pieces) + 3),
         out_specs=vmem(),
         compiler_params=pltpu.CompilerParams(vmem_limit_bytes=16 << 20),
-    )(total, *arrived, signs.reshape(1, -1), signs_twice())
+    )(total, *pieces, signs.reshape(1, -1), signs_twice())
 
 
 def solution(mesh):
@@ -205,23 +208,37 @@
         rest_rows = ((ends[0], ends[2]), (ends[4], ends[5]))
         own, diagonal, rest, *sends = down(hidden, down_w, (own_rows, ((ends[3], ends[4]),), rest_rows))
         diagonal = diagonal + swap(sends[1], (1, 1)).astype(jnp.float32)
-        diagonal = swap(diagonal.astype(jnp.bfloat16), square[2])
+        diagonal = diagonal.astype(jnp.bfloat16)
         rest_there, sends[0] = lax.optimization_barrier((swap(sends[2], (1, 1)), sends[0]))
         rest = rest + rest_there.astype(jnp.float32)
         leave = rest[count:].astype(jnp.bfloat16)
-        total = rest[:count]
-        for piece in (diagonal, swap(leave[:count], square[0]), swap(leave[count:], square[1])):
-            total = total + piece.astype(jnp.float32)
+        own = own + swap(sends[0], (1, 1)).astype(jnp.float32)
+        own, step = own[: 2 * rows], own[2 * rows :].astype(jnp.bfloat16)
+        beside = swap(step, square[0])
+
         arrived = []
-        for masks in reversed(far):
-            split = total.shape[0] // 2 // rows * rows
-            piece = swap(total[split:].astype(jnp.bfloat16), masks)
-            arrived.append(piece[:rows])
-            total = total[:split] + piece[rows:].astype(jnp.float32)
-
-        own = own + swap(sends[0], (1, 1)).astype(jnp.float32)
-        own = own[: 2 * rows] + swap(own[2 * rows :].astype(jnp.bfloat16), square[0]).astype(jnp.float32)
-        arrived.append(swap(own[rows:].astype(jnp.bfloat16), square[1]))
+        ends = [features * sum(PARTS[:k]) // sum(PARTS) for k in range(len(PARTS) + 1)]
+        for k in ORDER:
+            part = slice(ends[k], ends[k + 1])
+            pieces = [diagonal[:, part], leave[count:, part], leave[:count, part]]
+            if k == ORDER[-1]:
+                step, *pieces = lax.optimization_barrier((step, *pieces))
+            pieces = [swap(piece, masks) for piece, masks in zip(pieces, square[::-1])]
+            if k == ORDER[-1]:
+                beside, *pieces = lax.optimization_barrier((beside, *pieces))
+            total = rest[:count, part]
+            for piece in pieces:
+                total = total + piece.astype(jnp.float32)
+            arrived.append([])
+            for masks in reversed(far):
+                split = total.shape[0] // 2 // rows * rows
+                piece = swap(total[split:].astype(jnp.bfloat16), masks)
+                arrived[-1].append(piece[:rows])
+                total = total[:split] + piece[rows:].astype(jnp.float32)
+        arrived = list(zip(*(arrived[ORDER.index(k)] for k in range(len(PARTS)))))
+
+        own = own + beside.astype(jnp.float32)
+        arrived.append([swap(own[rows:].astype(jnp.bfloat16), square[1])])
         return rotate(own[:rows], arrived, sign_pattern)
 
     placed = (P(("groups", "gx"), None), P(None, "gx"), P(None, "gx"), P("gx", None), P())

time: 44.8 us -> 48.5 us (1.083)
  starting transfers between devices: 20.2 us -> 26.5 us
  waiting for transfers between devices: 16.1 us -> 13.5 us
    ppermute x19 -> x23, starting transfers between devices: 20.2 us -> 26.5 us  [swap(): lax.ppermute(value, 'gx', [(i, i ^ masks[i % 2]) for i in range(members)])]
    ppermute x19 -> x23, waiting for transfers between devices: 16.1 us -> 13.5 us  [swap(): lax.ppermute(value, 'gx', [(i, i ^ masks[i % 2]) for i in range(members)])]
  transfers between devices with their start and end apart: 19 -> 23, of which waited for: 9 -> 6; matrix products, arithmetic and copies ran while one was open for 1% -> 1% of each run, Pallas kernels for 12% -> 11%
where the time goes in v21:
time: 48.5 us; the launch traced here: 48.4 us
  starting transfers between devices  26.5 us (55%)
  waiting for transfers between devices  13.5 us (28%)
  Pallas kernels  7.51 us (15%)
    ppermute x23, starting transfers between devices, swap(): lax.ppermute(value, 'gx', [(i, i ^ masks[i % 2]) for i in range(members)])  26.5 us
    ppermute x23, waiting for transfers between devices, swap(): lax.ppermute(value, 'gx', [(i, i ^ masks[i % 2]) for i in range(members)])  13.5 us
    pallas_call x1, Pallas kernels, load(): pl.pallas_call(load_kernel, out_shape=(shape, shape, jax.ShapeDtypeStruct...  4.46 us
    pallas_call x2, Pallas kernels, hidden_units(): pl.pallas_call(functools.partial(hidden_kernel, start, last), out_shape=(...  1.45 us
  transfers between devices with their start and end apart: 23, of which 6 were waited for; matrix products, arithmetic and copies ran while one was open for 1% of the time, Pallas kernels for 11%

profile of v21, /device:TPU:0, one launch (start us, length us, event | category | flops | bytes accessed | tf_op | source)
XLA Modules:
  0.0 48.4 jit_solution(8236188452611792593)
XLA Ops:
  0.0 4.0 %collective-permute-start = (bf16[8,8192]{1,0:T(8,128)(2,1)}, bf16[8,8192]{1,0:T(8,128)(2,1)S(1)}, u32[]{:S(2)}, u32[]{:S(2)}) collective-permute-start(bf16[8,8192]{1,0:T(8,128)(2,1)} %param.5), channel_id=1, source_target_pairs={{0,8},{1,9},{2,10},{3,11},{4,12},{5,13},{6,14},{7,15},{8,0},{9,1},... | collective-permute-start | bytes 393224 | tf_op jit(solution)/shard_map/ppermute | solution.py:178
  4.0 1.6 %collective-permute-start.1 = (bf16[8,8192]{1,0:T(8,128)(2,1)}, bf16[8,8192]{1,0:T(8,128)(2,1)S(1)}, u32[]{:S(2)}, u32[]{:S(2)}) collective-permute-start(bf16[8,8192]{1,0:T(8,128)(2,1)} %param.5), channel_id=1, source_target_pairs={{0,4},{1,3},{2,6},{3,1},{4,0},{5,7},{6,2},{7,5},{8,12},{9,11},{10,... | collective-permute-start | bytes 393224 | tf_op jit(solution)/shard_map/ppermute | solution.py:178
  5.6 1.5 %collective-permute-start.3 = (bf16[8,8192]{1,0:T(8,128)(2,1)}, bf16[8,8192]{1,0:T(8,128)(2,1)S(1)}, u32[]{:S(2)}, u32[]{:S(2)}) collective-permute-start(bf16[8,8192]{1,0:T(8,128)(2,1)} %param.5), channel_id=1, source_target_pairs={{0,2},{1,5},{2,0},{3,7},{4,6},{5,1},{6,4},{7,3},{8,10},{9,13},{10,... | collective-permute-start | bytes 393224 | tf_op jit(solution)/shard_map/ppermute | solution.py:178
  7.1 0.4 collective-permute-start.4
  7.5 3.1 %collective-permute-done._ = bf16[8,8192]{1,0:T(8,128)(2,1)S(1)} collective-permute-done((bf16[8,8192]{1,0:T(8,128)(2,1)}, bf16[8,8192]{1,0:T(8,128)(2,1)S(1)}, u32[]{:S(2)}, u32[]{:S(2)}) %collective-permute-start) | collective-permute-done | bytes 131104 | tf_op jit(solution)/shard_map/ppermute | solution.py:178
  10.7 0.8 %collective-permute-start.2 = (bf16[8,8192]{1,0:T(8,128)(2,1)S(1)}, bf16[8,8192]{1,0:T(8,128)(2,1)S(1)}, u32[]{:S(2)}, u32[]{:S(2)}) collective-permute-start(bf16[8,8192]{1,0:T(8,128)(2,1)S(1)} %collective-permute-done._), channel_id=1, source_target_pairs={{0,4},{1,3},{2,6},{3,1},{4,0},{5,7},{6,2},{7,5},{8,12},{9,11},{10,... | collective-permute-start | bytes 393224 | tf_op jit(solution)/shard_map/ppermute | solution.py:178
  11.4 1.5 %collective-permute-start.5 = (bf16[8,8192]{1,0:T(8,128)(2,1)S(1)}, bf16[8,8192]{1,0:T(8,128)(2,1)S(1)}, u32[]{:S(2)}, u32[]{:S(2)}) collective-permute-start(bf16[8,8192]{1,0:T(8,128)(2,1)S(1)} %collective-permute-done._), channel_id=1, source_target_pairs={{0,2},{1,5},{2,0},{3,7},{4,6},{5,1},{6,4},{7,3},{8,10},{9,13},{10,... | collective-permute-start | bytes 393224 | tf_op jit(solution)/shard_map/ppermute | solution.py:178
  12.9 0.0 collective-permute-done.1
  12.9 1.5 %collective-permute-start.6 = (bf16[8,8192]{1,0:T(8,128)(2,1)S(1)}, bf16[8,8192]{1,0:T(8,128)(2,1)S(1)}, u32[]{:S(2)}, u32[]{:S(2)}) collective-permute-start(bf16[8,8192]{1,0:T(8,128)(2,1)S(1)} %collective-permute-done._), channel_id=1, source_target_pairs={{0,6},{1,7},{2,4},{3,5},{4,2},{5,3},{6,0},{7,1},{8,14},{9,15},{10,... | collective-permute-start | bytes 393224 | tf_op jit(solution)/shard_map/ppermute | solution.py:178
  14.4 0.0 copy-start.1
  14.4 4.5 %shard_map.55 = (bf16[8192,224]{1,0:T(8,128)(2,1)S(1)}, bf16[8192,224]{1,0:T(8,128)(2,1)S(1)}, bf16[224,8192]{1,0:T(8,128)(2,1)S(1)}) custom-call(bf16[224,8192]{1,0:T(8,128)(2,1)} %bitcast.4, bf16[224,8192]{1,0:T(8,128)(2,1)} %bitcast.5, bf16[224,8192]{1,0:T(8,128)(2,1)} %down_hbm.1, bf16[8,8192]{1,0:T(8,128)(2,1)S(1)} %collective-permute-done._), custom_call_target="tpu_custom_call" | custom-call | bytes 11010048 | tf_op jit(solution)/shard_map/pallas_call | solution.py:45
  18.9 0.0 collective-permute-done.3
  18.9 0.0 collective-permute-done.4
  18.9 0.0 collective-permute-done.2
  19.0 0.0 copy-done.1
  19.0 0.1 collective-permute-start.7
  19.1 1.4 %collective-permute-done.6 = bf16[8,8192]{1,0:T(8,128)(2,1)S(1)} collective-permute-done((bf16[8,8192]{1,0:T(8,128)(2,1)S(1)}, bf16[8,8192]{1,0:T(8,128)(2,1)S(1)}, u32[]{:S(2)}, u32[]{:S(2)}) %collective-permute-start.6) | collective-permute-done | bytes 131104 | tf_op jit(solution)/shard_map/ppermute | solution.py:178
  20.5 0.0 collective-permute-done.5
  20.6 0.1 collective-permute-start.9
  20.7 0.6 %collective-permute-start.8 = (bf16[16,4096]{1,0:T(8,128)(2,1)S(1)}, bf16[16,4096]{1,0:T(8,128)(2,1)S(1)}, u32[]{:S(2)}, u32[]{:S(2)}) collective-permute-start(bf16[16,4096]{1,0:T(8,128)(2,1)S(1)} %pad_maximum_fusion.refs_4_), channel_id=1, source_target_pairs={{0,1},{1,0},{2,3},{3,2},{4,5},{5,4},{6,7},{7,6},{8,9},{9,8},{10,11... | collective-permute-start | bytes 393224 | tf_op jit(solution)/shard_map/ppermute | solution.py:178
  21.2 0.8 %collective-permute-done.9.refs_5_ = bf16[16,4096]{1,0:T(8,128)(2,1)S(1)} collective-permute-done((bf16[16,4096]{1,0:T(8,128)(2,1)S(1)}, bf16[16,4096]{1,0:T(8,128)(2,1)S(1)}, u32[]{:S(2)}, u32[]{:S(2)}) %collective-permute-start.9) | collective-permute-done | bytes 131104 | tf_op jit(solution)/shard_map/ppermute | solution.py:178
  22.0 0.0 collective-permute-done.7.refs_3_
  22.0 0.7 %shard_map.56 = (f32[128,224]{1,0:T(8,128)S(1)}, f32[128,224]{1,0:T(8,128)S(1)}) custom-call(bf16[8192,224]{1,0:T(8,128)(2,1)S(1)} %get-tuple-element.47.refs_0_, bf16[8192,224]{1,0:T(8,128)(2,1)S(1)} %get-tuple-element.48.refs_1_, bf16[48,8192]{1,0:T(8,128)(2,1)S(1)} %constant_dynamic-update-slice_fusion.refs_2_, ...), custom_call_target="tpu_custom_call" | custom-call | flops 469762048 | bytes 3670016 | tf_op jit(solution)/shard_map/pallas_call | solution.py:85
  22.7 0.0 collective-permute-done.8.refs_5_
  22.7 0.7 %shard_map.57.hidden_ref = bf16[128,224]{1,0:T(8,128)(2,1)S(1)} custom-call(bf16[8192,224]{1,0:T(8,128)(2,1)S(1)} %get-tuple-element.47.refs_0_, bf16[8192,224]{1,0:T(8,128)(2,1)S(1)} %get-tuple-element.48.refs_1_, bf16[48,8192]{1,0:T(8,128)(2,1)S(1)} %constant_dynamic-update-slice_fusion.refs_2_, bf16[48,8192]{1,0:T(8,128)(2,1)S(1)} %collective-permute-done.7.refs_3_, ...), custom_call_target="tpu_custom_call" | custom-call | flops 469762048 | bytes 3670016 | tf_op jit(solution)/shard_map/pallas_call | solution.py:85
  23.4 0.7 %shard_map.58 = (f32[32,8192]{1,0:T(8,128)S(1)}, f32[8,8192]{1,0:T(8,128)S(1)}, f32[24,8192]{1,0:T(8,128)S(1)}, bf16[32,8192]{1,0:T(8,128)(2,1)S(1)}, bf16[8,819...) custom-call(bf16[128,224]{1,0:T(8,128)(2,1)S(1)} %shard_map.57.hidden_ref, bf16[224,8192]{1,0:T(8,128)(2,1)S(1)} %get-tuple-element.54.down_ref), custom_call_target="tpu_custom_call" | custom-call | flops 469762048 | bytes 3670016 | tf_op jit(solution)/shard_map/pallas_call | solution.py:114
  24.2 0.2 collective-permute-start.13
  24.4 0.4 collective-permute-start.10
  24.8 0.7 %collective-permute-done.13 = bf16[8,8192]{1,0:T(8,128)(2,1)S(1)} collective-permute-done((bf16[8,8192]{1,0:T(8,128)(2,1)S(1)}, bf16[8,8192]{1,0:T(8,128)(2,1)S(1)}, u32[]{:S(2)}, u32[]{:S(2)}) %collective-permute-start.13) | collective-permute-done | bytes 131104 | tf_op jit(solution)/shard_map/ppermute | solution.py:178
  25.6 1.2 %collective-permute-start.17 = (bf16[8,4608]{1,0:T(8,128)(2,1)S(1)}, bf16[8,4608]{1,0:T(8,128)(2,1)S(1)}, u32[]{:S(2)}, u32[]{:S(2)}) collective-permute-start(bf16[8,4608]{1,0:T(8,128)(2,1)S(1)} %slice.79), channel_id=1, source_target_pairs={{0,6},{1,7},{2,4},{3,5},{4,2},{5,3},{6,0},{7,1},{8,14},{9,15},{10,... | collective-permute-start | bytes 221192 | tf_op jit(solution)/shard_map/ppermute | solution.py:178
  26.8 0.0 collective-permute-done.10
  26.9 0.0 collective-permute-start.11
  26.9 0.1 fusion.10
  26.9 0.0 copy-start
  27.0 1.6 %collective-permute-start.18 = (bf16[8,4608]{1,0:T(8,128)(2,1)S(1)}, bf16[8,4608]{1,0:T(8,128)(2,1)S(1)}, u32[]{:S(2)}, u32[]{:S(2)}) collective-permute-start(bf16[8,4608]{1,0:T(8,128)(2,1)S(1)} %get-tuple-element.73), channel_id=1, source_target_pairs={{0,2},{1,5},{2,0},{3,7},{4,6},{5,1},{6,4},{7,3},{8,10},{9,13},{10,... | collective-permute-start | bytes 221192 | tf_op jit(solution)/shard_map/ppermute | solution.py:178
  28.5 0.9 %collective-permute-start.19 = (bf16[8,4608]{1,0:T(8,128)(2,1)S(1)}, bf16[8,4608]{1,0:T(8,128)(2,1)S(1)}, u32[]{:S(2)}, u32[]{:S(2)}) collective-permute-start(bf16[8,4608]{1,0:T(8,128)(2,1)S(1)} %get-tuple-element.74), channel_id=1, source_target_pairs={{0,4},{1,3},{2,6},{3,1},{4,0},{5,7},{6,2},{7,5},{8,12},{9,11},{10,... | collective-permute-start | bytes 221192 | tf_op jit(solution)/shard_map/ppermute | solution.py:178
  29.4 0.0 collective-permute-done.11
  29.4 0.1 convert_add_fusion
  29.5 1.2 %collective-permute-start.12 = (bf16[16,8192]{1,0:T(8,128)(2,1)S(1)}, bf16[16,8192]{1,0:T(8,128)(2,1)S(1)}, u32[]{:S(2)}, u32[]{:S(2)}) collective-permute-start(bf16[16,8192]{1,0:T(8,128)(2,1)S(1)} %slice.101), channel_id=1, source_target_pairs={{0,4},{1,3},{2,6},{3,1},{4,0},{5,7},{6,2},{7,5},{8,12},{9,11},{10,... | collective-permute-start | bytes 786440 | tf_op jit(solution)/shard_map/ppermute | solution.py:178
  30.8 1.8 %collective-permute-start.14 = (bf16[8,3584]{1,0:T(8,128)(2,1)S(1)}, bf16[8,3584]{1,0:T(8,128)(2,1)S(1)}, u32[]{:S(2)}, u32[]{:S(2)}) collective-permute-start(bf16[8,3584]{1,0:T(8,128)(2,1)S(1)} %slice.74), channel_id=1, source_target_pairs={{0,6},{1,7},{2,4},{3,5},{4,2},{5,3},{6,0},{7,1},{8,14},{9,15},{10,... | collective-permute-start | bytes 172040 | tf_op jit(solution)/shard_map/ppermute | solution.py:178
  32.6 0.0 collective-permute-done.17
  32.6 0.7 %collective-permute-start.15 = (bf16[8,3584]{1,0:T(8,128)(2,1)S(1)}, bf16[8,3584]{1,0:T(8,128)(2,1)S(1)}, u32[]{:S(2)}, u32[]{:S(2)}) collective-permute-start(bf16[8,3584]{1,0:T(8,128)(2,1)S(1)} %get-tuple-element.64), channel_id=1, source_target_pairs={{0,2},{1,5},{2,0},{3,7},{4,6},{5,1},{6,4},{7,3},{8,10},{9,13},{10,... | collective-permute-start | bytes 172040 | tf_op jit(solution)/shard_map/ppermute | solution.py:178
  33.2 0.0 collective-permute-done.18
  33.2 1.0 %collective-permute-start.16 = (bf16[8,3584]{1,0:T(8,128)(2,1)S(1)}, bf16[8,3584]{1,0:T(8,128)(2,1)S(1)}, u32[]{:S(2)}, u32[]{:S(2)}) collective-permute-start(bf16[8,3584]{1,0:T(8,128)(2,1)S(1)} %get-tuple-element.65), channel_id=1, source_target_pairs={{0,4},{1,3},{2,6},{3,1},{4,0},{5,7},{6,2},{7,5},{8,12},{9,11},{10,... | collective-permute-start | bytes 172040 | tf_op jit(solution)/shard_map/ppermute | solution.py:178
  34.3 0.0 collective-permute-done.19
  34.3 2.5 %collective-permute-start.20 = (bf16[8,4608]{1,0:T(8,128)(2,1)S(1)}, bf16[8,4608]{1,0:T(8,128)(2,1)S(1)}, u32[]{:S(2)}, u32[]{:S(2)}) collective-permute-start(bf16[8,4608]{1,0:T(8,128)(2,1)S(1)} %fusion.2), channel_id=1, source_target_pairs={{0,8},{1,9},{2,10},{3,11},{4,12},{5,13},{6,14},{7,15},{8,0},{9,1},... | collective-permute-start | bytes 221192 | tf_op jit(solution)/shard_map/ppermute | solution.py:178
  36.8 3.0 %collective-permute-done.14 = bf16[8,3584]{1,0:T(8,128)(2,1)S(1)} collective-permute-done((bf16[8,3584]{1,0:T(8,128)(2,1)S(1)}, bf16[8,3584]{1,0:T(8,128)(2,1)S(1)}, u32[]{:S(2)}, u32[]{:S(2)}) %collective-permute-start.14) | collective-permute-done | bytes 57376 | tf_op jit(solution)/shard_map/ppermute | solution.py:178
  39.9 0.0 collective-permute-done.15
  39.9 0.0 collective-permute-done.16
  39.9 0.0 collective-permute-done.12
  39.9 0.1 slice_add_fusion
  40.0 1.7 %collective-permute-start.22 = (bf16[8,8192]{1,0:T(8,128)(2,1)S(1)}, bf16[8,8192]{1,0:T(8,128)(2,1)S(1)}, u32[]{:S(2)}, u32[]{:S(2)}) collective-permute-start(bf16[8,8192]{1,0:T(8,128)(2,1)S(1)} %slice.102), channel_id=1, source_target_pairs={{0,2},{1,5},{2,0},{3,7},{4,6},{5,1},{6,4},{7,3},{8,10},{9,13},{10,... | collective-permute-start | bytes 393224 | tf_op jit(solution)/shard_map/ppermute | solution.py:178
  41.7 1.3 %collective-permute-start.21 = (bf16[8,3584]{1,0:T(8,128)(2,1)S(1)}, bf16[8,3584]{1,0:T(8,128)(2,1)S(1)}, u32[]{:S(2)}, u32[]{:S(2)}) collective-permute-start(bf16[8,3584]{1,0:T(8,128)(2,1)S(1)} %fusion.5), channel_id=1, source_target_pairs={{0,8},{1,9},{2,10},{3,11},{4,12},{5,13},{6,14},{7,15},{8,0},{9,1},... | collective-permute-start | bytes 172040 | tf_op jit(solution)/shard_map/ppermute | solution.py:178
  43.0 0.0 collective-permute-done.20.refs_1_
  43.1 4.4 %collective-permute-done.21.refs_2_ = bf16[8,3584]{1,0:T(8,128)(2,1)S(1)} collective-permute-done((bf16[8,3584]{1,0:T(8,128)(2,1)S(1)}, bf16[8,3584]{1,0:T(8,128)(2,1)S(1)}, u32[]{:S(2)}, u32[]{:S(2)}) %collective-permute-start.21) | collective-permute-done | bytes 57376 | tf_op jit(solution)/shard_map/ppermute | solution.py:178
  47.4 0.0 collective-permute-done.22.refs_3_
  47.5 0.0 copy-done
  47.5 0.9 %shard_map.59 = bf16[8,8192]{1,0:T(8,128)(2,1)} custom-call(f32[8,8192]{1,0:T(8,128)S(1)} %slice.77.refs_0_, bf16[8,4608]{1,0:T(8,128)(2,1)S(1)} %collective-permute-done.20.refs_1_, bf16[8,3584]{1,0:T(8,128)(2,1)S(1)} %collective-permute-done.21.refs_2_, bf16[8,8192]{1,0:T(8,128)(2,1)S(1)} %collective-permute-done.22.refs_3_, s32[1,8192]{1,0:T(1,128)S(1)} %bitcast.3, ...), custom_call_target="tpu_custom_call" | custom-call | tf_op jit(solution)/shard_map/pallas_call | solution.py:156
  (21 shorter events, 0.3 us)
Async XLA Ops:
  0.0 10.7 %collective-permute-start = (bf16[8,8192]{1,0:T(8,128)(2,1)}, bf16[8,8192]{1,0:T(8,128)(2,1)S(1)}, u32[]{:S(2)}, u32[]{:S(2)}) collective-permute-start(bf16[8,8192]{1,0:T(8,128)(2,1)} %param.5), channel_id=1, source_target_pairs={{0,8},{1,9},{2,10},{3,11},{4,12},{5,13},{6,14},{7,15},{8,0},{9,1},... | collective-permute-start | bytes 393224 | tf_op jit(solution)/shard_map/ppermute | solution.py:178
  4.0 8.9 %collective-permute-start.1 = (bf16[8,8192]{1,0:T(8,128)(2,1)}, bf16[8,8192]{1,0:T(8,128)(2,1)S(1)}, u32[]{:S(2)}, u32[]{:S(2)}) collective-permute-start(bf16[8,8192]{1,0:T(8,128)(2,1)} %param.5), channel_id=1, source_target_pairs={{0,4},{1,3},{2,6},{3,1},{4,0},{5,7},{6,2},{7,5},{8,12},{9,11},{10,... | collective-permute-start | bytes 393224 | tf_op jit(solution)/shard_map/ppermute | solution.py:178
  5.6 13.3 %collective-permute-start.3 = (bf16[8,8192]{1,0:T(8,128)(2,1)}, bf16[8,8192]{1,0:T(8,128)(2,1)S(1)}, u32[]{:S(2)}, u32[]{:S(2)}) collective-permute-start(bf16[8,8192]{1,0:T(8,128)(2,1)} %param.5), channel_id=1, source_target_pairs={{0,2},{1,5},{2,0},{3,7},{4,6},{5,1},{6,4},{7,3},{8,10},{9,13},{10,... | collective-permute-start | bytes 393224 | tf_op jit(solution)/shard_map/ppermute | solution.py:178
  7.1 11.7 %collective-permute-start.4 = (bf16[8,8192]{1,0:T(8,128)(2,1)}, bf16[8,8192]{1,0:T(8,128)(2,1)S(1)}, u32[]{:S(2)}, u32[]{:S(2)}) collective-permute-start(bf16[8,8192]{1,0:T(8,128)(2,1)} %param.5), channel_id=1, source_target_pairs={{0,6},{1,7},{2,4},{3,5},{4,2},{5,3},{6,0},{7,1},{8,14},{9,15},{10,... | collective-permute-start | bytes 393224 | tf_op jit(solution)/shard_map/ppermute | solution.py:178
  10.7 8.2 %collective-permute-start.2 = (bf16[8,8192]{1,0:T(8,128)(2,1)S(1)}, bf16[8,8192]{1,0:T(8,128)(2,1)S(1)}, u32[]{:S(2)}, u32[]{:S(2)}) collective-permute-start(bf16[8,8192]{1,0:T(8,128)(2,1)S(1)} %collective-permute-done._), channel_id=1, source_target_pairs={{0,4},{1,3},{2,6},{3,1},{4,0},{5,7},{6,2},{7,5},{8,12},{9,11},{10,... | collective-permute-start | bytes 393224 | tf_op jit(solution)/shard_map/ppermute | solution.py:178
  11.4 9.1 %collective-permute-start.5 = (bf16[8,8192]{1,0:T(8,128)(2,1)S(1)}, bf16[8,8192]{1,0:T(8,128)(2,1)S(1)}, u32[]{:S(2)}, u32[]{:S(2)}) collective-permute-start(bf16[8,8192]{1,0:T(8,128)(2,1)S(1)} %collective-permute-done._), channel_id=1, source_target_pairs={{0,2},{1,5},{2,0},{3,7},{4,6},{5,1},{6,4},{7,3},{8,10},{9,13},{10,... | collective-permute-start | bytes 393224 | tf_op jit(solution)/shard_map/ppermute | solution.py:178
  12.9 7.6 %collective-permute-start.6 = (bf16[8,8192]{1,0:T(8,128)(2,1)S(1)}, bf16[8,8192]{1,0:T(8,128)(2,1)S(1)}, u32[]{:S(2)}, u32[]{:S(2)}) collective-permute-start(bf16[8,8192]{1,0:T(8,128)(2,1)S(1)} %collective-permute-done._), channel_id=1, source_target_pairs={{0,6},{1,7},{2,4},{3,5},{4,2},{5,3},{6,0},{7,1},{8,14},{9,15},{10,... | collective-permute-start | bytes 393224 | tf_op jit(solution)/shard_map/ppermute | solution.py:178
  14.4 4.6 %copy-start.1 = (bf16[8,8192]{1,0:T(8,128)(2,1)S(1)}, bf16[8,8192]{1,0:T(8,128)(2,1)}, u32[]{:S(2)}) copy-start(bf16[8,8192]{1,0:T(8,128)(2,1)} %param.5) | copy-start | bytes 393220
  19.0 3.0 %collective-permute-start.7 = (bf16[48,8192]{1,0:T(8,128)(2,1)S(1)}, bf16[48,8192]{1,0:T(8,128)(2,1)S(1)}, u32[]{:S(2)}, u32[]{:S(2)}) collective-permute-start(bf16[48,8192]{1,0:T(8,128)(2,1)S(1)} %constant_dynamic-update-slice_fusion.refs_2_), channel_id=1, source_target_pairs={{0,1},{1,0},{2,3},{3,2},{4,5},{5,4},{6,7},{7,6},{8,9},{9,8},{10,11... | collective-permute-start | bytes 2359304 | tf_op jit(solution)/shard_map/ppermute | solution.py:178
  20.6 1.4 %collective-permute-start.9 = (bf16[16,4096]{1,0:T(8,128)(2,1)S(1)}, bf16[16,4096]{1,0:T(8,128)(2,1)S(1)}, u32[]{:S(2)}, u32[]{:S(2)}) collective-permute-start(bf16[16,4096]{1,0:T(8,128)(2,1)S(1)} %pad_maximum_fusion.1.refs_4_), channel_id=1, source_target_pairs={{0,1},{1,0},{2,3},{3,2},{4,5},{5,4},{6,7},{7,6},{8,9},{9,8},{10,11... | collective-permute-start | bytes 393224 | tf_op jit(solution)/shard_map/ppermute | solution.py:178
  20.7 2.0 %collective-permute-start.8 = (bf16[16,4096]{1,0:T(8,128)(2,1)S(1)}, bf16[16,4096]{1,0:T(8,128)(2,1)S(1)}, u32[]{:S(2)}, u32[]{:S(2)}) collective-permute-start(bf16[16,4096]{1,0:T(8,128)(2,1)S(1)} %pad_maximum_fusion.refs_4_), channel_id=1, source_target_pairs={{0,1},{1,0},{2,3},{3,2},{4,5},{5,4},{6,7},{7,6},{8,9},{9,8},{10,11... | collective-permute-start | bytes 393224 | tf_op jit(solution)/shard_map/ppermute | solution.py:178
  24.2 1.4 %collective-permute-start.13 = (bf16[8,8192]{1,0:T(8,128)(2,1)S(1)}, bf16[8,8192]{1,0:T(8,128)(2,1)S(1)}, u32[]{:S(2)}, u32[]{:S(2)}) collective-permute-start(bf16[8,8192]{1,0:T(8,128)(2,1)S(1)} %get-tuple-element.60), channel_id=1, source_target_pairs={{0,1},{1,0},{2,3},{3,2},{4,5},{5,4},{6,7},{7,6},{8,9},{9,8},{10,11... | collective-permute-start | bytes 393224 | tf_op jit(solution)/shard_map/ppermute | solution.py:178
  24.4 2.4 %collective-permute-start.10 = (bf16[24,8192]{1,0:T(8,128)(2,1)S(1)}, bf16[24,8192]{1,0:T(8,128)(2,1)S(1)}, u32[]{:S(2)}, u32[]{:S(2)}) collective-permute-start(bf16[24,8192]{1,0:T(8,128)(2,1)S(1)} %get-tuple-element.56), channel_id=1, source_target_pairs={{0,1},{1,0},{2,3},{3,2},{4,5},{5,4},{6,7},{7,6},{8,9},{9,8},{10,11... | collective-permute-start | bytes 1179656 | tf_op jit(solution)/shard_map/ppermute | solution.py:178
  25.6 6.9 %collective-permute-start.17 = (bf16[8,4608]{1,0:T(8,128)(2,1)S(1)}, bf16[8,4608]{1,0:T(8,128)(2,1)S(1)}, u32[]{:S(2)}, u32[]{:S(2)}) collective-permute-start(bf16[8,4608]{1,0:T(8,128)(2,1)S(1)} %slice.79), channel_id=1, source_target_pairs={{0,6},{1,7},{2,4},{3,5},{4,2},{5,3},{6,0},{7,1},{8,14},{9,15},{10,... | collective-permute-start | bytes 221192 | tf_op jit(solution)/shard_map/ppermute | solution.py:178
  26.9 2.5 %collective-permute-start.11 = (bf16[32,8192]{1,0:T(8,128)(2,1)S(1)}, bf16[32,8192]{1,0:T(8,128)(2,1)S(1)}, u32[]{:S(2)}, u32[]{:S(2)}) collective-permute-start(bf16[32,8192]{1,0:T(8,128)(2,1)S(1)} %get-tuple-element.58), channel_id=1, source_target_pairs={{0,1},{1,0},{2,3},{3,2},{4,5},{5,4},{6,7},{7,6},{8,9},{9,8},{10,11... | collective-permute-start | bytes 1572872 | tf_op jit(solution)/shard_map/ppermute | solution.py:178
  26.9 20.5 %copy-start = (s32[8192]{0:T(1024)S(1)}, s32[8192]{0:T(1024)}, u32[]{:S(2)}) copy-start(s32[8192]{0:T(1024)} %param.9) | copy-start | bytes 98308
  27.0 6.3 %collective-permute-start.18 = (bf16[8,4608]{1,0:T(8,128)(2,1)S(1)}, bf16[8,4608]{1,0:T(8,128)(2,1)S(1)}, u32[]{:S(2)}, u32[]{:S(2)}) collective-permute-start(bf16[8,4608]{1,0:T(8,128)(2,1)S(1)} %get-tuple-element.73), channel_id=1, source_target_pairs={{0,2},{1,5},{2,0},{3,7},{4,6},{5,1},{6,4},{7,3},{8,10},{9,13},{10,... | collective-permute-start | bytes 221192 | tf_op jit(solution)/shard_map/ppermute | solution.py:178
  28.5 5.8 %collective-permute-start.19 = (bf16[8,4608]{1,0:T(8,128)(2,1)S(1)}, bf16[8,4608]{1,0:T(8,128)(2,1)S(1)}, u32[]{:S(2)}, u32[]{:S(2)}) collective-permute-start(bf16[8,4608]{1,0:T(8,128)(2,1)S(1)} %get-tuple-element.74), channel_id=1, source_target_pairs={{0,4},{1,3},{2,6},{3,1},{4,0},{5,7},{6,2},{7,5},{8,12},{9,11},{10,... | collective-permute-start | bytes 221192 | tf_op jit(solution)/shard_map/ppermute | solution.py:178
  29.5 10.3 %collective-permute-start.12 = (bf16[16,8192]{1,0:T(8,128)(2,1)S(1)}, bf16[16,8192]{1,0:T(8,128)(2,1)S(1)}, u32[]{:S(2)}, u32[]{:S(2)}) collective-permute-start(bf16[16,8192]{1,0:T(8,128)(2,1)S(1)} %slice.101), channel_id=1, source_target_pairs={{0,4},{1,3},{2,6},{3,1},{4,0},{5,7},{6,2},{7,5},{8,12},{9,11},{10,... | collective-permute-start | bytes 786440 | tf_op jit(solution)/shard_map/ppermute | solution.py:178
  30.8 9.1 %collective-permute-start.14 = (bf16[8,3584]{1,0:T(8,128)(2,1)S(1)}, bf16[8,3584]{1,0:T(8,128)(2,1)S(1)}, u32[]{:S(2)}, u32[]{:S(2)}) collective-permute-start(bf16[8,3584]{1,0:T(8,128)(2,1)S(1)} %slice.74), channel_id=1, source_target_pairs={{0,6},{1,7},{2,4},{3,5},{4,2},{5,3},{6,0},{7,1},{8,14},{9,15},{10,... | collective-permute-start | bytes 172040 | tf_op jit(solution)/shard_map/ppermute | solution.py:178
  32.6 7.3 %collective-permute-start.15 = (bf16[8,3584]{1,0:T(8,128)(2,1)S(1)}, bf16[8,3584]{1,0:T(8,128)(2,1)S(1)}, u32[]{:S(2)}, u32[]{:S(2)}) collective-permute-start(bf16[8,3584]{1,0:T(8,128)(2,1)S(1)} %get-tuple-element.64), channel_id=1, source_target_pairs={{0,2},{1,5},{2,0},{3,7},{4,6},{5,1},{6,4},{7,3},{8,10},{9,13},{10,... | collective-permute-start | bytes 172040 | tf_op jit(solution)/shard_map/ppermute | solution.py:178
  33.2 6.6 %collective-permute-start.16 = (bf16[8,3584]{1,0:T(8,128)(2,1)S(1)}, bf16[8,3584]{1,0:T(8,128)(2,1)S(1)}, u32[]{:S(2)}, u32[]{:S(2)}) collective-permute-start(bf16[8,3584]{1,0:T(8,128)(2,1)S(1)} %get-tuple-element.65), channel_id=1, source_target_pairs={{0,4},{1,3},{2,6},{3,1},{4,0},{5,7},{6,2},{7,5},{8,12},{9,11},{10,... | collective-permute-start | bytes 172040 | tf_op jit(solution)/shard_map/ppermute | solution.py:178
  34.3 8.7 %collective-permute-start.20 = (bf16[8,4608]{1,0:T(8,128)(2,1)S(1)}, bf16[8,4608]{1,0:T(8,128)(2,1)S(1)}, u32[]{:S(2)}, u32[]{:S(2)}) collective-permute-start(bf16[8,4608]{1,0:T(8,128)(2,1)S(1)} %fusion.2), channel_id=1, source_target_pairs={{0,8},{1,9},{2,10},{3,11},{4,12},{5,13},{6,14},{7,15},{8,0},{9,1},... | collective-permute-start | bytes 221192 | tf_op jit(solution)/shard_map/ppermute | solution.py:178
  40.0 7.5 %collective-permute-start.22 = (bf16[8,8192]{1,0:T(8,128)(2,1)S(1)}, bf16[8,8192]{1,0:T(8,128)(2,1)S(1)}, u32[]{:S(2)}, u32[]{:S(2)}) collective-permute-start(bf16[8,8192]{1,0:T(8,128)(2,1)S(1)} %slice.102), channel_id=1, source_target_pairs={{0,2},{1,5},{2,0},{3,7},{4,6},{5,1},{6,4},{7,3},{8,10},{9,13},{10,... | collective-permute-start | bytes 393224 | tf_op jit(solution)/shard_map/ppermute | solution.py:178
  41.7 5.7 %collective-permute-start.21 = (bf16[8,3584]{1,0:T(8,128)(2,1)S(1)}, bf16[8,3584]{1,0:T(8,128)(2,1)S(1)}, u32[]{:S(2)}, u32[]{:S(2)}) collective-permute-start(bf16[8,3584]{1,0:T(8,128)(2,1)S(1)} %fusion.5), channel_id=1, source_target_pairs={{0,8},{1,9},{2,10},{3,11},{4,12},{5,13},{6,14},{7,15},{8,0},{9,1},... | collective-permute-start | bytes 172040 | tf_op jit(solution)/shard_map/ppermute | solution.py:178

commit v22 on v20

--- a/solution.py
+++ b/solution.py
@@ -183,9 +183,11 @@
         away = jnp.concatenate(away)
         near = [swap(tokens, m) for m in square]
         away, sign_pattern = lax.optimization_barrier((away, sign_pattern))
-        there = [swap(away, m) for m in square[:2]]
+        there = [None] * 3
+        for k in (2, 0):
+            there[k] = swap(away, square[k])
         away, near[0] = lax.optimization_barrier((away, near[0]))
-        there.append(swap(away, square[2]))
+        there[1] = swap(away, square[1])
         gate_w, up_w, down_w = load(gate_weight.T, up_weight.T, down_weight, away)
         there[0], *near = lax.optimization_barrier((there[0], *near))
         early = jnp.concatenate([near[1], near[0], near[2], away, there[0], tokens])

time: 44.8 us -> 44.9 us (level)
  waiting for transfers between devices: 16.1 us -> 16.9 us
  starting transfers between devices: 20.2 us -> 19.5 us
    ppermute x19, waiting for transfers between devices: 16.1 us -> 16.9 us  [swap(): lax.ppermute(value, 'gx', [(i, i ^ masks[i % 2]) for i in range(members)])]
    ppermute x19, starting transfers between devices: 20.2 us -> 19.5 us  [swap(): lax.ppermute(value, 'gx', [(i, i ^ masks[i % 2]) for i in range(members)])]
where the time goes in v22:
time: 44.9 us; the launch traced here: 44.7 us
  starting transfers between devices  19.5 us (43%)
  waiting for transfers between devices  16.9 us (38%)
  Pallas kernels  7.51 us (17%)
    ppermute x19, starting transfers between devices, swap(): lax.ppermute(value, 'gx', [(i, i ^ masks[i % 2]) for i in range(members)])  19.5 us
    ppermute x19, waiting for transfers between devices, swap(): lax.ppermute(value, 'gx', [(i, i ^ masks[i % 2]) for i in range(members)])  16.9 us
    pallas_call x1, Pallas kernels, load(): pl.pallas_call(load_kernel, out_shape=(shape, shape, jax.ShapeDtypeStruct...  4.46 us
    pallas_call x2, Pallas kernels, hidden_units(): pl.pallas_call(functools.partial(hidden_kernel, start, last), out_shape=(...  1.45 us
  transfers between devices with their start and end apart: 19, of which 9 were waited for; matrix products, arithmetic and copies ran while one was open for 1% of the time, Pallas kernels for 12%

profile of v22, /device:TPU:0, one launch (start us, length us, event | category | flops | bytes accessed | tf_op | source)
XLA Modules:
  0.0 44.7 jit_solution(5871213496394605577)
XLA Ops:
  0.0 4.0 %collective-permute-start = (bf16[8,8192]{1,0:T(8,128)(2,1)}, bf16[8,8192]{1,0:T(8,128)(2,1)S(1)}, u32[]{:S(2)}, u32[]{:S(2)}) collective-permute-start(bf16[8,8192]{1,0:T(8,128)(2,1)} %param.5), channel_id=1, source_target_pairs={{0,8},{1,9},{2,10},{3,11},{4,12},{5,13},{6,14},{7,15},{8,0},{9,1},... | collective-permute-start | bytes 393224 | tf_op jit(solution)/shard_map/ppermute | solution.py:175
  4.0 1.6 %collective-permute-start.1 = (bf16[8,8192]{1,0:T(8,128)(2,1)}, bf16[8,8192]{1,0:T(8,128)(2,1)S(1)}, u32[]{:S(2)}, u32[]{:S(2)}) collective-permute-start(bf16[8,8192]{1,0:T(8,128)(2,1)} %param.5), channel_id=1, source_target_pairs={{0,4},{1,3},{2,6},{3,1},{4,0},{5,7},{6,2},{7,5},{8,12},{9,11},{10,... | collective-permute-start | bytes 393224 | tf_op jit(solution)/shard_map/ppermute | solution.py:175
  5.6 1.5 %collective-permute-start.3 = (bf16[8,8192]{1,0:T(8,128)(2,1)}, bf16[8,8192]{1,0:T(8,128)(2,1)S(1)}, u32[]{:S(2)}, u32[]{:S(2)}) collective-permute-start(bf16[8,8192]{1,0:T(8,128)(2,1)} %param.5), channel_id=1, source_target_pairs={{0,2},{1,5},{2,0},{3,7},{4,6},{5,1},{6,4},{7,3},{8,10},{9,13},{10,... | collective-permute-start | bytes 393224 | tf_op jit(solution)/shard_map/ppermute | solution.py:175
  7.1 0.4 collective-permute-start.4
  7.5 3.1 %collective-permute-done._ = bf16[8,8192]{1,0:T(8,128)(2,1)S(1)} collective-permute-done((bf16[8,8192]{1,0:T(8,128)(2,1)}, bf16[8,8192]{1,0:T(8,128)(2,1)S(1)}, u32[]{:S(2)}, u32[]{:S(2)}) %collective-permute-start) | collective-permute-done | bytes 131104 | tf_op jit(solution)/shard_map/ppermute | solution.py:175
  10.7 0.8 %collective-permute-start.2 = (bf16[8,8192]{1,0:T(8,128)(2,1)S(1)}, bf16[8,8192]{1,0:T(8,128)(2,1)S(1)}, u32[]{:S(2)}, u32[]{:S(2)}) collective-permute-start(bf16[8,8192]{1,0:T(8,128)(2,1)S(1)} %collective-permute-done._), channel_id=1, source_target_pairs={{0,4},{1,3},{2,6},{3,1},{4,0},{5,7},{6,2},{7,5},{8,12},{9,11},{10,... | collective-permute-start | bytes 393224 | tf_op jit(solution)/shard_map/ppermute | solution.py:175
  11.4 2.3 %collective-permute-start.6 = (bf16[8,8192]{1,0:T(8,128)(2,1)S(1)}, bf16[8,8192]{1,0:T(8,128)(2,1)S(1)}, u32[]{:S(2)}, u32[]{:S(2)}) collective-permute-start(bf16[8,8192]{1,0:T(8,128)(2,1)S(1)} %collective-permute-done._), channel_id=1, source_target_pairs={{0,6},{1,7},{2,4},{3,5},{4,2},{5,3},{6,0},{7,1},{8,14},{9,15},{10,... | collective-permute-start | bytes 393224 | tf_op jit(solution)/shard_map/ppermute | solution.py:175
  13.7 0.0 collective-permute-done.1
  13.7 0.5 %collective-permute-start.5 = (bf16[8,8192]{1,0:T(8,128)(2,1)S(1)}, bf16[8,8192]{1,0:T(8,128)(2,1)S(1)}, u32[]{:S(2)}, u32[]{:S(2)}) collective-permute-start(bf16[8,8192]{1,0:T(8,128)(2,1)S(1)} %collective-permute-done._), channel_id=1, source_target_pairs={{0,2},{1,5},{2,0},{3,7},{4,6},{5,1},{6,4},{7,3},{8,10},{9,13},{10,... | collective-permute-start | bytes 393224 | tf_op jit(solution)/shard_map/ppermute | solution.py:175
  14.2 0.0 copy-start.1
  14.2 4.5 %shard_map.55 = (bf16[8192,224]{1,0:T(8,128)(2,1)S(1)}, bf16[8192,224]{1,0:T(8,128)(2,1)S(1)}, bf16[224,8192]{1,0:T(8,128)(2,1)S(1)}) custom-call(bf16[224,8192]{1,0:T(8,128)(2,1)} %bitcast.4, bf16[224,8192]{1,0:T(8,128)(2,1)} %bitcast.5, bf16[224,8192]{1,0:T(8,128)(2,1)} %down_hbm.1, bf16[8,8192]{1,0:T(8,128)(2,1)S(1)} %collective-permute-done._), custom_call_target="tpu_custom_call" | custom-call | bytes 11010048 | tf_op jit(solution)/shard_map/pallas_call | solution.py:44
  18.6 0.0 collective-permute-done.3
  18.6 0.0 collective-permute-done.4
  18.6 0.0 collective-permute-done.2
  18.7 0.0 copy-done.1
  18.8 0.1 collective-permute-start.7
  18.9 0.0 collective-permute-done.5
  18.9 1.7 %collective-permute-done.6 = bf16[8,8192]{1,0:T(8,128)(2,1)S(1)} collective-permute-done((bf16[8,8192]{1,0:T(8,128)(2,1)S(1)}, bf16[8,8192]{1,0:T(8,128)(2,1)S(1)}, u32[]{:S(2)}, u32[]{:S(2)}) %collective-permute-start.6) | collective-permute-done | bytes 131104 | tf_op jit(solution)/shard_map/ppermute | solution.py:175
  20.6 0.1 collective-permute-start.9
  20.7 0.6 %collective-permute-start.8 = (bf16[16,4096]{1,0:T(8,128)(2,1)S(1)}, bf16[16,4096]{1,0:T(8,128)(2,1)S(1)}, u32[]{:S(2)}, u32[]{:S(2)}) collective-permute-start(bf16[16,4096]{1,0:T(8,128)(2,1)S(1)} %pad_maximum_fusion.refs_4_), channel_id=1, source_target_pairs={{0,1},{1,0},{2,3},{3,2},{4,5},{5,4},{6,7},{7,6},{8,9},{9,8},{10,11... | collective-permute-start | bytes 393224 | tf_op jit(solution)/shard_map/ppermute | solution.py:175
  21.3 0.8 %collective-permute-done.9.refs_5_ = bf16[16,4096]{1,0:T(8,128)(2,1)S(1)} collective-permute-done((bf16[16,4096]{1,0:T(8,128)(2,1)S(1)}, bf16[16,4096]{1,0:T(8,128)(2,1)S(1)}, u32[]{:S(2)}, u32[]{:S(2)}) %collective-permute-start.9) | collective-permute-done | bytes 131104 | tf_op jit(solution)/shard_map/ppermute | solution.py:175
  22.0 0.0 collective-permute-done.7.refs_3_
  22.0 0.7 %shard_map.56 = (f32[128,224]{1,0:T(8,128)S(1)}, f32[128,224]{1,0:T(8,128)S(1)}) custom-call(bf16[8192,224]{1,0:T(8,128)(2,1)S(1)} %get-tuple-element.40.refs_0_, bf16[8192,224]{1,0:T(8,128)(2,1)S(1)} %get-tuple-element.41.refs_1_, bf16[48,8192]{1,0:T(8,128)(2,1)S(1)} %constant_dynamic-update-slice_fusion.refs_2_, ...), custom_call_target="tpu_custom_call" | custom-call | flops 469762048 | bytes 3670016 | tf_op jit(solution)/shard_map/pallas_call | solution.py:84
  22.7 0.0 collective-permute-done.8.refs_5_
  22.7 0.7 %shard_map.57.hidden_ref = bf16[128,224]{1,0:T(8,128)(2,1)S(1)} custom-call(bf16[8192,224]{1,0:T(8,128)(2,1)S(1)} %get-tuple-element.40.refs_0_, bf16[8192,224]{1,0:T(8,128)(2,1)S(1)} %get-tuple-element.41.refs_1_, bf16[48,8192]{1,0:T(8,128)(2,1)S(1)} %constant_dynamic-update-slice_fusion.refs_2_, bf16[48,8192]{1,0:T(8,128)(2,1)S(1)} %collective-permute-done.7.refs_3_, ...), custom_call_target="tpu_custom_call" | custom-call | flops 469762048 | bytes 3670016 | tf_op jit(solution)/shard_map/pallas_call | solution.py:84
  23.5 0.7 %shard_map.58 = (f32[32,8192]{1,0:T(8,128)S(1)}, f32[8,8192]{1,0:T(8,128)S(1)}, f32[24,8192]{1,0:T(8,128)S(1)}, bf16[32,8192]{1,0:T(8,128)(2,1)S(1)}, bf16[8,819...) custom-call(bf16[128,224]{1,0:T(8,128)(2,1)S(1)} %shard_map.57.hidden_ref, bf16[224,8192]{1,0:T(8,128)(2,1)S(1)} %get-tuple-element.47.down_ref), custom_call_target="tpu_custom_call" | custom-call | flops 469762048 | bytes 3670016 | tf_op jit(solution)/shard_map/pallas_call | solution.py:113
  24.2 0.2 collective-permute-start.13
  24.4 0.4 collective-permute-start.10
  24.8 0.8 %collective-permute-done.13 = bf16[8,8192]{1,0:T(8,128)(2,1)S(1)} collective-permute-done((bf16[8,8192]{1,0:T(8,128)(2,1)S(1)}, bf16[8,8192]{1,0:T(8,128)(2,1)S(1)}, u32[]{:S(2)}, u32[]{:S(2)}) %collective-permute-start.13) | collective-permute-done | bytes 131104 | tf_op jit(solution)/shard_map/ppermute | solution.py:175
  25.6 1.2 %collective-permute-start.14 = (bf16[8,8192]{1,0:T(8,128)(2,1)S(1)}, bf16[8,8192]{1,0:T(8,128)(2,1)S(1)}, u32[]{:S(2)}, u32[]{:S(2)}) collective-permute-start(bf16[8,8192]{1,0:T(8,128)(2,1)S(1)} %add_convert_fusion), channel_id=1, source_target_pairs={{0,6},{1,7},{2,4},{3,5},{4,2},{5,3},{6,0},{7,1},{8,14},{9,15},{10,... | collective-permute-start | bytes 393224 | tf_op jit(solution)/shard_map/ppermute | solution.py:175
  26.8 0.0 collective-permute-done.10
  26.8 0.0 collective-permute-start.11
  26.8 0.1 fusion.7
  26.9 0.0 copy-start
  26.9 1.9 %collective-permute-start.15 = (bf16[8,8192]{1,0:T(8,128)(2,1)S(1)}, bf16[8,8192]{1,0:T(8,128)(2,1)S(1)}, u32[]{:S(2)}, u32[]{:S(2)}) collective-permute-start(bf16[8,8192]{1,0:T(8,128)(2,1)S(1)} %get-tuple-element.59), channel_id=1, source_target_pairs={{0,4},{1,3},{2,6},{3,1},{4,0},{5,7},{6,2},{7,5},{8,12},{9,11},{10,... | collective-permute-start | bytes 393224 | tf_op jit(solution)/shard_map/ppermute | solution.py:175
  28.8 0.6 %collective-permute-start.16 = (bf16[8,8192]{1,0:T(8,128)(2,1)S(1)}, bf16[8,8192]{1,0:T(8,128)(2,1)S(1)}, u32[]{:S(2)}, u32[]{:S(2)}) collective-permute-start(bf16[8,8192]{1,0:T(8,128)(2,1)S(1)} %get-tuple-element.60), channel_id=1, source_target_pairs={{0,2},{1,5},{2,0},{3,7},{4,6},{5,1},{6,4},{7,3},{8,10},{9,13},{10,... | collective-permute-start | bytes 393224 | tf_op jit(solution)/shard_map/ppermute | solution.py:175
  29.4 0.0 collective-permute-done.11
  29.4 0.1 convert_add_fusion
  29.5 1.2 %collective-permute-start.12 = (bf16[16,8192]{1,0:T(8,128)(2,1)S(1)}, bf16[16,8192]{1,0:T(8,128)(2,1)S(1)}, u32[]{:S(2)}, u32[]{:S(2)}) collective-permute-start(bf16[16,8192]{1,0:T(8,128)(2,1)S(1)} %slice.67), channel_id=1, source_target_pairs={{0,4},{1,3},{2,6},{3,1},{4,0},{5,7},{6,2},{7,5},{8,12},{9,11},{10,... | collective-permute-start | bytes 786440 | tf_op jit(solution)/shard_map/ppermute | solution.py:175
  30.7 2.2 %collective-permute-done.14 = bf16[8,8192]{1,0:T(8,128)(2,1)S(1)} collective-permute-done((bf16[8,8192]{1,0:T(8,128)(2,1)S(1)}, bf16[8,8192]{1,0:T(8,128)(2,1)S(1)}, u32[]{:S(2)}, u32[]{:S(2)}) %collective-permute-start.14) | collective-permute-done | bytes 131104 | tf_op jit(solution)/shard_map/ppermute | solution.py:175
  32.9 2.0 %collective-permute-done.15 = bf16[8,8192]{1,0:T(8,128)(2,1)S(1)} collective-permute-done((bf16[8,8192]{1,0:T(8,128)(2,1)S(1)}, bf16[8,8192]{1,0:T(8,128)(2,1)S(1)}, u32[]{:S(2)}, u32[]{:S(2)}) %collective-permute-start.15) | collective-permute-done | bytes 131104 | tf_op jit(solution)/shard_map/ppermute | solution.py:175
  35.0 0.6 %collective-permute-done.16 = bf16[8,8192]{1,0:T(8,128)(2,1)S(1)} collective-permute-done((bf16[8,8192]{1,0:T(8,128)(2,1)S(1)}, bf16[8,8192]{1,0:T(8,128)(2,1)S(1)}, u32[]{:S(2)}, u32[]{:S(2)}) %collective-permute-start.16) | collective-permute-done | bytes 131104 | tf_op jit(solution)/shard_map/ppermute | solution.py:175
  35.5 0.1 fusion.2
  35.6 1.8 %collective-permute-start.17 = (bf16[8,8192]{1,0:T(8,128)(2,1)S(1)}, bf16[8,8192]{1,0:T(8,128)(2,1)S(1)}, u32[]{:S(2)}, u32[]{:S(2)}) collective-permute-start(bf16[8,8192]{1,0:T(8,128)(2,1)S(1)} %fusion.2), channel_id=1, source_target_pairs={{0,8},{1,9},{2,10},{3,11},{4,12},{5,13},{6,14},{7,15},{8,0},{9,1},... | collective-permute-start | bytes 393224 | tf_op jit(solution)/shard_map/ppermute | solution.py:175
  37.4 0.4 collective-permute-done.12
  37.8 0.1 slice_add_fusion
  37.9 0.6 %collective-permute-start.18 = (bf16[8,8192]{1,0:T(8,128)(2,1)S(1)}, bf16[8,8192]{1,0:T(8,128)(2,1)S(1)}, u32[]{:S(2)}, u32[]{:S(2)}) collective-permute-start(bf16[8,8192]{1,0:T(8,128)(2,1)S(1)} %slice.68), channel_id=1, source_target_pairs={{0,2},{1,5},{2,0},{3,7},{4,6},{5,1},{6,4},{7,3},{8,10},{9,13},{10,... | collective-permute-start | bytes 393224 | tf_op jit(solution)/shard_map/ppermute | solution.py:175
  38.6 5.2 %collective-permute-done.17.refs_1_ = bf16[8,8192]{1,0:T(8,128)(2,1)S(1)} collective-permute-done((bf16[8,8192]{1,0:T(8,128)(2,1)S(1)}, bf16[8,8192]{1,0:T(8,128)(2,1)S(1)}, u32[]{:S(2)}, u32[]{:S(2)}) %collective-permute-start.17) | collective-permute-done | bytes 131104 | tf_op jit(solution)/shard_map/ppermute | solution.py:175
  43.8 0.0 collective-permute-done.18.refs_2_
  43.8 0.0 copy-done
  43.8 0.9 %shard_map.59 = bf16[8,8192]{1,0:T(8,128)(2,1)} custom-call(f32[8,8192]{1,0:T(8,128)S(1)} %slice.52.refs_0_, bf16[8,8192]{1,0:T(8,128)(2,1)S(1)} %collective-permute-done.17.refs_1_, bf16[8,8192]{1,0:T(8,128)(2,1)S(1)} %collective-permute-done.18.refs_2_, s32[1,8192]{1,0:T(1,128)S(1)} %bitcast.3, bf16[256,128]{1,0:T(8,128)(2,1)S(1)} %pad_maximum_fusion.2.refs_4_), custom_call_target="tpu_custom_call" | custom-call | tf_op jit(solution)/shard_map/pallas_call | solution.py:153
  (16 shorter events, 0.3 us)
Async XLA Ops:
  0.0 10.7 %collective-permute-start = (bf16[8,8192]{1,0:T(8,128)(2,1)}, bf16[8,8192]{1,0:T(8,128)(2,1)S(1)}, u32[]{:S(2)}, u32[]{:S(2)}) collective-permute-start(bf16[8,8192]{1,0:T(8,128)(2,1)} %param.5), channel_id=1, source_target_pairs={{0,8},{1,9},{2,10},{3,11},{4,12},{5,13},{6,14},{7,15},{8,0},{9,1},... | collective-permute-start | bytes 393224 | tf_op jit(solution)/shard_map/ppermute | solution.py:175
  4.0 9.7 %collective-permute-start.1 = (bf16[8,8192]{1,0:T(8,128)(2,1)}, bf16[8,8192]{1,0:T(8,128)(2,1)S(1)}, u32[]{:S(2)}, u32[]{:S(2)}) collective-permute-start(bf16[8,8192]{1,0:T(8,128)(2,1)} %param.5), channel_id=1, source_target_pairs={{0,4},{1,3},{2,6},{3,1},{4,0},{5,7},{6,2},{7,5},{8,12},{9,11},{10,... | collective-permute-start | bytes 393224 | tf_op jit(solution)/shard_map/ppermute | solution.py:175
  5.6 13.0 %collective-permute-start.3 = (bf16[8,8192]{1,0:T(8,128)(2,1)}, bf16[8,8192]{1,0:T(8,128)(2,1)S(1)}, u32[]{:S(2)}, u32[]{:S(2)}) collective-permute-start(bf16[8,8192]{1,0:T(8,128)(2,1)} %param.5), channel_id=1, source_target_pairs={{0,2},{1,5},{2,0},{3,7},{4,6},{5,1},{6,4},{7,3},{8,10},{9,13},{10,... | collective-permute-start | bytes 393224 | tf_op jit(solution)/shard_map/ppermute | solution.py:175
  7.1 11.5 %collective-permute-start.4 = (bf16[8,8192]{1,0:T(8,128)(2,1)}, bf16[8,8192]{1,0:T(8,128)(2,1)S(1)}, u32[]{:S(2)}, u32[]{:S(2)}) collective-permute-start(bf16[8,8192]{1,0:T(8,128)(2,1)} %param.5), channel_id=1, source_target_pairs={{0,6},{1,7},{2,4},{3,5},{4,2},{5,3},{6,0},{7,1},{8,14},{9,15},{10,... | collective-permute-start | bytes 393224 | tf_op jit(solution)/shard_map/ppermute | solution.py:175
  10.7 8.0 %collective-permute-start.2 = (bf16[8,8192]{1,0:T(8,128)(2,1)S(1)}, bf16[8,8192]{1,0:T(8,128)(2,1)S(1)}, u32[]{:S(2)}, u32[]{:S(2)}) collective-permute-start(bf16[8,8192]{1,0:T(8,128)(2,1)S(1)} %collective-permute-done._), channel_id=1, source_target_pairs={{0,4},{1,3},{2,6},{3,1},{4,0},{5,7},{6,2},{7,5},{8,12},{9,11},{10,... | collective-permute-start | bytes 393224 | tf_op jit(solution)/shard_map/ppermute | solution.py:175
  11.4 9.1 %collective-permute-start.6 = (bf16[8,8192]{1,0:T(8,128)(2,1)S(1)}, bf16[8,8192]{1,0:T(8,128)(2,1)S(1)}, u32[]{:S(2)}, u32[]{:S(2)}) collective-permute-start(bf16[8,8192]{1,0:T(8,128)(2,1)S(1)} %collective-permute-done._), channel_id=1, source_target_pairs={{0,6},{1,7},{2,4},{3,5},{4,2},{5,3},{6,0},{7,1},{8,14},{9,15},{10,... | collective-permute-start | bytes 393224 | tf_op jit(solution)/shard_map/ppermute | solution.py:175
  13.7 5.2 %collective-permute-start.5 = (bf16[8,8192]{1,0:T(8,128)(2,1)S(1)}, bf16[8,8192]{1,0:T(8,128)(2,1)S(1)}, u32[]{:S(2)}, u32[]{:S(2)}) collective-permute-start(bf16[8,8192]{1,0:T(8,128)(2,1)S(1)} %collective-permute-done._), channel_id=1, source_target_pairs={{0,2},{1,5},{2,0},{3,7},{4,6},{5,1},{6,4},{7,3},{8,10},{9,13},{10,... | collective-permute-start | bytes 393224 | tf_op jit(solution)/shard_map/ppermute | solution.py:175
  14.2 4.6 %copy-start.1 = (bf16[8,8192]{1,0:T(8,128)(2,1)S(1)}, bf16[8,8192]{1,0:T(8,128)(2,1)}, u32[]{:S(2)}) copy-start(bf16[8,8192]{1,0:T(8,128)(2,1)} %param.5) | copy-start | bytes 393220
  18.8 3.2 %collective-permute-start.7 = (bf16[48,8192]{1,0:T(8,128)(2,1)S(1)}, bf16[48,8192]{1,0:T(8,128)(2,1)S(1)}, u32[]{:S(2)}, u32[]{:S(2)}) collective-permute-start(bf16[48,8192]{1,0:T(8,128)(2,1)S(1)} %constant_dynamic-update-slice_fusion.refs_2_), channel_id=1, source_target_pairs={{0,1},{1,0},{2,3},{3,2},{4,5},{5,4},{6,7},{7,6},{8,9},{9,8},{10,11... | collective-permute-start | bytes 2359304 | tf_op jit(solution)/shard_map/ppermute | solution.py:175
  20.6 1.4 %collective-permute-start.9 = (bf16[16,4096]{1,0:T(8,128)(2,1)S(1)}, bf16[16,4096]{1,0:T(8,128)(2,1)S(1)}, u32[]{:S(2)}, u32[]{:S(2)}) collective-permute-start(bf16[16,4096]{1,0:T(8,128)(2,1)S(1)} %pad_maximum_fusion.1.refs_4_), channel_id=1, source_target_pairs={{0,1},{1,0},{2,3},{3,2},{4,5},{5,4},{6,7},{7,6},{8,9},{9,8},{10,11... | collective-permute-start | bytes 393224 | tf_op jit(solution)/shard_map/ppermute | solution.py:175
  20.7 2.0 %collective-permute-start.8 = (bf16[16,4096]{1,0:T(8,128)(2,1)S(1)}, bf16[16,4096]{1,0:T(8,128)(2,1)S(1)}, u32[]{:S(2)}, u32[]{:S(2)}) collective-permute-start(bf16[16,4096]{1,0:T(8,128)(2,1)S(1)} %pad_maximum_fusion.refs_4_), channel_id=1, source_target_pairs={{0,1},{1,0},{2,3},{3,2},{4,5},{5,4},{6,7},{7,6},{8,9},{9,8},{10,11... | collective-permute-start | bytes 393224 | tf_op jit(solution)/shard_map/ppermute | solution.py:175
  24.2 1.4 %collective-permute-start.13 = (bf16[8,8192]{1,0:T(8,128)(2,1)S(1)}, bf16[8,8192]{1,0:T(8,128)(2,1)S(1)}, u32[]{:S(2)}, u32[]{:S(2)}) collective-permute-start(bf16[8,8192]{1,0:T(8,128)(2,1)S(1)} %get-tuple-element.55), channel_id=1, source_target_pairs={{0,1},{1,0},{2,3},{3,2},{4,5},{5,4},{6,7},{7,6},{8,9},{9,8},{10,11... | collective-permute-start | bytes 393224 | tf_op jit(solution)/shard_map/ppermute | solution.py:175
  24.4 2.4 %collective-permute-start.10 = (bf16[24,8192]{1,0:T(8,128)(2,1)S(1)}, bf16[24,8192]{1,0:T(8,128)(2,1)S(1)}, u32[]{:S(2)}, u32[]{:S(2)}) collective-permute-start(bf16[24,8192]{1,0:T(8,128)(2,1)S(1)} %get-tuple-element.49), channel_id=1, source_target_pairs={{0,1},{1,0},{2,3},{3,2},{4,5},{5,4},{6,7},{7,6},{8,9},{9,8},{10,11... | collective-permute-start | bytes 1179656 | tf_op jit(solution)/shard_map/ppermute | solution.py:175
  25.6 7.3 %collective-permute-start.14 = (bf16[8,8192]{1,0:T(8,128)(2,1)S(1)}, bf16[8,8192]{1,0:T(8,128)(2,1)S(1)}, u32[]{:S(2)}, u32[]{:S(2)}) collective-permute-start(bf16[8,8192]{1,0:T(8,128)(2,1)S(1)} %add_convert_fusion), channel_id=1, source_target_pairs={{0,6},{1,7},{2,4},{3,5},{4,2},{5,3},{6,0},{7,1},{8,14},{9,15},{10,... | collective-permute-start | bytes 393224 | tf_op jit(solution)/shard_map/ppermute | solution.py:175
  26.8 2.6 %collective-permute-start.11 = (bf16[32,8192]{1,0:T(8,128)(2,1)S(1)}, bf16[32,8192]{1,0:T(8,128)(2,1)S(1)}, u32[]{:S(2)}, u32[]{:S(2)}) collective-permute-start(bf16[32,8192]{1,0:T(8,128)(2,1)S(1)} %get-tuple-element.51), channel_id=1, source_target_pairs={{0,1},{1,0},{2,3},{3,2},{4,5},{5,4},{6,7},{7,6},{8,9},{9,8},{10,11... | collective-permute-start | bytes 1572872 | tf_op jit(solution)/shard_map/ppermute | solution.py:175
  26.9 16.9 %copy-start = (s32[8192]{0:T(1024)S(1)}, s32[8192]{0:T(1024)}, u32[]{:S(2)}) copy-start(s32[8192]{0:T(1024)} %param.9) | copy-start | bytes 98308
  26.9 8.0 %collective-permute-start.15 = (bf16[8,8192]{1,0:T(8,128)(2,1)S(1)}, bf16[8,8192]{1,0:T(8,128)(2,1)S(1)}, u32[]{:S(2)}, u32[]{:S(2)}) collective-permute-start(bf16[8,8192]{1,0:T(8,128)(2,1)S(1)} %get-tuple-element.59), channel_id=1, source_target_pairs={{0,4},{1,3},{2,6},{3,1},{4,0},{5,7},{6,2},{7,5},{8,12},{9,11},{10,... | collective-permute-start | bytes 393224 | tf_op jit(solution)/shard_map/ppermute | solution.py:175
  28.8 6.7 %collective-permute-start.16 = (bf16[8,8192]{1,0:T(8,128)(2,1)S(1)}, bf16[8,8192]{1,0:T(8,128)(2,1)S(1)}, u32[]{:S(2)}, u32[]{:S(2)}) collective-permute-start(bf16[8,8192]{1,0:T(8,128)(2,1)S(1)} %get-tuple-element.60), channel_id=1, source_target_pairs={{0,2},{1,5},{2,0},{3,7},{4,6},{5,1},{6,4},{7,3},{8,10},{9,13},{10,... | collective-permute-start | bytes 393224 | tf_op jit(solution)/shard_map/ppermute | solution.py:175
  29.5 8.2 %collective-permute-start.12 = (bf16[16,8192]{1,0:T(8,128)(2,1)S(1)}, bf16[16,8192]{1,0:T(8,128)(2,1)S(1)}, u32[]{:S(2)}, u32[]{:S(2)}) collective-permute-start(bf16[16,8192]{1,0:T(8,128)(2,1)S(1)} %slice.67), channel_id=1, source_target_pairs={{0,4},{1,3},{2,6},{3,1},{4,0},{5,7},{6,2},{7,5},{8,12},{9,11},{10,... | collective-permute-start | bytes 786440 | tf_op jit(solution)/shard_map/ppermute | solution.py:175
  35.6 8.2 %collective-permute-start.17 = (bf16[8,8192]{1,0:T(8,128)(2,1)S(1)}, bf16[8,8192]{1,0:T(8,128)(2,1)S(1)}, u32[]{:S(2)}, u32[]{:S(2)}) collective-permute-start(bf16[8,8192]{1,0:T(8,128)(2,1)S(1)} %fusion.2), channel_id=1, source_target_pairs={{0,8},{1,9},{2,10},{3,11},{4,12},{5,13},{6,14},{7,15},{8,0},{9,1},... | collective-permute-start | bytes 393224 | tf_op jit(solution)/shard_map/ppermute | solution.py:175
  37.9 6.0 %collective-permute-start.18 = (bf16[8,8192]{1,0:T(8,128)(2,1)S(1)}, bf16[8,8192]{1,0:T(8,128)(2,1)S(1)}, u32[]{:S(2)}, u32[]{:S(2)}) collective-permute-start(bf16[8,8192]{1,0:T(8,128)(2,1)S(1)} %slice.68), channel_id=1, source_target_pairs={{0,2},{1,5},{2,0},{3,7},{4,6},{5,1},{6,4},{7,3},{8,10},{9,13},{10,... | collective-permute-start | bytes 393224 | tf_op jit(solution)/shard_map/ppermute | solution.py:175

commit v23 on v20

--- a/solution.py
+++ b/solution.py
@@ -163,7 +163,7 @@
     members = mesh.shape["gx"]
     assert members & (members - 1) == 0 and members >= 16
 
-    square = ((4, 2), (2, 4), (6, 6))
+    square = ((2, 4), (4, 2), (6, 6))
     far = []
     mask = members // 2
     while mask > 4:

time: 44.8 us -> 46.8 us (1.045)
  waiting for transfers between devices: 16.1 us -> 18 us
    ppermute x19, waiting for transfers between devices: 16.1 us -> 18 us  [swap(): lax.ppermute(value, 'gx', [(i, i ^ masks[i % 2]) for i in range(members)])]
  transfers between devices with their start and end apart: 19 -> 19, of which waited for: 9 -> 11; matrix products, arithmetic and copies ran while one was open for 1% -> 1% of each run, Pallas kernels for 12% -> 11%
where the time goes in v23:
time: 46.8 us; the launch traced here: 46.6 us
  starting transfers between devices  20.3 us (43%)
  waiting for transfers between devices  18 us (38%)
  Pallas kernels  7.51 us (16%)
    ppermute x19, starting transfers between devices, swap(): lax.ppermute(value, 'gx', [(i, i ^ masks[i % 2]) for i in range(members)])  20.3 us
    ppermute x19, waiting for transfers between devices, swap(): lax.ppermute(value, 'gx', [(i, i ^ masks[i % 2]) for i in range(members)])  18 us
    pallas_call x1, Pallas kernels, load(): pl.pallas_call(load_kernel, out_shape=(shape, shape, jax.ShapeDtypeStruct...  4.46 us
    pallas_call x2, Pallas kernels, hidden_units(): pl.pallas_call(functools.partial(hidden_kernel, start, last), out_shape=(...  1.45 us
  transfers between devices with their start and end apart: 19, of which 11 were waited for; matrix products, arithmetic and copies ran while one was open for 1% of the time, Pallas kernels for 11%

profile of v23, /device:TPU:0, one launch (start us, length us, event | category | flops | bytes accessed | tf_op | source)
XLA Modules:
  0.0 46.6 jit_solution(9572818648744366030)
XLA Ops:
  0.0 4.0 %collective-permute-start = (bf16[8,8192]{1,0:T(8,128)(2,1)}, bf16[8,8192]{1,0:T(8,128)(2,1)S(1)}, u32[]{:S(2)}, u32[]{:S(2)}) collective-permute-start(bf16[8,8192]{1,0:T(8,128)(2,1)} %param.5), channel_id=1, source_target_pairs={{0,8},{1,9},{2,10},{3,11},{4,12},{5,13},{6,14},{7,15},{8,0},{9,1},... | collective-permute-start | bytes 393224 | tf_op jit(solution)/shard_map/ppermute | solution.py:175
  4.0 1.5 %collective-permute-start.1 = (bf16[8,8192]{1,0:T(8,128)(2,1)}, bf16[8,8192]{1,0:T(8,128)(2,1)S(1)}, u32[]{:S(2)}, u32[]{:S(2)}) collective-permute-start(bf16[8,8192]{1,0:T(8,128)(2,1)} %param.5), channel_id=1, source_target_pairs={{0,2},{1,5},{2,0},{3,7},{4,6},{5,1},{6,4},{7,3},{8,10},{9,13},{10,... | collective-permute-start | bytes 393224 | tf_op jit(solution)/shard_map/ppermute | solution.py:175
  5.6 1.6 %collective-permute-start.3 = (bf16[8,8192]{1,0:T(8,128)(2,1)}, bf16[8,8192]{1,0:T(8,128)(2,1)S(1)}, u32[]{:S(2)}, u32[]{:S(2)}) collective-permute-start(bf16[8,8192]{1,0:T(8,128)(2,1)} %param.5), channel_id=1, source_target_pairs={{0,4},{1,3},{2,6},{3,1},{4,0},{5,7},{6,2},{7,5},{8,12},{9,11},{10,... | collective-permute-start | bytes 393224 | tf_op jit(solution)/shard_map/ppermute | solution.py:175
  7.1 0.4 collective-permute-start.4
  7.5 3.1 %collective-permute-done._ = bf16[8,8192]{1,0:T(8,128)(2,1)S(1)} collective-permute-done((bf16[8,8192]{1,0:T(8,128)(2,1)}, bf16[8,8192]{1,0:T(8,128)(2,1)S(1)}, u32[]{:S(2)}, u32[]{:S(2)}) %collective-permute-start) | collective-permute-done | bytes 131104 | tf_op jit(solution)/shard_map/ppermute | solution.py:175
  10.6 1.6 %collective-permute-start.2 = (bf16[8,8192]{1,0:T(8,128)(2,1)S(1)}, bf16[8,8192]{1,0:T(8,128)(2,1)S(1)}, u32[]{:S(2)}, u32[]{:S(2)}) collective-permute-start(bf16[8,8192]{1,0:T(8,128)(2,1)S(1)} %collective-permute-done._), channel_id=1, source_target_pairs={{0,2},{1,5},{2,0},{3,7},{4,6},{5,1},{6,4},{7,3},{8,10},{9,13},{10,... | collective-permute-start | bytes 393224 | tf_op jit(solution)/shard_map/ppermute | solution.py:175
  12.2 0.7 %collective-permute-start.5 = (bf16[8,8192]{1,0:T(8,128)(2,1)S(1)}, bf16[8,8192]{1,0:T(8,128)(2,1)S(1)}, u32[]{:S(2)}, u32[]{:S(2)}) collective-permute-start(bf16[8,8192]{1,0:T(8,128)(2,1)S(1)} %collective-permute-done._), channel_id=1, source_target_pairs={{0,4},{1,3},{2,6},{3,1},{4,0},{5,7},{6,2},{7,5},{8,12},{9,11},{10,... | collective-permute-start | bytes 393224 | tf_op jit(solution)/shard_map/ppermute | solution.py:175
  12.9 0.0 collective-permute-done.1
  12.9 1.2 %collective-permute-start.6 = (bf16[8,8192]{1,0:T(8,128)(2,1)S(1)}, bf16[8,8192]{1,0:T(8,128)(2,1)S(1)}, u32[]{:S(2)}, u32[]{:S(2)}) collective-permute-start(bf16[8,8192]{1,0:T(8,128)(2,1)S(1)} %collective-permute-done._), channel_id=1, source_target_pairs={{0,6},{1,7},{2,4},{3,5},{4,2},{5,3},{6,0},{7,1},{8,14},{9,15},{10,... | collective-permute-start | bytes 393224 | tf_op jit(solution)/shard_map/ppermute | solution.py:175
  14.1 0.0 copy-start.1
  14.1 4.5 %shard_map.55 = (bf16[8192,224]{1,0:T(8,128)(2,1)S(1)}, bf16[8192,224]{1,0:T(8,128)(2,1)S(1)}, bf16[224,8192]{1,0:T(8,128)(2,1)S(1)}) custom-call(bf16[224,8192]{1,0:T(8,128)(2,1)} %bitcast.4, bf16[224,8192]{1,0:T(8,128)(2,1)} %bitcast.5, bf16[224,8192]{1,0:T(8,128)(2,1)} %down_hbm.1, bf16[8,8192]{1,0:T(8,128)(2,1)S(1)} %collective-permute-done._), custom_call_target="tpu_custom_call" | custom-call | bytes 11010048 | tf_op jit(solution)/shard_map/pallas_call | solution.py:44
  18.6 0.0 collective-permute-done.3
  18.6 0.0 collective-permute-done.4
  18.6 0.8 %collective-permute-done.2 = bf16[8,8192]{1,0:T(8,128)(2,1)S(1)} collective-permute-done((bf16[8,8192]{1,0:T(8,128)(2,1)S(1)}, bf16[8,8192]{1,0:T(8,128)(2,1)S(1)}, u32[]{:S(2)}, u32[]{:S(2)}) %collective-permute-start.2) | collective-permute-done | bytes 131104 | tf_op jit(solution)/shard_map/ppermute | solution.py:175
  19.6 0.0 copy-done.1
  19.6 0.1 collective-permute-start.7
  19.7 0.9 %collective-permute-done.6 = bf16[8,8192]{1,0:T(8,128)(2,1)S(1)} collective-permute-done((bf16[8,8192]{1,0:T(8,128)(2,1)S(1)}, bf16[8,8192]{1,0:T(8,128)(2,1)S(1)}, u32[]{:S(2)}, u32[]{:S(2)}) %collective-permute-start.6) | collective-permute-done | bytes 131104 | tf_op jit(solution)/shard_map/ppermute | solution.py:175
  20.6 0.0 collective-permute-done.5
  20.6 0.1 collective-permute-start.9
  20.7 0.6 %collective-permute-start.8 = (bf16[16,4096]{1,0:T(8,128)(2,1)S(1)}, bf16[16,4096]{1,0:T(8,128)(2,1)S(1)}, u32[]{:S(2)}, u32[]{:S(2)}) collective-permute-start(bf16[16,4096]{1,0:T(8,128)(2,1)S(1)} %pad_maximum_fusion.refs_4_), channel_id=1, source_target_pairs={{0,1},{1,0},{2,3},{3,2},{4,5},{5,4},{6,7},{7,6},{8,9},{9,8},{10,11... | collective-permute-start | bytes 393224 | tf_op jit(solution)/shard_map/ppermute | solution.py:175
  21.3 0.9 %collective-permute-done.9.refs_5_ = bf16[16,4096]{1,0:T(8,128)(2,1)S(1)} collective-permute-done((bf16[16,4096]{1,0:T(8,128)(2,1)S(1)}, bf16[16,4096]{1,0:T(8,128)(2,1)S(1)}, u32[]{:S(2)}, u32[]{:S(2)}) %collective-permute-start.9) | collective-permute-done | bytes 131104 | tf_op jit(solution)/shard_map/ppermute | solution.py:175
  22.1 0.0 collective-permute-done.7.refs_3_
  22.1 0.7 %shard_map.56 = (f32[128,224]{1,0:T(8,128)S(1)}, f32[128,224]{1,0:T(8,128)S(1)}) custom-call(bf16[8192,224]{1,0:T(8,128)(2,1)S(1)} %get-tuple-element.40.refs_0_, bf16[8192,224]{1,0:T(8,128)(2,1)S(1)} %get-tuple-element.41.refs_1_, bf16[48,8192]{1,0:T(8,128)(2,1)S(1)} %constant_dynamic-update-slice_fusion.refs_2_, ...), custom_call_target="tpu_custom_call" | custom-call | flops 469762048 | bytes 3670016 | tf_op jit(solution)/shard_map/pallas_call | solution.py:84
  22.8 0.0 collective-permute-done.8.refs_5_
  22.9 0.7 %shard_map.57.hidden_ref = bf16[128,224]{1,0:T(8,128)(2,1)S(1)} custom-call(bf16[8192,224]{1,0:T(8,128)(2,1)S(1)} %get-tuple-element.40.refs_0_, bf16[8192,224]{1,0:T(8,128)(2,1)S(1)} %get-tuple-element.41.refs_1_, bf16[48,8192]{1,0:T(8,128)(2,1)S(1)} %constant_dynamic-update-slice_fusion.refs_2_, bf16[48,8192]{1,0:T(8,128)(2,1)S(1)} %collective-permute-done.7.refs_3_, ...), custom_call_target="tpu_custom_call" | custom-call | flops 469762048 | bytes 3670016 | tf_op jit(solution)/shard_map/pallas_call | solution.py:84
  23.6 0.7 %shard_map.58 = (f32[32,8192]{1,0:T(8,128)S(1)}, f32[8,8192]{1,0:T(8,128)S(1)}, f32[24,8192]{1,0:T(8,128)S(1)}, bf16[32,8192]{1,0:T(8,128)(2,1)S(1)}, bf16[8,819...) custom-call(bf16[128,224]{1,0:T(8,128)(2,1)S(1)} %shard_map.57.hidden_ref, bf16[224,8192]{1,0:T(8,128)(2,1)S(1)} %get-tuple-element.47.down_ref), custom_call_target="tpu_custom_call" | custom-call | flops 469762048 | bytes 3670016 | tf_op jit(solution)/shard_map/pallas_call | solution.py:113
  24.3 0.2 collective-permute-start.13
  24.5 0.4 collective-permute-start.10
  24.9 0.8 %collective-permute-done.13 = bf16[8,8192]{1,0:T(8,128)(2,1)S(1)} collective-permute-done((bf16[8,8192]{1,0:T(8,128)(2,1)S(1)}, bf16[8,8192]{1,0:T(8,128)(2,1)S(1)}, u32[]{:S(2)}, u32[]{:S(2)}) %collective-permute-start.13) | collective-permute-done | bytes 131104 | tf_op jit(solution)/shard_map/ppermute | solution.py:175
  25.8 1.0 %collective-permute-start.14 = (bf16[8,8192]{1,0:T(8,128)(2,1)S(1)}, bf16[8,8192]{1,0:T(8,128)(2,1)S(1)}, u32[]{:S(2)}, u32[]{:S(2)}) collective-permute-start(bf16[8,8192]{1,0:T(8,128)(2,1)S(1)} %add_convert_fusion), channel_id=1, source_target_pairs={{0,6},{1,7},{2,4},{3,5},{4,2},{5,3},{6,0},{7,1},{8,14},{9,15},{10,... | collective-permute-start | bytes 393224 | tf_op jit(solution)/shard_map/ppermute | solution.py:175
  26.8 0.0 collective-permute-done.10
  26.8 0.0 collective-permute-start.11
  26.8 0.1 fusion.7
  26.9 0.0 copy-start
  26.9 2.3 %collective-permute-start.15 = (bf16[8,8192]{1,0:T(8,128)(2,1)S(1)}, bf16[8,8192]{1,0:T(8,128)(2,1)S(1)}, u32[]{:S(2)}, u32[]{:S(2)}) collective-permute-start(bf16[8,8192]{1,0:T(8,128)(2,1)S(1)} %get-tuple-element.59), channel_id=1, source_target_pairs={{0,2},{1,5},{2,0},{3,7},{4,6},{5,1},{6,4},{7,3},{8,10},{9,13},{10,... | collective-permute-start | bytes 393224 | tf_op jit(solution)/shard_map/ppermute | solution.py:175
  29.3 0.8 %collective-permute-start.16 = (bf16[8,8192]{1,0:T(8,128)(2,1)S(1)}, bf16[8,8192]{1,0:T(8,128)(2,1)S(1)}, u32[]{:S(2)}, u32[]{:S(2)}) collective-permute-start(bf16[8,8192]{1,0:T(8,128)(2,1)S(1)} %get-tuple-element.60), channel_id=1, source_target_pairs={{0,4},{1,3},{2,6},{3,1},{4,0},{5,7},{6,2},{7,5},{8,12},{9,11},{10,... | collective-permute-start | bytes 393224 | tf_op jit(solution)/shard_map/ppermute | solution.py:175
  30.0 0.0 collective-permute-done.11
  30.0 0.1 convert_add_fusion
  30.2 2.0 %collective-permute-start.12 = (bf16[16,8192]{1,0:T(8,128)(2,1)S(1)}, bf16[16,8192]{1,0:T(8,128)(2,1)S(1)}, u32[]{:S(2)}, u32[]{:S(2)}) collective-permute-start(bf16[16,8192]{1,0:T(8,128)(2,1)S(1)} %slice.67), channel_id=1, source_target_pairs={{0,2},{1,5},{2,0},{3,7},{4,6},{5,1},{6,4},{7,3},{8,10},{9,13},{10,... | collective-permute-start | bytes 786440 | tf_op jit(solution)/shard_map/ppermute | solution.py:175
  32.2 0.9 %collective-permute-done.14 = bf16[8,8192]{1,0:T(8,128)(2,1)S(1)} collective-permute-done((bf16[8,8192]{1,0:T(8,128)(2,1)S(1)}, bf16[8,8192]{1,0:T(8,128)(2,1)S(1)}, u32[]{:S(2)}, u32[]{:S(2)}) %collective-permute-start.14) | collective-permute-done | bytes 131104 | tf_op jit(solution)/shard_map/ppermute | solution.py:175
  33.0 2.0 %collective-permute-done.15 = bf16[8,8192]{1,0:T(8,128)(2,1)S(1)} collective-permute-done((bf16[8,8192]{1,0:T(8,128)(2,1)S(1)}, bf16[8,8192]{1,0:T(8,128)(2,1)S(1)}, u32[]{:S(2)}, u32[]{:S(2)}) %collective-permute-start.15) | collective-permute-done | bytes 131104 | tf_op jit(solution)/shard_map/ppermute | solution.py:175
  35.0 1.8 %collective-permute-done.16 = bf16[8,8192]{1,0:T(8,128)(2,1)S(1)} collective-permute-done((bf16[8,8192]{1,0:T(8,128)(2,1)S(1)}, bf16[8,8192]{1,0:T(8,128)(2,1)S(1)}, u32[]{:S(2)}, u32[]{:S(2)}) %collective-permute-start.16) | collective-permute-done | bytes 131104 | tf_op jit(solution)/shard_map/ppermute | solution.py:175
  36.9 0.1 fusion.2
  36.9 0.3 collective-permute-start.17
  37.3 0.6 %collective-permute-done.12 = bf16[16,8192]{1,0:T(8,128)(2,1)S(1)} collective-permute-done((bf16[16,8192]{1,0:T(8,128)(2,1)S(1)}, bf16[16,8192]{1,0:T(8,128)(2,1)S(1)}, u32[]{:S(2)}, u32[]{:S(2)}) %collective-permute-start.12) | collective-permute-done | bytes 262176 | tf_op jit(solution)/shard_map/ppermute | solution.py:175
  37.9 0.1 slice_add_fusion
  38.0 1.5 %collective-permute-start.18 = (bf16[8,8192]{1,0:T(8,128)(2,1)S(1)}, bf16[8,8192]{1,0:T(8,128)(2,1)S(1)}, u32[]{:S(2)}, u32[]{:S(2)}) collective-permute-start(bf16[8,8192]{1,0:T(8,128)(2,1)S(1)} %slice.68), channel_id=1, source_target_pairs={{0,4},{1,3},{2,6},{3,1},{4,0},{5,7},{6,2},{7,5},{8,12},{9,11},{10,... | collective-permute-start | bytes 393224 | tf_op jit(solution)/shard_map/ppermute | solution.py:175
  39.6 5.5 %collective-permute-done.17.refs_1_ = bf16[8,8192]{1,0:T(8,128)(2,1)S(1)} collective-permute-done((bf16[8,8192]{1,0:T(8,128)(2,1)S(1)}, bf16[8,8192]{1,0:T(8,128)(2,1)S(1)}, u32[]{:S(2)}, u32[]{:S(2)}) %collective-permute-start.17) | collective-permute-done | bytes 131104 | tf_op jit(solution)/shard_map/ppermute | solution.py:175
  45.1 0.6 %collective-permute-done.18.refs_2_ = bf16[8,8192]{1,0:T(8,128)(2,1)S(1)} collective-permute-done((bf16[8,8192]{1,0:T(8,128)(2,1)S(1)}, bf16[8,8192]{1,0:T(8,128)(2,1)S(1)}, u32[]{:S(2)}, u32[]{:S(2)}) %collective-permute-start.18) | collective-permute-done | bytes 131104 | tf_op jit(solution)/shard_map/ppermute | solution.py:175
  45.7 0.0 copy-done
  45.7 0.9 %shard_map.59 = bf16[8,8192]{1,0:T(8,128)(2,1)} custom-call(f32[8,8192]{1,0:T(8,128)S(1)} %slice.52.refs_0_, bf16[8,8192]{1,0:T(8,128)(2,1)S(1)} %collective-permute-done.17.refs_1_, bf16[8,8192]{1,0:T(8,128)(2,1)S(1)} %collective-permute-done.18.refs_2_, s32[1,8192]{1,0:T(1,128)S(1)} %bitcast.3, bf16[256,128]{1,0:T(8,128)(2,1)S(1)} %pad_maximum_fusion.2.refs_4_), custom_call_target="tpu_custom_call" | custom-call | tf_op jit(solution)/shard_map/pallas_call | solution.py:153
  (16 shorter events, 0.3 us)
Async XLA Ops:
  0.0 10.6 %collective-permute-start = (bf16[8,8192]{1,0:T(8,128)(2,1)}, bf16[8,8192]{1,0:T(8,128)(2,1)S(1)}, u32[]{:S(2)}, u32[]{:S(2)}) collective-permute-start(bf16[8,8192]{1,0:T(8,128)(2,1)} %param.5), channel_id=1, source_target_pairs={{0,8},{1,9},{2,10},{3,11},{4,12},{5,13},{6,14},{7,15},{8,0},{9,1},... | collective-permute-start | bytes 393224 | tf_op jit(solution)/shard_map/ppermute | solution.py:175
  4.0 8.9 %collective-permute-start.1 = (bf16[8,8192]{1,0:T(8,128)(2,1)}, bf16[8,8192]{1,0:T(8,128)(2,1)S(1)}, u32[]{:S(2)}, u32[]{:S(2)}) collective-permute-start(bf16[8,8192]{1,0:T(8,128)(2,1)} %param.5), channel_id=1, source_target_pairs={{0,2},{1,5},{2,0},{3,7},{4,6},{5,1},{6,4},{7,3},{8,10},{9,13},{10,... | collective-permute-start | bytes 393224 | tf_op jit(solution)/shard_map/ppermute | solution.py:175
  5.6 13.1 %collective-permute-start.3 = (bf16[8,8192]{1,0:T(8,128)(2,1)}, bf16[8,8192]{1,0:T(8,128)(2,1)S(1)}, u32[]{:S(2)}, u32[]{:S(2)}) collective-permute-start(bf16[8,8192]{1,0:T(8,128)(2,1)} %param.5), channel_id=1, source_target_pairs={{0,4},{1,3},{2,6},{3,1},{4,0},{5,7},{6,2},{7,5},{8,12},{9,11},{10,... | collective-permute-start | bytes 393224 | tf_op jit(solution)/shard_map/ppermute | solution.py:175
  7.1 11.5 %collective-permute-start.4 = (bf16[8,8192]{1,0:T(8,128)(2,1)}, bf16[8,8192]{1,0:T(8,128)(2,1)S(1)}, u32[]{:S(2)}, u32[]{:S(2)}) collective-permute-start(bf16[8,8192]{1,0:T(8,128)(2,1)} %param.5), channel_id=1, source_target_pairs={{0,6},{1,7},{2,4},{3,5},{4,2},{5,3},{6,0},{7,1},{8,14},{9,15},{10,... | collective-permute-start | bytes 393224 | tf_op jit(solution)/shard_map/ppermute | solution.py:175
  10.6 8.8 %collective-permute-start.2 = (bf16[8,8192]{1,0:T(8,128)(2,1)S(1)}, bf16[8,8192]{1,0:T(8,128)(2,1)S(1)}, u32[]{:S(2)}, u32[]{:S(2)}) collective-permute-start(bf16[8,8192]{1,0:T(8,128)(2,1)S(1)} %collective-permute-done._), channel_id=1, source_target_pairs={{0,2},{1,5},{2,0},{3,7},{4,6},{5,1},{6,4},{7,3},{8,10},{9,13},{10,... | collective-permute-start | bytes 393224 | tf_op jit(solution)/shard_map/ppermute | solution.py:175
  12.2 8.3 %collective-permute-start.5 = (bf16[8,8192]{1,0:T(8,128)(2,1)S(1)}, bf16[8,8192]{1,0:T(8,128)(2,1)S(1)}, u32[]{:S(2)}, u32[]{:S(2)}) collective-permute-start(bf16[8,8192]{1,0:T(8,128)(2,1)S(1)} %collective-permute-done._), channel_id=1, source_target_pairs={{0,4},{1,3},{2,6},{3,1},{4,0},{5,7},{6,2},{7,5},{8,12},{9,11},{10,... | collective-permute-start | bytes 393224 | tf_op jit(solution)/shard_map/ppermute | solution.py:175
  12.9 7.6 %collective-permute-start.6 = (bf16[8,8192]{1,0:T(8,128)(2,1)S(1)}, bf16[8,8192]{1,0:T(8,128)(2,1)S(1)}, u32[]{:S(2)}, u32[]{:S(2)}) collective-permute-start(bf16[8,8192]{1,0:T(8,128)(2,1)S(1)} %collective-permute-done._), channel_id=1, source_target_pairs={{0,6},{1,7},{2,4},{3,5},{4,2},{5,3},{6,0},{7,1},{8,14},{9,15},{10,... | collective-permute-start | bytes 393224 | tf_op jit(solution)/shard_map/ppermute | solution.py:175
  14.1 5.4 %copy-start.1 = (bf16[8,8192]{1,0:T(8,128)(2,1)S(1)}, bf16[8,8192]{1,0:T(8,128)(2,1)}, u32[]{:S(2)}) copy-start(bf16[8,8192]{1,0:T(8,128)(2,1)} %param.5) | copy-start | bytes 393220
  19.6 2.5 %collective-permute-start.7 = (bf16[48,8192]{1,0:T(8,128)(2,1)S(1)}, bf16[48,8192]{1,0:T(8,128)(2,1)S(1)}, u32[]{:S(2)}, u32[]{:S(2)}) collective-permute-start(bf16[48,8192]{1,0:T(8,128)(2,1)S(1)} %constant_dynamic-update-slice_fusion.refs_2_), channel_id=1, source_target_pairs={{0,1},{1,0},{2,3},{3,2},{4,5},{5,4},{6,7},{7,6},{8,9},{9,8},{10,11... | collective-permute-start | bytes 2359304 | tf_op jit(solution)/shard_map/ppermute | solution.py:175
  20.6 1.5 %collective-permute-start.9 = (bf16[16,4096]{1,0:T(8,128)(2,1)S(1)}, bf16[16,4096]{1,0:T(8,128)(2,1)S(1)}, u32[]{:S(2)}, u32[]{:S(2)}) collective-permute-start(bf16[16,4096]{1,0:T(8,128)(2,1)S(1)} %pad_maximum_fusion.1.refs_4_), channel_id=1, source_target_pairs={{0,1},{1,0},{2,3},{3,2},{4,5},{5,4},{6,7},{7,6},{8,9},{9,8},{10,11... | collective-permute-start | bytes 393224 | tf_op jit(solution)/shard_map/ppermute | solution.py:175
  20.7 2.1 %collective-permute-start.8 = (bf16[16,4096]{1,0:T(8,128)(2,1)S(1)}, bf16[16,4096]{1,0:T(8,128)(2,1)S(1)}, u32[]{:S(2)}, u32[]{:S(2)}) collective-permute-start(bf16[16,4096]{1,0:T(8,128)(2,1)S(1)} %pad_maximum_fusion.refs_4_), channel_id=1, source_target_pairs={{0,1},{1,0},{2,3},{3,2},{4,5},{5,4},{6,7},{7,6},{8,9},{9,8},{10,11... | collective-permute-start | bytes 393224 | tf_op jit(solution)/shard_map/ppermute | solution.py:175
  24.3 1.4 %collective-permute-start.13 = (bf16[8,8192]{1,0:T(8,128)(2,1)S(1)}, bf16[8,8192]{1,0:T(8,128)(2,1)S(1)}, u32[]{:S(2)}, u32[]{:S(2)}) collective-permute-start(bf16[8,8192]{1,0:T(8,128)(2,1)S(1)} %get-tuple-element.55), channel_id=1, source_target_pairs={{0,1},{1,0},{2,3},{3,2},{4,5},{5,4},{6,7},{7,6},{8,9},{9,8},{10,11... | collective-permute-start | bytes 393224 | tf_op jit(solution)/shard_map/ppermute | solution.py:175
  24.5 2.3 %collective-permute-start.10 = (bf16[24,8192]{1,0:T(8,128)(2,1)S(1)}, bf16[24,8192]{1,0:T(8,128)(2,1)S(1)}, u32[]{:S(2)}, u32[]{:S(2)}) collective-permute-start(bf16[24,8192]{1,0:T(8,128)(2,1)S(1)} %get-tuple-element.49), channel_id=1, source_target_pairs={{0,1},{1,0},{2,3},{3,2},{4,5},{5,4},{6,7},{7,6},{8,9},{9,8},{10,11... | collective-permute-start | bytes 1179656 | tf_op jit(solution)/shard_map/ppermute | solution.py:175
  25.8 7.3 %collective-permute-start.14 = (bf16[8,8192]{1,0:T(8,128)(2,1)S(1)}, bf16[8,8192]{1,0:T(8,128)(2,1)S(1)}, u32[]{:S(2)}, u32[]{:S(2)}) collective-permute-start(bf16[8,8192]{1,0:T(8,128)(2,1)S(1)} %add_convert_fusion), channel_id=1, source_target_pairs={{0,6},{1,7},{2,4},{3,5},{4,2},{5,3},{6,0},{7,1},{8,14},{9,15},{10,... | collective-permute-start | bytes 393224 | tf_op jit(solution)/shard_map/ppermute | solution.py:175
  26.8 3.2 %collective-permute-start.11 = (bf16[32,8192]{1,0:T(8,128)(2,1)S(1)}, bf16[32,8192]{1,0:T(8,128)(2,1)S(1)}, u32[]{:S(2)}, u32[]{:S(2)}) collective-permute-start(bf16[32,8192]{1,0:T(8,128)(2,1)S(1)} %get-tuple-element.51), channel_id=1, source_target_pairs={{0,1},{1,0},{2,3},{3,2},{4,5},{5,4},{6,7},{7,6},{8,9},{9,8},{10,11... | collective-permute-start | bytes 1572872 | tf_op jit(solution)/shard_map/ppermute | solution.py:175
  26.9 18.8 %copy-start = (s32[8192]{0:T(1024)S(1)}, s32[8192]{0:T(1024)}, u32[]{:S(2)}) copy-start(s32[8192]{0:T(1024)} %param.9) | copy-start | bytes 98308
  26.9 8.1 %collective-permute-start.15 = (bf16[8,8192]{1,0:T(8,128)(2,1)S(1)}, bf16[8,8192]{1,0:T(8,128)(2,1)S(1)}, u32[]{:S(2)}, u32[]{:S(2)}) collective-permute-start(bf16[8,8192]{1,0:T(8,128)(2,1)S(1)} %get-tuple-element.59), channel_id=1, source_target_pairs={{0,2},{1,5},{2,0},{3,7},{4,6},{5,1},{6,4},{7,3},{8,10},{9,13},{10,... | collective-permute-start | bytes 393224 | tf_op jit(solution)/shard_map/ppermute | solution.py:175
  29.3 7.6 %collective-permute-start.16 = (bf16[8,8192]{1,0:T(8,128)(2,1)S(1)}, bf16[8,8192]{1,0:T(8,128)(2,1)S(1)}, u32[]{:S(2)}, u32[]{:S(2)}) collective-permute-start(bf16[8,8192]{1,0:T(8,128)(2,1)S(1)} %get-tuple-element.60), channel_id=1, source_target_pairs={{0,4},{1,3},{2,6},{3,1},{4,0},{5,7},{6,2},{7,5},{8,12},{9,11},{10,... | collective-permute-start | bytes 393224 | tf_op jit(solution)/shard_map/ppermute | solution.py:175
  30.2 7.7 %collective-permute-start.12 = (bf16[16,8192]{1,0:T(8,128)(2,1)S(1)}, bf16[16,8192]{1,0:T(8,128)(2,1)S(1)}, u32[]{:S(2)}, u32[]{:S(2)}) collective-permute-start(bf16[16,8192]{1,0:T(8,128)(2,1)S(1)} %slice.67), channel_id=1, source_target_pairs={{0,2},{1,5},{2,0},{3,7},{4,6},{5,1},{6,4},{7,3},{8,10},{9,13},{10,... | collective-permute-start | bytes 786440 | tf_op jit(solution)/shard_map/ppermute | solution.py:175
  36.9 8.2 %collective-permute-start.17 = (bf16[8,8192]{1,0:T(8,128)(2,1)S(1)}, bf16[8,8192]{1,0:T(8,128)(2,1)S(1)}, u32[]{:S(2)}, u32[]{:S(2)}) collective-permute-start(bf16[8,8192]{1,0:T(8,128)(2,1)S(1)} %fusion.2), channel_id=1, source_target_pairs={{0,8},{1,9},{2,10},{3,11},{4,12},{5,13},{6,14},{7,15},{8,0},{9,1},... | collective-permute-start | bytes 393224 | tf_op jit(solution)/shard_map/ppermute | solution.py:175
  38.0 7.7 %collective-permute-start.18 = (bf16[8,8192]{1,0:T(8,128)(2,1)S(1)}, bf16[8,8192]{1,0:T(8,128)(2,1)S(1)}, u32[]{:S(2)}, u32[]{:S(2)}) collective-permute-start(bf16[8,8192]{1,0:T(8,128)(2,1)S(1)} %slice.68), channel_id=1, source_target_pairs={{0,4},{1,3},{2,6},{3,1},{4,0},{5,7},{6,2},{7,5},{8,12},{9,11},{10,... | collective-permute-start | bytes 393224 | tf_op jit(solution)/shard_map/ppermute | solution.py:175

commit v24 on v20

--- a/solution.py
+++ b/solution.py
@@ -209,6 +209,7 @@
         rest_there, sends[0] = lax.optimization_barrier((swap(sends[2], (1, 1)), sends[0]))
         rest = rest + rest_there.astype(jnp.float32)
         leave = rest[count:].astype(jnp.bfloat16)
+        diagonal, own = lax.optimization_barrier((diagonal, own))
         total = rest[:count]
         for piece in (diagonal, swap(leave[:count], square[0]), swap(leave[count:], square[1])):
             total = total + piece.astype(jnp.float32)

time: 44.8 us -> 49.8 us (1.11)
  waiting for transfers between devices: 16.1 us -> 20 us
  starting transfers between devices: 20.2 us -> 21.3 us
    ppermute x19, waiting for transfers between devices: 16.1 us -> 20 us  [swap(): lax.ppermute(value, 'gx', [(i, i ^ masks[i % 2]) for i in range(members)])]
    ppermute x19, starting transfers between devices: 20.2 us -> 21.3 us  [swap(): lax.ppermute(value, 'gx', [(i, i ^ masks[i % 2]) for i in range(members)])]
  transfers between devices with their start and end apart: 19 -> 19, of which waited for: 9 -> 8; matrix products, arithmetic and copies ran while one was open for 1% -> 1% of each run, Pallas kernels for 12% -> 10%
where the time goes in v24:
time: 49.8 us; the launch traced here: 49.7 us
  starting transfers between devices  21.3 us (43%)
  waiting for transfers between devices  20 us (40%)
  Pallas kernels  7.51 us (15%)
    ppermute x19, starting transfers between devices, swap(): lax.ppermute(value, 'gx', [(i, i ^ masks[i % 2]) for i in range(members)])  21.3 us
    ppermute x19, waiting for transfers between devices, swap(): lax.ppermute(value, 'gx', [(i, i ^ masks[i % 2]) for i in range(members)])  20 us
    pallas_call x1, Pallas kernels, load(): pl.pallas_call(load_kernel, out_shape=(shape, shape, jax.ShapeDtypeStruct...  4.46 us
    pallas_call x2, Pallas kernels, hidden_units(): pl.pallas_call(functools.partial(hidden_kernel, start, last), out_shape=(...  1.45 us
  transfers between devices with their start and end apart: 19, of which 8 were waited for; matrix products, arithmetic and copies ran while one was open for 1% of the time, Pallas kernels for 10%

profile of v24, /device:TPU:0, one launch (start us, length us, event | category | flops | bytes accessed | tf_op | source)
XLA Modules:
  0.0 49.7 jit_solution(14490878713827398785)
XLA Ops:
  0.0 4.0 %collective-permute-start = (bf16[8,8192]{1,0:T(8,128)(2,1)}, bf16[8,8192]{1,0:T(8,128)(2,1)S(1)}, u32[]{:S(2)}, u32[]{:S(2)}) collective-permute-start(bf16[8,8192]{1,0:T(8,128)(2,1)} %param.5), channel_id=1, source_target_pairs={{0,8},{1,9},{2,10},{3,11},{4,12},{5,13},{6,14},{7,15},{8,0},{9,1},... | collective-permute-start | bytes 393224 | tf_op jit(solution)/shard_map/ppermute | solution.py:175
  4.0 1.6 %collective-permute-start.1 = (bf16[8,8192]{1,0:T(8,128)(2,1)}, bf16[8,8192]{1,0:T(8,128)(2,1)S(1)}, u32[]{:S(2)}, u32[]{:S(2)}) collective-permute-start(bf16[8,8192]{1,0:T(8,128)(2,1)} %param.5), channel_id=1, source_target_pairs={{0,4},{1,3},{2,6},{3,1},{4,0},{5,7},{6,2},{7,5},{8,12},{9,11},{10,... | collective-permute-start | bytes 393224 | tf_op jit(solution)/shard_map/ppermute | solution.py:175
  5.6 1.5 %collective-permute-start.3 = (bf16[8,8192]{1,0:T(8,128)(2,1)}, bf16[8,8192]{1,0:T(8,128)(2,1)S(1)}, u32[]{:S(2)}, u32[]{:S(2)}) collective-permute-start(bf16[8,8192]{1,0:T(8,128)(2,1)} %param.5), channel_id=1, source_target_pairs={{0,2},{1,5},{2,0},{3,7},{4,6},{5,1},{6,4},{7,3},{8,10},{9,13},{10,... | collective-permute-start | bytes 393224 | tf_op jit(solution)/shard_map/ppermute | solution.py:175
  7.1 0.4 collective-permute-start.4
  7.5 3.1 %collective-permute-done._ = bf16[8,8192]{1,0:T(8,128)(2,1)S(1)} collective-permute-done((bf16[8,8192]{1,0:T(8,128)(2,1)}, bf16[8,8192]{1,0:T(8,128)(2,1)S(1)}, u32[]{:S(2)}, u32[]{:S(2)}) %collective-permute-start) | collective-permute-done | bytes 131104 | tf_op jit(solution)/shard_map/ppermute | solution.py:175
  10.7 0.8 %collective-permute-start.2 = (bf16[8,8192]{1,0:T(8,128)(2,1)S(1)}, bf16[8,8192]{1,0:T(8,128)(2,1)S(1)}, u32[]{:S(2)}, u32[]{:S(2)}) collective-permute-start(bf16[8,8192]{1,0:T(8,128)(2,1)S(1)} %collective-permute-done._), channel_id=1, source_target_pairs={{0,4},{1,3},{2,6},{3,1},{4,0},{5,7},{6,2},{7,5},{8,12},{9,11},{10,... | collective-permute-start | bytes 393224 | tf_op jit(solution)/shard_map/ppermute | solution.py:175
  11.4 1.5 %collective-permute-start.5 = (bf16[8,8192]{1,0:T(8,128)(2,1)S(1)}, bf16[8,8192]{1,0:T(8,128)(2,1)S(1)}, u32[]{:S(2)}, u32[]{:S(2)}) collective-permute-start(bf16[8,8192]{1,0:T(8,128)(2,1)S(1)} %collective-permute-done._), channel_id=1, source_target_pairs={{0,2},{1,5},{2,0},{3,7},{4,6},{5,1},{6,4},{7,3},{8,10},{9,13},{10,... | collective-permute-start | bytes 393224 | tf_op jit(solution)/shard_map/ppermute | solution.py:175
  12.9 0.0 collective-permute-done.1
  12.9 1.5 %collective-permute-start.6 = (bf16[8,8192]{1,0:T(8,128)(2,1)S(1)}, bf16[8,8192]{1,0:T(8,128)(2,1)S(1)}, u32[]{:S(2)}, u32[]{:S(2)}) collective-permute-start(bf16[8,8192]{1,0:T(8,128)(2,1)S(1)} %collective-permute-done._), channel_id=1, source_target_pairs={{0,6},{1,7},{2,4},{3,5},{4,2},{5,3},{6,0},{7,1},{8,14},{9,15},{10,... | collective-permute-start | bytes 393224 | tf_op jit(solution)/shard_map/ppermute | solution.py:175
  14.4 0.0 copy-start.1
  14.4 4.5 %shard_map.55 = (bf16[8192,224]{1,0:T(8,128)(2,1)S(1)}, bf16[8192,224]{1,0:T(8,128)(2,1)S(1)}, bf16[224,8192]{1,0:T(8,128)(2,1)S(1)}) custom-call(bf16[224,8192]{1,0:T(8,128)(2,1)} %bitcast.4, bf16[224,8192]{1,0:T(8,128)(2,1)} %bitcast.5, bf16[224,8192]{1,0:T(8,128)(2,1)} %down_hbm.1, bf16[8,8192]{1,0:T(8,128)(2,1)S(1)} %collective-permute-done._), custom_call_target="tpu_custom_call" | custom-call | bytes 11010048 | tf_op jit(solution)/shard_map/pallas_call | solution.py:44
  18.9 0.0 collective-permute-done.3
  18.9 0.0 collective-permute-done.4
  18.9 0.0 collective-permute-done.2
  19.0 0.0 copy-done.1
  19.0 0.1 collective-permute-start.7
  19.1 1.4 %collective-permute-done.6 = bf16[8,8192]{1,0:T(8,128)(2,1)S(1)} collective-permute-done((bf16[8,8192]{1,0:T(8,128)(2,1)S(1)}, bf16[8,8192]{1,0:T(8,128)(2,1)S(1)}, u32[]{:S(2)}, u32[]{:S(2)}) %collective-permute-start.6) | collective-permute-done | bytes 131104 | tf_op jit(solution)/shard_map/ppermute | solution.py:175
  20.5 0.0 collective-permute-done.5
  20.6 0.1 collective-permute-start.9
  20.7 0.6 %collective-permute-start.8 = (bf16[16,4096]{1,0:T(8,128)(2,1)S(1)}, bf16[16,4096]{1,0:T(8,128)(2,1)S(1)}, u32[]{:S(2)}, u32[]{:S(2)}) collective-permute-start(bf16[16,4096]{1,0:T(8,128)(2,1)S(1)} %pad_maximum_fusion.refs_4_), channel_id=1, source_target_pairs={{0,1},{1,0},{2,3},{3,2},{4,5},{5,4},{6,7},{7,6},{8,9},{9,8},{10,11... | collective-permute-start | bytes 393224 | tf_op jit(solution)/shard_map/ppermute | solution.py:175
  21.2 0.8 %collective-permute-done.9.refs_5_ = bf16[16,4096]{1,0:T(8,128)(2,1)S(1)} collective-permute-done((bf16[16,4096]{1,0:T(8,128)(2,1)S(1)}, bf16[16,4096]{1,0:T(8,128)(2,1)S(1)}, u32[]{:S(2)}, u32[]{:S(2)}) %collective-permute-start.9) | collective-permute-done | bytes 131104 | tf_op jit(solution)/shard_map/ppermute | solution.py:175
  22.0 0.0 collective-permute-done.7.refs_3_
  22.0 0.7 %shard_map.56 = (f32[128,224]{1,0:T(8,128)S(1)}, f32[128,224]{1,0:T(8,128)S(1)}) custom-call(bf16[8192,224]{1,0:T(8,128)(2,1)S(1)} %get-tuple-element.42.refs_0_, bf16[8192,224]{1,0:T(8,128)(2,1)S(1)} %get-tuple-element.43.refs_1_, bf16[48,8192]{1,0:T(8,128)(2,1)S(1)} %constant_dynamic-update-slice_fusion.refs_2_, ...), custom_call_target="tpu_custom_call" | custom-call | flops 469762048 | bytes 3670016 | tf_op jit(solution)/shard_map/pallas_call | solution.py:84
  22.7 0.0 collective-permute-done.8.refs_5_
  22.7 0.7 %shard_map.57.hidden_ref = bf16[128,224]{1,0:T(8,128)(2,1)S(1)} custom-call(bf16[8192,224]{1,0:T(8,128)(2,1)S(1)} %get-tuple-element.42.refs_0_, bf16[8192,224]{1,0:T(8,128)(2,1)S(1)} %get-tuple-element.43.refs_1_, bf16[48,8192]{1,0:T(8,128)(2,1)S(1)} %constant_dynamic-update-slice_fusion.refs_2_, bf16[48,8192]{1,0:T(8,128)(2,1)S(1)} %collective-permute-done.7.refs_3_, ...), custom_call_target="tpu_custom_call" | custom-call | flops 469762048 | bytes 3670016 | tf_op jit(solution)/shard_map/pallas_call | solution.py:84
  23.4 0.7 %shard_map.58 = (f32[32,8192]{1,0:T(8,128)S(1)}, f32[8,8192]{1,0:T(8,128)S(1)}, f32[24,8192]{1,0:T(8,128)S(1)}, bf16[32,8192]{1,0:T(8,128)(2,1)S(1)}, bf16[8,819...) custom-call(bf16[128,224]{1,0:T(8,128)(2,1)S(1)} %shard_map.57.hidden_ref, bf16[224,8192]{1,0:T(8,128)(2,1)S(1)} %get-tuple-element.49.down_ref), custom_call_target="tpu_custom_call" | custom-call | flops 469762048 | bytes 3670016 | tf_op jit(solution)/shard_map/pallas_call | solution.py:113
  24.2 0.2 collective-permute-start.10
  24.4 0.4 collective-permute-start.12
  24.7 0.8 %collective-permute-done.10 = bf16[8,8192]{1,0:T(8,128)(2,1)S(1)} collective-permute-done((bf16[8,8192]{1,0:T(8,128)(2,1)S(1)}, bf16[8,8192]{1,0:T(8,128)(2,1)S(1)}, u32[]{:S(2)}, u32[]{:S(2)}) %collective-permute-start.10) | collective-permute-done | bytes 131104 | tf_op jit(solution)/shard_map/ppermute | solution.py:175
  25.6 1.2 %collective-permute-start.11 = (bf16[8,8192]{1,0:T(8,128)(2,1)S(1)}, bf16[8,8192]{1,0:T(8,128)(2,1)S(1)}, u32[]{:S(2)}, u32[]{:S(2)}) collective-permute-start(bf16[8,8192]{1,0:T(8,128)(2,1)S(1)} %add_convert_fusion), channel_id=1, source_target_pairs={{0,6},{1,7},{2,4},{3,5},{4,2},{5,3},{6,0},{7,1},{8,14},{9,15},{10,... | collective-permute-start | bytes 393224 | tf_op jit(solution)/shard_map/ppermute | solution.py:175
  26.8 5.3 %collective-permute-done.11 = bf16[8,8192]{1,0:T(8,128)(2,1)S(1)} collective-permute-done((bf16[8,8192]{1,0:T(8,128)(2,1)S(1)}, bf16[8,8192]{1,0:T(8,128)(2,1)S(1)}, u32[]{:S(2)}, u32[]{:S(2)}) %collective-permute-start.11) | collective-permute-done | bytes 131104 | tf_op jit(solution)/shard_map/ppermute | solution.py:175
  32.1 0.0 collective-permute-done.12
  32.1 0.0 collective-permute-start.13
  32.1 0.1 fusion.7
  32.2 0.0 copy-start
  32.2 1.2 %collective-permute-start.15 = (bf16[8,8192]{1,0:T(8,128)(2,1)S(1)}, bf16[8,8192]{1,0:T(8,128)(2,1)S(1)}, u32[]{:S(2)}, u32[]{:S(2)}) collective-permute-start(bf16[8,8192]{1,0:T(8,128)(2,1)S(1)} %get-tuple-element.63), channel_id=1, source_target_pairs={{0,4},{1,3},{2,6},{3,1},{4,0},{5,7},{6,2},{7,5},{8,12},{9,11},{10,... | collective-permute-start | bytes 393224 | tf_op jit(solution)/shard_map/ppermute | solution.py:175
  33.5 0.5 %collective-permute-start.16 = (bf16[8,8192]{1,0:T(8,128)(2,1)S(1)}, bf16[8,8192]{1,0:T(8,128)(2,1)S(1)}, u32[]{:S(2)}, u32[]{:S(2)}) collective-permute-start(bf16[8,8192]{1,0:T(8,128)(2,1)S(1)} %get-tuple-element.64), channel_id=1, source_target_pairs={{0,2},{1,5},{2,0},{3,7},{4,6},{5,1},{6,4},{7,3},{8,10},{9,13},{10,... | collective-permute-start | bytes 393224 | tf_op jit(solution)/shard_map/ppermute | solution.py:175
  34.0 0.0 collective-permute-done.13
  34.0 0.1 convert_add_fusion
  34.2 1.9 %collective-permute-start.14 = (bf16[16,8192]{1,0:T(8,128)(2,1)S(1)}, bf16[16,8192]{1,0:T(8,128)(2,1)S(1)}, u32[]{:S(2)}, u32[]{:S(2)}) collective-permute-start(bf16[16,8192]{1,0:T(8,128)(2,1)S(1)} %slice.67), channel_id=1, source_target_pairs={{0,4},{1,3},{2,6},{3,1},{4,0},{5,7},{6,2},{7,5},{8,12},{9,11},{10,... | collective-permute-start | bytes 786440 | tf_op jit(solution)/shard_map/ppermute | solution.py:175
  36.0 1.9 %collective-permute-done.15 = bf16[8,8192]{1,0:T(8,128)(2,1)S(1)} collective-permute-done((bf16[8,8192]{1,0:T(8,128)(2,1)S(1)}, bf16[8,8192]{1,0:T(8,128)(2,1)S(1)}, u32[]{:S(2)}, u32[]{:S(2)}) %collective-permute-start.15) | collective-permute-done | bytes 131104 | tf_op jit(solution)/shard_map/ppermute | solution.py:175
  38.0 1.9 %collective-permute-done.16 = bf16[8,8192]{1,0:T(8,128)(2,1)S(1)} collective-permute-done((bf16[8,8192]{1,0:T(8,128)(2,1)S(1)}, bf16[8,8192]{1,0:T(8,128)(2,1)S(1)}, u32[]{:S(2)}, u32[]{:S(2)}) %collective-permute-start.16) | collective-permute-done | bytes 131104 | tf_op jit(solution)/shard_map/ppermute | solution.py:175
  39.9 0.1 fusion.2
  39.9 2.1 %collective-permute-start.17 = (bf16[8,8192]{1,0:T(8,128)(2,1)S(1)}, bf16[8,8192]{1,0:T(8,128)(2,1)S(1)}, u32[]{:S(2)}, u32[]{:S(2)}) collective-permute-start(bf16[8,8192]{1,0:T(8,128)(2,1)S(1)} %fusion.2), channel_id=1, source_target_pairs={{0,8},{1,9},{2,10},{3,11},{4,12},{5,13},{6,14},{7,15},{8,0},{9,1},... | collective-permute-start | bytes 393224 | tf_op jit(solution)/shard_map/ppermute | solution.py:175
  42.0 0.0 collective-permute-done.14
  42.0 0.1 slice_add_fusion
  42.1 1.9 %collective-permute-start.18 = (bf16[8,8192]{1,0:T(8,128)(2,1)S(1)}, bf16[8,8192]{1,0:T(8,128)(2,1)S(1)}, u32[]{:S(2)}, u32[]{:S(2)}) collective-permute-start(bf16[8,8192]{1,0:T(8,128)(2,1)S(1)} %slice.68), channel_id=1, source_target_pairs={{0,2},{1,5},{2,0},{3,7},{4,6},{5,1},{6,4},{7,3},{8,10},{9,13},{10,... | collective-permute-start | bytes 393224 | tf_op jit(solution)/shard_map/ppermute | solution.py:175
  44.0 4.8 %collective-permute-done.17.refs_1_ = bf16[8,8192]{1,0:T(8,128)(2,1)S(1)} collective-permute-done((bf16[8,8192]{1,0:T(8,128)(2,1)S(1)}, bf16[8,8192]{1,0:T(8,128)(2,1)S(1)}, u32[]{:S(2)}, u32[]{:S(2)}) %collective-permute-start.17) | collective-permute-done | bytes 131104 | tf_op jit(solution)/shard_map/ppermute | solution.py:175
  48.8 0.0 collective-permute-done.18.refs_2_
  48.8 0.0 copy-done
  48.8 0.9 %shard_map.59 = bf16[8,8192]{1,0:T(8,128)(2,1)} custom-call(f32[8,8192]{1,0:T(8,128)S(1)} %slice.52.refs_0_, bf16[8,8192]{1,0:T(8,128)(2,1)S(1)} %collective-permute-done.17.refs_1_, bf16[8,8192]{1,0:T(8,128)(2,1)S(1)} %collective-permute-done.18.refs_2_, s32[1,8192]{1,0:T(1,128)S(1)} %bitcast.3, bf16[256,128]{1,0:T(8,128)(2,1)S(1)} %pad_maximum_fusion.2.refs_4_), custom_call_target="tpu_custom_call" | custom-call | tf_op jit(solution)/shard_map/pallas_call | solution.py:153
  (16 shorter events, 0.3 us)
Async XLA Ops:
  0.0 10.7 %collective-permute-start = (bf16[8,8192]{1,0:T(8,128)(2,1)}, bf16[8,8192]{1,0:T(8,128)(2,1)S(1)}, u32[]{:S(2)}, u32[]{:S(2)}) collective-permute-start(bf16[8,8192]{1,0:T(8,128)(2,1)} %param.5), channel_id=1, source_target_pairs={{0,8},{1,9},{2,10},{3,11},{4,12},{5,13},{6,14},{7,15},{8,0},{9,1},... | collective-permute-start | bytes 393224 | tf_op jit(solution)/shard_map/ppermute | solution.py:175
  4.0 8.9 %collective-permute-start.1 = (bf16[8,8192]{1,0:T(8,128)(2,1)}, bf16[8,8192]{1,0:T(8,128)(2,1)S(1)}, u32[]{:S(2)}, u32[]{:S(2)}) collective-permute-start(bf16[8,8192]{1,0:T(8,128)(2,1)} %param.5), channel_id=1, source_target_pairs={{0,4},{1,3},{2,6},{3,1},{4,0},{5,7},{6,2},{7,5},{8,12},{9,11},{10,... | collective-permute-start | bytes 393224 | tf_op jit(solution)/shard_map/ppermute | solution.py:175
  5.6 13.3 %collective-permute-start.3 = (bf16[8,8192]{1,0:T(8,128)(2,1)}, bf16[8,8192]{1,0:T(8,128)(2,1)S(1)}, u32[]{:S(2)}, u32[]{:S(2)}) collective-permute-start(bf16[8,8192]{1,0:T(8,128)(2,1)} %param.5), channel_id=1, source_target_pairs={{0,2},{1,5},{2,0},{3,7},{4,6},{5,1},{6,4},{7,3},{8,10},{9,13},{10,... | collective-permute-start | bytes 393224 | tf_op jit(solution)/shard_map/ppermute | solution.py:175
  7.1 11.7 %collective-permute-start.4 = (bf16[8,8192]{1,0:T(8,128)(2,1)}, bf16[8,8192]{1,0:T(8,128)(2,1)S(1)}, u32[]{:S(2)}, u32[]{:S(2)}) collective-permute-start(bf16[8,8192]{1,0:T(8,128)(2,1)} %param.5), channel_id=1, source_target_pairs={{0,6},{1,7},{2,4},{3,5},{4,2},{5,3},{6,0},{7,1},{8,14},{9,15},{10,... | collective-permute-start | bytes 393224 | tf_op jit(solution)/shard_map/ppermute | solution.py:175
  10.7 8.2 %collective-permute-start.2 = (bf16[8,8192]{1,0:T(8,128)(2,1)S(1)}, bf16[8,8192]{1,0:T(8,128)(2,1)S(1)}, u32[]{:S(2)}, u32[]{:S(2)}) collective-permute-start(bf16[8,8192]{1,0:T(8,128)(2,1)S(1)} %collective-permute-done._), channel_id=1, source_target_pairs={{0,4},{1,3},{2,6},{3,1},{4,0},{5,7},{6,2},{7,5},{8,12},{9,11},{10,... | collective-permute-start | bytes 393224 | tf_op jit(solution)/shard_map/ppermute | solution.py:175
  11.4 9.1 %collective-permute-start.5 = (bf16[8,8192]{1,0:T(8,128)(2,1)S(1)}, bf16[8,8192]{1,0:T(8,128)(2,1)S(1)}, u32[]{:S(2)}, u32[]{:S(2)}) collective-permute-start(bf16[8,8192]{1,0:T(8,128)(2,1)S(1)} %collective-permute-done._), channel_id=1, source_target_pairs={{0,2},{1,5},{2,0},{3,7},{4,6},{5,1},{6,4},{7,3},{8,10},{9,13},{10,... | collective-permute-start | bytes 393224 | tf_op jit(solution)/shard_map/ppermute | solution.py:175
  12.9 7.6 %collective-permute-start.6 = (bf16[8,8192]{1,0:T(8,128)(2,1)S(1)}, bf16[8,8192]{1,0:T(8,128)(2,1)S(1)}, u32[]{:S(2)}, u32[]{:S(2)}) collective-permute-start(bf16[8,8192]{1,0:T(8,128)(2,1)S(1)} %collective-permute-done._), channel_id=1, source_target_pairs={{0,6},{1,7},{2,4},{3,5},{4,2},{5,3},{6,0},{7,1},{8,14},{9,15},{10,... | collective-permute-start | bytes 393224 | tf_op jit(solution)/shard_map/ppermute | solution.py:175
  14.4 4.6 %copy-start.1 = (bf16[8,8192]{1,0:T(8,128)(2,1)S(1)}, bf16[8,8192]{1,0:T(8,128)(2,1)}, u32[]{:S(2)}) copy-start(bf16[8,8192]{1,0:T(8,128)(2,1)} %param.5) | copy-start | bytes 393220
  19.0 3.0 %collective-permute-start.7 = (bf16[48,8192]{1,0:T(8,128)(2,1)S(1)}, bf16[48,8192]{1,0:T(8,128)(2,1)S(1)}, u32[]{:S(2)}, u32[]{:S(2)}) collective-permute-start(bf16[48,8192]{1,0:T(8,128)(2,1)S(1)} %constant_dynamic-update-slice_fusion.refs_2_), channel_id=1, source_target_pairs={{0,1},{1,0},{2,3},{3,2},{4,5},{5,4},{6,7},{7,6},{8,9},{9,8},{10,11... | collective-permute-start | bytes 2359304 | tf_op jit(solution)/shard_map/ppermute | solution.py:175
  20.6 1.4 %collective-permute-start.9 = (bf16[16,4096]{1,0:T(8,128)(2,1)S(1)}, bf16[16,4096]{1,0:T(8,128)(2,1)S(1)}, u32[]{:S(2)}, u32[]{:S(2)}) collective-permute-start(bf16[16,4096]{1,0:T(8,128)(2,1)S(1)} %pad_maximum_fusion.1.refs_4_), channel_id=1, source_target_pairs={{0,1},{1,0},{2,3},{3,2},{4,5},{5,4},{6,7},{7,6},{8,9},{9,8},{10,11... | collective-permute-start | bytes 393224 | tf_op jit(solution)/shard_map/ppermute | solution.py:175
  20.7 2.0 %collective-permute-start.8 = (bf16[16,4096]{1,0:T(8,128)(2,1)S(1)}, bf16[16,4096]{1,0:T(8,128)(2,1)S(1)}, u32[]{:S(2)}, u32[]{:S(2)}) collective-permute-start(bf16[16,4096]{1,0:T(8,128)(2,1)S(1)} %pad_maximum_fusion.refs_4_), channel_id=1, source_target_pairs={{0,1},{1,0},{2,3},{3,2},{4,5},{5,4},{6,7},{7,6},{8,9},{9,8},{10,11... | collective-permute-start | bytes 393224 | tf_op jit(solution)/shard_map/ppermute | solution.py:175
  24.2 1.4 %collective-permute-start.10 = (bf16[8,8192]{1,0:T(8,128)(2,1)S(1)}, bf16[8,8192]{1,0:T(8,128)(2,1)S(1)}, u32[]{:S(2)}, u32[]{:S(2)}) collective-permute-start(bf16[8,8192]{1,0:T(8,128)(2,1)S(1)} %get-tuple-element.51), channel_id=1, source_target_pairs={{0,1},{1,0},{2,3},{3,2},{4,5},{5,4},{6,7},{7,6},{8,9},{9,8},{10,11... | collective-permute-start | bytes 393224 | tf_op jit(solution)/shard_map/ppermute | solution.py:175
  24.4 7.7 %collective-permute-start.12 = (bf16[24,8192]{1,0:T(8,128)(2,1)S(1)}, bf16[24,8192]{1,0:T(8,128)(2,1)S(1)}, u32[]{:S(2)}, u32[]{:S(2)}) collective-permute-start(bf16[24,8192]{1,0:T(8,128)(2,1)S(1)} %get-tuple-element.54), channel_id=1, source_target_pairs={{0,1},{1,0},{2,3},{3,2},{4,5},{5,4},{6,7},{7,6},{8,9},{9,8},{10,11... | collective-permute-start | bytes 1179656 | tf_op jit(solution)/shard_map/ppermute | solution.py:175
  25.6 6.5 %collective-permute-start.11 = (bf16[8,8192]{1,0:T(8,128)(2,1)S(1)}, bf16[8,8192]{1,0:T(8,128)(2,1)S(1)}, u32[]{:S(2)}, u32[]{:S(2)}) collective-permute-start(bf16[8,8192]{1,0:T(8,128)(2,1)S(1)} %add_convert_fusion), channel_id=1, source_target_pairs={{0,6},{1,7},{2,4},{3,5},{4,2},{5,3},{6,0},{7,1},{8,14},{9,15},{10,... | collective-permute-start | bytes 393224 | tf_op jit(solution)/shard_map/ppermute | solution.py:175
  32.1 1.9 %collective-permute-start.13 = (bf16[32,8192]{1,0:T(8,128)(2,1)S(1)}, bf16[32,8192]{1,0:T(8,128)(2,1)S(1)}, u32[]{:S(2)}, u32[]{:S(2)}) collective-permute-start(bf16[32,8192]{1,0:T(8,128)(2,1)S(1)} %get-tuple-element.56), channel_id=1, source_target_pairs={{0,1},{1,0},{2,3},{3,2},{4,5},{5,4},{6,7},{7,6},{8,9},{9,8},{10,11... | collective-permute-start | bytes 1572872 | tf_op jit(solution)/shard_map/ppermute | solution.py:175
  32.2 16.6 %copy-start = (s32[8192]{0:T(1024)S(1)}, s32[8192]{0:T(1024)}, u32[]{:S(2)}) copy-start(s32[8192]{0:T(1024)} %param.9) | copy-start | bytes 98308
  32.2 5.7 %collective-permute-start.15 = (bf16[8,8192]{1,0:T(8,128)(2,1)S(1)}, bf16[8,8192]{1,0:T(8,128)(2,1)S(1)}, u32[]{:S(2)}, u32[]{:S(2)}) collective-permute-start(bf16[8,8192]{1,0:T(8,128)(2,1)S(1)} %get-tuple-element.63), channel_id=1, source_target_pairs={{0,4},{1,3},{2,6},{3,1},{4,0},{5,7},{6,2},{7,5},{8,12},{9,11},{10,... | collective-permute-start | bytes 393224 | tf_op jit(solution)/shard_map/ppermute | solution.py:175
  33.5 6.4 %collective-permute-start.16 = (bf16[8,8192]{1,0:T(8,128)(2,1)S(1)}, bf16[8,8192]{1,0:T(8,128)(2,1)S(1)}, u32[]{:S(2)}, u32[]{:S(2)}) collective-permute-start(bf16[8,8192]{1,0:T(8,128)(2,1)S(1)} %get-tuple-element.64), channel_id=1, source_target_pairs={{0,2},{1,5},{2,0},{3,7},{4,6},{5,1},{6,4},{7,3},{8,10},{9,13},{10,... | collective-permute-start | bytes 393224 | tf_op jit(solution)/shard_map/ppermute | solution.py:175
  34.2 7.8 %collective-permute-start.14 = (bf16[16,8192]{1,0:T(8,128)(2,1)S(1)}, bf16[16,8192]{1,0:T(8,128)(2,1)S(1)}, u32[]{:S(2)}, u32[]{:S(2)}) collective-permute-start(bf16[16,8192]{1,0:T(8,128)(2,1)S(1)} %slice.67), channel_id=1, source_target_pairs={{0,4},{1,3},{2,6},{3,1},{4,0},{5,7},{6,2},{7,5},{8,12},{9,11},{10,... | collective-permute-start | bytes 786440 | tf_op jit(solution)/shard_map/ppermute | solution.py:175
  39.9 8.8 %collective-permute-start.17 = (bf16[8,8192]{1,0:T(8,128)(2,1)S(1)}, bf16[8,8192]{1,0:T(8,128)(2,1)S(1)}, u32[]{:S(2)}, u32[]{:S(2)}) collective-permute-start(bf16[8,8192]{1,0:T(8,128)(2,1)S(1)} %fusion.2), channel_id=1, source_target_pairs={{0,8},{1,9},{2,10},{3,11},{4,12},{5,13},{6,14},{7,15},{8,0},{9,1},... | collective-permute-start | bytes 393224 | tf_op jit(solution)/shard_map/ppermute | solution.py:175
  42.1 6.7 %collective-permute-start.18 = (bf16[8,8192]{1,0:T(8,128)(2,1)S(1)}, bf16[8,8192]{1,0:T(8,128)(2,1)S(1)}, u32[]{:S(2)}, u32[]{:S(2)}) collective-permute-start(bf16[8,8192]{1,0:T(8,128)(2,1)S(1)} %slice.68), channel_id=1, source_target_pairs={{0,2},{1,5},{2,0},{3,7},{4,6},{5,1},{6,4},{7,3},{8,10},{9,13},{10,... | collective-permute-start | bytes 393224 | tf_op jit(solution)/shard_map/ppermute | solution.py:175

commit v25 on v22

--- a/solution.py
+++ b/solution.py
@@ -211,6 +211,7 @@
         rest_there, sends[0] = lax.optimization_barrier((swap(sends[2], (1, 1)), sends[0]))
         rest = rest + rest_there.astype(jnp.float32)
         leave = rest[count:].astype(jnp.bfloat16)
+        own_there, diagonal = lax.optimization_barrier((swap(sends[0], (1, 1)), diagonal))
         total = rest[:count]
         for piece in (diagonal, swap(leave[:count], square[0]), swap(leave[count:], square[1])):
             total = total + piece.astype(jnp.float32)
@@ -221,7 +222,7 @@
             arrived.append(piece[:rows])
             total = total[:split] + piece[rows:].astype(jnp.float32)
 
-        own = own + swap(sends[0], (1, 1)).astype(jnp.float32)
+        own = own + own_there.astype(jnp.float32)
         own = own[: 2 * rows] + swap(own[2 * rows :].astype(jnp.bfloat16), square[0]).astype(jnp.float32)
         arrived.append(swap(own[rows:].astype(jnp.bfloat16), square[1]))
         return rotate(own[:rows], arrived, sign_pattern)

time: 44.9 us -> 48.9 us (1.089)
  waiting for transfers between devices: 16.9 us -> 22.1 us
  starting transfers between devices: 19.5 us -> 18.3 us
    ppermute x19, waiting for transfers between devices: 16.9 us -> 22.1 us  [swap(): lax.ppermute(value, 'gx', [(i, i ^ masks[i % 2]) for i in range(members)])]
    ppermute x19, starting transfers between devices: 19.5 us -> 18.3 us  [swap(): lax.ppermute(value, 'gx', [(i, i ^ masks[i % 2]) for i in range(members)])]
  transfers between devices with their start and end apart: 19 -> 19, of which waited for: 9 -> 9; matrix products, arithmetic and copies ran while one was open for 1% -> 1% of each run, Pallas kernels for 12% -> 11%
where the time goes in v25:
time: 48.9 us; the launch traced here: 48.8 us
  waiting for transfers between devices  22.1 us (45%)
  starting transfers between devices  18.3 us (37%)
  Pallas kernels  7.5 us (15%)
    ppermute x19, waiting for transfers between devices, swap(): lax.ppermute(value, 'gx', [(i, i ^ masks[i % 2]) for i in range(members)])  22.1 us
    ppermute x19, starting transfers between devices, swap(): lax.ppermute(value, 'gx', [(i, i ^ masks[i % 2]) for i in range(members)])  18.3 us
    pallas_call x1, Pallas kernels, load(): pl.pallas_call(load_kernel, out_shape=(shape, shape, jax.ShapeDtypeStruct...  4.46 us
    pallas_call x2, Pallas kernels, hidden_units(): pl.pallas_call(functools.partial(hidden_kernel, start, last), out_shape=(...  1.45 us
  transfers between devices with their start and end apart: 19, of which 9 were waited for; matrix products, arithmetic and copies ran while one was open for 1% of the time, Pallas kernels for 11%

profile of v25, /device:TPU:0, one launch (start us, length us, event | category | flops | bytes accessed | tf_op | source)
XLA Modules:
  0.0 48.8 jit_solution(5309280035614727719)
XLA Ops:
  0.0 4.0 %collective-permute-start = (bf16[8,8192]{1,0:T(8,128)(2,1)}, bf16[8,8192]{1,0:T(8,128)(2,1)S(1)}, u32[]{:S(2)}, u32[]{:S(2)}) collective-permute-start(bf16[8,8192]{1,0:T(8,128)(2,1)} %param.5), channel_id=1, source_target_pairs={{0,8},{1,9},{2,10},{3,11},{4,12},{5,13},{6,14},{7,15},{8,0},{9,1},... | collective-permute-start | bytes 393224 | tf_op jit(solution)/shard_map/ppermute | solution.py:175
  4.0 1.6 %collective-permute-start.1 = (bf16[8,8192]{1,0:T(8,128)(2,1)}, bf16[8,8192]{1,0:T(8,128)(2,1)S(1)}, u32[]{:S(2)}, u32[]{:S(2)}) collective-permute-start(bf16[8,8192]{1,0:T(8,128)(2,1)} %param.5), channel_id=1, source_target_pairs={{0,4},{1,3},{2,6},{3,1},{4,0},{5,7},{6,2},{7,5},{8,12},{9,11},{10,... | collective-permute-start | bytes 393224 | tf_op jit(solution)/shard_map/ppermute | solution.py:175
  5.6 1.5 %collective-permute-start.3 = (bf16[8,8192]{1,0:T(8,128)(2,1)}, bf16[8,8192]{1,0:T(8,128)(2,1)S(1)}, u32[]{:S(2)}, u32[]{:S(2)}) collective-permute-start(bf16[8,8192]{1,0:T(8,128)(2,1)} %param.5), channel_id=1, source_target_pairs={{0,2},{1,5},{2,0},{3,7},{4,6},{5,1},{6,4},{7,3},{8,10},{9,13},{10,... | collective-permute-start | bytes 393224 | tf_op jit(solution)/shard_map/ppermute | solution.py:175
  7.1 0.4 collective-permute-start.4
  7.5 3.1 %collective-permute-done._ = bf16[8,8192]{1,0:T(8,128)(2,1)S(1)} collective-permute-done((bf16[8,8192]{1,0:T(8,128)(2,1)}, bf16[8,8192]{1,0:T(8,128)(2,1)S(1)}, u32[]{:S(2)}, u32[]{:S(2)}) %collective-permute-start) | collective-permute-done | bytes 131104 | tf_op jit(solution)/shard_map/ppermute | solution.py:175
  10.7 0.8 %collective-permute-start.2 = (bf16[8,8192]{1,0:T(8,128)(2,1)S(1)}, bf16[8,8192]{1,0:T(8,128)(2,1)S(1)}, u32[]{:S(2)}, u32[]{:S(2)}) collective-permute-start(bf16[8,8192]{1,0:T(8,128)(2,1)S(1)} %collective-permute-done._), channel_id=1, source_target_pairs={{0,4},{1,3},{2,6},{3,1},{4,0},{5,7},{6,2},{7,5},{8,12},{9,11},{10,... | collective-permute-start | bytes 393224 | tf_op jit(solution)/shard_map/ppermute | solution.py:175
  11.4 2.3 %collective-permute-start.6 = (bf16[8,8192]{1,0:T(8,128)(2,1)S(1)}, bf16[8,8192]{1,0:T(8,128)(2,1)S(1)}, u32[]{:S(2)}, u32[]{:S(2)}) collective-permute-start(bf16[8,8192]{1,0:T(8,128)(2,1)S(1)} %collective-permute-done._), channel_id=1, source_target_pairs={{0,6},{1,7},{2,4},{3,5},{4,2},{5,3},{6,0},{7,1},{8,14},{9,15},{10,... | collective-permute-start | bytes 393224 | tf_op jit(solution)/shard_map/ppermute | solution.py:175
  13.7 0.0 collective-permute-done.1
  13.7 0.5 collective-permute-start.5
  14.2 0.0 copy-start.1
  14.2 4.5 %shard_map.55 = (bf16[8192,224]{1,0:T(8,128)(2,1)S(1)}, bf16[8192,224]{1,0:T(8,128)(2,1)S(1)}, bf16[224,8192]{1,0:T(8,128)(2,1)S(1)}) custom-call(bf16[224,8192]{1,0:T(8,128)(2,1)} %bitcast.4, bf16[224,8192]{1,0:T(8,128)(2,1)} %bitcast.5, bf16[224,8192]{1,0:T(8,128)(2,1)} %down_hbm.1, bf16[8,8192]{1,0:T(8,128)(2,1)S(1)} %collective-permute-done._), custom_call_target="tpu_custom_call" | custom-call | bytes 11010048 | tf_op jit(solution)/shard_map/pallas_call | solution.py:44
  18.6 0.0 collective-permute-done.3
  18.6 0.0 collective-permute-done.4
  18.6 0.0 collective-permute-done.2
  18.7 0.0 copy-done.1
  18.8 0.1 collective-permute-start.7
  18.9 0.0 collective-permute-done.5
  18.9 1.7 %collective-permute-done.6 = bf16[8,8192]{1,0:T(8,128)(2,1)S(1)} collective-permute-done((bf16[8,8192]{1,0:T(8,128)(2,1)S(1)}, bf16[8,8192]{1,0:T(8,128)(2,1)S(1)}, u32[]{:S(2)}, u32[]{:S(2)}) %collective-permute-start.6) | collective-permute-done | bytes 131104 | tf_op jit(solution)/shard_map/ppermute | solution.py:175
  20.6 0.1 collective-permute-start.9
  20.7 0.6 %collective-permute-start.8 = (bf16[16,4096]{1,0:T(8,128)(2,1)S(1)}, bf16[16,4096]{1,0:T(8,128)(2,1)S(1)}, u32[]{:S(2)}, u32[]{:S(2)}) collective-permute-start(bf16[16,4096]{1,0:T(8,128)(2,1)S(1)} %pad_maximum_fusion.refs_4_), channel_id=1, source_target_pairs={{0,1},{1,0},{2,3},{3,2},{4,5},{5,4},{6,7},{7,6},{8,9},{9,8},{10,11... | collective-permute-start | bytes 393224 | tf_op jit(solution)/shard_map/ppermute | solution.py:175
  21.3 0.8 %collective-permute-done.9.refs_5_ = bf16[16,4096]{1,0:T(8,128)(2,1)S(1)} collective-permute-done((bf16[16,4096]{1,0:T(8,128)(2,1)S(1)}, bf16[16,4096]{1,0:T(8,128)(2,1)S(1)}, u32[]{:S(2)}, u32[]{:S(2)}) %collective-permute-start.9) | collective-permute-done | bytes 131104 | tf_op jit(solution)/shard_map/ppermute | solution.py:175
  22.0 0.0 collective-permute-done.7.refs_3_
  22.0 0.7 %shard_map.56 = (f32[128,224]{1,0:T(8,128)S(1)}, f32[128,224]{1,0:T(8,128)S(1)}) custom-call(bf16[8192,224]{1,0:T(8,128)(2,1)S(1)} %get-tuple-element.42.refs_0_, bf16[8192,224]{1,0:T(8,128)(2,1)S(1)} %get-tuple-element.43.refs_1_, bf16[48,8192]{1,0:T(8,128)(2,1)S(1)} %constant_dynamic-update-slice_fusion.refs_2_, ...), custom_call_target="tpu_custom_call" | custom-call | flops 469762048 | bytes 3670016 | tf_op jit(solution)/shard_map/pallas_call | solution.py:84
  22.7 0.0 collective-permute-done.8.refs_5_
  22.7 0.7 %shard_map.57.hidden_ref = bf16[128,224]{1,0:T(8,128)(2,1)S(1)} custom-call(bf16[8192,224]{1,0:T(8,128)(2,1)S(1)} %get-tuple-element.42.refs_0_, bf16[8192,224]{1,0:T(8,128)(2,1)S(1)} %get-tuple-element.43.refs_1_, bf16[48,8192]{1,0:T(8,128)(2,1)S(1)} %constant_dynamic-update-slice_fusion.refs_2_, bf16[48,8192]{1,0:T(8,128)(2,1)S(1)} %collective-permute-done.7.refs_3_, ...), custom_call_target="tpu_custom_call" | custom-call | flops 469762048 | bytes 3670016 | tf_op jit(solution)/shard_map/pallas_call | solution.py:84
  23.5 0.7 %shard_map.58 = (f32[32,8192]{1,0:T(8,128)S(1)}, f32[8,8192]{1,0:T(8,128)S(1)}, f32[24,8192]{1,0:T(8,128)S(1)}, bf16[32,8192]{1,0:T(8,128)(2,1)S(1)}, bf16[8,819...) custom-call(bf16[128,224]{1,0:T(8,128)(2,1)S(1)} %shard_map.57.hidden_ref, bf16[224,8192]{1,0:T(8,128)(2,1)S(1)} %get-tuple-element.49.down_ref), custom_call_target="tpu_custom_call" | custom-call | flops 469762048 | bytes 3670016 | tf_op jit(solution)/shard_map/pallas_call | solution.py:113
  24.2 0.2 collective-permute-start.12
  24.4 0.4 collective-permute-start.10
  24.8 0.8 %collective-permute-done.12 = bf16[8,8192]{1,0:T(8,128)(2,1)S(1)} collective-permute-done((bf16[8,8192]{1,0:T(8,128)(2,1)S(1)}, bf16[8,8192]{1,0:T(8,128)(2,1)S(1)}, u32[]{:S(2)}, u32[]{:S(2)}) %collective-permute-start.12) | collective-permute-done | bytes 131104 | tf_op jit(solution)/shard_map/ppermute | solution.py:175
  25.6 1.2 %collective-permute-start.13 = (bf16[8,8192]{1,0:T(8,128)(2,1)S(1)}, bf16[8,8192]{1,0:T(8,128)(2,1)S(1)}, u32[]{:S(2)}, u32[]{:S(2)}) collective-permute-start(bf16[8,8192]{1,0:T(8,128)(2,1)S(1)} %add_convert_fusion), channel_id=1, source_target_pairs={{0,6},{1,7},{2,4},{3,5},{4,2},{5,3},{6,0},{7,1},{8,14},{9,15},{10,... | collective-permute-start | bytes 393224 | tf_op jit(solution)/shard_map/ppermute | solution.py:175
  26.8 0.0 collective-permute-done.10
  26.8 0.0 collective-permute-start.11
  26.8 0.1 fusion.7
  26.9 0.0 copy-start
  26.9 1.9 %collective-permute-start.15 = (bf16[8,8192]{1,0:T(8,128)(2,1)S(1)}, bf16[8,8192]{1,0:T(8,128)(2,1)S(1)}, u32[]{:S(2)}, u32[]{:S(2)}) collective-permute-start(bf16[8,8192]{1,0:T(8,128)(2,1)S(1)} %get-tuple-element.63), channel_id=1, source_target_pairs={{0,4},{1,3},{2,6},{3,1},{4,0},{5,7},{6,2},{7,5},{8,12},{9,11},{10,... | collective-permute-start | bytes 393224 | tf_op jit(solution)/shard_map/ppermute | solution.py:175
  28.8 0.6 %collective-permute-start.16 = (bf16[8,8192]{1,0:T(8,128)(2,1)S(1)}, bf16[8,8192]{1,0:T(8,128)(2,1)S(1)}, u32[]{:S(2)}, u32[]{:S(2)}) collective-permute-start(bf16[8,8192]{1,0:T(8,128)(2,1)S(1)} %get-tuple-element.64), channel_id=1, source_target_pairs={{0,2},{1,5},{2,0},{3,7},{4,6},{5,1},{6,4},{7,3},{8,10},{9,13},{10,... | collective-permute-start | bytes 393224 | tf_op jit(solution)/shard_map/ppermute | solution.py:175
  29.4 3.5 %collective-permute-done.13 = bf16[8,8192]{1,0:T(8,128)(2,1)S(1)} collective-permute-done((bf16[8,8192]{1,0:T(8,128)(2,1)S(1)}, bf16[8,8192]{1,0:T(8,128)(2,1)S(1)}, u32[]{:S(2)}, u32[]{:S(2)}) %collective-permute-start.13) | collective-permute-done | bytes 131104 | tf_op jit(solution)/shard_map/ppermute | solution.py:175
  32.9 0.0 collective-permute-done.11
  32.9 0.1 convert_add_fusion
  33.1 0.4 collective-permute-start.14
  33.5 1.5 %collective-permute-done.15 = bf16[8,8192]{1,0:T(8,128)(2,1)S(1)} collective-permute-done((bf16[8,8192]{1,0:T(8,128)(2,1)S(1)}, bf16[8,8192]{1,0:T(8,128)(2,1)S(1)}, u32[]{:S(2)}, u32[]{:S(2)}) %collective-permute-start.15) | collective-permute-done | bytes 131104 | tf_op jit(solution)/shard_map/ppermute | solution.py:175
  35.0 0.6 %collective-permute-done.16 = bf16[8,8192]{1,0:T(8,128)(2,1)S(1)} collective-permute-done((bf16[8,8192]{1,0:T(8,128)(2,1)S(1)}, bf16[8,8192]{1,0:T(8,128)(2,1)S(1)}, u32[]{:S(2)}, u32[]{:S(2)}) %collective-permute-start.16) | collective-permute-done | bytes 131104 | tf_op jit(solution)/shard_map/ppermute | solution.py:175
  35.5 0.1 fusion.2
  35.6 1.9 %collective-permute-start.17 = (bf16[8,8192]{1,0:T(8,128)(2,1)S(1)}, bf16[8,8192]{1,0:T(8,128)(2,1)S(1)}, u32[]{:S(2)}, u32[]{:S(2)}) collective-permute-start(bf16[8,8192]{1,0:T(8,128)(2,1)S(1)} %fusion.2), channel_id=1, source_target_pairs={{0,8},{1,9},{2,10},{3,11},{4,12},{5,13},{6,14},{7,15},{8,0},{9,1},... | collective-permute-start | bytes 393224 | tf_op jit(solution)/shard_map/ppermute | solution.py:175
  37.5 5.3 %collective-permute-done.14 = bf16[16,8192]{1,0:T(8,128)(2,1)S(1)} collective-permute-done((bf16[16,8192]{1,0:T(8,128)(2,1)S(1)}, bf16[16,8192]{1,0:T(8,128)(2,1)S(1)}, u32[]{:S(2)}, u32[]{:S(2)}) %collective-permute-start.14) | collective-permute-done | bytes 262176 | tf_op jit(solution)/shard_map/ppermute | solution.py:175
  42.8 0.1 slice_add_fusion
  42.8 0.1 collective-permute-start.18
  43.0 0.0 collective-permute-done.17.refs_1_
  43.0 4.9 %collective-permute-done.18.refs_2_ = bf16[8,8192]{1,0:T(8,128)(2,1)S(1)} collective-permute-done((bf16[8,8192]{1,0:T(8,128)(2,1)S(1)}, bf16[8,8192]{1,0:T(8,128)(2,1)S(1)}, u32[]{:S(2)}, u32[]{:S(2)}) %collective-permute-start.18) | collective-permute-done | bytes 131104 | tf_op jit(solution)/shard_map/ppermute | solution.py:175
  47.9 0.0 copy-done
  47.9 0.9 %shard_map.59 = bf16[8,8192]{1,0:T(8,128)(2,1)} custom-call(f32[8,8192]{1,0:T(8,128)S(1)} %slice.52.refs_0_, bf16[8,8192]{1,0:T(8,128)(2,1)S(1)} %collective-permute-done.17.refs_1_, bf16[8,8192]{1,0:T(8,128)(2,1)S(1)} %collective-permute-done.18.refs_2_, s32[1,8192]{1,0:T(1,128)S(1)} %bitcast.3, bf16[256,128]{1,0:T(8,128)(2,1)S(1)} %pad_maximum_fusion.2.refs_4_), custom_call_target="tpu_custom_call" | custom-call | tf_op jit(solution)/shard_map/pallas_call | solution.py:153
  (16 shorter events, 0.3 us)
Async XLA Ops:
  0.0 10.7 %collective-permute-start = (bf16[8,8192]{1,0:T(8,128)(2,1)}, bf16[8,8192]{1,0:T(8,128)(2,1)S(1)}, u32[]{:S(2)}, u32[]{:S(2)}) collective-permute-start(bf16[8,8192]{1,0:T(8,128)(2,1)} %param.5), channel_id=1, source_target_pairs={{0,8},{1,9},{2,10},{3,11},{4,12},{5,13},{6,14},{7,15},{8,0},{9,1},... | collective-permute-start | bytes 393224 | tf_op jit(solution)/shard_map/ppermute | solution.py:175
  4.0 9.7 %collective-permute-start.1 = (bf16[8,8192]{1,0:T(8,128)(2,1)}, bf16[8,8192]{1,0:T(8,128)(2,1)S(1)}, u32[]{:S(2)}, u32[]{:S(2)}) collective-permute-start(bf16[8,8192]{1,0:T(8,128)(2,1)} %param.5), channel_id=1, source_target_pairs={{0,4},{1,3},{2,6},{3,1},{4,0},{5,7},{6,2},{7,5},{8,12},{9,11},{10,... | collective-permute-start | bytes 393224 | tf_op jit(solution)/shard_map/ppermute | solution.py:175
  5.6 13.0 %collective-permute-start.3 = (bf16[8,8192]{1,0:T(8,128)(2,1)}, bf16[8,8192]{1,0:T(8,128)(2,1)S(1)}, u32[]{:S(2)}, u32[]{:S(2)}) collective-permute-start(bf16[8,8192]{1,0:T(8,128)(2,1)} %param.5), channel_id=1, source_target_pairs={{0,2},{1,5},{2,0},{3,7},{4,6},{5,1},{6,4},{7,3},{8,10},{9,13},{10,... | collective-permute-start | bytes 393224 | tf_op jit(solution)/shard_map/ppermute | solution.py:175
  7.1 11.5 %collective-permute-start.4 = (bf16[8,8192]{1,0:T(8,128)(2,1)}, bf16[8,8192]{1,0:T(8,128)(2,1)S(1)}, u32[]{:S(2)}, u32[]{:S(2)}) collective-permute-start(bf16[8,8192]{1,0:T(8,128)(2,1)} %param.5), channel_id=1, source_target_pairs={{0,6},{1,7},{2,4},{3,5},{4,2},{5,3},{6,0},{7,1},{8,14},{9,15},{10,... | collective-permute-start | bytes 393224 | tf_op jit(solution)/shard_map/ppermute | solution.py:175
  10.7 8.0 %collective-permute-start.2 = (bf16[8,8192]{1,0:T(8,128)(2,1)S(1)}, bf16[8,8192]{1,0:T(8,128)(2,1)S(1)}, u32[]{:S(2)}, u32[]{:S(2)}) collective-permute-start(bf16[8,8192]{1,0:T(8,128)(2,1)S(1)} %collective-permute-done._), channel_id=1, source_target_pairs={{0,4},{1,3},{2,6},{3,1},{4,0},{5,7},{6,2},{7,5},{8,12},{9,11},{10,... | collective-permute-start | bytes 393224 | tf_op jit(solution)/shard_map/ppermute | solution.py:175
  11.4 9.1 %collective-permute-start.6 = (bf16[8,8192]{1,0:T(8,128)(2,1)S(1)}, bf16[8,8192]{1,0:T(8,128)(2,1)S(1)}, u32[]{:S(2)}, u32[]{:S(2)}) collective-permute-start(bf16[8,8192]{1,0:T(8,128)(2,1)S(1)} %collective-permute-done._), channel_id=1, source_target_pairs={{0,6},{1,7},{2,4},{3,5},{4,2},{5,3},{6,0},{7,1},{8,14},{9,15},{10,... | collective-permute-start | bytes 393224 | tf_op jit(solution)/shard_map/ppermute | solution.py:175
  13.7 5.2 %collective-permute-start.5 = (bf16[8,8192]{1,0:T(8,128)(2,1)S(1)}, bf16[8,8192]{1,0:T(8,128)(2,1)S(1)}, u32[]{:S(2)}, u32[]{:S(2)}) collective-permute-start(bf16[8,8192]{1,0:T(8,128)(2,1)S(1)} %collective-permute-done._), channel_id=1, source_target_pairs={{0,2},{1,5},{2,0},{3,7},{4,6},{5,1},{6,4},{7,3},{8,10},{9,13},{10,... | collective-permute-start | bytes 393224 | tf_op jit(solution)/shard_map/ppermute | solution.py:175
  14.2 4.6 %copy-start.1 = (bf16[8,8192]{1,0:T(8,128)(2,1)S(1)}, bf16[8,8192]{1,0:T(8,128)(2,1)}, u32[]{:S(2)}) copy-start(bf16[8,8192]{1,0:T(8,128)(2,1)} %param.5) | copy-start | bytes 393220
  18.8 3.2 %collective-permute-start.7 = (bf16[48,8192]{1,0:T(8,128)(2,1)S(1)}, bf16[48,8192]{1,0:T(8,128)(2,1)S(1)}, u32[]{:S(2)}, u32[]{:S(2)}) collective-permute-start(bf16[48,8192]{1,0:T(8,128)(2,1)S(1)} %constant_dynamic-update-slice_fusion.refs_2_), channel_id=1, source_target_pairs={{0,1},{1,0},{2,3},{3,2},{4,5},{5,4},{6,7},{7,6},{8,9},{9,8},{10,11... | collective-permute-start | bytes 2359304 | tf_op jit(solution)/shard_map/ppermute | solution.py:175
  20.6 1.4 %collective-permute-start.9 = (bf16[16,4096]{1,0:T(8,128)(2,1)S(1)}, bf16[16,4096]{1,0:T(8,128)(2,1)S(1)}, u32[]{:S(2)}, u32[]{:S(2)}) collective-permute-start(bf16[16,4096]{1,0:T(8,128)(2,1)S(1)} %pad_maximum_fusion.1.refs_4_), channel_id=1, source_target_pairs={{0,1},{1,0},{2,3},{3,2},{4,5},{5,4},{6,7},{7,6},{8,9},{9,8},{10,11... | collective-permute-start | bytes 393224 | tf_op jit(solution)/shard_map/ppermute | solution.py:175
  20.7 2.0 %collective-permute-start.8 = (bf16[16,4096]{1,0:T(8,128)(2,1)S(1)}, bf16[16,4096]{1,0:T(8,128)(2,1)S(1)}, u32[]{:S(2)}, u32[]{:S(2)}) collective-permute-start(bf16[16,4096]{1,0:T(8,128)(2,1)S(1)} %pad_maximum_fusion.refs_4_), channel_id=1, source_target_pairs={{0,1},{1,0},{2,3},{3,2},{4,5},{5,4},{6,7},{7,6},{8,9},{9,8},{10,11... | collective-permute-start | bytes 393224 | tf_op jit(solution)/shard_map/ppermute | solution.py:175
  24.2 1.4 %collective-permute-start.12 = (bf16[8,8192]{1,0:T(8,128)(2,1)S(1)}, bf16[8,8192]{1,0:T(8,128)(2,1)S(1)}, u32[]{:S(2)}, u32[]{:S(2)}) collective-permute-start(bf16[8,8192]{1,0:T(8,128)(2,1)S(1)} %get-tuple-element.55), channel_id=1, source_target_pairs={{0,1},{1,0},{2,3},{3,2},{4,5},{5,4},{6,7},{7,6},{8,9},{9,8},{10,11... | collective-permute-start | bytes 393224 | tf_op jit(solution)/shard_map/ppermute | solution.py:175
  24.4 2.4 %collective-permute-start.10 = (bf16[24,8192]{1,0:T(8,128)(2,1)S(1)}, bf16[24,8192]{1,0:T(8,128)(2,1)S(1)}, u32[]{:S(2)}, u32[]{:S(2)}) collective-permute-start(bf16[24,8192]{1,0:T(8,128)(2,1)S(1)} %get-tuple-element.51), channel_id=1, source_target_pairs={{0,1},{1,0},{2,3},{3,2},{4,5},{5,4},{6,7},{7,6},{8,9},{9,8},{10,11... | collective-permute-start | bytes 1179656 | tf_op jit(solution)/shard_map/ppermute | solution.py:175
  25.6 7.3 %collective-permute-start.13 = (bf16[8,8192]{1,0:T(8,128)(2,1)S(1)}, bf16[8,8192]{1,0:T(8,128)(2,1)S(1)}, u32[]{:S(2)}, u32[]{:S(2)}) collective-permute-start(bf16[8,8192]{1,0:T(8,128)(2,1)S(1)} %add_convert_fusion), channel_id=1, source_target_pairs={{0,6},{1,7},{2,4},{3,5},{4,2},{5,3},{6,0},{7,1},{8,14},{9,15},{10,... | collective-permute-start | bytes 393224 | tf_op jit(solution)/shard_map/ppermute | solution.py:175
  26.8 6.1 %collective-permute-start.11 = (bf16[32,8192]{1,0:T(8,128)(2,1)S(1)}, bf16[32,8192]{1,0:T(8,128)(2,1)S(1)}, u32[]{:S(2)}, u32[]{:S(2)}) collective-permute-start(bf16[32,8192]{1,0:T(8,128)(2,1)S(1)} %get-tuple-element.53), channel_id=1, source_target_pairs={{0,1},{1,0},{2,3},{3,2},{4,5},{5,4},{6,7},{7,6},{8,9},{9,8},{10,11... | collective-permute-start | bytes 1572872 | tf_op jit(solution)/shard_map/ppermute | solution.py:175
  26.9 21.0 %copy-start = (s32[8192]{0:T(1024)S(1)}, s32[8192]{0:T(1024)}, u32[]{:S(2)}) copy-start(s32[8192]{0:T(1024)} %param.9) | copy-start | bytes 98308
  26.9 8.0 %collective-permute-start.15 = (bf16[8,8192]{1,0:T(8,128)(2,1)S(1)}, bf16[8,8192]{1,0:T(8,128)(2,1)S(1)}, u32[]{:S(2)}, u32[]{:S(2)}) collective-permute-start(bf16[8,8192]{1,0:T(8,128)(2,1)S(1)} %get-tuple-element.63), channel_id=1, source_target_pairs={{0,4},{1,3},{2,6},{3,1},{4,0},{5,7},{6,2},{7,5},{8,12},{9,11},{10,... | collective-permute-start | bytes 393224 | tf_op jit(solution)/shard_map/ppermute | solution.py:175
  28.8 6.7 %collective-permute-start.16 = (bf16[8,8192]{1,0:T(8,128)(2,1)S(1)}, bf16[8,8192]{1,0:T(8,128)(2,1)S(1)}, u32[]{:S(2)}, u32[]{:S(2)}) collective-permute-start(bf16[8,8192]{1,0:T(8,128)(2,1)S(1)} %get-tuple-element.64), channel_id=1, source_target_pairs={{0,2},{1,5},{2,0},{3,7},{4,6},{5,1},{6,4},{7,3},{8,10},{9,13},{10,... | collective-permute-start | bytes 393224 | tf_op jit(solution)/shard_map/ppermute | solution.py:175
  33.1 9.7 %collective-permute-start.14 = (bf16[16,8192]{1,0:T(8,128)(2,1)S(1)}, bf16[16,8192]{1,0:T(8,128)(2,1)S(1)}, u32[]{:S(2)}, u32[]{:S(2)}) collective-permute-start(bf16[16,8192]{1,0:T(8,128)(2,1)S(1)} %slice.67), channel_id=1, source_target_pairs={{0,4},{1,3},{2,6},{3,1},{4,0},{5,7},{6,2},{7,5},{8,12},{9,11},{10,... | collective-permute-start | bytes 786440 | tf_op jit(solution)/shard_map/ppermute | solution.py:175
  35.6 7.4 %collective-permute-start.17 = (bf16[8,8192]{1,0:T(8,128)(2,1)S(1)}, bf16[8,8192]{1,0:T(8,128)(2,1)S(1)}, u32[]{:S(2)}, u32[]{:S(2)}) collective-permute-start(bf16[8,8192]{1,0:T(8,128)(2,1)S(1)} %fusion.2), channel_id=1, source_target_pairs={{0,8},{1,9},{2,10},{3,11},{4,12},{5,13},{6,14},{7,15},{8,0},{9,1},... | collective-permute-start | bytes 393224 | tf_op jit(solution)/shard_map/ppermute | solution.py:175
  42.8 5.0 %collective-permute-start.18 = (bf16[8,8192]{1,0:T(8,128)(2,1)S(1)}, bf16[8,8192]{1,0:T(8,128)(2,1)S(1)}, u32[]{:S(2)}, u32[]{:S(2)}) collective-permute-start(bf16[8,8192]{1,0:T(8,128)(2,1)S(1)} %slice.68), channel_id=1, source_target_pairs={{0,2},{1,5},{2,0},{3,7},{4,6},{5,1},{6,4},{7,3},{8,10},{9,13},{10,... | collective-permute-start | bytes 393224 | tf_op jit(solution)/shard_map/ppermute | solution.py:175

commit v26 on v20

--- a/solution.py
+++ b/solution.py
@@ -210,7 +210,7 @@
         rest = rest + rest_there.astype(jnp.float32)
         leave = rest[count:].astype(jnp.bfloat16)
         total = rest[:count]
-        for piece in (diagonal, swap(leave[:count], square[0]), swap(leave[count:], square[1])):
+        for piece in (diagonal, swap(leave[count:], square[1]), swap(leave[:count], square[0])):
             total = total + piece.astype(jnp.float32)
         arrived = []
         for masks in reversed(far):

time: 44.8 us -> 45.3 us (1.011)
  transfers between devices with their start and end apart: 19 -> 19, of which waited for: 9 -> 9; matrix products, arithmetic and copies ran while one was open for 1% -> 1% of each run, Pallas kernels for 12% -> 11%
where the time goes in v26:
time: 45.3 us; the launch traced here: 45.2 us
  starting transfers between devices  20.5 us (45%)
  waiting for transfers between devices  16.4 us (36%)
  Pallas kernels  7.51 us (17%)
    ppermute x19, starting transfers between devices, swap(): lax.ppermute(value, 'gx', [(i, i ^ masks[i % 2]) for i in range(members)])  20.5 us
    ppermute x19, waiting for transfers between devices, swap(): lax.ppermute(value, 'gx', [(i, i ^ masks[i % 2]) for i in range(members)])  16.4 us
    pallas_call x1, Pallas kernels, load(): pl.pallas_call(load_kernel, out_shape=(shape, shape, jax.ShapeDtypeStruct...  4.46 us
    pallas_call x2, Pallas kernels, hidden_units(): pl.pallas_call(functools.partial(hidden_kernel, start, last), out_shape=(...  1.45 us
  transfers between devices with their start and end apart: 19, of which 9 were waited for; matrix products, arithmetic and copies ran while one was open for 1% of the time, Pallas kernels for 11%

profile of v26, /device:TPU:0, one launch (start us, length us, event | category | flops | bytes accessed | tf_op | source)
XLA Modules:
  0.0 45.2 jit_solution(17177561596187945730)
XLA Ops:
  0.0 4.0 %collective-permute-start = (bf16[8,8192]{1,0:T(8,128)(2,1)}, bf16[8,8192]{1,0:T(8,128)(2,1)S(1)}, u32[]{:S(2)}, u32[]{:S(2)}) collective-permute-start(bf16[8,8192]{1,0:T(8,128)(2,1)} %param.5), channel_id=1, source_target_pairs={{0,8},{1,9},{2,10},{3,11},{4,12},{5,13},{6,14},{7,15},{8,0},{9,1},... | collective-permute-start | bytes 393224 | tf_op jit(solution)/shard_map/ppermute | solution.py:175
  4.0 1.6 %collective-permute-start.1 = (bf16[8,8192]{1,0:T(8,128)(2,1)}, bf16[8,8192]{1,0:T(8,128)(2,1)S(1)}, u32[]{:S(2)}, u32[]{:S(2)}) collective-permute-start(bf16[8,8192]{1,0:T(8,128)(2,1)} %param.5), channel_id=1, source_target_pairs={{0,4},{1,3},{2,6},{3,1},{4,0},{5,7},{6,2},{7,5},{8,12},{9,11},{10,... | collective-permute-start | bytes 393224 | tf_op jit(solution)/shard_map/ppermute | solution.py:175
  5.6 1.5 %collective-permute-start.3 = (bf16[8,8192]{1,0:T(8,128)(2,1)}, bf16[8,8192]{1,0:T(8,128)(2,1)S(1)}, u32[]{:S(2)}, u32[]{:S(2)}) collective-permute-start(bf16[8,8192]{1,0:T(8,128)(2,1)} %param.5), channel_id=1, source_target_pairs={{0,2},{1,5},{2,0},{3,7},{4,6},{5,1},{6,4},{7,3},{8,10},{9,13},{10,... | collective-permute-start | bytes 393224 | tf_op jit(solution)/shard_map/ppermute | solution.py:175
  7.1 0.4 collective-permute-start.4
  7.5 3.1 %collective-permute-done._ = bf16[8,8192]{1,0:T(8,128)(2,1)S(1)} collective-permute-done((bf16[8,8192]{1,0:T(8,128)(2,1)}, bf16[8,8192]{1,0:T(8,128)(2,1)S(1)}, u32[]{:S(2)}, u32[]{:S(2)}) %collective-permute-start) | collective-permute-done | bytes 131104 | tf_op jit(solution)/shard_map/ppermute | solution.py:175
  10.7 0.8 %collective-permute-start.2 = (bf16[8,8192]{1,0:T(8,128)(2,1)S(1)}, bf16[8,8192]{1,0:T(8,128)(2,1)S(1)}, u32[]{:S(2)}, u32[]{:S(2)}) collective-permute-start(bf16[8,8192]{1,0:T(8,128)(2,1)S(1)} %collective-permute-done._), channel_id=1, source_target_pairs={{0,4},{1,3},{2,6},{3,1},{4,0},{5,7},{6,2},{7,5},{8,12},{9,11},{10,... | collective-permute-start | bytes 393224 | tf_op jit(solution)/shard_map/ppermute | solution.py:175
  11.4 1.5 %collective-permute-start.5 = (bf16[8,8192]{1,0:T(8,128)(2,1)S(1)}, bf16[8,8192]{1,0:T(8,128)(2,1)S(1)}, u32[]{:S(2)}, u32[]{:S(2)}) collective-permute-start(bf16[8,8192]{1,0:T(8,128)(2,1)S(1)} %collective-permute-done._), channel_id=1, source_target_pairs={{0,2},{1,5},{2,0},{3,7},{4,6},{5,1},{6,4},{7,3},{8,10},{9,13},{10,... | collective-permute-start | bytes 393224 | tf_op jit(solution)/shard_map/ppermute | solution.py:175
  12.9 0.0 collective-permute-done.1
  12.9 1.5 %collective-permute-start.6 = (bf16[8,8192]{1,0:T(8,128)(2,1)S(1)}, bf16[8,8192]{1,0:T(8,128)(2,1)S(1)}, u32[]{:S(2)}, u32[]{:S(2)}) collective-permute-start(bf16[8,8192]{1,0:T(8,128)(2,1)S(1)} %collective-permute-done._), channel_id=1, source_target_pairs={{0,6},{1,7},{2,4},{3,5},{4,2},{5,3},{6,0},{7,1},{8,14},{9,15},{10,... | collective-permute-start | bytes 393224 | tf_op jit(solution)/shard_map/ppermute | solution.py:175
  14.4 0.0 copy-start.1
  14.4 4.5 %shard_map.55 = (bf16[8192,224]{1,0:T(8,128)(2,1)S(1)}, bf16[8192,224]{1,0:T(8,128)(2,1)S(1)}, bf16[224,8192]{1,0:T(8,128)(2,1)S(1)}) custom-call(bf16[224,8192]{1,0:T(8,128)(2,1)} %bitcast.4, bf16[224,8192]{1,0:T(8,128)(2,1)} %bitcast.5, bf16[224,8192]{1,0:T(8,128)(2,1)} %down_hbm.1, bf16[8,8192]{1,0:T(8,128)(2,1)S(1)} %collective-permute-done._), custom_call_target="tpu_custom_call" | custom-call | bytes 11010048 | tf_op jit(solution)/shard_map/pallas_call | solution.py:44
  18.9 0.0 collective-permute-done.3
  18.9 0.0 collective-permute-done.4
  18.9 0.0 collective-permute-done.2
  19.0 0.0 copy-done.1
  19.0 0.1 collective-permute-start.7
  19.1 1.4 %collective-permute-done.6 = bf16[8,8192]{1,0:T(8,128)(2,1)S(1)} collective-permute-done((bf16[8,8192]{1,0:T(8,128)(2,1)S(1)}, bf16[8,8192]{1,0:T(8,128)(2,1)S(1)}, u32[]{:S(2)}, u32[]{:S(2)}) %collective-permute-start.6) | collective-permute-done | bytes 131104 | tf_op jit(solution)/shard_map/ppermute | solution.py:175
  20.5 0.0 collective-permute-done.5
  20.6 0.1 collective-permute-start.9
  20.7 0.6 %collective-permute-start.8 = (bf16[16,4096]{1,0:T(8,128)(2,1)S(1)}, bf16[16,4096]{1,0:T(8,128)(2,1)S(1)}, u32[]{:S(2)}, u32[]{:S(2)}) collective-permute-start(bf16[16,4096]{1,0:T(8,128)(2,1)S(1)} %pad_maximum_fusion.refs_4_), channel_id=1, source_target_pairs={{0,1},{1,0},{2,3},{3,2},{4,5},{5,4},{6,7},{7,6},{8,9},{9,8},{10,11... | collective-permute-start | bytes 393224 | tf_op jit(solution)/shard_map/ppermute | solution.py:175
  21.2 0.8 %collective-permute-done.9.refs_5_ = bf16[16,4096]{1,0:T(8,128)(2,1)S(1)} collective-permute-done((bf16[16,4096]{1,0:T(8,128)(2,1)S(1)}, bf16[16,4096]{1,0:T(8,128)(2,1)S(1)}, u32[]{:S(2)}, u32[]{:S(2)}) %collective-permute-start.9) | collective-permute-done | bytes 131104 | tf_op jit(solution)/shard_map/ppermute | solution.py:175
  22.0 0.0 collective-permute-done.7.refs_3_
  22.0 0.7 %shard_map.56 = (f32[128,224]{1,0:T(8,128)S(1)}, f32[128,224]{1,0:T(8,128)S(1)}) custom-call(bf16[8192,224]{1,0:T(8,128)(2,1)S(1)} %get-tuple-element.40.refs_0_, bf16[8192,224]{1,0:T(8,128)(2,1)S(1)} %get-tuple-element.41.refs_1_, bf16[48,8192]{1,0:T(8,128)(2,1)S(1)} %constant_dynamic-update-slice_fusion.refs_2_, ...), custom_call_target="tpu_custom_call" | custom-call | flops 469762048 | bytes 3670016 | tf_op jit(solution)/shard_map/pallas_call | solution.py:84
  22.7 0.0 collective-permute-done.8.refs_5_
  22.7 0.7 %shard_map.57.hidden_ref = bf16[128,224]{1,0:T(8,128)(2,1)S(1)} custom-call(bf16[8192,224]{1,0:T(8,128)(2,1)S(1)} %get-tuple-element.40.refs_0_, bf16[8192,224]{1,0:T(8,128)(2,1)S(1)} %get-tuple-element.41.refs_1_, bf16[48,8192]{1,0:T(8,128)(2,1)S(1)} %constant_dynamic-update-slice_fusion.refs_2_, bf16[48,8192]{1,0:T(8,128)(2,1)S(1)} %collective-permute-done.7.refs_3_, ...), custom_call_target="tpu_custom_call" | custom-call | flops 469762048 | bytes 3670016 | tf_op jit(solution)/shard_map/pallas_call | solution.py:84
  23.4 0.7 %shard_map.58 = (f32[32,8192]{1,0:T(8,128)S(1)}, f32[8,8192]{1,0:T(8,128)S(1)}, f32[24,8192]{1,0:T(8,128)S(1)}, bf16[32,8192]{1,0:T(8,128)(2,1)S(1)}, bf16[8,819...) custom-call(bf16[128,224]{1,0:T(8,128)(2,1)S(1)} %shard_map.57.hidden_ref, bf16[224,8192]{1,0:T(8,128)(2,1)S(1)} %get-tuple-element.47.down_ref), custom_call_target="tpu_custom_call" | custom-call | flops 469762048 | bytes 3670016 | tf_op jit(solution)/shard_map/pallas_call | solution.py:113
  24.2 0.2 collective-permute-start.13
  24.4 0.4 collective-permute-start.10
  24.7 0.8 %collective-permute-done.13 = bf16[8,8192]{1,0:T(8,128)(2,1)S(1)} collective-permute-done((bf16[8,8192]{1,0:T(8,128)(2,1)S(1)}, bf16[8,8192]{1,0:T(8,128)(2,1)S(1)}, u32[]{:S(2)}, u32[]{:S(2)}) %collective-permute-start.13) | collective-permute-done | bytes 131104 | tf_op jit(solution)/shard_map/ppermute | solution.py:175
  25.6 1.2 %collective-permute-start.14 = (bf16[8,8192]{1,0:T(8,128)(2,1)S(1)}, bf16[8,8192]{1,0:T(8,128)(2,1)S(1)}, u32[]{:S(2)}, u32[]{:S(2)}) collective-permute-start(bf16[8,8192]{1,0:T(8,128)(2,1)S(1)} %add_convert_fusion), channel_id=1, source_target_pairs={{0,6},{1,7},{2,4},{3,5},{4,2},{5,3},{6,0},{7,1},{8,14},{9,15},{10,... | collective-permute-start | bytes 393224 | tf_op jit(solution)/shard_map/ppermute | solution.py:175
  26.8 0.0 collective-permute-done.10
  26.8 0.0 collective-permute-start.11
  26.8 0.1 fusion.7
  26.9 0.0 copy-start
  26.9 1.6 %collective-permute-start.15 = (bf16[8,8192]{1,0:T(8,128)(2,1)S(1)}, bf16[8,8192]{1,0:T(8,128)(2,1)S(1)}, u32[]{:S(2)}, u32[]{:S(2)}) collective-permute-start(bf16[8,8192]{1,0:T(8,128)(2,1)S(1)} %get-tuple-element.59), channel_id=1, source_target_pairs={{0,2},{1,5},{2,0},{3,7},{4,6},{5,1},{6,4},{7,3},{8,10},{9,13},{10,... | collective-permute-start | bytes 393224 | tf_op jit(solution)/shard_map/ppermute | solution.py:175
  28.5 0.9 %collective-permute-start.16 = (bf16[8,8192]{1,0:T(8,128)(2,1)S(1)}, bf16[8,8192]{1,0:T(8,128)(2,1)S(1)}, u32[]{:S(2)}, u32[]{:S(2)}) collective-permute-start(bf16[8,8192]{1,0:T(8,128)(2,1)S(1)} %get-tuple-element.60), channel_id=1, source_target_pairs={{0,4},{1,3},{2,6},{3,1},{4,0},{5,7},{6,2},{7,5},{8,12},{9,11},{10,... | collective-permute-start | bytes 393224 | tf_op jit(solution)/shard_map/ppermute | solution.py:175
  29.4 0.0 collective-permute-done.11
  29.4 0.1 convert_add_fusion
  29.5 1.3 %collective-permute-start.12 = (bf16[16,8192]{1,0:T(8,128)(2,1)S(1)}, bf16[16,8192]{1,0:T(8,128)(2,1)S(1)}, u32[]{:S(2)}, u32[]{:S(2)}) collective-permute-start(bf16[16,8192]{1,0:T(8,128)(2,1)S(1)} %slice.67), channel_id=1, source_target_pairs={{0,4},{1,3},{2,6},{3,1},{4,0},{5,7},{6,2},{7,5},{8,12},{9,11},{10,... | collective-permute-start | bytes 786440 | tf_op jit(solution)/shard_map/ppermute | solution.py:175
  30.8 2.2 %collective-permute-done.14 = bf16[8,8192]{1,0:T(8,128)(2,1)S(1)} collective-permute-done((bf16[8,8192]{1,0:T(8,128)(2,1)S(1)}, bf16[8,8192]{1,0:T(8,128)(2,1)S(1)}, u32[]{:S(2)}, u32[]{:S(2)}) %collective-permute-start.14) | collective-permute-done | bytes 131104 | tf_op jit(solution)/shard_map/ppermute | solution.py:175
  32.9 1.8 %collective-permute-done.15 = bf16[8,8192]{1,0:T(8,128)(2,1)S(1)} collective-permute-done((bf16[8,8192]{1,0:T(8,128)(2,1)S(1)}, bf16[8,8192]{1,0:T(8,128)(2,1)S(1)}, u32[]{:S(2)}, u32[]{:S(2)}) %collective-permute-start.15) | collective-permute-done | bytes 131104 | tf_op jit(solution)/shard_map/ppermute | solution.py:175
  34.8 0.2 collective-permute-done.16
  35.0 0.1 fusion.2
  35.0 2.2 %collective-permute-start.17 = (bf16[8,8192]{1,0:T(8,128)(2,1)S(1)}, bf16[8,8192]{1,0:T(8,128)(2,1)S(1)}, u32[]{:S(2)}, u32[]{:S(2)}) collective-permute-start(bf16[8,8192]{1,0:T(8,128)(2,1)S(1)} %fusion.2), channel_id=1, source_target_pairs={{0,8},{1,9},{2,10},{3,11},{4,12},{5,13},{6,14},{7,15},{8,0},{9,1},... | collective-permute-start | bytes 393224 | tf_op jit(solution)/shard_map/ppermute | solution.py:175
  37.2 0.5 %collective-permute-done.12 = bf16[16,8192]{1,0:T(8,128)(2,1)S(1)} collective-permute-done((bf16[16,8192]{1,0:T(8,128)(2,1)S(1)}, bf16[16,8192]{1,0:T(8,128)(2,1)S(1)}, u32[]{:S(2)}, u32[]{:S(2)}) %collective-permute-start.12) | collective-permute-done | bytes 262176 | tf_op jit(solution)/shard_map/ppermute | solution.py:175
  37.8 0.1 slice_add_fusion
  37.9 0.9 %collective-permute-start.18 = (bf16[8,8192]{1,0:T(8,128)(2,1)S(1)}, bf16[8,8192]{1,0:T(8,128)(2,1)S(1)}, u32[]{:S(2)}, u32[]{:S(2)}) collective-permute-start(bf16[8,8192]{1,0:T(8,128)(2,1)S(1)} %slice.68), channel_id=1, source_target_pairs={{0,2},{1,5},{2,0},{3,7},{4,6},{5,1},{6,4},{7,3},{8,10},{9,13},{10,... | collective-permute-start | bytes 393224 | tf_op jit(solution)/shard_map/ppermute | solution.py:175
  38.9 5.4 %collective-permute-done.17.refs_1_ = bf16[8,8192]{1,0:T(8,128)(2,1)S(1)} collective-permute-done((bf16[8,8192]{1,0:T(8,128)(2,1)S(1)}, bf16[8,8192]{1,0:T(8,128)(2,1)S(1)}, u32[]{:S(2)}, u32[]{:S(2)}) %collective-permute-start.17) | collective-permute-done | bytes 131104 | tf_op jit(solution)/shard_map/ppermute | solution.py:175
  44.3 0.0 collective-permute-done.18.refs_2_
  44.3 0.0 copy-done
  44.3 0.9 %shard_map.59 = bf16[8,8192]{1,0:T(8,128)(2,1)} custom-call(f32[8,8192]{1,0:T(8,128)S(1)} %slice.52.refs_0_, bf16[8,8192]{1,0:T(8,128)(2,1)S(1)} %collective-permute-done.17.refs_1_, bf16[8,8192]{1,0:T(8,128)(2,1)S(1)} %collective-permute-done.18.refs_2_, s32[1,8192]{1,0:T(1,128)S(1)} %bitcast.3, bf16[256,128]{1,0:T(8,128)(2,1)S(1)} %pad_maximum_fusion.2.refs_4_), custom_call_target="tpu_custom_call" | custom-call | tf_op jit(solution)/shard_map/pallas_call | solution.py:153
  (16 shorter events, 0.3 us)
Async XLA Ops:
  0.0 10.7 %collective-permute-start = (bf16[8,8192]{1,0:T(8,128)(2,1)}, bf16[8,8192]{1,0:T(8,128)(2,1)S(1)}, u32[]{:S(2)}, u32[]{:S(2)}) collective-permute-start(bf16[8,8192]{1,0:T(8,128)(2,1)} %param.5), channel_id=1, source_target_pairs={{0,8},{1,9},{2,10},{3,11},{4,12},{5,13},{6,14},{7,15},{8,0},{9,1},... | collective-permute-start | bytes 393224 | tf_op jit(solution)/shard_map/ppermute | solution.py:175
  4.0 8.9 %collective-permute-start.1 = (bf16[8,8192]{1,0:T(8,128)(2,1)}, bf16[8,8192]{1,0:T(8,128)(2,1)S(1)}, u32[]{:S(2)}, u32[]{:S(2)}) collective-permute-start(bf16[8,8192]{1,0:T(8,128)(2,1)} %param.5), channel_id=1, source_target_pairs={{0,4},{1,3},{2,6},{3,1},{4,0},{5,7},{6,2},{7,5},{8,12},{9,11},{10,... | collective-permute-start | bytes 393224 | tf_op jit(solution)/shard_map/ppermute | solution.py:175
  5.6 13.3 %collective-permute-start.3 = (bf16[8,8192]{1,0:T(8,128)(2,1)}, bf16[8,8192]{1,0:T(8,128)(2,1)S(1)}, u32[]{:S(2)}, u32[]{:S(2)}) collective-permute-start(bf16[8,8192]{1,0:T(8,128)(2,1)} %param.5), channel_id=1, source_target_pairs={{0,2},{1,5},{2,0},{3,7},{4,6},{5,1},{6,4},{7,3},{8,10},{9,13},{10,... | collective-permute-start | bytes 393224 | tf_op jit(solution)/shard_map/ppermute | solution.py:175
  7.1 11.7 %collective-permute-start.4 = (bf16[8,8192]{1,0:T(8,128)(2,1)}, bf16[8,8192]{1,0:T(8,128)(2,1)S(1)}, u32[]{:S(2)}, u32[]{:S(2)}) collective-permute-start(bf16[8,8192]{1,0:T(8,128)(2,1)} %param.5), channel_id=1, source_target_pairs={{0,6},{1,7},{2,4},{3,5},{4,2},{5,3},{6,0},{7,1},{8,14},{9,15},{10,... | collective-permute-start | bytes 393224 | tf_op jit(solution)/shard_map/ppermute | solution.py:175
  10.7 8.2 %collective-permute-start.2 = (bf16[8,8192]{1,0:T(8,128)(2,1)S(1)}, bf16[8,8192]{1,0:T(8,128)(2,1)S(1)}, u32[]{:S(2)}, u32[]{:S(2)}) collective-permute-start(bf16[8,8192]{1,0:T(8,128)(2,1)S(1)} %collective-permute-done._), channel_id=1, source_target_pairs={{0,4},{1,3},{2,6},{3,1},{4,0},{5,7},{6,2},{7,5},{8,12},{9,11},{10,... | collective-permute-start | bytes 393224 | tf_op jit(solution)/shard_map/ppermute | solution.py:175
  11.4 9.1 %collective-permute-start.5 = (bf16[8,8192]{1,0:T(8,128)(2,1)S(1)}, bf16[8,8192]{1,0:T(8,128)(2,1)S(1)}, u32[]{:S(2)}, u32[]{:S(2)}) collective-permute-start(bf16[8,8192]{1,0:T(8,128)(2,1)S(1)} %collective-permute-done._), channel_id=1, source_target_pairs={{0,2},{1,5},{2,0},{3,7},{4,6},{5,1},{6,4},{7,3},{8,10},{9,13},{10,... | collective-permute-start | bytes 393224 | tf_op jit(solution)/shard_map/ppermute | solution.py:175
  12.9 7.6 %collective-permute-start.6 = (bf16[8,8192]{1,0:T(8,128)(2,1)S(1)}, bf16[8,8192]{1,0:T(8,128)(2,1)S(1)}, u32[]{:S(2)}, u32[]{:S(2)}) collective-permute-start(bf16[8,8192]{1,0:T(8,128)(2,1)S(1)} %collective-permute-done._), channel_id=1, source_target_pairs={{0,6},{1,7},{2,4},{3,5},{4,2},{5,3},{6,0},{7,1},{8,14},{9,15},{10,... | collective-permute-start | bytes 393224 | tf_op jit(solution)/shard_map/ppermute | solution.py:175
  14.4 4.6 %copy-start.1 = (bf16[8,8192]{1,0:T(8,128)(2,1)S(1)}, bf16[8,8192]{1,0:T(8,128)(2,1)}, u32[]{:S(2)}) copy-start(bf16[8,8192]{1,0:T(8,128)(2,1)} %param.5) | copy-start | bytes 393220
  19.0 3.0 %collective-permute-start.7 = (bf16[48,8192]{1,0:T(8,128)(2,1)S(1)}, bf16[48,8192]{1,0:T(8,128)(2,1)S(1)}, u32[]{:S(2)}, u32[]{:S(2)}) collective-permute-start(bf16[48,8192]{1,0:T(8,128)(2,1)S(1)} %constant_dynamic-update-slice_fusion.refs_2_), channel_id=1, source_target_pairs={{0,1},{1,0},{2,3},{3,2},{4,5},{5,4},{6,7},{7,6},{8,9},{9,8},{10,11... | collective-permute-start | bytes 2359304 | tf_op jit(solution)/shard_map/ppermute | solution.py:175
  20.6 1.4 %collective-permute-start.9 = (bf16[16,4096]{1,0:T(8,128)(2,1)S(1)}, bf16[16,4096]{1,0:T(8,128)(2,1)S(1)}, u32[]{:S(2)}, u32[]{:S(2)}) collective-permute-start(bf16[16,4096]{1,0:T(8,128)(2,1)S(1)} %pad_maximum_fusion.1.refs_4_), channel_id=1, source_target_pairs={{0,1},{1,0},{2,3},{3,2},{4,5},{5,4},{6,7},{7,6},{8,9},{9,8},{10,11... | collective-permute-start | bytes 393224 | tf_op jit(solution)/shard_map/ppermute | solution.py:175
  20.7 2.0 %collective-permute-start.8 = (bf16[16,4096]{1,0:T(8,128)(2,1)S(1)}, bf16[16,4096]{1,0:T(8,128)(2,1)S(1)}, u32[]{:S(2)}, u32[]{:S(2)}) collective-permute-start(bf16[16,4096]{1,0:T(8,128)(2,1)S(1)} %pad_maximum_fusion.refs_4_), channel_id=1, source_target_pairs={{0,1},{1,0},{2,3},{3,2},{4,5},{5,4},{6,7},{7,6},{8,9},{9,8},{10,11... | collective-permute-start | bytes 393224 | tf_op jit(solution)/shard_map/ppermute | solution.py:175
  24.2 1.4 %collective-permute-start.13 = (bf16[8,8192]{1,0:T(8,128)(2,1)S(1)}, bf16[8,8192]{1,0:T(8,128)(2,1)S(1)}, u32[]{:S(2)}, u32[]{:S(2)}) collective-permute-start(bf16[8,8192]{1,0:T(8,128)(2,1)S(1)} %get-tuple-element.55), channel_id=1, source_target_pairs={{0,1},{1,0},{2,3},{3,2},{4,5},{5,4},{6,7},{7,6},{8,9},{9,8},{10,11... | collective-permute-start | bytes 393224 | tf_op jit(solution)/shard_map/ppermute | solution.py:175
  24.4 2.4 %collective-permute-start.10 = (bf16[24,8192]{1,0:T(8,128)(2,1)S(1)}, bf16[24,8192]{1,0:T(8,128)(2,1)S(1)}, u32[]{:S(2)}, u32[]{:S(2)}) collective-permute-start(bf16[24,8192]{1,0:T(8,128)(2,1)S(1)} %get-tuple-element.49), channel_id=1, source_target_pairs={{0,1},{1,0},{2,3},{3,2},{4,5},{5,4},{6,7},{7,6},{8,9},{9,8},{10,11... | collective-permute-start | bytes 1179656 | tf_op jit(solution)/shard_map/ppermute | solution.py:175
  25.6 7.3 %collective-permute-start.14 = (bf16[8,8192]{1,0:T(8,128)(2,1)S(1)}, bf16[8,8192]{1,0:T(8,128)(2,1)S(1)}, u32[]{:S(2)}, u32[]{:S(2)}) collective-permute-start(bf16[8,8192]{1,0:T(8,128)(2,1)S(1)} %add_convert_fusion), channel_id=1, source_target_pairs={{0,6},{1,7},{2,4},{3,5},{4,2},{5,3},{6,0},{7,1},{8,14},{9,15},{10,... | collective-permute-start | bytes 393224 | tf_op jit(solution)/shard_map/ppermute | solution.py:175
  26.8 2.5 %collective-permute-start.11 = (bf16[32,8192]{1,0:T(8,128)(2,1)S(1)}, bf16[32,8192]{1,0:T(8,128)(2,1)S(1)}, u32[]{:S(2)}, u32[]{:S(2)}) collective-permute-start(bf16[32,8192]{1,0:T(8,128)(2,1)S(1)} %get-tuple-element.51), channel_id=1, source_target_pairs={{0,1},{1,0},{2,3},{3,2},{4,5},{5,4},{6,7},{7,6},{8,9},{9,8},{10,11... | collective-permute-start | bytes 1572872 | tf_op jit(solution)/shard_map/ppermute | solution.py:175
  26.9 17.4 %copy-start = (s32[8192]{0:T(1024)S(1)}, s32[8192]{0:T(1024)}, u32[]{:S(2)}) copy-start(s32[8192]{0:T(1024)} %param.9) | copy-start | bytes 98308
  26.9 7.8 %collective-permute-start.15 = (bf16[8,8192]{1,0:T(8,128)(2,1)S(1)}, bf16[8,8192]{1,0:T(8,128)(2,1)S(1)}, u32[]{:S(2)}, u32[]{:S(2)}) collective-permute-start(bf16[8,8192]{1,0:T(8,128)(2,1)S(1)} %get-tuple-element.59), channel_id=1, source_target_pairs={{0,2},{1,5},{2,0},{3,7},{4,6},{5,1},{6,4},{7,3},{8,10},{9,13},{10,... | collective-permute-start | bytes 393224 | tf_op jit(solution)/shard_map/ppermute | solution.py:175
  28.5 6.5 %collective-permute-start.16 = (bf16[8,8192]{1,0:T(8,128)(2,1)S(1)}, bf16[8,8192]{1,0:T(8,128)(2,1)S(1)}, u32[]{:S(2)}, u32[]{:S(2)}) collective-permute-start(bf16[8,8192]{1,0:T(8,128)(2,1)S(1)} %get-tuple-element.60), channel_id=1, source_target_pairs={{0,4},{1,3},{2,6},{3,1},{4,0},{5,7},{6,2},{7,5},{8,12},{9,11},{10,... | collective-permute-start | bytes 393224 | tf_op jit(solution)/shard_map/ppermute | solution.py:175
  29.5 8.3 %collective-permute-start.12 = (bf16[16,8192]{1,0:T(8,128)(2,1)S(1)}, bf16[16,8192]{1,0:T(8,128)(2,1)S(1)}, u32[]{:S(2)}, u32[]{:S(2)}) collective-permute-start(bf16[16,8192]{1,0:T(8,128)(2,1)S(1)} %slice.67), channel_id=1, source_target_pairs={{0,4},{1,3},{2,6},{3,1},{4,0},{5,7},{6,2},{7,5},{8,12},{9,11},{10,... | collective-permute-start | bytes 786440 | tf_op jit(solution)/shard_map/ppermute | solution.py:175
  35.0 9.2 %collective-permute-start.17 = (bf16[8,8192]{1,0:T(8,128)(2,1)S(1)}, bf16[8,8192]{1,0:T(8,128)(2,1)S(1)}, u32[]{:S(2)}, u32[]{:S(2)}) collective-permute-start(bf16[8,8192]{1,0:T(8,128)(2,1)S(1)} %fusion.2), channel_id=1, source_target_pairs={{0,8},{1,9},{2,10},{3,11},{4,12},{5,13},{6,14},{7,15},{8,0},{9,1},... | collective-permute-start | bytes 393224 | tf_op jit(solution)/shard_map/ppermute | solution.py:175
  37.9 6.4 %collective-permute-start.18 = (bf16[8,8192]{1,0:T(8,128)(2,1)S(1)}, bf16[8,8192]{1,0:T(8,128)(2,1)S(1)}, u32[]{:S(2)}, u32[]{:S(2)}) collective-permute-start(bf16[8,8192]{1,0:T(8,128)(2,1)S(1)} %slice.68), channel_id=1, source_target_pairs={{0,2},{1,5},{2,0},{3,7},{4,6},{5,1},{6,4},{7,3},{8,10},{9,13},{10,... | collective-permute-start | bytes 393224 | tf_op jit(solution)/shard_map/ppermute | solution.py:175

commit v27 on v20

--- a/solution.py
+++ b/solution.py
@@ -18,42 +18,49 @@
     return pl.BlockSpec(memory_space=pltpu.VMEM)
 
 
-def load_kernel(gate_hbm, up_hbm, down_hbm, _, gate_ref, up_ref, down_ref, staged, sems, down_sem):
-    tile = staged.shape[2] // sems.shape[1]
+def load_kernel(turned, *refs):
+    count = len(turned)
+    sources, outs = refs[:count], refs[count + 1 : 2 * count + 1]
+    staged, sems = refs[2 * count + 1 :]
+    tile = staged.shape[1] // (sems.shape[0] - 1)
     copies = []
-    for k in range(sems.shape[1]):
-        here = slice(k * tile, (k + 1) * tile)
-        for j, source in enumerate((gate_hbm, up_hbm)):
-            copies.append(
-                pltpu.make_async_copy(source.at[:, here], staged.at[j, :, here], sems.at[j, k])
-            )
-            copies[-1].start()
-    down_copy = pltpu.make_async_copy(down_hbm, down_ref, down_sem)
-    down_copy.start()
-    for k in range(sems.shape[1]):
-        here = slice(k * tile, (k + 1) * tile)
-        for j, out in enumerate((gate_ref, up_ref)):
-            copies[2 * k + j].wait()
-            out[here, :] = staged[j, :, here].T
-    down_copy.wait()
-
-
-def load(gate_w, up_w, down_w, after):
-    units, features = gate_w.shape
-    shape = jax.ShapeDtypeStruct((features, units), gate_w.dtype)
+    for source, out, turn in zip(sources, outs, turned):
+        if not turn:
+            continue
+        for k in range(sems.shape[0] - 1):
+            here = slice(k * tile, (k + 1) * tile)
+            copies.append((pltpu.make_async_copy(source.at[:, here], staged.at[:, here], sems.at[k]), out, here))
+    others = [
+        pltpu.make_async_copy(source, out, sems.at[sems.shape[0] - 1])
+        for source, out, turn in zip(sources, outs, turned)
+        if not turn
+    ]
+    for copy, _, _ in copies:
+        copy.start()
+    for copy in others:
+        copy.start()
+    for copy, out, here in copies:
+        copy.wait()
+        out[here, :] = staged[:, here].T
+    for copy in others:
+        copy.wait()
+
+
+def load(weights, turned, after):
+    shapes = [w.shape[::-1] if turn else w.shape for w, turn in zip(weights, turned)]
+    size = sum(w.size for w in weights)
     return pl.pallas_call(
-        load_kernel,
-        out_shape=(shape, shape, jax.ShapeDtypeStruct(down_w.shape, down_w.dtype)),
-        in_specs=[pl.BlockSpec(memory_space=pltpu.HBM)] * 3 + [pl.BlockSpec(memory_space=pl.ANY)],
-        out_specs=(vmem(),) * 3,
+        functools.partial(load_kernel, turned),
+        out_shape=[jax.ShapeDtypeStruct(shape, weights[0].dtype) for shape in shapes],
+        in_specs=[pl.BlockSpec(memory_space=pltpu.HBM)] * len(weights) + [pl.BlockSpec(memory_space=pl.ANY)],
+        out_specs=[vmem()] * len(weights),
         scratch_shapes=[
-            pltpu.VMEM((2, units, features), gate_w.dtype),
-            pltpu.SemaphoreType.DMA((2, TURNS)),
-            pltpu.SemaphoreType.DMA,
+            pltpu.VMEM(weights[0].shape, weights[0].dtype),
+            pltpu.SemaphoreType.DMA((TURNS + 1,)),
         ],
-        cost_estimate=pl.CostEstimate(flops=0, bytes_accessed=6 * units * features, transcendentals=0),
-        compiler_params=pltpu.CompilerParams(vmem_limit_bytes=24 << 20),
-    )(*(pltpu.with_memory_space_constraint(w, pltpu.HBM) for w in (gate_w, up_w, down_w)), after)
+        cost_estimate=pl.CostEstimate(flops=0, bytes_accessed=4 * size, transcendentals=0),
+        compiler_params=pltpu.CompilerParams(vmem_limit_bytes=16 << 20),
+    )(*(pltpu.with_memory_space_constraint(w, pltpu.HBM) for w in weights), after)
 
 
 def hidden_kernel(start, last, *refs):
@@ -182,11 +189,13 @@
             away.append(swap(jnp.concatenate([tokens] + away), masks))
         away = jnp.concatenate(away)
         near = [swap(tokens, m) for m in square]
-        away, sign_pattern = lax.optimization_barrier((away, sign_pattern))
+        gate_w = pltpu.with_memory_space_constraint(gate_weight.T, pltpu.HBM)
+        (gate_w,) = load((gate_w,), (True,), gate_w)
+        away, gate_w = lax.optimization_barrier((away, gate_w))
         there = [swap(away, m) for m in square[:2]]
         away, near[0] = lax.optimization_barrier((away, near[0]))
         there.append(swap(away, square[2]))
-        gate_w, up_w, down_w = load(gate_weight.T, up_weight.T, down_weight, away)
+        up_w, down_w = load((up_weight.T, down_weight), (True, False), away)
         there[0], *near = lax.optimization_barrier((there[0], *near))
         early = jnp.concatenate([near[1], near[0], near[2], away, there[0], tokens])
         early_there = swap(early, (1, 1))

time: 44.8 us -> 44.8 us (level)
  Pallas kernels: 7.51 us -> 9.02 us
  waiting for transfers between devices: 16.1 us -> 14.6 us
    pallas_call x1 -> x2, Pallas kernels: 4.46 us -> 5.96 us  [load(): pl.pallas_call(functools.partial(load_kernel, turned), out_shape=[jax.Sha...]
    ppermute x19, waiting for transfers between devices: 16.1 us -> 14.6 us  [swap(): lax.ppermute(value, 'gx', [(i, i ^ masks[i % 2]) for i in range(members)])]
  transfers between devices with their start and end apart: 19 -> 19, of which waited for: 9 -> 10; matrix products, arithmetic and copies ran while one was open for 1% -> 1% of each run, Pallas kernels for 12% -> 15%
where the time goes in v27:
time: 44.8 us; the launch traced here: 44.7 us
  starting transfers between devices  20.2 us (45%)
  waiting for transfers between devices  14.6 us (33%)
  Pallas kernels  9.02 us (20%)
    ppermute x19, starting transfers between devices, swap(): lax.ppermute(value, 'gx', [(i, i ^ masks[i % 2]) for i in range(members)])  20.2 us
    ppermute x19, waiting for transfers between devices, swap(): lax.ppermute(value, 'gx', [(i, i ^ masks[i % 2]) for i in range(members)])  14.6 us
    pallas_call x2, Pallas kernels, load(): pl.pallas_call(functools.partial(load_kernel, turned), out_shape=[jax.Sha...  5.96 us
    pallas_call x2, Pallas kernels, hidden_units(): pl.pallas_call(functools.partial(hidden_kernel, start, last), out_shape=(...  1.45 us
    pallas_call x1, Pallas kernels, rotate(): pl.pallas_call(functools.partial(rotate_kernel, len(arrived)), out_shape=...  0.9 us
  transfers between devices with their start and end apart: 19, of which 10 were waited for; matrix products, arithmetic and copies ran while one was open for 1% of the time, Pallas kernels for 15%

profile of v27, /device:TPU:0, one launch (start us, length us, event | category | flops | bytes accessed | tf_op | source)
XLA Modules:
  0.0 44.7 jit_solution(2230995969194973028)
XLA Ops:
  0.0 4.0 %collective-permute-start = (bf16[8,8192]{1,0:T(8,128)(2,1)}, bf16[8,8192]{1,0:T(8,128)(2,1)S(1)}, u32[]{:S(2)}, u32[]{:S(2)}) collective-permute-start(bf16[8,8192]{1,0:T(8,128)(2,1)} %param.5), channel_id=1, source_target_pairs={{0,8},{1,9},{2,10},{3,11},{4,12},{5,13},{6,14},{7,15},{8,0},{9,1},... | collective-permute-start | bytes 393224 | tf_op jit(solution)/shard_map/ppermute | solution.py:182
  4.0 1.6 %collective-permute-start.1 = (bf16[8,8192]{1,0:T(8,128)(2,1)}, bf16[8,8192]{1,0:T(8,128)(2,1)S(1)}, u32[]{:S(2)}, u32[]{:S(2)}) collective-permute-start(bf16[8,8192]{1,0:T(8,128)(2,1)} %param.5), channel_id=1, source_target_pairs={{0,4},{1,3},{2,6},{3,1},{4,0},{5,7},{6,2},{7,5},{8,12},{9,11},{10,... | collective-permute-start | bytes 393224 | tf_op jit(solution)/shard_map/ppermute | solution.py:182
  5.6 1.5 %collective-permute-start.3 = (bf16[8,8192]{1,0:T(8,128)(2,1)}, bf16[8,8192]{1,0:T(8,128)(2,1)S(1)}, u32[]{:S(2)}, u32[]{:S(2)}) collective-permute-start(bf16[8,8192]{1,0:T(8,128)(2,1)} %param.5), channel_id=1, source_target_pairs={{0,2},{1,5},{2,0},{3,7},{4,6},{5,1},{6,4},{7,3},{8,10},{9,13},{10,... | collective-permute-start | bytes 393224 | tf_op jit(solution)/shard_map/ppermute | solution.py:182
  7.1 0.4 collective-permute-start.4
  7.5 2.7 %shard_map.55.refs_0_ = bf16[8192,224]{1,0:T(8,128)(2,1)S(1)} custom-call(bf16[224,8192]{1,0:T(8,128)(2,1)} %bitcast.4, bf16[224,8192]{1,0:T(8,128)(2,1)} %bitcast.5), custom_call_target="tpu_custom_call" | custom-call | bytes 7340032 | tf_op jit(solution)/shard_map/pallas_call | solution.py:52
  10.2 0.5 %collective-permute-done.refs_2_ = bf16[8,8192]{1,0:T(8,128)(2,1)S(1)} collective-permute-done((bf16[8,8192]{1,0:T(8,128)(2,1)}, bf16[8,8192]{1,0:T(8,128)(2,1)S(1)}, u32[]{:S(2)}, u32[]{:S(2)}) %collective-permute-start) | collective-permute-done | bytes 131104 | tf_op jit(solution)/shard_map/ppermute | solution.py:182
  10.7 1.2 %collective-permute-start.2 = (bf16[8,8192]{1,0:T(8,128)(2,1)S(1)}, bf16[8,8192]{1,0:T(8,128)(2,1)S(1)}, u32[]{:S(2)}, u32[]{:S(2)}) collective-permute-start(bf16[8,8192]{1,0:T(8,128)(2,1)S(1)} %collective-permute-done.refs_2_), channel_id=1, source_target_pairs={{0,4},{1,3},{2,6},{3,1},{4,0},{5,7},{6,2},{7,5},{8,12},{9,11},{10,... | collective-permute-start | bytes 393224 | tf_op jit(solution)/shard_map/ppermute | solution.py:182
  11.9 1.5 %collective-permute-start.5 = (bf16[8,8192]{1,0:T(8,128)(2,1)S(1)}, bf16[8,8192]{1,0:T(8,128)(2,1)S(1)}, u32[]{:S(2)}, u32[]{:S(2)}) collective-permute-start(bf16[8,8192]{1,0:T(8,128)(2,1)S(1)} %collective-permute-done.refs_2_), channel_id=1, source_target_pairs={{0,2},{1,5},{2,0},{3,7},{4,6},{5,1},{6,4},{7,3},{8,10},{9,13},{10,... | collective-permute-start | bytes 393224 | tf_op jit(solution)/shard_map/ppermute | solution.py:182
  13.4 0.0 collective-permute-done.1
  13.4 1.0 %collective-permute-start.6 = (bf16[8,8192]{1,0:T(8,128)(2,1)S(1)}, bf16[8,8192]{1,0:T(8,128)(2,1)S(1)}, u32[]{:S(2)}, u32[]{:S(2)}) collective-permute-start(bf16[8,8192]{1,0:T(8,128)(2,1)S(1)} %collective-permute-done.refs_2_), channel_id=1, source_target_pairs={{0,6},{1,7},{2,4},{3,5},{4,2},{5,3},{6,0},{7,1},{8,14},{9,15},{10,... | collective-permute-start | bytes 393224 | tf_op jit(solution)/shard_map/ppermute | solution.py:182
  14.4 0.0 copy-start.1
  14.4 3.3 %shard_map.56 = (bf16[8192,224]{1,0:T(8,128)(2,1)S(1)}, bf16[224,8192]{1,0:T(8,128)(2,1)S(1)}) custom-call(bf16[224,8192]{1,0:T(8,128)(2,1)} %bitcast.6, bf16[224,8192]{1,0:T(8,128)(2,1)} %refs_1_.1, bf16[8,8192]{1,0:T(8,128)(2,1)S(1)} %collective-permute-done.refs_2_), custom_call_target="tpu_custom_call" | custom-call | bytes 14680064 | tf_op jit(solution)/shard_map/pallas_call | solution.py:52
  17.7 0.0 collective-permute-done.3
  17.7 0.0 collective-permute-done.4
  17.7 0.2 collective-permute-done.2
  18.0 0.0 copy-done.1
  18.0 0.1 collective-permute-start.7
  18.1 2.4 %collective-permute-done.6 = bf16[8,8192]{1,0:T(8,128)(2,1)S(1)} collective-permute-done((bf16[8,8192]{1,0:T(8,128)(2,1)S(1)}, bf16[8,8192]{1,0:T(8,128)(2,1)S(1)}, u32[]{:S(2)}, u32[]{:S(2)}) %collective-permute-start.6) | collective-permute-done | bytes 131104 | tf_op jit(solution)/shard_map/ppermute | solution.py:182
  20.5 0.0 collective-permute-done.5
  20.6 0.1 collective-permute-start.9
  20.7 0.6 %collective-permute-start.8 = (bf16[16,4096]{1,0:T(8,128)(2,1)S(1)}, bf16[16,4096]{1,0:T(8,128)(2,1)S(1)}, u32[]{:S(2)}, u32[]{:S(2)}) collective-permute-start(bf16[16,4096]{1,0:T(8,128)(2,1)S(1)} %pad_maximum_fusion.refs_4_), channel_id=1, source_target_pairs={{0,1},{1,0},{2,3},{3,2},{4,5},{5,4},{6,7},{7,6},{8,9},{9,8},{10,11... | collective-permute-start | bytes 393224 | tf_op jit(solution)/shard_map/ppermute | solution.py:182
  21.2 0.8 %collective-permute-done.9.refs_5_ = bf16[16,4096]{1,0:T(8,128)(2,1)S(1)} collective-permute-done((bf16[16,4096]{1,0:T(8,128)(2,1)S(1)}, bf16[16,4096]{1,0:T(8,128)(2,1)S(1)}, u32[]{:S(2)}, u32[]{:S(2)}) %collective-permute-start.9) | collective-permute-done | bytes 131104 | tf_op jit(solution)/shard_map/ppermute | solution.py:182
  22.0 0.0 collective-permute-done.7.refs_3_
  22.0 0.7 %shard_map.57 = (f32[128,224]{1,0:T(8,128)S(1)}, f32[128,224]{1,0:T(8,128)S(1)}) custom-call(bf16[8192,224]{1,0:T(8,128)(2,1)S(1)} %shard_map.55.refs_0_, bf16[8192,224]{1,0:T(8,128)(2,1)S(1)} %get-tuple-element.40.refs_1_, bf16[48,8192]{1,0:T(8,128)(2,1)S(1)} %constant_dynamic-update-slice_fusion.refs_2_, ...), custom_call_target="tpu_custom_call" | custom-call | flops 469762048 | bytes 3670016 | tf_op jit(solution)/shard_map/pallas_call | solution.py:91
  22.7 0.0 collective-permute-done.8.refs_5_
  22.7 0.7 %shard_map.58.hidden_ref = bf16[128,224]{1,0:T(8,128)(2,1)S(1)} custom-call(bf16[8192,224]{1,0:T(8,128)(2,1)S(1)} %shard_map.55.refs_0_, bf16[8192,224]{1,0:T(8,128)(2,1)S(1)} %get-tuple-element.40.refs_1_, bf16[48,8192]{1,0:T(8,128)(2,1)S(1)} %constant_dynamic-update-slice_fusion.refs_2_, bf16[48,8192]{1,0:T(8,128)(2,1)S(1)} %collective-permute-done.7.refs_3_, ...), custom_call_target="tpu_custom_call" | custom-call | flops 469762048 | bytes 3670016 | tf_op jit(solution)/shard_map/pallas_call | solution.py:91
  23.4 0.7 %shard_map.59 = (f32[32,8192]{1,0:T(8,128)S(1)}, f32[8,8192]{1,0:T(8,128)S(1)}, f32[24,8192]{1,0:T(8,128)S(1)}, bf16[32,8192]{1,0:T(8,128)(2,1)S(1)}, bf16[8,819...) custom-call(bf16[128,224]{1,0:T(8,128)(2,1)S(1)} %shard_map.58.hidden_ref, bf16[224,8192]{1,0:T(8,128)(2,1)S(1)} %get-tuple-element.46.down_ref), custom_call_target="tpu_custom_call" | custom-call | flops 469762048 | bytes 3670016 | tf_op jit(solution)/shard_map/pallas_call | solution.py:120
  24.2 0.2 collective-permute-start.13
  24.4 0.4 collective-permute-start.10
  24.7 0.8 %collective-permute-done.13 = bf16[8,8192]{1,0:T(8,128)(2,1)S(1)} collective-permute-done((bf16[8,8192]{1,0:T(8,128)(2,1)S(1)}, bf16[8,8192]{1,0:T(8,128)(2,1)S(1)}, u32[]{:S(2)}, u32[]{:S(2)}) %collective-permute-start.13) | collective-permute-done | bytes 131104 | tf_op jit(solution)/shard_map/ppermute | solution.py:182
  25.6 1.4 %collective-permute-start.14 = (bf16[8,8192]{1,0:T(8,128)(2,1)S(1)}, bf16[8,8192]{1,0:T(8,128)(2,1)S(1)}, u32[]{:S(2)}, u32[]{:S(2)}) collective-permute-start(bf16[8,8192]{1,0:T(8,128)(2,1)S(1)} %add_convert_fusion), channel_id=1, source_target_pairs={{0,6},{1,7},{2,4},{3,5},{4,2},{5,3},{6,0},{7,1},{8,14},{9,15},{10,... | collective-permute-start | bytes 393224 | tf_op jit(solution)/shard_map/ppermute | solution.py:182
  27.0 0.0 collective-permute-done.10
  27.0 0.0 collective-permute-start.11
  27.0 0.1 fusion.7
  27.0 0.0 copy-start
  27.1 1.8 %collective-permute-start.15 = (bf16[8,8192]{1,0:T(8,128)(2,1)S(1)}, bf16[8,8192]{1,0:T(8,128)(2,1)S(1)}, u32[]{:S(2)}, u32[]{:S(2)}) collective-permute-start(bf16[8,8192]{1,0:T(8,128)(2,1)S(1)} %get-tuple-element.57), channel_id=1, source_target_pairs={{0,4},{1,3},{2,6},{3,1},{4,0},{5,7},{6,2},{7,5},{8,12},{9,11},{10,... | collective-permute-start | bytes 393224 | tf_op jit(solution)/shard_map/ppermute | solution.py:182
  28.8 0.5 %collective-permute-start.16 = (bf16[8,8192]{1,0:T(8,128)(2,1)S(1)}, bf16[8,8192]{1,0:T(8,128)(2,1)S(1)}, u32[]{:S(2)}, u32[]{:S(2)}) collective-permute-start(bf16[8,8192]{1,0:T(8,128)(2,1)S(1)} %get-tuple-element.58), channel_id=1, source_target_pairs={{0,2},{1,5},{2,0},{3,7},{4,6},{5,1},{6,4},{7,3},{8,10},{9,13},{10,... | collective-permute-start | bytes 393224 | tf_op jit(solution)/shard_map/ppermute | solution.py:182
  29.4 0.0 collective-permute-done.11
  29.4 0.1 convert_add_fusion
  29.5 1.3 %collective-permute-start.12 = (bf16[16,8192]{1,0:T(8,128)(2,1)S(1)}, bf16[16,8192]{1,0:T(8,128)(2,1)S(1)}, u32[]{:S(2)}, u32[]{:S(2)}) collective-permute-start(bf16[16,8192]{1,0:T(8,128)(2,1)S(1)} %slice.67), channel_id=1, source_target_pairs={{0,4},{1,3},{2,6},{3,1},{4,0},{5,7},{6,2},{7,5},{8,12},{9,11},{10,... | collective-permute-start | bytes 786440 | tf_op jit(solution)/shard_map/ppermute | solution.py:182
  30.8 2.0 %collective-permute-done.14 = bf16[8,8192]{1,0:T(8,128)(2,1)S(1)} collective-permute-done((bf16[8,8192]{1,0:T(8,128)(2,1)S(1)}, bf16[8,8192]{1,0:T(8,128)(2,1)S(1)}, u32[]{:S(2)}, u32[]{:S(2)}) %collective-permute-start.14) | collective-permute-done | bytes 131104 | tf_op jit(solution)/shard_map/ppermute | solution.py:182
  32.8 2.2 %collective-permute-done.15 = bf16[8,8192]{1,0:T(8,128)(2,1)S(1)} collective-permute-done((bf16[8,8192]{1,0:T(8,128)(2,1)S(1)}, bf16[8,8192]{1,0:T(8,128)(2,1)S(1)}, u32[]{:S(2)}, u32[]{:S(2)}) %collective-permute-start.15) | collective-permute-done | bytes 131104 | tf_op jit(solution)/shard_map/ppermute | solution.py:182
  35.0 0.5 %collective-permute-done.16 = bf16[8,8192]{1,0:T(8,128)(2,1)S(1)} collective-permute-done((bf16[8,8192]{1,0:T(8,128)(2,1)S(1)}, bf16[8,8192]{1,0:T(8,128)(2,1)S(1)}, u32[]{:S(2)}, u32[]{:S(2)}) %collective-permute-start.16) | collective-permute-done | bytes 131104 | tf_op jit(solution)/shard_map/ppermute | solution.py:182
  35.5 0.1 fusion.2
  35.5 1.8 %collective-permute-start.17 = (bf16[8,8192]{1,0:T(8,128)(2,1)S(1)}, bf16[8,8192]{1,0:T(8,128)(2,1)S(1)}, u32[]{:S(2)}, u32[]{:S(2)}) collective-permute-start(bf16[8,8192]{1,0:T(8,128)(2,1)S(1)} %fusion.2), channel_id=1, source_target_pairs={{0,8},{1,9},{2,10},{3,11},{4,12},{5,13},{6,14},{7,15},{8,0},{9,1},... | collective-permute-start | bytes 393224 | tf_op jit(solution)/shard_map/ppermute | solution.py:182
  37.4 0.4 collective-permute-done.12
  37.8 0.1 slice_add_fusion
  37.9 1.0 %collective-permute-start.18 = (bf16[8,8192]{1,0:T(8,128)(2,1)S(1)}, bf16[8,8192]{1,0:T(8,128)(2,1)S(1)}, u32[]{:S(2)}, u32[]{:S(2)}) collective-permute-start(bf16[8,8192]{1,0:T(8,128)(2,1)S(1)} %slice.68), channel_id=1, source_target_pairs={{0,2},{1,5},{2,0},{3,7},{4,6},{5,1},{6,4},{7,3},{8,10},{9,13},{10,... | collective-permute-start | bytes 393224 | tf_op jit(solution)/shard_map/ppermute | solution.py:182
  38.9 4.8 %collective-permute-done.17.refs_1_ = bf16[8,8192]{1,0:T(8,128)(2,1)S(1)} collective-permute-done((bf16[8,8192]{1,0:T(8,128)(2,1)S(1)}, bf16[8,8192]{1,0:T(8,128)(2,1)S(1)}, u32[]{:S(2)}, u32[]{:S(2)}) %collective-permute-start.17) | collective-permute-done | bytes 131104 | tf_op jit(solution)/shard_map/ppermute | solution.py:182
  43.8 0.0 collective-permute-done.18.refs_2_
  43.8 0.0 copy-done
  43.8 0.9 %shard_map.60 = bf16[8,8192]{1,0:T(8,128)(2,1)} custom-call(f32[8,8192]{1,0:T(8,128)S(1)} %slice.52.refs_0_, bf16[8,8192]{1,0:T(8,128)(2,1)S(1)} %collective-permute-done.17.refs_1_, bf16[8,8192]{1,0:T(8,128)(2,1)S(1)} %collective-permute-done.18.refs_2_, s32[1,8192]{1,0:T(1,128)S(1)} %bitcast.3, bf16[256,128]{1,0:T(8,128)(2,1)S(1)} %pad_maximum_fusion.2.refs_4_), custom_call_target="tpu_custom_call" | custom-call | tf_op jit(solution)/shard_map/pallas_call | solution.py:160
  (16 shorter events, 0.3 us)
Async XLA Ops:
  0.0 10.7 %collective-permute-start = (bf16[8,8192]{1,0:T(8,128)(2,1)}, bf16[8,8192]{1,0:T(8,128)(2,1)S(1)}, u32[]{:S(2)}, u32[]{:S(2)}) collective-permute-start(bf16[8,8192]{1,0:T(8,128)(2,1)} %param.5), channel_id=1, source_target_pairs={{0,8},{1,9},{2,10},{3,11},{4,12},{5,13},{6,14},{7,15},{8,0},{9,1},... | collective-permute-start | bytes 393224 | tf_op jit(solution)/shard_map/ppermute | solution.py:182
  4.0 9.3 %collective-permute-start.1 = (bf16[8,8192]{1,0:T(8,128)(2,1)}, bf16[8,8192]{1,0:T(8,128)(2,1)S(1)}, u32[]{:S(2)}, u32[]{:S(2)}) collective-permute-start(bf16[8,8192]{1,0:T(8,128)(2,1)} %param.5), channel_id=1, source_target_pairs={{0,4},{1,3},{2,6},{3,1},{4,0},{5,7},{6,2},{7,5},{8,12},{9,11},{10,... | collective-permute-start | bytes 393224 | tf_op jit(solution)/shard_map/ppermute | solution.py:182
  5.6 12.1 %collective-permute-start.3 = (bf16[8,8192]{1,0:T(8,128)(2,1)}, bf16[8,8192]{1,0:T(8,128)(2,1)S(1)}, u32[]{:S(2)}, u32[]{:S(2)}) collective-permute-start(bf16[8,8192]{1,0:T(8,128)(2,1)} %param.5), channel_id=1, source_target_pairs={{0,2},{1,5},{2,0},{3,7},{4,6},{5,1},{6,4},{7,3},{8,10},{9,13},{10,... | collective-permute-start | bytes 393224 | tf_op jit(solution)/shard_map/ppermute | solution.py:182
  7.1 10.6 %collective-permute-start.4 = (bf16[8,8192]{1,0:T(8,128)(2,1)}, bf16[8,8192]{1,0:T(8,128)(2,1)S(1)}, u32[]{:S(2)}, u32[]{:S(2)}) collective-permute-start(bf16[8,8192]{1,0:T(8,128)(2,1)} %param.5), channel_id=1, source_target_pairs={{0,6},{1,7},{2,4},{3,5},{4,2},{5,3},{6,0},{7,1},{8,14},{9,15},{10,... | collective-permute-start | bytes 393224 | tf_op jit(solution)/shard_map/ppermute | solution.py:182
  10.7 7.3 %collective-permute-start.2 = (bf16[8,8192]{1,0:T(8,128)(2,1)S(1)}, bf16[8,8192]{1,0:T(8,128)(2,1)S(1)}, u32[]{:S(2)}, u32[]{:S(2)}) collective-permute-start(bf16[8,8192]{1,0:T(8,128)(2,1)S(1)} %collective-permute-done.refs_2_), channel_id=1, source_target_pairs={{0,4},{1,3},{2,6},{3,1},{4,0},{5,7},{6,2},{7,5},{8,12},{9,11},{10,... | collective-permute-start | bytes 393224 | tf_op jit(solution)/shard_map/ppermute | solution.py:182
  11.9 8.7 %collective-permute-start.5 = (bf16[8,8192]{1,0:T(8,128)(2,1)S(1)}, bf16[8,8192]{1,0:T(8,128)(2,1)S(1)}, u32[]{:S(2)}, u32[]{:S(2)}) collective-permute-start(bf16[8,8192]{1,0:T(8,128)(2,1)S(1)} %collective-permute-done.refs_2_), channel_id=1, source_target_pairs={{0,2},{1,5},{2,0},{3,7},{4,6},{5,1},{6,4},{7,3},{8,10},{9,13},{10,... | collective-permute-start | bytes 393224 | tf_op jit(solution)/shard_map/ppermute | solution.py:182
  13.4 7.1 %collective-permute-start.6 = (bf16[8,8192]{1,0:T(8,128)(2,1)S(1)}, bf16[8,8192]{1,0:T(8,128)(2,1)S(1)}, u32[]{:S(2)}, u32[]{:S(2)}) collective-permute-start(bf16[8,8192]{1,0:T(8,128)(2,1)S(1)} %collective-permute-done.refs_2_), channel_id=1, source_target_pairs={{0,6},{1,7},{2,4},{3,5},{4,2},{5,3},{6,0},{7,1},{8,14},{9,15},{10,... | collective-permute-start | bytes 393224 | tf_op jit(solution)/shard_map/ppermute | solution.py:182
  14.4 3.6 %copy-start.1 = (bf16[8,8192]{1,0:T(8,128)(2,1)S(1)}, bf16[8,8192]{1,0:T(8,128)(2,1)}, u32[]{:S(2)}) copy-start(bf16[8,8192]{1,0:T(8,128)(2,1)} %param.5) | copy-start | bytes 393220
  18.0 3.9 %collective-permute-start.7 = (bf16[48,8192]{1,0:T(8,128)(2,1)S(1)}, bf16[48,8192]{1,0:T(8,128)(2,1)S(1)}, u32[]{:S(2)}, u32[]{:S(2)}) collective-permute-start(bf16[48,8192]{1,0:T(8,128)(2,1)S(1)} %constant_dynamic-update-slice_fusion.refs_2_), channel_id=1, source_target_pairs={{0,1},{1,0},{2,3},{3,2},{4,5},{5,4},{6,7},{7,6},{8,9},{9,8},{10,11... | collective-permute-start | bytes 2359304 | tf_op jit(solution)/shard_map/ppermute | solution.py:182
  20.6 1.4 %collective-permute-start.9 = (bf16[16,4096]{1,0:T(8,128)(2,1)S(1)}, bf16[16,4096]{1,0:T(8,128)(2,1)S(1)}, u32[]{:S(2)}, u32[]{:S(2)}) collective-permute-start(bf16[16,4096]{1,0:T(8,128)(2,1)S(1)} %pad_maximum_fusion.1.refs_4_), channel_id=1, source_target_pairs={{0,1},{1,0},{2,3},{3,2},{4,5},{5,4},{6,7},{7,6},{8,9},{9,8},{10,11... | collective-permute-start | bytes 393224 | tf_op jit(solution)/shard_map/ppermute | solution.py:182
  20.7 2.0 %collective-permute-start.8 = (bf16[16,4096]{1,0:T(8,128)(2,1)S(1)}, bf16[16,4096]{1,0:T(8,128)(2,1)S(1)}, u32[]{:S(2)}, u32[]{:S(2)}) collective-permute-start(bf16[16,4096]{1,0:T(8,128)(2,1)S(1)} %pad_maximum_fusion.refs_4_), channel_id=1, source_target_pairs={{0,1},{1,0},{2,3},{3,2},{4,5},{5,4},{6,7},{7,6},{8,9},{9,8},{10,11... | collective-permute-start | bytes 393224 | tf_op jit(solution)/shard_map/ppermute | solution.py:182
  24.2 1.4 %collective-permute-start.13 = (bf16[8,8192]{1,0:T(8,128)(2,1)S(1)}, bf16[8,8192]{1,0:T(8,128)(2,1)S(1)}, u32[]{:S(2)}, u32[]{:S(2)}) collective-permute-start(bf16[8,8192]{1,0:T(8,128)(2,1)S(1)} %get-tuple-element.54), channel_id=1, source_target_pairs={{0,1},{1,0},{2,3},{3,2},{4,5},{5,4},{6,7},{7,6},{8,9},{9,8},{10,11... | collective-permute-start | bytes 393224 | tf_op jit(solution)/shard_map/ppermute | solution.py:182
  24.4 2.6 %collective-permute-start.10 = (bf16[24,8192]{1,0:T(8,128)(2,1)S(1)}, bf16[24,8192]{1,0:T(8,128)(2,1)S(1)}, u32[]{:S(2)}, u32[]{:S(2)}) collective-permute-start(bf16[24,8192]{1,0:T(8,128)(2,1)S(1)} %get-tuple-element.48), channel_id=1, source_target_pairs={{0,1},{1,0},{2,3},{3,2},{4,5},{5,4},{6,7},{7,6},{8,9},{9,8},{10,11... | collective-permute-start | bytes 1179656 | tf_op jit(solution)/shard_map/ppermute | solution.py:182
  25.6 7.2 %collective-permute-start.14 = (bf16[8,8192]{1,0:T(8,128)(2,1)S(1)}, bf16[8,8192]{1,0:T(8,128)(2,1)S(1)}, u32[]{:S(2)}, u32[]{:S(2)}) collective-permute-start(bf16[8,8192]{1,0:T(8,128)(2,1)S(1)} %add_convert_fusion), channel_id=1, source_target_pairs={{0,6},{1,7},{2,4},{3,5},{4,2},{5,3},{6,0},{7,1},{8,14},{9,15},{10,... | collective-permute-start | bytes 393224 | tf_op jit(solution)/shard_map/ppermute | solution.py:182
  27.0 2.4 %collective-permute-start.11 = (bf16[32,8192]{1,0:T(8,128)(2,1)S(1)}, bf16[32,8192]{1,0:T(8,128)(2,1)S(1)}, u32[]{:S(2)}, u32[]{:S(2)}) collective-permute-start(bf16[32,8192]{1,0:T(8,128)(2,1)S(1)} %get-tuple-element.50), channel_id=1, source_target_pairs={{0,1},{1,0},{2,3},{3,2},{4,5},{5,4},{6,7},{7,6},{8,9},{9,8},{10,11... | collective-permute-start | bytes 1572872 | tf_op jit(solution)/shard_map/ppermute | solution.py:182
  27.0 16.7 %copy-start = (s32[8192]{0:T(1024)S(1)}, s32[8192]{0:T(1024)}, u32[]{:S(2)}) copy-start(s32[8192]{0:T(1024)} %param.9) | copy-start | bytes 98308
  27.1 7.9 %collective-permute-start.15 = (bf16[8,8192]{1,0:T(8,128)(2,1)S(1)}, bf16[8,8192]{1,0:T(8,128)(2,1)S(1)}, u32[]{:S(2)}, u32[]{:S(2)}) collective-permute-start(bf16[8,8192]{1,0:T(8,128)(2,1)S(1)} %get-tuple-element.57), channel_id=1, source_target_pairs={{0,4},{1,3},{2,6},{3,1},{4,0},{5,7},{6,2},{7,5},{8,12},{9,11},{10,... | collective-permute-start | bytes 393224 | tf_op jit(solution)/shard_map/ppermute | solution.py:182
  28.8 6.6 %collective-permute-start.16 = (bf16[8,8192]{1,0:T(8,128)(2,1)S(1)}, bf16[8,8192]{1,0:T(8,128)(2,1)S(1)}, u32[]{:S(2)}, u32[]{:S(2)}) collective-permute-start(bf16[8,8192]{1,0:T(8,128)(2,1)S(1)} %get-tuple-element.58), channel_id=1, source_target_pairs={{0,2},{1,5},{2,0},{3,7},{4,6},{5,1},{6,4},{7,3},{8,10},{9,13},{10,... | collective-permute-start | bytes 393224 | tf_op jit(solution)/shard_map/ppermute | solution.py:182
  29.5 8.3 %collective-permute-start.12 = (bf16[16,8192]{1,0:T(8,128)(2,1)S(1)}, bf16[16,8192]{1,0:T(8,128)(2,1)S(1)}, u32[]{:S(2)}, u32[]{:S(2)}) collective-permute-start(bf16[16,8192]{1,0:T(8,128)(2,1)S(1)} %slice.67), channel_id=1, source_target_pairs={{0,4},{1,3},{2,6},{3,1},{4,0},{5,7},{6,2},{7,5},{8,12},{9,11},{10,... | collective-permute-start | bytes 786440 | tf_op jit(solution)/shard_map/ppermute | solution.py:182
  35.5 8.2 %collective-permute-start.17 = (bf16[8,8192]{1,0:T(8,128)(2,1)S(1)}, bf16[8,8192]{1,0:T(8,128)(2,1)S(1)}, u32[]{:S(2)}, u32[]{:S(2)}) collective-permute-start(bf16[8,8192]{1,0:T(8,128)(2,1)S(1)} %fusion.2), channel_id=1, source_target_pairs={{0,8},{1,9},{2,10},{3,11},{4,12},{5,13},{6,14},{7,15},{8,0},{9,1},... | collective-permute-start | bytes 393224 | tf_op jit(solution)/shard_map/ppermute | solution.py:182
  37.9 5.9 %collective-permute-start.18 = (bf16[8,8192]{1,0:T(8,128)(2,1)S(1)}, bf16[8,8192]{1,0:T(8,128)(2,1)S(1)}, u32[]{:S(2)}, u32[]{:S(2)}) collective-permute-start(bf16[8,8192]{1,0:T(8,128)(2,1)S(1)} %slice.68), channel_id=1, source_target_pairs={{0,2},{1,5},{2,0},{3,7},{4,6},{5,1},{6,4},{7,3},{8,10},{9,13},{10,... | collective-permute-start | bytes 393224 | tf_op jit(solution)/shard_map/ppermute | solution.py:182

commit v28 on v27

--- a/solution.py
+++ b/solution.py
@@ -173,9 +173,10 @@
     square = ((4, 2), (2, 4), (6, 6))
     far = []
     mask = members // 2
-    while mask > 4:
+    while mask > 8:
         far.append((mask, mask))
         mask //= 2
+    far.append((8, 12))
     others = members // 8 - 1
 
     def swap(value, masks):

time: 44.8 us -> 46 us (1.027)
  waiting for transfers between devices: 14.6 us -> 15.8 us
    ppermute x19, waiting for transfers between devices: 14.6 us -> 15.8 us  [swap(): lax.ppermute(value, 'gx', [(i, i ^ masks[i % 2]) for i in range(members)])]
  transfers between devices with their start and end apart: 19 -> 19, of which waited for: 10 -> 9; matrix products, arithmetic and copies ran while one was open for 1% -> 1% of each run, Pallas kernels for 15% -> 15%
where the time goes in v28:
time: 46 us; the launch traced here: 45.9 us
  starting transfers between devices  20.2 us (44%)
  waiting for transfers between devices  15.8 us (34%)
  Pallas kernels  9.02 us (20%)
    ppermute x19, starting transfers between devices, swap(): lax.ppermute(value, 'gx', [(i, i ^ masks[i % 2]) for i in range(members)])  20.2 us
    ppermute x19, waiting for transfers between devices, swap(): lax.ppermute(value, 'gx', [(i, i ^ masks[i % 2]) for i in range(members)])  15.8 us
    pallas_call x2, Pallas kernels, load(): pl.pallas_call(functools.partial(load_kernel, turned), out_shape=[jax.Sha...  5.96 us
    pallas_call x2, Pallas kernels, hidden_units(): pl.pallas_call(functools.partial(hidden_kernel, start, last), out_shape=(...  1.45 us
  transfers between devices with their start and end apart: 19, of which 9 were waited for; matrix products, arithmetic and copies ran while one was open for 1% of the time, Pallas kernels for 15%

profile of v28, /device:TPU:0, one launch (start us, length us, event | category | flops | bytes accessed | tf_op | source)
XLA Modules:
  0.0 45.9 jit_solution(3862864673600734134)
XLA Ops:
  0.0 4.0 %collective-permute-start = (bf16[8,8192]{1,0:T(8,128)(2,1)}, bf16[8,8192]{1,0:T(8,128)(2,1)S(1)}, u32[]{:S(2)}, u32[]{:S(2)}) collective-permute-start(bf16[8,8192]{1,0:T(8,128)(2,1)} %param.5), channel_id=1, source_target_pairs={{0,8},{1,13},{2,10},{3,15},{4,12},{5,9},{6,14},{7,11},{8,0},{9,5},... | collective-permute-start | bytes 393224 | tf_op jit(solution)/shard_map/ppermute | solution.py:183
  4.0 1.6 %collective-permute-start.1 = (bf16[8,8192]{1,0:T(8,128)(2,1)}, bf16[8,8192]{1,0:T(8,128)(2,1)S(1)}, u32[]{:S(2)}, u32[]{:S(2)}) collective-permute-start(bf16[8,8192]{1,0:T(8,128)(2,1)} %param.5), channel_id=1, source_target_pairs={{0,4},{1,3},{2,6},{3,1},{4,0},{5,7},{6,2},{7,5},{8,12},{9,11},{10,... | collective-permute-start | bytes 393224 | tf_op jit(solution)/shard_map/ppermute | solution.py:183
  5.6 1.5 %collective-permute-start.3 = (bf16[8,8192]{1,0:T(8,128)(2,1)}, bf16[8,8192]{1,0:T(8,128)(2,1)S(1)}, u32[]{:S(2)}, u32[]{:S(2)}) collective-permute-start(bf16[8,8192]{1,0:T(8,128)(2,1)} %param.5), channel_id=1, source_target_pairs={{0,2},{1,5},{2,0},{3,7},{4,6},{5,1},{6,4},{7,3},{8,10},{9,13},{10,... | collective-permute-start | bytes 393224 | tf_op jit(solution)/shard_map/ppermute | solution.py:183
  7.1 0.4 collective-permute-start.4
  7.5 2.7 %shard_map.55.refs_0_ = bf16[8192,224]{1,0:T(8,128)(2,1)S(1)} custom-call(bf16[224,8192]{1,0:T(8,128)(2,1)} %bitcast.4, bf16[224,8192]{1,0:T(8,128)(2,1)} %bitcast.5), custom_call_target="tpu_custom_call" | custom-call | bytes 7340032 | tf_op jit(solution)/shard_map/pallas_call | solution.py:52
  10.2 0.6 %collective-permute-done.refs_2_ = bf16[8,8192]{1,0:T(8,128)(2,1)S(1)} collective-permute-done((bf16[8,8192]{1,0:T(8,128)(2,1)}, bf16[8,8192]{1,0:T(8,128)(2,1)S(1)}, u32[]{:S(2)}, u32[]{:S(2)}) %collective-permute-start) | collective-permute-done | bytes 131104 | tf_op jit(solution)/shard_map/ppermute | solution.py:183
  10.8 1.0 %collective-permute-start.2 = (bf16[8,8192]{1,0:T(8,128)(2,1)S(1)}, bf16[8,8192]{1,0:T(8,128)(2,1)S(1)}, u32[]{:S(2)}, u32[]{:S(2)}) collective-permute-start(bf16[8,8192]{1,0:T(8,128)(2,1)S(1)} %collective-permute-done.refs_2_), channel_id=1, source_target_pairs={{0,4},{1,3},{2,6},{3,1},{4,0},{5,7},{6,2},{7,5},{8,12},{9,11},{10,... | collective-permute-start | bytes 393224 | tf_op jit(solution)/shard_map/ppermute | solution.py:183
  11.9 1.5 %collective-permute-start.5 = (bf16[8,8192]{1,0:T(8,128)(2,1)S(1)}, bf16[8,8192]{1,0:T(8,128)(2,1)S(1)}, u32[]{:S(2)}, u32[]{:S(2)}) collective-permute-start(bf16[8,8192]{1,0:T(8,128)(2,1)S(1)} %collective-permute-done.refs_2_), channel_id=1, source_target_pairs={{0,2},{1,5},{2,0},{3,7},{4,6},{5,1},{6,4},{7,3},{8,10},{9,13},{10,... | collective-permute-start | bytes 393224 | tf_op jit(solution)/shard_map/ppermute | solution.py:183
  13.4 0.0 collective-permute-done.1
  13.4 1.0 %collective-permute-start.6 = (bf16[8,8192]{1,0:T(8,128)(2,1)S(1)}, bf16[8,8192]{1,0:T(8,128)(2,1)S(1)}, u32[]{:S(2)}, u32[]{:S(2)}) collective-permute-start(bf16[8,8192]{1,0:T(8,128)(2,1)S(1)} %collective-permute-done.refs_2_), channel_id=1, source_target_pairs={{0,6},{1,7},{2,4},{3,5},{4,2},{5,3},{6,0},{7,1},{8,14},{9,15},{10,... | collective-permute-start | bytes 393224 | tf_op jit(solution)/shard_map/ppermute | solution.py:183
  14.4 0.0 copy-start.1
  14.4 3.3 %shard_map.56 = (bf16[8192,224]{1,0:T(8,128)(2,1)S(1)}, bf16[224,8192]{1,0:T(8,128)(2,1)S(1)}) custom-call(bf16[224,8192]{1,0:T(8,128)(2,1)} %bitcast.6, bf16[224,8192]{1,0:T(8,128)(2,1)} %refs_1_.1, bf16[8,8192]{1,0:T(8,128)(2,1)S(1)} %collective-permute-done.refs_2_), custom_call_target="tpu_custom_call" | custom-call | bytes 14680064 | tf_op jit(solution)/shard_map/pallas_call | solution.py:52
  17.7 0.0 collective-permute-done.3
  17.7 0.0 collective-permute-done.4
  17.8 0.0 collective-permute-done.2
  17.9 0.0 copy-done.1
  17.9 0.3 collective-permute-start.7
  18.2 3.1 %collective-permute-done.6 = bf16[8,8192]{1,0:T(8,128)(2,1)S(1)} collective-permute-done((bf16[8,8192]{1,0:T(8,128)(2,1)S(1)}, bf16[8,8192]{1,0:T(8,128)(2,1)S(1)}, u32[]{:S(2)}, u32[]{:S(2)}) %collective-permute-start.6) | collective-permute-done | bytes 131104 | tf_op jit(solution)/shard_map/ppermute | solution.py:183
  21.3 0.0 collective-permute-done.5
  21.4 0.1 collective-permute-start.9
  21.5 0.6 %collective-permute-start.8 = (bf16[16,4096]{1,0:T(8,128)(2,1)S(1)}, bf16[16,4096]{1,0:T(8,128)(2,1)S(1)}, u32[]{:S(2)}, u32[]{:S(2)}) collective-permute-start(bf16[16,4096]{1,0:T(8,128)(2,1)S(1)} %pad_maximum_fusion.refs_4_), channel_id=1, source_target_pairs={{0,1},{1,0},{2,3},{3,2},{4,5},{5,4},{6,7},{7,6},{8,9},{9,8},{10,11... | collective-permute-start | bytes 393224 | tf_op jit(solution)/shard_map/ppermute | solution.py:183
  22.0 0.8 %collective-permute-done.9.refs_5_ = bf16[16,4096]{1,0:T(8,128)(2,1)S(1)} collective-permute-done((bf16[16,4096]{1,0:T(8,128)(2,1)S(1)}, bf16[16,4096]{1,0:T(8,128)(2,1)S(1)}, u32[]{:S(2)}, u32[]{:S(2)}) %collective-permute-start.9) | collective-permute-done | bytes 131104 | tf_op jit(solution)/shard_map/ppermute | solution.py:183
  22.8 0.0 collective-permute-done.7.refs_3_
  22.8 0.7 %shard_map.57 = (f32[128,224]{1,0:T(8,128)S(1)}, f32[128,224]{1,0:T(8,128)S(1)}) custom-call(bf16[8192,224]{1,0:T(8,128)(2,1)S(1)} %shard_map.55.refs_0_, bf16[8192,224]{1,0:T(8,128)(2,1)S(1)} %get-tuple-element.40.refs_1_, bf16[48,8192]{1,0:T(8,128)(2,1)S(1)} %constant_dynamic-update-slice_fusion.refs_2_, ...), custom_call_target="tpu_custom_call" | custom-call | flops 469762048 | bytes 3670016 | tf_op jit(solution)/shard_map/pallas_call | solution.py:91
  23.5 0.0 collective-permute-done.8.refs_5_
  23.5 0.7 %shard_map.58.hidden_ref = bf16[128,224]{1,0:T(8,128)(2,1)S(1)} custom-call(bf16[8192,224]{1,0:T(8,128)(2,1)S(1)} %shard_map.55.refs_0_, bf16[8192,224]{1,0:T(8,128)(2,1)S(1)} %get-tuple-element.40.refs_1_, bf16[48,8192]{1,0:T(8,128)(2,1)S(1)} %constant_dynamic-update-slice_fusion.refs_2_, bf16[48,8192]{1,0:T(8,128)(2,1)S(1)} %collective-permute-done.7.refs_3_, ...), custom_call_target="tpu_custom_call" | custom-call | flops 469762048 | bytes 3670016 | tf_op jit(solution)/shard_map/pallas_call | solution.py:91
  24.2 0.7 %shard_map.59 = (f32[32,8192]{1,0:T(8,128)S(1)}, f32[8,8192]{1,0:T(8,128)S(1)}, f32[24,8192]{1,0:T(8,128)S(1)}, bf16[32,8192]{1,0:T(8,128)(2,1)S(1)}, bf16[8,819...) custom-call(bf16[128,224]{1,0:T(8,128)(2,1)S(1)} %shard_map.58.hidden_ref, bf16[224,8192]{1,0:T(8,128)(2,1)S(1)} %get-tuple-element.46.down_ref), custom_call_target="tpu_custom_call" | custom-call | flops 469762048 | bytes 3670016 | tf_op jit(solution)/shard_map/pallas_call | solution.py:120
  25.0 0.2 collective-permute-start.13
  25.2 0.4 collective-permute-start.10
  25.5 0.8 %collective-permute-done.13 = bf16[8,8192]{1,0:T(8,128)(2,1)S(1)} collective-permute-done((bf16[8,8192]{1,0:T(8,128)(2,1)S(1)}, bf16[8,8192]{1,0:T(8,128)(2,1)S(1)}, u32[]{:S(2)}, u32[]{:S(2)}) %collective-permute-start.13) | collective-permute-done | bytes 131104 | tf_op jit(solution)/shard_map/ppermute | solution.py:183
  26.4 1.5 %collective-permute-start.14 = (bf16[8,8192]{1,0:T(8,128)(2,1)S(1)}, bf16[8,8192]{1,0:T(8,128)(2,1)S(1)}, u32[]{:S(2)}, u32[]{:S(2)}) collective-permute-start(bf16[8,8192]{1,0:T(8,128)(2,1)S(1)} %add_convert_fusion), channel_id=1, source_target_pairs={{0,6},{1,7},{2,4},{3,5},{4,2},{5,3},{6,0},{7,1},{8,14},{9,15},{10,... | collective-permute-start | bytes 393224 | tf_op jit(solution)/shard_map/ppermute | solution.py:183
  27.9 0.0 collective-permute-done.10
  27.9 0.0 collective-permute-start.11
  27.9 0.1 fusion.7
  28.0 0.0 copy-start
  28.0 0.9 %collective-permute-start.15 = (bf16[8,8192]{1,0:T(8,128)(2,1)S(1)}, bf16[8,8192]{1,0:T(8,128)(2,1)S(1)}, u32[]{:S(2)}, u32[]{:S(2)}) collective-permute-start(bf16[8,8192]{1,0:T(8,128)(2,1)S(1)} %get-tuple-element.57), channel_id=1, source_target_pairs={{0,4},{1,3},{2,6},{3,1},{4,0},{5,7},{6,2},{7,5},{8,12},{9,11},{10,... | collective-permute-start | bytes 393224 | tf_op jit(solution)/shard_map/ppermute | solution.py:183
  28.9 1.2 %collective-permute-start.16 = (bf16[8,8192]{1,0:T(8,128)(2,1)S(1)}, bf16[8,8192]{1,0:T(8,128)(2,1)S(1)}, u32[]{:S(2)}, u32[]{:S(2)}) collective-permute-start(bf16[8,8192]{1,0:T(8,128)(2,1)S(1)} %get-tuple-element.58), channel_id=1, source_target_pairs={{0,2},{1,5},{2,0},{3,7},{4,6},{5,1},{6,4},{7,3},{8,10},{9,13},{10,... | collective-permute-start | bytes 393224 | tf_op jit(solution)/shard_map/ppermute | solution.py:183
  30.2 0.0 collective-permute-done.11
  30.2 0.1 convert_add_fusion
  30.3 1.5 %collective-permute-start.12 = (bf16[16,8192]{1,0:T(8,128)(2,1)S(1)}, bf16[16,8192]{1,0:T(8,128)(2,1)S(1)}, u32[]{:S(2)}, u32[]{:S(2)}) collective-permute-start(bf16[16,8192]{1,0:T(8,128)(2,1)S(1)} %slice.67), channel_id=1, source_target_pairs={{0,4},{1,3},{2,6},{3,1},{4,0},{5,7},{6,2},{7,5},{8,12},{9,11},{10,... | collective-permute-start | bytes 786440 | tf_op jit(solution)/shard_map/ppermute | solution.py:183
  31.8 1.6 %collective-permute-done.14 = bf16[8,8192]{1,0:T(8,128)(2,1)S(1)} collective-permute-done((bf16[8,8192]{1,0:T(8,128)(2,1)S(1)}, bf16[8,8192]{1,0:T(8,128)(2,1)S(1)}, u32[]{:S(2)}, u32[]{:S(2)}) %collective-permute-start.14) | collective-permute-done | bytes 131104 | tf_op jit(solution)/shard_map/ppermute | solution.py:183
  33.4 0.4 collective-permute-done.15
  33.8 2.0 %collective-permute-done.16 = bf16[8,8192]{1,0:T(8,128)(2,1)S(1)} collective-permute-done((bf16[8,8192]{1,0:T(8,128)(2,1)S(1)}, bf16[8,8192]{1,0:T(8,128)(2,1)S(1)}, u32[]{:S(2)}, u32[]{:S(2)}) %collective-permute-start.16) | collective-permute-done | bytes 131104 | tf_op jit(solution)/shard_map/ppermute | solution.py:183
  35.8 0.1 fusion.2
  35.9 0.7 %collective-permute-start.17 = (bf16[8,8192]{1,0:T(8,128)(2,1)S(1)}, bf16[8,8192]{1,0:T(8,128)(2,1)S(1)}, u32[]{:S(2)}, u32[]{:S(2)}) collective-permute-start(bf16[8,8192]{1,0:T(8,128)(2,1)S(1)} %fusion.2), channel_id=1, source_target_pairs={{0,8},{1,13},{2,10},{3,15},{4,12},{5,9},{6,14},{7,11},{8,0},{9,5},... | collective-permute-start | bytes 393224 | tf_op jit(solution)/shard_map/ppermute | solution.py:183
  36.5 0.8 %collective-permute-done.12 = bf16[16,8192]{1,0:T(8,128)(2,1)S(1)} collective-permute-done((bf16[16,8192]{1,0:T(8,128)(2,1)S(1)}, bf16[16,8192]{1,0:T(8,128)(2,1)S(1)}, u32[]{:S(2)}, u32[]{:S(2)}) %collective-permute-start.12) | collective-permute-done | bytes 262176 | tf_op jit(solution)/shard_map/ppermute | solution.py:183
  37.4 0.1 slice_add_fusion
  37.5 1.8 %collective-permute-start.18 = (bf16[8,8192]{1,0:T(8,128)(2,1)S(1)}, bf16[8,8192]{1,0:T(8,128)(2,1)S(1)}, u32[]{:S(2)}, u32[]{:S(2)}) collective-permute-start(bf16[8,8192]{1,0:T(8,128)(2,1)S(1)} %slice.68), channel_id=1, source_target_pairs={{0,2},{1,5},{2,0},{3,7},{4,6},{5,1},{6,4},{7,3},{8,10},{9,13},{10,... | collective-permute-start | bytes 393224 | tf_op jit(solution)/shard_map/ppermute | solution.py:183
  39.3 5.7 %collective-permute-done.17.refs_1_ = bf16[8,8192]{1,0:T(8,128)(2,1)S(1)} collective-permute-done((bf16[8,8192]{1,0:T(8,128)(2,1)S(1)}, bf16[8,8192]{1,0:T(8,128)(2,1)S(1)}, u32[]{:S(2)}, u32[]{:S(2)}) %collective-permute-start.17) | collective-permute-done | bytes 131104 | tf_op jit(solution)/shard_map/ppermute | solution.py:183
  45.0 0.0 collective-permute-done.18.refs_2_
  45.0 0.0 copy-done
  45.0 0.9 %shard_map.60 = bf16[8,8192]{1,0:T(8,128)(2,1)} custom-call(f32[8,8192]{1,0:T(8,128)S(1)} %slice.52.refs_0_, bf16[8,8192]{1,0:T(8,128)(2,1)S(1)} %collective-permute-done.17.refs_1_, bf16[8,8192]{1,0:T(8,128)(2,1)S(1)} %collective-permute-done.18.refs_2_, s32[1,8192]{1,0:T(1,128)S(1)} %bitcast.3, bf16[256,128]{1,0:T(8,128)(2,1)S(1)} %pad_maximum_fusion.2.refs_4_), custom_call_target="tpu_custom_call" | custom-call | tf_op jit(solution)/shard_map/pallas_call | solution.py:160
  (16 shorter events, 0.3 us)
Async XLA Ops:
  0.0 10.8 %collective-permute-start = (bf16[8,8192]{1,0:T(8,128)(2,1)}, bf16[8,8192]{1,0:T(8,128)(2,1)S(1)}, u32[]{:S(2)}, u32[]{:S(2)}) collective-permute-start(bf16[8,8192]{1,0:T(8,128)(2,1)} %param.5), channel_id=1, source_target_pairs={{0,8},{1,13},{2,10},{3,15},{4,12},{5,9},{6,14},{7,11},{8,0},{9,5},... | collective-permute-start | bytes 393224 | tf_op jit(solution)/shard_map/ppermute | solution.py:183
  4.0 9.3 %collective-permute-start.1 = (bf16[8,8192]{1,0:T(8,128)(2,1)}, bf16[8,8192]{1,0:T(8,128)(2,1)S(1)}, u32[]{:S(2)}, u32[]{:S(2)}) collective-permute-start(bf16[8,8192]{1,0:T(8,128)(2,1)} %param.5), channel_id=1, source_target_pairs={{0,4},{1,3},{2,6},{3,1},{4,0},{5,7},{6,2},{7,5},{8,12},{9,11},{10,... | collective-permute-start | bytes 393224 | tf_op jit(solution)/shard_map/ppermute | solution.py:183
  5.6 12.1 %collective-permute-start.3 = (bf16[8,8192]{1,0:T(8,128)(2,1)}, bf16[8,8192]{1,0:T(8,128)(2,1)S(1)}, u32[]{:S(2)}, u32[]{:S(2)}) collective-permute-start(bf16[8,8192]{1,0:T(8,128)(2,1)} %param.5), channel_id=1, source_target_pairs={{0,2},{1,5},{2,0},{3,7},{4,6},{5,1},{6,4},{7,3},{8,10},{9,13},{10,... | collective-permute-start | bytes 393224 | tf_op jit(solution)/shard_map/ppermute | solution.py:183
  7.1 10.6 %collective-permute-start.4 = (bf16[8,8192]{1,0:T(8,128)(2,1)}, bf16[8,8192]{1,0:T(8,128)(2,1)S(1)}, u32[]{:S(2)}, u32[]{:S(2)}) collective-permute-start(bf16[8,8192]{1,0:T(8,128)(2,1)} %param.5), channel_id=1, source_target_pairs={{0,6},{1,7},{2,4},{3,5},{4,2},{5,3},{6,0},{7,1},{8,14},{9,15},{10,... | collective-permute-start | bytes 393224 | tf_op jit(solution)/shard_map/ppermute | solution.py:183
  10.8 6.9 %collective-permute-start.2 = (bf16[8,8192]{1,0:T(8,128)(2,1)S(1)}, bf16[8,8192]{1,0:T(8,128)(2,1)S(1)}, u32[]{:S(2)}, u32[]{:S(2)}) collective-permute-start(bf16[8,8192]{1,0:T(8,128)(2,1)S(1)} %collective-permute-done.refs_2_), channel_id=1, source_target_pairs={{0,4},{1,3},{2,6},{3,1},{4,0},{5,7},{6,2},{7,5},{8,12},{9,11},{10,... | collective-permute-start | bytes 393224 | tf_op jit(solution)/shard_map/ppermute | solution.py:183
  11.9 9.5 %collective-permute-start.5 = (bf16[8,8192]{1,0:T(8,128)(2,1)S(1)}, bf16[8,8192]{1,0:T(8,128)(2,1)S(1)}, u32[]{:S(2)}, u32[]{:S(2)}) collective-permute-start(bf16[8,8192]{1,0:T(8,128)(2,1)S(1)} %collective-permute-done.refs_2_), channel_id=1, source_target_pairs={{0,2},{1,5},{2,0},{3,7},{4,6},{5,1},{6,4},{7,3},{8,10},{9,13},{10,... | collective-permute-start | bytes 393224 | tf_op jit(solution)/shard_map/ppermute | solution.py:183
  13.4 7.9 %collective-permute-start.6 = (bf16[8,8192]{1,0:T(8,128)(2,1)S(1)}, bf16[8,8192]{1,0:T(8,128)(2,1)S(1)}, u32[]{:S(2)}, u32[]{:S(2)}) collective-permute-start(bf16[8,8192]{1,0:T(8,128)(2,1)S(1)} %collective-permute-done.refs_2_), channel_id=1, source_target_pairs={{0,6},{1,7},{2,4},{3,5},{4,2},{5,3},{6,0},{7,1},{8,14},{9,15},{10,... | collective-permute-start | bytes 393224 | tf_op jit(solution)/shard_map/ppermute | solution.py:183
  14.4 3.4 %copy-start.1 = (bf16[8,8192]{1,0:T(8,128)(2,1)S(1)}, bf16[8,8192]{1,0:T(8,128)(2,1)}, u32[]{:S(2)}) copy-start(bf16[8,8192]{1,0:T(8,128)(2,1)} %param.5) | copy-start | bytes 393220
  17.9 4.9 %collective-permute-start.7 = (bf16[48,8192]{1,0:T(8,128)(2,1)S(1)}, bf16[48,8192]{1,0:T(8,128)(2,1)S(1)}, u32[]{:S(2)}, u32[]{:S(2)}) collective-permute-start(bf16[48,8192]{1,0:T(8,128)(2,1)S(1)} %constant_dynamic-update-slice_fusion.refs_2_), channel_id=1, source_target_pairs={{0,1},{1,0},{2,3},{3,2},{4,5},{5,4},{6,7},{7,6},{8,9},{9,8},{10,11... | collective-permute-start | bytes 2359304 | tf_op jit(solution)/shard_map/ppermute | solution.py:183
  21.4 1.4 %collective-permute-start.9 = (bf16[16,4096]{1,0:T(8,128)(2,1)S(1)}, bf16[16,4096]{1,0:T(8,128)(2,1)S(1)}, u32[]{:S(2)}, u32[]{:S(2)}) collective-permute-start(bf16[16,4096]{1,0:T(8,128)(2,1)S(1)} %pad_maximum_fusion.1.refs_4_), channel_id=1, source_target_pairs={{0,1},{1,0},{2,3},{3,2},{4,5},{5,4},{6,7},{7,6},{8,9},{9,8},{10,11... | collective-permute-start | bytes 393224 | tf_op jit(solution)/shard_map/ppermute | solution.py:183
  21.5 2.0 %collective-permute-start.8 = (bf16[16,4096]{1,0:T(8,128)(2,1)S(1)}, bf16[16,4096]{1,0:T(8,128)(2,1)S(1)}, u32[]{:S(2)}, u32[]{:S(2)}) collective-permute-start(bf16[16,4096]{1,0:T(8,128)(2,1)S(1)} %pad_maximum_fusion.refs_4_), channel_id=1, source_target_pairs={{0,1},{1,0},{2,3},{3,2},{4,5},{5,4},{6,7},{7,6},{8,9},{9,8},{10,11... | collective-permute-start | bytes 393224 | tf_op jit(solution)/shard_map/ppermute | solution.py:183
  25.0 1.4 %collective-permute-start.13 = (bf16[8,8192]{1,0:T(8,128)(2,1)S(1)}, bf16[8,8192]{1,0:T(8,128)(2,1)S(1)}, u32[]{:S(2)}, u32[]{:S(2)}) collective-permute-start(bf16[8,8192]{1,0:T(8,128)(2,1)S(1)} %get-tuple-element.54), channel_id=1, source_target_pairs={{0,1},{1,0},{2,3},{3,2},{4,5},{5,4},{6,7},{7,6},{8,9},{9,8},{10,11... | collective-permute-start | bytes 393224 | tf_op jit(solution)/shard_map/ppermute | solution.py:183
  25.2 2.7 %collective-permute-start.10 = (bf16[24,8192]{1,0:T(8,128)(2,1)S(1)}, bf16[24,8192]{1,0:T(8,128)(2,1)S(1)}, u32[]{:S(2)}, u32[]{:S(2)}) collective-permute-start(bf16[24,8192]{1,0:T(8,128)(2,1)S(1)} %get-tuple-element.48), channel_id=1, source_target_pairs={{0,1},{1,0},{2,3},{3,2},{4,5},{5,4},{6,7},{7,6},{8,9},{9,8},{10,11... | collective-permute-start | bytes 1179656 | tf_op jit(solution)/shard_map/ppermute | solution.py:183
  26.4 7.0 %collective-permute-start.14 = (bf16[8,8192]{1,0:T(8,128)(2,1)S(1)}, bf16[8,8192]{1,0:T(8,128)(2,1)S(1)}, u32[]{:S(2)}, u32[]{:S(2)}) collective-permute-start(bf16[8,8192]{1,0:T(8,128)(2,1)S(1)} %add_convert_fusion), channel_id=1, source_target_pairs={{0,6},{1,7},{2,4},{3,5},{4,2},{5,3},{6,0},{7,1},{8,14},{9,15},{10,... | collective-permute-start | bytes 393224 | tf_op jit(solution)/shard_map/ppermute | solution.py:183
  27.9 2.3 %collective-permute-start.11 = (bf16[32,8192]{1,0:T(8,128)(2,1)S(1)}, bf16[32,8192]{1,0:T(8,128)(2,1)S(1)}, u32[]{:S(2)}, u32[]{:S(2)}) collective-permute-start(bf16[32,8192]{1,0:T(8,128)(2,1)S(1)} %get-tuple-element.50), channel_id=1, source_target_pairs={{0,1},{1,0},{2,3},{3,2},{4,5},{5,4},{6,7},{7,6},{8,9},{9,8},{10,11... | collective-permute-start | bytes 1572872 | tf_op jit(solution)/shard_map/ppermute | solution.py:183
  28.0 17.0 %copy-start = (s32[8192]{0:T(1024)S(1)}, s32[8192]{0:T(1024)}, u32[]{:S(2)}) copy-start(s32[8192]{0:T(1024)} %param.9) | copy-start | bytes 98308
  28.0 5.8 %collective-permute-start.15 = (bf16[8,8192]{1,0:T(8,128)(2,1)S(1)}, bf16[8,8192]{1,0:T(8,128)(2,1)S(1)}, u32[]{:S(2)}, u32[]{:S(2)}) collective-permute-start(bf16[8,8192]{1,0:T(8,128)(2,1)S(1)} %get-tuple-element.57), channel_id=1, source_target_pairs={{0,4},{1,3},{2,6},{3,1},{4,0},{5,7},{6,2},{7,5},{8,12},{9,11},{10,... | collective-permute-start | bytes 393224 | tf_op jit(solution)/shard_map/ppermute | solution.py:183
  28.9 6.9 %collective-permute-start.16 = (bf16[8,8192]{1,0:T(8,128)(2,1)S(1)}, bf16[8,8192]{1,0:T(8,128)(2,1)S(1)}, u32[]{:S(2)}, u32[]{:S(2)}) collective-permute-start(bf16[8,8192]{1,0:T(8,128)(2,1)S(1)} %get-tuple-element.58), channel_id=1, source_target_pairs={{0,2},{1,5},{2,0},{3,7},{4,6},{5,1},{6,4},{7,3},{8,10},{9,13},{10,... | collective-permute-start | bytes 393224 | tf_op jit(solution)/shard_map/ppermute | solution.py:183
  30.3 7.1 %collective-permute-start.12 = (bf16[16,8192]{1,0:T(8,128)(2,1)S(1)}, bf16[16,8192]{1,0:T(8,128)(2,1)S(1)}, u32[]{:S(2)}, u32[]{:S(2)}) collective-permute-start(bf16[16,8192]{1,0:T(8,128)(2,1)S(1)} %slice.67), channel_id=1, source_target_pairs={{0,4},{1,3},{2,6},{3,1},{4,0},{5,7},{6,2},{7,5},{8,12},{9,11},{10,... | collective-permute-start | bytes 786440 | tf_op jit(solution)/shard_map/ppermute | solution.py:183
  35.9 9.1 %collective-permute-start.17 = (bf16[8,8192]{1,0:T(8,128)(2,1)S(1)}, bf16[8,8192]{1,0:T(8,128)(2,1)S(1)}, u32[]{:S(2)}, u32[]{:S(2)}) collective-permute-start(bf16[8,8192]{1,0:T(8,128)(2,1)S(1)} %fusion.2), channel_id=1, source_target_pairs={{0,8},{1,13},{2,10},{3,15},{4,12},{5,9},{6,14},{7,11},{8,0},{9,5},... | collective-permute-start | bytes 393224 | tf_op jit(solution)/shard_map/ppermute | solution.py:183
  37.5 7.5 %collective-permute-start.18 = (bf16[8,8192]{1,0:T(8,128)(2,1)S(1)}, bf16[8,8192]{1,0:T(8,128)(2,1)S(1)}, u32[]{:S(2)}, u32[]{:S(2)}) collective-permute-start(bf16[8,8192]{1,0:T(8,128)(2,1)S(1)} %slice.68), channel_id=1, source_target_pairs={{0,2},{1,5},{2,0},{3,7},{4,6},{5,1},{6,4},{7,3},{8,10},{9,13},{10,... | collective-permute-start | bytes 393224 | tf_op jit(solution)/shard_map/ppermute | solution.py:183

commit v29 on v28

--- a/solution.py
+++ b/solution.py
@@ -176,7 +176,7 @@
     while mask > 8:
         far.append((mask, mask))
         mask //= 2
-    far.append((8, 12))
+    far.append((12, 8))
     others = members // 8 - 1
 
     def swap(value, masks):

time: 46 us -> 44.3 us (0.963)
  waiting for transfers between devices: 15.8 us -> 11.9 us
  starting transfers between devices: 20.2 us -> 22.3 us
    ppermute x19, waiting for transfers between devices: 15.8 us -> 11.9 us  [swap(): lax.ppermute(value, 'gx', [(i, i ^ masks[i % 2]) for i in range(members)])]
    ppermute x19, starting transfers between devices: 20.2 us -> 22.3 us  [swap(): lax.ppermute(value, 'gx', [(i, i ^ masks[i % 2]) for i in range(members)])]
where the time goes in v29:
time: 44.3 us; the launch traced here: 44 us
  starting transfers between devices  22.3 us (50%)
  waiting for transfers between devices  11.9 us (27%)
  Pallas kernels  9.01 us (20%)
    ppermute x19, starting transfers between devices, swap(): lax.ppermute(value, 'gx', [(i, i ^ masks[i % 2]) for i in range(members)])  22.3 us
    ppermute x19, waiting for transfers between devices, swap(): lax.ppermute(value, 'gx', [(i, i ^ masks[i % 2]) for i in range(members)])  11.9 us
    pallas_call x2, Pallas kernels, load(): pl.pallas_call(functools.partial(load_kernel, turned), out_shape=[jax.Sha...  5.96 us
    pallas_call x2, Pallas kernels, hidden_units(): pl.pallas_call(functools.partial(hidden_kernel, start, last), out_shape=(...  1.45 us
    pallas_call x1, Pallas kernels, rotate(): pl.pallas_call(functools.partial(rotate_kernel, len(arrived)), out_shape=...  0.89 us
  transfers between devices with their start and end apart: 19, of which 9 were waited for; matrix products, arithmetic and copies ran while one was open for 1% of the time, Pallas kernels for 15%

profile of v29, /device:TPU:0, one launch (start us, length us, event | category | flops | bytes accessed | tf_op | source)
XLA Modules:
  0.0 44.0 jit_solution(6258202643020011229)
XLA Ops:
  0.0 5.0 %collective-permute-start = (bf16[8,8192]{1,0:T(8,128)(2,1)}, bf16[8,8192]{1,0:T(8,128)(2,1)S(1)}, u32[]{:S(2)}, u32[]{:S(2)}) collective-permute-start(bf16[8,8192]{1,0:T(8,128)(2,1)} %param.5), channel_id=1, source_target_pairs={{0,12},{1,9},{2,14},{3,11},{4,8},{5,13},{6,10},{7,15},{8,4},{9,1},... | collective-permute-start | bytes 393224 | tf_op jit(solution)/shard_map/ppermute | solution.py:183
  5.0 0.0 collective-permute-start.1
  5.1 1.5 %collective-permute-start.3 = (bf16[8,8192]{1,0:T(8,128)(2,1)}, bf16[8,8192]{1,0:T(8,128)(2,1)S(1)}, u32[]{:S(2)}, u32[]{:S(2)}) collective-permute-start(bf16[8,8192]{1,0:T(8,128)(2,1)} %param.5), channel_id=1, source_target_pairs={{0,2},{1,5},{2,0},{3,7},{4,6},{5,1},{6,4},{7,3},{8,10},{9,13},{10,... | collective-permute-start | bytes 393224 | tf_op jit(solution)/shard_map/ppermute | solution.py:183
  6.6 2.0 %collective-permute-start.4 = (bf16[8,8192]{1,0:T(8,128)(2,1)}, bf16[8,8192]{1,0:T(8,128)(2,1)S(1)}, u32[]{:S(2)}, u32[]{:S(2)}) collective-permute-start(bf16[8,8192]{1,0:T(8,128)(2,1)} %param.5), channel_id=1, source_target_pairs={{0,6},{1,7},{2,4},{3,5},{4,2},{5,3},{6,0},{7,1},{8,14},{9,15},{10,... | collective-permute-start | bytes 393224 | tf_op jit(solution)/shard_map/ppermute | solution.py:183
  8.5 2.7 %shard_map.55.refs_0_ = bf16[8192,224]{1,0:T(8,128)(2,1)S(1)} custom-call(bf16[224,8192]{1,0:T(8,128)(2,1)} %bitcast.4, bf16[224,8192]{1,0:T(8,128)(2,1)} %bitcast.5), custom_call_target="tpu_custom_call" | custom-call | bytes 7340032 | tf_op jit(solution)/shard_map/pallas_call | solution.py:52
  11.2 0.0 collective-permute-done.refs_2_
  11.2 0.2 collective-permute-start.2
  11.4 1.5 %collective-permute-start.5 = (bf16[8,8192]{1,0:T(8,128)(2,1)S(1)}, bf16[8,8192]{1,0:T(8,128)(2,1)S(1)}, u32[]{:S(2)}, u32[]{:S(2)}) collective-permute-start(bf16[8,8192]{1,0:T(8,128)(2,1)S(1)} %collective-permute-done.refs_2_), channel_id=1, source_target_pairs={{0,2},{1,5},{2,0},{3,7},{4,6},{5,1},{6,4},{7,3},{8,10},{9,13},{10,... | collective-permute-start | bytes 393224 | tf_op jit(solution)/shard_map/ppermute | solution.py:183
  12.9 0.0 collective-permute-done.1
  12.9 1.9 %collective-permute-start.6 = (bf16[8,8192]{1,0:T(8,128)(2,1)S(1)}, bf16[8,8192]{1,0:T(8,128)(2,1)S(1)}, u32[]{:S(2)}, u32[]{:S(2)}) collective-permute-start(bf16[8,8192]{1,0:T(8,128)(2,1)S(1)} %collective-permute-done.refs_2_), channel_id=1, source_target_pairs={{0,6},{1,7},{2,4},{3,5},{4,2},{5,3},{6,0},{7,1},{8,14},{9,15},{10,... | collective-permute-start | bytes 393224 | tf_op jit(solution)/shard_map/ppermute | solution.py:183
  14.8 0.0 copy-start.1
  14.8 3.3 %shard_map.56 = (bf16[8192,224]{1,0:T(8,128)(2,1)S(1)}, bf16[224,8192]{1,0:T(8,128)(2,1)S(1)}) custom-call(bf16[224,8192]{1,0:T(8,128)(2,1)} %bitcast.6, bf16[224,8192]{1,0:T(8,128)(2,1)} %refs_1_.1, bf16[8,8192]{1,0:T(8,128)(2,1)S(1)} %collective-permute-done.refs_2_), custom_call_target="tpu_custom_call" | custom-call | bytes 14680064 | tf_op jit(solution)/shard_map/pallas_call | solution.py:52
  18.1 0.0 collective-permute-done.3
  18.1 0.0 collective-permute-done.4
  18.1 0.0 collective-permute-done.2
  18.2 0.0 copy-done.1
  18.2 0.1 collective-permute-start.7
  18.3 2.2 %collective-permute-done.6 = bf16[8,8192]{1,0:T(8,128)(2,1)S(1)} collective-permute-done((bf16[8,8192]{1,0:T(8,128)(2,1)S(1)}, bf16[8,8192]{1,0:T(8,128)(2,1)S(1)}, u32[]{:S(2)}, u32[]{:S(2)}) %collective-permute-start.6) | collective-permute-done | bytes 131104 | tf_op jit(solution)/shard_map/ppermute | solution.py:183
  20.5 0.0 collective-permute-done.5
  20.6 0.1 collective-permute-start.9
  20.7 0.6 %collective-permute-start.8 = (bf16[16,4096]{1,0:T(8,128)(2,1)S(1)}, bf16[16,4096]{1,0:T(8,128)(2,1)S(1)}, u32[]{:S(2)}, u32[]{:S(2)}) collective-permute-start(bf16[16,4096]{1,0:T(8,128)(2,1)S(1)} %pad_maximum_fusion.refs_4_), channel_id=1, source_target_pairs={{0,1},{1,0},{2,3},{3,2},{4,5},{5,4},{6,7},{7,6},{8,9},{9,8},{10,11... | collective-permute-start | bytes 393224 | tf_op jit(solution)/shard_map/ppermute | solution.py:183
  21.2 0.8 %collective-permute-done.9.refs_5_ = bf16[16,4096]{1,0:T(8,128)(2,1)S(1)} collective-permute-done((bf16[16,4096]{1,0:T(8,128)(2,1)S(1)}, bf16[16,4096]{1,0:T(8,128)(2,1)S(1)}, u32[]{:S(2)}, u32[]{:S(2)}) %collective-permute-start.9) | collective-permute-done | bytes 131104 | tf_op jit(solution)/shard_map/ppermute | solution.py:183
  22.0 0.0 collective-permute-done.7.refs_3_
  22.0 0.7 %shard_map.57 = (f32[128,224]{1,0:T(8,128)S(1)}, f32[128,224]{1,0:T(8,128)S(1)}) custom-call(bf16[8192,224]{1,0:T(8,128)(2,1)S(1)} %shard_map.55.refs_0_, bf16[8192,224]{1,0:T(8,128)(2,1)S(1)} %get-tuple-element.40.refs_1_, bf16[48,8192]{1,0:T(8,128)(2,1)S(1)} %constant_dynamic-update-slice_fusion.refs_2_, ...), custom_call_target="tpu_custom_call" | custom-call | flops 469762048 | bytes 3670016 | tf_op jit(solution)/shard_map/pallas_call | solution.py:91
  22.7 0.0 collective-permute-done.8.refs_5_
  22.7 0.7 %shard_map.58.hidden_ref = bf16[128,224]{1,0:T(8,128)(2,1)S(1)} custom-call(bf16[8192,224]{1,0:T(8,128)(2,1)S(1)} %shard_map.55.refs_0_, bf16[8192,224]{1,0:T(8,128)(2,1)S(1)} %get-tuple-element.40.refs_1_, bf16[48,8192]{1,0:T(8,128)(2,1)S(1)} %constant_dynamic-update-slice_fusion.refs_2_, bf16[48,8192]{1,0:T(8,128)(2,1)S(1)} %collective-permute-done.7.refs_3_, ...), custom_call_target="tpu_custom_call" | custom-call | flops 469762048 | bytes 3670016 | tf_op jit(solution)/shard_map/pallas_call | solution.py:91
  23.4 0.7 %shard_map.59 = (f32[32,8192]{1,0:T(8,128)S(1)}, f32[8,8192]{1,0:T(8,128)S(1)}, f32[24,8192]{1,0:T(8,128)S(1)}, bf16[32,8192]{1,0:T(8,128)(2,1)S(1)}, bf16[8,819...) custom-call(bf16[128,224]{1,0:T(8,128)(2,1)S(1)} %shard_map.58.hidden_ref, bf16[224,8192]{1,0:T(8,128)(2,1)S(1)} %get-tuple-element.46.down_ref), custom_call_target="tpu_custom_call" | custom-call | flops 469762048 | bytes 3670016 | tf_op jit(solution)/shard_map/pallas_call | solution.py:120
  24.2 0.2 collective-permute-start.13
  24.4 0.4 collective-permute-start.10
  24.7 0.8 %collective-permute-done.13 = bf16[8,8192]{1,0:T(8,128)(2,1)S(1)} collective-permute-done((bf16[8,8192]{1,0:T(8,128)(2,1)S(1)}, bf16[8,8192]{1,0:T(8,128)(2,1)S(1)}, u32[]{:S(2)}, u32[]{:S(2)}) %collective-permute-start.13) | collective-permute-done | bytes 131104 | tf_op jit(solution)/shard_map/ppermute | solution.py:183
  25.6 2.0 %collective-permute-start.14 = (bf16[8,8192]{1,0:T(8,128)(2,1)S(1)}, bf16[8,8192]{1,0:T(8,128)(2,1)S(1)}, u32[]{:S(2)}, u32[]{:S(2)}) collective-permute-start(bf16[8,8192]{1,0:T(8,128)(2,1)S(1)} %add_convert_fusion), channel_id=1, source_target_pairs={{0,6},{1,7},{2,4},{3,5},{4,2},{5,3},{6,0},{7,1},{8,14},{9,15},{10,... | collective-permute-start | bytes 393224 | tf_op jit(solution)/shard_map/ppermute | solution.py:183
  27.6 0.0 collective-permute-done.10
  27.6 0.0 collective-permute-start.11
  27.6 0.1 fusion.7
  27.7 0.0 copy-start
  27.7 0.8 %collective-permute-start.15 = (bf16[8,8192]{1,0:T(8,128)(2,1)S(1)}, bf16[8,8192]{1,0:T(8,128)(2,1)S(1)}, u32[]{:S(2)}, u32[]{:S(2)}) collective-permute-start(bf16[8,8192]{1,0:T(8,128)(2,1)S(1)} %get-tuple-element.57), channel_id=1, source_target_pairs={{0,4},{1,3},{2,6},{3,1},{4,0},{5,7},{6,2},{7,5},{8,12},{9,11},{10,... | collective-permute-start | bytes 393224 | tf_op jit(solution)/shard_map/ppermute | solution.py:183
  28.5 0.9 %collective-permute-start.16 = (bf16[8,8192]{1,0:T(8,128)(2,1)S(1)}, bf16[8,8192]{1,0:T(8,128)(2,1)S(1)}, u32[]{:S(2)}, u32[]{:S(2)}) collective-permute-start(bf16[8,8192]{1,0:T(8,128)(2,1)S(1)} %get-tuple-element.58), channel_id=1, source_target_pairs={{0,2},{1,5},{2,0},{3,7},{4,6},{5,1},{6,4},{7,3},{8,10},{9,13},{10,... | collective-permute-start | bytes 393224 | tf_op jit(solution)/shard_map/ppermute | solution.py:183
  29.4 0.1 collective-permute-done.11
  29.5 0.1 convert_add_fusion
  29.6 1.2 %collective-permute-start.12 = (bf16[16,8192]{1,0:T(8,128)(2,1)S(1)}, bf16[16,8192]{1,0:T(8,128)(2,1)S(1)}, u32[]{:S(2)}, u32[]{:S(2)}) collective-permute-start(bf16[16,8192]{1,0:T(8,128)(2,1)S(1)} %slice.67), channel_id=1, source_target_pairs={{0,4},{1,3},{2,6},{3,1},{4,0},{5,7},{6,2},{7,5},{8,12},{9,11},{10,... | collective-permute-start | bytes 786440 | tf_op jit(solution)/shard_map/ppermute | solution.py:183
  30.8 1.4 %collective-permute-done.14 = bf16[8,8192]{1,0:T(8,128)(2,1)S(1)} collective-permute-done((bf16[8,8192]{1,0:T(8,128)(2,1)S(1)}, bf16[8,8192]{1,0:T(8,128)(2,1)S(1)}, u32[]{:S(2)}, u32[]{:S(2)}) %collective-permute-start.14) | collective-permute-done | bytes 131104 | tf_op jit(solution)/shard_map/ppermute | solution.py:183
  32.2 2.4 %collective-permute-done.15 = bf16[8,8192]{1,0:T(8,128)(2,1)S(1)} collective-permute-done((bf16[8,8192]{1,0:T(8,128)(2,1)S(1)}, bf16[8,8192]{1,0:T(8,128)(2,1)S(1)}, u32[]{:S(2)}, u32[]{:S(2)}) %collective-permute-start.15) | collective-permute-done | bytes 131104 | tf_op jit(solution)/shard_map/ppermute | solution.py:183
  34.6 0.4 collective-permute-done.16
  35.0 0.1 fusion.2
  35.1 2.9 %collective-permute-start.17 = (bf16[8,8192]{1,0:T(8,128)(2,1)S(1)}, bf16[8,8192]{1,0:T(8,128)(2,1)S(1)}, u32[]{:S(2)}, u32[]{:S(2)}) collective-permute-start(bf16[8,8192]{1,0:T(8,128)(2,1)S(1)} %fusion.2), channel_id=1, source_target_pairs={{0,12},{1,9},{2,14},{3,11},{4,8},{5,13},{6,10},{7,15},{8,4},{9,1},... | collective-permute-start | bytes 393224 | tf_op jit(solution)/shard_map/ppermute | solution.py:183
  37.9 0.0 collective-permute-done.12
  37.9 0.1 slice_add_fusion
  38.0 1.2 %collective-permute-start.18 = (bf16[8,8192]{1,0:T(8,128)(2,1)S(1)}, bf16[8,8192]{1,0:T(8,128)(2,1)S(1)}, u32[]{:S(2)}, u32[]{:S(2)}) collective-permute-start(bf16[8,8192]{1,0:T(8,128)(2,1)S(1)} %slice.68), channel_id=1, source_target_pairs={{0,2},{1,5},{2,0},{3,7},{4,6},{5,1},{6,4},{7,3},{8,10},{9,13},{10,... | collective-permute-start | bytes 393224 | tf_op jit(solution)/shard_map/ppermute | solution.py:183
  39.3 2.9 %collective-permute-done.17.refs_1_ = bf16[8,8192]{1,0:T(8,128)(2,1)S(1)} collective-permute-done((bf16[8,8192]{1,0:T(8,128)(2,1)S(1)}, bf16[8,8192]{1,0:T(8,128)(2,1)S(1)}, u32[]{:S(2)}, u32[]{:S(2)}) %collective-permute-start.17) | collective-permute-done | bytes 131104 | tf_op jit(solution)/shard_map/ppermute | solution.py:183
  42.2 0.8 %collective-permute-done.18.refs_2_ = bf16[8,8192]{1,0:T(8,128)(2,1)S(1)} collective-permute-done((bf16[8,8192]{1,0:T(8,128)(2,1)S(1)}, bf16[8,8192]{1,0:T(8,128)(2,1)S(1)}, u32[]{:S(2)}, u32[]{:S(2)}) %collective-permute-start.18) | collective-permute-done | bytes 131104 | tf_op jit(solution)/shard_map/ppermute | solution.py:183
  43.1 0.0 copy-done
  43.1 0.9 %shard_map.60 = bf16[8,8192]{1,0:T(8,128)(2,1)} custom-call(f32[8,8192]{1,0:T(8,128)S(1)} %slice.52.refs_0_, bf16[8,8192]{1,0:T(8,128)(2,1)S(1)} %collective-permute-done.17.refs_1_, bf16[8,8192]{1,0:T(8,128)(2,1)S(1)} %collective-permute-done.18.refs_2_, s32[1,8192]{1,0:T(1,128)S(1)} %bitcast.3, bf16[256,128]{1,0:T(8,128)(2,1)S(1)} %pad_maximum_fusion.2.refs_4_), custom_call_target="tpu_custom_call" | custom-call | tf_op jit(solution)/shard_map/pallas_call | solution.py:160
  (16 shorter events, 0.3 us)
Async XLA Ops:
  0.0 11.2 %collective-permute-start = (bf16[8,8192]{1,0:T(8,128)(2,1)}, bf16[8,8192]{1,0:T(8,128)(2,1)S(1)}, u32[]{:S(2)}, u32[]{:S(2)}) collective-permute-start(bf16[8,8192]{1,0:T(8,128)(2,1)} %param.5), channel_id=1, source_target_pairs={{0,12},{1,9},{2,14},{3,11},{4,8},{5,13},{6,10},{7,15},{8,4},{9,1},... | collective-permute-start | bytes 393224 | tf_op jit(solution)/shard_map/ppermute | solution.py:183
  5.0 7.9 %collective-permute-start.1 = (bf16[8,8192]{1,0:T(8,128)(2,1)}, bf16[8,8192]{1,0:T(8,128)(2,1)S(1)}, u32[]{:S(2)}, u32[]{:S(2)}) collective-permute-start(bf16[8,8192]{1,0:T(8,128)(2,1)} %param.5), channel_id=1, source_target_pairs={{0,4},{1,3},{2,6},{3,1},{4,0},{5,7},{6,2},{7,5},{8,12},{9,11},{10,... | collective-permute-start | bytes 393224 | tf_op jit(solution)/shard_map/ppermute | solution.py:183
  5.1 13.0 %collective-permute-start.3 = (bf16[8,8192]{1,0:T(8,128)(2,1)}, bf16[8,8192]{1,0:T(8,128)(2,1)S(1)}, u32[]{:S(2)}, u32[]{:S(2)}) collective-permute-start(bf16[8,8192]{1,0:T(8,128)(2,1)} %param.5), channel_id=1, source_target_pairs={{0,2},{1,5},{2,0},{3,7},{4,6},{5,1},{6,4},{7,3},{8,10},{9,13},{10,... | collective-permute-start | bytes 393224 | tf_op jit(solution)/shard_map/ppermute | solution.py:183
  6.6 11.5 %collective-permute-start.4 = (bf16[8,8192]{1,0:T(8,128)(2,1)}, bf16[8,8192]{1,0:T(8,128)(2,1)S(1)}, u32[]{:S(2)}, u32[]{:S(2)}) collective-permute-start(bf16[8,8192]{1,0:T(8,128)(2,1)} %param.5), channel_id=1, source_target_pairs={{0,6},{1,7},{2,4},{3,5},{4,2},{5,3},{6,0},{7,1},{8,14},{9,15},{10,... | collective-permute-start | bytes 393224 | tf_op jit(solution)/shard_map/ppermute | solution.py:183
  11.2 6.9 %collective-permute-start.2 = (bf16[8,8192]{1,0:T(8,128)(2,1)S(1)}, bf16[8,8192]{1,0:T(8,128)(2,1)S(1)}, u32[]{:S(2)}, u32[]{:S(2)}) collective-permute-start(bf16[8,8192]{1,0:T(8,128)(2,1)S(1)} %collective-permute-done.refs_2_), channel_id=1, source_target_pairs={{0,4},{1,3},{2,6},{3,1},{4,0},{5,7},{6,2},{7,5},{8,12},{9,11},{10,... | collective-permute-start | bytes 393224 | tf_op jit(solution)/shard_map/ppermute | solution.py:183
  11.4 9.1 %collective-permute-start.5 = (bf16[8,8192]{1,0:T(8,128)(2,1)S(1)}, bf16[8,8192]{1,0:T(8,128)(2,1)S(1)}, u32[]{:S(2)}, u32[]{:S(2)}) collective-permute-start(bf16[8,8192]{1,0:T(8,128)(2,1)S(1)} %collective-permute-done.refs_2_), channel_id=1, source_target_pairs={{0,2},{1,5},{2,0},{3,7},{4,6},{5,1},{6,4},{7,3},{8,10},{9,13},{10,... | collective-permute-start | bytes 393224 | tf_op jit(solution)/shard_map/ppermute | solution.py:183
  12.9 7.6 %collective-permute-start.6 = (bf16[8,8192]{1,0:T(8,128)(2,1)S(1)}, bf16[8,8192]{1,0:T(8,128)(2,1)S(1)}, u32[]{:S(2)}, u32[]{:S(2)}) collective-permute-start(bf16[8,8192]{1,0:T(8,128)(2,1)S(1)} %collective-permute-done.refs_2_), channel_id=1, source_target_pairs={{0,6},{1,7},{2,4},{3,5},{4,2},{5,3},{6,0},{7,1},{8,14},{9,15},{10,... | collective-permute-start | bytes 393224 | tf_op jit(solution)/shard_map/ppermute | solution.py:183
  14.8 3.4 %copy-start.1 = (bf16[8,8192]{1,0:T(8,128)(2,1)S(1)}, bf16[8,8192]{1,0:T(8,128)(2,1)}, u32[]{:S(2)}) copy-start(bf16[8,8192]{1,0:T(8,128)(2,1)} %param.5) | copy-start | bytes 393220
  18.2 3.7 %collective-permute-start.7 = (bf16[48,8192]{1,0:T(8,128)(2,1)S(1)}, bf16[48,8192]{1,0:T(8,128)(2,1)S(1)}, u32[]{:S(2)}, u32[]{:S(2)}) collective-permute-start(bf16[48,8192]{1,0:T(8,128)(2,1)S(1)} %constant_dynamic-update-slice_fusion.refs_2_), channel_id=1, source_target_pairs={{0,1},{1,0},{2,3},{3,2},{4,5},{5,4},{6,7},{7,6},{8,9},{9,8},{10,11... | collective-permute-start | bytes 2359304 | tf_op jit(solution)/shard_map/ppermute | solution.py:183
  20.6 1.4 %collective-permute-start.9 = (bf16[16,4096]{1,0:T(8,128)(2,1)S(1)}, bf16[16,4096]{1,0:T(8,128)(2,1)S(1)}, u32[]{:S(2)}, u32[]{:S(2)}) collective-permute-start(bf16[16,4096]{1,0:T(8,128)(2,1)S(1)} %pad_maximum_fusion.1.refs_4_), channel_id=1, source_target_pairs={{0,1},{1,0},{2,3},{3,2},{4,5},{5,4},{6,7},{7,6},{8,9},{9,8},{10,11... | collective-permute-start | bytes 393224 | tf_op jit(solution)/shard_map/ppermute | solution.py:183
  20.7 2.0 %collective-permute-start.8 = (bf16[16,4096]{1,0:T(8,128)(2,1)S(1)}, bf16[16,4096]{1,0:T(8,128)(2,1)S(1)}, u32[]{:S(2)}, u32[]{:S(2)}) collective-permute-start(bf16[16,4096]{1,0:T(8,128)(2,1)S(1)} %pad_maximum_fusion.refs_4_), channel_id=1, source_target_pairs={{0,1},{1,0},{2,3},{3,2},{4,5},{5,4},{6,7},{7,6},{8,9},{9,8},{10,11... | collective-permute-start | bytes 393224 | tf_op jit(solution)/shard_map/ppermute | solution.py:183
  24.2 1.4 %collective-permute-start.13 = (bf16[8,8192]{1,0:T(8,128)(2,1)S(1)}, bf16[8,8192]{1,0:T(8,128)(2,1)S(1)}, u32[]{:S(2)}, u32[]{:S(2)}) collective-permute-start(bf16[8,8192]{1,0:T(8,128)(2,1)S(1)} %get-tuple-element.54), channel_id=1, source_target_pairs={{0,1},{1,0},{2,3},{3,2},{4,5},{5,4},{6,7},{7,6},{8,9},{9,8},{10,11... | collective-permute-start | bytes 393224 | tf_op jit(solution)/shard_map/ppermute | solution.py:183
  24.4 3.2 %collective-permute-start.10 = (bf16[24,8192]{1,0:T(8,128)(2,1)S(1)}, bf16[24,8192]{1,0:T(8,128)(2,1)S(1)}, u32[]{:S(2)}, u32[]{:S(2)}) collective-permute-start(bf16[24,8192]{1,0:T(8,128)(2,1)S(1)} %get-tuple-element.48), channel_id=1, source_target_pairs={{0,1},{1,0},{2,3},{3,2},{4,5},{5,4},{6,7},{7,6},{8,9},{9,8},{10,11... | collective-permute-start | bytes 1179656 | tf_op jit(solution)/shard_map/ppermute | solution.py:183
  25.6 6.6 %collective-permute-start.14 = (bf16[8,8192]{1,0:T(8,128)(2,1)S(1)}, bf16[8,8192]{1,0:T(8,128)(2,1)S(1)}, u32[]{:S(2)}, u32[]{:S(2)}) collective-permute-start(bf16[8,8192]{1,0:T(8,128)(2,1)S(1)} %add_convert_fusion), channel_id=1, source_target_pairs={{0,6},{1,7},{2,4},{3,5},{4,2},{5,3},{6,0},{7,1},{8,14},{9,15},{10,... | collective-permute-start | bytes 393224 | tf_op jit(solution)/shard_map/ppermute | solution.py:183
  27.6 1.9 %collective-permute-start.11 = (bf16[32,8192]{1,0:T(8,128)(2,1)S(1)}, bf16[32,8192]{1,0:T(8,128)(2,1)S(1)}, u32[]{:S(2)}, u32[]{:S(2)}) collective-permute-start(bf16[32,8192]{1,0:T(8,128)(2,1)S(1)} %get-tuple-element.50), channel_id=1, source_target_pairs={{0,1},{1,0},{2,3},{3,2},{4,5},{5,4},{6,7},{7,6},{8,9},{9,8},{10,11... | collective-permute-start | bytes 1572872 | tf_op jit(solution)/shard_map/ppermute | solution.py:183
  27.7 15.4 %copy-start = (s32[8192]{0:T(1024)S(1)}, s32[8192]{0:T(1024)}, u32[]{:S(2)}) copy-start(s32[8192]{0:T(1024)} %param.9) | copy-start | bytes 98308
  27.7 6.9 %collective-permute-start.15 = (bf16[8,8192]{1,0:T(8,128)(2,1)S(1)}, bf16[8,8192]{1,0:T(8,128)(2,1)S(1)}, u32[]{:S(2)}, u32[]{:S(2)}) collective-permute-start(bf16[8,8192]{1,0:T(8,128)(2,1)S(1)} %get-tuple-element.57), channel_id=1, source_target_pairs={{0,4},{1,3},{2,6},{3,1},{4,0},{5,7},{6,2},{7,5},{8,12},{9,11},{10,... | collective-permute-start | bytes 393224 | tf_op jit(solution)/shard_map/ppermute | solution.py:183
  28.5 6.6 %collective-permute-start.16 = (bf16[8,8192]{1,0:T(8,128)(2,1)S(1)}, bf16[8,8192]{1,0:T(8,128)(2,1)S(1)}, u32[]{:S(2)}, u32[]{:S(2)}) collective-permute-start(bf16[8,8192]{1,0:T(8,128)(2,1)S(1)} %get-tuple-element.58), channel_id=1, source_target_pairs={{0,2},{1,5},{2,0},{3,7},{4,6},{5,1},{6,4},{7,3},{8,10},{9,13},{10,... | collective-permute-start | bytes 393224 | tf_op jit(solution)/shard_map/ppermute | solution.py:183
  29.6 8.3 %collective-permute-start.12 = (bf16[16,8192]{1,0:T(8,128)(2,1)S(1)}, bf16[16,8192]{1,0:T(8,128)(2,1)S(1)}, u32[]{:S(2)}, u32[]{:S(2)}) collective-permute-start(bf16[16,8192]{1,0:T(8,128)(2,1)S(1)} %slice.67), channel_id=1, source_target_pairs={{0,4},{1,3},{2,6},{3,1},{4,0},{5,7},{6,2},{7,5},{8,12},{9,11},{10,... | collective-permute-start | bytes 786440 | tf_op jit(solution)/shard_map/ppermute | solution.py:183
  35.1 7.2 %collective-permute-start.17 = (bf16[8,8192]{1,0:T(8,128)(2,1)S(1)}, bf16[8,8192]{1,0:T(8,128)(2,1)S(1)}, u32[]{:S(2)}, u32[]{:S(2)}) collective-permute-start(bf16[8,8192]{1,0:T(8,128)(2,1)S(1)} %fusion.2), channel_id=1, source_target_pairs={{0,12},{1,9},{2,14},{3,11},{4,8},{5,13},{6,10},{7,15},{8,4},{9,1},... | collective-permute-start | bytes 393224 | tf_op jit(solution)/shard_map/ppermute | solution.py:183
  38.0 5.0 %collective-permute-start.18 = (bf16[8,8192]{1,0:T(8,128)(2,1)S(1)}, bf16[8,8192]{1,0:T(8,128)(2,1)S(1)}, u32[]{:S(2)}, u32[]{:S(2)}) collective-permute-start(bf16[8,8192]{1,0:T(8,128)(2,1)S(1)} %slice.68), channel_id=1, source_target_pairs={{0,2},{1,5},{2,0},{3,7},{4,6},{5,1},{6,4},{7,3},{8,10},{9,13},{10,... | collective-permute-start | bytes 393224 | tf_op jit(solution)/shard_map/ppermute | solution.py:183

commit v30 on v29

--- a/solution.py
+++ b/solution.py
@@ -193,9 +193,11 @@
         gate_w = pltpu.with_memory_space_constraint(gate_weight.T, pltpu.HBM)
         (gate_w,) = load((gate_w,), (True,), gate_w)
         away, gate_w = lax.optimization_barrier((away, gate_w))
-        there = [swap(away, m) for m in square[:2]]
+        there = [None] * 3
+        for k in (2, 0):
+            there[k] = swap(away, square[k])
         away, near[0] = lax.optimization_barrier((away, near[0]))
-        there.append(swap(away, square[2]))
+        there[1] = swap(away, square[1])
         up_w, down_w = load((up_weight.T, down_weight), (True, False), away)
         there[0], *near = lax.optimization_barrier((there[0], *near))
         early = jnp.concatenate([near[1], near[0], near[2], away, there[0], tokens])

time: 44.3 us -> 44.6 us (level)
  no operation moved by 1% of the time
where the time goes in v30:
time: 44.6 us; the launch traced here: 44.2 us
  starting transfers between devices  22.3 us (50%)
  waiting for transfers between devices  12.1 us (27%)
  Pallas kernels  9.03 us (20%)
    ppermute x19, starting transfers between devices, swap(): lax.ppermute(value, 'gx', [(i, i ^ masks[i % 2]) for i in range(members)])  22.3 us
    ppermute x19, waiting for transfers between devices, swap(): lax.ppermute(value, 'gx', [(i, i ^ masks[i % 2]) for i in range(members)])  12.1 us
    pallas_call x2, Pallas kernels, load(): pl.pallas_call(functools.partial(load_kernel, turned), out_shape=[jax.Sha...  5.96 us
    pallas_call x2, Pallas kernels, hidden_units(): pl.pallas_call(functools.partial(hidden_kernel, start, last), out_shape=(...  1.45 us
    pallas_call x1, Pallas kernels, rotate(): pl.pallas_call(functools.partial(rotate_kernel, len(arrived)), out_shape=...  0.89 us
  transfers between devices with their start and end apart: 19, of which 9 were waited for; matrix products, arithmetic and copies ran while one was open for 1% of the time, Pallas kernels for 15%

profile of v30, /device:TPU:0, one launch (start us, length us, event | category | flops | bytes accessed | tf_op | source)
XLA Modules:
  0.0 44.2 jit_solution(17216273918159831359)
XLA Ops:
  0.0 5.0 %collective-permute-start = (bf16[8,8192]{1,0:T(8,128)(2,1)}, bf16[8,8192]{1,0:T(8,128)(2,1)S(1)}, u32[]{:S(2)}, u32[]{:S(2)}) collective-permute-start(bf16[8,8192]{1,0:T(8,128)(2,1)} %param.5), channel_id=1, source_target_pairs={{0,12},{1,9},{2,14},{3,11},{4,8},{5,13},{6,10},{7,15},{8,4},{9,1},... | collective-permute-start | bytes 393224 | tf_op jit(solution)/shard_map/ppermute | solution.py:183
  5.0 0.0 collective-permute-start.1
  5.1 1.5 %collective-permute-start.3 = (bf16[8,8192]{1,0:T(8,128)(2,1)}, bf16[8,8192]{1,0:T(8,128)(2,1)S(1)}, u32[]{:S(2)}, u32[]{:S(2)}) collective-permute-start(bf16[8,8192]{1,0:T(8,128)(2,1)} %param.5), channel_id=1, source_target_pairs={{0,2},{1,5},{2,0},{3,7},{4,6},{5,1},{6,4},{7,3},{8,10},{9,13},{10,... | collective-permute-start | bytes 393224 | tf_op jit(solution)/shard_map/ppermute | solution.py:183
  6.6 2.0 %collective-permute-start.4 = (bf16[8,8192]{1,0:T(8,128)(2,1)}, bf16[8,8192]{1,0:T(8,128)(2,1)S(1)}, u32[]{:S(2)}, u32[]{:S(2)}) collective-permute-start(bf16[8,8192]{1,0:T(8,128)(2,1)} %param.5), channel_id=1, source_target_pairs={{0,6},{1,7},{2,4},{3,5},{4,2},{5,3},{6,0},{7,1},{8,14},{9,15},{10,... | collective-permute-start | bytes 393224 | tf_op jit(solution)/shard_map/ppermute | solution.py:183
  8.5 2.7 %shard_map.55.refs_0_ = bf16[8192,224]{1,0:T(8,128)(2,1)S(1)} custom-call(bf16[224,8192]{1,0:T(8,128)(2,1)} %bitcast.4, bf16[224,8192]{1,0:T(8,128)(2,1)} %bitcast.5), custom_call_target="tpu_custom_call" | custom-call | bytes 7340032 | tf_op jit(solution)/shard_map/pallas_call | solution.py:52
  11.2 0.0 collective-permute-done.refs_2_
  11.2 0.2 collective-permute-start.2
  11.4 2.9 %collective-permute-start.6 = (bf16[8,8192]{1,0:T(8,128)(2,1)S(1)}, bf16[8,8192]{1,0:T(8,128)(2,1)S(1)}, u32[]{:S(2)}, u32[]{:S(2)}) collective-permute-start(bf16[8,8192]{1,0:T(8,128)(2,1)S(1)} %collective-permute-done.refs_2_), channel_id=1, source_target_pairs={{0,6},{1,7},{2,4},{3,5},{4,2},{5,3},{6,0},{7,1},{8,14},{9,15},{10,... | collective-permute-start | bytes 393224 | tf_op jit(solution)/shard_map/ppermute | solution.py:183
  14.3 0.0 collective-permute-done.1
  14.3 0.5 %collective-permute-start.5 = (bf16[8,8192]{1,0:T(8,128)(2,1)S(1)}, bf16[8,8192]{1,0:T(8,128)(2,1)S(1)}, u32[]{:S(2)}, u32[]{:S(2)}) collective-permute-start(bf16[8,8192]{1,0:T(8,128)(2,1)S(1)} %collective-permute-done.refs_2_), channel_id=1, source_target_pairs={{0,2},{1,5},{2,0},{3,7},{4,6},{5,1},{6,4},{7,3},{8,10},{9,13},{10,... | collective-permute-start | bytes 393224 | tf_op jit(solution)/shard_map/ppermute | solution.py:183
  14.8 0.0 copy-start.1
  14.8 3.3 %shard_map.56 = (bf16[8192,224]{1,0:T(8,128)(2,1)S(1)}, bf16[224,8192]{1,0:T(8,128)(2,1)S(1)}) custom-call(bf16[224,8192]{1,0:T(8,128)(2,1)} %bitcast.6, bf16[224,8192]{1,0:T(8,128)(2,1)} %refs_1_.1, bf16[8,8192]{1,0:T(8,128)(2,1)S(1)} %collective-permute-done.refs_2_), custom_call_target="tpu_custom_call" | custom-call | bytes 14680064 | tf_op jit(solution)/shard_map/pallas_call | solution.py:52
  18.1 0.0 collective-permute-done.3
  18.1 0.0 collective-permute-done.4
  18.1 0.0 collective-permute-done.2
  18.2 0.0 copy-done.1
  18.2 0.1 collective-permute-start.7
  18.3 1.4 %collective-permute-done.5 = bf16[8,8192]{1,0:T(8,128)(2,1)S(1)} collective-permute-done((bf16[8,8192]{1,0:T(8,128)(2,1)S(1)}, bf16[8,8192]{1,0:T(8,128)(2,1)S(1)}, u32[]{:S(2)}, u32[]{:S(2)}) %collective-permute-start.5) | collective-permute-done | bytes 131104 | tf_op jit(solution)/shard_map/ppermute | solution.py:183
  19.8 0.9 %collective-permute-done.6 = bf16[8,8192]{1,0:T(8,128)(2,1)S(1)} collective-permute-done((bf16[8,8192]{1,0:T(8,128)(2,1)S(1)}, bf16[8,8192]{1,0:T(8,128)(2,1)S(1)}, u32[]{:S(2)}, u32[]{:S(2)}) %collective-permute-start.6) | collective-permute-done | bytes 131104 | tf_op jit(solution)/shard_map/ppermute | solution.py:183
  20.7 0.1 collective-permute-start.9
  20.8 0.6 %collective-permute-start.8 = (bf16[16,4096]{1,0:T(8,128)(2,1)S(1)}, bf16[16,4096]{1,0:T(8,128)(2,1)S(1)}, u32[]{:S(2)}, u32[]{:S(2)}) collective-permute-start(bf16[16,4096]{1,0:T(8,128)(2,1)S(1)} %pad_maximum_fusion.refs_4_), channel_id=1, source_target_pairs={{0,1},{1,0},{2,3},{3,2},{4,5},{5,4},{6,7},{7,6},{8,9},{9,8},{10,11... | collective-permute-start | bytes 393224 | tf_op jit(solution)/shard_map/ppermute | solution.py:183
  21.3 0.8 %collective-permute-done.9.refs_5_ = bf16[16,4096]{1,0:T(8,128)(2,1)S(1)} collective-permute-done((bf16[16,4096]{1,0:T(8,128)(2,1)S(1)}, bf16[16,4096]{1,0:T(8,128)(2,1)S(1)}, u32[]{:S(2)}, u32[]{:S(2)}) %collective-permute-start.9) | collective-permute-done | bytes 131104 | tf_op jit(solution)/shard_map/ppermute | solution.py:183
  22.1 0.0 collective-permute-done.7.refs_3_
  22.1 0.7 %shard_map.57 = (f32[128,224]{1,0:T(8,128)S(1)}, f32[128,224]{1,0:T(8,128)S(1)}) custom-call(bf16[8192,224]{1,0:T(8,128)(2,1)S(1)} %shard_map.55.refs_0_, bf16[8192,224]{1,0:T(8,128)(2,1)S(1)} %get-tuple-element.40.refs_1_, bf16[48,8192]{1,0:T(8,128)(2,1)S(1)} %constant_dynamic-update-slice_fusion.refs_2_, ...), custom_call_target="tpu_custom_call" | custom-call | flops 469762048 | bytes 3670016 | tf_op jit(solution)/shard_map/pallas_call | solution.py:91
  22.8 0.0 collective-permute-done.8.refs_5_
  22.8 0.7 %shard_map.58.hidden_ref = bf16[128,224]{1,0:T(8,128)(2,1)S(1)} custom-call(bf16[8192,224]{1,0:T(8,128)(2,1)S(1)} %shard_map.55.refs_0_, bf16[8192,224]{1,0:T(8,128)(2,1)S(1)} %get-tuple-element.40.refs_1_, bf16[48,8192]{1,0:T(8,128)(2,1)S(1)} %constant_dynamic-update-slice_fusion.refs_2_, bf16[48,8192]{1,0:T(8,128)(2,1)S(1)} %collective-permute-done.7.refs_3_, ...), custom_call_target="tpu_custom_call" | custom-call | flops 469762048 | bytes 3670016 | tf_op jit(solution)/shard_map/pallas_call | solution.py:91
  23.6 0.7 %shard_map.59 = (f32[32,8192]{1,0:T(8,128)S(1)}, f32[8,8192]{1,0:T(8,128)S(1)}, f32[24,8192]{1,0:T(8,128)S(1)}, bf16[32,8192]{1,0:T(8,128)(2,1)S(1)}, bf16[8,819...) custom-call(bf16[128,224]{1,0:T(8,128)(2,1)S(1)} %shard_map.58.hidden_ref, bf16[224,8192]{1,0:T(8,128)(2,1)S(1)} %get-tuple-element.46.down_ref), custom_call_target="tpu_custom_call" | custom-call | flops 469762048 | bytes 3670016 | tf_op jit(solution)/shard_map/pallas_call | solution.py:120
  24.3 0.2 collective-permute-start.13
  24.5 0.4 collective-permute-start.10
  24.9 0.8 %collective-permute-done.13 = bf16[8,8192]{1,0:T(8,128)(2,1)S(1)} collective-permute-done((bf16[8,8192]{1,0:T(8,128)(2,1)S(1)}, bf16[8,8192]{1,0:T(8,128)(2,1)S(1)}, u32[]{:S(2)}, u32[]{:S(2)}) %collective-permute-start.13) | collective-permute-done | bytes 131104 | tf_op jit(solution)/shard_map/ppermute | solution.py:183
  25.8 1.8 %collective-permute-start.14 = (bf16[8,8192]{1,0:T(8,128)(2,1)S(1)}, bf16[8,8192]{1,0:T(8,128)(2,1)S(1)}, u32[]{:S(2)}, u32[]{:S(2)}) collective-permute-start(bf16[8,8192]{1,0:T(8,128)(2,1)S(1)} %add_convert_fusion), channel_id=1, source_target_pairs={{0,6},{1,7},{2,4},{3,5},{4,2},{5,3},{6,0},{7,1},{8,14},{9,15},{10,... | collective-permute-start | bytes 393224 | tf_op jit(solution)/shard_map/ppermute | solution.py:183
  27.6 0.0 collective-permute-done.10
  27.6 0.0 collective-permute-start.11
  27.6 0.1 fusion.7
  27.7 0.0 copy-start
  27.7 0.8 %collective-permute-start.15 = (bf16[8,8192]{1,0:T(8,128)(2,1)S(1)}, bf16[8,8192]{1,0:T(8,128)(2,1)S(1)}, u32[]{:S(2)}, u32[]{:S(2)}) collective-permute-start(bf16[8,8192]{1,0:T(8,128)(2,1)S(1)} %get-tuple-element.57), channel_id=1, source_target_pairs={{0,4},{1,3},{2,6},{3,1},{4,0},{5,7},{6,2},{7,5},{8,12},{9,11},{10,... | collective-permute-start | bytes 393224 | tf_op jit(solution)/shard_map/ppermute | solution.py:183
  28.5 1.0 %collective-permute-start.16 = (bf16[8,8192]{1,0:T(8,128)(2,1)S(1)}, bf16[8,8192]{1,0:T(8,128)(2,1)S(1)}, u32[]{:S(2)}, u32[]{:S(2)}) collective-permute-start(bf16[8,8192]{1,0:T(8,128)(2,1)S(1)} %get-tuple-element.58), channel_id=1, source_target_pairs={{0,2},{1,5},{2,0},{3,7},{4,6},{5,1},{6,4},{7,3},{8,10},{9,13},{10,... | collective-permute-start | bytes 393224 | tf_op jit(solution)/shard_map/ppermute | solution.py:183
  29.5 0.0 collective-permute-done.11
  29.5 0.1 convert_add_fusion
  29.6 1.2 %collective-permute-start.12 = (bf16[16,8192]{1,0:T(8,128)(2,1)S(1)}, bf16[16,8192]{1,0:T(8,128)(2,1)S(1)}, u32[]{:S(2)}, u32[]{:S(2)}) collective-permute-start(bf16[16,8192]{1,0:T(8,128)(2,1)S(1)} %slice.67), channel_id=1, source_target_pairs={{0,4},{1,3},{2,6},{3,1},{4,0},{5,7},{6,2},{7,5},{8,12},{9,11},{10,... | collective-permute-start | bytes 786440 | tf_op jit(solution)/shard_map/ppermute | solution.py:183
  30.9 1.6 %collective-permute-done.14 = bf16[8,8192]{1,0:T(8,128)(2,1)S(1)} collective-permute-done((bf16[8,8192]{1,0:T(8,128)(2,1)S(1)}, bf16[8,8192]{1,0:T(8,128)(2,1)S(1)}, u32[]{:S(2)}, u32[]{:S(2)}) %collective-permute-start.14) | collective-permute-done | bytes 131104 | tf_op jit(solution)/shard_map/ppermute | solution.py:183
  32.4 2.2 %collective-permute-done.15 = bf16[8,8192]{1,0:T(8,128)(2,1)S(1)} collective-permute-done((bf16[8,8192]{1,0:T(8,128)(2,1)S(1)}, bf16[8,8192]{1,0:T(8,128)(2,1)S(1)}, u32[]{:S(2)}, u32[]{:S(2)}) %collective-permute-start.15) | collective-permute-done | bytes 131104 | tf_op jit(solution)/shard_map/ppermute | solution.py:183
  34.6 0.6 %collective-permute-done.16 = bf16[8,8192]{1,0:T(8,128)(2,1)S(1)} collective-permute-done((bf16[8,8192]{1,0:T(8,128)(2,1)S(1)}, bf16[8,8192]{1,0:T(8,128)(2,1)S(1)}, u32[]{:S(2)}, u32[]{:S(2)}) %collective-permute-start.16) | collective-permute-done | bytes 131104 | tf_op jit(solution)/shard_map/ppermute | solution.py:183
  35.2 0.1 fusion.2
  35.2 3.0 %collective-permute-start.17 = (bf16[8,8192]{1,0:T(8,128)(2,1)S(1)}, bf16[8,8192]{1,0:T(8,128)(2,1)S(1)}, u32[]{:S(2)}, u32[]{:S(2)}) collective-permute-start(bf16[8,8192]{1,0:T(8,128)(2,1)S(1)} %fusion.2), channel_id=1, source_target_pairs={{0,12},{1,9},{2,14},{3,11},{4,8},{5,13},{6,10},{7,15},{8,4},{9,1},... | collective-permute-start | bytes 393224 | tf_op jit(solution)/shard_map/ppermute | solution.py:183
  38.2 0.0 collective-permute-done.12
  38.2 0.1 slice_add_fusion
  38.3 1.1 %collective-permute-start.18 = (bf16[8,8192]{1,0:T(8,128)(2,1)S(1)}, bf16[8,8192]{1,0:T(8,128)(2,1)S(1)}, u32[]{:S(2)}, u32[]{:S(2)}) collective-permute-start(bf16[8,8192]{1,0:T(8,128)(2,1)S(1)} %slice.68), channel_id=1, source_target_pairs={{0,2},{1,5},{2,0},{3,7},{4,6},{5,1},{6,4},{7,3},{8,10},{9,13},{10,... | collective-permute-start | bytes 393224 | tf_op jit(solution)/shard_map/ppermute | solution.py:183
  39.5 2.9 %collective-permute-done.17.refs_1_ = bf16[8,8192]{1,0:T(8,128)(2,1)S(1)} collective-permute-done((bf16[8,8192]{1,0:T(8,128)(2,1)S(1)}, bf16[8,8192]{1,0:T(8,128)(2,1)S(1)}, u32[]{:S(2)}, u32[]{:S(2)}) %collective-permute-start.17) | collective-permute-done | bytes 131104 | tf_op jit(solution)/shard_map/ppermute | solution.py:183
  42.4 1.0 %collective-permute-done.18.refs_2_ = bf16[8,8192]{1,0:T(8,128)(2,1)S(1)} collective-permute-done((bf16[8,8192]{1,0:T(8,128)(2,1)S(1)}, bf16[8,8192]{1,0:T(8,128)(2,1)S(1)}, u32[]{:S(2)}, u32[]{:S(2)}) %collective-permute-start.18) | collective-permute-done | bytes 131104 | tf_op jit(solution)/shard_map/ppermute | solution.py:183
  43.4 0.0 copy-done
  43.4 0.9 %shard_map.60 = bf16[8,8192]{1,0:T(8,128)(2,1)} custom-call(f32[8,8192]{1,0:T(8,128)S(1)} %slice.52.refs_0_, bf16[8,8192]{1,0:T(8,128)(2,1)S(1)} %collective-permute-done.17.refs_1_, bf16[8,8192]{1,0:T(8,128)(2,1)S(1)} %collective-permute-done.18.refs_2_, s32[1,8192]{1,0:T(1,128)S(1)} %bitcast.3, bf16[256,128]{1,0:T(8,128)(2,1)S(1)} %pad_maximum_fusion.2.refs_4_), custom_call_target="tpu_custom_call" | custom-call | tf_op jit(solution)/shard_map/pallas_call | solution.py:160
  (16 shorter events, 0.3 us)
Async XLA Ops:
  0.0 11.2 %collective-permute-start = (bf16[8,8192]{1,0:T(8,128)(2,1)}, bf16[8,8192]{1,0:T(8,128)(2,1)S(1)}, u32[]{:S(2)}, u32[]{:S(2)}) collective-permute-start(bf16[8,8192]{1,0:T(8,128)(2,1)} %param.5), channel_id=1, source_target_pairs={{0,12},{1,9},{2,14},{3,11},{4,8},{5,13},{6,10},{7,15},{8,4},{9,1},... | collective-permute-start | bytes 393224 | tf_op jit(solution)/shard_map/ppermute | solution.py:183
  5.0 9.2 %collective-permute-start.1 = (bf16[8,8192]{1,0:T(8,128)(2,1)}, bf16[8,8192]{1,0:T(8,128)(2,1)S(1)}, u32[]{:S(2)}, u32[]{:S(2)}) collective-permute-start(bf16[8,8192]{1,0:T(8,128)(2,1)} %param.5), channel_id=1, source_target_pairs={{0,4},{1,3},{2,6},{3,1},{4,0},{5,7},{6,2},{7,5},{8,12},{9,11},{10,... | collective-permute-start | bytes 393224 | tf_op jit(solution)/shard_map/ppermute | solution.py:183
  5.1 13.0 %collective-permute-start.3 = (bf16[8,8192]{1,0:T(8,128)(2,1)}, bf16[8,8192]{1,0:T(8,128)(2,1)S(1)}, u32[]{:S(2)}, u32[]{:S(2)}) collective-permute-start(bf16[8,8192]{1,0:T(8,128)(2,1)} %param.5), channel_id=1, source_target_pairs={{0,2},{1,5},{2,0},{3,7},{4,6},{5,1},{6,4},{7,3},{8,10},{9,13},{10,... | collective-permute-start | bytes 393224 | tf_op jit(solution)/shard_map/ppermute | solution.py:183
  6.6 11.5 %collective-permute-start.4 = (bf16[8,8192]{1,0:T(8,128)(2,1)}, bf16[8,8192]{1,0:T(8,128)(2,1)S(1)}, u32[]{:S(2)}, u32[]{:S(2)}) collective-permute-start(bf16[8,8192]{1,0:T(8,128)(2,1)} %param.5), channel_id=1, source_target_pairs={{0,6},{1,7},{2,4},{3,5},{4,2},{5,3},{6,0},{7,1},{8,14},{9,15},{10,... | collective-permute-start | bytes 393224 | tf_op jit(solution)/shard_map/ppermute | solution.py:183
  11.2 6.9 %collective-permute-start.2 = (bf16[8,8192]{1,0:T(8,128)(2,1)S(1)}, bf16[8,8192]{1,0:T(8,128)(2,1)S(1)}, u32[]{:S(2)}, u32[]{:S(2)}) collective-permute-start(bf16[8,8192]{1,0:T(8,128)(2,1)S(1)} %collective-permute-done.refs_2_), channel_id=1, source_target_pairs={{0,4},{1,3},{2,6},{3,1},{4,0},{5,7},{6,2},{7,5},{8,12},{9,11},{10,... | collective-permute-start | bytes 393224 | tf_op jit(solution)/shard_map/ppermute | solution.py:183
  11.4 9.3 %collective-permute-start.6 = (bf16[8,8192]{1,0:T(8,128)(2,1)S(1)}, bf16[8,8192]{1,0:T(8,128)(2,1)S(1)}, u32[]{:S(2)}, u32[]{:S(2)}) collective-permute-start(bf16[8,8192]{1,0:T(8,128)(2,1)S(1)} %collective-permute-done.refs_2_), channel_id=1, source_target_pairs={{0,6},{1,7},{2,4},{3,5},{4,2},{5,3},{6,0},{7,1},{8,14},{9,15},{10,... | collective-permute-start | bytes 393224 | tf_op jit(solution)/shard_map/ppermute | solution.py:183
  14.3 5.5 %collective-permute-start.5 = (bf16[8,8192]{1,0:T(8,128)(2,1)S(1)}, bf16[8,8192]{1,0:T(8,128)(2,1)S(1)}, u32[]{:S(2)}, u32[]{:S(2)}) collective-permute-start(bf16[8,8192]{1,0:T(8,128)(2,1)S(1)} %collective-permute-done.refs_2_), channel_id=1, source_target_pairs={{0,2},{1,5},{2,0},{3,7},{4,6},{5,1},{6,4},{7,3},{8,10},{9,13},{10,... | collective-permute-start | bytes 393224 | tf_op jit(solution)/shard_map/ppermute | solution.py:183
  14.8 3.4 %copy-start.1 = (bf16[8,8192]{1,0:T(8,128)(2,1)S(1)}, bf16[8,8192]{1,0:T(8,128)(2,1)}, u32[]{:S(2)}) copy-start(bf16[8,8192]{1,0:T(8,128)(2,1)} %param.5) | copy-start | bytes 393220
  18.2 3.9 %collective-permute-start.7 = (bf16[48,8192]{1,0:T(8,128)(2,1)S(1)}, bf16[48,8192]{1,0:T(8,128)(2,1)S(1)}, u32[]{:S(2)}, u32[]{:S(2)}) collective-permute-start(bf16[48,8192]{1,0:T(8,128)(2,1)S(1)} %constant_dynamic-update-slice_fusion.refs_2_), channel_id=1, source_target_pairs={{0,1},{1,0},{2,3},{3,2},{4,5},{5,4},{6,7},{7,6},{8,9},{9,8},{10,11... | collective-permute-start | bytes 2359304 | tf_op jit(solution)/shard_map/ppermute | solution.py:183
  20.7 1.4 %collective-permute-start.9 = (bf16[16,4096]{1,0:T(8,128)(2,1)S(1)}, bf16[16,4096]{1,0:T(8,128)(2,1)S(1)}, u32[]{:S(2)}, u32[]{:S(2)}) collective-permute-start(bf16[16,4096]{1,0:T(8,128)(2,1)S(1)} %pad_maximum_fusion.1.refs_4_), channel_id=1, source_target_pairs={{0,1},{1,0},{2,3},{3,2},{4,5},{5,4},{6,7},{7,6},{8,9},{9,8},{10,11... | collective-permute-start | bytes 393224 | tf_op jit(solution)/shard_map/ppermute | solution.py:183
  20.8 2.0 %collective-permute-start.8 = (bf16[16,4096]{1,0:T(8,128)(2,1)S(1)}, bf16[16,4096]{1,0:T(8,128)(2,1)S(1)}, u32[]{:S(2)}, u32[]{:S(2)}) collective-permute-start(bf16[16,4096]{1,0:T(8,128)(2,1)S(1)} %pad_maximum_fusion.refs_4_), channel_id=1, source_target_pairs={{0,1},{1,0},{2,3},{3,2},{4,5},{5,4},{6,7},{7,6},{8,9},{9,8},{10,11... | collective-permute-start | bytes 393224 | tf_op jit(solution)/shard_map/ppermute | solution.py:183
  24.3 1.4 %collective-permute-start.13 = (bf16[8,8192]{1,0:T(8,128)(2,1)S(1)}, bf16[8,8192]{1,0:T(8,128)(2,1)S(1)}, u32[]{:S(2)}, u32[]{:S(2)}) collective-permute-start(bf16[8,8192]{1,0:T(8,128)(2,1)S(1)} %get-tuple-element.54), channel_id=1, source_target_pairs={{0,1},{1,0},{2,3},{3,2},{4,5},{5,4},{6,7},{7,6},{8,9},{9,8},{10,11... | collective-permute-start | bytes 393224 | tf_op jit(solution)/shard_map/ppermute | solution.py:183
  24.5 3.0 %collective-permute-start.10 = (bf16[24,8192]{1,0:T(8,128)(2,1)S(1)}, bf16[24,8192]{1,0:T(8,128)(2,1)S(1)}, u32[]{:S(2)}, u32[]{:S(2)}) collective-permute-start(bf16[24,8192]{1,0:T(8,128)(2,1)S(1)} %get-tuple-element.48), channel_id=1, source_target_pairs={{0,1},{1,0},{2,3},{3,2},{4,5},{5,4},{6,7},{7,6},{8,9},{9,8},{10,11... | collective-permute-start | bytes 1179656 | tf_op jit(solution)/shard_map/ppermute | solution.py:183
  25.8 6.7 %collective-permute-start.14 = (bf16[8,8192]{1,0:T(8,128)(2,1)S(1)}, bf16[8,8192]{1,0:T(8,128)(2,1)S(1)}, u32[]{:S(2)}, u32[]{:S(2)}) collective-permute-start(bf16[8,8192]{1,0:T(8,128)(2,1)S(1)} %add_convert_fusion), channel_id=1, source_target_pairs={{0,6},{1,7},{2,4},{3,5},{4,2},{5,3},{6,0},{7,1},{8,14},{9,15},{10,... | collective-permute-start | bytes 393224 | tf_op jit(solution)/shard_map/ppermute | solution.py:183
  27.6 1.9 %collective-permute-start.11 = (bf16[32,8192]{1,0:T(8,128)(2,1)S(1)}, bf16[32,8192]{1,0:T(8,128)(2,1)S(1)}, u32[]{:S(2)}, u32[]{:S(2)}) collective-permute-start(bf16[32,8192]{1,0:T(8,128)(2,1)S(1)} %get-tuple-element.50), channel_id=1, source_target_pairs={{0,1},{1,0},{2,3},{3,2},{4,5},{5,4},{6,7},{7,6},{8,9},{9,8},{10,11... | collective-permute-start | bytes 1572872 | tf_op jit(solution)/shard_map/ppermute | solution.py:183
  27.7 15.7 %copy-start = (s32[8192]{0:T(1024)S(1)}, s32[8192]{0:T(1024)}, u32[]{:S(2)}) copy-start(s32[8192]{0:T(1024)} %param.9) | copy-start | bytes 98308
  27.7 6.9 %collective-permute-start.15 = (bf16[8,8192]{1,0:T(8,128)(2,1)S(1)}, bf16[8,8192]{1,0:T(8,128)(2,1)S(1)}, u32[]{:S(2)}, u32[]{:S(2)}) collective-permute-start(bf16[8,8192]{1,0:T(8,128)(2,1)S(1)} %get-tuple-element.57), channel_id=1, source_target_pairs={{0,4},{1,3},{2,6},{3,1},{4,0},{5,7},{6,2},{7,5},{8,12},{9,11},{10,... | collective-permute-start | bytes 393224 | tf_op jit(solution)/shard_map/ppermute | solution.py:183
  28.5 6.7 %collective-permute-start.16 = (bf16[8,8192]{1,0:T(8,128)(2,1)S(1)}, bf16[8,8192]{1,0:T(8,128)(2,1)S(1)}, u32[]{:S(2)}, u32[]{:S(2)}) collective-permute-start(bf16[8,8192]{1,0:T(8,128)(2,1)S(1)} %get-tuple-element.58), channel_id=1, source_target_pairs={{0,2},{1,5},{2,0},{3,7},{4,6},{5,1},{6,4},{7,3},{8,10},{9,13},{10,... | collective-permute-start | bytes 393224 | tf_op jit(solution)/shard_map/ppermute | solution.py:183
  29.6 8.6 %collective-permute-start.12 = (bf16[16,8192]{1,0:T(8,128)(2,1)S(1)}, bf16[16,8192]{1,0:T(8,128)(2,1)S(1)}, u32[]{:S(2)}, u32[]{:S(2)}) collective-permute-start(bf16[16,8192]{1,0:T(8,128)(2,1)S(1)} %slice.67), channel_id=1, source_target_pairs={{0,4},{1,3},{2,6},{3,1},{4,0},{5,7},{6,2},{7,5},{8,12},{9,11},{10,... | collective-permute-start | bytes 786440 | tf_op jit(solution)/shard_map/ppermute | solution.py:183
  35.2 7.2 %collective-permute-start.17 = (bf16[8,8192]{1,0:T(8,128)(2,1)S(1)}, bf16[8,8192]{1,0:T(8,128)(2,1)S(1)}, u32[]{:S(2)}, u32[]{:S(2)}) collective-permute-start(bf16[8,8192]{1,0:T(8,128)(2,1)S(1)} %fusion.2), channel_id=1, source_target_pairs={{0,12},{1,9},{2,14},{3,11},{4,8},{5,13},{6,10},{7,15},{8,4},{9,1},... | collective-permute-start | bytes 393224 | tf_op jit(solution)/shard_map/ppermute | solution.py:183
  38.3 5.0 %collective-permute-start.18 = (bf16[8,8192]{1,0:T(8,128)(2,1)S(1)}, bf16[8,8192]{1,0:T(8,128)(2,1)S(1)}, u32[]{:S(2)}, u32[]{:S(2)}) collective-permute-start(bf16[8,8192]{1,0:T(8,128)(2,1)S(1)} %slice.68), channel_id=1, source_target_pairs={{0,2},{1,5},{2,0},{3,7},{4,6},{5,1},{6,4},{7,3},{8,10},{9,13},{10,... | collective-permute-start | bytes 393224 | tf_op jit(solution)/shard_map/ppermute | solution.py:183

commit v31 on v29

--- a/solution.py
+++ b/solution.py
@@ -211,7 +211,7 @@
         count = others * rows
         ends = [3 * rows, 3 * rows + count, 3 * rows + 2 * count, 4 * rows + 2 * count]
         ends += [ends[3] + count, ends[3] + 2 * count]
-        own_rows = ((ends[2], ends[3]), (0, ends[0]))
+        own_rows = ((ends[2], ends[3]), (rows, 2 * rows), (0, rows), (2 * rows, ends[0]))
         rest_rows = ((ends[0], ends[2]), (ends[4], ends[5]))
         own, diagonal, rest, *sends = down(hidden, down_w, (own_rows, ((ends[3], ends[4]),), rest_rows))
         diagonal = diagonal + swap(sends[1], (1, 1)).astype(jnp.float32)
@@ -230,8 +230,8 @@
             total = total[:split] + piece[rows:].astype(jnp.float32)
 
         own = own + swap(sends[0], (1, 1)).astype(jnp.float32)
-        own = own[: 2 * rows] + swap(own[2 * rows :].astype(jnp.bfloat16), square[0]).astype(jnp.float32)
-        arrived.append(swap(own[rows:].astype(jnp.bfloat16), square[1]))
+        own = own[: 2 * rows] + swap(own[2 * rows :].astype(jnp.bfloat16), square[1]).astype(jnp.float32)
+        arrived.append(swap(own[rows:].astype(jnp.bfloat16), square[0]))
         return rotate(own[:rows], arrived, sign_pattern)
 
     placed = (P(("groups", "gx"), None), P(None, "gx"), P(None, "gx"), P("gx", None), P())

time: 44.3 us -> 45.2 us (1.020)
  waiting for transfers between devices: 11.9 us -> 13.1 us
    ppermute x19, waiting for transfers between devices: 11.9 us -> 13.1 us  [swap(): lax.ppermute(value, 'gx', [(i, i ^ masks[i % 2]) for i in range(members)])]
  transfers between devices with their start and end apart: 19 -> 19, of which waited for: 9 -> 8; matrix products, arithmetic and copies ran while one was open for 1% -> 1% of each run, Pallas kernels for 15% -> 15%
where the time goes in v31:
time: 45.2 us; the launch traced here: 45.1 us
  starting transfers between devices  22.1 us (49%)
  waiting for transfers between devices  13.1 us (29%)
  Pallas kernels  9.02 us (20%)
    ppermute x19, starting transfers between devices, swap(): lax.ppermute(value, 'gx', [(i, i ^ masks[i % 2]) for i in range(members)])  22.1 us
    ppermute x19, waiting for transfers between devices, swap(): lax.ppermute(value, 'gx', [(i, i ^ masks[i % 2]) for i in range(members)])  13.1 us
    pallas_call x2, Pallas kernels, load(): pl.pallas_call(functools.partial(load_kernel, turned), out_shape=[jax.Sha...  5.96 us
    pallas_call x2, Pallas kernels, hidden_units(): pl.pallas_call(functools.partial(hidden_kernel, start, last), out_shape=(...  1.45 us
  transfers between devices with their start and end apart: 19, of which 8 were waited for; matrix products, arithmetic and copies ran while one was open for 1% of the time, Pallas kernels for 15%

profile of v31, /device:TPU:0, one launch (start us, length us, event | category | flops | bytes accessed | tf_op | source)
XLA Modules:
  0.0 45.1 jit_solution(6017266701778847654)
XLA Ops:
  0.0 5.0 %collective-permute-start = (bf16[8,8192]{1,0:T(8,128)(2,1)}, bf16[8,8192]{1,0:T(8,128)(2,1)S(1)}, u32[]{:S(2)}, u32[]{:S(2)}) collective-permute-start(bf16[8,8192]{1,0:T(8,128)(2,1)} %param.5), channel_id=1, source_target_pairs={{0,12},{1,9},{2,14},{3,11},{4,8},{5,13},{6,10},{7,15},{8,4},{9,1},... | collective-permute-start | bytes 393224 | tf_op jit(solution)/shard_map/ppermute | solution.py:183
  5.0 0.0 collective-permute-start.1
  5.1 1.5 %collective-permute-start.3 = (bf16[8,8192]{1,0:T(8,128)(2,1)}, bf16[8,8192]{1,0:T(8,128)(2,1)S(1)}, u32[]{:S(2)}, u32[]{:S(2)}) collective-permute-start(bf16[8,8192]{1,0:T(8,128)(2,1)} %param.5), channel_id=1, source_target_pairs={{0,2},{1,5},{2,0},{3,7},{4,6},{5,1},{6,4},{7,3},{8,10},{9,13},{10,... | collective-permute-start | bytes 393224 | tf_op jit(solution)/shard_map/ppermute | solution.py:183
  6.6 2.0 %collective-permute-start.4 = (bf16[8,8192]{1,0:T(8,128)(2,1)}, bf16[8,8192]{1,0:T(8,128)(2,1)S(1)}, u32[]{:S(2)}, u32[]{:S(2)}) collective-permute-start(bf16[8,8192]{1,0:T(8,128)(2,1)} %param.5), channel_id=1, source_target_pairs={{0,6},{1,7},{2,4},{3,5},{4,2},{5,3},{6,0},{7,1},{8,14},{9,15},{10,... | collective-permute-start | bytes 393224 | tf_op jit(solution)/shard_map/ppermute | solution.py:183
  8.5 2.7 %shard_map.55.refs_0_ = bf16[8192,224]{1,0:T(8,128)(2,1)S(1)} custom-call(bf16[224,8192]{1,0:T(8,128)(2,1)} %bitcast.4, bf16[224,8192]{1,0:T(8,128)(2,1)} %bitcast.5), custom_call_target="tpu_custom_call" | custom-call | bytes 7340032 | tf_op jit(solution)/shard_map/pallas_call | solution.py:52
  11.2 0.0 collective-permute-done.refs_2_
  11.2 0.2 collective-permute-start.2
  11.4 1.5 %collective-permute-start.5 = (bf16[8,8192]{1,0:T(8,128)(2,1)S(1)}, bf16[8,8192]{1,0:T(8,128)(2,1)S(1)}, u32[]{:S(2)}, u32[]{:S(2)}) collective-permute-start(bf16[8,8192]{1,0:T(8,128)(2,1)S(1)} %collective-permute-done.refs_2_), channel_id=1, source_target_pairs={{0,2},{1,5},{2,0},{3,7},{4,6},{5,1},{6,4},{7,3},{8,10},{9,13},{10,... | collective-permute-start | bytes 393224 | tf_op jit(solution)/shard_map/ppermute | solution.py:183
  12.9 0.0 collective-permute-done.1
  12.9 1.9 %collective-permute-start.6 = (bf16[8,8192]{1,0:T(8,128)(2,1)S(1)}, bf16[8,8192]{1,0:T(8,128)(2,1)S(1)}, u32[]{:S(2)}, u32[]{:S(2)}) collective-permute-start(bf16[8,8192]{1,0:T(8,128)(2,1)S(1)} %collective-permute-done.refs_2_), channel_id=1, source_target_pairs={{0,6},{1,7},{2,4},{3,5},{4,2},{5,3},{6,0},{7,1},{8,14},{9,15},{10,... | collective-permute-start | bytes 393224 | tf_op jit(solution)/shard_map/ppermute | solution.py:183
  14.8 0.0 copy-start.1
  14.8 3.3 %shard_map.56 = (bf16[8192,224]{1,0:T(8,128)(2,1)S(1)}, bf16[224,8192]{1,0:T(8,128)(2,1)S(1)}) custom-call(bf16[224,8192]{1,0:T(8,128)(2,1)} %bitcast.6, bf16[224,8192]{1,0:T(8,128)(2,1)} %refs_1_.1, bf16[8,8192]{1,0:T(8,128)(2,1)S(1)} %collective-permute-done.refs_2_), custom_call_target="tpu_custom_call" | custom-call | bytes 14680064 | tf_op jit(solution)/shard_map/pallas_call | solution.py:52
  18.1 0.0 collective-permute-done.3
  18.1 0.0 collective-permute-done.4
  18.1 0.0 collective-permute-done.2
  18.2 0.0 copy-done.1
  18.2 0.1 collective-permute-start.7
  18.3 2.2 %collective-permute-done.6 = bf16[8,8192]{1,0:T(8,128)(2,1)S(1)} collective-permute-done((bf16[8,8192]{1,0:T(8,128)(2,1)S(1)}, bf16[8,8192]{1,0:T(8,128)(2,1)S(1)}, u32[]{:S(2)}, u32[]{:S(2)}) %collective-permute-start.6) | collective-permute-done | bytes 131104 | tf_op jit(solution)/shard_map/ppermute | solution.py:183
  20.5 0.0 collective-permute-done.5
  20.6 0.1 collective-permute-start.9
  20.7 0.6 %collective-permute-start.8 = (bf16[16,4096]{1,0:T(8,128)(2,1)S(1)}, bf16[16,4096]{1,0:T(8,128)(2,1)S(1)}, u32[]{:S(2)}, u32[]{:S(2)}) collective-permute-start(bf16[16,4096]{1,0:T(8,128)(2,1)S(1)} %pad_maximum_fusion.refs_4_), channel_id=1, source_target_pairs={{0,1},{1,0},{2,3},{3,2},{4,5},{5,4},{6,7},{7,6},{8,9},{9,8},{10,11... | collective-permute-start | bytes 393224 | tf_op jit(solution)/shard_map/ppermute | solution.py:183
  21.2 0.8 %collective-permute-done.9.refs_5_ = bf16[16,4096]{1,0:T(8,128)(2,1)S(1)} collective-permute-done((bf16[16,4096]{1,0:T(8,128)(2,1)S(1)}, bf16[16,4096]{1,0:T(8,128)(2,1)S(1)}, u32[]{:S(2)}, u32[]{:S(2)}) %collective-permute-start.9) | collective-permute-done | bytes 131104 | tf_op jit(solution)/shard_map/ppermute | solution.py:183
  22.0 0.0 collective-permute-done.7.refs_3_
  22.0 0.7 %shard_map.57 = (f32[128,224]{1,0:T(8,128)S(1)}, f32[128,224]{1,0:T(8,128)S(1)}) custom-call(bf16[8192,224]{1,0:T(8,128)(2,1)S(1)} %shard_map.55.refs_0_, bf16[8192,224]{1,0:T(8,128)(2,1)S(1)} %get-tuple-element.40.refs_1_, bf16[48,8192]{1,0:T(8,128)(2,1)S(1)} %constant_dynamic-update-slice_fusion.refs_2_, ...), custom_call_target="tpu_custom_call" | custom-call | flops 469762048 | bytes 3670016 | tf_op jit(solution)/shard_map/pallas_call | solution.py:91
  22.7 0.0 collective-permute-done.8.refs_5_
  22.7 0.7 %shard_map.58.hidden_ref = bf16[128,224]{1,0:T(8,128)(2,1)S(1)} custom-call(bf16[8192,224]{1,0:T(8,128)(2,1)S(1)} %shard_map.55.refs_0_, bf16[8192,224]{1,0:T(8,128)(2,1)S(1)} %get-tuple-element.40.refs_1_, bf16[48,8192]{1,0:T(8,128)(2,1)S(1)} %constant_dynamic-update-slice_fusion.refs_2_, bf16[48,8192]{1,0:T(8,128)(2,1)S(1)} %collective-permute-done.7.refs_3_, ...), custom_call_target="tpu_custom_call" | custom-call | flops 469762048 | bytes 3670016 | tf_op jit(solution)/shard_map/pallas_call | solution.py:91
  23.4 0.7 %shard_map.59 = (f32[32,8192]{1,0:T(8,128)S(1)}, f32[8,8192]{1,0:T(8,128)S(1)}, f32[24,8192]{1,0:T(8,128)S(1)}, bf16[32,8192]{1,0:T(8,128)(2,1)S(1)}, bf16[8,819...) custom-call(bf16[128,224]{1,0:T(8,128)(2,1)S(1)} %shard_map.58.hidden_ref, bf16[224,8192]{1,0:T(8,128)(2,1)S(1)} %get-tuple-element.46.down_ref), custom_call_target="tpu_custom_call" | custom-call | flops 469762048 | bytes 3670016 | tf_op jit(solution)/shard_map/pallas_call | solution.py:120
  24.2 0.2 collective-permute-start.13
  24.4 0.4 collective-permute-start.10
  24.7 0.8 %collective-permute-done.13 = bf16[8,8192]{1,0:T(8,128)(2,1)S(1)} collective-permute-done((bf16[8,8192]{1,0:T(8,128)(2,1)S(1)}, bf16[8,8192]{1,0:T(8,128)(2,1)S(1)}, u32[]{:S(2)}, u32[]{:S(2)}) %collective-permute-start.13) | collective-permute-done | bytes 131104 | tf_op jit(solution)/shard_map/ppermute | solution.py:183
  25.6 2.0 %collective-permute-start.14 = (bf16[8,8192]{1,0:T(8,128)(2,1)S(1)}, bf16[8,8192]{1,0:T(8,128)(2,1)S(1)}, u32[]{:S(2)}, u32[]{:S(2)}) collective-permute-start(bf16[8,8192]{1,0:T(8,128)(2,1)S(1)} %add_convert_fusion), channel_id=1, source_target_pairs={{0,6},{1,7},{2,4},{3,5},{4,2},{5,3},{6,0},{7,1},{8,14},{9,15},{10,... | collective-permute-start | bytes 393224 | tf_op jit(solution)/shard_map/ppermute | solution.py:183
  27.6 0.0 collective-permute-done.10
  27.6 0.0 collective-permute-start.11
  27.6 0.1 fusion.7
  27.7 0.0 copy-start
  27.7 0.8 %collective-permute-start.15 = (bf16[8,8192]{1,0:T(8,128)(2,1)S(1)}, bf16[8,8192]{1,0:T(8,128)(2,1)S(1)}, u32[]{:S(2)}, u32[]{:S(2)}) collective-permute-start(bf16[8,8192]{1,0:T(8,128)(2,1)S(1)} %get-tuple-element.57), channel_id=1, source_target_pairs={{0,4},{1,3},{2,6},{3,1},{4,0},{5,7},{6,2},{7,5},{8,12},{9,11},{10,... | collective-permute-start | bytes 393224 | tf_op jit(solution)/shard_map/ppermute | solution.py:183
  28.5 0.9 %collective-permute-start.16 = (bf16[8,8192]{1,0:T(8,128)(2,1)S(1)}, bf16[8,8192]{1,0:T(8,128)(2,1)S(1)}, u32[]{:S(2)}, u32[]{:S(2)}) collective-permute-start(bf16[8,8192]{1,0:T(8,128)(2,1)S(1)} %get-tuple-element.58), channel_id=1, source_target_pairs={{0,2},{1,5},{2,0},{3,7},{4,6},{5,1},{6,4},{7,3},{8,10},{9,13},{10,... | collective-permute-start | bytes 393224 | tf_op jit(solution)/shard_map/ppermute | solution.py:183
  29.4 0.1 collective-permute-done.11
  29.5 0.1 convert_add_fusion
  29.6 1.1 %collective-permute-start.12 = (bf16[16,8192]{1,0:T(8,128)(2,1)S(1)}, bf16[16,8192]{1,0:T(8,128)(2,1)S(1)}, u32[]{:S(2)}, u32[]{:S(2)}) collective-permute-start(bf16[16,8192]{1,0:T(8,128)(2,1)S(1)} %slice.67), channel_id=1, source_target_pairs={{0,2},{1,5},{2,0},{3,7},{4,6},{5,1},{6,4},{7,3},{8,10},{9,13},{10,... | collective-permute-start | bytes 786440 | tf_op jit(solution)/shard_map/ppermute | solution.py:183
  30.7 1.5 %collective-permute-done.14 = bf16[8,8192]{1,0:T(8,128)(2,1)S(1)} collective-permute-done((bf16[8,8192]{1,0:T(8,128)(2,1)S(1)}, bf16[8,8192]{1,0:T(8,128)(2,1)S(1)}, u32[]{:S(2)}, u32[]{:S(2)}) %collective-permute-start.14) | collective-permute-done | bytes 131104 | tf_op jit(solution)/shard_map/ppermute | solution.py:183
  32.2 2.7 %collective-permute-done.15 = bf16[8,8192]{1,0:T(8,128)(2,1)S(1)} collective-permute-done((bf16[8,8192]{1,0:T(8,128)(2,1)S(1)}, bf16[8,8192]{1,0:T(8,128)(2,1)S(1)}, u32[]{:S(2)}, u32[]{:S(2)}) %collective-permute-start.15) | collective-permute-done | bytes 131104 | tf_op jit(solution)/shard_map/ppermute | solution.py:183
  34.9 0.0 collective-permute-done.16
  34.9 0.1 fusion.2
  35.0 2.9 %collective-permute-start.17 = (bf16[8,8192]{1,0:T(8,128)(2,1)S(1)}, bf16[8,8192]{1,0:T(8,128)(2,1)S(1)}, u32[]{:S(2)}, u32[]{:S(2)}) collective-permute-start(bf16[8,8192]{1,0:T(8,128)(2,1)S(1)} %fusion.2), channel_id=1, source_target_pairs={{0,12},{1,9},{2,14},{3,11},{4,8},{5,13},{6,10},{7,15},{8,4},{9,1},... | collective-permute-start | bytes 393224 | tf_op jit(solution)/shard_map/ppermute | solution.py:183
  37.9 0.0 collective-permute-done.12
  37.9 0.1 slice_add_fusion
  38.0 1.2 %collective-permute-start.18 = (bf16[8,8192]{1,0:T(8,128)(2,1)S(1)}, bf16[8,8192]{1,0:T(8,128)(2,1)S(1)}, u32[]{:S(2)}, u32[]{:S(2)}) collective-permute-start(bf16[8,8192]{1,0:T(8,128)(2,1)S(1)} %slice.68), channel_id=1, source_target_pairs={{0,4},{1,3},{2,6},{3,1},{4,0},{5,7},{6,2},{7,5},{8,12},{9,11},{10,... | collective-permute-start | bytes 393224 | tf_op jit(solution)/shard_map/ppermute | solution.py:183
  39.2 2.8 %collective-permute-done.17.refs_1_ = bf16[8,8192]{1,0:T(8,128)(2,1)S(1)} collective-permute-done((bf16[8,8192]{1,0:T(8,128)(2,1)S(1)}, bf16[8,8192]{1,0:T(8,128)(2,1)S(1)}, u32[]{:S(2)}, u32[]{:S(2)}) %collective-permute-start.17) | collective-permute-done | bytes 131104 | tf_op jit(solution)/shard_map/ppermute | solution.py:183
  42.0 2.1 %collective-permute-done.18.refs_2_ = bf16[8,8192]{1,0:T(8,128)(2,1)S(1)} collective-permute-done((bf16[8,8192]{1,0:T(8,128)(2,1)S(1)}, bf16[8,8192]{1,0:T(8,128)(2,1)S(1)}, u32[]{:S(2)}, u32[]{:S(2)}) %collective-permute-start.18) | collective-permute-done | bytes 131104 | tf_op jit(solution)/shard_map/ppermute | solution.py:183
  44.2 0.0 copy-done
  44.2 0.9 %shard_map.60 = bf16[8,8192]{1,0:T(8,128)(2,1)} custom-call(f32[8,8192]{1,0:T(8,128)S(1)} %slice.52.refs_0_, bf16[8,8192]{1,0:T(8,128)(2,1)S(1)} %collective-permute-done.17.refs_1_, bf16[8,8192]{1,0:T(8,128)(2,1)S(1)} %collective-permute-done.18.refs_2_, s32[1,8192]{1,0:T(1,128)S(1)} %bitcast.3, bf16[256,128]{1,0:T(8,128)(2,1)S(1)} %pad_maximum_fusion.2.refs_4_), custom_call_target="tpu_custom_call" | custom-call | tf_op jit(solution)/shard_map/pallas_call | solution.py:160
  (16 shorter events, 0.3 us)
Async XLA Ops:
  0.0 11.2 %collective-permute-start = (bf16[8,8192]{1,0:T(8,128)(2,1)}, bf16[8,8192]{1,0:T(8,128)(2,1)S(1)}, u32[]{:S(2)}, u32[]{:S(2)}) collective-permute-start(bf16[8,8192]{1,0:T(8,128)(2,1)} %param.5), channel_id=1, source_target_pairs={{0,12},{1,9},{2,14},{3,11},{4,8},{5,13},{6,10},{7,15},{8,4},{9,1},... | collective-permute-start | bytes 393224 | tf_op jit(solution)/shard_map/ppermute | solution.py:183
  5.0 7.9 %collective-permute-start.1 = (bf16[8,8192]{1,0:T(8,128)(2,1)}, bf16[8,8192]{1,0:T(8,128)(2,1)S(1)}, u32[]{:S(2)}, u32[]{:S(2)}) collective-permute-start(bf16[8,8192]{1,0:T(8,128)(2,1)} %param.5), channel_id=1, source_target_pairs={{0,4},{1,3},{2,6},{3,1},{4,0},{5,7},{6,2},{7,5},{8,12},{9,11},{10,... | collective-permute-start | bytes 393224 | tf_op jit(solution)/shard_map/ppermute | solution.py:183
  5.1 13.0 %collective-permute-start.3 = (bf16[8,8192]{1,0:T(8,128)(2,1)}, bf16[8,8192]{1,0:T(8,128)(2,1)S(1)}, u32[]{:S(2)}, u32[]{:S(2)}) collective-permute-start(bf16[8,8192]{1,0:T(8,128)(2,1)} %param.5), channel_id=1, source_target_pairs={{0,2},{1,5},{2,0},{3,7},{4,6},{5,1},{6,4},{7,3},{8,10},{9,13},{10,... | collective-permute-start | bytes 393224 | tf_op jit(solution)/shard_map/ppermute | solution.py:183
  6.6 11.5 %collective-permute-start.4 = (bf16[8,8192]{1,0:T(8,128)(2,1)}, bf16[8,8192]{1,0:T(8,128)(2,1)S(1)}, u32[]{:S(2)}, u32[]{:S(2)}) collective-permute-start(bf16[8,8192]{1,0:T(8,128)(2,1)} %param.5), channel_id=1, source_target_pairs={{0,6},{1,7},{2,4},{3,5},{4,2},{5,3},{6,0},{7,1},{8,14},{9,15},{10,... | collective-permute-start | bytes 393224 | tf_op jit(solution)/shard_map/ppermute | solution.py:183
  11.2 6.9 %collective-permute-start.2 = (bf16[8,8192]{1,0:T(8,128)(2,1)S(1)}, bf16[8,8192]{1,0:T(8,128)(2,1)S(1)}, u32[]{:S(2)}, u32[]{:S(2)}) collective-permute-start(bf16[8,8192]{1,0:T(8,128)(2,1)S(1)} %collective-permute-done.refs_2_), channel_id=1, source_target_pairs={{0,4},{1,3},{2,6},{3,1},{4,0},{5,7},{6,2},{7,5},{8,12},{9,11},{10,... | collective-permute-start | bytes 393224 | tf_op jit(solution)/shard_map/ppermute | solution.py:183
  11.4 9.1 %collective-permute-start.5 = (bf16[8,8192]{1,0:T(8,128)(2,1)S(1)}, bf16[8,8192]{1,0:T(8,128)(2,1)S(1)}, u32[]{:S(2)}, u32[]{:S(2)}) collective-permute-start(bf16[8,8192]{1,0:T(8,128)(2,1)S(1)} %collective-permute-done.refs_2_), channel_id=1, source_target_pairs={{0,2},{1,5},{2,0},{3,7},{4,6},{5,1},{6,4},{7,3},{8,10},{9,13},{10,... | collective-permute-start | bytes 393224 | tf_op jit(solution)/shard_map/ppermute | solution.py:183
  12.9 7.6 %collective-permute-start.6 = (bf16[8,8192]{1,0:T(8,128)(2,1)S(1)}, bf16[8,8192]{1,0:T(8,128)(2,1)S(1)}, u32[]{:S(2)}, u32[]{:S(2)}) collective-permute-start(bf16[8,8192]{1,0:T(8,128)(2,1)S(1)} %collective-permute-done.refs_2_), channel_id=1, source_target_pairs={{0,6},{1,7},{2,4},{3,5},{4,2},{5,3},{6,0},{7,1},{8,14},{9,15},{10,... | collective-permute-start | bytes 393224 | tf_op jit(solution)/shard_map/ppermute | solution.py:183
  14.8 3.4 %copy-start.1 = (bf16[8,8192]{1,0:T(8,128)(2,1)S(1)}, bf16[8,8192]{1,0:T(8,128)(2,1)}, u32[]{:S(2)}) copy-start(bf16[8,8192]{1,0:T(8,128)(2,1)} %param.5) | copy-start | bytes 393220
  18.2 3.7 %collective-permute-start.7 = (bf16[48,8192]{1,0:T(8,128)(2,1)S(1)}, bf16[48,8192]{1,0:T(8,128)(2,1)S(1)}, u32[]{:S(2)}, u32[]{:S(2)}) collective-permute-start(bf16[48,8192]{1,0:T(8,128)(2,1)S(1)} %constant_dynamic-update-slice_fusion.refs_2_), channel_id=1, source_target_pairs={{0,1},{1,0},{2,3},{3,2},{4,5},{5,4},{6,7},{7,6},{8,9},{9,8},{10,11... | collective-permute-start | bytes 2359304 | tf_op jit(solution)/shard_map/ppermute | solution.py:183
  20.6 1.4 %collective-permute-start.9 = (bf16[16,4096]{1,0:T(8,128)(2,1)S(1)}, bf16[16,4096]{1,0:T(8,128)(2,1)S(1)}, u32[]{:S(2)}, u32[]{:S(2)}) collective-permute-start(bf16[16,4096]{1,0:T(8,128)(2,1)S(1)} %pad_maximum_fusion.1.refs_4_), channel_id=1, source_target_pairs={{0,1},{1,0},{2,3},{3,2},{4,5},{5,4},{6,7},{7,6},{8,9},{9,8},{10,11... | collective-permute-start | bytes 393224 | tf_op jit(solution)/shard_map/ppermute | solution.py:183
  20.7 2.0 %collective-permute-start.8 = (bf16[16,4096]{1,0:T(8,128)(2,1)S(1)}, bf16[16,4096]{1,0:T(8,128)(2,1)S(1)}, u32[]{:S(2)}, u32[]{:S(2)}) collective-permute-start(bf16[16,4096]{1,0:T(8,128)(2,1)S(1)} %pad_maximum_fusion.refs_4_), channel_id=1, source_target_pairs={{0,1},{1,0},{2,3},{3,2},{4,5},{5,4},{6,7},{7,6},{8,9},{9,8},{10,11... | collective-permute-start | bytes 393224 | tf_op jit(solution)/shard_map/ppermute | solution.py:183
  24.2 1.4 %collective-permute-start.13 = (bf16[8,8192]{1,0:T(8,128)(2,1)S(1)}, bf16[8,8192]{1,0:T(8,128)(2,1)S(1)}, u32[]{:S(2)}, u32[]{:S(2)}) collective-permute-start(bf16[8,8192]{1,0:T(8,128)(2,1)S(1)} %get-tuple-element.54), channel_id=1, source_target_pairs={{0,1},{1,0},{2,3},{3,2},{4,5},{5,4},{6,7},{7,6},{8,9},{9,8},{10,11... | collective-permute-start | bytes 393224 | tf_op jit(solution)/shard_map/ppermute | solution.py:183
  24.4 3.2 %collective-permute-start.10 = (bf16[24,8192]{1,0:T(8,128)(2,1)S(1)}, bf16[24,8192]{1,0:T(8,128)(2,1)S(1)}, u32[]{:S(2)}, u32[]{:S(2)}) collective-permute-start(bf16[24,8192]{1,0:T(8,128)(2,1)S(1)} %get-tuple-element.48), channel_id=1, source_target_pairs={{0,1},{1,0},{2,3},{3,2},{4,5},{5,4},{6,7},{7,6},{8,9},{9,8},{10,11... | collective-permute-start | bytes 1179656 | tf_op jit(solution)/shard_map/ppermute | solution.py:183
  25.6 6.6 %collective-permute-start.14 = (bf16[8,8192]{1,0:T(8,128)(2,1)S(1)}, bf16[8,8192]{1,0:T(8,128)(2,1)S(1)}, u32[]{:S(2)}, u32[]{:S(2)}) collective-permute-start(bf16[8,8192]{1,0:T(8,128)(2,1)S(1)} %add_convert_fusion), channel_id=1, source_target_pairs={{0,6},{1,7},{2,4},{3,5},{4,2},{5,3},{6,0},{7,1},{8,14},{9,15},{10,... | collective-permute-start | bytes 393224 | tf_op jit(solution)/shard_map/ppermute | solution.py:183
  27.6 1.9 %collective-permute-start.11 = (bf16[32,8192]{1,0:T(8,128)(2,1)S(1)}, bf16[32,8192]{1,0:T(8,128)(2,1)S(1)}, u32[]{:S(2)}, u32[]{:S(2)}) collective-permute-start(bf16[32,8192]{1,0:T(8,128)(2,1)S(1)} %get-tuple-element.50), channel_id=1, source_target_pairs={{0,1},{1,0},{2,3},{3,2},{4,5},{5,4},{6,7},{7,6},{8,9},{9,8},{10,11... | collective-permute-start | bytes 1572872 | tf_op jit(solution)/shard_map/ppermute | solution.py:183
  27.7 16.5 %copy-start = (s32[8192]{0:T(1024)S(1)}, s32[8192]{0:T(1024)}, u32[]{:S(2)}) copy-start(s32[8192]{0:T(1024)} %param.9) | copy-start | bytes 98308
  27.7 7.2 %collective-permute-start.15 = (bf16[8,8192]{1,0:T(8,128)(2,1)S(1)}, bf16[8,8192]{1,0:T(8,128)(2,1)S(1)}, u32[]{:S(2)}, u32[]{:S(2)}) collective-permute-start(bf16[8,8192]{1,0:T(8,128)(2,1)S(1)} %get-tuple-element.57), channel_id=1, source_target_pairs={{0,4},{1,3},{2,6},{3,1},{4,0},{5,7},{6,2},{7,5},{8,12},{9,11},{10,... | collective-permute-start | bytes 393224 | tf_op jit(solution)/shard_map/ppermute | solution.py:183
  28.5 6.5 %collective-permute-start.16 = (bf16[8,8192]{1,0:T(8,128)(2,1)S(1)}, bf16[8,8192]{1,0:T(8,128)(2,1)S(1)}, u32[]{:S(2)}, u32[]{:S(2)}) collective-permute-start(bf16[8,8192]{1,0:T(8,128)(2,1)S(1)} %get-tuple-element.58), channel_id=1, source_target_pairs={{0,2},{1,5},{2,0},{3,7},{4,6},{5,1},{6,4},{7,3},{8,10},{9,13},{10,... | collective-permute-start | bytes 393224 | tf_op jit(solution)/shard_map/ppermute | solution.py:183
  29.6 8.3 %collective-permute-start.12 = (bf16[16,8192]{1,0:T(8,128)(2,1)S(1)}, bf16[16,8192]{1,0:T(8,128)(2,1)S(1)}, u32[]{:S(2)}, u32[]{:S(2)}) collective-permute-start(bf16[16,8192]{1,0:T(8,128)(2,1)S(1)} %slice.67), channel_id=1, source_target_pairs={{0,2},{1,5},{2,0},{3,7},{4,6},{5,1},{6,4},{7,3},{8,10},{9,13},{10,... | collective-permute-start | bytes 786440 | tf_op jit(solution)/shard_map/ppermute | solution.py:183
  35.0 7.1 %collective-permute-start.17 = (bf16[8,8192]{1,0:T(8,128)(2,1)S(1)}, bf16[8,8192]{1,0:T(8,128)(2,1)S(1)}, u32[]{:S(2)}, u32[]{:S(2)}) collective-permute-start(bf16[8,8192]{1,0:T(8,128)(2,1)S(1)} %fusion.2), channel_id=1, source_target_pairs={{0,12},{1,9},{2,14},{3,11},{4,8},{5,13},{6,10},{7,15},{8,4},{9,1},... | collective-permute-start | bytes 393224 | tf_op jit(solution)/shard_map/ppermute | solution.py:183
  38.0 6.2 %collective-permute-start.18 = (bf16[8,8192]{1,0:T(8,128)(2,1)S(1)}, bf16[8,8192]{1,0:T(8,128)(2,1)S(1)}, u32[]{:S(2)}, u32[]{:S(2)}) collective-permute-start(bf16[8,8192]{1,0:T(8,128)(2,1)S(1)} %slice.68), channel_id=1, source_target_pairs={{0,4},{1,3},{2,6},{3,1},{4,0},{5,7},{6,2},{7,5},{8,12},{9,11},{10,... | collective-permute-start | bytes 393224 | tf_op jit(solution)/shard_map/ppermute | solution.py:183
